TPU v7x, 32 devices: a whole 2x2x4 slice. The times are simulated.
32 devices in a mesh: cell: 4 (over y, x), snap: 8 (over z, core).
Axes of the slice: x: 2, y: 2, z: 4, core: 2. Of those that a mesh axis runs over, the one named last changes fastest.
Arguments:
- snapshots: float32 [4096, 2048], P('cell', 'snap'), as said below
- sketch: float32 [2048, 256], P('snap'), may hold values from -6 to 6
Outputs:
- q_basis: float32 [4096, 256], P(('cell', 'snap'))
- z_sketch: float32 [2048, 256], P('snap')
- column_scales: float32 [5, 256], replicated
Inputs may be any that keep to these rules, and one draw needn't show every extreme that they name: `snapshots`: finite values with row and column scales of varying size.
All inputs are finite; a program needn't handle non-finite values.
Results may differ from a plain program's by a relative error of at most 0.0003.
Values sent between devices are 32-bit elements; how exact they have to be, the bound alone decides.
No kernel may reach another device: no remote copies, remote signals or barrier semaphores. Data moves between devices by JAX's collectives and lax.ppermute only.
A program may use at most 64 MiB of HBM per device.

v0:
```python
import jax
import jax.numpy as jnp
from jax import lax
from jax.sharding import PartitionSpec as P

ITERS = 2


def local(snapshots, sketch):
    high = lax.Precision.HIGHEST
    local_cells = snapshots.shape[0]
    local_snaps = snapshots.shape[1]
    rank_width = sketch.shape[1]
    all_cells = local_cells * lax.axis_size("cell")
    all_snaps = local_snaps * lax.axis_size("snap")

    def scattered_section(z_input, pending):
        y_raw = lax.psum_scatter(
            jnp.dot(snapshots, z_input, precision=high, preferred_element_type=jnp.float32),
            "snap",
            scatter_dimension=0,
            tiled=True,
        )
        total = lax.psum(jnp.sum(y_raw * y_raw, axis=0), ("cell", "snap"))
        scale_y = jnp.sqrt(total / (pending * pending) / all_cells + 1e-05)
        return (y_raw, scale_y)

    unit_scale = jnp.ones((rank_width,), jnp.float32)
    scales = []
    z_local = jnp.zeros((local_snaps, rank_width), jnp.float32)
    current = sketch
    pending = unit_scale
    for section_index in range(ITERS):
        y_raw, scale_y = scattered_section(current, pending)
        outgoing = y_raw / (pending * scale_y)
        partial_z = lax.dot_general(
            snapshots,
            lax.all_gather(outgoing, "snap", axis=0, tiled=True),
            (((0,), (0,)), ((), ())),
            precision=high,
            preferred_element_type=jnp.float32,
        )
        scales.append(scale_y)
        summed = lax.psum(partial_z, "cell") / unit_scale
        co_total = lax.psum(jnp.sum(summed * summed, axis=0), "snap")
        scale_z = jnp.sqrt(co_total / all_snaps + 1e-05)
        summed, scale_z = (summed, scale_z)
        scales.append(scale_z)
        z_local = summed / scale_z
        current = z_local
        pending = unit_scale
    y_raw, scale_last = scattered_section(current, pending)
    q_final = y_raw / (pending * scale_last)
    scales.append(scale_last)
    return (q_final, z_local, jnp.stack(scales))


def solution(mesh):
    return jax.shard_map(
        local,
        mesh=mesh,
        in_specs=(P("cell", "snap"), P("snap", None)),
        out_specs=(P(("cell", "snap"), None), P("snap", None), P()),
        check_vma=False,
    )
```

profile of v0, /device:TPU:0, one launch (start us, length us, event | category | flops | bytes accessed | tf_op | source)
XLA Modules:
  0.0 410.1 jit_solution(8120376266615561066)
XLA Ops:
  7.2 0.0 copy-start
  7.2 0.0 reduce-scatter.4.cloned.1.call-start
  7.2 1.2 copy-done
  8.4 2.9 fusion.2
  11.3 0.0 reduce-scatter.4.cloned.1.call-update
  11.3 0.0 all-gather.3.cloned.1.call-start
  11.4 35.0 %reduce-scatter.4.cloned.1.call-done = f32[128,256]{1,0:T(8,128)} async-done(((f32[1024,256]{1,0:T(8,128)}), f32[128,256]{1,0:T(8,128)}) %reduce-scatter.4.cloned.1.call-update) | async-done | bytes 131088 | tf_op jit(solution)/shard_map/reduce_scatter | solution.py:18
  46.4 0.0 copy-start.3
  46.4 1.0 multiply_reduce_fusion.4
  47.4 37.9 %psum.49 = f32[256]{0:T(256)S(1)} all-reduce(f32[256]{0:T(256)S(1)} %multiply_reduce_fusion.4), channel_id=1, replica_groups=mesh['cell'=4,'snap'=8] {'cell','snap'}, use_global_device_ids=true, to_apply=%region_2.0 | all-reduce | flops 256 | bytes 2048 | tf_op jit(solution)/shard_map/psum | solution.py:24
  85.4 0.0 copy-done.3
  85.4 0.7 broadcast_divide_fusion.3
  86.1 0.0 all-gather.3.cloned.1.call-update
  86.1 0.0 all-reduce.3.cloned.1.call-start
  86.1 22.6 %all-gather.3.cloned.1.call-done = f32[1024,256]{1,0:T(8,128)} async-done(((f32[128,256]{1,0:T(8,128)}), f32[1024,256]{1,0:T(8,128)}) %all-gather.3.cloned.1.call-update) | async-done | bytes 1048592 | tf_op jit(solution)/shard_map/all_gather | solution.py:38
  108.8 3.8 convolution_bitcast_fusion.3
  112.5 0.0 all-reduce.3.cloned.1.call-update
  112.5 0.0 reduce-scatter.6.cloned.1.call-start
  112.6 42.7 %all-reduce.3.cloned.1.call-done = f32[256,256]{0,1:T(8,128)} async-done(((f32[256,256]{0,1:T(8,128)}), f32[256,256]{0,1:T(8,128)}) %all-reduce.3.cloned.1.call-update) | async-done | bytes 262160 | tf_op jit(solution)/shard_map/psum | solution.py:44
  155.3 0.0 copy-start.1
  155.3 1.1 multiply_reduce_fusion.1
  156.4 15.9 %psum.51 = f32[256]{0:T(256)S(1)} all-reduce(f32[256]{0:T(256)S(1)} %multiply_reduce_fusion.1), channel_id=1, replica_groups=mesh['cell'=4,'snap'=8] {'snap'}, use_global_device_ids=true, to_apply=%region_5.0 | all-reduce | flops 256 | bytes 2048 | tf_op jit(solution)/shard_map/psum | solution.py:45
  172.4 0.0 copy-done.1
  172.4 2.1 convolution_bitcast_fusion.1
  174.4 0.0 reduce-scatter.6.cloned.1.call-update
  174.5 0.0 all-gather.5.cloned.1.call-start
  174.5 29.7 %reduce-scatter.6.cloned.1.call-done = f32[128,256]{0,1:T(8,128)} async-done(((f32[1024,256]{0,1:T(8,128)}), f32[128,256]{0,1:T(8,128)}) %reduce-scatter.6.cloned.1.call-update) | async-done | bytes 131088 | tf_op jit(solution)/shard_map/reduce_scatter | solution.py:18
  204.2 0.0 copy-start.4
  204.2 1.1 multiply_reduce_fusion.3
  205.3 38.0 %psum.52 = f32[256]{0:T(256)S(1)} all-reduce(f32[256]{0:T(256)S(1)} %multiply_reduce_fusion.3), channel_id=1, replica_groups=mesh['cell'=4,'snap'=8] {'cell','snap'}, use_global_device_ids=true, to_apply=%region_8.0 | all-reduce | flops 256 | bytes 2048 | tf_op jit(solution)/shard_map/psum | solution.py:24
  243.3 0.0 copy-done.4
  243.3 0.8 broadcast_divide_fusion.2
  244.1 0.0 all-gather.5.cloned.1.call-update
  244.1 0.0 all-reduce.5.cloned.1.call-start
  244.1 24.5 %all-gather.5.cloned.1.call-done = f32[1024,256]{0,1:T(8,128)} async-done(((f32[128,256]{0,1:T(8,128)}), f32[1024,256]{0,1:T(8,128)}) %all-gather.5.cloned.1.call-update) | async-done | bytes 1048592 | tf_op jit(solution)/shard_map/all_gather | solution.py:38
  268.6 2.9 convolution_bitcast_fusion.2
  271.6 0.0 all-reduce.5.cloned.1.call-update
  271.6 0.0 reduce-scatter.8.cloned.1.call-start
  271.7 42.2 %all-reduce.5.cloned.1.call-done = f32[256,256]{0,1:T(8,128)} async-done(((f32[256,256]{0,1:T(8,128)}), f32[256,256]{0,1:T(8,128)}) %all-reduce.5.cloned.1.call-update) | async-done | bytes 262160 | tf_op jit(solution)/shard_map/psum | solution.py:44
  313.8 0.0 copy-start.2
  313.8 1.1 multiply_reduce_fusion
  315.0 15.9 %psum.54 = f32[256]{0:T(256)S(1)} all-reduce(f32[256]{0:T(256)S(1)} %multiply_reduce_fusion), channel_id=1, replica_groups=mesh['cell'=4,'snap'=8] {'snap'}, use_global_device_ids=true, to_apply=%region_11.0 | all-reduce | flops 256 | bytes 2048 | tf_op jit(solution)/shard_map/psum | solution.py:45
  330.9 0.0 copy-done.2
  330.9 0.1 broadcast_divide_fusion
  331.0 2.0 convolution_bitcast_fusion
  333.1 0.0 reduce-scatter.8.cloned.1.call-update
  333.1 0.8 copy.6
  333.9 28.7 %reduce-scatter.8.cloned.1.call-done = f32[128,256]{0,1:T(8,128)} async-done(((f32[1024,256]{0,1:T(8,128)}), f32[128,256]{0,1:T(8,128)}) %reduce-scatter.8.cloned.1.call-update) | async-done | bytes 131088 | tf_op jit(solution)/shard_map/reduce_scatter | solution.py:18
  362.6 0.0 copy-start.5
  362.6 1.1 multiply_reduce_fusion.2
  363.7 38.1 %psum.55 = f32[256]{0:T(256)S(1)} all-reduce(f32[256]{0:T(256)S(1)} %multiply_reduce_fusion.2), channel_id=1, replica_groups=mesh['cell'=4,'snap'=8] {'cell','snap'}, use_global_device_ids=true, to_apply=%region_14.0 | all-reduce | flops 256 | bytes 2048 | tf_op jit(solution)/shard_map/psum | solution.py:24
  401.8 0.0 copy-done.5
  401.8 0.1 broadcast_divide_fusion.1
  401.9 0.8 copy.5
  402.7 0.6 stack.2
  (5 shorter events, 0.0 us)
Async XLA Ops:
  7.2 1.2 copy-start
  7.2 39.2 %reduce-scatter.4.cloned.1.call-start = ((), (), s32[]{:S(2)}) async-start(), calls=%async_computation.3 | async-start | bytes 1179648 | tf_op jit(solution)/shard_map/reduce_scatter | solution.py:18
  11.3 97.4 %all-gather.3.cloned.1.call-start = ((), (), s32[]{:S(2)}) async-start(), calls=%async_computation.4 | async-start | bytes 1179648 | tf_op jit(solution)/shard_map/all_gather | solution.py:38
  46.4 39.0 %copy-start.3 = (f32[128,256]{1,0:T(8,128)S(1)}, f32[128,256]{1,0:T(8,128)}, u32[]{:S(2)}) copy-start(f32[128,256]{1,0:T(8,128)} %reduce-scatter.4.cloned.1.call-done) | copy-start | bytes 393220
  86.1 69.2 %all-reduce.3.cloned.1.call-start = ((), (), s32[]{:S(2)}) async-start(), calls=%async_computation.5 | async-start | bytes 524288 | tf_op jit(solution)/shard_map/psum | solution.py:44
  112.5 91.7 %reduce-scatter.6.cloned.1.call-start = ((), (), s32[]{:S(2)}) async-start(), calls=%async_computation.6 | async-start | bytes 1179648 | tf_op jit(solution)/shard_map/reduce_scatter | solution.py:18
  155.3 17.1 %copy-start.1 = (f32[256,256]{0,1:T(8,128)S(1)}, f32[256,256]{0,1:T(8,128)}, u32[]{:S(2)}) copy-start(f32[256,256]{0,1:T(8,128)} %all-reduce.3.cloned.1.call-done) | copy-start | bytes 786436
  174.5 94.2 %all-gather.5.cloned.1.call-start = ((), (), s32[]{:S(2)}) async-start(), calls=%async_computation.7 | async-start | bytes 1179648 | tf_op jit(solution)/shard_map/all_gather | solution.py:38
  204.2 39.1 %copy-start.4 = (f32[128,256]{0,1:T(8,128)S(1)}, f32[128,256]{0,1:T(8,128)}, u32[]{:S(2)}) copy-start(f32[128,256]{0,1:T(8,128)} %reduce-scatter.6.cloned.1.call-done) | copy-start | bytes 393220
  244.1 69.7 %all-reduce.5.cloned.1.call-start = ((), (), s32[]{:S(2)}) async-start(), calls=%async_computation.8 | async-start | bytes 524288 | tf_op jit(solution)/shard_map/psum | solution.py:44
  271.6 91.0 %reduce-scatter.8.cloned.1.call-start = ((), (), s32[]{:S(2)}) async-start(), calls=%async_computation.9 | async-start | bytes 1179648 | tf_op jit(solution)/shard_map/reduce_scatter | solution.py:18
  313.8 17.1 %copy-start.2 = (f32[256,256]{0,1:T(8,128)S(1)}, f32[256,256]{0,1:T(8,128)}, u32[]{:S(2)}) copy-start(f32[256,256]{0,1:T(8,128)} %all-reduce.5.cloned.1.call-done) | copy-start | bytes 786436
  362.6 39.2 %copy-start.5 = (f32[128,256]{0,1:T(8,128)S(1)}, f32[128,256]{0,1:T(8,128)}, u32[]{:S(2)}) copy-start(f32[128,256]{0,1:T(8,128)} %reduce-scatter.8.cloned.1.call-done) | copy-start | bytes 393220
Sparse Core Ops, SparseCore 0:
  11.5 34.9 reduce-scatter.3
  86.2 22.5 all-gather.2
  112.7 42.5 all-reduce.2
  174.6 29.5 reduce-scatter.5
  244.2 24.3 all-gather.4
  272.2 41.5 all-reduce.4
  333.2 29.3 reduce-scatter.7
where the time goes:
time: 411 us; the launch traced here: 410 us
  waiting for transfers between devices  225 us (55%)
  blocking collectives  146 us (36%)
  between operations  14.2 us (3%)
  matrix products  13.8 us (3%)
  other arithmetic  7.14 us (2%)
    psum x3, blocking collectives, scattered_section(): total = lax.psum(jnp.sum(y_raw * y_raw, axis=0), ('cell', 'snap'))  114 us
    reduce_scatter x3, waiting for transfers between devices, scattered_section(): lax.psum_scatter(jnp.dot(snapshots, z_input, precision=high, preferred_el...  93.4 us
    psum x2, waiting for transfers between devices, local(): summed = lax.psum(partial_z, 'cell') / unit_scale  84.8 us
    all_gather x2, waiting for transfers between devices, local(): lax.all_gather(outgoing, 'snap', axis=0, tiled=True)  47.1 us
    psum x2, blocking collectives, local(): co_total = lax.psum(jnp.sum(summed * summed, axis=0), 'snap')  31.9 us
  transfers between devices with their start and end apart: 7, of which 7 were waited for; matrix products, arithmetic and copies ran while one was open for 0% of the time, Pallas kernels for 0%

commit v1 on v0

v1 whole, which is shorter than its diff:
```python
import jax
import jax.numpy as jnp
from jax import lax
from jax.sharding import PartitionSpec as P

ITERS = 2
EPS = 1e-05
TILE = 8
DIRECT = 8


def local(snapshots, sketch):
    groups = lax.axis_size("cell")
    places = lax.axis_size("snap")
    chips = places // 2
    rows, width = snapshots.shape
    rank = sketch.shape[1]
    half = rank // 2
    chunk = rows // chips
    all_cells = rows * groups
    all_snaps = width * places
    place = lax.axis_index("snap")
    core = place % 2
    chip = place // 2
    same_core = [[2 * z + k for z in range(chips)] for k in range(2)]
    swap = [(i, i ^ 1) for i in range(places)]

    def swap_core(x):
        return lax.ppermute(x, "snap", swap)

    def exchange_z(x):
        return lax.all_to_all(x, "snap", 0, 0, axis_index_groups=same_core, tiled=True)

    def exchange_cell(x):
        return lax.all_to_all(x, "cell", 0, 0, tiled=True)

    def scatter_sum(y, extra):
        if chips > DIRECT:
            mine = lax.psum_scatter(y, "snap", scatter_dimension=0, axis_index_groups=same_core, tiled=True)
            return mine, lax.psum(extra, "snap", axis_index_groups=same_core)
        pieces = y.reshape(chips, chunk, half)
        extras = jnp.broadcast_to(extra, (chips,) + extra.shape)
        got = exchange_z(jnp.concatenate([pieces, extras], axis=1))
        total = jnp.sum(got, axis=0)
        return total[:chunk], total[chunk:]

    def gather_rows(part, extra):
        if chips > DIRECT:
            full = lax.all_gather(part, "snap", axis=0, axis_index_groups=same_core, tiled=True)
            return full, lax.psum(extra, "snap", axis_index_groups=same_core)
        sent = jnp.concatenate([part, extra], axis=0)
        got = exchange_z(jnp.broadcast_to(sent, (chips,) + sent.shape))
        return got[:, :chunk].reshape(rows, half), jnp.sum(got[:, chunk:], axis=0)

    def cell_sum(z, extra):
        if groups != 4:
            return lax.psum(z, "cell"), lax.psum(extra, "cell")
        part = z.shape[0] // groups
        pieces = z.reshape(groups, part, half)
        extras = jnp.broadcast_to(extra, (groups,) + extra.shape)
        mine = jnp.sum(exchange_cell(jnp.concatenate([pieces, extras], axis=1)), axis=0)
        got = exchange_cell(jnp.broadcast_to(mine[:part], (groups, part, half)))
        return got.reshape(z.shape), mine[part:]

    def dot(a, b, contract):
        return lax.dot_general(
            a, b, (((contract,), (0,)), ((), ())), precision=lax.Precision.HIGH, preferred_element_type=jnp.float32
        )

    def squares(x):
        return jnp.broadcast_to(jnp.sum(x * x, axis=0, keepdims=True), (TILE, half))

    def rms(total, count):
        return jnp.sqrt(total[0:1] / count + EPS)

    other = swap_core(snapshots)
    split = sketch.reshape(width, 2, half)
    z_own = lax.dynamic_index_in_dim(split, core, 1, keepdims=False)
    z_other = swap_core(lax.dynamic_index_in_dim(split, 1 - core, 1, keepdims=False))
    z_extra = jnp.zeros((TILE, half), jnp.float32)

    scales = []
    for section in range(ITERS + 1):
        partial = dot(snapshots, z_own, 1) + dot(other, z_other, 1)
        y, z_total = scatter_sum(partial, z_extra)
        if section > 0:
            scale_z = rms(z_total, all_snaps)
            scales.append(scale_z)
            y = y / scale_z
            z_own, z_other = z_own / scale_z, z_other / scale_z
        if section == ITERS:
            break
        y_all, y_total = gather_rows(y, squares(y))
        z = jnp.concatenate([dot(snapshots, y_all, 0), dot(other, y_all, 0)], axis=0)
        z, y_total = cell_sum(z, y_total)
        scale_y = rms(y_total, all_cells)
        scales.append(scale_y)
        z_own, z_other = z[:width] / scale_y, z[width:] / scale_y
        z_extra = squares(z_own) + squares(z_other)

    def join(own, got):
        pair = jnp.where(core == 0, jnp.stack([own, got]), jnp.stack([got, own]))
        return jnp.moveaxis(pair, 0, 1).reshape(own.shape[0], rank)

    z_out = join(z_own, swap_core(z_other))
    y_split = y.reshape(2, chunk // 2, half)
    y_own = lax.dynamic_index_in_dim(y_split, core, 0, keepdims=False)
    y_send = lax.dynamic_index_in_dim(y_split, 1 - core, 0, keepdims=False)
    known = jnp.concatenate(scales + [squares(y)[: TILE - len(scales)]], axis=0)
    sent = jnp.concatenate([y_send, known], axis=0)
    got = swap_core(sent)
    y_join = join(y_own, got[: chunk // 2])
    known = join(known, got[chunk // 2 :])
    if chips > DIRECT or groups != 4:
        tail = lax.psum(known, ("cell", "snap")) / 2
    else:
        tail = jnp.sum(exchange_z(jnp.broadcast_to(known, (chips,) + known.shape)), axis=0)
        tail = jnp.sum(exchange_cell(jnp.broadcast_to(tail, (groups,) + tail.shape)), axis=0)
    scale_y = rms(tail[TILE - 1 :], all_cells)
    q_out = y_join / scale_y
    return q_out, z_out, jnp.concatenate([known[: len(scales)], scale_y], axis=0)


def solution(mesh):
    return jax.shard_map(
        local,
        mesh=mesh,
        in_specs=(P("cell", "snap"), P("snap", None)),
        out_specs=(P(("cell", "snap"), None), P("snap", None), P()),
        check_vma=False,
    )
```

time: 411 us -> 158 us (0.38)
  waiting for transfers between devices: 225 us -> 32 us
  blocking collectives: 146 us -> 87 us
  starting transfers between devices: 0.29 us -> 18.1 us
  between operations: 14.2 us -> 1.24 us
  matrix products: 13.8 us -> 6.56 us
  local copies, waits for them, and re-layouts: 3.4 us -> 9.62 us
    psum x5 -> x0, blocking collectives: 146 us -> none  [the longest x3 114 us: scattered_section(): total = lax.psum(jnp.sum(y_raw * y_raw, axis=0), ('cell', 'snap'))]
    reduce_scatter x3 -> x0, waiting for transfers between devices: 93.4 us -> none  [scattered_section(): lax.psum_scatter(jnp.dot(snapshots, z_input, precision=high, preferred_el...]
    all_to_all x0 -> x6, blocking collectives: none -> 87 us  [the longest x4 68.9 us: exchange_z(): lax.all_to_all(x, 'snap', 0, 0, axis_index_groups=same_core, tiled=True)]
    psum x2 -> x0, waiting for transfers between devices: 84.8 us -> none  [local(): summed = lax.psum(partial_z, 'cell') / unit_scale]
    all_gather x2 -> x0, waiting for transfers between devices: 47.1 us -> none  [local(): lax.all_gather(outgoing, 'snap', axis=0, tiled=True)]
    all_to_all x0 -> x5, waiting for transfers between devices: none -> 30.8 us  [the longest x2 16.6 us: exchange_z(): lax.all_to_all(x, 'snap', 0, 0, axis_index_groups=same_core, tiled=True)]
    all_to_all x0 -> x5, starting transfers between devices: none -> 16.8 us  [the longest x3 10.1 us: exchange_cell(): return lax.all_to_all(x, 'cell', 0, 0, tiled=True)]
    dot_general x5 -> x10, matrix products: 13.8 us -> 6.56 us  [dot(): lax.dot_general(a, b, (((contract,), (0,)), ((), ())), precision=lax.Prec...]
  transfers between devices with their start and end apart: 7 -> 9, of which waited for: 7 -> 7; matrix products, arithmetic and copies ran while one was open for 0% -> 3% of each run, Pallas kernels for 0% -> 0%
where the time goes in v1:
time: 158 us
  blocking collectives  87 us (55%)
  waiting for transfers between devices  32 us (20%)
  starting transfers between devices  18.1 us (11%)
  local copies, waits for them, and re-layouts  9.62 us (6%)
  matrix products  6.56 us (4%)
  other arithmetic  3.09 us (2%)
    all_to_all x4, blocking collectives, exchange_z(): lax.all_to_all(x, 'snap', 0, 0, axis_index_groups=same_core, tiled=True)  68.9 us
    all_to_all x2, blocking collectives, exchange_cell(): return lax.all_to_all(x, 'cell', 0, 0, tiled=True)  18.1 us
    all_to_all x2, waiting for transfers between devices, exchange_z(): lax.all_to_all(x, 'snap', 0, 0, axis_index_groups=same_core, tiled=True)  16.6 us
    all_to_all x3, waiting for transfers between devices, exchange_cell(): return lax.all_to_all(x, 'cell', 0, 0, tiled=True)  14.3 us
    all_to_all x3, starting transfers between devices, exchange_cell(): return lax.all_to_all(x, 'cell', 0, 0, tiled=True)  10.1 us
    all_to_all x2, starting transfers between devices, exchange_z(): lax.all_to_all(x, 'snap', 0, 0, axis_index_groups=same_core, tiled=True)  6.74 us
    dot_general x10, matrix products, dot(): lax.dot_general(a, b, (((contract,), (0,)), ((), ())), precision=lax.Prec...  6.56 us
  transfers between devices with their start and end apart: 9, of which 7 were waited for; matrix products, arithmetic and copies ran while one was open for 3% of the time, Pallas kernels for 0%

profile of v1, /device:TPU:0, one launch (start us, length us, event | category | flops | bytes accessed | tf_op | source)
XLA Modules:
  0.0 157.7 jit_solution(8416377782242007488)
XLA Ops:
  0.6 0.5 collective-permute-start.1
  1.2 1.1 reshape.113
  2.3 0.2 constant_dynamic-slice_fusion.2
  2.5 0.2 collective-permute-start
  2.7 0.7 fusion.16
  3.4 0.5 collective-permute-done
  3.9 0.7 fusion
  4.6 0.2 copy.137
  4.9 21.2 %all_to_all.55 = f32[4,264,128]{2,1,0:T(8,128)S(1)} all-to-all(f32[4,264,128]{2,1,0:T(8,128)S(1)} %concatenate.37), channel_id=1, replica_groups={{0,2,4,6},{1,3,5,7},{8,10,12,14},{9,11,13,15},{16,18,20,22},{17,19,21,2..., dimensions={0} | all-to-all | bytes 1081344 | tf_op jit(solution)/shard_map/all_to_all | solution.py:32
  26.1 0.1 copy.147
  26.2 0.1 multiply_reduce_fusion.6
  26.4 0.1 copy.112
  26.6 17.3 %all_to_all.56 = f32[4,264,128]{2,1,0:T(8,128)S(1)} all-to-all(f32[4,264,128]{2,1,0:T(8,128)S(1)} %broadcast_in_dim.25), channel_id=1, replica_groups={{0,2,4,6},{1,3,5,7},{8,10,12,14},{9,11,13,15},{16,18,20,22},{17,19,21,2..., dimensions={0} | all-to-all | bytes 1081344 | tf_op jit(solution)/shard_map/all_to_all | solution.py:32
  43.9 0.6 convolution_bitcast_fusion.3
  44.5 0.6 convolution_bitcast_fusion.2
  45.1 0.1 copy.138
  45.3 9.6 %all_to_all.57 = f32[4,136,128]{2,1,0:T(8,128)S(1)} all-to-all(f32[4,136,128]{2,1,0:T(8,128)S(1)} %pad_maximum_fusion.2), channel_id=1, replica_groups=mesh['cell'=4,'snap'=8] {'cell'}, dimensions={0} | all-to-all | bytes 557056 | tf_op jit(solution)/shard_map/all_to_all | solution.py:35
  55.0 0.7 broadcast_in_dim.27
  55.7 3.4 %all-to-all-start.3 = ((f32[4,128,128]{2,1,0:T(8,128)}), f32[4,128,128]{2,1,0:T(8,128)S(1)}, u32[]{:S(2)}, u32[]{:S(2)}) async-start(f32[4,128,128]{2,1,0:T(8,128)} %broadcast_in_dim.27), calls=%async_computation.3 | async-start | bytes 524288 | tf_op jit(solution)/shard_map/all_to_all | solution.py:35
  59.1 5.3 %all-to-all-done.3 = f32[4,128,128]{2,1,0:T(8,128)S(1)} async-done(((f32[4,128,128]{2,1,0:T(8,128)}), f32[4,128,128]{2,1,0:T(8,128)S(1)}, u32[]{:S(2)}, u32[]{:S(2)}) %all-to-all-start.3) | async-done | bytes 262176 | tf_op jit(solution)/shard_map/all_to_all | solution.py:35
  64.5 0.7 fusion.17
  65.2 0.7 fusion.1
  66.0 0.2 copy.139
  66.2 14.3 %all_to_all.58 = f32[4,264,128]{2,1,0:T(8,128)S(1)} all-to-all(f32[4,264,128]{2,1,0:T(8,128)S(1)} %pad_maximum_fusion), channel_id=1, replica_groups={{0,2,4,6},{1,3,5,7},{8,10,12,14},{9,11,13,15},{16,18,20,22},{17,19,21,2..., dimensions={0} | all-to-all | bytes 1081344 | tf_op jit(solution)/shard_map/all_to_all | solution.py:32
  80.6 0.1 copy.155
  80.7 0.2 multiply_reduce_fusion.3
  81.2 16.1 %all_to_all.59 = f32[4,264,128]{2,1,0:T(8,128)S(1)} all-to-all(f32[4,264,128]{2,1,0:T(8,128)S(1)} %broadcast_in_dim.30), channel_id=1, replica_groups={{0,2,4,6},{1,3,5,7},{8,10,12,14},{9,11,13,15},{16,18,20,22},{17,19,21,2..., dimensions={0} | all-to-all | bytes 1081344 | tf_op jit(solution)/shard_map/all_to_all | solution.py:32
  97.3 0.6 convolution_bitcast_fusion.1
  97.9 0.6 convolution_bitcast_fusion
  98.5 0.1 copy.140
  98.7 8.5 %all_to_all.60 = f32[4,136,128]{2,1,0:T(8,128)S(1)} all-to-all(f32[4,136,128]{2,1,0:T(8,128)S(1)} %pad_maximum_fusion.3), channel_id=1, replica_groups=mesh['cell'=4,'snap'=8] {'cell'}, dimensions={0} | all-to-all | bytes 557056 | tf_op jit(solution)/shard_map/all_to_all | solution.py:35
  107.2 0.7 broadcast_in_dim.32
  107.9 3.4 %all-to-all-start.7 = ((f32[4,128,128]{2,1,0:T(8,128)}), f32[4,128,128]{2,1,0:T(8,128)S(1)}, u32[]{:S(2)}, u32[]{:S(2)}) async-start(f32[4,128,128]{2,1,0:T(8,128)} %broadcast_in_dim.32), calls=%async_computation.7 | async-start | bytes 524288 | tf_op jit(solution)/shard_map/all_to_all | solution.py:35
  111.3 5.3 %all-to-all-done.7 = f32[4,128,128]{2,1,0:T(8,128)S(1)} async-done(((f32[4,128,128]{2,1,0:T(8,128)}), f32[4,128,128]{2,1,0:T(8,128)S(1)}, u32[]{:S(2)}, u32[]{:S(2)}) %all-to-all-start.7) | async-done | bytes 262176 | tf_op jit(solution)/shard_map/all_to_all | solution.py:35
  116.8 0.7 fusion.18
  117.5 0.7 fusion.2
  118.2 0.2 copy.141
  118.4 0.8 pad_maximum_fusion.1
  119.2 3.5 %all-to-all-start.8 = ((f32[4,264,128]{2,1,0:T(8,128)}), f32[4,264,128]{2,1,0:T(8,128)S(1)}, u32[]{:S(2)}, u32[]{:S(2)}) async-start(f32[4,264,128]{2,1,0:T(8,128)} %pad_maximum_fusion.1), calls=%async_computation.8 | async-start | bytes 1081344 | tf_op jit(solution)/shard_map/all_to_all | solution.py:32
  122.7 0.1 copy.129
  122.8 0.1 copy.130
  123.0 0.1 copy.131
  123.1 11.0 %all-to-all-done.8 = f32[4,264,128]{2,1,0:T(8,128)S(1)} async-done(((f32[4,264,128]{2,1,0:T(8,128)}), f32[4,264,128]{2,1,0:T(8,128)S(1)}, u32[]{:S(2)}, u32[]{:S(2)}) %all-to-all-start.8) | async-done | bytes 540704 | tf_op jit(solution)/shard_map/all_to_all | solution.py:32
  134.1 0.6 copy-done.1
  134.8 0.9 slice-done
  135.7 0.1 copy.159
  135.8 0.1 copy.132
  135.9 0.2 multiply_reduce_fusion
  136.2 0.1 constant_dynamic-slice_fusion.1
  136.4 0.1 concatenate.46
  136.6 0.1 broadcast_divide_fusion
  136.7 0.6 collective-permute-start.3
  137.3 0.6 collective-permute-done.2
  138.0 0.6 broadcast_in_dim.34
  138.6 3.3 %all-to-all-start.9 = ((f32[4,8,256]{2,1,0:T(8,128)}), f32[4,8,256]{2,1,0:T(8,128)S(1)}, u32[]{:S(2)}, u32[]{:S(2)}) async-start(f32[4,8,256]{2,1,0:T(8,128)} %broadcast_in_dim.34), calls=%async_computation.9 | async-start | bytes 65536 | tf_op jit(solution)/shard_map/all_to_all | solution.py:32
  141.9 5.6 %all-to-all-done.9 = f32[4,8,256]{2,1,0:T(8,128)S(1)} async-done(((f32[4,8,256]{2,1,0:T(8,128)}), f32[4,8,256]{2,1,0:T(8,128)S(1)}, u32[]{:S(2)}, u32[]{:S(2)}) %all-to-all-start.9) | async-done | bytes 32800 | tf_op jit(solution)/shard_map/all_to_all | solution.py:32
  147.5 0.6 broadcast_in_dim.35
  148.2 3.3 %all-to-all-start.10 = ((f32[4,8,256]{2,1,0:T(8,128)}), f32[4,8,256]{2,1,0:T(8,128)S(1)}, u32[]{:S(2)}, u32[]{:S(2)}) async-start(f32[4,8,256]{2,1,0:T(8,128)} %broadcast_in_dim.35), calls=%async_computation.10 | async-start | bytes 65536 | tf_op jit(solution)/shard_map/all_to_all | solution.py:35
  151.4 0.4 maximum_select_fusion
  151.8 0.7 copy.163
  152.6 3.6 %all-to-all-done.10 = f32[4,8,256]{2,1,0:T(8,128)S(1)} async-done(((f32[4,8,256]{2,1,0:T(8,128)}), f32[4,8,256]{2,1,0:T(8,128)S(1)}, u32[]{:S(2)}, u32[]{:S(2)}) %all-to-all-start.10) | async-done | bytes 32800 | tf_op jit(solution)/shard_map/all_to_all | solution.py:35
  156.2 0.1 bitcast_divide_fusion
  156.3 0.8 copy.136
  157.1 0.6 pad_maximum_fusion.8
  (64 shorter events, 1.4 us)
Async XLA Ops:
  0.6 2.1 %copy-start = (f32[1024,256]{1,0:T(8,128)S(1)}, f32[1024,256]{1,0:T(8,128)}, u32[]{:S(2)}) copy-start(f32[1024,256]{1,0:T(8,128)} %param.2) | copy-start | bytes 3145732
  0.6 3.3 %collective-permute-start.1 = (f32[1024,256]{1,0:T(8,128)}, f32[1024,256]{1,0:T(8,128)S(1)}, u32[]{:S(2)}, u32[]{:S(2)}) collective-permute-start(f32[1024,256]{1,0:T(8,128)} %param.2), channel_id=1, source_target_pairs={{0,1},{1,0},{2,3},{3,2},{4,5},{5,4},{6,7},{7,6},{8,9},{9,8},{10,11... | collective-permute-start | bytes 3145736 | tf_op jit(solution)/shard_map/ppermute | solution.py:29
  2.5 1.4 collective-permute-start
  55.7 8.8 %all-to-all-start.3 = ((f32[4,128,128]{2,1,0:T(8,128)}), f32[4,128,128]{2,1,0:T(8,128)S(1)}, u32[]{:S(2)}, u32[]{:S(2)}) async-start(f32[4,128,128]{2,1,0:T(8,128)} %broadcast_in_dim.27), calls=%async_computation.3 | async-start | bytes 524288 | tf_op jit(solution)/shard_map/all_to_all | solution.py:35
  107.9 8.8 %all-to-all-start.7 = ((f32[4,128,128]{2,1,0:T(8,128)}), f32[4,128,128]{2,1,0:T(8,128)S(1)}, u32[]{:S(2)}, u32[]{:S(2)}) async-start(f32[4,128,128]{2,1,0:T(8,128)} %broadcast_in_dim.32), calls=%async_computation.7 | async-start | bytes 524288 | tf_op jit(solution)/shard_map/all_to_all | solution.py:35
  119.2 14.9 %all-to-all-start.8 = ((f32[4,264,128]{2,1,0:T(8,128)}), f32[4,264,128]{2,1,0:T(8,128)S(1)}, u32[]{:S(2)}, u32[]{:S(2)}) async-start(f32[4,264,128]{2,1,0:T(8,128)} %pad_maximum_fusion.1), calls=%async_computation.8 | async-start | bytes 1081344 | tf_op jit(solution)/shard_map/all_to_all | solution.py:32
  134.1 0.7 copy-start.1
  134.8 0.9 slice-start
  136.5 1.4 collective-permute-start.2
  136.7 14.7 %collective-permute-start.3 = (f32[256,128]{1,0:T(8,128)S(1)}, f32[256,128]{1,0:T(8,128)S(1)}, u32[]{:S(2)}, u32[]{:S(2)}) collective-permute-start(f32[256,128]{1,0:T(8,128)S(1)} %bitcast_divide_fusion.1), channel_id=1, source_target_pairs={{0,1},{1,0},{2,3},{3,2},{4,5},{5,4},{6,7},{7,6},{8,9},{9,8},{10,11... | collective-permute-start | bytes 393224 | tf_op jit(solution)/shard_map/ppermute | solution.py:29
  138.6 8.9 %all-to-all-start.9 = ((f32[4,8,256]{2,1,0:T(8,128)}), f32[4,8,256]{2,1,0:T(8,128)S(1)}, u32[]{:S(2)}, u32[]{:S(2)}) async-start(f32[4,8,256]{2,1,0:T(8,128)} %broadcast_in_dim.34), calls=%async_computation.9 | async-start | bytes 65536 | tf_op jit(solution)/shard_map/all_to_all | solution.py:32
  148.2 8.0 %all-to-all-start.10 = ((f32[4,8,256]{2,1,0:T(8,128)}), f32[4,8,256]{2,1,0:T(8,128)S(1)}, u32[]{:S(2)}, u32[]{:S(2)}) async-start(f32[4,8,256]{2,1,0:T(8,128)} %broadcast_in_dim.35), calls=%async_computation.10 | async-start | bytes 65536 | tf_op jit(solution)/shard_map/all_to_all | solution.py:35

commit v2 on v0

v2 whole, which is shorter than its diff:
```python
import functools

import jax
import jax.numpy as jnp
from jax import lax
from jax.experimental import pallas as pl
from jax.experimental.pallas import tpu as pltpu
from jax.sharding import PartitionSpec as P

ITERS = 2
EPS = 1e-05
LANES = 128
TILE = 8
PARTS = 4


def split(x):
    high = x.astype(jnp.bfloat16)
    return high, (x - high.astype(jnp.float32)).astype(jnp.bfloat16)


def product(high, low, a_high, a_low, contract):
    dims = (((1,), (contract,)), ((), ()))
    both = lax.dot_general(
        jnp.concatenate([high, low], axis=0), a_high, dims, preferred_element_type=jnp.float32
    )
    cross = lax.dot_general(high, a_low, dims, preferred_element_type=jnp.float32)
    cols = high.shape[0]
    return both[:cols] + both[cols:] + cross


def eye(cols):
    shape = (cols, LANES)
    return lax.broadcasted_iota(jnp.int32, shape, 0) == lax.broadcasted_iota(jnp.int32, shape, 1)


def to_column(row, cols):
    return jnp.sum(jnp.where(eye(cols), row, 0.0), axis=1, keepdims=True)


def to_row(column):
    return jnp.sum(jnp.where(eye(column.shape[0]), column, 0.0), axis=0, keepdims=True)


def squares_row(x):
    return to_row(jnp.sum(x * x, axis=1, keepdims=True))


def rms(total, count):
    return jnp.sqrt(total / count + EPS)


def wide(ref, cols, count):
    return jnp.concatenate([ref[j * cols : (j + 1) * cols, :] for j in range(count)], axis=1)


def store_blocks(ref, start, x):
    cols = x.shape[0]
    for j in range(x.shape[1] // LANES):
        ref[start + j * cols : start + (j + 1) * cols, :] = x[:, j * LANES : (j + 1) * LANES]


def first_kernel(near_ref, far_ref, own_ref, core_ref, side_ref, diagonal_ref, y_ref, high_ref, low_ref):
    width = own_ref.shape[1]
    for b, ref in enumerate((own_ref, core_ref, side_ref, diagonal_ref)):
        high, low = split(ref[...])
        high_ref[:, b * width : (b + 1) * width] = high
        low_ref[:, b * width : (b + 1) * width] = low
    high, low = split(jnp.concatenate([near_ref[...], far_ref[...]], axis=1))
    store_blocks(y_ref, 0, product(high, low, high_ref[...], low_ref[...], 1))


def send_z(y, high_refs, low_refs, z_ref):
    high, low = split(y)
    part = high_refs[0].shape[0]
    z = None
    for i, (high_ref, low_ref) in enumerate(zip(high_refs, low_refs)):
        cut = slice(i * part, (i + 1) * part)
        term = product(high[:, cut], low[:, cut], high_ref[...], low_ref[...], 0)
        z = term if z is None else z + term
    store_blocks(z_ref, 0, z)
    z_ref[-TILE:, :] = jnp.broadcast_to(squares_row(y), (TILE, LANES))


def first_z_kernel(*refs):
    own, got, high, low = (refs[i * PARTS : (i + 1) * PARTS] for i in range(4))
    cols = own[0].shape[0] * LANES // high[0].shape[0]
    blocks = own[0].shape[0] // cols
    y = jnp.concatenate([wide(a, cols, blocks) + wide(b, cols, blocks) for a, b in zip(own, got)], axis=1)
    send_z(y, high, low, refs[-1])


def z_kernel(count, *refs):
    own_ref, got_ref = refs[:2]
    high, low = refs[2 : 2 + PARTS], refs[2 + PARTS : 2 + 2 * PARTS]
    z_ref, scale_ref = refs[-2:]
    blocks = high[0].shape[0] * PARTS // LANES
    cols = (own_ref.shape[0] - TILE) // blocks
    scale = rms(own_ref[-TILE:, :] + got_ref[-TILE:, :], count)
    scale_ref[...] = scale
    y = (wide(own_ref, cols, blocks) + wide(got_ref, cols, blocks)) / to_column(scale[:1], cols)
    send_z(y, high, low, z_ref)


def y_kernel(count, *refs):
    own_ref, got_ref = refs[:2]
    high_refs, low_refs = refs[2 : 2 + PARTS], refs[2 + PARTS : 2 + 2 * PARTS]
    y_ref, scale_ref, z_ref = refs[-3:]
    blocks = high_refs[0].shape[1] // LANES
    cols = (own_ref.shape[0] - TILE) // blocks
    scale = rms(own_ref[-TILE:, :] + got_ref[-TILE:, :], count)
    scale_ref[...] = scale
    z = (wide(own_ref, cols, blocks) + wide(got_ref, cols, blocks)) / to_column(scale[:1], cols)
    store_blocks(z_ref, 0, z)
    high, low = split(z)
    step = cols * high_refs[0].shape[0] // LANES
    for i, (high_ref, low_ref) in enumerate(zip(high_refs, low_refs)):
        store_blocks(y_ref, i * step, product(high, low, high_ref[...], low_ref[...], 1))
    y_ref[-TILE:, :] = jnp.broadcast_to(squares_row(z), (TILE, LANES))


def prepare_kernel(place_ref, near_ref, got_ref, mine_ref, theirs_ref):
    cols = mine_ref.shape[0]
    width = near_ref.shape[0]
    for b, ref in enumerate((near_ref, got_ref)):
        flipped = ref[...].T
        for ours, out in ((0, mine_ref), (1, theirs_ref)):
            first = place_ref[1] == ours
            out[:, b * width : (b + 1) * width] = jnp.where(first, flipped[:cols], flipped[cols:])


def call(kernel, outs, *args, scalars=0):
    specs = [pl.BlockSpec(memory_space=pltpu.SMEM)] * scalars
    specs += [pl.BlockSpec(memory_space=pltpu.VMEM)] * (len(args) - scalars)
    return pl.pallas_call(
        kernel,
        out_shape=[jax.ShapeDtypeStruct(shape, dtype) for shape, dtype in outs],
        in_specs=specs,
        out_specs=[pl.BlockSpec(memory_space=pltpu.VMEM)] * len(outs),
        compiler_params=pltpu.CompilerParams(vmem_limit_bytes=24 * 1024 * 1024),
    )(*args)


def local(snapshots, sketch):
    f32 = jnp.float32
    groups = lax.axis_size("cell")
    places = lax.axis_size("snap")
    pairs = places // 4
    rows, width = snapshots.shape
    rank = sketch.shape[1]
    half = rank // 2
    cols = rank // 4
    all_cells = rows * groups
    all_snaps = width * places
    place = lax.axis_index("snap")
    core = place % 2
    side = (place // 2) % 2
    pair = place // 4
    where = jnp.stack([core, side, pair]).astype(jnp.int32)
    same_seat = [[4 * p + s for p in range(pairs)] for s in range(4)]

    def swap_core(x):
        return lax.ppermute(x, "snap", [(i, i ^ 1) for i in range(places)])

    def swap_side(x):
        return lax.ppermute(x, "snap", [(i, i ^ 2) for i in range(places)])

    def swap_pair(x):
        if pairs == 2:
            return lax.ppermute(x, "snap", [(i, i ^ 4) for i in range(places)])
        return lax.psum(x, "snap", axis_index_groups=same_seat) - x

    def swap_cell(x, step):
        def target(cell, seat):
            return cell ^ (1 if seat % 2 == step else 2)

        perm = [(c * places + i, target(c, i) * places + i) for c in range(groups) for i in range(places)]
        return lax.ppermute(x, ("cell", "snap"), perm)

    def cell_sum(x):
        if groups != 4:
            return lax.psum(x, "cell"), jnp.zeros_like(x)
        x = x + swap_cell(x, 0)
        return x, swap_cell(x, 1)

    def pick(x, index, count, axis):
        size = x.shape[axis] // count
        return lax.dynamic_slice_in_dim(x, index * size, size, axis)

    def order(flag, own, got, axis):
        first = jnp.where(flag == 0, own, got)
        second = jnp.where(flag == 0, got, own)
        return jnp.concatenate([first, second], axis=axis)

    def unpack(x):
        return jnp.moveaxis(x.reshape(-1, cols, LANES), 0, 1).reshape(cols, -1)

    part = rows // PARTS
    chunks = [snapshots[i * part : (i + 1) * part] for i in range(PARTS)]
    side_chunks = [swap_side(chunks[0])]
    got = swap_core(pick(sketch, 1 - core, 2, 1))
    mine, theirs = call(
        prepare_kernel, [((cols, 2 * width), f32)] * 2, where, pick(sketch, core, 2, 1), got, scalars=1
    )
    far = swap_side(theirs)
    core_block = swap_core(snapshots)
    side_chunks += [swap_side(c) for c in chunks[1:]]
    diagonal_chunks = [swap_core(c) for c in side_chunks]

    high, low, own = [], [], []
    for i in range(PARTS):
        y, a_high, a_low = call(
            first_kernel,
            [((cols * part // LANES, LANES), f32)] + [((part, 4 * width), jnp.bfloat16)] * 2,
            mine, far, chunks[i], core_block[i * part : (i + 1) * part], side_chunks[i], diagonal_chunks[i],
        )
        high.append(a_high)
        low.append(a_low)
        own.append(y)
    got = [swap_pair(y) for y in own]

    sent_shape = ((cols * 4 * width // LANES + TILE, LANES), f32)
    y_shape = ((cols * rows // LANES + TILE, LANES), f32)
    scale_shape = ((TILE, LANES), f32)
    z_shape = ((cols * 4 * width // LANES, LANES), f32)
    (sent,) = call(first_z_kernel, [sent_shape], *own, *got, *high, *low)
    scales = []
    for section in range(ITERS):
        a, b = cell_sum(sent)
        y, scale, z = call(
            functools.partial(y_kernel, all_cells), [y_shape, scale_shape, z_shape], a, b, *high, *low
        )
        scales.append(scale)
        if section == ITERS - 1:
            break
        sent, scale = call(
            functools.partial(z_kernel, all_snaps), [sent_shape, scale_shape], y, swap_pair(y), *high, *low
        )
        scales.append(scale)

    near, far = z[: z.shape[0] // 2], z[z.shape[0] // 2 :]
    z = order(side, unpack(near), unpack(swap_side(far)), 0)
    z = order(core, z[:, :width], swap_core(z[:, width:]), 0)

    tail = y[-TILE:]
    y = y[:-TILE]
    if pairs == 2:
        got = swap_pair(jnp.concatenate([pick(y, 1 - pair, 2, 0), tail], axis=0))
        y, tail = unpack(pick(y, pair, 2, 0) + got[:-TILE]), tail + got[-TILE:]
    else:
        y = lax.psum(unpack(y), "snap", axis_index_groups=same_seat)
        y = pick(y, pair, pairs, 1)
        tail = lax.psum(tail, "snap", axis_index_groups=same_seat)
    scales.append(rms(tail, all_snaps))
    known = jnp.concatenate([s[:1, :cols] for s in scales], axis=0).T
    y = y / known[:, -1:]
    known = jnp.concatenate([known, jnp.sum(y * y, axis=1, keepdims=True)], axis=1)
    known = jnp.pad(known, ((0, 0), (0, LANES - known.shape[1])))
    got = swap_side(jnp.concatenate([pick(y, 1 - side, 2, 1), known], axis=1))
    y = order(side, jnp.concatenate([pick(y, side, 2, 1), known], axis=1), got, 0)
    y, known = y[:, :-LANES], y[:, -LANES:]
    got = swap_core(jnp.concatenate([pick(y, 1 - core, 2, 1), known], axis=1))
    y = order(core, jnp.concatenate([pick(y, core, 2, 1), known], axis=1), got, 0)
    y, known = y[:, :-LANES], y[:, -LANES:].T[: 2 * ITERS + 1]
    total = known + swap_pair(known)
    a, b = cell_sum(total)
    scale_y = rms((a + b)[2 * ITERS :], all_cells)
    q_out = y.T / scale_y
    z_out = z.T / known[2 * ITERS - 1 : 2 * ITERS]
    return q_out, z_out, jnp.concatenate([known[: 2 * ITERS], scale_y], axis=0)


def solution(mesh):
    return jax.shard_map(
        local,
        mesh=mesh,
        in_specs=(P("cell", "snap"), P("snap", None)),
        out_specs=(P(("cell", "snap"), None), P("snap", None), P()),
        check_vma=False,
    )
```

time: 411 us -> 129 us (0.31)
  blocking collectives: 146 us -> 0 us
  waiting for transfers between devices: 225 us -> 82.8 us
  starting transfers between devices: 0.29 us -> 25.1 us
  matrix products: 13.8 us -> 0 us
  between operations: 14.2 us -> 1.01 us
  Pallas kernels: 0 us -> 9.7 us
    psum x5 -> x0, blocking collectives: 146 us -> none  [the longest x3 114 us: scattered_section(): total = lax.psum(jnp.sum(y_raw * y_raw, axis=0), ('cell', 'snap'))]
    reduce_scatter x3 -> x0, waiting for transfers between devices: 93.4 us -> none  [scattered_section(): lax.psum_scatter(jnp.dot(snapshots, z_input, precision=high, preferred_el...]
    psum x2 -> x0, waiting for transfers between devices: 84.8 us -> none  [local(): summed = lax.psum(partial_z, 'cell') / unit_scale]
    ppermute x0 -> x28, waiting for transfers between devices: none -> 82.8 us  [the longest x7 32.6 us: swap_side(): return lax.ppermute(x, 'snap', [(i, i ^ 2) for i in range(places)])]
    all_gather x2 -> x0, waiting for transfers between devices: 47.1 us -> none  [local(): lax.all_gather(outgoing, 'snap', axis=0, tiled=True)]
    ppermute x0 -> x28, starting transfers between devices: none -> 25.1 us  [the longest x6 9.28 us: swap_cell(): return lax.ppermute(x, ('cell', 'snap'), perm)]
    dot_general x5 -> x0, matrix products: 13.8 us -> none  [the longest x3 7.05 us: scattered_section(): jnp.dot(snapshots, z_input, precision=high, preferred_element_type=jnp.fl...]
    pallas_call x0 -> x9, Pallas kernels: none -> 9.7 us  [call(): pl.pallas_call(kernel, out_shape=[jax.ShapeDtypeStruct(shape, dtype) for...]
  transfers between devices with their start and end apart: 7 -> 28, of which waited for: 7 -> 20; matrix products, arithmetic and copies ran while one was open for 0% -> 4% of each run, Pallas kernels for 0% -> 3%
where the time goes in v2:
time: 129 us
  waiting for transfers between devices  82.8 us (64%)
  starting transfers between devices  25.1 us (19%)
  Pallas kernels  9.7 us (8%)
  local copies, waits for them, and re-layouts  6.75 us (5%)
  other arithmetic  3.62 us (3%)
    ppermute x7, waiting for transfers between devices, swap_side(): return lax.ppermute(x, 'snap', [(i, i ^ 2) for i in range(places)])  32.6 us
    ppermute x7, waiting for transfers between devices, swap_pair(): return lax.ppermute(x, 'snap', [(i, i ^ 4) for i in range(places)])  25.2 us
    ppermute x6, waiting for transfers between devices, swap_cell(): return lax.ppermute(x, ('cell', 'snap'), perm)  23.7 us
    pallas_call x9, Pallas kernels, call(): pl.pallas_call(kernel, out_shape=[jax.ShapeDtypeStruct(shape, dtype) for...  9.7 us
    ppermute x6, starting transfers between devices, swap_cell(): return lax.ppermute(x, ('cell', 'snap'), perm)  9.28 us
    ppermute x7, starting transfers between devices, swap_pair(): return lax.ppermute(x, 'snap', [(i, i ^ 4) for i in range(places)])  7.84 us
    ppermute x7, starting transfers between devices, swap_side(): return lax.ppermute(x, 'snap', [(i, i ^ 2) for i in range(places)])  7.16 us
    unnamed x24, local copies, waits for them, and re-layouts  2.74 us
  transfers between devices with their start and end apart: 28, of which 20 were waited for; matrix products, arithmetic and copies ran while one was open for 4% of the time, Pallas kernels for 3%

profile of v2, /device:TPU:0, one launch (start us, length us, event | category | flops | bytes accessed | tf_op | source)
XLA Modules:
  0.0 129.0 jit_solution(7660721932811995075)
XLA Ops:
  0.6 0.5 collective-permute-start.2
  1.1 1.0 constant_dynamic-slice_fusion.5
  2.1 0.1 collective-permute-start
  2.3 1.3 fusion.16
  3.5 3.1 %collective-permute-start.3 = (f32[256,256]{1,0:T(8,128)S(1)}, f32[256,256]{1,0:T(8,128)S(1)}, u32[]{:S(2)}, u32[]{:S(2)}) collective-permute-start(f32[256,256]{1,0:T(8,128)S(1)} %get-tuple-element.53.own_ref), channel_id=1, source_target_pairs={{0,2},{1,3},{2,0},{3,1},{4,6},{5,7},{6,4},{7,5},{8,10},{9,11},{10,... | collective-permute-start | bytes 786440 | tf_op jit(solution)/shard_map/ppermute | solution.py:166
  6.7 1.9 %collective-permute-start.7 = (f32[256,256]{1,0:T(8,128)S(1)}, f32[256,256]{1,0:T(8,128)S(1)}, u32[]{:S(2)}, u32[]{:S(2)}) collective-permute-start(f32[256,256]{1,0:T(8,128)S(1)} %get-tuple-element.54.own_ref), channel_id=1, source_target_pairs={{0,2},{1,3},{2,0},{3,1},{4,6},{5,7},{6,4},{7,5},{8,10},{9,11},{10,... | collective-permute-start | bytes 786440 | tf_op jit(solution)/shard_map/ppermute | solution.py:166
  8.7 5.0 %collective-permute-done.3.side_ref = f32[256,256]{1,0:T(8,128)S(1)} collective-permute-done((f32[256,256]{1,0:T(8,128)S(1)}, f32[256,256]{1,0:T(8,128)S(1)}, u32[]{:S(2)}, u32[]{:S(2)}) %collective-permute-start.3) | collective-permute-done | bytes 262176 | tf_op jit(solution)/shard_map/ppermute | solution.py:166
  13.7 5.6 %collective-permute-done.5.side_ref = f32[256,256]{1,0:T(8,128)S(1)} collective-permute-done((f32[256,256]{1,0:T(8,128)S(1)}, f32[256,256]{1,0:T(8,128)S(1)}, u32[]{:S(2)}, u32[]{:S(2)}) %collective-permute-start.5) | collective-permute-done | bytes 262176 | tf_op jit(solution)/shard_map/ppermute | solution.py:166
  19.4 5.6 %collective-permute-done.7.side_ref = f32[256,256]{1,0:T(8,128)S(1)} collective-permute-done((f32[256,256]{1,0:T(8,128)S(1)}, f32[256,256]{1,0:T(8,128)S(1)}, u32[]{:S(2)}, u32[]{:S(2)}) %collective-permute-start.7) | collective-permute-done | bytes 262176 | tf_op jit(solution)/shard_map/ppermute | solution.py:166
  25.0 5.1 %collective-permute-done.9.side_ref = f32[256,256]{1,0:T(8,128)} collective-permute-done((f32[256,256]{1,0:T(8,128)S(1)}, f32[256,256]{1,0:T(8,128)}, u32[]{:S(2)}, u32[]{:S(2)}) %collective-permute-start.9) | collective-permute-done | bytes 262176 | tf_op jit(solution)/shard_map/ppermute | solution.py:166
  30.2 0.7 shard_map.49
  30.9 1.8 %collective-permute-start.1 = (f32[64,512]{1,0:T(8,128)S(1)}, f32[64,512]{1,0:T(8,128)S(1)}, u32[]{:S(2)}, u32[]{:S(2)}) collective-permute-start(f32[64,512]{1,0:T(8,128)S(1)} %get-tuple-element.25), channel_id=1, source_target_pairs={{0,2},{1,3},{2,0},{3,1},{4,6},{5,7},{6,4},{7,5},{8,10},{9,11},{10,... | collective-permute-start | bytes 393224 | tf_op jit(solution)/shard_map/ppermute | solution.py:166
  32.7 1.3 fusion.15
  34.0 2.9 %collective-permute-done.1.far_ref = f32[64,512]{1,0:T(8,128)S(1)} collective-permute-done((f32[64,512]{1,0:T(8,128)S(1)}, f32[64,512]{1,0:T(8,128)S(1)}, u32[]{:S(2)}, u32[]{:S(2)}) %collective-permute-start.1) | collective-permute-done | bytes 131104 | tf_op jit(solution)/shard_map/ppermute | solution.py:166
  36.9 0.5 shard_map.50
  37.3 2.8 %collective-permute-start.11 = (f32[128,128]{1,0:T(8,128)S(1)}, f32[128,128]{1,0:T(8,128)S(1)}, u32[]{:S(2)}, u32[]{:S(2)}) collective-permute-start(f32[128,128]{1,0:T(8,128)S(1)} %get-tuple-element.26.refs_0_), channel_id=1, source_target_pairs={{0,4},{1,5},{2,6},{3,7},{4,0},{5,1},{6,2},{7,3},{8,12},{9,13},{10,... | collective-permute-start | bytes 196616 | tf_op jit(solution)/shard_map/ppermute | solution.py:170
  40.2 0.5 shard_map.51
  40.6 0.5 collective-permute-start.12
  41.2 0.5 shard_map.52
  41.7 2.5 %collective-permute-start.13 = (f32[128,128]{1,0:T(8,128)S(1)}, f32[128,128]{1,0:T(8,128)S(1)}, u32[]{:S(2)}, u32[]{:S(2)}) collective-permute-start(f32[128,128]{1,0:T(8,128)S(1)} %get-tuple-element.28.refs_2_), channel_id=1, source_target_pairs={{0,4},{1,5},{2,6},{3,7},{4,0},{5,1},{6,2},{7,3},{8,12},{9,13},{10,... | collective-permute-start | bytes 196616 | tf_op jit(solution)/shard_map/ppermute | solution.py:170
  44.2 1.4 %shard_map.53 = (f32[128,128]{1,0:T(8,128)S(1)}, bf16[256,1024]{1,0:T(8,128)(2,1)S(1)}, bf16[256,1024]{1,0:T(8,128)(2,1)S(1)}) custom-call(f32[64,512]{1,0:T(8,128)S(1)} %get-tuple-element.24.near_ref, f32[64,512]{1,0:T(8,128)S(1)} %collective-permute-done.1.far_ref, f32[256,256]{1,0:T(8,128)S(1)} %get-tuple-element.51.own_ref, ...), custom_call_target="tpu_custom_call" | custom-call | tf_op jit(solution)/shard_map/pallas_call | solution.py:135
  45.6 0.5 collective-permute-start.14
  46.2 2.8 %collective-permute-done.12.refs_5_ = f32[128,128]{1,0:T(8,128)S(1)} collective-permute-done((f32[128,128]{1,0:T(8,128)S(1)}, f32[128,128]{1,0:T(8,128)S(1)}, u32[]{:S(2)}, u32[]{:S(2)}) %collective-permute-start.12) | collective-permute-done | bytes 65568 | tf_op jit(solution)/shard_map/ppermute | solution.py:170
  48.9 2.1 %collective-permute-done.13.refs_6_ = f32[128,128]{1,0:T(8,128)S(1)} collective-permute-done((f32[128,128]{1,0:T(8,128)S(1)}, f32[128,128]{1,0:T(8,128)S(1)}, u32[]{:S(2)}, u32[]{:S(2)}) %collective-permute-start.13) | collective-permute-done | bytes 65568 | tf_op jit(solution)/shard_map/ppermute | solution.py:170
  51.0 1.4 %collective-permute-done.14.refs_7_ = f32[128,128]{1,0:T(8,128)S(1)} collective-permute-done((f32[128,128]{1,0:T(8,128)S(1)}, f32[128,128]{1,0:T(8,128)S(1)}, u32[]{:S(2)}, u32[]{:S(2)}) %collective-permute-start.14) | collective-permute-done | bytes 65568 | tf_op jit(solution)/shard_map/ppermute | solution.py:170
  52.4 0.8 shard_map.54
  53.2 1.6 %collective-permute-start.15 = (f32[520,128]{1,0:T(8,128)S(1)}, f32[520,128]{1,0:T(8,128)S(1)}, u32[]{:S(2)}, u32[]{:S(2)}) collective-permute-start(f32[520,128]{1,0:T(8,128)S(1)} %shard_map.54), channel_id=1, source_target_pairs={{0,8},{1,17},{2,10},{3,19},{4,12},{5,21},{6,14},{7,23},{8,0},{9,25... | collective-permute-start | bytes 798728 | tf_op jit(solution)/shard_map/ppermute | solution.py:178
  54.8 4.9 %collective-permute-done.15 = f32[520,128]{1,0:T(8,128)S(1)} collective-permute-done((f32[520,128]{1,0:T(8,128)S(1)}, f32[520,128]{1,0:T(8,128)S(1)}, u32[]{:S(2)}, u32[]{:S(2)}) %collective-permute-start.15) | collective-permute-done | bytes 266272 | tf_op jit(solution)/shard_map/ppermute | solution.py:178
  59.7 1.6 %collective-permute-start.16 = (f32[520,128]{1,0:T(8,128)S(1)}, f32[520,128]{1,0:T(8,128)S(1)}, u32[]{:S(2)}, u32[]{:S(2)}) collective-permute-start(f32[520,128]{1,0:T(8,128)S(1)} %add.68.refs_0_), channel_id=1, source_target_pairs={{0,16},{1,9},{2,18},{3,11},{4,20},{5,13},{6,22},{7,15},{8,24},{9,1... | collective-permute-start | bytes 798728 | tf_op jit(solution)/shard_map/ppermute | solution.py:178
  61.3 4.9 %collective-permute-done.16.refs_1_ = f32[520,128]{1,0:T(8,128)S(1)} collective-permute-done((f32[520,128]{1,0:T(8,128)S(1)}, f32[520,128]{1,0:T(8,128)S(1)}, u32[]{:S(2)}, u32[]{:S(2)}) %collective-permute-start.16) | collective-permute-done | bytes 266272 | tf_op jit(solution)/shard_map/ppermute | solution.py:178
  66.2 2.0 %shard_map.55 = (f32[520,128]{1,0:T(8,128)S(1)}, f32[8,128]{1,0:T(8,128)S(1)}, f32[512,128]{1,0:T(8,128)}) custom-call(f32[520,128]{1,0:T(8,128)S(1)} %add.68.refs_0_, f32[520,128]{1,0:T(8,128)S(1)} %collective-permute-done.16.refs_1_, bf16[256,1024]{1,0:T(8,128)(2,1)S(1)} %get-tuple-element.30.refs_8_.refs_2_, ...), custom_call_target="tpu_custom_call" | custom-call | tf_op jit(solution)/shard_map/pallas_call | solution.py:135
  68.2 11.6 %collective-permute-done.17.refs_1_ = f32[520,128]{1,0:T(8,128)S(1)} collective-permute-done((f32[520,128]{1,0:T(8,128)S(1)}, f32[520,128]{1,0:T(8,128)S(1)}, u32[]{:S(2)}, u32[]{:S(2)}) %collective-permute-start.17) | collective-permute-done | bytes 266272 | tf_op jit(solution)/shard_map/ppermute | solution.py:170
  79.8 0.9 shard_map.56
  80.7 1.6 %collective-permute-start.18 = (f32[520,128]{1,0:T(8,128)S(1)}, f32[520,128]{1,0:T(8,128)S(1)}, u32[]{:S(2)}, u32[]{:S(2)}) collective-permute-start(f32[520,128]{1,0:T(8,128)S(1)} %get-tuple-element.39), channel_id=1, source_target_pairs={{0,8},{1,17},{2,10},{3,19},{4,12},{5,21},{6,14},{7,23},{8,0},{9,25... | collective-permute-start | bytes 798728 | tf_op jit(solution)/shard_map/ppermute | solution.py:178
  82.3 5.3 %collective-permute-done.18 = f32[520,128]{1,0:T(8,128)S(1)} collective-permute-done((f32[520,128]{1,0:T(8,128)S(1)}, f32[520,128]{1,0:T(8,128)S(1)}, u32[]{:S(2)}, u32[]{:S(2)}) %collective-permute-start.18) | collective-permute-done | bytes 266272 | tf_op jit(solution)/shard_map/ppermute | solution.py:178
  87.6 1.6 %collective-permute-start.19 = (f32[520,128]{1,0:T(8,128)S(1)}, f32[520,128]{1,0:T(8,128)}, u32[]{:S(2)}, u32[]{:S(2)}) collective-permute-start(f32[520,128]{1,0:T(8,128)S(1)} %add.69.refs_0_), channel_id=1, source_target_pairs={{0,16},{1,9},{2,18},{3,11},{4,20},{5,13},{6,22},{7,15},{8,24},{9,1... | collective-permute-start | bytes 798728 | tf_op jit(solution)/shard_map/ppermute | solution.py:178
  89.2 5.0 %collective-permute-done.19.refs_1_ = f32[520,128]{1,0:T(8,128)} collective-permute-done((f32[520,128]{1,0:T(8,128)S(1)}, f32[520,128]{1,0:T(8,128)}, u32[]{:S(2)}, u32[]{:S(2)}) %collective-permute-start.19) | collective-permute-done | bytes 266272 | tf_op jit(solution)/shard_map/ppermute | solution.py:178
  94.2 1.0 copy-done.1
  95.3 1.0 copy-done.3
  96.3 2.4 %shard_map.57 = (f32[520,128]{1,0:T(8,128)S(1)}, f32[8,128]{1,0:T(8,128)S(1)}, f32[512,128]{1,0:T(8,128)S(1)}) custom-call(f32[520,128]{1,0:T(8,128)S(1)} %add.69.refs_0_, f32[520,128]{1,0:T(8,128)} %collective-permute-done.19.refs_1_, bf16[256,1024]{1,0:T(8,128)(2,1)S(1)} %get-tuple-element.30.refs_8_.refs_2_, ...), custom_call_target="tpu_custom_call" | custom-call | tf_op jit(solution)/shard_map/pallas_call | solution.py:135
  98.9 0.5 copy-done.6
  99.5 1.4 %collective-permute-start.20 = (f32[264,128]{1,0:T(8,128)S(1)}, f32[264,128]{1,0:T(8,128)S(1)}, u32[]{:S(2)}, u32[]{:S(2)}) collective-permute-start(f32[264,128]{1,0:T(8,128)S(1)} %pad_maximum_fusion.2), channel_id=1, source_target_pairs={{0,4},{1,5},{2,6},{3,7},{4,0},{5,1},{6,2},{7,3},{8,12},{9,13},{10,... | collective-permute-start | bytes 405512 | tf_op jit(solution)/shard_map/ppermute | solution.py:170
  100.9 2.9 %collective-permute-done.26 = f32[256,128]{1,0:T(8,128)S(1)} collective-permute-done((f32[256,128]{1,0:T(8,128)S(1)}, f32[256,128]{1,0:T(8,128)S(1)}, u32[]{:S(2)}, u32[]{:S(2)}) %collective-permute-start.26) | collective-permute-done | bytes 131104 | tf_op jit(solution)/shard_map/ppermute | solution.py:166
  103.9 0.1 copy.7
  104.0 0.1 copy.6
  104.1 2.9 %collective-permute-done.20 = f32[264,128]{1,0:T(8,128)S(1)} collective-permute-done((f32[264,128]{1,0:T(8,128)S(1)}, f32[264,128]{1,0:T(8,128)S(1)}, u32[]{:S(2)}, u32[]{:S(2)}) %collective-permute-start.20) | collective-permute-done | bytes 135200 | tf_op jit(solution)/shard_map/ppermute | solution.py:170
  107.0 0.7 fusion.13
  107.7 0.1 copy.5
  107.9 0.2 multiply_reduce_fusion
  108.2 0.1 collective-permute-start.21
  108.3 0.1 pad_maximum_fusion.3
  108.4 5.5 %collective-permute-done.21 = f32[64,384]{0,1:T(8,128)S(1)} collective-permute-done((f32[64,384]{0,1:T(8,128)S(1)}, f32[64,384]{0,1:T(8,128)S(1)}, u32[]{:S(2)}, u32[]{:S(2)}) %collective-permute-start.21) | collective-permute-done | bytes 98336 | tf_op jit(solution)/shard_map/ppermute | solution.py:166
  113.9 0.1 fusion.3
  114.1 0.1 pad_maximum_fusion.6
  114.3 1.3 %collective-permute-done.22 = f32[128,256]{0,1:T(8,128)S(1)} collective-permute-done((f32[128,256]{0,1:T(8,128)S(1)}, f32[128,256]{0,1:T(8,128)S(1)}, u32[]{:S(2)}, u32[]{:S(2)}) %collective-permute-start.22) | collective-permute-done | bytes 131104 | tf_op jit(solution)/shard_map/ppermute | solution.py:163
  115.6 0.1 fusion.9
  115.8 4.5 %collective-permute-done.23 = f32[5,256]{1,0:T(8,128)S(1)} collective-permute-done((f32[5,256]{1,0:T(8,128)S(1)}, f32[5,256]{1,0:T(8,128)S(1)}, u32[]{:S(2)}, u32[]{:S(2)}) %collective-permute-start.23) | collective-permute-done | bytes 5152 | tf_op jit(solution)/shard_map/ppermute | solution.py:170
  120.4 1.5 %collective-permute-start.24 = (f32[5,256]{1,0:T(8,128)S(1)}, f32[5,256]{1,0:T(8,128)S(1)}, u32[]{:S(2)}, u32[]{:S(2)}) collective-permute-start(f32[5,256]{1,0:T(8,128)S(1)} %slice_add_fusion.3), channel_id=1, source_target_pairs={{0,8},{1,17},{2,10},{3,19},{4,12},{5,21},{6,14},{7,23},{8,0},{9,25... | collective-permute-start | bytes 15368 | tf_op jit(solution)/shard_map/ppermute | solution.py:178
  121.9 2.2 %collective-permute-done.24 = f32[5,256]{1,0:T(8,128)S(1)} collective-permute-done((f32[5,256]{1,0:T(8,128)S(1)}, f32[5,256]{1,0:T(8,128)S(1)}, u32[]{:S(2)}, u32[]{:S(2)}) %collective-permute-start.24) | collective-permute-done | bytes 5152 | tf_op jit(solution)/shard_map/ppermute | solution.py:178
  124.0 1.5 %collective-permute-start.25 = (f32[5,256]{1,0:T(8,128)S(1)}, f32[5,256]{1,0:T(8,128)S(1)}, u32[]{:S(2)}, u32[]{:S(2)}) collective-permute-start(f32[5,256]{1,0:T(8,128)S(1)} %add.79), channel_id=1, source_target_pairs={{0,16},{1,9},{2,18},{3,11},{4,20},{5,13},{6,22},{7,15},{8,24},{9,1... | collective-permute-start | bytes 15368 | tf_op jit(solution)/shard_map/ppermute | solution.py:178
  125.5 0.7 fusion
  126.3 1.4 %collective-permute-done.25 = f32[5,256]{1,0:T(8,128)S(1)} collective-permute-done((f32[5,256]{1,0:T(8,128)S(1)}, f32[5,256]{1,0:T(8,128)S(1)}, u32[]{:S(2)}, u32[]{:S(2)}) %collective-permute-start.25) | collective-permute-done | bytes 5152 | tf_op jit(solution)/shard_map/ppermute | solution.py:178
  127.7 0.7 fusion.7
  128.4 0.6 pad_maximum_fusion.7
  (70 shorter events, 1.0 us)
Async XLA Ops:
  0.6 30.2 %collective-permute-start.2 = (f32[1024,256]{1,0:T(8,128)}, f32[1024,256]{1,0:T(8,128)}, u32[]{:S(2)}, u32[]{:S(2)}) collective-permute-start(f32[1024,256]{1,0:T(8,128)} %param.2), channel_id=1, source_target_pairs={{0,1},{1,0},{2,3},{3,2},{4,5},{5,4},{6,7},{7,6},{8,9},{9,8},{10,11... | collective-permute-start | bytes 3145736 | tf_op jit(solution)/shard_map/ppermute | solution.py:163
  2.1 6.5 %collective-permute-start = (f32[256,128]{1,0:T(8,128)S(1)}, f32[256,128]{1,0:T(8,128)S(1)}, u32[]{:S(2)}, u32[]{:S(2)}) collective-permute-start(f32[256,128]{1,0:T(8,128)S(1)} %get-tuple-element.65), channel_id=1, source_target_pairs={{0,1},{1,0},{2,3},{3,2},{4,5},{5,4},{6,7},{7,6},{8,9},{9,8},{10,11... | collective-permute-start | bytes 393224 | tf_op jit(solution)/shard_map/ppermute | solution.py:163
  3.5 30.4 %copy-start.4 = (f32[256,256]{1,0:T(8,128)}, f32[256,256]{1,0:T(8,128)S(1)}, u32[]{:S(2)}) copy-start(f32[256,256]{1,0:T(8,128)S(1)} %get-tuple-element.54.own_ref) | copy-start | bytes 786436
  3.5 10.2 %collective-permute-start.3 = (f32[256,256]{1,0:T(8,128)S(1)}, f32[256,256]{1,0:T(8,128)S(1)}, u32[]{:S(2)}, u32[]{:S(2)}) collective-permute-start(f32[256,256]{1,0:T(8,128)S(1)} %get-tuple-element.53.own_ref), channel_id=1, source_target_pairs={{0,2},{1,3},{2,0},{3,1},{4,6},{5,7},{6,4},{7,5},{8,10},{9,11},{10,... | collective-permute-start | bytes 786440 | tf_op jit(solution)/shard_map/ppermute | solution.py:166
  6.6 12.7 %collective-permute-start.5 = (f32[256,256]{1,0:T(8,128)S(1)}, f32[256,256]{1,0:T(8,128)S(1)}, u32[]{:S(2)}, u32[]{:S(2)}) collective-permute-start(f32[256,256]{1,0:T(8,128)S(1)} %get-tuple-element.52.own_ref), channel_id=1, source_target_pairs={{0,2},{1,3},{2,0},{3,1},{4,6},{5,7},{6,4},{7,5},{8,10},{9,11},{10,... | collective-permute-start | bytes 786440 | tf_op jit(solution)/shard_map/ppermute | solution.py:166
  6.7 18.3 %collective-permute-start.7 = (f32[256,256]{1,0:T(8,128)S(1)}, f32[256,256]{1,0:T(8,128)S(1)}, u32[]{:S(2)}, u32[]{:S(2)}) collective-permute-start(f32[256,256]{1,0:T(8,128)S(1)} %get-tuple-element.54.own_ref), channel_id=1, source_target_pairs={{0,2},{1,3},{2,0},{3,1},{4,6},{5,7},{6,4},{7,5},{8,10},{9,11},{10,... | collective-permute-start | bytes 786440 | tf_op jit(solution)/shard_map/ppermute | solution.py:166
  8.7 21.4 %collective-permute-start.9 = (f32[256,256]{1,0:T(8,128)S(1)}, f32[256,256]{1,0:T(8,128)}, u32[]{:S(2)}, u32[]{:S(2)}) collective-permute-start(f32[256,256]{1,0:T(8,128)S(1)} %get-tuple-element.51.own_ref), channel_id=1, source_target_pairs={{0,2},{1,3},{2,0},{3,1},{4,6},{5,7},{6,4},{7,5},{8,10},{9,11},{10,... | collective-permute-start | bytes 786440 | tf_op jit(solution)/shard_map/ppermute | solution.py:166
  13.7 23.1 %collective-permute-start.4 = (f32[256,256]{1,0:T(8,128)S(1)}, f32[256,256]{1,0:T(8,128)S(1)}, u32[]{:S(2)}, u32[]{:S(2)}) collective-permute-start(f32[256,256]{1,0:T(8,128)S(1)} %collective-permute-done.3.side_ref), channel_id=1, source_target_pairs={{0,1},{1,0},{2,3},{3,2},{4,5},{5,4},{6,7},{7,6},{8,9},{9,8},{10,11... | collective-permute-start | bytes 786440 | tf_op jit(solution)/shard_map/ppermute | solution.py:163
  19.4 14.6 %copy-start.9 = (f32[256,256]{1,0:T(8,128)}, f32[256,256]{1,0:T(8,128)S(1)}, u32[]{:S(2)}) copy-start(f32[256,256]{1,0:T(8,128)S(1)} %collective-permute-done.5.side_ref) | copy-start | bytes 786436
  19.4 20.8 %collective-permute-start.6 = (f32[256,256]{1,0:T(8,128)S(1)}, f32[256,256]{1,0:T(8,128)S(1)}, u32[]{:S(2)}, u32[]{:S(2)}) collective-permute-start(f32[256,256]{1,0:T(8,128)S(1)} %collective-permute-done.5.side_ref), channel_id=1, source_target_pairs={{0,1},{1,0},{2,3},{3,2},{4,5},{5,4},{6,7},{7,6},{8,9},{9,8},{10,11... | collective-permute-start | bytes 786440 | tf_op jit(solution)/shard_map/ppermute | solution.py:163
  25.0 9.0 %copy-start.7 = (f32[256,256]{1,0:T(8,128)}, f32[256,256]{1,0:T(8,128)S(1)}, u32[]{:S(2)}) copy-start(f32[256,256]{1,0:T(8,128)S(1)} %collective-permute-done.7.side_ref) | copy-start | bytes 786436
  25.0 16.1 %collective-permute-start.8 = (f32[256,256]{1,0:T(8,128)S(1)}, f32[256,256]{1,0:T(8,128)S(1)}, u32[]{:S(2)}, u32[]{:S(2)}) collective-permute-start(f32[256,256]{1,0:T(8,128)S(1)} %collective-permute-done.7.side_ref), channel_id=1, source_target_pairs={{0,1},{1,0},{2,3},{3,2},{4,5},{5,4},{6,7},{7,6},{8,9},{9,8},{10,11... | collective-permute-start | bytes 786440 | tf_op jit(solution)/shard_map/ppermute | solution.py:163
  30.1 14.1 %collective-permute-start.10 = (f32[256,256]{1,0:T(8,128)}, f32[256,256]{1,0:T(8,128)S(1)}, u32[]{:S(2)}, u32[]{:S(2)}) collective-permute-start(f32[256,256]{1,0:T(8,128)} %collective-permute-done.9.side_ref), channel_id=1, source_target_pairs={{0,1},{1,0},{2,3},{3,2},{4,5},{5,4},{6,7},{7,6},{8,9},{9,8},{10,11... | collective-permute-start | bytes 786440 | tf_op jit(solution)/shard_map/ppermute | solution.py:163
  30.9 6.0 %collective-permute-start.1 = (f32[64,512]{1,0:T(8,128)S(1)}, f32[64,512]{1,0:T(8,128)S(1)}, u32[]{:S(2)}, u32[]{:S(2)}) collective-permute-start(f32[64,512]{1,0:T(8,128)S(1)} %get-tuple-element.25), channel_id=1, source_target_pairs={{0,2},{1,3},{2,0},{3,1},{4,6},{5,7},{6,4},{7,5},{8,10},{9,11},{10,... | collective-permute-start | bytes 393224 | tf_op jit(solution)/shard_map/ppermute | solution.py:166
  36.9 3.3 %copy-start.10 = (f32[256,256]{1,0:T(8,128)S(1)}, f32[256,256]{1,0:T(8,128)}, u32[]{:S(2)}) copy-start(f32[256,256]{1,0:T(8,128)} %copy-done.9) | copy-start | bytes 786436
  37.3 8.8 %collective-permute-start.11 = (f32[128,128]{1,0:T(8,128)S(1)}, f32[128,128]{1,0:T(8,128)S(1)}, u32[]{:S(2)}, u32[]{:S(2)}) collective-permute-start(f32[128,128]{1,0:T(8,128)S(1)} %get-tuple-element.26.refs_0_), channel_id=1, source_target_pairs={{0,4},{1,5},{2,6},{3,7},{4,0},{5,1},{6,2},{7,3},{8,12},{9,13},{10,... | collective-permute-start | bytes 196616 | tf_op jit(solution)/shard_map/ppermute | solution.py:170
  40.2 1.0 copy-start.5
  40.2 1.0 copy-start.8
  40.6 8.3 %collective-permute-start.12 = (f32[128,128]{1,0:T(8,128)S(1)}, f32[128,128]{1,0:T(8,128)S(1)}, u32[]{:S(2)}, u32[]{:S(2)}) collective-permute-start(f32[128,128]{1,0:T(8,128)S(1)} %get-tuple-element.27.refs_1_), channel_id=1, source_target_pairs={{0,4},{1,5},{2,6},{3,7},{4,0},{5,1},{6,2},{7,3},{8,12},{9,13},{10,... | collective-permute-start | bytes 196616 | tf_op jit(solution)/shard_map/ppermute | solution.py:170
  41.7 9.3 %collective-permute-start.13 = (f32[128,128]{1,0:T(8,128)S(1)}, f32[128,128]{1,0:T(8,128)S(1)}, u32[]{:S(2)}, u32[]{:S(2)}) collective-permute-start(f32[128,128]{1,0:T(8,128)S(1)} %get-tuple-element.28.refs_2_), channel_id=1, source_target_pairs={{0,4},{1,5},{2,6},{3,7},{4,0},{5,1},{6,2},{7,3},{8,12},{9,13},{10,... | collective-permute-start | bytes 196616 | tf_op jit(solution)/shard_map/ppermute | solution.py:170
  45.6 34.2 %copy-start = (bf16[256,1024]{1,0:T(8,128)(2,1)}, bf16[256,1024]{1,0:T(8,128)(2,1)S(1)}, u32[]{:S(2)}) copy-start(bf16[256,1024]{1,0:T(8,128)(2,1)S(1)} %get-tuple-element.33.refs_11_.refs_5_) | copy-start | bytes 1572868
  45.6 34.2 %copy-start.2 = (bf16[256,1024]{1,0:T(8,128)(2,1)}, bf16[256,1024]{1,0:T(8,128)(2,1)S(1)}, u32[]{:S(2)}) copy-start(bf16[256,1024]{1,0:T(8,128)(2,1)S(1)} %get-tuple-element.37.refs_15_.refs_9_) | copy-start | bytes 1572868
  45.6 6.7 %collective-permute-start.14 = (f32[128,128]{1,0:T(8,128)S(1)}, f32[128,128]{1,0:T(8,128)S(1)}, u32[]{:S(2)}, u32[]{:S(2)}) collective-permute-start(f32[128,128]{1,0:T(8,128)S(1)} %get-tuple-element.29.refs_3_), channel_id=1, source_target_pairs={{0,4},{1,5},{2,6},{3,7},{4,0},{5,1},{6,2},{7,3},{8,12},{9,13},{10,... | collective-permute-start | bytes 196616 | tf_op jit(solution)/shard_map/ppermute | solution.py:170
  53.2 6.5 %collective-permute-start.15 = (f32[520,128]{1,0:T(8,128)S(1)}, f32[520,128]{1,0:T(8,128)S(1)}, u32[]{:S(2)}, u32[]{:S(2)}) collective-permute-start(f32[520,128]{1,0:T(8,128)S(1)} %shard_map.54), channel_id=1, source_target_pairs={{0,8},{1,17},{2,10},{3,19},{4,12},{5,21},{6,14},{7,23},{8,0},{9,25... | collective-permute-start | bytes 798728 | tf_op jit(solution)/shard_map/ppermute | solution.py:178
  59.7 6.5 %collective-permute-start.16 = (f32[520,128]{1,0:T(8,128)S(1)}, f32[520,128]{1,0:T(8,128)S(1)}, u32[]{:S(2)}, u32[]{:S(2)}) collective-permute-start(f32[520,128]{1,0:T(8,128)S(1)} %add.68.refs_0_), channel_id=1, source_target_pairs={{0,16},{1,9},{2,18},{3,11},{4,20},{5,13},{6,22},{7,15},{8,24},{9,1... | collective-permute-start | bytes 798728 | tf_op jit(solution)/shard_map/ppermute | solution.py:178
  68.2 11.6 %collective-permute-start.17 = (f32[520,128]{1,0:T(8,128)S(1)}, f32[520,128]{1,0:T(8,128)S(1)}, u32[]{:S(2)}, u32[]{:S(2)}) collective-permute-start(f32[520,128]{1,0:T(8,128)S(1)} %get-tuple-element.38.refs_0_), channel_id=1, source_target_pairs={{0,4},{1,5},{2,6},{3,7},{4,0},{5,1},{6,2},{7,3},{8,12},{9,13},{10,... | collective-permute-start | bytes 798728 | tf_op jit(solution)/shard_map/ppermute | solution.py:170
  80.7 6.9 %collective-permute-start.18 = (f32[520,128]{1,0:T(8,128)S(1)}, f32[520,128]{1,0:T(8,128)S(1)}, u32[]{:S(2)}, u32[]{:S(2)}) collective-permute-start(f32[520,128]{1,0:T(8,128)S(1)} %get-tuple-element.39), channel_id=1, source_target_pairs={{0,8},{1,17},{2,10},{3,19},{4,12},{5,21},{6,14},{7,23},{8,0},{9,25... | collective-permute-start | bytes 798728 | tf_op jit(solution)/shard_map/ppermute | solution.py:178
  87.6 6.6 %collective-permute-start.19 = (f32[520,128]{1,0:T(8,128)S(1)}, f32[520,128]{1,0:T(8,128)}, u32[]{:S(2)}, u32[]{:S(2)}) collective-permute-start(f32[520,128]{1,0:T(8,128)S(1)} %add.69.refs_0_), channel_id=1, source_target_pairs={{0,16},{1,9},{2,18},{3,11},{4,20},{5,13},{6,22},{7,15},{8,24},{9,1... | collective-permute-start | bytes 798728 | tf_op jit(solution)/shard_map/ppermute | solution.py:178
  94.2 1.0 copy-start.1
  95.3 1.0 copy-start.3
  98.7 0.7 copy-start.6
  98.8 5.0 %collective-permute-start.26 = (f32[256,128]{1,0:T(8,128)S(1)}, f32[256,128]{1,0:T(8,128)S(1)}, u32[]{:S(2)}, u32[]{:S(2)}) collective-permute-start(f32[256,128]{1,0:T(8,128)S(1)} %slice.113), channel_id=1, source_target_pairs={{0,2},{1,3},{2,0},{3,1},{4,6},{5,7},{6,4},{7,5},{8,10},{9,11},{10,... | collective-permute-start | bytes 393224 | tf_op jit(solution)/shard_map/ppermute | solution.py:166
  99.5 7.5 %collective-permute-start.20 = (f32[264,128]{1,0:T(8,128)S(1)}, f32[264,128]{1,0:T(8,128)S(1)}, u32[]{:S(2)}, u32[]{:S(2)}) collective-permute-start(f32[264,128]{1,0:T(8,128)S(1)} %pad_maximum_fusion.2), channel_id=1, source_target_pairs={{0,4},{1,5},{2,6},{3,7},{4,0},{5,1},{6,2},{7,3},{8,12},{9,13},{10,... | collective-permute-start | bytes 405512 | tf_op jit(solution)/shard_map/ppermute | solution.py:170
  108.2 5.7 %collective-permute-start.21 = (f32[64,384]{0,1:T(8,128)S(1)}, f32[64,384]{0,1:T(8,128)S(1)}, u32[]{:S(2)}, u32[]{:S(2)}) collective-permute-start(f32[64,384]{0,1:T(8,128)S(1)} %pad_maximum_fusion), channel_id=1, source_target_pairs={{0,2},{1,3},{2,0},{3,1},{4,6},{5,7},{6,4},{7,5},{8,10},{9,11},{10,... | collective-permute-start | bytes 294920 | tf_op jit(solution)/shard_map/ppermute | solution.py:166
  108.4 5.9 %collective-permute-start.27 = (f32[128,256]{0,1:T(8,128)S(1)}, f32[128,256]{0,1:T(8,128)S(1)}, u32[]{:S(2)}, u32[]{:S(2)}) collective-permute-start(f32[128,256]{0,1:T(8,128)S(1)} %pad_maximum_fusion.3), channel_id=1, source_target_pairs={{0,1},{1,0},{2,3},{3,2},{4,5},{5,4},{6,7},{7,6},{8,9},{9,8},{10,11... | collective-permute-start | bytes 393224 | tf_op jit(solution)/shard_map/ppermute | solution.py:163
  114.2 1.4 %collective-permute-start.22 = (f32[128,256]{0,1:T(8,128)S(1)}, f32[128,256]{0,1:T(8,128)S(1)}, u32[]{:S(2)}, u32[]{:S(2)}) collective-permute-start(f32[128,256]{0,1:T(8,128)S(1)} %get-tuple-element.45), channel_id=1, source_target_pairs={{0,1},{1,0},{2,3},{3,2},{4,5},{5,4},{6,7},{7,6},{8,9},{9,8},{10,11... | collective-permute-start | bytes 393224 | tf_op jit(solution)/shard_map/ppermute | solution.py:163
  115.7 10.5 %copy-start.11 = (f32[128,256]{1,0:T(8,128)}, f32[128,256]{1,0:T(8,128)S(1)}, u32[]{:S(2)}) copy-start(f32[128,256]{1,0:T(8,128)S(1)} %fusion.8) | copy-start | bytes 393220
  115.8 4.6 %collective-permute-start.23 = (f32[5,256]{1,0:T(8,128)S(1)}, f32[5,256]{1,0:T(8,128)S(1)}, u32[]{:S(2)}, u32[]{:S(2)}) collective-permute-start(f32[5,256]{1,0:T(8,128)S(1)} %slice.128), channel_id=1, source_target_pairs={{0,4},{1,5},{2,6},{3,7},{4,0},{5,1},{6,2},{7,3},{8,12},{9,13},{10,... | collective-permute-start | bytes 15368 | tf_op jit(solution)/shard_map/ppermute | solution.py:170
  120.4 3.7 %collective-permute-start.24 = (f32[5,256]{1,0:T(8,128)S(1)}, f32[5,256]{1,0:T(8,128)S(1)}, u32[]{:S(2)}, u32[]{:S(2)}) collective-permute-start(f32[5,256]{1,0:T(8,128)S(1)} %slice_add_fusion.3), channel_id=1, source_target_pairs={{0,8},{1,17},{2,10},{3,19},{4,12},{5,21},{6,14},{7,23},{8,0},{9,25... | collective-permute-start | bytes 15368 | tf_op jit(solution)/shard_map/ppermute | solution.py:178
  124.0 3.7 %collective-permute-start.25 = (f32[5,256]{1,0:T(8,128)S(1)}, f32[5,256]{1,0:T(8,128)S(1)}, u32[]{:S(2)}, u32[]{:S(2)}) collective-permute-start(f32[5,256]{1,0:T(8,128)S(1)} %add.79), channel_id=1, source_target_pairs={{0,16},{1,9},{2,18},{3,11},{4,20},{5,13},{6,22},{7,15},{8,24},{9,1... | collective-permute-start | bytes 15368 | tf_op jit(solution)/shard_map/ppermute | solution.py:178
  127.7 0.7 slice-start

commit v3 on v2

v3 whole, which is shorter than its diff:
```python
import functools

import jax
import jax.numpy as jnp
from jax import lax
from jax.experimental import pallas as pl
from jax.experimental.pallas import tpu as pltpu
from jax.sharding import PartitionSpec as P

ITERS = 2
EPS = 1e-05
LANES = 128
TILE = 8
PARTS = (2, 2, 2, 1, 1)
BF16 = jnp.bfloat16
F32 = jnp.float32


def split(x):
    high = x.astype(BF16).astype(F32)
    return high, x - high


def dot(a, b):
    return lax.dot_general(a, b, (((1,), (0,)), ((), ())), preferred_element_type=F32)


def eye(cols):
    shape = (cols, LANES)
    return lax.broadcasted_iota(jnp.int32, shape, 0) == lax.broadcasted_iota(jnp.int32, shape, 1)


def to_column(row, cols):
    return jnp.sum(jnp.where(eye(cols), row, 0.0), axis=1, keepdims=True)


def to_row(column):
    return jnp.sum(jnp.where(eye(column.shape[0]), column, 0.0), axis=0, keepdims=True)


def squares_row(x):
    return to_row(jnp.sum(x * x, axis=1, keepdims=True))


def rms(total, count):
    return jnp.sqrt(total / count + EPS)


def wide(x, cols):
    return jnp.concatenate([x[j * cols : (j + 1) * cols] for j in range(x.shape[0] // cols)], axis=1)


def store_blocks(ref, start, x):
    cols = x.shape[0]
    for j in range(x.shape[1] // LANES):
        ref[start + j * cols : start + (j + 1) * cols, :] = x[:, j * LANES : (j + 1) * LANES]


def turn(x, cols):
    return pltpu.roll(x, cols, 1)


def left(shape, cols):
    return lax.broadcasted_iota(jnp.int32, shape, 1) < cols


def fold_blocks(total, cols):
    flipped = total.T
    return flipped[:cols] + flipped[cols:]


def sketch_sides(x):
    cols = LANES // 2
    high, low = split(x)
    first = left(x.shape, cols)
    own = jnp.where(first, high, turn(low, cols))
    other = jnp.where(first, turn(high, cols), low)
    return own.astype(BF16), other.astype(BF16)


def prepare_kernel(place_ref, near_ref, got_ref, a_ref, mine_ref, theirs_ref, *refs):
    outs, sems = refs[:-1], refs[-1]
    start = a_ref.shape[0] - sum(out.shape[0] for out in outs)
    copies = []
    for i, out in enumerate(outs):
        copies.append(pltpu.make_async_copy(a_ref.at[pl.ds(start, out.shape[0])], out, sems.at[i]))
        start += out.shape[0]
        copies[-1].start()
    cols = LANES // 2
    near, got = near_ref[...], got_ref[...]
    first = left(near.shape, cols)
    low = jnp.where(first, near, turn(got, cols))
    high = jnp.where(first, turn(near, cols), got)
    zero = place_ref[1] == 0
    mine_ref[...] = jnp.where(zero, low, high)
    theirs_ref[...] = jnp.where(zero, high, low)
    for copy in copies:
        copy.wait()


def near_kernel(own_ref, core_ref, mine_ref, y_ref, high_ref, low_ref):
    width = own_ref.shape[1]
    cols = LANES // 2
    rhs = jnp.concatenate(sketch_sides(mine_ref[...]), axis=0)
    for b in range(own_ref.shape[0] // LANES):
        cut = slice(b * LANES, (b + 1) * LANES)
        for s, ref in enumerate((own_ref, core_ref)):
            high, low = split(ref[cut, :])
            high_ref[cut, s * width : (s + 1) * width] = high.astype(BF16)
            low_ref[cut, s * width : (s + 1) * width] = low.astype(BF16)
    for b in range(own_ref.shape[0] // LANES):
        cut = slice(b * LANES, (b + 1) * LANES)
        total = dot(high_ref[cut, :], rhs) + dot(low_ref[cut, :], rhs)
        y_ref[b * cols : (b + 1) * cols, :] = fold_blocks(total, cols)


def far_kernel(start, side_ref, diagonal_ref, far_ref, near_ref, y_ref, high_ref, low_ref):
    width = side_ref.shape[1]
    cols = LANES // 2
    rhs = jnp.concatenate(sketch_sides(far_ref[...]), axis=0)
    for s, ref in enumerate((side_ref, diagonal_ref)):
        high, low = split(ref[...])
        high_ref[:, s * width : (s + 1) * width] = high.astype(BF16)
        low_ref[:, s * width : (s + 1) * width] = low.astype(BF16)
    for b in range(side_ref.shape[0] // LANES):
        cut = slice(b * LANES, (b + 1) * LANES)
        total = dot(high_ref[cut, :], rhs) + dot(low_ref[cut, :], rhs)
        at = (start // LANES + b) * cols
        y_ref[b * cols : (b + 1) * cols, :] = fold_blocks(total, cols) + near_ref[at : at + cols, :]


def unfold(total):
    cols = total.shape[0] // 2
    return total[:cols] + total[cols:]


def send_z(y, high_refs, low_refs, z_ref):
    lhs = jnp.concatenate(split(y), axis=0).astype(BF16)
    near = dot(lhs, high_refs[0][...]) + dot(lhs, low_refs[0][...])
    far, at = None, 0
    for high_ref, low_ref in zip(high_refs[1:], low_refs[1:]):
        cut = slice(at, at + high_ref.shape[0])
        term = dot(lhs[:, cut], high_ref[...]) + dot(lhs[:, cut], low_ref[...])
        far = term if far is None else far + term
        at += high_ref.shape[0]
    near, far = unfold(near), unfold(far)
    store_blocks(z_ref, 0, near)
    store_blocks(z_ref, (z_ref.shape[0] - TILE) // 2, far)
    z_ref[-TILE:, :] = jnp.broadcast_to(squares_row(y), (TILE, LANES))


def first_z_kernel(*refs):
    count = len(PARTS)
    cols = LANES // 2
    own, got = refs[:count], refs[count : 2 * count]
    high, low = refs[2 * count : 3 * count + 1], refs[3 * count + 1 : 4 * count + 2]
    y = jnp.concatenate([wide(a[...] + b[...], cols) for a, b in zip(own, got)], axis=1)
    send_z(y, high, low, refs[-1])


def scaled(own_ref, got_ref, count):
    cols = LANES // 2
    total = own_ref[...] + got_ref[...]
    scale = rms(total[-TILE:], count)
    return wide(total[:-TILE], cols) / to_column(scale[:1], cols), scale


def z_kernel(count, *refs):
    own_ref, got_ref = refs[:2]
    parts = len(PARTS) + 1
    high, low = refs[2 : 2 + parts], refs[2 + parts : 2 + 2 * parts]
    z_ref, scale_ref = refs[-2:]
    y, scale = scaled(own_ref, got_ref, count)
    scale_ref[...] = scale
    send_z(y, high, low, z_ref)


def product_y(z, high_refs, low_refs):
    cols = z.shape[0]
    rhs = jnp.concatenate(split(z), axis=0).T.astype(BF16)
    middle = rhs.shape[0] // 2
    rows, at = [], 0
    for high_ref, low_ref in zip(high_refs[1:], low_refs[1:]):
        for b in range(high_ref.shape[0] // LANES):
            near = slice(at, at + LANES)
            far = slice(b * LANES, (b + 1) * LANES)
            total = dot(high_refs[0][near, :], rhs[:middle]) + dot(low_refs[0][near, :], rhs[:middle])
            total += dot(high_ref[far, :], rhs[middle:]) + dot(low_ref[far, :], rhs[middle:])
            rows.append(fold_blocks(total, cols))
            at += LANES
    return rows


def y_kernel(count, *refs):
    own_ref, got_ref = refs[:2]
    parts = len(PARTS) + 1
    high, low = refs[2 : 2 + parts], refs[2 + parts : 2 + 2 * parts]
    y_ref, scale_ref = refs[-2:]
    z, scale = scaled(own_ref, got_ref, count)
    scale_ref[...] = scale
    cols = z.shape[0]
    for j, block in enumerate(product_y(z, high, low)):
        y_ref[j * cols : (j + 1) * cols, :] = block
    y_ref[-TILE:, :] = jnp.broadcast_to(squares_row(z), (TILE, LANES))


def last_y_kernel(count, place_ref, *refs):
    own_ref, got_ref = refs[:2]
    parts = len(PARTS) + 1
    high, low = refs[2 : 2 + parts], refs[2 + parts : 2 + 2 * parts]
    keep_ref, send_ref, scale_ref, z_ref = refs[-4:]
    z, scale = scaled(own_ref, got_ref, count)
    scale_ref[...] = scale
    store_blocks(z_ref, 0, z)
    cols = z.shape[0]
    blocks = product_y(z, high, low)
    middle = len(blocks) // 2
    zero = place_ref[2] == 0
    for j in range(middle):
        cut = slice(j * cols, (j + 1) * cols)
        keep_ref[cut, :] = jnp.where(zero, blocks[j], blocks[middle + j])
        send_ref[cut, :] = jnp.where(zero, blocks[middle + j], blocks[j])
    tail = jnp.broadcast_to(squares_row(z), (TILE, LANES))
    keep_ref[-TILE:, :] = tail
    send_ref[-TILE:, :] = tail


def side_kernel(count, place_ref, keep_ref, got_ref, *refs):
    scales, (own_ref, send_ref) = refs[:-2], refs[-2:]
    y, scale = scaled(keep_ref, got_ref, count)
    row = lax.broadcasted_iota(jnp.int32, (TILE, LANES), 0)
    tail = jnp.broadcast_to(squares_row(y), (TILE, LANES))
    for i, known in enumerate([ref[...] for ref in scales] + [scale]):
        tail = jnp.where(row == i, known, tail)
    middle = y.shape[1] // 2
    zero = place_ref[1] == 0
    store_blocks(own_ref, 0, jnp.where(zero, y[:, :middle], y[:, middle:]))
    store_blocks(send_ref, 0, jnp.where(zero, y[:, middle:], y[:, :middle]))
    own_ref[-TILE:, :] = tail
    send_ref[-TILE:, :] = tail


def core_kernel(place_ref, own_ref, got_ref, keep_ref, send_ref):
    cols = LANES // 2
    zero_side, zero_core = place_ref[1] == 0, place_ref[0] == 0
    own, got = own_ref[...], got_ref[...]
    for s, x in enumerate((jnp.where(zero_side, own, got), jnp.where(zero_side, got, own))):
        first, second, tail = x[:cols], x[cols : 2 * cols], x[2 * cols :]
        keep_ref[s * cols : (s + 1) * cols, :] = jnp.where(zero_core, first, second)
        send_ref[s * cols : (s + 1) * cols, :] = jnp.where(zero_core, second, first)
        at = 2 * cols + s * TILE
        keep_ref[at : at + TILE, :] = tail
        send_ref[at : at + TILE, :] = tail


def join_kernel(place_ref, keep_ref, got_ref, y_ref, known_ref):
    cols = LANES // 2
    zero = place_ref[0] == 0
    keep, got = keep_ref[...], got_ref[...]
    first = left((TILE, LANES), cols)
    for s, x in enumerate((jnp.where(zero, keep, got), jnp.where(zero, got, keep))):
        cut = slice(s * LANES, (s + 1) * LANES)
        y_ref[:, cut] = x[:LANES].T
        known_ref[:, cut] = jnp.where(first, x[LANES : LANES + TILE], turn(x[LANES + TILE :], cols))


def z_out_kernel(place_ref, near_ref, got_ref, core_ref, known_ref, z_ref):
    cols = LANES // 2
    zero_side, zero_core = place_ref[1] == 0, place_ref[0] == 0

    def side_order(own, other):
        pairs = [wide(jnp.where(zero_side, a, b), cols) for a, b in ((own, other), (other, own))]
        return jnp.concatenate(pairs, axis=0)

    middle = core_ref.shape[0] // 2
    mine = side_order(near_ref[:middle, :], got_ref[:middle, :])
    theirs = side_order(core_ref[:middle, :], core_ref[middle:, :])
    for s, x in enumerate((jnp.where(zero_core, mine, theirs), jnp.where(zero_core, theirs, mine))):
        cut = slice(s * LANES, (s + 1) * LANES)
        z_ref[:, cut] = x.T / known_ref[2 * ITERS - 1 : 2 * ITERS, cut]


def q_out_kernel(count, y_ref, known_ref, a_ref, b_ref, q_ref, scale_ref):
    last = 2 * ITERS
    scale = rms((a_ref[...] + b_ref[...])[last : last + 1], count)
    q_ref[...] = y_ref[...] / scale
    scale_ref[:last, :] = known_ref[:last, :]
    scale_ref[last:, :] = scale


def call(kernel, outs, *args, scalars=0, any_space=(), scratch=(), plain=False):
    specs = [pl.BlockSpec(memory_space=pltpu.SMEM)] * scalars
    for i in range(scalars, len(args)):
        specs.append(pl.BlockSpec(memory_space=pl.ANY if i in any_space else pltpu.VMEM))
    out_spec = pl.BlockSpec() if plain else pl.BlockSpec(memory_space=pltpu.VMEM)
    return pl.pallas_call(
        kernel,
        out_shape=[jax.ShapeDtypeStruct(shape, dtype) for shape, dtype in outs],
        in_specs=specs,
        out_specs=[out_spec] * len(outs),
        scratch_shapes=scratch,
        compiler_params=pltpu.CompilerParams(vmem_limit_bytes=16 * 1024 * 1024),
    )(*args)


def local(snapshots, sketch):
    groups = lax.axis_size("cell")
    places = lax.axis_size("snap")
    pairs = places // 4
    rows, width = snapshots.shape
    rank = sketch.shape[1]
    cols = rank // 4
    all_cells = rows * groups
    all_snaps = width * places
    place = lax.axis_index("snap")
    core = place % 2
    side = (place // 2) % 2
    pair = place // 4
    where = jnp.stack([core, side, pair]).astype(jnp.int32)
    same_seat = [[4 * p + s for p in range(pairs)] for s in range(4)]
    same_pair = [[4 * p + s for s in range(4)] for p in range(pairs)]

    def swap_core(x):
        return lax.ppermute(x, "snap", [(i, i ^ 1) for i in range(places)])

    def swap_side(x):
        return lax.ppermute(x, "snap", [(i, i ^ 2) for i in range(places)])

    def swap_pair(x):
        if pairs == 2:
            return lax.ppermute(x, "snap", [(i, i ^ 4) for i in range(places)])
        return lax.psum(x, "snap", axis_index_groups=same_seat) - x

    def swap_cell(x, step):
        def target(cell, seat):
            return cell ^ (1 if seat % 2 == step else 2)

        perm = [(c * places + i, target(c, i) * places + i) for c in range(groups) for i in range(places)]
        return lax.ppermute(x, ("cell", "snap"), perm)

    def cell_sum(x):
        if groups != 4:
            return lax.psum(x, "cell"), jnp.zeros_like(x)
        x = x + swap_cell(x, 0)
        return x, swap_cell(x, 1)

    def half(x, index):
        size = x.shape[1] // 2
        return lax.dynamic_slice_in_dim(x, index * size, size, 1)

    sizes = [n * rows // sum(PARTS) for n in PARTS]
    starts = [sum(sizes[:i]) for i in range(len(sizes))]

    core_block = swap_core(snapshots)
    side_chunks = [swap_side(snapshots[: sizes[0]])]
    got = swap_core(half(sketch, 1 - core))
    packed = ((width, LANES), F32)
    mine, theirs, *chunks = call(
        prepare_kernel,
        [packed, packed] + [((n, width), F32) for n in sizes[1:]],
        where, half(sketch, core), got, snapshots,
        scalars=1, any_space=(3,), scratch=[pltpu.SemaphoreType.DMA((len(sizes) - 1,))],
    )
    far = swap_side(theirs)
    side_chunks += [swap_side(c) for c in chunks]
    diagonal_chunks = [swap_core(c) for c in side_chunks]

    def factor(count):
        return [((count, 2 * width), BF16)] * 2

    near_y, *near = call(
        near_kernel, [((cols * rows // LANES, LANES), F32)] + factor(rows), snapshots, core_block, mine
    )
    high, low, own = [near[0]], [near[1]], []
    for i, size in enumerate(sizes):
        y, a_high, a_low = call(
            functools.partial(far_kernel, starts[i]),
            [((cols * size // LANES, LANES), F32)] + factor(size),
            side_chunks[i], diagonal_chunks[i], far, near_y,
        )
        high.append(a_high)
        low.append(a_low)
        own.append(y)
    got = [swap_pair(y) for y in own]

    sent_shape = ((cols * 4 * width // LANES + TILE, LANES), F32)
    y_shape = ((cols * rows // LANES + TILE, LANES), F32)
    scale_shape = ((TILE, LANES), F32)
    z_shape = ((cols * 4 * width // LANES, LANES), F32)
    (sent,) = call(first_z_kernel, [sent_shape], *own, *got, *high, *low)
    scales = []
    for section in range(ITERS - 1):
        a, b = cell_sum(sent)
        y, scale_y = call(
            functools.partial(y_kernel, all_cells), [y_shape, scale_shape], a, b, *high, *low
        )
        sent, scale_z = call(
            functools.partial(z_kernel, all_snaps), [sent_shape, scale_shape], y, swap_pair(y), *high, *low
        )
        scales += [scale_y, scale_z]
    a, b = cell_sum(sent)
    half_shape = ((cols * rows // LANES // 2 + TILE, LANES), F32)
    keep, send, scale, z = call(
        functools.partial(last_y_kernel, all_cells),
        [half_shape, half_shape, scale_shape, z_shape],
        where, a, b, *high, *low, scalars=1,
    )
    scales.append(scale)

    middle = z.shape[0] // 2
    z_near, z_far = z[:middle], z[middle:]

    if pairs == 2 and groups == 4:
        got = swap_pair(send)
        z_got = swap_side(z_far)
        z_core = swap_core(jnp.concatenate([z_near[middle // 2 :], z_got[middle // 2 :]], axis=0))
        quarter = ((2 * cols + TILE, LANES), F32)
        own, send = call(
            functools.partial(side_kernel, all_snaps), [quarter, quarter], where, keep, got, *scales, scalars=1
        )
        joint = ((2 * cols + 2 * TILE, LANES), F32)
        keep, send = call(core_kernel, [joint, joint], where, own, swap_side(send), scalars=1)
        y, known = call(
            join_kernel, [((LANES, rank), F32), ((TILE, rank), F32)], where, keep, swap_core(send), scalars=1
        )
        total = known + swap_pair(known)
        a, b = cell_sum(total)
        (z_out,) = call(
            z_out_kernel, [((width, rank), F32)], where, z_near, z_got, z_core, known, scalars=1, plain=True
        )
        q_out, scale_out = call(
            functools.partial(q_out_kernel, all_cells),
            [((LANES, rank), F32), ((2 * ITERS + 1, rank), F32)],
            y, known, a, b, plain=True,
        )
        return q_out, z_out, scale_out

    z_got = swap_side(z_far)
    z_core = swap_core(jnp.concatenate([z_near[middle // 2 :], z_got[middle // 2 :]], axis=0))
    first = jnp.where(pair == 0, keep[:-TILE], send[:-TILE])
    second = jnp.where(pair == 0, send[:-TILE], keep[:-TILE])
    y = jnp.concatenate([first, second], axis=0).reshape(-1, cols, LANES)
    y = jnp.moveaxis(y, 0, 1).reshape(cols, rows)
    y = lax.psum(y, "snap", axis_index_groups=same_seat)
    total = lax.psum(keep[-TILE:], "snap", axis_index_groups=same_seat)
    scales.append(rms(total, all_snaps))
    known = jnp.stack([s[0, :cols] for s in scales], axis=1)
    y = y / known[:, -1:]
    scale_y = rms(lax.psum(jnp.sum(y * y, axis=1, keepdims=True), "cell"), all_cells)
    y = y / scale_y
    gathered = lax.all_gather(jnp.concatenate([y, known, scale_y], axis=1), "snap", axis_index_groups=same_pair)
    gathered = gathered.reshape(2, 2, cols, -1).swapaxes(0, 1).reshape(rank, -1)
    mine = rows // places
    q_out = lax.dynamic_slice_in_dim(gathered, place * mine, mine, 1).T
    scale_out = gathered[:, rows:].T
    known = jnp.pad(scale_out, ((0, TILE - scale_out.shape[0]), (0, 0)))
    (z_out,) = call(z_out_kernel, [((width, rank), F32)], where, z_near, z_got, z_core, known, scalars=1)
    return q_out, z_out, scale_out


def solution(mesh):
    return jax.shard_map(
        local,
        mesh=mesh,
        in_specs=(P("cell", "snap"), P("snap", None)),
        out_specs=(P(("cell", "snap"), None), P("snap", None), P()),
        check_vma=False,
    )
```

time: 129 us -> 123 us (0.953)
  waiting for transfers between devices: 82.8 us -> 70.2 us
  starting transfers between devices: 25.1 us -> 35.8 us
  local copies, waits for them, and re-layouts: 6.75 us -> 2.65 us
  Pallas kernels: 9.7 us -> 13.4 us
  other arithmetic: 3.62 us -> 0.15 us
    ppermute x7 -> x8, waiting for transfers between devices: 25.2 us -> 18.7 us  [swap_pair(): return lax.ppermute(x, 'snap', [(i, i ^ 4) for i in range(places)])]
    ppermute x7 -> x8, starting transfers between devices: 7.16 us -> 11.6 us  [swap_side(): return lax.ppermute(x, 'snap', [(i, i ^ 2) for i in range(places)])]
    ppermute x7 -> x8, starting transfers between devices: 7.84 us -> 11.8 us  [swap_pair(): return lax.ppermute(x, 'snap', [(i, i ^ 4) for i in range(places)])]
    ppermute x7 -> x8, waiting for transfers between devices: 32.6 us -> 28.8 us  [swap_side(): return lax.ppermute(x, 'snap', [(i, i ^ 2) for i in range(places)])]
    pallas_call x9 -> x16, Pallas kernels: 9.7 us -> 13.4 us  [call(): pl.pallas_call(kernel, out_shape=[jax.ShapeDtypeStruct(shape, dtype) for...]
    ppermute x6, waiting for transfers between devices: 23.7 us -> 21.4 us  [swap_cell(): return lax.ppermute(x, ('cell', 'snap'), perm)]
    unnamed x24 -> x6, local copies, waits for them, and re-layouts: 2.74 us -> 0.67 us
    slice x13 -> x5, local copies, waits for them, and re-layouts: 2.58 us -> 1 us  [the longest x1 0.97 us: local(): side_chunks = [swap_side(snapshots[:sizes[0]])]]
  transfers between devices with their start and end apart: 28 -> 31, of which waited for: 20 -> 17; matrix products, arithmetic and copies ran while one was open for 4% -> 2% of each run, Pallas kernels for 3% -> 5%
where the time goes in v3:
time: 123 us
  waiting for transfers between devices  70.2 us (57%)
  starting transfers between devices  35.8 us (29%)
  Pallas kernels  13.4 us (11%)
  local copies, waits for them, and re-layouts  2.65 us (2%)
    ppermute x8, waiting for transfers between devices, swap_side(): return lax.ppermute(x, 'snap', [(i, i ^ 2) for i in range(places)])  28.8 us
    ppermute x6, waiting for transfers between devices, swap_cell(): return lax.ppermute(x, ('cell', 'snap'), perm)  21.4 us
    ppermute x8, waiting for transfers between devices, swap_pair(): return lax.ppermute(x, 'snap', [(i, i ^ 4) for i in range(places)])  18.7 us
    pallas_call x16, Pallas kernels, call(): pl.pallas_call(kernel, out_shape=[jax.ShapeDtypeStruct(shape, dtype) for...  13.4 us
    ppermute x8, starting transfers between devices, swap_pair(): return lax.ppermute(x, 'snap', [(i, i ^ 4) for i in range(places)])  11.8 us
    ppermute x8, starting transfers between devices, swap_side(): return lax.ppermute(x, 'snap', [(i, i ^ 2) for i in range(places)])  11.6 us
    ppermute x6, starting transfers between devices, swap_cell(): return lax.ppermute(x, ('cell', 'snap'), perm)  10.4 us
  transfers between devices with their start and end apart: 31, of which 17 were waited for; matrix products, arithmetic and copies ran while one was open for 2% of the time, Pallas kernels for 5%

profile of v3, /device:TPU:0, one launch (start us, length us, event | category | flops | bytes accessed | tf_op | source)
XLA Modules:
  0.0 122.9 jit_solution(641060507053833935)
XLA Ops:
  0.6 0.5 collective-permute-start.4
  1.2 1.0 constant_dynamic-slice_fusion
  2.1 0.2 collective-permute-start.2
  2.3 1.0 slice.16
  3.3 3.0 %collective-permute-start = (f32[256,256]{1,0:T(8,128)S(1)}, f32[256,256]{1,0:T(8,128)S(1)}, u32[]{:S(2)}, u32[]{:S(2)}) collective-permute-start(f32[256,256]{1,0:T(8,128)S(1)} %slice.16), channel_id=1, source_target_pairs={{0,2},{1,3},{2,0},{3,1},{4,6},{5,7},{6,4},{7,5},{8,10},{9,11},{10,... | collective-permute-start | bytes 786440 | tf_op jit(solution)/shard_map/ppermute | solution.py:327
  6.3 0.1 pad_add_fusion.place_ref
  6.4 1.1 shard_map.49
  7.5 0.2 collective-permute-start.5
  7.8 1.9 %collective-permute-start.7 = (f32[256,256]{1,0:T(8,128)S(1)}, f32[256,256]{1,0:T(8,128)S(1)}, u32[]{:S(2)}, u32[]{:S(2)}) collective-permute-start(f32[256,256]{1,0:T(8,128)S(1)} %get-tuple-element.49), channel_id=1, source_target_pairs={{0,2},{1,3},{2,0},{3,1},{4,6},{5,7},{6,4},{7,5},{8,10},{9,11},{10,... | collective-permute-start | bytes 786440 | tf_op jit(solution)/shard_map/ppermute | solution.py:327
  9.6 0.2 collective-permute-start.3
  9.8 3.6 %collective-permute-done.side_ref = f32[256,256]{1,0:T(8,128)S(1)} collective-permute-done((f32[256,256]{1,0:T(8,128)S(1)}, f32[256,256]{1,0:T(8,128)S(1)}, u32[]{:S(2)}, u32[]{:S(2)}) %collective-permute-start) | collective-permute-done | bytes 262176 | tf_op jit(solution)/shard_map/ppermute | solution.py:327
  13.4 2.1 %collective-permute-start.9 = (f32[128,256]{1,0:T(8,128)S(1)}, f32[128,256]{1,0:T(8,128)S(1)}, u32[]{:S(2)}, u32[]{:S(2)}) collective-permute-start(f32[128,256]{1,0:T(8,128)S(1)} %get-tuple-element.51), channel_id=1, source_target_pairs={{0,2},{1,3},{2,0},{3,1},{4,6},{5,7},{6,4},{7,5},{8,10},{9,11},{10,... | collective-permute-start | bytes 393224 | tf_op jit(solution)/shard_map/ppermute | solution.py:327
  15.5 12.0 %collective-permute-done.3.far_ref = f32[256,128]{1,0:T(8,128)S(1)} collective-permute-done((f32[256,128]{1,0:T(8,128)S(1)}, f32[256,128]{1,0:T(8,128)S(1)}, u32[]{:S(2)}, u32[]{:S(2)}) %collective-permute-start.3) | collective-permute-done | bytes 131104 | tf_op jit(solution)/shard_map/ppermute | solution.py:327
  27.5 0.5 collective-permute-start.6
  28.1 1.7 %collective-permute-done.9.side_ref = f32[128,256]{1,0:T(8,128)S(1)} collective-permute-done((f32[128,256]{1,0:T(8,128)S(1)}, f32[128,256]{1,0:T(8,128)S(1)}, u32[]{:S(2)}, u32[]{:S(2)}) %collective-permute-start.9) | collective-permute-done | bytes 131104 | tf_op jit(solution)/shard_map/ppermute | solution.py:327
  29.8 1.7 %collective-permute-start.11 = (f32[128,256]{1,0:T(8,128)S(1)}, f32[128,256]{1,0:T(8,128)S(1)}, u32[]{:S(2)}, u32[]{:S(2)}) collective-permute-start(f32[128,256]{1,0:T(8,128)S(1)} %get-tuple-element.53), channel_id=1, source_target_pairs={{0,2},{1,3},{2,0},{3,1},{4,6},{5,7},{6,4},{7,5},{8,10},{9,11},{10,... | collective-permute-start | bytes 393224 | tf_op jit(solution)/shard_map/ppermute | solution.py:327
  31.5 3.3 %collective-permute-done.11.side_ref = f32[128,256]{1,0:T(8,128)S(1)} collective-permute-done((f32[128,256]{1,0:T(8,128)S(1)}, f32[128,256]{1,0:T(8,128)S(1)}, u32[]{:S(2)}, u32[]{:S(2)}) %collective-permute-start.11) | collective-permute-done | bytes 131104 | tf_op jit(solution)/shard_map/ppermute | solution.py:327
  34.8 0.5 collective-permute-start.12
  35.3 0.9 shard_map.50
  36.2 0.4 shard_map.51
  36.7 2.8 %collective-permute-start.13 = (f32[128,128]{1,0:T(8,128)S(1)}, f32[128,128]{1,0:T(8,128)S(1)}, u32[]{:S(2)}, u32[]{:S(2)}) collective-permute-start(f32[128,128]{1,0:T(8,128)S(1)} %get-tuple-element.46.refs_0_), channel_id=1, source_target_pairs={{0,4},{1,5},{2,6},{3,7},{4,0},{5,1},{6,2},{7,3},{8,12},{9,13},{10,... | collective-permute-start | bytes 196616 | tf_op jit(solution)/shard_map/ppermute | solution.py:331
  39.4 0.4 shard_map.52
  39.9 0.3 collective-permute-start.14
  40.2 0.4 shard_map.53
  40.6 2.8 %collective-permute-start.15 = (f32[128,128]{1,0:T(8,128)S(1)}, f32[128,128]{1,0:T(8,128)S(1)}, u32[]{:S(2)}, u32[]{:S(2)}) collective-permute-start(f32[128,128]{1,0:T(8,128)S(1)} %get-tuple-element.50.refs_2_), channel_id=1, source_target_pairs={{0,4},{1,5},{2,6},{3,7},{4,0},{5,1},{6,2},{7,3},{8,12},{9,13},{10,... | collective-permute-start | bytes 196616 | tf_op jit(solution)/shard_map/ppermute | solution.py:331
  43.4 0.4 shard_map.54
  43.8 0.3 collective-permute-start.16
  44.1 0.4 shard_map.55
  44.5 2.8 %collective-permute-start.17 = (f32[64,128]{1,0:T(8,128)S(1)}, f32[64,128]{1,0:T(8,128)S(1)}, u32[]{:S(2)}, u32[]{:S(2)}) collective-permute-start(f32[64,128]{1,0:T(8,128)S(1)} %get-tuple-element.54.refs_4_), channel_id=1, source_target_pairs={{0,4},{1,5},{2,6},{3,7},{4,0},{5,1},{6,2},{7,3},{8,12},{9,13},{10,... | collective-permute-start | bytes 98312 | tf_op jit(solution)/shard_map/ppermute | solution.py:331
  47.2 4.1 %collective-permute-done.16.refs_8_ = f32[64,128]{1,0:T(8,128)S(1)} collective-permute-done((f32[64,128]{1,0:T(8,128)S(1)}, f32[64,128]{1,0:T(8,128)S(1)}, u32[]{:S(2)}, u32[]{:S(2)}) %collective-permute-start.16) | collective-permute-done | bytes 32800 | tf_op jit(solution)/shard_map/ppermute | solution.py:331
  51.4 0.4 collective-permute-done.17.refs_9_
  51.7 0.8 shard_map.56
  52.5 1.7 %collective-permute-start.18 = (f32[520,128]{1,0:T(8,128)S(1)}, f32[520,128]{1,0:T(8,128)S(1)}, u32[]{:S(2)}, u32[]{:S(2)}) collective-permute-start(f32[520,128]{1,0:T(8,128)S(1)} %shard_map.56), channel_id=1, source_target_pairs={{0,8},{1,17},{2,10},{3,19},{4,12},{5,21},{6,14},{7,23},{8,0},{9,25... | collective-permute-start | bytes 798728 | tf_op jit(solution)/shard_map/ppermute | solution.py:339
  54.2 4.8 %collective-permute-done.18 = f32[520,128]{1,0:T(8,128)S(1)} collective-permute-done((f32[520,128]{1,0:T(8,128)S(1)}, f32[520,128]{1,0:T(8,128)S(1)}, u32[]{:S(2)}, u32[]{:S(2)}) %collective-permute-start.18) | collective-permute-done | bytes 266272 | tf_op jit(solution)/shard_map/ppermute | solution.py:339
  59.0 1.7 %collective-permute-start.19 = (f32[520,128]{1,0:T(8,128)S(1)}, f32[520,128]{1,0:T(8,128)S(1)}, u32[]{:S(2)}, u32[]{:S(2)}) collective-permute-start(f32[520,128]{1,0:T(8,128)S(1)} %add.31.refs_0_), channel_id=1, source_target_pairs={{0,16},{1,9},{2,18},{3,11},{4,20},{5,13},{6,22},{7,15},{8,24},{9,1... | collective-permute-start | bytes 798728 | tf_op jit(solution)/shard_map/ppermute | solution.py:339
  60.8 4.8 %collective-permute-done.19.refs_1_ = f32[520,128]{1,0:T(8,128)S(1)} collective-permute-done((f32[520,128]{1,0:T(8,128)S(1)}, f32[520,128]{1,0:T(8,128)S(1)}, u32[]{:S(2)}, u32[]{:S(2)}) %collective-permute-start.19) | collective-permute-done | bytes 266272 | tf_op jit(solution)/shard_map/ppermute | solution.py:339
  65.5 1.5 %shard_map.57 = (f32[520,128]{1,0:T(8,128)S(1)}, f32[8,128]{1,0:T(8,128)S(1)}) custom-call(f32[520,128]{1,0:T(8,128)S(1)} %add.31.refs_0_, f32[520,128]{1,0:T(8,128)S(1)} %collective-permute-done.19.refs_1_, bf16[1024,512]{1,0:T(8,128)(2,1)S(1)} %get-tuple-element.55.refs_10_.refs_2_, bf16[256,512]{1,0:T(8,128)(2,1)S(1)} %get-tuple-element.56.refs_11_.refs_3_, ...), custom_call_target="tpu_custom_call" | custom-call | tf_op jit(solution)/shard_map/pallas_call | solution.py:296
  67.1 0.5 collective-permute-start.20
  67.6 11.8 %collective-permute-done.20.refs_1_ = f32[520,128]{1,0:T(8,128)S(1)} collective-permute-done((f32[520,128]{1,0:T(8,128)S(1)}, f32[520,128]{1,0:T(8,128)S(1)}, u32[]{:S(2)}, u32[]{:S(2)}) %collective-permute-start.20) | collective-permute-done | bytes 266272 | tf_op jit(solution)/shard_map/ppermute | solution.py:331
  79.4 0.9 shard_map.58
  80.3 1.8 %collective-permute-start.21 = (f32[520,128]{1,0:T(8,128)S(1)}, f32[520,128]{1,0:T(8,128)S(1)}, u32[]{:S(2)}, u32[]{:S(2)}) collective-permute-start(f32[520,128]{1,0:T(8,128)S(1)} %get-tuple-element.68), channel_id=1, source_target_pairs={{0,8},{1,17},{2,10},{3,19},{4,12},{5,21},{6,14},{7,23},{8,0},{9,25... | collective-permute-start | bytes 798728 | tf_op jit(solution)/shard_map/ppermute | solution.py:339
  82.1 4.7 %collective-permute-done.21 = f32[520,128]{1,0:T(8,128)S(1)} collective-permute-done((f32[520,128]{1,0:T(8,128)S(1)}, f32[520,128]{1,0:T(8,128)S(1)}, u32[]{:S(2)}, u32[]{:S(2)}) %collective-permute-start.21) | collective-permute-done | bytes 266272 | tf_op jit(solution)/shard_map/ppermute | solution.py:339
  86.8 1.8 %collective-permute-start.22 = (f32[520,128]{1,0:T(8,128)S(1)}, f32[520,128]{1,0:T(8,128)S(1)}, u32[]{:S(2)}, u32[]{:S(2)}) collective-permute-start(f32[520,128]{1,0:T(8,128)S(1)} %add.32.refs_0_), channel_id=1, source_target_pairs={{0,16},{1,9},{2,18},{3,11},{4,20},{5,13},{6,22},{7,15},{8,24},{9,1... | collective-permute-start | bytes 798728 | tf_op jit(solution)/shard_map/ppermute | solution.py:339
  88.6 4.7 %collective-permute-done.22.refs_1_ = f32[520,128]{1,0:T(8,128)S(1)} collective-permute-done((f32[520,128]{1,0:T(8,128)S(1)}, f32[520,128]{1,0:T(8,128)S(1)}, u32[]{:S(2)}, u32[]{:S(2)}) %collective-permute-start.22) | collective-permute-done | bytes 266272 | tf_op jit(solution)/shard_map/ppermute | solution.py:339
  93.3 2.1 %shard_map.59 = (f32[264,128]{1,0:T(8,128)S(1)}, f32[264,128]{1,0:T(8,128)S(1)}, f32[8,128]{1,0:T(8,128)S(1)}, f32[512,128]{1,0:T(8,128)S(1)}) custom-call(s32[3]{0:T(128)S(1)} %pad_add_fusion.place_ref, f32[520,128]{1,0:T(8,128)S(1)} %add.32.refs_0_, f32[520,128]{1,0:T(8,128)S(1)} %collective-permute-done.22.refs_1_, ...), custom_call_target="tpu_custom_call" | custom-call | tf_op jit(solution)/shard_map/pallas_call | solution.py:296
  95.4 0.1 collective-permute-start.23
  95.5 2.0 %collective-permute-start.29 = (f32[256,128]{1,0:T(8,128)S(1)}, f32[256,128]{1,0:T(8,128)S(1)}, u32[]{:S(2)}, u32[]{:S(2)}) collective-permute-start(f32[256,128]{1,0:T(8,128)S(1)} %get-tuple-element.83), channel_id=1, source_target_pairs={{0,2},{1,3},{2,0},{3,1},{4,6},{5,7},{6,4},{7,5},{8,10},{9,11},{10,... | collective-permute-start | bytes 393224 | tf_op jit(solution)/shard_map/ppermute | solution.py:327
  97.5 4.5 %collective-permute-done.29.got_ref = f32[256,128]{1,0:T(8,128)S(1)} collective-permute-done((f32[256,128]{1,0:T(8,128)S(1)}, f32[256,128]{1,0:T(8,128)S(1)}, u32[]{:S(2)}, u32[]{:S(2)}) %collective-permute-start.29) | collective-permute-done | bytes 131104 | tf_op jit(solution)/shard_map/ppermute | solution.py:327
  102.0 0.7 copy-done.1
  102.6 0.7 shard_map.60
  103.4 0.6 collective-permute-start.24
  103.9 0.1 collective-permute-start.30
  104.0 3.7 %collective-permute-done.24.got_ref = f32[136,128]{1,0:T(8,128)S(1)} collective-permute-done((f32[136,128]{1,0:T(8,128)S(1)}, f32[136,128]{1,0:T(8,128)S(1)}, u32[]{:S(2)}, u32[]{:S(2)}) %collective-permute-start.24) | collective-permute-done | bytes 69664 | tf_op jit(solution)/shard_map/ppermute | solution.py:327
  107.7 0.6 shard_map.61
  108.4 1.3 %collective-permute-done.25.got_ref = f32[144,128]{1,0:T(8,128)S(1)} collective-permute-done((f32[144,128]{1,0:T(8,128)S(1)}, f32[144,128]{1,0:T(8,128)S(1)}, u32[]{:S(2)}, u32[]{:S(2)}) %collective-permute-start.25) | collective-permute-done | bytes 73760 | tf_op jit(solution)/shard_map/ppermute | solution.py:324
  109.6 0.7 shard_map.62
  110.3 2.3 %collective-permute-start.26 = (f32[8,256]{1,0:T(8,128)S(1)}, f32[8,256]{1,0:T(8,128)S(1)}, u32[]{:S(2)}, u32[]{:S(2)}) collective-permute-start(f32[8,256]{1,0:T(8,128)S(1)} %get-tuple-element.79.known_ref), channel_id=1, source_target_pairs={{0,4},{1,5},{2,6},{3,7},{4,0},{5,1},{6,2},{7,3},{8,12},{9,13},{10,... | collective-permute-start | bytes 24584 | tf_op jit(solution)/shard_map/ppermute | solution.py:331
  112.6 2.4 %collective-permute-done.26 = f32[8,256]{1,0:T(8,128)S(1)} collective-permute-done((f32[8,256]{1,0:T(8,128)S(1)}, f32[8,256]{1,0:T(8,128)S(1)}, u32[]{:S(2)}, u32[]{:S(2)}) %collective-permute-start.26) | collective-permute-done | bytes 8224 | tf_op jit(solution)/shard_map/ppermute | solution.py:331
  114.9 1.7 %collective-permute-start.27 = (f32[8,256]{1,0:T(8,128)S(1)}, f32[8,256]{1,0:T(8,128)S(1)}, u32[]{:S(2)}, u32[]{:S(2)}) collective-permute-start(f32[8,256]{1,0:T(8,128)S(1)} %add.33), channel_id=1, source_target_pairs={{0,8},{1,17},{2,10},{3,19},{4,12},{5,21},{6,14},{7,23},{8,0},{9,25... | collective-permute-start | bytes 24584 | tf_op jit(solution)/shard_map/ppermute | solution.py:339
  116.6 2.0 %collective-permute-done.27 = f32[8,256]{1,0:T(8,128)S(1)} collective-permute-done((f32[8,256]{1,0:T(8,128)S(1)}, f32[8,256]{1,0:T(8,128)S(1)}, u32[]{:S(2)}, u32[]{:S(2)}) %collective-permute-start.27) | collective-permute-done | bytes 8224 | tf_op jit(solution)/shard_map/ppermute | solution.py:339
  118.6 1.7 %collective-permute-start.28 = (f32[8,256]{1,0:T(8,128)S(1)}, f32[8,256]{1,0:T(8,128)S(1)}, u32[]{:S(2)}, u32[]{:S(2)}) collective-permute-start(f32[8,256]{1,0:T(8,128)S(1)} %add.34.a_ref), channel_id=1, source_target_pairs={{0,16},{1,9},{2,18},{3,11},{4,20},{5,13},{6,22},{7,15},{8,24},{9,1... | collective-permute-start | bytes 24584 | tf_op jit(solution)/shard_map/ppermute | solution.py:339
  120.3 1.4 %shard_map.64 = f32[256,256]{1,0:T(8,128)} custom-call(s32[3]{0:T(128)S(1)} %pad_add_fusion.place_ref, f32[256,128]{1,0:T(8,128)S(1)} %get-tuple-element.84.near_ref, f32[256,128]{1,0:T(8,128)S(1)} %copy-done.2, f32[256,128]{1,0:T(8,128)S(1)} %collective-permute-done.30.core_ref, f32[8,256]{1,0:T(8,128)S(1)} %get-tuple-element.79.known_ref), custom_call_target="tpu_custom_call" | custom-call | tf_op jit(solution)/shard_map/pallas_call | solution.py:296
  121.7 0.5 collective-permute-done.28.b_ref
  122.2 0.7 shard_map.63
  (32 shorter events, 0.3 us)
Async XLA Ops:
  0.6 5.8 %copy-start = (f32[1024,256]{1,0:T(8,128)S(1)}, f32[1024,256]{1,0:T(8,128)}, u32[]{:S(2)}) copy-start(f32[1024,256]{1,0:T(8,128)} %own_ref.1) | copy-start | bytes 3145732
  0.6 34.1 %collective-permute-start.4 = (f32[1024,256]{1,0:T(8,128)}, f32[1024,256]{1,0:T(8,128)S(1)}, u32[]{:S(2)}, u32[]{:S(2)}) collective-permute-start(f32[1024,256]{1,0:T(8,128)} %own_ref.1), channel_id=1, source_target_pairs={{0,1},{1,0},{2,3},{3,2},{4,5},{5,4},{6,7},{7,6},{8,9},{9,8},{10,11... | collective-permute-start | bytes 3145736 | tf_op jit(solution)/shard_map/ppermute | solution.py:324
  2.1 4.3 %collective-permute-start.2 = (f32[256,128]{1,0:T(8,128)S(1)}, f32[256,128]{1,0:T(8,128)S(1)}, u32[]{:S(2)}, u32[]{:S(2)}) collective-permute-start(f32[256,128]{1,0:T(8,128)S(1)} %get-tuple-element.85), channel_id=1, source_target_pairs={{0,1},{1,0},{2,3},{3,2},{4,5},{5,4},{6,7},{7,6},{8,9},{9,8},{10,11... | collective-permute-start | bytes 393224 | tf_op jit(solution)/shard_map/ppermute | solution.py:324
  3.3 10.1 %collective-permute-start = (f32[256,256]{1,0:T(8,128)S(1)}, f32[256,256]{1,0:T(8,128)S(1)}, u32[]{:S(2)}, u32[]{:S(2)}) collective-permute-start(f32[256,256]{1,0:T(8,128)S(1)} %slice.16), channel_id=1, source_target_pairs={{0,2},{1,3},{2,0},{3,1},{4,6},{5,7},{6,4},{7,5},{8,10},{9,11},{10,... | collective-permute-start | bytes 786440 | tf_op jit(solution)/shard_map/ppermute | solution.py:327
  7.5 20.0 %collective-permute-start.5 = (f32[256,256]{1,0:T(8,128)S(1)}, f32[256,256]{1,0:T(8,128)S(1)}, u32[]{:S(2)}, u32[]{:S(2)}) collective-permute-start(f32[256,256]{1,0:T(8,128)S(1)} %get-tuple-element.47), channel_id=1, source_target_pairs={{0,2},{1,3},{2,0},{3,1},{4,6},{5,7},{6,4},{7,5},{8,10},{9,11},{10,... | collective-permute-start | bytes 786440 | tf_op jit(solution)/shard_map/ppermute | solution.py:327
  7.8 20.2 %collective-permute-start.7 = (f32[256,256]{1,0:T(8,128)S(1)}, f32[256,256]{1,0:T(8,128)S(1)}, u32[]{:S(2)}, u32[]{:S(2)}) collective-permute-start(f32[256,256]{1,0:T(8,128)S(1)} %get-tuple-element.49), channel_id=1, source_target_pairs={{0,2},{1,3},{2,0},{3,1},{4,6},{5,7},{6,4},{7,5},{8,10},{9,11},{10,... | collective-permute-start | bytes 786440 | tf_op jit(solution)/shard_map/ppermute | solution.py:327
  9.6 17.9 %collective-permute-start.3 = (f32[256,128]{1,0:T(8,128)S(1)}, f32[256,128]{1,0:T(8,128)S(1)}, u32[]{:S(2)}, u32[]{:S(2)}) collective-permute-start(f32[256,128]{1,0:T(8,128)S(1)} %get-tuple-element.43), channel_id=1, source_target_pairs={{0,2},{1,3},{2,0},{3,1},{4,6},{5,7},{6,4},{7,5},{8,10},{9,11},{10,... | collective-permute-start | bytes 393224 | tf_op jit(solution)/shard_map/ppermute | solution.py:327
  13.4 16.3 %collective-permute-start.9 = (f32[128,256]{1,0:T(8,128)S(1)}, f32[128,256]{1,0:T(8,128)S(1)}, u32[]{:S(2)}, u32[]{:S(2)}) collective-permute-start(f32[128,256]{1,0:T(8,128)S(1)} %get-tuple-element.51), channel_id=1, source_target_pairs={{0,2},{1,3},{2,0},{3,1},{4,6},{5,7},{6,4},{7,5},{8,10},{9,11},{10,... | collective-permute-start | bytes 393224 | tf_op jit(solution)/shard_map/ppermute | solution.py:327
  27.5 8.7 %collective-permute-start.1 = (f32[256,256]{1,0:T(8,128)S(1)}, f32[256,256]{1,0:T(8,128)S(1)}, u32[]{:S(2)}, u32[]{:S(2)}) collective-permute-start(f32[256,256]{1,0:T(8,128)S(1)} %collective-permute-done.side_ref), channel_id=1, source_target_pairs={{0,1},{1,0},{2,3},{3,2},{4,5},{5,4},{6,7},{7,6},{8,9},{9,8},{10,11... | collective-permute-start | bytes 786440 | tf_op jit(solution)/shard_map/ppermute | solution.py:324
  27.5 12.0 %collective-permute-start.6 = (f32[256,256]{1,0:T(8,128)S(1)}, f32[256,256]{1,0:T(8,128)S(1)}, u32[]{:S(2)}, u32[]{:S(2)}) collective-permute-start(f32[256,256]{1,0:T(8,128)S(1)} %collective-permute-done.5.side_ref), channel_id=1, source_target_pairs={{0,1},{1,0},{2,3},{3,2},{4,5},{5,4},{6,7},{7,6},{8,9},{9,8},{10,11... | collective-permute-start | bytes 786440 | tf_op jit(solution)/shard_map/ppermute | solution.py:324
  28.0 12.2 %collective-permute-start.8 = (f32[256,256]{1,0:T(8,128)S(1)}, f32[256,256]{1,0:T(8,128)S(1)}, u32[]{:S(2)}, u32[]{:S(2)}) collective-permute-start(f32[256,256]{1,0:T(8,128)S(1)} %collective-permute-done.7.side_ref), channel_id=1, source_target_pairs={{0,1},{1,0},{2,3},{3,2},{4,5},{5,4},{6,7},{7,6},{8,9},{9,8},{10,11... | collective-permute-start | bytes 786440 | tf_op jit(solution)/shard_map/ppermute | solution.py:324
  29.8 5.0 %collective-permute-start.11 = (f32[128,256]{1,0:T(8,128)S(1)}, f32[128,256]{1,0:T(8,128)S(1)}, u32[]{:S(2)}, u32[]{:S(2)}) collective-permute-start(f32[128,256]{1,0:T(8,128)S(1)} %get-tuple-element.53), channel_id=1, source_target_pairs={{0,2},{1,3},{2,0},{3,1},{4,6},{5,7},{6,4},{7,5},{8,10},{9,11},{10,... | collective-permute-start | bytes 393224 | tf_op jit(solution)/shard_map/ppermute | solution.py:327
  34.8 8.7 %collective-permute-start.10 = (f32[128,256]{1,0:T(8,128)S(1)}, f32[128,256]{1,0:T(8,128)S(1)}, u32[]{:S(2)}, u32[]{:S(2)}) collective-permute-start(f32[128,256]{1,0:T(8,128)S(1)} %collective-permute-done.9.side_ref), channel_id=1, source_target_pairs={{0,1},{1,0},{2,3},{3,2},{4,5},{5,4},{6,7},{7,6},{8,9},{9,8},{10,11... | collective-permute-start | bytes 393224 | tf_op jit(solution)/shard_map/ppermute | solution.py:324
  34.8 9.3 %collective-permute-start.12 = (f32[128,256]{1,0:T(8,128)S(1)}, f32[128,256]{1,0:T(8,128)S(1)}, u32[]{:S(2)}, u32[]{:S(2)}) collective-permute-start(f32[128,256]{1,0:T(8,128)S(1)} %collective-permute-done.11.side_ref), channel_id=1, source_target_pairs={{0,1},{1,0},{2,3},{3,2},{4,5},{5,4},{6,7},{7,6},{8,9},{9,8},{10,11... | collective-permute-start | bytes 393224 | tf_op jit(solution)/shard_map/ppermute | solution.py:324
  36.7 15.1 %collective-permute-start.13 = (f32[128,128]{1,0:T(8,128)S(1)}, f32[128,128]{1,0:T(8,128)S(1)}, u32[]{:S(2)}, u32[]{:S(2)}) collective-permute-start(f32[128,128]{1,0:T(8,128)S(1)} %get-tuple-element.46.refs_0_), channel_id=1, source_target_pairs={{0,4},{1,5},{2,6},{3,7},{4,0},{5,1},{6,2},{7,3},{8,12},{9,13},{10,... | collective-permute-start | bytes 196616 | tf_op jit(solution)/shard_map/ppermute | solution.py:331
  39.9 11.8 %collective-permute-start.14 = (f32[128,128]{1,0:T(8,128)S(1)}, f32[128,128]{1,0:T(8,128)S(1)}, u32[]{:S(2)}, u32[]{:S(2)}) collective-permute-start(f32[128,128]{1,0:T(8,128)S(1)} %get-tuple-element.48.refs_1_), channel_id=1, source_target_pairs={{0,4},{1,5},{2,6},{3,7},{4,0},{5,1},{6,2},{7,3},{8,12},{9,13},{10,... | collective-permute-start | bytes 196616 | tf_op jit(solution)/shard_map/ppermute | solution.py:331
  40.6 11.1 %collective-permute-start.15 = (f32[128,128]{1,0:T(8,128)S(1)}, f32[128,128]{1,0:T(8,128)S(1)}, u32[]{:S(2)}, u32[]{:S(2)}) collective-permute-start(f32[128,128]{1,0:T(8,128)S(1)} %get-tuple-element.50.refs_2_), channel_id=1, source_target_pairs={{0,4},{1,5},{2,6},{3,7},{4,0},{5,1},{6,2},{7,3},{8,12},{9,13},{10,... | collective-permute-start | bytes 196616 | tf_op jit(solution)/shard_map/ppermute | solution.py:331
  43.8 7.6 %collective-permute-start.16 = (f32[64,128]{1,0:T(8,128)S(1)}, f32[64,128]{1,0:T(8,128)S(1)}, u32[]{:S(2)}, u32[]{:S(2)}) collective-permute-start(f32[64,128]{1,0:T(8,128)S(1)} %get-tuple-element.52.refs_3_), channel_id=1, source_target_pairs={{0,4},{1,5},{2,6},{3,7},{4,0},{5,1},{6,2},{7,3},{8,12},{9,13},{10,... | collective-permute-start | bytes 98312 | tf_op jit(solution)/shard_map/ppermute | solution.py:331
  44.5 7.3 %collective-permute-start.17 = (f32[64,128]{1,0:T(8,128)S(1)}, f32[64,128]{1,0:T(8,128)S(1)}, u32[]{:S(2)}, u32[]{:S(2)}) collective-permute-start(f32[64,128]{1,0:T(8,128)S(1)} %get-tuple-element.54.refs_4_), channel_id=1, source_target_pairs={{0,4},{1,5},{2,6},{3,7},{4,0},{5,1},{6,2},{7,3},{8,12},{9,13},{10,... | collective-permute-start | bytes 98312 | tf_op jit(solution)/shard_map/ppermute | solution.py:331
  52.5 6.5 %collective-permute-start.18 = (f32[520,128]{1,0:T(8,128)S(1)}, f32[520,128]{1,0:T(8,128)S(1)}, u32[]{:S(2)}, u32[]{:S(2)}) collective-permute-start(f32[520,128]{1,0:T(8,128)S(1)} %shard_map.56), channel_id=1, source_target_pairs={{0,8},{1,17},{2,10},{3,19},{4,12},{5,21},{6,14},{7,23},{8,0},{9,25... | collective-permute-start | bytes 798728 | tf_op jit(solution)/shard_map/ppermute | solution.py:339
  59.0 6.5 %collective-permute-start.19 = (f32[520,128]{1,0:T(8,128)S(1)}, f32[520,128]{1,0:T(8,128)S(1)}, u32[]{:S(2)}, u32[]{:S(2)}) collective-permute-start(f32[520,128]{1,0:T(8,128)S(1)} %add.31.refs_0_), channel_id=1, source_target_pairs={{0,16},{1,9},{2,18},{3,11},{4,20},{5,13},{6,22},{7,15},{8,24},{9,1... | collective-permute-start | bytes 798728 | tf_op jit(solution)/shard_map/ppermute | solution.py:339
  67.1 12.4 %collective-permute-start.20 = (f32[520,128]{1,0:T(8,128)S(1)}, f32[520,128]{1,0:T(8,128)S(1)}, u32[]{:S(2)}, u32[]{:S(2)}) collective-permute-start(f32[520,128]{1,0:T(8,128)S(1)} %get-tuple-element.67.refs_0_), channel_id=1, source_target_pairs={{0,4},{1,5},{2,6},{3,7},{4,0},{5,1},{6,2},{7,3},{8,12},{9,13},{10,... | collective-permute-start | bytes 798728 | tf_op jit(solution)/shard_map/ppermute | solution.py:331
  80.3 6.5 %collective-permute-start.21 = (f32[520,128]{1,0:T(8,128)S(1)}, f32[520,128]{1,0:T(8,128)S(1)}, u32[]{:S(2)}, u32[]{:S(2)}) collective-permute-start(f32[520,128]{1,0:T(8,128)S(1)} %get-tuple-element.68), channel_id=1, source_target_pairs={{0,8},{1,17},{2,10},{3,19},{4,12},{5,21},{6,14},{7,23},{8,0},{9,25... | collective-permute-start | bytes 798728 | tf_op jit(solution)/shard_map/ppermute | solution.py:339
  86.8 6.5 %collective-permute-start.22 = (f32[520,128]{1,0:T(8,128)S(1)}, f32[520,128]{1,0:T(8,128)S(1)}, u32[]{:S(2)}, u32[]{:S(2)}) collective-permute-start(f32[520,128]{1,0:T(8,128)S(1)} %add.32.refs_0_), channel_id=1, source_target_pairs={{0,16},{1,9},{2,18},{3,11},{4,20},{5,13},{6,22},{7,15},{8,24},{9,1... | collective-permute-start | bytes 798728 | tf_op jit(solution)/shard_map/ppermute | solution.py:339
  95.4 7.2 %collective-permute-start.23 = (f32[264,128]{1,0:T(8,128)S(1)}, f32[264,128]{1,0:T(8,128)S(1)}, u32[]{:S(2)}, u32[]{:S(2)}) collective-permute-start(f32[264,128]{1,0:T(8,128)S(1)} %get-tuple-element.70), channel_id=1, source_target_pairs={{0,4},{1,5},{2,6},{3,7},{4,0},{5,1},{6,2},{7,3},{8,12},{9,13},{10,... | collective-permute-start | bytes 405512 | tf_op jit(solution)/shard_map/ppermute | solution.py:331
  95.5 6.5 %collective-permute-start.29 = (f32[256,128]{1,0:T(8,128)S(1)}, f32[256,128]{1,0:T(8,128)S(1)}, u32[]{:S(2)}, u32[]{:S(2)}) collective-permute-start(f32[256,128]{1,0:T(8,128)S(1)} %get-tuple-element.83), channel_id=1, source_target_pairs={{0,2},{1,3},{2,0},{3,1},{4,6},{5,7},{6,4},{7,5},{8,10},{9,11},{10,... | collective-permute-start | bytes 393224 | tf_op jit(solution)/shard_map/ppermute | solution.py:327
  101.9 0.7 copy-start.1
  102.6 1.3 %slice-start = ((f32[256,128]{1,0:T(8,128)}), f32[128,128]{1,0:T(8,128)S(1)}, s32[]{:S(2)}) async-start(f32[256,128]{1,0:T(8,128)} %copy-done.1), calls=%async_computation | async-start | bytes 131072 | tf_op jit(solution)/shard_map/slice | solution.py:416
  103.4 4.4 %collective-permute-start.24 = (f32[136,128]{1,0:T(8,128)S(1)}, f32[136,128]{1,0:T(8,128)S(1)}, u32[]{:S(2)}, u32[]{:S(2)}) collective-permute-start(f32[136,128]{1,0:T(8,128)S(1)} %get-tuple-element.75), channel_id=1, source_target_pairs={{0,2},{1,3},{2,0},{3,1},{4,6},{5,7},{6,4},{7,5},{8,10},{9,11},{10,... | collective-permute-start | bytes 208904 | tf_op jit(solution)/shard_map/ppermute | solution.py:327
  103.9 16.4 %collective-permute-start.30 = (f32[256,128]{1,0:T(8,128)S(1)}, f32[256,128]{1,0:T(8,128)S(1)}, u32[]{:S(2)}, u32[]{:S(2)}) collective-permute-start(f32[256,128]{1,0:T(8,128)S(1)} %pad_maximum_fusion), channel_id=1, source_target_pairs={{0,1},{1,0},{2,3},{3,2},{4,5},{5,4},{6,7},{7,6},{8,9},{9,8},{10,11... | collective-permute-start | bytes 393224 | tf_op jit(solution)/shard_map/ppermute | solution.py:324
  108.3 12.0 %copy-start.2 = (f32[256,128]{1,0:T(8,128)S(1)}, f32[256,128]{1,0:T(8,128)}, u32[]{:S(2)}) copy-start(f32[256,128]{1,0:T(8,128)} %copy-done.1) | copy-start | bytes 393220
  108.3 1.3 %collective-permute-start.25 = (f32[144,128]{1,0:T(8,128)S(1)}, f32[144,128]{1,0:T(8,128)S(1)}, u32[]{:S(2)}, u32[]{:S(2)}) collective-permute-start(f32[144,128]{1,0:T(8,128)S(1)} %get-tuple-element.77), channel_id=1, source_target_pairs={{0,1},{1,0},{2,3},{3,2},{4,5},{5,4},{6,7},{7,6},{8,9},{9,8},{10,11... | collective-permute-start | bytes 221192 | tf_op jit(solution)/shard_map/ppermute | solution.py:324
  110.3 4.6 %collective-permute-start.26 = (f32[8,256]{1,0:T(8,128)S(1)}, f32[8,256]{1,0:T(8,128)S(1)}, u32[]{:S(2)}, u32[]{:S(2)}) collective-permute-start(f32[8,256]{1,0:T(8,128)S(1)} %get-tuple-element.79.known_ref), channel_id=1, source_target_pairs={{0,4},{1,5},{2,6},{3,7},{4,0},{5,1},{6,2},{7,3},{8,12},{9,13},{10,... | collective-permute-start | bytes 24584 | tf_op jit(solution)/shard_map/ppermute | solution.py:331
  114.9 3.7 %collective-permute-start.27 = (f32[8,256]{1,0:T(8,128)S(1)}, f32[8,256]{1,0:T(8,128)S(1)}, u32[]{:S(2)}, u32[]{:S(2)}) collective-permute-start(f32[8,256]{1,0:T(8,128)S(1)} %add.33), channel_id=1, source_target_pairs={{0,8},{1,17},{2,10},{3,19},{4,12},{5,21},{6,14},{7,23},{8,0},{9,25... | collective-permute-start | bytes 24584 | tf_op jit(solution)/shard_map/ppermute | solution.py:339
  118.6 3.7 %collective-permute-start.28 = (f32[8,256]{1,0:T(8,128)S(1)}, f32[8,256]{1,0:T(8,128)S(1)}, u32[]{:S(2)}, u32[]{:S(2)}) collective-permute-start(f32[8,256]{1,0:T(8,128)S(1)} %add.34.a_ref), channel_id=1, source_target_pairs={{0,16},{1,9},{2,18},{3,11},{4,20},{5,13},{6,22},{7,15},{8,24},{9,1... | collective-permute-start | bytes 24584 | tf_op jit(solution)/shard_map/ppermute | solution.py:339

commit v4 on v0

v4 whole, which is shorter than its diff:
```python
import functools

import jax
import jax.numpy as jnp
from jax import lax
from jax.experimental import pallas as pl
from jax.experimental.pallas import tpu as pltpu
from jax.sharding import PartitionSpec as P

ITERS = 2
EPS = 1e-05
LANES = 128
TILE = 8
CHIPS = 4
GROUPS = 4
HALVES = 2
BF16 = jnp.bfloat16
F32 = jnp.float32


def split(x):
    high = x.astype(BF16).astype(F32)
    return high, x - high


def dot(a, b):
    return lax.dot_general(a, b, (((1,), (0,)), ((), ())), preferred_element_type=F32)


def eye(cols):
    shape = (cols, LANES)
    return lax.broadcasted_iota(jnp.int32, shape, 0) == lax.broadcasted_iota(jnp.int32, shape, 1)


def to_column(row, cols):
    return jnp.sum(jnp.where(eye(cols), row, 0.0), axis=1, keepdims=True)


def to_row(column):
    return jnp.sum(jnp.where(eye(column.shape[0]), column, 0.0), axis=0, keepdims=True)


def squares_tile(x):
    row = to_row(jnp.sum(x * x, axis=1, keepdims=True))
    return jnp.broadcast_to(row, (TILE, LANES))


def rms(total, count):
    return jnp.sqrt(total / count + EPS)


def wide(x, cols):
    return jnp.concatenate([x[j * cols : (j + 1) * cols] for j in range(x.shape[0] // cols)], axis=1)


def store_blocks(ref, x):
    cols = x.shape[0]
    for j in range(x.shape[1] // LANES):
        ref[j * cols : (j + 1) * cols, :] = x[:, j * LANES : (j + 1) * LANES]


def turn(x, cols):
    return pltpu.roll(x, cols, 1)


def join_lanes(first, second, cols):
    left = lax.broadcasted_iota(jnp.int32, first.shape, 1) < cols
    return jnp.where(left, first, turn(second, cols))


def chunk_at(place_ref, shift):
    return lax.rem(place_ref[0] + shift + CHIPS, CHIPS)


def ordered_tiles(place_ref, tiles, scratch_ref):
    for shift, tile in enumerate(tiles):
        start = pl.multiple_of(chunk_at(place_ref, -shift) * TILE, TILE)
        scratch_ref[pl.ds(start, TILE), :] = tile
    total = scratch_ref[:TILE, :]
    for i in range(1, CHIPS):
        total += scratch_ref[i * TILE : (i + 1) * TILE, :]
    return total


def chunk_product(place_ref, shift, rows, rhs, high_ref, low_ref):
    cut = pl.ds(pl.multiple_of(chunk_at(place_ref, shift) * rows, rows), rows)
    total = dot(high_ref[cut, :], rhs) + dot(low_ref[cut, :], rhs)
    return total


def first_kernel(place_ref, own_ref, core_ref, near_ref, got_ref, *refs):
    sends, (high_ref, low_ref) = refs[:-2], refs[-2:]
    width = own_ref.shape[1]
    rows = own_ref.shape[0] // CHIPS
    for b in range(own_ref.shape[0] // LANES):
        cut = slice(b * LANES, (b + 1) * LANES)
        for s, ref in enumerate((own_ref, core_ref)):
            high, low = split(ref[cut, :])
            high_ref[cut, s * width : (s + 1) * width] = high.astype(BF16)
            low_ref[cut, s * width : (s + 1) * width] = low.astype(BF16)
    z = jnp.concatenate([near_ref[...], got_ref[...]], axis=0)
    rhs = jnp.concatenate(split(z), axis=1).astype(BF16)
    cols = LANES // HALVES
    for shift in range(CHIPS):
        total = chunk_product(place_ref, shift, rows, rhs, high_ref, low_ref)
        y = (total[:, :LANES] + total[:, LANES:]).T
        for h in range(HALVES):
            ref = sends[h * CHIPS + shift]
            store_blocks(ref, y[h * cols : (h + 1) * cols])
            ref[-TILE:, :] = jnp.zeros((TILE, LANES), F32)


def chunk_sum(count, place_ref, refs, scratch_ref):
    cols = LANES // HALVES
    total = refs[0][:-TILE, :]
    for ref in refs[1:]:
        total += ref[:-TILE, :]
    y = wide(total, cols)
    if count is None:
        return y, None
    scale = rms(ordered_tiles(place_ref, [ref[-TILE:, :] for ref in refs], scratch_ref), count)
    return y / to_column(scale[:1], cols), scale


def sum_kernel(count, place_ref, *refs):
    parts, outs, scratch_ref = refs[:CHIPS], refs[CHIPS:-1], refs[-1]
    y, scale = chunk_sum(count, place_ref, parts, scratch_ref)
    store_blocks(outs[0], y)
    outs[0][-TILE:, :] = squares_tile(y)
    if scale is not None:
        outs[1][...] = scale


def z_kernel(place_ref, *refs):
    parts, (high_ref, low_ref, z_ref, scratch_ref) = refs[:CHIPS], refs[CHIPS:]
    cols = LANES // HALVES
    rows = high_ref.shape[0] // CHIPS
    z = None
    for shift, ref in enumerate(parts):
        y = wide(ref[:-TILE, :], cols)
        lhs = jnp.concatenate(split(y), axis=0).astype(BF16)
        cut = pl.ds(pl.multiple_of(chunk_at(place_ref, -shift) * rows, rows), rows)
        term = dot(lhs, high_ref[cut, :]) + dot(lhs, low_ref[cut, :])
        z = term if z is None else z + term
    store_blocks(z_ref, z[:cols] + z[cols:])
    z_ref[-TILE:, :] = ordered_tiles(place_ref, [ref[-TILE:, :] for ref in parts], scratch_ref)


def y_kernel(count, place_ref, a_ref, b_ref, high_ref, low_ref, *refs):
    sends, scale_ref, z_refs = refs[:CHIPS], refs[CHIPS], refs[CHIPS + 1 :]
    cols = LANES // HALVES
    rows = high_ref.shape[0] // CHIPS
    total = a_ref[...] + b_ref[...]
    scale = rms(total[-TILE:], count)
    scale_ref[...] = scale
    z = wide(total[:-TILE], cols) / to_column(scale[:1], cols)
    for z_ref in z_refs:
        store_blocks(z_ref, z)
    tail = squares_tile(z)
    rhs = jnp.concatenate(split(z), axis=0).T.astype(BF16)
    for shift, ref in enumerate(sends):
        y = chunk_product(place_ref, shift, rows, rhs, high_ref, low_ref).T
        store_blocks(ref, y[:cols] + y[cols:])
        ref[-TILE:, :] = tail


def last_kernel(count, place_ref, first_ref, *refs):
    parts, scales = refs[:CHIPS], refs[CHIPS:-3]
    keep_ref, send_ref, scratch_ref = refs[-3:]
    cols = LANES // HALVES
    y, scale = chunk_sum(count, place_ref, parts, scratch_ref)
    middle = (len(scales) + 1) // 2
    row = lax.broadcasted_iota(jnp.int32, (TILE, LANES), 0)
    tail = join_lanes(first_ref[-TILE:, :], squares_tile(y), cols)
    second = [ref[...] for ref in scales[middle:]] + [scale]
    for i, (a_ref, b) in enumerate(zip(scales[:middle], second)):
        tail = jnp.where(row == i, join_lanes(a_ref[...], b, cols), tail)
    zero = place_ref[1] == 0
    blocks = ((first_ref[:cols, :], first_ref[cols : 2 * cols, :]), (y[:, :LANES], y[:, LANES:]))
    for h, (a, b) in enumerate(blocks):
        cut = slice(h * cols, (h + 1) * cols)
        keep_ref[cut, :] = jnp.where(zero, a, b)
        send_ref[cut, :] = jnp.where(zero, b, a)
    keep_ref[-TILE:, :] = tail
    send_ref[-TILE:, :] = tail


def join_kernel(place_ref, keep_ref, got_ref, y_ref, known_ref):
    zero = place_ref[1] == 0
    keep, got = keep_ref[...], got_ref[...]
    for s, x in enumerate((jnp.where(zero, keep, got), jnp.where(zero, got, keep))):
        cut = slice(s * LANES, (s + 1) * LANES)
        y_ref[:, cut] = x[:LANES].T
        known_ref[:, cut] = x[LANES:]


def z_out_kernel(place_ref, first_ref, second_ref, got_first_ref, got_second_ref, known_ref, z_ref):
    cols = LANES // HALVES
    zero = place_ref[1] == 0
    own_rows = first_ref.shape[0] // 2
    mine = jnp.concatenate([wide(ref[:own_rows, :], cols) for ref in (first_ref, second_ref)], axis=0)
    theirs = jnp.concatenate([wide(ref[...], cols) for ref in (got_first_ref, got_second_ref)], axis=0)
    for s, x in enumerate((jnp.where(zero, mine, theirs), jnp.where(zero, theirs, mine))):
        cut = slice(s * LANES, (s + 1) * LANES)
        z_ref[:, cut] = x.T / known_ref[2 * ITERS - 1 : 2 * ITERS, cut]


def q_out_kernel(count, y_ref, known_ref, a_ref, b_ref, q_ref, scale_ref):
    last = 2 * ITERS
    scale = rms((a_ref[...] + b_ref[...])[last : last + 1], count)
    q_ref[...] = y_ref[...] / scale
    scale_ref[:last, :] = known_ref[:last, :]
    scale_ref[last:, :] = scale


def call(kernel, outs, *args, scalars=1, plain=False, tiles=False):
    specs = [pl.BlockSpec(memory_space=pltpu.SMEM)] * scalars
    specs += [pl.BlockSpec(memory_space=pltpu.VMEM)] * (len(args) - scalars)
    out_spec = pl.BlockSpec() if plain else pl.BlockSpec(memory_space=pltpu.VMEM)
    return pl.pallas_call(
        kernel,
        out_shape=[jax.ShapeDtypeStruct(shape, dtype) for shape, dtype in outs],
        in_specs=specs,
        out_specs=[out_spec] * len(outs),
        scratch_shapes=[pltpu.VMEM((CHIPS * TILE, LANES), F32)] if tiles else [],
        compiler_params=pltpu.CompilerParams(vmem_limit_bytes=16 * 1024 * 1024),
    )(*args)


def general(snapshots, sketch):
    high = lax.Precision.HIGHEST
    all_cells = snapshots.shape[0] * lax.axis_size("cell")
    all_snaps = snapshots.shape[1] * lax.axis_size("snap")
    z, scales = sketch, []
    for section in range(ITERS + 1):
        partial = jnp.dot(snapshots, z, precision=high, preferred_element_type=F32)
        y = lax.psum_scatter(partial, "snap", scatter_dimension=0, tiled=True)
        scale = rms(lax.psum(jnp.sum(y * y, axis=0), ("cell", "snap")), all_cells)
        scales.append(scale)
        q = y / scale
        if section < ITERS:
            whole = lax.all_gather(q, "snap", axis=0, tiled=True)
            partial = jnp.dot(snapshots.T, whole, precision=high, preferred_element_type=F32)
            z = lax.psum(partial, "cell")
            scale = rms(lax.psum(jnp.sum(z * z, axis=0), "snap"), all_snaps)
            scales.append(scale)
            z = z / scale
    return q, z, jnp.stack(scales)


def local(snapshots, sketch):
    groups = lax.axis_size("cell")
    places = lax.axis_size("snap")
    rows, width = snapshots.shape
    rank = sketch.shape[1]
    if groups != GROUPS or places != 2 * CHIPS or rank != 2 * LANES or rows % (CHIPS * LANES) or width % LANES:
        return general(snapshots, sketch)
    cols = LANES // HALVES
    all_cells = rows * groups
    all_snaps = width * places
    seat = lax.axis_index("snap")
    core, chip = seat % 2, seat // 2
    place = jnp.stack([chip, core]).astype(jnp.int32)

    def swap(x, bits):
        return lax.ppermute(x, "snap", [(i, i ^ bits) for i in range(places)])

    def shift(x, d):
        return lax.ppermute(x, "snap", [(i, (i + 2 * d) % places) for i in range(places)])

    def swap_cell(x, step):
        def target(cell, i):
            return cell ^ (1 if i % 2 == step else 2)

        perm = [(c * places + i, target(c, i) * places + i) for c in range(groups) for i in range(places)]
        return lax.ppermute(x, ("cell", "snap"), perm)

    def cell_pair(x):
        x = x + swap_cell(x, 0)
        return x, swap_cell(x, 1)

    def scatter(parts):
        return [parts[0]] + [shift(parts[d], d) for d in range(1, CHIPS)]

    def gather(part):
        return [part] + [shift(part, d) for d in range(1, CHIPS)]

    def sketch_half(index):
        return lax.dynamic_slice_in_dim(sketch, index * LANES, LANES, 1)

    chunk_shape = ((cols * rows // CHIPS // LANES + TILE, LANES), F32)
    z_shape = ((cols * 2 * width // LANES + TILE, LANES), F32)
    out_shape = ((cols * 2 * width // LANES, LANES), F32)
    scale_shape = ((TILE, LANES), F32)
    factor = ((rows, 2 * width), BF16)

    *parts, high, low = call(
        first_kernel,
        [chunk_shape] * (HALVES * CHIPS) + [factor, factor],
        place, snapshots, swap(snapshots, 1), sketch_half(core), swap(sketch_half(1 - core), 1),
    )
    sends = [parts[h * CHIPS : (h + 1) * CHIPS] for h in range(HALVES)]
    scales = [[] for _ in range(HALVES)]
    z_parts = [None] * HALVES
    for section in range(ITERS):
        for h in range(HALVES):
            count = all_snaps if section else None
            y, *scale = call(
                functools.partial(sum_kernel, count),
                [chunk_shape] + [scale_shape] * (section > 0),
                place, *scatter(sends[h]), tiles=True,
            )
            scales[h] += scale
            (z,) = call(z_kernel, [z_shape], place, *gather(y), high, low, tiles=True)
            last = section == ITERS - 1
            *sends[h], scale = call(
                functools.partial(y_kernel, all_cells),
                [chunk_shape] * CHIPS + [scale_shape] + [out_shape] * last,
                place, *cell_pair(z), high, low,
            )[: CHIPS + 1 + last]
            if last:
                scale, z_parts[h] = sends[h].pop(), scale
            scales[h].append(scale)

    got_z = [swap(z[z.shape[0] // 2 :], 1) for z in z_parts]
    first, scale = call(
        functools.partial(sum_kernel, all_snaps), [chunk_shape, scale_shape],
        place, *scatter(sends[0]), tiles=True,
    )
    scales[0].append(scale)
    joint = ((LANES + TILE, LANES), F32)
    keep, send = call(
        functools.partial(last_kernel, all_snaps), [joint, joint],
        place, first, *scatter(sends[1]), *scales[0], *scales[1], tiles=True,
    )
    y, known = call(join_kernel, [((LANES, rank), F32), ((TILE, rank), F32)], place, keep, swap(send, 1))
    total = known + swap(known, 2)
    total = total + swap(total, 4)
    a, b = cell_pair(total)
    (z_out,) = call(z_out_kernel, [((width, rank), F32)], place, *z_parts, *got_z, known, plain=True)
    q_out, scale_out = call(
        functools.partial(q_out_kernel, all_cells),
        [((LANES, rank), F32), ((2 * ITERS + 1, rank), F32)],
        y, known, a, b, scalars=0, plain=True,
    )
    return q_out, z_out, scale_out


def solution(mesh):
    return jax.shard_map(
        local,
        mesh=mesh,
        in_specs=(P("cell", "snap"), P("snap", None)),
        out_specs=(P(("cell", "snap"), None), P("snap", None), P()),
        check_vma=False,
    )
```

time: 411 us -> 117 us (0.28)
  waiting for transfers between devices: 225 us -> 26.2 us
  blocking collectives: 146 us -> 0 us
  starting transfers between devices: 0.29 us -> 68.9 us
  Pallas kernels: 0 us -> 18.6 us
  matrix products: 13.8 us -> 0 us
  between operations: 14.2 us -> 0.86 us
  other arithmetic: 7.14 us -> 0.15 us
    psum x5 -> x0, blocking collectives: 146 us -> none  [the longest x3 114 us: scattered_section(): total = lax.psum(jnp.sum(y_raw * y_raw, axis=0), ('cell', 'snap'))]
    reduce_scatter x3 -> x0, waiting for transfers between devices: 93.4 us -> none  [scattered_section(): lax.psum_scatter(jnp.dot(snapshots, z_input, precision=high, preferred_el...]
    psum x2 -> x0, waiting for transfers between devices: 84.8 us -> none  [local(): summed = lax.psum(partial_z, 'cell') / unit_scale]
    ppermute x0 -> x47, starting transfers between devices: none -> 68.9 us  [the longest x30 47 us: shift(): lax.ppermute(x, 'snap', [(i, (i + 2 * d) % places) for i in range(places)])]
    all_gather x2 -> x0, waiting for transfers between devices: 47.1 us -> none  [local(): lax.all_gather(outgoing, 'snap', axis=0, tiled=True)]
    ppermute x0 -> x47, waiting for transfers between devices: none -> 26.2 us  [the longest x10 9.61 us: swap_cell(): return lax.ppermute(x, ('cell', 'snap'), perm)]
    pallas_call x0 -> x18, Pallas kernels: none -> 18.6 us  [call(): pl.pallas_call(kernel, out_shape=[jax.ShapeDtypeStruct(shape, dtype) for...]
    dot_general x5 -> x0, matrix products: 13.8 us -> none  [the longest x3 7.05 us: scattered_section(): jnp.dot(snapshots, z_input, precision=high, preferred_element_type=jnp.fl...]
  transfers between devices with their start and end apart: 7 -> 47, of which waited for: 7 -> 19; matrix products, arithmetic and copies ran while one was open for 0% -> 1% of each run, Pallas kernels for 0% -> 13%
where the time goes in v4:
time: 117 us
  starting transfers between devices  68.9 us (59%)
  waiting for transfers between devices  26.2 us (22%)
  Pallas kernels  18.6 us (16%)
  local copies, waits for them, and re-layouts  2.22 us (2%)
    ppermute x30, starting transfers between devices, shift(): lax.ppermute(x, 'snap', [(i, (i + 2 * d) % places) for i in range(places)])  47 us
    pallas_call x18, Pallas kernels, call(): pl.pallas_call(kernel, out_shape=[jax.ShapeDtypeStruct(shape, dtype) for...  18.6 us
    ppermute x10, starting transfers between devices, swap_cell(): return lax.ppermute(x, ('cell', 'snap'), perm)  17.9 us
    ppermute x10, waiting for transfers between devices, swap_cell(): return lax.ppermute(x, ('cell', 'snap'), perm)  9.61 us
    ppermute x30, waiting for transfers between devices, shift(): lax.ppermute(x, 'snap', [(i, (i + 2 * d) % places) for i in range(places)])  9.06 us
    ppermute x7, waiting for transfers between devices, swap(): return lax.ppermute(x, 'snap', [(i, i ^ bits) for i in range(places)])  7.5 us
    ppermute x7, starting transfers between devices, swap(): return lax.ppermute(x, 'snap', [(i, i ^ bits) for i in range(places)])  3.96 us
  transfers between devices with their start and end apart: 47, of which 19 were waited for; matrix products, arithmetic and copies ran while one was open for 1% of the time, Pallas kernels for 13%

profile of v4, /device:TPU:0, one launch (start us, length us, event | category | flops | bytes accessed | tf_op | source)
XLA Modules:
  0.0 116.8 jit_solution(15600406636242387930)
XLA Ops:
  1.1 1.0 constant_dynamic-slice_fusion
  2.3 1.3 %collective-permute-done.1.got_ref = f32[256,128]{1,0:T(8,128)S(1)} collective-permute-done((f32[256,128]{1,0:T(8,128)S(1)}, f32[256,128]{1,0:T(8,128)S(1)}, u32[]{:S(2)}, u32[]{:S(2)}) %collective-permute-start.1) | collective-permute-done | bytes 131104 | tf_op jit(solution)/shard_map/ppermute | solution.py:266
  3.6 1.2 %copy-done = f32[1024,256]{1,0:T(8,128)S(1)} copy-done((f32[1024,256]{1,0:T(8,128)S(1)}, f32[1024,256]{1,0:T(8,128)}, u32[]{:S(2)}) %copy-start) | copy-done | bytes 1048600
  4.9 1.6 %shard_map.49 = (f32[136,128]{1,0:T(8,128)S(1)}, f32[136,128]{1,0:T(8,128)S(1)}, f32[136,128]{1,0:T(8,128)S(1)}, f32[136,128]{1,0:T(8,128)S(1)}, f32[136,128]{1,...) custom-call(s32[2]{0:T(128)S(1)} %pad_add_fusion.place_ref, ...), custom_call_target="tpu_custom_call" | custom-call | tf_op jit(solution)/shard_map/pallas_call | solution.py:220
  6.5 3.0 %collective-permute-start.2 = (f32[136,128]{1,0:T(8,128)S(1)}, f32[136,128]{1,0:T(8,128)S(1)}, u32[]{:S(2)}, u32[]{:S(2)}) collective-permute-start(f32[136,128]{1,0:T(8,128)S(1)} %get-tuple-element.48), channel_id=1, source_target_pairs={{0,2},{1,3},{2,4},{3,5},{4,6},{5,7},{6,0},{7,1},{8,10},{9,11},{10,... | collective-permute-start | bytes 208904 | tf_op jit(solution)/shard_map/ppermute | solution.py:269
  9.5 2.6 %collective-permute-start.3 = (f32[136,128]{1,0:T(8,128)S(1)}, f32[136,128]{1,0:T(8,128)S(1)}, u32[]{:S(2)}, u32[]{:S(2)}) collective-permute-start(f32[136,128]{1,0:T(8,128)S(1)} %get-tuple-element.49), channel_id=1, source_target_pairs={{0,4},{1,5},{2,6},{3,7},{4,0},{5,1},{6,2},{7,3},{8,12},{9,13},{10,... | collective-permute-start | bytes 208904 | tf_op jit(solution)/shard_map/ppermute | solution.py:269
  12.1 1.3 %collective-permute-start.4 = (f32[136,128]{1,0:T(8,128)S(1)}, f32[136,128]{1,0:T(8,128)S(1)}, u32[]{:S(2)}, u32[]{:S(2)}) collective-permute-start(f32[136,128]{1,0:T(8,128)S(1)} %get-tuple-element.50), channel_id=1, source_target_pairs={{0,6},{1,7},{2,0},{3,1},{4,2},{5,3},{6,4},{7,5},{8,14},{9,15},{10,... | collective-permute-start | bytes 208904 | tf_op jit(solution)/shard_map/ppermute | solution.py:269
  13.4 0.7 collective-permute-start.21
  14.4 2.8 %collective-permute-start.23 = (f32[136,128]{1,0:T(8,128)S(1)}, f32[136,128]{1,0:T(8,128)S(1)}, u32[]{:S(2)}, u32[]{:S(2)}) collective-permute-start(f32[136,128]{1,0:T(8,128)S(1)} %get-tuple-element.66), channel_id=1, source_target_pairs={{0,6},{1,7},{2,0},{3,1},{4,2},{5,3},{6,4},{7,5},{8,14},{9,15},{10,... | collective-permute-start | bytes 208904 | tf_op jit(solution)/shard_map/ppermute | solution.py:269
  17.2 0.8 collective-permute-done.4.refs_3_
  18.7 3.0 %collective-permute-start.7 = (f32[136,128]{1,0:T(8,128)S(1)}, f32[136,128]{1,0:T(8,128)S(1)}, u32[]{:S(2)}, u32[]{:S(2)}) collective-permute-start(f32[136,128]{1,0:T(8,128)S(1)} %shard_map.50.refs_0_), channel_id=1, source_target_pairs={{0,6},{1,7},{2,0},{3,1},{4,2},{5,3},{6,4},{7,5},{8,14},{9,15},{10,... | collective-permute-start | bytes 208904 | tf_op jit(solution)/shard_map/ppermute | solution.py:269
  21.7 2.6 %collective-permute-start.6 = (f32[136,128]{1,0:T(8,128)S(1)}, f32[136,128]{1,0:T(8,128)S(1)}, u32[]{:S(2)}, u32[]{:S(2)}) collective-permute-start(f32[136,128]{1,0:T(8,128)S(1)} %shard_map.50.refs_0_), channel_id=1, source_target_pairs={{0,4},{1,5},{2,6},{3,7},{4,0},{5,1},{6,2},{7,3},{8,12},{9,13},{10,... | collective-permute-start | bytes 208904 | tf_op jit(solution)/shard_map/ppermute | solution.py:269
  24.9 3.9 %collective-permute-start.26 = (f32[136,128]{1,0:T(8,128)S(1)}, f32[136,128]{1,0:T(8,128)S(1)}, u32[]{:S(2)}, u32[]{:S(2)}) collective-permute-start(f32[136,128]{1,0:T(8,128)S(1)} %shard_map.57.refs_0_), channel_id=1, source_target_pairs={{0,6},{1,7},{2,0},{3,1},{4,2},{5,3},{6,4},{7,5},{8,14},{9,15},{10,... | collective-permute-start | bytes 208904 | tf_op jit(solution)/shard_map/ppermute | solution.py:269
  28.9 1.2 %collective-permute-start.24 = (f32[136,128]{1,0:T(8,128)S(1)}, f32[136,128]{1,0:T(8,128)S(1)}, u32[]{:S(2)}, u32[]{:S(2)}) collective-permute-start(f32[136,128]{1,0:T(8,128)S(1)} %shard_map.57.refs_0_), channel_id=1, source_target_pairs={{0,2},{1,3},{2,4},{3,5},{4,6},{5,7},{6,0},{7,1},{8,10},{9,11},{10,... | collective-permute-start | bytes 208904 | tf_op jit(solution)/shard_map/ppermute | solution.py:269
  30.1 3.9 %collective-permute-done.6.refs_2_ = f32[136,128]{1,0:T(8,128)S(1)} collective-permute-done((f32[136,128]{1,0:T(8,128)S(1)}, f32[136,128]{1,0:T(8,128)S(1)}, u32[]{:S(2)}, u32[]{:S(2)}) %collective-permute-start.6) | collective-permute-done | bytes 69664 | tf_op jit(solution)/shard_map/ppermute | solution.py:269
  34.0 1.0 shard_map.51
  35.0 1.6 %collective-permute-start.8 = (f32[264,128]{1,0:T(8,128)S(1)}, f32[264,128]{1,0:T(8,128)S(1)}, u32[]{:S(2)}, u32[]{:S(2)}) collective-permute-start(f32[264,128]{1,0:T(8,128)S(1)} %shard_map.51), channel_id=1, source_target_pairs={{0,8},{1,17},{2,10},{3,19},{4,12},{5,21},{6,14},{7,23},{8,0},{9,25... | collective-permute-start | bytes 405512 | tf_op jit(solution)/shard_map/ppermute | solution.py:276
  36.7 1.0 shard_map.58
  37.7 1.6 %collective-permute-start.27 = (f32[264,128]{1,0:T(8,128)S(1)}, f32[264,128]{1,0:T(8,128)S(1)}, u32[]{:S(2)}, u32[]{:S(2)}) collective-permute-start(f32[264,128]{1,0:T(8,128)S(1)} %shard_map.58), channel_id=1, source_target_pairs={{0,8},{1,17},{2,10},{3,19},{4,12},{5,21},{6,14},{7,23},{8,0},{9,25... | collective-permute-start | bytes 405512 | tf_op jit(solution)/shard_map/ppermute | solution.py:276
  39.2 0.8 collective-permute-done.8
  40.1 2.2 %collective-permute-start.9 = (f32[264,128]{1,0:T(8,128)S(1)}, f32[264,128]{1,0:T(8,128)S(1)}, u32[]{:S(2)}, u32[]{:S(2)}) collective-permute-start(f32[264,128]{1,0:T(8,128)S(1)} %add.35.a_ref), channel_id=1, source_target_pairs={{0,16},{1,9},{2,18},{3,11},{4,20},{5,13},{6,22},{7,15},{8,24},{9,1... | collective-permute-start | bytes 405512 | tf_op jit(solution)/shard_map/ppermute | solution.py:276
  42.3 1.2 %collective-permute-done.27 = f32[264,128]{1,0:T(8,128)S(1)} collective-permute-done((f32[264,128]{1,0:T(8,128)S(1)}, f32[264,128]{1,0:T(8,128)S(1)}, u32[]{:S(2)}, u32[]{:S(2)}) %collective-permute-start.27) | collective-permute-done | bytes 135200 | tf_op jit(solution)/shard_map/ppermute | solution.py:276
  43.6 1.0 collective-permute-start.28
  44.6 0.8 collective-permute-done.9.b_ref
  45.3 1.5 %shard_map.52 = (f32[136,128]{1,0:T(8,128)S(1)}, f32[136,128]{1,0:T(8,128)S(1)}, f32[136,128]{1,0:T(8,128)S(1)}, f32[136,128]{1,0:T(8,128)S(1)}, f32[8,128]{1,0:T(8,128)S(1)}) custom-call(s32[2]{0:T(128)S(1)} %pad_add_fusion.place_ref, f32[264,128]{1,0:T(8,128)S(1)} %add.35.a_ref, f32[264,128]{1,0:T(8,128)S(1)} %collective-permute-done.9.b_ref, ...), custom_call_target="tpu_custom_call" | custom-call | tf_op jit(solution)/shard_map/pallas_call | solution.py:220
  47.0 3.7 %collective-permute-start.12 = (f32[136,128]{1,0:T(8,128)S(1)}, f32[136,128]{1,0:T(8,128)S(1)}, u32[]{:S(2)}, u32[]{:S(2)}) collective-permute-start(f32[136,128]{1,0:T(8,128)S(1)} %get-tuple-element.56), channel_id=1, source_target_pairs={{0,6},{1,7},{2,0},{3,1},{4,2},{5,3},{6,4},{7,5},{8,14},{9,15},{10,... | collective-permute-start | bytes 208904 | tf_op jit(solution)/shard_map/ppermute | solution.py:269
  50.7 1.5 %shard_map.59 = (f32[136,128]{1,0:T(8,128)S(1)}, f32[136,128]{1,0:T(8,128)S(1)}, f32[136,128]{1,0:T(8,128)S(1)}, f32[136,128]{1,0:T(8,128)S(1)}, f32[8,128]{1,0:T(8,128)S(1)}) custom-call(s32[2]{0:T(128)S(1)} %pad_add_fusion.place_ref, f32[264,128]{1,0:T(8,128)S(1)} %add.37.a_ref, f32[264,128]{1,0:T(8,128)S(1)} %collective-permute-done.28.b_ref, ...), custom_call_target="tpu_custom_call" | custom-call | tf_op jit(solution)/shard_map/pallas_call | solution.py:220
  52.8 1.5 %collective-permute-start.30 = (f32[136,128]{1,0:T(8,128)S(1)}, f32[136,128]{1,0:T(8,128)S(1)}, u32[]{:S(2)}, u32[]{:S(2)}) collective-permute-start(f32[136,128]{1,0:T(8,128)S(1)} %get-tuple-element.69), channel_id=1, source_target_pairs={{0,4},{1,5},{2,6},{3,7},{4,0},{5,1},{6,2},{7,3},{8,12},{9,13},{10,... | collective-permute-start | bytes 208904 | tf_op jit(solution)/shard_map/ppermute | solution.py:269
  54.4 2.8 %collective-permute-start.31 = (f32[136,128]{1,0:T(8,128)S(1)}, f32[136,128]{1,0:T(8,128)S(1)}, u32[]{:S(2)}, u32[]{:S(2)}) collective-permute-start(f32[136,128]{1,0:T(8,128)S(1)} %get-tuple-element.70), channel_id=1, source_target_pairs={{0,6},{1,7},{2,0},{3,1},{4,2},{5,3},{6,4},{7,5},{8,14},{9,15},{10,... | collective-permute-start | bytes 208904 | tf_op jit(solution)/shard_map/ppermute | solution.py:269
  57.2 0.7 shard_map.53
  58.0 0.9 collective-permute-start.15
  58.9 1.1 collective-permute-start.14
  60.0 0.9 collective-permute-start.13
  61.3 0.7 shard_map.60
  62.1 3.1 %collective-permute-start.34 = (f32[136,128]{1,0:T(8,128)S(1)}, f32[136,128]{1,0:T(8,128)S(1)}, u32[]{:S(2)}, u32[]{:S(2)}) collective-permute-start(f32[136,128]{1,0:T(8,128)S(1)} %get-tuple-element.71.refs_0_), channel_id=1, source_target_pairs={{0,6},{1,7},{2,0},{3,1},{4,2},{5,3},{6,4},{7,5},{8,14},{9,15},{10,... | collective-permute-start | bytes 208904 | tf_op jit(solution)/shard_map/ppermute | solution.py:269
  65.1 1.0 collective-permute-start.33
  66.1 2.2 %collective-permute-start.32 = (f32[136,128]{1,0:T(8,128)S(1)}, f32[136,128]{1,0:T(8,128)S(1)}, u32[]{:S(2)}, u32[]{:S(2)}) collective-permute-start(f32[136,128]{1,0:T(8,128)S(1)} %get-tuple-element.71.refs_0_), channel_id=1, source_target_pairs={{0,2},{1,3},{2,4},{3,5},{4,6},{5,7},{6,0},{7,1},{8,10},{9,11},{10,... | collective-permute-start | bytes 208904 | tf_op jit(solution)/shard_map/ppermute | solution.py:269
  68.4 1.7 %collective-permute-done.14.refs_2_ = f32[136,128]{1,0:T(8,128)S(1)} collective-permute-done((f32[136,128]{1,0:T(8,128)S(1)}, f32[136,128]{1,0:T(8,128)S(1)}, u32[]{:S(2)}, u32[]{:S(2)}) %collective-permute-start.14) | collective-permute-done | bytes 69664 | tf_op jit(solution)/shard_map/ppermute | solution.py:269
  70.0 1.0 shard_map.54
  71.0 1.6 %collective-permute-start.16 = (f32[264,128]{1,0:T(8,128)S(1)}, f32[264,128]{1,0:T(8,128)S(1)}, u32[]{:S(2)}, u32[]{:S(2)}) collective-permute-start(f32[264,128]{1,0:T(8,128)S(1)} %shard_map.54), channel_id=1, source_target_pairs={{0,8},{1,17},{2,10},{3,19},{4,12},{5,21},{6,14},{7,23},{8,0},{9,25... | collective-permute-start | bytes 405512 | tf_op jit(solution)/shard_map/ppermute | solution.py:276
  72.6 1.0 shard_map.61
  73.6 1.3 %collective-permute-start.35 = (f32[264,128]{1,0:T(8,128)S(1)}, f32[264,128]{1,0:T(8,128)S(1)}, u32[]{:S(2)}, u32[]{:S(2)}) collective-permute-start(f32[264,128]{1,0:T(8,128)S(1)} %shard_map.61), channel_id=1, source_target_pairs={{0,8},{1,17},{2,10},{3,19},{4,12},{5,21},{6,14},{7,23},{8,0},{9,25... | collective-permute-start | bytes 405512 | tf_op jit(solution)/shard_map/ppermute | solution.py:276
  75.0 2.4 %collective-permute-done.16 = f32[264,128]{1,0:T(8,128)S(1)} collective-permute-done((f32[264,128]{1,0:T(8,128)S(1)}, f32[264,128]{1,0:T(8,128)S(1)}, u32[]{:S(2)}, u32[]{:S(2)}) %collective-permute-start.16) | collective-permute-done | bytes 135200 | tf_op jit(solution)/shard_map/ppermute | solution.py:276
  77.3 1.9 %collective-permute-start.17 = (f32[264,128]{1,0:T(8,128)S(1)}, f32[264,128]{1,0:T(8,128)S(1)}, u32[]{:S(2)}, u32[]{:S(2)}) collective-permute-start(f32[264,128]{1,0:T(8,128)S(1)} %add.36.a_ref), channel_id=1, source_target_pairs={{0,16},{1,9},{2,18},{3,11},{4,20},{5,13},{6,22},{7,15},{8,24},{9,1... | collective-permute-start | bytes 405512 | tf_op jit(solution)/shard_map/ppermute | solution.py:276
  79.9 2.8 %collective-permute-start.36 = (f32[264,128]{1,0:T(8,128)S(1)}, f32[264,128]{1,0:T(8,128)S(1)}, u32[]{:S(2)}, u32[]{:S(2)}) collective-permute-start(f32[264,128]{1,0:T(8,128)S(1)} %add.38.a_ref), channel_id=1, source_target_pairs={{0,16},{1,9},{2,18},{3,11},{4,20},{5,13},{6,22},{7,15},{8,24},{9,1... | collective-permute-start | bytes 405512 | tf_op jit(solution)/shard_map/ppermute | solution.py:276
  82.7 1.5 %shard_map.55 = (f32[136,128]{1,0:T(8,128)S(1)}, f32[136,128]{1,0:T(8,128)S(1)}, f32[136,128]{1,0:T(8,128)S(1)}, f32[136,128]{1,0:T(8,128)S(1)}, f32[8,128]{1,0:T(8,128)S(1)}, /*index=5*/f32[256,128]{1,0:T(8,128)S(1)}) custom-call(s32[2]{0:T(128)S(1)} %pad_add_fusion.place_ref, f32[264,128]{1,0:T(8,128)S(1)} %add.36.a_ref, ...), custom_call_target="tpu_custom_call" | custom-call | tf_op jit(solution)/shard_map/pallas_call | solution.py:220
  84.2 1.4 %collective-permute-done.36.b_ref = f32[264,128]{1,0:T(8,128)S(1)} collective-permute-done((f32[264,128]{1,0:T(8,128)S(1)}, f32[264,128]{1,0:T(8,128)S(1)}, u32[]{:S(2)}, u32[]{:S(2)}) %collective-permute-start.36) | collective-permute-done | bytes 135200 | tf_op jit(solution)/shard_map/ppermute | solution.py:276
  85.7 1.5 %shard_map.62 = (f32[136,128]{1,0:T(8,128)S(1)}, f32[136,128]{1,0:T(8,128)S(1)}, f32[136,128]{1,0:T(8,128)S(1)}, f32[136,128]{1,0:T(8,128)S(1)}, f32[8,128]{1,0:T(8,128)S(1)}, /*index=5*/f32[256,128]{1,0:T(8,128)S(1)}) custom-call(s32[2]{0:T(128)S(1)} %pad_add_fusion.place_ref, f32[264,128]{1,0:T(8,128)S(1)} %add.38.a_ref, ...), custom_call_target="tpu_custom_call" | custom-call | tf_op jit(solution)/shard_map/pallas_call | solution.py:220
  87.2 2.9 %collective-permute-start.19 = (f32[136,128]{1,0:T(8,128)S(1)}, f32[136,128]{1,0:T(8,128)S(1)}, u32[]{:S(2)}, u32[]{:S(2)}) collective-permute-start(f32[136,128]{1,0:T(8,128)S(1)} %get-tuple-element.60), channel_id=1, source_target_pairs={{0,4},{1,5},{2,6},{3,7},{4,0},{5,1},{6,2},{7,3},{8,12},{9,13},{10,... | collective-permute-start | bytes 208904 | tf_op jit(solution)/shard_map/ppermute | solution.py:269
  90.2 0.9 collective-permute-start.20
  91.0 2.0 %collective-permute-start.38 = (f32[136,128]{1,0:T(8,128)S(1)}, f32[136,128]{1,0:T(8,128)S(1)}, u32[]{:S(2)}, u32[]{:S(2)}) collective-permute-start(f32[136,128]{1,0:T(8,128)S(1)} %get-tuple-element.74), channel_id=1, source_target_pairs={{0,4},{1,5},{2,6},{3,7},{4,0},{5,1},{6,2},{7,3},{8,12},{9,13},{10,... | collective-permute-start | bytes 208904 | tf_op jit(solution)/shard_map/ppermute | solution.py:269
  93.1 1.5 %collective-permute-start.39 = (f32[136,128]{1,0:T(8,128)S(1)}, f32[136,128]{1,0:T(8,128)S(1)}, u32[]{:S(2)}, u32[]{:S(2)}) collective-permute-start(f32[136,128]{1,0:T(8,128)S(1)} %get-tuple-element.75), channel_id=1, source_target_pairs={{0,6},{1,7},{2,0},{3,1},{4,2},{5,3},{6,4},{7,5},{8,14},{9,15},{10,... | collective-permute-start | bytes 208904 | tf_op jit(solution)/shard_map/ppermute | solution.py:269
  94.6 0.7 shard_map.56
  95.3 1.8 %collective-permute-done.38.refs_2_ = f32[136,128]{1,0:T(8,128)S(1)} collective-permute-done((f32[136,128]{1,0:T(8,128)S(1)}, f32[136,128]{1,0:T(8,128)S(1)}, u32[]{:S(2)}, u32[]{:S(2)}) %collective-permute-start.38) | collective-permute-done | bytes 69664 | tf_op jit(solution)/shard_map/ppermute | solution.py:269
  97.4 0.8 shard_map.63
  100.2 0.9 collective-permute-start.41
  101.1 2.8 %collective-permute-done.41 = f32[8,256]{1,0:T(8,128)S(1)} collective-permute-done((f32[8,256]{1,0:T(8,128)S(1)}, f32[8,256]{1,0:T(8,128)S(1)}, u32[]{:S(2)}, u32[]{:S(2)}) %collective-permute-start.41) | collective-permute-done | bytes 8224 | tf_op jit(solution)/shard_map/ppermute | solution.py:266
  103.9 1.8 %collective-permute-start.42 = (f32[8,256]{1,0:T(8,128)S(1)}, f32[8,256]{1,0:T(8,128)S(1)}, u32[]{:S(2)}, u32[]{:S(2)}) collective-permute-start(f32[8,256]{1,0:T(8,128)S(1)} %add.39), channel_id=1, source_target_pairs={{0,4},{1,5},{2,6},{3,7},{4,0},{5,1},{6,2},{7,3},{8,12},{9,13},{10,... | collective-permute-start | bytes 24584 | tf_op jit(solution)/shard_map/ppermute | solution.py:266
  105.7 2.8 %collective-permute-done.42 = f32[8,256]{1,0:T(8,128)S(1)} collective-permute-done((f32[8,256]{1,0:T(8,128)S(1)}, f32[8,256]{1,0:T(8,128)S(1)}, u32[]{:S(2)}, u32[]{:S(2)}) %collective-permute-start.42) | collective-permute-done | bytes 8224 | tf_op jit(solution)/shard_map/ppermute | solution.py:266
  108.4 1.5 %collective-permute-start.43 = (f32[8,256]{1,0:T(8,128)S(1)}, f32[8,256]{1,0:T(8,128)S(1)}, u32[]{:S(2)}, u32[]{:S(2)}) collective-permute-start(f32[8,256]{1,0:T(8,128)S(1)} %add.40), channel_id=1, source_target_pairs={{0,8},{1,17},{2,10},{3,19},{4,12},{5,21},{6,14},{7,23},{8,0},{9,25... | collective-permute-start | bytes 24584 | tf_op jit(solution)/shard_map/ppermute | solution.py:276
  110.0 2.1 %collective-permute-done.43 = f32[8,256]{1,0:T(8,128)S(1)} collective-permute-done((f32[8,256]{1,0:T(8,128)S(1)}, f32[8,256]{1,0:T(8,128)S(1)}, u32[]{:S(2)}, u32[]{:S(2)}) %collective-permute-start.43) | collective-permute-done | bytes 8224 | tf_op jit(solution)/shard_map/ppermute | solution.py:276
  112.1 2.4 %collective-permute-start.44 = (f32[8,256]{1,0:T(8,128)S(1)}, f32[8,256]{1,0:T(8,128)S(1)}, u32[]{:S(2)}, u32[]{:S(2)}) collective-permute-start(f32[8,256]{1,0:T(8,128)S(1)} %add.41.a_ref), channel_id=1, source_target_pairs={{0,16},{1,9},{2,18},{3,11},{4,20},{5,13},{6,22},{7,15},{8,24},{9,1... | collective-permute-start | bytes 24584 | tf_op jit(solution)/shard_map/ppermute | solution.py:276
  114.5 1.4 %shard_map.66 = f32[256,256]{1,0:T(8,128)} custom-call(s32[2]{0:T(128)S(1)} %pad_add_fusion.place_ref, f32[256,128]{1,0:T(8,128)S(1)} %get-tuple-element.88.first_ref, f32[256,128]{1,0:T(8,128)S(1)} %get-tuple-element.89.second_ref, f32[128,128]{1,0:T(8,128)S(1)} %collective-permute-done.45.got_first_ref, ...), custom_call_target="tpu_custom_call" | custom-call | tf_op jit(solution)/shard_map/pallas_call | solution.py:220
  116.2 0.7 shard_map.65
  (61 shorter events, 7.0 us)
Async XLA Ops:
  0.6 3.0 %collective-permute-start = (f32[1024,256]{1,0:T(8,128)}, f32[1024,256]{1,0:T(8,128)S(1)}, u32[]{:S(2)}, u32[]{:S(2)}) collective-permute-start(f32[1024,256]{1,0:T(8,128)} %own_ref.1), channel_id=1, source_target_pairs={{0,1},{1,0},{2,3},{3,2},{4,5},{5,4},{6,7},{7,6},{8,9},{9,8},{10,11... | collective-permute-start | bytes 3145736 | tf_op jit(solution)/shard_map/ppermute | solution.py:266
  2.1 1.5 %collective-permute-start.1 = (f32[256,128]{1,0:T(8,128)S(1)}, f32[256,128]{1,0:T(8,128)S(1)}, u32[]{:S(2)}, u32[]{:S(2)}) collective-permute-start(f32[256,128]{1,0:T(8,128)S(1)} %get-tuple-element.91), channel_id=1, source_target_pairs={{0,1},{1,0},{2,3},{3,2},{4,5},{5,4},{6,7},{7,6},{8,9},{9,8},{10,11... | collective-permute-start | bytes 393224 | tf_op jit(solution)/shard_map/ppermute | solution.py:266
  3.6 1.2 %copy-start = (f32[1024,256]{1,0:T(8,128)S(1)}, f32[1024,256]{1,0:T(8,128)}, u32[]{:S(2)}) copy-start(f32[1024,256]{1,0:T(8,128)} %own_ref.1) | copy-start | bytes 3145732
  6.5 7.9 %collective-permute-start.2 = (f32[136,128]{1,0:T(8,128)S(1)}, f32[136,128]{1,0:T(8,128)S(1)}, u32[]{:S(2)}, u32[]{:S(2)}) collective-permute-start(f32[136,128]{1,0:T(8,128)S(1)} %get-tuple-element.48), channel_id=1, source_target_pairs={{0,2},{1,3},{2,4},{3,5},{4,6},{5,7},{6,0},{7,1},{8,10},{9,11},{10,... | collective-permute-start | bytes 208904 | tf_op jit(solution)/shard_map/ppermute | solution.py:269
  9.5 7.8 %collective-permute-start.3 = (f32[136,128]{1,0:T(8,128)S(1)}, f32[136,128]{1,0:T(8,128)S(1)}, u32[]{:S(2)}, u32[]{:S(2)}) collective-permute-start(f32[136,128]{1,0:T(8,128)S(1)} %get-tuple-element.49), channel_id=1, source_target_pairs={{0,4},{1,5},{2,6},{3,7},{4,0},{5,1},{6,2},{7,3},{8,12},{9,13},{10,... | collective-permute-start | bytes 208904 | tf_op jit(solution)/shard_map/ppermute | solution.py:269
  12.1 6.0 %collective-permute-start.4 = (f32[136,128]{1,0:T(8,128)S(1)}, f32[136,128]{1,0:T(8,128)S(1)}, u32[]{:S(2)}, u32[]{:S(2)}) collective-permute-start(f32[136,128]{1,0:T(8,128)S(1)} %get-tuple-element.50), channel_id=1, source_target_pairs={{0,6},{1,7},{2,0},{3,1},{4,2},{5,3},{6,4},{7,5},{8,14},{9,15},{10,... | collective-permute-start | bytes 208904 | tf_op jit(solution)/shard_map/ppermute | solution.py:269
  13.4 10.9 %collective-permute-start.21 = (f32[136,128]{1,0:T(8,128)S(1)}, f32[136,128]{1,0:T(8,128)S(1)}, u32[]{:S(2)}, u32[]{:S(2)}) collective-permute-start(f32[136,128]{1,0:T(8,128)S(1)} %get-tuple-element.64), channel_id=1, source_target_pairs={{0,2},{1,3},{2,4},{3,5},{4,6},{5,7},{6,0},{7,1},{8,10},{9,11},{10,... | collective-permute-start | bytes 208904 | tf_op jit(solution)/shard_map/ppermute | solution.py:269
  14.1 10.2 %collective-permute-start.22 = (f32[136,128]{1,0:T(8,128)S(1)}, f32[136,128]{1,0:T(8,128)S(1)}, u32[]{:S(2)}, u32[]{:S(2)}) collective-permute-start(f32[136,128]{1,0:T(8,128)S(1)} %get-tuple-element.65), channel_id=1, source_target_pairs={{0,4},{1,5},{2,6},{3,7},{4,0},{5,1},{6,2},{7,3},{8,12},{9,13},{10,... | collective-permute-start | bytes 208904 | tf_op jit(solution)/shard_map/ppermute | solution.py:269
  14.4 9.9 %collective-permute-start.23 = (f32[136,128]{1,0:T(8,128)S(1)}, f32[136,128]{1,0:T(8,128)S(1)}, u32[]{:S(2)}, u32[]{:S(2)}) collective-permute-start(f32[136,128]{1,0:T(8,128)S(1)} %get-tuple-element.66), channel_id=1, source_target_pairs={{0,6},{1,7},{2,0},{3,1},{4,2},{5,3},{6,4},{7,5},{8,14},{9,15},{10,... | collective-permute-start | bytes 208904 | tf_op jit(solution)/shard_map/ppermute | solution.py:269
  18.7 10.2 %collective-permute-start.7 = (f32[136,128]{1,0:T(8,128)S(1)}, f32[136,128]{1,0:T(8,128)S(1)}, u32[]{:S(2)}, u32[]{:S(2)}) collective-permute-start(f32[136,128]{1,0:T(8,128)S(1)} %shard_map.50.refs_0_), channel_id=1, source_target_pairs={{0,6},{1,7},{2,0},{3,1},{4,2},{5,3},{6,4},{7,5},{8,14},{9,15},{10,... | collective-permute-start | bytes 208904 | tf_op jit(solution)/shard_map/ppermute | solution.py:269
  21.7 12.3 %collective-permute-start.6 = (f32[136,128]{1,0:T(8,128)S(1)}, f32[136,128]{1,0:T(8,128)S(1)}, u32[]{:S(2)}, u32[]{:S(2)}) collective-permute-start(f32[136,128]{1,0:T(8,128)S(1)} %shard_map.50.refs_0_), channel_id=1, source_target_pairs={{0,4},{1,5},{2,6},{3,7},{4,0},{5,1},{6,2},{7,3},{8,12},{9,13},{10,... | collective-permute-start | bytes 208904 | tf_op jit(solution)/shard_map/ppermute | solution.py:269
  24.3 9.7 %collective-permute-start.5 = (f32[136,128]{1,0:T(8,128)S(1)}, f32[136,128]{1,0:T(8,128)S(1)}, u32[]{:S(2)}, u32[]{:S(2)}) collective-permute-start(f32[136,128]{1,0:T(8,128)S(1)} %shard_map.50.refs_0_), channel_id=1, source_target_pairs={{0,2},{1,3},{2,4},{3,5},{4,6},{5,7},{6,0},{7,1},{8,10},{9,11},{10,... | collective-permute-start | bytes 208904 | tf_op jit(solution)/shard_map/ppermute | solution.py:269
  24.9 11.6 %collective-permute-start.26 = (f32[136,128]{1,0:T(8,128)S(1)}, f32[136,128]{1,0:T(8,128)S(1)}, u32[]{:S(2)}, u32[]{:S(2)}) collective-permute-start(f32[136,128]{1,0:T(8,128)S(1)} %shard_map.57.refs_0_), channel_id=1, source_target_pairs={{0,6},{1,7},{2,0},{3,1},{4,2},{5,3},{6,4},{7,5},{8,14},{9,15},{10,... | collective-permute-start | bytes 208904 | tf_op jit(solution)/shard_map/ppermute | solution.py:269
  28.9 7.8 %collective-permute-start.25 = (f32[136,128]{1,0:T(8,128)S(1)}, f32[136,128]{1,0:T(8,128)S(1)}, u32[]{:S(2)}, u32[]{:S(2)}) collective-permute-start(f32[136,128]{1,0:T(8,128)S(1)} %shard_map.57.refs_0_), channel_id=1, source_target_pairs={{0,4},{1,5},{2,6},{3,7},{4,0},{5,1},{6,2},{7,3},{8,12},{9,13},{10,... | collective-permute-start | bytes 208904 | tf_op jit(solution)/shard_map/ppermute | solution.py:269
  28.9 7.8 %collective-permute-start.24 = (f32[136,128]{1,0:T(8,128)S(1)}, f32[136,128]{1,0:T(8,128)S(1)}, u32[]{:S(2)}, u32[]{:S(2)}) collective-permute-start(f32[136,128]{1,0:T(8,128)S(1)} %shard_map.57.refs_0_), channel_id=1, source_target_pairs={{0,2},{1,3},{2,4},{3,5},{4,6},{5,7},{6,0},{7,1},{8,10},{9,11},{10,... | collective-permute-start | bytes 208904 | tf_op jit(solution)/shard_map/ppermute | solution.py:269
  35.0 5.1 %collective-permute-start.8 = (f32[264,128]{1,0:T(8,128)S(1)}, f32[264,128]{1,0:T(8,128)S(1)}, u32[]{:S(2)}, u32[]{:S(2)}) collective-permute-start(f32[264,128]{1,0:T(8,128)S(1)} %shard_map.51), channel_id=1, source_target_pairs={{0,8},{1,17},{2,10},{3,19},{4,12},{5,21},{6,14},{7,23},{8,0},{9,25... | collective-permute-start | bytes 405512 | tf_op jit(solution)/shard_map/ppermute | solution.py:276
  37.7 5.9 %collective-permute-start.27 = (f32[264,128]{1,0:T(8,128)S(1)}, f32[264,128]{1,0:T(8,128)S(1)}, u32[]{:S(2)}, u32[]{:S(2)}) collective-permute-start(f32[264,128]{1,0:T(8,128)S(1)} %shard_map.58), channel_id=1, source_target_pairs={{0,8},{1,17},{2,10},{3,19},{4,12},{5,21},{6,14},{7,23},{8,0},{9,25... | collective-permute-start | bytes 405512 | tf_op jit(solution)/shard_map/ppermute | solution.py:276
  40.1 5.2 %collective-permute-start.9 = (f32[264,128]{1,0:T(8,128)S(1)}, f32[264,128]{1,0:T(8,128)S(1)}, u32[]{:S(2)}, u32[]{:S(2)}) collective-permute-start(f32[264,128]{1,0:T(8,128)S(1)} %add.35.a_ref), channel_id=1, source_target_pairs={{0,16},{1,9},{2,18},{3,11},{4,20},{5,13},{6,22},{7,15},{8,24},{9,1... | collective-permute-start | bytes 405512 | tf_op jit(solution)/shard_map/ppermute | solution.py:276
  43.6 7.1 %collective-permute-start.28 = (f32[264,128]{1,0:T(8,128)S(1)}, f32[264,128]{1,0:T(8,128)S(1)}, u32[]{:S(2)}, u32[]{:S(2)}) collective-permute-start(f32[264,128]{1,0:T(8,128)S(1)} %add.37.a_ref), channel_id=1, source_target_pairs={{0,16},{1,9},{2,18},{3,11},{4,20},{5,13},{6,22},{7,15},{8,24},{9,1... | collective-permute-start | bytes 405512 | tf_op jit(solution)/shard_map/ppermute | solution.py:276
  46.8 7.5 %collective-permute-start.10 = (f32[136,128]{1,0:T(8,128)S(1)}, f32[136,128]{1,0:T(8,128)S(1)}, u32[]{:S(2)}, u32[]{:S(2)}) collective-permute-start(f32[136,128]{1,0:T(8,128)S(1)} %get-tuple-element.54), channel_id=1, source_target_pairs={{0,2},{1,3},{2,4},{3,5},{4,6},{5,7},{6,0},{7,1},{8,10},{9,11},{10,... | collective-permute-start | bytes 208904 | tf_op jit(solution)/shard_map/ppermute | solution.py:269
  46.9 10.3 %collective-permute-start.11 = (f32[136,128]{1,0:T(8,128)S(1)}, f32[136,128]{1,0:T(8,128)S(1)}, u32[]{:S(2)}, u32[]{:S(2)}) collective-permute-start(f32[136,128]{1,0:T(8,128)S(1)} %get-tuple-element.55), channel_id=1, source_target_pairs={{0,4},{1,5},{2,6},{3,7},{4,0},{5,1},{6,2},{7,3},{8,12},{9,13},{10,... | collective-permute-start | bytes 208904 | tf_op jit(solution)/shard_map/ppermute | solution.py:269
  47.0 10.3 %collective-permute-start.12 = (f32[136,128]{1,0:T(8,128)S(1)}, f32[136,128]{1,0:T(8,128)S(1)}, u32[]{:S(2)}, u32[]{:S(2)}) collective-permute-start(f32[136,128]{1,0:T(8,128)S(1)} %get-tuple-element.56), channel_id=1, source_target_pairs={{0,6},{1,7},{2,0},{3,1},{4,2},{5,3},{6,4},{7,5},{8,14},{9,15},{10,... | collective-permute-start | bytes 208904 | tf_op jit(solution)/shard_map/ppermute | solution.py:269
  52.2 7.8 %collective-permute-start.29 = (f32[136,128]{1,0:T(8,128)S(1)}, f32[136,128]{1,0:T(8,128)S(1)}, u32[]{:S(2)}, u32[]{:S(2)}) collective-permute-start(f32[136,128]{1,0:T(8,128)S(1)} %get-tuple-element.68), channel_id=1, source_target_pairs={{0,2},{1,3},{2,4},{3,5},{4,6},{5,7},{6,0},{7,1},{8,10},{9,11},{10,... | collective-permute-start | bytes 208904 | tf_op jit(solution)/shard_map/ppermute | solution.py:269
  52.8 8.5 %collective-permute-start.30 = (f32[136,128]{1,0:T(8,128)S(1)}, f32[136,128]{1,0:T(8,128)S(1)}, u32[]{:S(2)}, u32[]{:S(2)}) collective-permute-start(f32[136,128]{1,0:T(8,128)S(1)} %get-tuple-element.69), channel_id=1, source_target_pairs={{0,4},{1,5},{2,6},{3,7},{4,0},{5,1},{6,2},{7,3},{8,12},{9,13},{10,... | collective-permute-start | bytes 208904 | tf_op jit(solution)/shard_map/ppermute | solution.py:269
  54.4 7.0 %collective-permute-start.31 = (f32[136,128]{1,0:T(8,128)S(1)}, f32[136,128]{1,0:T(8,128)S(1)}, u32[]{:S(2)}, u32[]{:S(2)}) collective-permute-start(f32[136,128]{1,0:T(8,128)S(1)} %get-tuple-element.70), channel_id=1, source_target_pairs={{0,6},{1,7},{2,0},{3,1},{4,2},{5,3},{6,4},{7,5},{8,14},{9,15},{10,... | collective-permute-start | bytes 208904 | tf_op jit(solution)/shard_map/ppermute | solution.py:269
  58.0 8.2 %collective-permute-start.15 = (f32[136,128]{1,0:T(8,128)S(1)}, f32[136,128]{1,0:T(8,128)S(1)}, u32[]{:S(2)}, u32[]{:S(2)}) collective-permute-start(f32[136,128]{1,0:T(8,128)S(1)} %get-tuple-element.57.refs_0_), channel_id=1, source_target_pairs={{0,6},{1,7},{2,0},{3,1},{4,2},{5,3},{6,4},{7,5},{8,14},{9,15},{10,... | collective-permute-start | bytes 208904 | tf_op jit(solution)/shard_map/ppermute | solution.py:269
  58.9 11.1 %collective-permute-start.14 = (f32[136,128]{1,0:T(8,128)S(1)}, f32[136,128]{1,0:T(8,128)S(1)}, u32[]{:S(2)}, u32[]{:S(2)}) collective-permute-start(f32[136,128]{1,0:T(8,128)S(1)} %get-tuple-element.57.refs_0_), channel_id=1, source_target_pairs={{0,4},{1,5},{2,6},{3,7},{4,0},{5,1},{6,2},{7,3},{8,12},{9,13},{10,... | collective-permute-start | bytes 208904 | tf_op jit(solution)/shard_map/ppermute | solution.py:269
  60.0 10.0 %collective-permute-start.13 = (f32[136,128]{1,0:T(8,128)S(1)}, f32[136,128]{1,0:T(8,128)S(1)}, u32[]{:S(2)}, u32[]{:S(2)}) collective-permute-start(f32[136,128]{1,0:T(8,128)S(1)} %get-tuple-element.57.refs_0_), channel_id=1, source_target_pairs={{0,2},{1,3},{2,4},{3,5},{4,6},{5,7},{6,0},{7,1},{8,10},{9,11},{10,... | collective-permute-start | bytes 208904 | tf_op jit(solution)/shard_map/ppermute | solution.py:269
  62.1 10.5 %collective-permute-start.34 = (f32[136,128]{1,0:T(8,128)S(1)}, f32[136,128]{1,0:T(8,128)S(1)}, u32[]{:S(2)}, u32[]{:S(2)}) collective-permute-start(f32[136,128]{1,0:T(8,128)S(1)} %get-tuple-element.71.refs_0_), channel_id=1, source_target_pairs={{0,6},{1,7},{2,0},{3,1},{4,2},{5,3},{6,4},{7,5},{8,14},{9,15},{10,... | collective-permute-start | bytes 208904 | tf_op jit(solution)/shard_map/ppermute | solution.py:269
  65.1 7.5 %collective-permute-start.33 = (f32[136,128]{1,0:T(8,128)S(1)}, f32[136,128]{1,0:T(8,128)S(1)}, u32[]{:S(2)}, u32[]{:S(2)}) collective-permute-start(f32[136,128]{1,0:T(8,128)S(1)} %get-tuple-element.71.refs_0_), channel_id=1, source_target_pairs={{0,4},{1,5},{2,6},{3,7},{4,0},{5,1},{6,2},{7,3},{8,12},{9,13},{10,... | collective-permute-start | bytes 208904 | tf_op jit(solution)/shard_map/ppermute | solution.py:269
  66.1 6.5 %collective-permute-start.32 = (f32[136,128]{1,0:T(8,128)S(1)}, f32[136,128]{1,0:T(8,128)S(1)}, u32[]{:S(2)}, u32[]{:S(2)}) collective-permute-start(f32[136,128]{1,0:T(8,128)S(1)} %get-tuple-element.71.refs_0_), channel_id=1, source_target_pairs={{0,2},{1,3},{2,4},{3,5},{4,6},{5,7},{6,0},{7,1},{8,10},{9,11},{10,... | collective-permute-start | bytes 208904 | tf_op jit(solution)/shard_map/ppermute | solution.py:269
  71.0 6.3 %collective-permute-start.16 = (f32[264,128]{1,0:T(8,128)S(1)}, f32[264,128]{1,0:T(8,128)S(1)}, u32[]{:S(2)}, u32[]{:S(2)}) collective-permute-start(f32[264,128]{1,0:T(8,128)S(1)} %shard_map.54), channel_id=1, source_target_pairs={{0,8},{1,17},{2,10},{3,19},{4,12},{5,21},{6,14},{7,23},{8,0},{9,25... | collective-permute-start | bytes 405512 | tf_op jit(solution)/shard_map/ppermute | solution.py:276
  73.6 6.3 %collective-permute-start.35 = (f32[264,128]{1,0:T(8,128)S(1)}, f32[264,128]{1,0:T(8,128)S(1)}, u32[]{:S(2)}, u32[]{:S(2)}) collective-permute-start(f32[264,128]{1,0:T(8,128)S(1)} %shard_map.61), channel_id=1, source_target_pairs={{0,8},{1,17},{2,10},{3,19},{4,12},{5,21},{6,14},{7,23},{8,0},{9,25... | collective-permute-start | bytes 405512 | tf_op jit(solution)/shard_map/ppermute | solution.py:276
  77.3 5.3 %collective-permute-start.17 = (f32[264,128]{1,0:T(8,128)S(1)}, f32[264,128]{1,0:T(8,128)S(1)}, u32[]{:S(2)}, u32[]{:S(2)}) collective-permute-start(f32[264,128]{1,0:T(8,128)S(1)} %add.36.a_ref), channel_id=1, source_target_pairs={{0,16},{1,9},{2,18},{3,11},{4,20},{5,13},{6,22},{7,15},{8,24},{9,1... | collective-permute-start | bytes 405512 | tf_op jit(solution)/shard_map/ppermute | solution.py:276
  79.9 5.8 %collective-permute-start.36 = (f32[264,128]{1,0:T(8,128)S(1)}, f32[264,128]{1,0:T(8,128)S(1)}, u32[]{:S(2)}, u32[]{:S(2)}) collective-permute-start(f32[264,128]{1,0:T(8,128)S(1)} %add.38.a_ref), channel_id=1, source_target_pairs={{0,16},{1,9},{2,18},{3,11},{4,20},{5,13},{6,22},{7,15},{8,24},{9,1... | collective-permute-start | bytes 405512 | tf_op jit(solution)/shard_map/ppermute | solution.py:276
  84.2 8.9 %collective-permute-start.18 = (f32[136,128]{1,0:T(8,128)S(1)}, f32[136,128]{1,0:T(8,128)S(1)}, u32[]{:S(2)}, u32[]{:S(2)}) collective-permute-start(f32[136,128]{1,0:T(8,128)S(1)} %get-tuple-element.59), channel_id=1, source_target_pairs={{0,2},{1,3},{2,4},{3,5},{4,6},{5,7},{6,0},{7,1},{8,10},{9,11},{10,... | collective-permute-start | bytes 208904 | tf_op jit(solution)/shard_map/ppermute | solution.py:269
  87.2 8.2 %collective-permute-start.37 = (f32[136,128]{1,0:T(8,128)S(1)}, f32[136,128]{1,0:T(8,128)S(1)}, u32[]{:S(2)}, u32[]{:S(2)}) collective-permute-start(f32[136,128]{1,0:T(8,128)S(1)} %get-tuple-element.73), channel_id=1, source_target_pairs={{0,2},{1,3},{2,4},{3,5},{4,6},{5,7},{6,0},{7,1},{8,10},{9,11},{10,... | collective-permute-start | bytes 208904 | tf_op jit(solution)/shard_map/ppermute | solution.py:269
  87.2 7.3 %collective-permute-start.19 = (f32[136,128]{1,0:T(8,128)S(1)}, f32[136,128]{1,0:T(8,128)S(1)}, u32[]{:S(2)}, u32[]{:S(2)}) collective-permute-start(f32[136,128]{1,0:T(8,128)S(1)} %get-tuple-element.60), channel_id=1, source_target_pairs={{0,4},{1,5},{2,6},{3,7},{4,0},{5,1},{6,2},{7,3},{8,12},{9,13},{10,... | collective-permute-start | bytes 208904 | tf_op jit(solution)/shard_map/ppermute | solution.py:269
  90.2 4.4 %collective-permute-start.20 = (f32[136,128]{1,0:T(8,128)S(1)}, f32[136,128]{1,0:T(8,128)S(1)}, u32[]{:S(2)}, u32[]{:S(2)}) collective-permute-start(f32[136,128]{1,0:T(8,128)S(1)} %get-tuple-element.61), channel_id=1, source_target_pairs={{0,6},{1,7},{2,0},{3,1},{4,2},{5,3},{6,4},{7,5},{8,14},{9,15},{10,... | collective-permute-start | bytes 208904 | tf_op jit(solution)/shard_map/ppermute | solution.py:269
  91.0 6.1 %collective-permute-start.38 = (f32[136,128]{1,0:T(8,128)S(1)}, f32[136,128]{1,0:T(8,128)S(1)}, u32[]{:S(2)}, u32[]{:S(2)}) collective-permute-start(f32[136,128]{1,0:T(8,128)S(1)} %get-tuple-element.74), channel_id=1, source_target_pairs={{0,4},{1,5},{2,6},{3,7},{4,0},{5,1},{6,2},{7,3},{8,12},{9,13},{10,... | collective-permute-start | bytes 208904 | tf_op jit(solution)/shard_map/ppermute | solution.py:269
  93.1 4.4 %collective-permute-start.39 = (f32[136,128]{1,0:T(8,128)S(1)}, f32[136,128]{1,0:T(8,128)S(1)}, u32[]{:S(2)}, u32[]{:S(2)}) collective-permute-start(f32[136,128]{1,0:T(8,128)S(1)} %get-tuple-element.75), channel_id=1, source_target_pairs={{0,6},{1,7},{2,0},{3,1},{4,2},{5,3},{6,4},{7,5},{8,14},{9,15},{10,... | collective-permute-start | bytes 208904 | tf_op jit(solution)/shard_map/ppermute | solution.py:269
  98.2 1.3 %collective-permute-start.40 = (f32[136,128]{1,0:T(8,128)S(1)}, f32[136,128]{1,0:T(8,128)S(1)}, u32[]{:S(2)}, u32[]{:S(2)}) collective-permute-start(f32[136,128]{1,0:T(8,128)S(1)} %get-tuple-element.84), channel_id=1, source_target_pairs={{0,1},{1,0},{2,3},{3,2},{4,5},{5,4},{6,7},{7,6},{8,9},{9,8},{10,11... | collective-permute-start | bytes 208904 | tf_op jit(solution)/shard_map/ppermute | solution.py:266
  98.3 16.2 %collective-permute-start.46 = (f32[128,128]{1,0:T(8,128)S(1)}, f32[128,128]{1,0:T(8,128)S(1)}, u32[]{:S(2)}, u32[]{:S(2)}) collective-permute-start(f32[128,128]{1,0:T(8,128)S(1)} %slice.7), channel_id=1, source_target_pairs={{0,1},{1,0},{2,3},{3,2},{4,5},{5,4},{6,7},{7,6},{8,9},{9,8},{10,11... | collective-permute-start | bytes 196616 | tf_op jit(solution)/shard_map/ppermute | solution.py:266
  98.8 15.8 %collective-permute-start.45 = (f32[128,128]{1,0:T(8,128)S(1)}, f32[128,128]{1,0:T(8,128)S(1)}, u32[]{:S(2)}, u32[]{:S(2)}) collective-permute-start(f32[128,128]{1,0:T(8,128)S(1)} %slice.6), channel_id=1, source_target_pairs={{0,1},{1,0},{2,3},{3,2},{4,5},{5,4},{6,7},{7,6},{8,9},{9,8},{10,11... | collective-permute-start | bytes 196616 | tf_op jit(solution)/shard_map/ppermute | solution.py:266
  100.2 3.7 %collective-permute-start.41 = (f32[8,256]{1,0:T(8,128)S(1)}, f32[8,256]{1,0:T(8,128)S(1)}, u32[]{:S(2)}, u32[]{:S(2)}) collective-permute-start(f32[8,256]{1,0:T(8,128)S(1)} %get-tuple-element.86.known_ref), channel_id=1, source_target_pairs={{0,2},{1,3},{2,0},{3,1},{4,6},{5,7},{6,4},{7,5},{8,10},{9,11},{10,... | collective-permute-start | bytes 24584 | tf_op jit(solution)/shard_map/ppermute | solution.py:266
  103.9 4.5 %collective-permute-start.42 = (f32[8,256]{1,0:T(8,128)S(1)}, f32[8,256]{1,0:T(8,128)S(1)}, u32[]{:S(2)}, u32[]{:S(2)}) collective-permute-start(f32[8,256]{1,0:T(8,128)S(1)} %add.39), channel_id=1, source_target_pairs={{0,4},{1,5},{2,6},{3,7},{4,0},{5,1},{6,2},{7,3},{8,12},{9,13},{10,... | collective-permute-start | bytes 24584 | tf_op jit(solution)/shard_map/ppermute | solution.py:266
  108.4 3.7 %collective-permute-start.43 = (f32[8,256]{1,0:T(8,128)S(1)}, f32[8,256]{1,0:T(8,128)S(1)}, u32[]{:S(2)}, u32[]{:S(2)}) collective-permute-start(f32[8,256]{1,0:T(8,128)S(1)} %add.40), channel_id=1, source_target_pairs={{0,8},{1,17},{2,10},{3,19},{4,12},{5,21},{6,14},{7,23},{8,0},{9,25... | collective-permute-start | bytes 24584 | tf_op jit(solution)/shard_map/ppermute | solution.py:276
  112.1 4.0 %collective-permute-start.44 = (f32[8,256]{1,0:T(8,128)S(1)}, f32[8,256]{1,0:T(8,128)S(1)}, u32[]{:S(2)}, u32[]{:S(2)}) collective-permute-start(f32[8,256]{1,0:T(8,128)S(1)} %add.41.a_ref), channel_id=1, source_target_pairs={{0,16},{1,9},{2,18},{3,11},{4,20},{5,13},{6,22},{7,15},{8,24},{9,1... | collective-permute-start | bytes 24584 | tf_op jit(solution)/shard_map/ppermute | solution.py:276

commit v5 on v0

v5 whole, which is shorter than its diff:
```python
import functools

import jax
import jax.numpy as jnp
from jax import lax
from jax.experimental import pallas as pl
from jax.experimental.pallas import tpu as pltpu
from jax.sharding import PartitionSpec as P

ITERS = 2
EPS = 1e-05
LANES = 128
TILE = 8
HALVES = 2
QUARTER = 64
COLS = QUARTER // HALVES
SHARES = (3, 1)
BF16 = jnp.bfloat16
F32 = jnp.float32


def split(x):
    high = x.astype(BF16).astype(F32)
    return high, x - high


def dot(a, b):
    return lax.dot_general(a, b, (((1,), (0,)), ((), ())), preferred_element_type=F32)


def eye(cols):
    shape = (cols, LANES)
    return lax.broadcasted_iota(jnp.int32, shape, 0) == lax.broadcasted_iota(jnp.int32, shape, 1)


def to_column(row, cols):
    return jnp.sum(jnp.where(eye(cols), row, 0.0), axis=1, keepdims=True)


def to_row(column):
    return jnp.sum(jnp.where(eye(column.shape[0]), column, 0.0), axis=0, keepdims=True)


def squares_tile(x):
    row = to_row(jnp.sum(x * x, axis=1, keepdims=True))
    return jnp.broadcast_to(row, (TILE, LANES))


def rms(total, count):
    return jnp.sqrt(total / count + EPS)


def wide(x, cols):
    return jnp.concatenate([x[j * cols : (j + 1) * cols] for j in range(x.shape[0] // cols)], axis=1)


def store_blocks(ref, start, x):
    cols = x.shape[0]
    for j in range(x.shape[1] // LANES):
        ref[start + j * cols : start + (j + 1) * cols, :] = x[:, j * LANES : (j + 1) * LANES]


def turn(x, cols):
    return pltpu.roll(x, cols, 1)


def join_lanes(first, second, cols):
    left = lax.broadcasted_iota(jnp.int32, first.shape, 1) < cols
    return jnp.where(left, first, turn(second, cols))


def unfold(total):
    cols = total.shape[0] // 2
    return total[:cols] + total[cols:]


def sketch_side(place_ref, x):
    x = jnp.where(place_ref[0] == 0, x, turn(x, QUARTER))
    return join_lanes(*split(x), QUARTER).astype(BF16)


def store_factors(high_ref, low_ref, blocks):
    for s, block in enumerate(blocks):
        high, low = split(block)
        cut = slice(s * block.shape[1], (s + 1) * block.shape[1])
        high_ref[:, cut] = high.astype(BF16)
        low_ref[:, cut] = low.astype(BF16)


def prepare_kernel(place_ref, sketch_ref, a_ref, mine_ref, first_ref, sem):
    lead = sketch_ref.shape[0] // 2
    count = first_ref.shape[0] - lead
    copy = pltpu.make_async_copy(a_ref.at[pl.ds(0, count)], first_ref.at[pl.ds(lead, count)], sem)
    copy.start()
    near, far = sketch_ref[:, :LANES], sketch_ref[:, LANES:]
    low = join_lanes(near, far, QUARTER)
    high = join_lanes(turn(near, QUARTER), turn(far, QUARTER), QUARTER)
    zero = place_ref[1] == 0
    mine_ref[...] = jnp.where(zero, low, high)
    theirs = jnp.where(zero, high, low)
    first_ref[:lead, :LANES] = theirs[:lead]
    first_ref[:lead, LANES:] = theirs[lead:]
    copy.wait()


def near_kernel(place_ref, own_ref, core_ref, mine_ref, got_ref, y_ref, high_ref, low_ref, rest_ref):
    rest_ref[...] = own_ref[own_ref.shape[0] - rest_ref.shape[0] :, :]
    store_factors(high_ref, low_ref, (own_ref[...], core_ref[...]))
    rhs = jnp.concatenate([sketch_side(place_ref, ref[...]) for ref in (mine_ref, got_ref)], axis=0)
    for b in range(own_ref.shape[0] // LANES):
        cut = slice(b * LANES, (b + 1) * LANES)
        total = dot(high_ref[cut, :], rhs) + dot(low_ref[cut, :], rhs)
        y_ref[b * QUARTER : (b + 1) * QUARTER, :] = unfold(total.T)


def far_kernel(start, skip, place_ref, side_ref, diagonal_ref, *refs):
    sketches, (near_ref, y_ref, high_ref, low_ref) = refs[:-4], refs[-4:]
    if not sketches:
        sketches = (side_ref, diagonal_ref)
    store_factors(high_ref, low_ref, (side_ref[skip:, :], diagonal_ref[skip:, :]))
    rhs = []
    for ref in sketches:
        for s in range(2):
            rhs.append(sketch_side(place_ref, ref[:LANES, s * LANES : (s + 1) * LANES]))
    rhs = jnp.concatenate(rhs, axis=0)
    for b in range(high_ref.shape[0] // LANES):
        cut = slice(b * LANES, (b + 1) * LANES)
        total = dot(high_ref[cut, :], rhs) + dot(low_ref[cut, :], rhs)
        at = (start // LANES + b) * QUARTER
        y_ref[b * QUARTER : (b + 1) * QUARTER, :] = unfold(total.T) + near_ref[at : at + QUARTER, :]


def send_z(y, high_refs, low_refs, z_ref):
    lhs = jnp.concatenate(split(y), axis=0).astype(BF16)
    near = dot(lhs, high_refs[0][...]) + dot(lhs, low_refs[0][...])
    far, at = None, 0
    for high_ref, low_ref in zip(high_refs[1:], low_refs[1:]):
        cut = slice(at, at + high_ref.shape[0])
        term = dot(lhs[:, cut], high_ref[...]) + dot(lhs[:, cut], low_ref[...])
        far = term if far is None else far + term
        at += high_ref.shape[0]
    store_blocks(z_ref, 0, unfold(near))
    store_blocks(z_ref, (z_ref.shape[0] - TILE) // 2, unfold(far))
    z_ref[-TILE:, :] = squares_tile(y)


def factors(refs):
    count = len(SHARES) + 1
    return refs[:count], refs[count : 2 * count]


def first_z_kernel(h, *refs):
    count = len(SHARES)
    high, low = factors(refs[2 * count :])
    pieces = []
    for a_ref, b_ref in zip(refs[:count], refs[count : 2 * count]):
        for j in range(a_ref.shape[0] // QUARTER):
            cut = slice(j * QUARTER + h * COLS, j * QUARTER + (h + 1) * COLS)
            pieces.append(a_ref[cut, :] + b_ref[cut, :])
    send_z(jnp.concatenate(pieces, axis=1), high, low, refs[-1])


def scaled(own_ref, got_ref, count):
    total = own_ref[...] + got_ref[...]
    scale = rms(total[-TILE:], count)
    return wide(total[:-TILE], COLS) / to_column(scale[:1], COLS), scale


def z_kernel(count, *refs):
    high, low = factors(refs[2:])
    z_ref, scale_ref = refs[-2:]
    y, scale = scaled(refs[0], refs[1], count)
    scale_ref[...] = scale
    send_z(y, high, low, z_ref)


def y_kernel(count, *refs):
    high_refs, low_refs = factors(refs[2:])
    y_ref, scale_ref, *z_refs = refs[2 + 2 * len(high_refs) :]
    z, scale = scaled(refs[0], refs[1], count)
    scale_ref[...] = scale
    for z_ref in z_refs:
        store_blocks(z_ref, 0, z)
    y_ref[-TILE:, :] = squares_tile(z)
    rhs = jnp.concatenate(split(z), axis=0).T.astype(BF16)
    middle = rhs.shape[0] // 2
    at = 0
    for high_ref, low_ref in zip(high_refs[1:], low_refs[1:]):
        for b in range(high_ref.shape[0] // LANES):
            near = slice(at * LANES, (at + 1) * LANES)
            far = slice(b * LANES, (b + 1) * LANES)
            total = dot(high_refs[0][near, :], rhs[:middle]) + dot(low_refs[0][near, :], rhs[:middle])
            total += dot(high_ref[far, :], rhs[middle:]) + dot(low_ref[far, :], rhs[middle:])
            y_ref[at * COLS : (at + 1) * COLS, :] = unfold(total.T)
            at += 1


def end_kernel(count, carried, place_ref, own_ref, got_ref, *refs):
    parts, scales, (keep_ref, send_ref, y_ref) = refs[:carried], refs[carried:-3], refs[-3:]
    y, scale = scaled(own_ref, got_ref, count)
    store_blocks(y_ref, 0, y)
    row = lax.broadcasted_iota(jnp.int32, (TILE, LANES), 0)
    tail = squares_tile(y)
    for i, known in enumerate([ref[...] for ref in scales] + [scale]):
        tail = jnp.where(row == i, known, tail)
    size = 2 * COLS
    for ref, chip in ((keep_ref, place_ref[2]), (send_ref, place_ref[3])):
        start = pl.multiple_of(chip * size, size)
        ref[:size, :] = y_ref[pl.ds(start, size), :]
        ref[size : size + TILE, :] = tail
    at = size + TILE
    for ref in parts:
        middle = ref.shape[0] // 2
        send_ref[at : at + middle, :] = ref[middle:, :]
        at += middle


def core_kernel(place_ref, *refs):
    keeps, gots, parts = (refs[i * HALVES : (i + 1) * HALVES] for i in range(3))
    keep_ref, send_ref = refs[3 * HALVES :]
    zero_side, zero_core = place_ref[1] == 0, place_ref[0] == 0
    tail = None
    for s in range(2):
        for h in range(HALVES):
            a, b = keeps[h][...], gots[h][: keeps[h].shape[0], :]
            x = jnp.where(zero_side, a, b) if s == 0 else jnp.where(zero_side, b, a)
            first, second, known = x[:COLS], x[COLS : 2 * COLS], x[2 * COLS :]
            at = (s * HALVES + h) * COLS
            keep_ref[at : at + COLS, :] = jnp.where(zero_core, first, second)
            send_ref[at : at + COLS, :] = jnp.where(zero_core, second, first)
            tail = known if tail is None else join_lanes(tail, known, at)
    keep_ref[LANES : LANES + TILE, :] = tail
    send_ref[LANES : LANES + TILE, :] = tail
    size = 2 * COLS
    for h, ref in enumerate(parts):
        at = LANES + TILE + h * size
        send_ref[at : at + size, :] = ref[size : 2 * size, :]
        at += HALVES * size
        start = keeps[0].shape[0] + (2 * h + 1) * size
        send_ref[at : at + size, :] = gots[0][start : start + size, :]


def join_kernel(place_ref, keep_ref, got_ref, y_ref, known_ref):
    zero = place_ref[0] == 0
    keep, got = keep_ref[...], got_ref[: LANES + TILE, :]
    for s, x in enumerate((jnp.where(zero, keep, got), jnp.where(zero, got, keep))):
        cut = slice(s * LANES, (s + 1) * LANES)
        y_ref[:, cut] = x[:LANES].T
        known_ref[:, cut] = x[LANES:]


def z_out_kernel(place_ref, *refs):
    parts, (side_ref, core_ref, known_ref, z_ref) = refs[:HALVES], refs[HALVES:]
    zero_side, zero_core = place_ref[1] == 0, place_ref[0] == 0
    size = 2 * COLS
    side_at, core_at = size + TILE, LANES + TILE
    mine = [ref[:size, :] for ref in parts]
    side = [side_ref[side_at + 2 * h * size : side_at + (2 * h + 1) * size, :] for h in range(HALVES)]
    core = [core_ref[core_at + h * size : core_at + (h + 1) * size, :] for h in range(2 * HALVES)]

    def side_order(own, other):
        low = [jnp.where(zero_side, a, b) for a, b in zip(own, other)]
        high = [jnp.where(zero_side, b, a) for a, b in zip(own, other)]
        return jnp.concatenate([wide(x, COLS) for x in low + high], axis=0)

    ours, theirs = side_order(mine, side), side_order(core[:HALVES], core[HALVES:])
    for s, x in enumerate((jnp.where(zero_core, ours, theirs), jnp.where(zero_core, theirs, ours))):
        cut = slice(s * LANES, (s + 1) * LANES)
        z_ref[:, cut] = x.T / known_ref[2 * ITERS - 1 : 2 * ITERS, cut]


def q_out_kernel(count, y_ref, known_ref, a_ref, b_ref, q_ref, scale_ref):
    last = 2 * ITERS
    scale = rms((a_ref[...] + b_ref[...])[last : last + 1], count)
    q_ref[...] = y_ref[...] / scale
    scale_ref[:last, :] = known_ref[:last, :]
    scale_ref[last:, :] = scale


def call(kernel, outs, *args, scalars=1, plain=False, in_place=(), scratch=()):
    specs = [pl.BlockSpec(memory_space=pltpu.SMEM)] * scalars
    for i in range(scalars, len(args)):
        specs.append(pl.BlockSpec(memory_space=pltpu.HBM if i in in_place else pltpu.VMEM))
    out_spec = pl.BlockSpec() if plain else pl.BlockSpec(memory_space=pltpu.VMEM)
    return pl.pallas_call(
        kernel,
        out_shape=[jax.ShapeDtypeStruct(shape, dtype) for shape, dtype in outs],
        in_specs=specs,
        out_specs=[out_spec] * len(outs),
        scratch_shapes=scratch,
        compiler_params=pltpu.CompilerParams(vmem_limit_bytes=16 * 1024 * 1024),
    )(*args)


def general(snapshots, sketch):
    high = lax.Precision.HIGHEST
    all_cells = snapshots.shape[0] * lax.axis_size("cell")
    all_snaps = snapshots.shape[1] * lax.axis_size("snap")
    z, scales = sketch, []
    for section in range(ITERS + 1):
        partial = jnp.dot(snapshots, z, precision=high, preferred_element_type=F32)
        y = lax.psum_scatter(partial, "snap", scatter_dimension=0, tiled=True)
        scale = rms(lax.psum(jnp.sum(y * y, axis=0), ("cell", "snap")), all_cells)
        scales.append(scale)
        q = y / scale
        if section < ITERS:
            whole = lax.all_gather(q, "snap", axis=0, tiled=True)
            partial = jnp.dot(snapshots.T, whole, precision=high, preferred_element_type=F32)
            z = lax.psum(partial, "cell")
            scale = rms(lax.psum(jnp.sum(z * z, axis=0), "snap"), all_snaps)
            scales.append(scale)
            z = z / scale
    return q, z, jnp.stack(scales)


def local(snapshots, sketch):
    groups = lax.axis_size("cell")
    places = lax.axis_size("snap")
    rows, width = snapshots.shape
    rank = sketch.shape[1]
    fits = groups == 4 and places == 8 and rank == 4 * QUARTER and rows == 8 * LANES and width == 2 * LANES
    if not fits:
        return general(snapshots, sketch)
    all_cells = rows * groups
    all_snaps = width * places
    seat = lax.axis_index("snap")
    chip = seat // 2
    place = jnp.stack([seat % 2, chip % 2, chip, chip ^ 1]).astype(jnp.int32)

    def swap(x, bits):
        return lax.ppermute(x, "snap", [(i, i ^ bits) for i in range(places)])

    swap_core = functools.partial(swap, bits=1)
    swap_side = functools.partial(swap, bits=2)
    swap_pair = functools.partial(swap, bits=4)

    def swap_cell(x, step):
        def target(cell, i):
            return cell ^ (1 if i % 2 == step else 2)

        perm = [(c * places + i, target(c, i) * places + i) for c in range(groups) for i in range(places)]
        return lax.ppermute(x, ("cell", "snap"), perm)

    def cell_pair(x):
        x = x + swap_cell(x, 0)
        return x, swap_cell(x, 1)

    sizes = [n * rows // sum(SHARES) for n in SHARES]
    lead = width // 2

    def factor(count):
        return [((count, 2 * width), BF16)] * 2

    mine, first = call(
        prepare_kernel, [((width, LANES), F32), ((lead + sizes[0], width), F32)],
        place, sketch, snapshots, in_place=(2,), scratch=[pltpu.SemaphoreType.DMA],
    )
    side_first = swap_side(first)
    near_y, near_high, near_low, rest = call(
        near_kernel,
        [((rows // LANES * QUARTER, LANES), F32)] + factor(rows) + [((sizes[1], width), F32)],
        place, snapshots, swap_core(snapshots), mine, swap_core(mine),
    )
    side_rest = swap_side(rest)
    side_first, near_y = lax.optimization_barrier((side_first, near_y))
    core_first = swap_core(side_first)
    own_first, high_first, low_first = call(
        functools.partial(far_kernel, 0, lead),
        [((sizes[0] // LANES * QUARTER, LANES), F32)] + factor(sizes[0]),
        place, side_first, core_first, near_y,
    )
    side_rest, own_first = lax.optimization_barrier((side_rest, own_first))
    own_rest, high_rest, low_rest = call(
        functools.partial(far_kernel, sizes[0], 0),
        [((sizes[1] // LANES * QUARTER, LANES), F32)] + factor(sizes[1]),
        place, side_rest, swap_core(side_rest), side_first, core_first, near_y,
    )
    matrix = (near_high, high_first, high_rest, near_low, low_first, low_rest)
    own = (own_first, own_rest)
    got = tuple(swap_pair(y) for y in own)

    flat = (COLS * rows // LANES + TILE, LANES)
    sent_shape = ((COLS * 4 * width // LANES + TILE, LANES), F32)
    y_shape = (flat, F32)
    scale_shape = ((TILE, LANES), F32)
    z_shape = ((COLS * 4 * width // LANES, LANES), F32)
    scales = [[] for _ in range(HALVES)]
    sent = [
        call(functools.partial(first_z_kernel, h), [sent_shape], *own, *got, *matrix, scalars=0)[0]
        for h in range(HALVES)
    ]
    ys, zs = [None] * HALVES, [None] * HALVES
    for section in range(ITERS):
        last = section == ITERS - 1
        for h in range(HALVES):
            ys[h], scale, *z = call(
                functools.partial(y_kernel, all_cells), [y_shape, scale_shape] + [z_shape] * last,
                *cell_pair(sent[h]), *matrix, scalars=0,
            )
            scales[h].append(scale)
            if last:
                zs[h] = z[0]
                continue
            sent[h], scale = call(
                functools.partial(z_kernel, all_snaps), [sent_shape, scale_shape],
                ys[h], swap_pair(ys[h]), *matrix, scalars=0,
            )
            scales[h].append(scale)

    small = (2 * COLS + TILE, LANES)
    carried = HALVES * z_shape[0][0] // 2
    keeps, gots = [], []
    for h in range(HALVES):
        parts = zs if h == 0 else []
        keep, send, _ = call(
            functools.partial(end_kernel, all_snaps, len(parts)),
            [(small, F32), ((small[0] + carried * (h == 0), LANES), F32), ((flat[0] - TILE, LANES), F32)],
            place, ys[h], swap_pair(ys[h]), *parts, *scales[h],
        )
        keeps.append(keep)
        gots.append(swap_side(send))
    keep, send = call(
        core_kernel, [((LANES + TILE, LANES), F32), ((LANES + TILE + carried, LANES), F32)],
        place, *keeps, *gots, *zs,
    )
    core_got = swap_core(send)
    y, known = call(join_kernel, [((LANES, rank), F32), ((TILE, rank), F32)], place, keep, core_got)
    a, b = cell_pair(known)
    (z_out,) = call(z_out_kernel, [((width, rank), F32)], place, *zs, gots[0], core_got, known, plain=True)
    q_out, scale_out = call(
        functools.partial(q_out_kernel, all_cells),
        [((LANES, rank), F32), ((2 * ITERS + 1, rank), F32)],
        y, known, a, b, scalars=0, plain=True,
    )
    return q_out, z_out, scale_out


def solution(mesh):
    return jax.shard_map(
        local,
        mesh=mesh,
        in_specs=(P("cell", "snap"), P("snap", None)),
        out_specs=(P(("cell", "snap"), None), P("snap", None), P()),
        check_vma=False,
    )
```

time: 411 us -> 118 us (0.29)
  waiting for transfers between devices: 225 us -> 64.8 us
  blocking collectives: 146 us -> 0 us
  starting transfers between devices: 0.29 us -> 29.2 us
  Pallas kernels: 0 us -> 20.4 us
  matrix products: 13.8 us -> 0 us
  between operations: 14.2 us -> 0.73 us
  other arithmetic: 7.14 us -> 0.16 us
    psum x5 -> x0, blocking collectives: 146 us -> none  [the longest x3 114 us: scattered_section(): total = lax.psum(jnp.sum(y_raw * y_raw, axis=0), ('cell', 'snap'))]
    reduce_scatter x3 -> x0, waiting for transfers between devices: 93.4 us -> none  [scattered_section(): lax.psum_scatter(jnp.dot(snapshots, z_input, precision=high, preferred_el...]
    psum x2 -> x0, waiting for transfers between devices: 84.8 us -> none  [local(): summed = lax.psum(partial_z, 'cell') / unit_scale]
    ppermute x0 -> x25, waiting for transfers between devices: none -> 64.8 us  [the longest x15 51.7 us: swap(): return lax.ppermute(x, 'snap', [(i, i ^ bits) for i in range(places)])]
    all_gather x2 -> x0, waiting for transfers between devices: 47.1 us -> none  [local(): lax.all_gather(outgoing, 'snap', axis=0, tiled=True)]
    ppermute x0 -> x25, starting transfers between devices: none -> 29.2 us  [the longest x15 15 us: swap(): return lax.ppermute(x, 'snap', [(i, i ^ bits) for i in range(places)])]
    pallas_call x0 -> x18, Pallas kernels: none -> 20.4 us  [call(): pl.pallas_call(kernel, out_shape=[jax.ShapeDtypeStruct(shape, dtype) for...]
    dot_general x5 -> x0, matrix products: 13.8 us -> none  [the longest x3 7.05 us: scattered_section(): jnp.dot(snapshots, z_input, precision=high, preferred_element_type=jnp.fl...]
  transfers between devices with their start and end apart: 7 -> 25, of which waited for: 7 -> 22; matrix products, arithmetic and copies ran while one was open for 0% -> 0% of each run, Pallas kernels for 0% -> 15%
where the time goes in v5:
time: 118 us; the launch traced here: 117 us
  waiting for transfers between devices  64.8 us (55%)
  starting transfers between devices  29.2 us (25%)
  Pallas kernels  20.4 us (17%)
  local copies, waits for them, and re-layouts  2.18 us (2%)
    ppermute x15, waiting for transfers between devices, swap(): return lax.ppermute(x, 'snap', [(i, i ^ bits) for i in range(places)])  51.7 us
    pallas_call x18, Pallas kernels, call(): pl.pallas_call(kernel, out_shape=[jax.ShapeDtypeStruct(shape, dtype) for...  20.4 us
    ppermute x15, starting transfers between devices, swap(): return lax.ppermute(x, 'snap', [(i, i ^ bits) for i in range(places)])  15 us
    ppermute x10, starting transfers between devices, swap_cell(): return lax.ppermute(x, ('cell', 'snap'), perm)  14.1 us
    ppermute x10, waiting for transfers between devices, swap_cell(): return lax.ppermute(x, ('cell', 'snap'), perm)  13 us
  transfers between devices with their start and end apart: 25, of which 22 were waited for; matrix products, arithmetic and copies ran while one was open for 0% of the time, Pallas kernels for 15%

profile of v5, /device:TPU:0, one launch (start us, length us, event | category | flops | bytes accessed | tf_op | source)
XLA Modules:
  0.0 117.4 jit_solution(4283101969329778770)
XLA Ops:
  0.6 0.5 collective-permute-start
  1.1 0.1 pad_add_fusion.place_ref
  1.2 1.2 %copy-done = f32[1024,256]{1,0:T(8,128)S(1)} copy-done((f32[1024,256]{1,0:T(8,128)S(1)}, f32[1024,256]{1,0:T(8,128)}, u32[]{:S(2)}) %copy-start) | copy-done | bytes 1048600
  2.5 0.9 copy-done.2
  3.4 0.8 shard_map.49
  4.2 2.7 %collective-permute-start.3 = (f32[896,256]{1,0:T(8,128)S(1)}, f32[896,256]{1,0:T(8,128)S(1)}, u32[]{:S(2)}, u32[]{:S(2)}) collective-permute-start(f32[896,256]{1,0:T(8,128)S(1)} %get-tuple-element.45), channel_id=1, source_target_pairs={{0,2},{1,3},{2,0},{3,1},{4,6},{5,7},{6,4},{7,5},{8,10},{9,11},{10,... | collective-permute-start | bytes 2752520 | tf_op jit(solution)/shard_map/ppermute | solution.py:331
  6.9 0.2 collective-permute-start.1
  7.1 1.2 collective-permute-done.1.got_ref
  8.2 1.6 %shard_map.50 = (f32[512,128]{1,0:T(8,128)S(1)}, bf16[1024,512]{1,0:T(8,128)(2,1)S(1)}, bf16[1024,512]{1,0:T(8,128)(2,1)S(1)}, f32[256,256]{1,0:T(8,128)S(1)}) custom-call(s32[4]{0:T(128)S(1)} %pad_add_fusion.place_ref, f32[1024,256]{1,0:T(8,128)S(1)} %copy-done.1, f32[1024,256]{1,0:T(8,128)S(1)} %collective-permute-done.core_ref, ...), custom_call_target="tpu_custom_call" | custom-call | tf_op jit(solution)/shard_map/pallas_call | solution.py:285
  9.8 18.0 %collective-permute-done.3.side_ref.refs_0_ = f32[896,256]{1,0:T(8,128)S(1)} collective-permute-done((f32[896,256]{1,0:T(8,128)S(1)}, f32[896,256]{1,0:T(8,128)S(1)}, u32[]{:S(2)}, u32[]{:S(2)}) %collective-permute-start.3) | collective-permute-done | bytes 917536 | tf_op jit(solution)/shard_map/ppermute | solution.py:331
  27.9 1.7 %collective-permute-start.2 = (f32[256,256]{1,0:T(8,128)S(1)}, f32[256,256]{1,0:T(8,128)S(1)}, u32[]{:S(2)}, u32[]{:S(2)}) collective-permute-start(f32[256,256]{1,0:T(8,128)S(1)} %get-tuple-element.44), channel_id=1, source_target_pairs={{0,2},{1,3},{2,0},{3,1},{4,6},{5,7},{6,4},{7,5},{8,10},{9,11},{10,... | collective-permute-start | bytes 786440 | tf_op jit(solution)/shard_map/ppermute | solution.py:331
  29.6 0.7 collective-permute-done.4.diagonal_ref.refs_1_
  30.3 1.4 %shard_map.51 = (f32[384,128]{1,0:T(8,128)S(1)}, bf16[768,512]{1,0:T(8,128)(2,1)S(1)}, bf16[768,512]{1,0:T(8,128)(2,1)S(1)}) custom-call(s32[4]{0:T(128)S(1)} %pad_add_fusion.place_ref, f32[896,256]{1,0:T(8,128)S(1)} %collective-permute-done.3.side_ref.refs_0_, f32[896,256]{1,0:T(8,128)S(1)} %collective-permute-done.4.diagonal_ref.refs_1_, ...), custom_call_target="tpu_custom_call" | custom-call | tf_op jit(solution)/shard_map/pallas_call | solution.py:285
  31.8 4.8 %collective-permute-done.2.side_ref = f32[256,256]{1,0:T(8,128)S(1)} collective-permute-done((f32[256,256]{1,0:T(8,128)S(1)}, f32[256,256]{1,0:T(8,128)S(1)}, u32[]{:S(2)}, u32[]{:S(2)}) %collective-permute-start.2) | collective-permute-done | bytes 262176 | tf_op jit(solution)/shard_map/ppermute | solution.py:331
  36.6 2.8 %collective-permute-start.6 = (f32[384,128]{1,0:T(8,128)S(1)}, f32[384,128]{1,0:T(8,128)S(1)}, u32[]{:S(2)}, u32[]{:S(2)}) collective-permute-start(f32[384,128]{1,0:T(8,128)S(1)} %get-tuple-element.50.refs_0_), channel_id=1, source_target_pairs={{0,4},{1,5},{2,6},{3,7},{4,0},{5,1},{6,2},{7,3},{8,12},{9,13},{10,... | collective-permute-start | bytes 589832 | tf_op jit(solution)/shard_map/ppermute | solution.py:331
  39.3 1.1 shard_map.52
  40.4 1.6 %collective-permute-start.7 = (f32[128,128]{1,0:T(8,128)S(1)}, f32[128,128]{1,0:T(8,128)S(1)}, u32[]{:S(2)}, u32[]{:S(2)}) collective-permute-start(f32[128,128]{1,0:T(8,128)S(1)} %get-tuple-element.52.refs_1_), channel_id=1, source_target_pairs={{0,4},{1,5},{2,6},{3,7},{4,0},{5,1},{6,2},{7,3},{8,12},{9,13},{10,... | collective-permute-start | bytes 196616 | tf_op jit(solution)/shard_map/ppermute | solution.py:331
  42.0 8.7 %collective-permute-done.6.refs_2_ = f32[384,128]{1,0:T(8,128)S(1)} collective-permute-done((f32[384,128]{1,0:T(8,128)S(1)}, f32[384,128]{1,0:T(8,128)S(1)}, u32[]{:S(2)}, u32[]{:S(2)}) %collective-permute-start.6) | collective-permute-done | bytes 196640 | tf_op jit(solution)/shard_map/ppermute | solution.py:331
  50.8 1.1 collective-permute-done.7.refs_3_
  51.9 0.8 shard_map.53
  52.7 1.6 %collective-permute-start.8 = (f32[264,128]{1,0:T(8,128)S(1)}, f32[264,128]{1,0:T(8,128)S(1)}, u32[]{:S(2)}, u32[]{:S(2)}) collective-permute-start(f32[264,128]{1,0:T(8,128)S(1)} %shard_map.53), channel_id=1, source_target_pairs={{0,8},{1,17},{2,10},{3,19},{4,12},{5,21},{6,14},{7,23},{8,0},{9,25... | collective-permute-start | bytes 405512 | tf_op jit(solution)/shard_map/ppermute | solution.py:342
  54.3 0.8 shard_map.57
  55.1 0.5 collective-permute-start.14
  55.6 2.1 %collective-permute-done.8 = f32[264,128]{1,0:T(8,128)S(1)} collective-permute-done((f32[264,128]{1,0:T(8,128)S(1)}, f32[264,128]{1,0:T(8,128)S(1)}, u32[]{:S(2)}, u32[]{:S(2)}) %collective-permute-start.8) | collective-permute-done | bytes 135200 | tf_op jit(solution)/shard_map/ppermute | solution.py:342
  57.8 1.6 %collective-permute-start.9 = (f32[264,128]{1,0:T(8,128)S(1)}, f32[264,128]{1,0:T(8,128)S(1)}, u32[]{:S(2)}, u32[]{:S(2)}) collective-permute-start(f32[264,128]{1,0:T(8,128)S(1)} %add.25.refs_0_), channel_id=1, source_target_pairs={{0,16},{1,9},{2,18},{3,11},{4,20},{5,13},{6,22},{7,15},{8,24},{9,1... | collective-permute-start | bytes 405512 | tf_op jit(solution)/shard_map/ppermute | solution.py:342
  59.4 1.5 %collective-permute-done.14 = f32[264,128]{1,0:T(8,128)S(1)} collective-permute-done((f32[264,128]{1,0:T(8,128)S(1)}, f32[264,128]{1,0:T(8,128)S(1)}, u32[]{:S(2)}, u32[]{:S(2)}) %collective-permute-start.14) | collective-permute-done | bytes 135200 | tf_op jit(solution)/shard_map/ppermute | solution.py:342
  60.9 1.7 %collective-permute-start.15 = (f32[264,128]{1,0:T(8,128)S(1)}, f32[264,128]{1,0:T(8,128)S(1)}, u32[]{:S(2)}, u32[]{:S(2)}) collective-permute-start(f32[264,128]{1,0:T(8,128)S(1)} %add.27.refs_0_), channel_id=1, source_target_pairs={{0,16},{1,9},{2,18},{3,11},{4,20},{5,13},{6,22},{7,15},{8,24},{9,1... | collective-permute-start | bytes 405512 | tf_op jit(solution)/shard_map/ppermute | solution.py:342
  62.6 0.3 collective-permute-done.9.refs_1_
  62.9 1.5 %shard_map.54 = (f32[264,128]{1,0:T(8,128)S(1)}, f32[8,128]{1,0:T(8,128)S(1)}) custom-call(f32[264,128]{1,0:T(8,128)S(1)} %add.25.refs_0_, f32[264,128]{1,0:T(8,128)S(1)} %collective-permute-done.9.refs_1_, bf16[1024,512]{1,0:T(8,128)(2,1)S(1)} %get-tuple-element.53.refs_4_.refs_2_, bf16[768,512]{1,0:T(8,128)(2,1)S(1)} %get-tuple-element.54.refs_5_.refs_3_, ...), custom_call_target="tpu_custom_call" | custom-call | tf_op jit(solution)/shard_map/pallas_call | solution.py:285
  64.4 0.1 collective-permute-start.10
  64.4 1.5 %collective-permute-done.15.refs_1_ = f32[264,128]{1,0:T(8,128)S(1)} collective-permute-done((f32[264,128]{1,0:T(8,128)S(1)}, f32[264,128]{1,0:T(8,128)S(1)}, u32[]{:S(2)}, u32[]{:S(2)}) %collective-permute-start.15) | collective-permute-done | bytes 135200 | tf_op jit(solution)/shard_map/ppermute | solution.py:342
  66.0 1.5 %shard_map.58 = (f32[264,128]{1,0:T(8,128)S(1)}, f32[8,128]{1,0:T(8,128)S(1)}) custom-call(f32[264,128]{1,0:T(8,128)S(1)} %add.27.refs_0_, f32[264,128]{1,0:T(8,128)S(1)} %collective-permute-done.15.refs_1_, bf16[1024,512]{1,0:T(8,128)(2,1)S(1)} %get-tuple-element.53.refs_4_.refs_2_, bf16[768,512]{1,0:T(8,128)(2,1)S(1)} %get-tuple-element.54.refs_5_.refs_3_, ...), custom_call_target="tpu_custom_call" | custom-call | tf_op jit(solution)/shard_map/pallas_call | solution.py:285
  67.5 1.4 %collective-permute-start.16 = (f32[264,128]{1,0:T(8,128)S(1)}, f32[264,128]{1,0:T(8,128)S(1)}, u32[]{:S(2)}, u32[]{:S(2)}) collective-permute-start(f32[264,128]{1,0:T(8,128)S(1)} %get-tuple-element.63.refs_0_), channel_id=1, source_target_pairs={{0,4},{1,5},{2,6},{3,7},{4,0},{5,1},{6,2},{7,3},{8,12},{9,13},{10,... | collective-permute-start | bytes 405512 | tf_op jit(solution)/shard_map/ppermute | solution.py:331
  68.9 7.5 %collective-permute-done.10.refs_1_ = f32[264,128]{1,0:T(8,128)S(1)} collective-permute-done((f32[264,128]{1,0:T(8,128)S(1)}, f32[264,128]{1,0:T(8,128)S(1)}, u32[]{:S(2)}, u32[]{:S(2)}) %collective-permute-start.10) | collective-permute-done | bytes 135200 | tf_op jit(solution)/shard_map/ppermute | solution.py:331
  76.5 0.9 shard_map.55
  77.4 0.9 collective-permute-start.11
  78.2 0.1 collective-permute-done.16.refs_1_
  78.4 0.9 shard_map.59
  79.3 1.1 collective-permute-start.17
  80.3 2.1 %collective-permute-done.11 = f32[264,128]{1,0:T(8,128)S(1)} collective-permute-done((f32[264,128]{1,0:T(8,128)S(1)}, f32[264,128]{1,0:T(8,128)S(1)}, u32[]{:S(2)}, u32[]{:S(2)}) %collective-permute-start.11) | collective-permute-done | bytes 135200 | tf_op jit(solution)/shard_map/ppermute | solution.py:342
  82.5 2.7 %collective-permute-start.12 = (f32[264,128]{1,0:T(8,128)S(1)}, f32[264,128]{1,0:T(8,128)S(1)}, u32[]{:S(2)}, u32[]{:S(2)}) collective-permute-start(f32[264,128]{1,0:T(8,128)S(1)} %add.26.refs_0_), channel_id=1, source_target_pairs={{0,16},{1,9},{2,18},{3,11},{4,20},{5,13},{6,22},{7,15},{8,24},{9,1... | collective-permute-start | bytes 405512 | tf_op jit(solution)/shard_map/ppermute | solution.py:342
  85.1 0.2 collective-permute-done.17
  85.3 1.6 %collective-permute-start.18 = (f32[264,128]{1,0:T(8,128)S(1)}, f32[264,128]{1,0:T(8,128)S(1)}, u32[]{:S(2)}, u32[]{:S(2)}) collective-permute-start(f32[264,128]{1,0:T(8,128)S(1)} %add.28.refs_0_), channel_id=1, source_target_pairs={{0,16},{1,9},{2,18},{3,11},{4,20},{5,13},{6,22},{7,15},{8,24},{9,1... | collective-permute-start | bytes 405512 | tf_op jit(solution)/shard_map/ppermute | solution.py:342
  86.9 1.2 %collective-permute-done.12.refs_1_ = f32[264,128]{1,0:T(8,128)S(1)} collective-permute-done((f32[264,128]{1,0:T(8,128)S(1)}, f32[264,128]{1,0:T(8,128)S(1)}, u32[]{:S(2)}, u32[]{:S(2)}) %collective-permute-start.12) | collective-permute-done | bytes 135200 | tf_op jit(solution)/shard_map/ppermute | solution.py:342
  88.1 1.5 %shard_map.56 = (f32[264,128]{1,0:T(8,128)S(1)}, f32[8,128]{1,0:T(8,128)S(1)}, f32[256,128]{1,0:T(8,128)S(1)}) custom-call(f32[264,128]{1,0:T(8,128)S(1)} %add.26.refs_0_, f32[264,128]{1,0:T(8,128)S(1)} %collective-permute-done.12.refs_1_, bf16[1024,512]{1,0:T(8,128)(2,1)S(1)} %get-tuple-element.53.refs_4_.refs_2_, ...), custom_call_target="tpu_custom_call" | custom-call | tf_op jit(solution)/shard_map/pallas_call | solution.py:285
  89.6 0.1 collective-permute-start.13
  89.7 0.7 collective-permute-done.18.refs_1_
  90.4 1.5 %shard_map.60 = (f32[264,128]{1,0:T(8,128)S(1)}, f32[8,128]{1,0:T(8,128)S(1)}, f32[256,128]{1,0:T(8,128)S(1)}) custom-call(f32[264,128]{1,0:T(8,128)S(1)} %add.28.refs_0_, f32[264,128]{1,0:T(8,128)S(1)} %collective-permute-done.18.refs_1_, bf16[1024,512]{1,0:T(8,128)(2,1)S(1)} %get-tuple-element.53.refs_4_.refs_2_, ...), custom_call_target="tpu_custom_call" | custom-call | tf_op jit(solution)/shard_map/pallas_call | solution.py:285
  91.9 2.2 %collective-permute-start.19 = (f32[264,128]{1,0:T(8,128)S(1)}, f32[264,128]{1,0:T(8,128)S(1)}, u32[]{:S(2)}, u32[]{:S(2)}) collective-permute-start(f32[264,128]{1,0:T(8,128)S(1)} %get-tuple-element.70.own_ref), channel_id=1, source_target_pairs={{0,4},{1,5},{2,6},{3,7},{4,0},{5,1},{6,2},{7,3},{8,12},{9,13},{10,... | collective-permute-start | bytes 405512 | tf_op jit(solution)/shard_map/ppermute | solution.py:331
  94.2 5.3 %collective-permute-done.13.got_ref = f32[264,128]{1,0:T(8,128)S(1)} collective-permute-done((f32[264,128]{1,0:T(8,128)S(1)}, f32[264,128]{1,0:T(8,128)S(1)}, u32[]{:S(2)}, u32[]{:S(2)}) %collective-permute-start.13) | collective-permute-done | bytes 135200 | tf_op jit(solution)/shard_map/ppermute | solution.py:331
  99.5 1.3 %shard_map.61 = (f32[72,128]{1,0:T(8,128)S(1)}, f32[328,128]{1,0:T(8,128)S(1)}, f32[256,128]{1,0:T(8,128)}) custom-call(s32[4]{0:T(128)S(1)} %pad_add_fusion.place_ref, f32[264,128]{1,0:T(8,128)S(1)} %get-tuple-element.61.own_ref, f32[264,128]{1,0:T(8,128)S(1)} %collective-permute-done.13.got_ref, f32[256,128]{1,0:T(8,128)S(1)} %get-tuple-element.62.refs_0_.refs_4_, ...), custom_call_target="tpu_custom_call" | custom-call | tf_op jit(solution)/shard_map/pallas_call | solution.py:285
  100.8 0.3 collective-permute-done.19.got_ref
  101.1 1.3 %shard_map.62 = (f32[72,128]{1,0:T(8,128)S(1)}, f32[72,128]{1,0:T(8,128)S(1)}, f32[256,128]{1,0:T(8,128)}) custom-call(s32[4]{0:T(128)S(1)} %pad_add_fusion.place_ref, f32[264,128]{1,0:T(8,128)S(1)} %get-tuple-element.70.own_ref, f32[264,128]{1,0:T(8,128)S(1)} %collective-permute-done.19.got_ref, f32[8,128]{1,0:T(8,128)S(1)} %get-tuple-element.71.refs_0_, ...), custom_call_target="tpu_custom_call" | custom-call | tf_op jit(solution)/shard_map/pallas_call | solution.py:285
  102.4 1.8 %collective-permute-start.21 = (f32[72,128]{1,0:T(8,128)S(1)}, f32[72,128]{1,0:T(8,128)S(1)}, u32[]{:S(2)}, u32[]{:S(2)}) collective-permute-start(f32[72,128]{1,0:T(8,128)S(1)} %get-tuple-element.76), channel_id=1, source_target_pairs={{0,2},{1,3},{2,0},{3,1},{4,6},{5,7},{6,4},{7,5},{8,10},{9,11},{10,... | collective-permute-start | bytes 110600 | tf_op jit(solution)/shard_map/ppermute | solution.py:331
  104.1 2.4 %collective-permute-done.21.refs_3_ = f32[72,128]{1,0:T(8,128)S(1)} collective-permute-done((f32[72,128]{1,0:T(8,128)S(1)}, f32[72,128]{1,0:T(8,128)S(1)}, u32[]{:S(2)}, u32[]{:S(2)}) %collective-permute-start.21) | collective-permute-done | bytes 36896 | tf_op jit(solution)/shard_map/ppermute | solution.py:331
  106.6 0.6 shard_map.63
  107.2 1.4 %collective-permute-done.22.got_ref.refs_3_ = f32[392,128]{1,0:T(8,128)S(1)} collective-permute-done((f32[392,128]{1,0:T(8,128)S(1)}, f32[392,128]{1,0:T(8,128)S(1)}, u32[]{:S(2)}, u32[]{:S(2)}) %collective-permute-start.22) | collective-permute-done | bytes 200736 | tf_op jit(solution)/shard_map/ppermute | solution.py:331
  108.7 0.6 shard_map.64
  109.3 1.4 %collective-permute-start.23 = (f32[8,256]{1,0:T(8,128)S(1)}, f32[8,256]{1,0:T(8,128)S(1)}, u32[]{:S(2)}, u32[]{:S(2)}) collective-permute-start(f32[8,256]{1,0:T(8,128)S(1)} %get-tuple-element.80.known_ref.refs_4_), channel_id=1, source_target_pairs={{0,8},{1,17},{2,10},{3,19},{4,12},{5,21},{6,14},{7,23},{8,0},{9,25... | collective-permute-start | bytes 24584 | tf_op jit(solution)/shard_map/ppermute | solution.py:342
  110.7 2.3 %collective-permute-done.23 = f32[8,256]{1,0:T(8,128)S(1)} collective-permute-done((f32[8,256]{1,0:T(8,128)S(1)}, f32[8,256]{1,0:T(8,128)S(1)}, u32[]{:S(2)}, u32[]{:S(2)}) %collective-permute-start.23) | collective-permute-done | bytes 8224 | tf_op jit(solution)/shard_map/ppermute | solution.py:342
  113.0 1.2 collective-permute-start.24
  114.2 1.4 %shard_map.66 = f32[256,256]{1,0:T(8,128)} custom-call(s32[4]{0:T(128)S(1)} %pad_add_fusion.place_ref, f32[256,128]{1,0:T(8,128)S(1)} %get-tuple-element.62.refs_0_.refs_4_, f32[256,128]{1,0:T(8,128)S(1)} %get-tuple-element.65.refs_1_.refs_5_, f32[328,128]{1,0:T(8,128)S(1)} %collective-permute-done.20.refs_2_, ...), custom_call_target="tpu_custom_call" | custom-call | tf_op jit(solution)/shard_map/pallas_call | solution.py:285
  115.6 1.1 collective-permute-done.24.b_ref
  116.7 0.7 shard_map.65
  (16 shorter events, 0.1 us)
Async XLA Ops:
  0.6 7.6 %collective-permute-start = (f32[1024,256]{1,0:T(8,128)}, f32[1024,256]{1,0:T(8,128)S(1)}, u32[]{:S(2)}, u32[]{:S(2)}) collective-permute-start(f32[1024,256]{1,0:T(8,128)} %own_ref.1), channel_id=1, source_target_pairs={{0,1},{1,0},{2,3},{3,2},{4,5},{5,4},{6,7},{7,6},{8,9},{9,8},{10,11... | collective-permute-start | bytes 3145736 | tf_op jit(solution)/shard_map/ppermute | solution.py:331
  1.2 1.2 %copy-start = (f32[1024,256]{1,0:T(8,128)S(1)}, f32[1024,256]{1,0:T(8,128)}, u32[]{:S(2)}) copy-start(f32[1024,256]{1,0:T(8,128)} %own_ref.1) | copy-start | bytes 3145732
  2.5 0.9 copy-start.2
  3.4 4.8 %copy-start.1 = (f32[1024,256]{1,0:T(8,128)S(1)}, f32[1024,256]{1,0:T(8,128)}, u32[]{:S(2)}) copy-start(f32[1024,256]{1,0:T(8,128)} %own_ref.1) | copy-start | bytes 3145732
  4.2 23.7 %collective-permute-start.3 = (f32[896,256]{1,0:T(8,128)S(1)}, f32[896,256]{1,0:T(8,128)S(1)}, u32[]{:S(2)}, u32[]{:S(2)}) collective-permute-start(f32[896,256]{1,0:T(8,128)S(1)} %get-tuple-element.45), channel_id=1, source_target_pairs={{0,2},{1,3},{2,0},{3,1},{4,6},{5,7},{6,4},{7,5},{8,10},{9,11},{10,... | collective-permute-start | bytes 2752520 | tf_op jit(solution)/shard_map/ppermute | solution.py:331
  6.9 1.3 %collective-permute-start.1 = (f32[256,128]{1,0:T(8,128)S(1)}, f32[256,128]{1,0:T(8,128)S(1)}, u32[]{:S(2)}, u32[]{:S(2)}) collective-permute-start(f32[256,128]{1,0:T(8,128)S(1)} %get-tuple-element.43.mine_ref), channel_id=1, source_target_pairs={{0,1},{1,0},{2,3},{3,2},{4,5},{5,4},{6,7},{7,6},{8,9},{9,8},{10,11... | collective-permute-start | bytes 393224 | tf_op jit(solution)/shard_map/ppermute | solution.py:331
  27.8 2.5 %collective-permute-start.4 = (f32[896,256]{1,0:T(8,128)S(1)}, f32[896,256]{1,0:T(8,128)S(1)}, u32[]{:S(2)}, u32[]{:S(2)}) collective-permute-start(f32[896,256]{1,0:T(8,128)S(1)} %collective-permute-done.3.side_ref.refs_0_), channel_id=1, source_target_pairs={{0,1},{1,0},{2,3},{3,2},{4,5},{5,4},{6,7},{7,6},{8,9},{9,8},{10,11... | collective-permute-start | bytes 2752520 | tf_op jit(solution)/shard_map/ppermute | solution.py:331
  27.9 8.7 %collective-permute-start.2 = (f32[256,256]{1,0:T(8,128)S(1)}, f32[256,256]{1,0:T(8,128)S(1)}, u32[]{:S(2)}, u32[]{:S(2)}) collective-permute-start(f32[256,256]{1,0:T(8,128)S(1)} %get-tuple-element.44), channel_id=1, source_target_pairs={{0,2},{1,3},{2,0},{3,1},{4,6},{5,7},{6,4},{7,5},{8,10},{9,11},{10,... | collective-permute-start | bytes 786440 | tf_op jit(solution)/shard_map/ppermute | solution.py:331
  36.6 2.8 %collective-permute-start.5 = (f32[256,256]{1,0:T(8,128)S(1)}, f32[256,256]{1,0:T(8,128)S(1)}, u32[]{:S(2)}, u32[]{:S(2)}) collective-permute-start(f32[256,256]{1,0:T(8,128)S(1)} %collective-permute-done.2.side_ref), channel_id=1, source_target_pairs={{0,1},{1,0},{2,3},{3,2},{4,5},{5,4},{6,7},{7,6},{8,9},{9,8},{10,11... | collective-permute-start | bytes 786440 | tf_op jit(solution)/shard_map/ppermute | solution.py:331
  36.6 14.2 %collective-permute-start.6 = (f32[384,128]{1,0:T(8,128)S(1)}, f32[384,128]{1,0:T(8,128)S(1)}, u32[]{:S(2)}, u32[]{:S(2)}) collective-permute-start(f32[384,128]{1,0:T(8,128)S(1)} %get-tuple-element.50.refs_0_), channel_id=1, source_target_pairs={{0,4},{1,5},{2,6},{3,7},{4,0},{5,1},{6,2},{7,3},{8,12},{9,13},{10,... | collective-permute-start | bytes 589832 | tf_op jit(solution)/shard_map/ppermute | solution.py:331
  40.4 11.5 %collective-permute-start.7 = (f32[128,128]{1,0:T(8,128)S(1)}, f32[128,128]{1,0:T(8,128)S(1)}, u32[]{:S(2)}, u32[]{:S(2)}) collective-permute-start(f32[128,128]{1,0:T(8,128)S(1)} %get-tuple-element.52.refs_1_), channel_id=1, source_target_pairs={{0,4},{1,5},{2,6},{3,7},{4,0},{5,1},{6,2},{7,3},{8,12},{9,13},{10,... | collective-permute-start | bytes 196616 | tf_op jit(solution)/shard_map/ppermute | solution.py:331
  52.7 5.0 %collective-permute-start.8 = (f32[264,128]{1,0:T(8,128)S(1)}, f32[264,128]{1,0:T(8,128)S(1)}, u32[]{:S(2)}, u32[]{:S(2)}) collective-permute-start(f32[264,128]{1,0:T(8,128)S(1)} %shard_map.53), channel_id=1, source_target_pairs={{0,8},{1,17},{2,10},{3,19},{4,12},{5,21},{6,14},{7,23},{8,0},{9,25... | collective-permute-start | bytes 405512 | tf_op jit(solution)/shard_map/ppermute | solution.py:342
  55.1 5.8 %collective-permute-start.14 = (f32[264,128]{1,0:T(8,128)S(1)}, f32[264,128]{1,0:T(8,128)S(1)}, u32[]{:S(2)}, u32[]{:S(2)}) collective-permute-start(f32[264,128]{1,0:T(8,128)S(1)} %shard_map.57), channel_id=1, source_target_pairs={{0,8},{1,17},{2,10},{3,19},{4,12},{5,21},{6,14},{7,23},{8,0},{9,25... | collective-permute-start | bytes 405512 | tf_op jit(solution)/shard_map/ppermute | solution.py:342
  57.8 5.1 %collective-permute-start.9 = (f32[264,128]{1,0:T(8,128)S(1)}, f32[264,128]{1,0:T(8,128)S(1)}, u32[]{:S(2)}, u32[]{:S(2)}) collective-permute-start(f32[264,128]{1,0:T(8,128)S(1)} %add.25.refs_0_), channel_id=1, source_target_pairs={{0,16},{1,9},{2,18},{3,11},{4,20},{5,13},{6,22},{7,15},{8,24},{9,1... | collective-permute-start | bytes 405512 | tf_op jit(solution)/shard_map/ppermute | solution.py:342
  60.9 5.1 %collective-permute-start.15 = (f32[264,128]{1,0:T(8,128)S(1)}, f32[264,128]{1,0:T(8,128)S(1)}, u32[]{:S(2)}, u32[]{:S(2)}) collective-permute-start(f32[264,128]{1,0:T(8,128)S(1)} %add.27.refs_0_), channel_id=1, source_target_pairs={{0,16},{1,9},{2,18},{3,11},{4,20},{5,13},{6,22},{7,15},{8,24},{9,1... | collective-permute-start | bytes 405512 | tf_op jit(solution)/shard_map/ppermute | solution.py:342
  64.4 12.1 %collective-permute-start.10 = (f32[264,128]{1,0:T(8,128)S(1)}, f32[264,128]{1,0:T(8,128)S(1)}, u32[]{:S(2)}, u32[]{:S(2)}) collective-permute-start(f32[264,128]{1,0:T(8,128)S(1)} %get-tuple-element.59.refs_0_), channel_id=1, source_target_pairs={{0,4},{1,5},{2,6},{3,7},{4,0},{5,1},{6,2},{7,3},{8,12},{9,13},{10,... | collective-permute-start | bytes 405512 | tf_op jit(solution)/shard_map/ppermute | solution.py:331
  67.5 10.9 %collective-permute-start.16 = (f32[264,128]{1,0:T(8,128)S(1)}, f32[264,128]{1,0:T(8,128)S(1)}, u32[]{:S(2)}, u32[]{:S(2)}) collective-permute-start(f32[264,128]{1,0:T(8,128)S(1)} %get-tuple-element.63.refs_0_), channel_id=1, source_target_pairs={{0,4},{1,5},{2,6},{3,7},{4,0},{5,1},{6,2},{7,3},{8,12},{9,13},{10,... | collective-permute-start | bytes 405512 | tf_op jit(solution)/shard_map/ppermute | solution.py:331
  77.4 5.1 %collective-permute-start.11 = (f32[264,128]{1,0:T(8,128)S(1)}, f32[264,128]{1,0:T(8,128)S(1)}, u32[]{:S(2)}, u32[]{:S(2)}) collective-permute-start(f32[264,128]{1,0:T(8,128)S(1)} %get-tuple-element.60), channel_id=1, source_target_pairs={{0,8},{1,17},{2,10},{3,19},{4,12},{5,21},{6,14},{7,23},{8,0},{9,25... | collective-permute-start | bytes 405512 | tf_op jit(solution)/shard_map/ppermute | solution.py:342
  79.3 6.1 %collective-permute-start.17 = (f32[264,128]{1,0:T(8,128)S(1)}, f32[264,128]{1,0:T(8,128)S(1)}, u32[]{:S(2)}, u32[]{:S(2)}) collective-permute-start(f32[264,128]{1,0:T(8,128)S(1)} %get-tuple-element.64), channel_id=1, source_target_pairs={{0,8},{1,17},{2,10},{3,19},{4,12},{5,21},{6,14},{7,23},{8,0},{9,25... | collective-permute-start | bytes 405512 | tf_op jit(solution)/shard_map/ppermute | solution.py:342
  82.5 5.6 %collective-permute-start.12 = (f32[264,128]{1,0:T(8,128)S(1)}, f32[264,128]{1,0:T(8,128)S(1)}, u32[]{:S(2)}, u32[]{:S(2)}) collective-permute-start(f32[264,128]{1,0:T(8,128)S(1)} %add.26.refs_0_), channel_id=1, source_target_pairs={{0,16},{1,9},{2,18},{3,11},{4,20},{5,13},{6,22},{7,15},{8,24},{9,1... | collective-permute-start | bytes 405512 | tf_op jit(solution)/shard_map/ppermute | solution.py:342
  85.3 5.1 %collective-permute-start.18 = (f32[264,128]{1,0:T(8,128)S(1)}, f32[264,128]{1,0:T(8,128)S(1)}, u32[]{:S(2)}, u32[]{:S(2)}) collective-permute-start(f32[264,128]{1,0:T(8,128)S(1)} %add.28.refs_0_), channel_id=1, source_target_pairs={{0,16},{1,9},{2,18},{3,11},{4,20},{5,13},{6,22},{7,15},{8,24},{9,1... | collective-permute-start | bytes 405512 | tf_op jit(solution)/shard_map/ppermute | solution.py:342
  89.6 9.9 %collective-permute-start.13 = (f32[264,128]{1,0:T(8,128)S(1)}, f32[264,128]{1,0:T(8,128)S(1)}, u32[]{:S(2)}, u32[]{:S(2)}) collective-permute-start(f32[264,128]{1,0:T(8,128)S(1)} %get-tuple-element.61.own_ref), channel_id=1, source_target_pairs={{0,4},{1,5},{2,6},{3,7},{4,0},{5,1},{6,2},{7,3},{8,12},{9,13},{10,... | collective-permute-start | bytes 405512 | tf_op jit(solution)/shard_map/ppermute | solution.py:331
  91.9 9.1 %collective-permute-start.19 = (f32[264,128]{1,0:T(8,128)S(1)}, f32[264,128]{1,0:T(8,128)S(1)}, u32[]{:S(2)}, u32[]{:S(2)}) collective-permute-start(f32[264,128]{1,0:T(8,128)S(1)} %get-tuple-element.70.own_ref), channel_id=1, source_target_pairs={{0,4},{1,5},{2,6},{3,7},{4,0},{5,1},{6,2},{7,3},{8,12},{9,13},{10,... | collective-permute-start | bytes 405512 | tf_op jit(solution)/shard_map/ppermute | solution.py:331
  100.8 5.8 %collective-permute-start.20 = (f32[328,128]{1,0:T(8,128)S(1)}, f32[328,128]{1,0:T(8,128)S(1)}, u32[]{:S(2)}, u32[]{:S(2)}) collective-permute-start(f32[328,128]{1,0:T(8,128)S(1)} %get-tuple-element.75), channel_id=1, source_target_pairs={{0,2},{1,3},{2,0},{3,1},{4,6},{5,7},{6,4},{7,5},{8,10},{9,11},{10,... | collective-permute-start | bytes 503816 | tf_op jit(solution)/shard_map/ppermute | solution.py:331
  102.4 4.2 %collective-permute-start.21 = (f32[72,128]{1,0:T(8,128)S(1)}, f32[72,128]{1,0:T(8,128)S(1)}, u32[]{:S(2)}, u32[]{:S(2)}) collective-permute-start(f32[72,128]{1,0:T(8,128)S(1)} %get-tuple-element.76), channel_id=1, source_target_pairs={{0,2},{1,3},{2,0},{3,1},{4,6},{5,7},{6,4},{7,5},{8,10},{9,11},{10,... | collective-permute-start | bytes 110600 | tf_op jit(solution)/shard_map/ppermute | solution.py:331
  107.2 1.5 %collective-permute-start.22 = (f32[392,128]{1,0:T(8,128)S(1)}, f32[392,128]{1,0:T(8,128)S(1)}, u32[]{:S(2)}, u32[]{:S(2)}) collective-permute-start(f32[392,128]{1,0:T(8,128)S(1)} %get-tuple-element.78), channel_id=1, source_target_pairs={{0,1},{1,0},{2,3},{3,2},{4,5},{5,4},{6,7},{7,6},{8,9},{9,8},{10,11... | collective-permute-start | bytes 602120 | tf_op jit(solution)/shard_map/ppermute | solution.py:331
  109.3 3.7 %collective-permute-start.23 = (f32[8,256]{1,0:T(8,128)S(1)}, f32[8,256]{1,0:T(8,128)S(1)}, u32[]{:S(2)}, u32[]{:S(2)}) collective-permute-start(f32[8,256]{1,0:T(8,128)S(1)} %get-tuple-element.80.known_ref.refs_4_), channel_id=1, source_target_pairs={{0,8},{1,17},{2,10},{3,19},{4,12},{5,21},{6,14},{7,23},{8,0},{9,25... | collective-permute-start | bytes 24584 | tf_op jit(solution)/shard_map/ppermute | solution.py:342
  113.0 3.7 %collective-permute-start.24 = (f32[8,256]{1,0:T(8,128)S(1)}, f32[8,256]{1,0:T(8,128)S(1)}, u32[]{:S(2)}, u32[]{:S(2)}) collective-permute-start(f32[8,256]{1,0:T(8,128)S(1)} %add.29.a_ref), channel_id=1, source_target_pairs={{0,16},{1,9},{2,18},{3,11},{4,20},{5,13},{6,22},{7,15},{8,24},{9,1... | collective-permute-start | bytes 24584 | tf_op jit(solution)/shard_map/ppermute | solution.py:342

commit v6 on v4

--- a/solution.py
+++ b/solution.py
@@ -68,13 +68,13 @@
     return jnp.where(left, first, turn(second, cols))
 
 
-def chunk_at(place_ref, shift):
-    return lax.rem(place_ref[0] + shift + CHIPS, CHIPS)
+def chunk_at(place_ref, other):
+    return place_ref[0] ^ other
 
 
 def ordered_tiles(place_ref, tiles, scratch_ref):
-    for shift, tile in enumerate(tiles):
-        start = pl.multiple_of(chunk_at(place_ref, -shift) * TILE, TILE)
+    for other, tile in enumerate(tiles):
+        start = pl.multiple_of(chunk_at(place_ref, other) * TILE, TILE)
         scratch_ref[pl.ds(start, TILE), :] = tile
     total = scratch_ref[:TILE, :]
     for i in range(1, CHIPS):
@@ -82,8 +82,8 @@
     return total
 
 
-def chunk_product(place_ref, shift, rows, rhs, high_ref, low_ref):
-    cut = pl.ds(pl.multiple_of(chunk_at(place_ref, shift) * rows, rows), rows)
+def chunk_product(place_ref, other, rows, rhs, high_ref, low_ref):
+    cut = pl.ds(pl.multiple_of(chunk_at(place_ref, other) * rows, rows), rows)
     total = dot(high_ref[cut, :], rhs) + dot(low_ref[cut, :], rhs)
     return total
 
@@ -101,11 +101,11 @@
     z = jnp.concatenate([near_ref[...], got_ref[...]], axis=0)
     rhs = jnp.concatenate(split(z), axis=1).astype(BF16)
     cols = LANES // HALVES
-    for shift in range(CHIPS):
-        total = chunk_product(place_ref, shift, rows, rhs, high_ref, low_ref)
+    for other in range(CHIPS):
+        total = chunk_product(place_ref, other, rows, rhs, high_ref, low_ref)
         y = (total[:, :LANES] + total[:, LANES:]).T
         for h in range(HALVES):
-            ref = sends[h * CHIPS + shift]
+            ref = sends[h * CHIPS + other]
             store_blocks(ref, y[h * cols : (h + 1) * cols])
             ref[-TILE:, :] = jnp.zeros((TILE, LANES), F32)
 
@@ -136,10 +136,10 @@
     cols = LANES // HALVES
     rows = high_ref.shape[0] // CHIPS
     z = None
-    for shift, ref in enumerate(parts):
+    for other, ref in enumerate(parts):
         y = wide(ref[:-TILE, :], cols)
         lhs = jnp.concatenate(split(y), axis=0).astype(BF16)
-        cut = pl.ds(pl.multiple_of(chunk_at(place_ref, -shift) * rows, rows), rows)
+        cut = pl.ds(pl.multiple_of(chunk_at(place_ref, other) * rows, rows), rows)
         term = dot(lhs, high_ref[cut, :]) + dot(lhs, low_ref[cut, :])
         z = term if z is None else z + term
     store_blocks(z_ref, z[:cols] + z[cols:])
@@ -158,8 +158,8 @@
         store_blocks(z_ref, z)
     tail = squares_tile(z)
     rhs = jnp.concatenate(split(z), axis=0).T.astype(BF16)
-    for shift, ref in enumerate(sends):
-        y = chunk_product(place_ref, shift, rows, rhs, high_ref, low_ref).T
+    for other, ref in enumerate(sends):
+        y = chunk_product(place_ref, other, rows, rhs, high_ref, low_ref).T
         store_blocks(ref, y[:cols] + y[cols:])
         ref[-TILE:, :] = tail
 
@@ -265,9 +265,6 @@
     def swap(x, bits):
         return lax.ppermute(x, "snap", [(i, i ^ bits) for i in range(places)])
 
-    def shift(x, d):
-        return lax.ppermute(x, "snap", [(i, (i + 2 * d) % places) for i in range(places)])
-
     def swap_cell(x, step):
         def target(cell, i):
             return cell ^ (1 if i % 2 == step else 2)
@@ -280,10 +277,10 @@
         return x, swap_cell(x, 1)
 
     def scatter(parts):
-        return [parts[0]] + [shift(parts[d], d) for d in range(1, CHIPS)]
+        return [parts[0]] + [swap(parts[d], 2 * d) for d in range(1, CHIPS)]
 
     def gather(part):
-        return [part] + [shift(part, d) for d in range(1, CHIPS)]
+        return [part] + [swap(part, 2 * d) for d in range(1, CHIPS)]
 
     def sketch_half(index):
         return lax.dynamic_slice_in_dim(sketch, index * LANES, LANES, 1)

time: 117 us -> 118 us (level)
    ppermute x7 -> x37, starting transfers between devices: 3.96 us -> 54.5 us  [swap(): return lax.ppermute(x, 'snap', [(i, i ^ bits) for i in range(places)])]
    ppermute x30 -> x0, starting transfers between devices: 47 us -> none  [shift(): lax.ppermute(x, 'snap', [(i, (i + 2 * d) % places) for i in range(places)])]
    ppermute x7 -> x37, waiting for transfers between devices: 7.5 us -> 18.8 us  [swap(): return lax.ppermute(x, 'snap', [(i, i ^ bits) for i in range(places)])]
    ppermute x30 -> x0, waiting for transfers between devices: 9.06 us -> none  [shift(): lax.ppermute(x, 'snap', [(i, (i + 2 * d) % places) for i in range(places)])]
    ppermute x10, starting transfers between devices: 17.9 us -> 14.9 us  [swap_cell(): return lax.ppermute(x, ('cell', 'snap'), perm)]
    ppermute x10, waiting for transfers between devices: 9.61 us -> 8.23 us  [swap_cell(): return lax.ppermute(x, ('cell', 'snap'), perm)]
  transfers between devices with their start and end apart: 47 -> 47, of which waited for: 19 -> 20; matrix products, arithmetic and copies ran while one was open for 1% -> 1% of each run, Pallas kernels for 13% -> 13%
where the time goes in v6:
time: 118 us
  starting transfers between devices  69.4 us (59%)
  waiting for transfers between devices  27 us (23%)
  Pallas kernels  18.6 us (16%)
  local copies, waits for them, and re-layouts  2.22 us (2%)
    ppermute x37, starting transfers between devices, swap(): return lax.ppermute(x, 'snap', [(i, i ^ bits) for i in range(places)])  54.5 us
    ppermute x37, waiting for transfers between devices, swap(): return lax.ppermute(x, 'snap', [(i, i ^ bits) for i in range(places)])  18.8 us
    pallas_call x18, Pallas kernels, call(): pl.pallas_call(kernel, out_shape=[jax.ShapeDtypeStruct(shape, dtype) for...  18.6 us
    ppermute x10, starting transfers between devices, swap_cell(): return lax.ppermute(x, ('cell', 'snap'), perm)  14.9 us
    ppermute x10, waiting for transfers between devices, swap_cell(): return lax.ppermute(x, ('cell', 'snap'), perm)  8.23 us
  transfers between devices with their start and end apart: 47, of which 20 were waited for; matrix products, arithmetic and copies ran while one was open for 1% of the time, Pallas kernels for 13%

profile of v6, /device:TPU:0, one launch (start us, length us, event | category | flops | bytes accessed | tf_op | source)
XLA Modules:
  0.0 118.2 jit_solution(6556833955134432156)
XLA Ops:
  1.1 1.0 constant_dynamic-slice_fusion
  2.3 1.3 %collective-permute-done.1.got_ref = f32[256,128]{1,0:T(8,128)S(1)} collective-permute-done((f32[256,128]{1,0:T(8,128)S(1)}, f32[256,128]{1,0:T(8,128)S(1)}, u32[]{:S(2)}, u32[]{:S(2)}) %collective-permute-start.1) | collective-permute-done | bytes 131104 | tf_op jit(solution)/shard_map/ppermute | solution.py:266
  3.6 1.2 %copy-done = f32[1024,256]{1,0:T(8,128)S(1)} copy-done((f32[1024,256]{1,0:T(8,128)S(1)}, f32[1024,256]{1,0:T(8,128)}, u32[]{:S(2)}) %copy-start) | copy-done | bytes 1048600
  4.9 1.7 %shard_map.49 = (f32[136,128]{1,0:T(8,128)S(1)}, f32[136,128]{1,0:T(8,128)S(1)}, f32[136,128]{1,0:T(8,128)S(1)}, f32[136,128]{1,0:T(8,128)S(1)}, f32[136,128]{1,...) custom-call(s32[2]{0:T(128)S(1)} %pad_add_fusion.place_ref, ...), custom_call_target="tpu_custom_call" | custom-call | tf_op jit(solution)/shard_map/pallas_call | solution.py:220
  6.5 3.0 %collective-permute-start.2 = (f32[136,128]{1,0:T(8,128)S(1)}, f32[136,128]{1,0:T(8,128)S(1)}, u32[]{:S(2)}, u32[]{:S(2)}) collective-permute-start(f32[136,128]{1,0:T(8,128)S(1)} %get-tuple-element.48), channel_id=1, source_target_pairs={{0,2},{1,3},{2,0},{3,1},{4,6},{5,7},{6,4},{7,5},{8,10},{9,11},{10,... | collective-permute-start | bytes 208904 | tf_op jit(solution)/shard_map/ppermute | solution.py:266
  9.5 2.6 %collective-permute-start.3 = (f32[136,128]{1,0:T(8,128)S(1)}, f32[136,128]{1,0:T(8,128)S(1)}, u32[]{:S(2)}, u32[]{:S(2)}) collective-permute-start(f32[136,128]{1,0:T(8,128)S(1)} %get-tuple-element.49), channel_id=1, source_target_pairs={{0,4},{1,5},{2,6},{3,7},{4,0},{5,1},{6,2},{7,3},{8,12},{9,13},{10,... | collective-permute-start | bytes 208904 | tf_op jit(solution)/shard_map/ppermute | solution.py:266
  12.1 0.9 collective-permute-start.21
  13.0 3.5 %collective-permute-start.22 = (f32[136,128]{1,0:T(8,128)S(1)}, f32[136,128]{1,0:T(8,128)S(1)}, u32[]{:S(2)}, u32[]{:S(2)}) collective-permute-start(f32[136,128]{1,0:T(8,128)S(1)} %get-tuple-element.65), channel_id=1, source_target_pairs={{0,4},{1,5},{2,6},{3,7},{4,0},{5,1},{6,2},{7,3},{8,12},{9,13},{10,... | collective-permute-start | bytes 208904 | tf_op jit(solution)/shard_map/ppermute | solution.py:266
  16.6 0.7 collective-permute-done.3.refs_2_
  17.4 1.8 %collective-permute-done.4.refs_3_ = f32[136,128]{1,0:T(8,128)S(1)} collective-permute-done((f32[136,128]{1,0:T(8,128)S(1)}, f32[136,128]{1,0:T(8,128)S(1)}, u32[]{:S(2)}, u32[]{:S(2)}) %collective-permute-start.4) | collective-permute-done | bytes 69664 | tf_op jit(solution)/shard_map/ppermute | solution.py:266
  19.8 6.5 %collective-permute-start.7 = (f32[136,128]{1,0:T(8,128)S(1)}, f32[136,128]{1,0:T(8,128)S(1)}, u32[]{:S(2)}, u32[]{:S(2)}) collective-permute-start(f32[136,128]{1,0:T(8,128)S(1)} %shard_map.50.refs_0_), channel_id=1, source_target_pairs={{0,6},{1,7},{2,4},{3,5},{4,2},{5,3},{6,0},{7,1},{8,14},{9,15},{10,... | collective-permute-start | bytes 208904 | tf_op jit(solution)/shard_map/ppermute | solution.py:266
  28.0 3.4 %collective-permute-start.26 = (f32[136,128]{1,0:T(8,128)S(1)}, f32[136,128]{1,0:T(8,128)S(1)}, u32[]{:S(2)}, u32[]{:S(2)}) collective-permute-start(f32[136,128]{1,0:T(8,128)S(1)} %shard_map.57.refs_0_), channel_id=1, source_target_pairs={{0,6},{1,7},{2,4},{3,5},{4,2},{5,3},{6,0},{7,1},{8,14},{9,15},{10,... | collective-permute-start | bytes 208904 | tf_op jit(solution)/shard_map/ppermute | solution.py:266
  31.4 1.4 %collective-permute-start.24 = (f32[136,128]{1,0:T(8,128)S(1)}, f32[136,128]{1,0:T(8,128)S(1)}, u32[]{:S(2)}, u32[]{:S(2)}) collective-permute-start(f32[136,128]{1,0:T(8,128)S(1)} %shard_map.57.refs_0_), channel_id=1, source_target_pairs={{0,2},{1,3},{2,0},{3,1},{4,6},{5,7},{6,4},{7,5},{8,10},{9,11},{10,... | collective-permute-start | bytes 208904 | tf_op jit(solution)/shard_map/ppermute | solution.py:266
  32.8 0.8 collective-permute-done.6.refs_2_
  33.6 1.0 shard_map.51
  34.6 1.6 %collective-permute-start.8 = (f32[264,128]{1,0:T(8,128)S(1)}, f32[264,128]{1,0:T(8,128)S(1)}, u32[]{:S(2)}, u32[]{:S(2)}) collective-permute-start(f32[264,128]{1,0:T(8,128)S(1)} %shard_map.51), channel_id=1, source_target_pairs={{0,8},{1,17},{2,10},{3,19},{4,12},{5,21},{6,14},{7,23},{8,0},{9,25... | collective-permute-start | bytes 405512 | tf_op jit(solution)/shard_map/ppermute | solution.py:273
  36.2 0.8 collective-permute-done.25.refs_2_
  36.9 1.0 shard_map.58
  37.9 1.5 %collective-permute-start.27 = (f32[264,128]{1,0:T(8,128)S(1)}, f32[264,128]{1,0:T(8,128)S(1)}, u32[]{:S(2)}, u32[]{:S(2)}) collective-permute-start(f32[264,128]{1,0:T(8,128)S(1)} %shard_map.58), channel_id=1, source_target_pairs={{0,8},{1,17},{2,10},{3,19},{4,12},{5,21},{6,14},{7,23},{8,0},{9,25... | collective-permute-start | bytes 405512 | tf_op jit(solution)/shard_map/ppermute | solution.py:273
  39.7 2.7 %collective-permute-start.9 = (f32[264,128]{1,0:T(8,128)S(1)}, f32[264,128]{1,0:T(8,128)S(1)}, u32[]{:S(2)}, u32[]{:S(2)}) collective-permute-start(f32[264,128]{1,0:T(8,128)S(1)} %add.35.a_ref), channel_id=1, source_target_pairs={{0,16},{1,9},{2,18},{3,11},{4,20},{5,13},{6,22},{7,15},{8,24},{9,1... | collective-permute-start | bytes 405512 | tf_op jit(solution)/shard_map/ppermute | solution.py:273
  42.4 1.1 collective-permute-done.27
  43.5 1.4 %collective-permute-start.28 = (f32[264,128]{1,0:T(8,128)S(1)}, f32[264,128]{1,0:T(8,128)S(1)}, u32[]{:S(2)}, u32[]{:S(2)}) collective-permute-start(f32[264,128]{1,0:T(8,128)S(1)} %add.37.a_ref), channel_id=1, source_target_pairs={{0,16},{1,9},{2,18},{3,11},{4,20},{5,13},{6,22},{7,15},{8,24},{9,1... | collective-permute-start | bytes 405512 | tf_op jit(solution)/shard_map/ppermute | solution.py:273
  45.4 1.5 %shard_map.52 = (f32[136,128]{1,0:T(8,128)S(1)}, f32[136,128]{1,0:T(8,128)S(1)}, f32[136,128]{1,0:T(8,128)S(1)}, f32[136,128]{1,0:T(8,128)S(1)}, f32[8,128]{1,0:T(8,128)S(1)}) custom-call(s32[2]{0:T(128)S(1)} %pad_add_fusion.place_ref, f32[264,128]{1,0:T(8,128)S(1)} %add.35.a_ref, f32[264,128]{1,0:T(8,128)S(1)} %collective-permute-done.9.b_ref, ...), custom_call_target="tpu_custom_call" | custom-call | tf_op jit(solution)/shard_map/pallas_call | solution.py:220
  46.9 1.0 collective-permute-start.10
  47.9 3.5 %collective-permute-start.11 = (f32[136,128]{1,0:T(8,128)S(1)}, f32[136,128]{1,0:T(8,128)S(1)}, u32[]{:S(2)}, u32[]{:S(2)}) collective-permute-start(f32[136,128]{1,0:T(8,128)S(1)} %get-tuple-element.55), channel_id=1, source_target_pairs={{0,4},{1,5},{2,6},{3,7},{4,0},{5,1},{6,2},{7,3},{8,12},{9,13},{10,... | collective-permute-start | bytes 208904 | tf_op jit(solution)/shard_map/ppermute | solution.py:266
  51.4 1.5 %shard_map.59 = (f32[136,128]{1,0:T(8,128)S(1)}, f32[136,128]{1,0:T(8,128)S(1)}, f32[136,128]{1,0:T(8,128)S(1)}, f32[136,128]{1,0:T(8,128)S(1)}, f32[8,128]{1,0:T(8,128)S(1)}) custom-call(s32[2]{0:T(128)S(1)} %pad_add_fusion.place_ref, f32[264,128]{1,0:T(8,128)S(1)} %add.37.a_ref, f32[264,128]{1,0:T(8,128)S(1)} %collective-permute-done.28.b_ref, ...), custom_call_target="tpu_custom_call" | custom-call | tf_op jit(solution)/shard_map/pallas_call | solution.py:220
  53.5 3.8 %collective-permute-start.30 = (f32[136,128]{1,0:T(8,128)S(1)}, f32[136,128]{1,0:T(8,128)S(1)}, u32[]{:S(2)}, u32[]{:S(2)}) collective-permute-start(f32[136,128]{1,0:T(8,128)S(1)} %get-tuple-element.69), channel_id=1, source_target_pairs={{0,4},{1,5},{2,6},{3,7},{4,0},{5,1},{6,2},{7,3},{8,12},{9,13},{10,... | collective-permute-start | bytes 208904 | tf_op jit(solution)/shard_map/ppermute | solution.py:266
  57.3 0.9 collective-permute-done.12.refs_3_
  58.3 0.7 shard_map.53
  59.0 3.0 %collective-permute-start.15 = (f32[136,128]{1,0:T(8,128)S(1)}, f32[136,128]{1,0:T(8,128)S(1)}, u32[]{:S(2)}, u32[]{:S(2)}) collective-permute-start(f32[136,128]{1,0:T(8,128)S(1)} %get-tuple-element.57.refs_0_), channel_id=1, source_target_pairs={{0,6},{1,7},{2,4},{3,5},{4,2},{5,3},{6,0},{7,1},{8,14},{9,15},{10,... | collective-permute-start | bytes 208904 | tf_op jit(solution)/shard_map/ppermute | solution.py:266
  62.0 1.7 %collective-permute-start.14 = (f32[136,128]{1,0:T(8,128)S(1)}, f32[136,128]{1,0:T(8,128)S(1)}, u32[]{:S(2)}, u32[]{:S(2)}) collective-permute-start(f32[136,128]{1,0:T(8,128)S(1)} %get-tuple-element.57.refs_0_), channel_id=1, source_target_pairs={{0,4},{1,5},{2,6},{3,7},{4,0},{5,1},{6,2},{7,3},{8,12},{9,13},{10,... | collective-permute-start | bytes 208904 | tf_op jit(solution)/shard_map/ppermute | solution.py:266
  63.7 1.1 collective-permute-done.30.refs_2_
  64.8 0.7 shard_map.60
  65.5 2.5 %collective-permute-start.34 = (f32[136,128]{1,0:T(8,128)S(1)}, f32[136,128]{1,0:T(8,128)S(1)}, u32[]{:S(2)}, u32[]{:S(2)}) collective-permute-start(f32[136,128]{1,0:T(8,128)S(1)} %get-tuple-element.71.refs_0_), channel_id=1, source_target_pairs={{0,6},{1,7},{2,4},{3,5},{4,2},{5,3},{6,0},{7,1},{8,14},{9,15},{10,... | collective-permute-start | bytes 208904 | tf_op jit(solution)/shard_map/ppermute | solution.py:266
  68.0 2.2 %collective-permute-start.33 = (f32[136,128]{1,0:T(8,128)S(1)}, f32[136,128]{1,0:T(8,128)S(1)}, u32[]{:S(2)}, u32[]{:S(2)}) collective-permute-start(f32[136,128]{1,0:T(8,128)S(1)} %get-tuple-element.71.refs_0_), channel_id=1, source_target_pairs={{0,4},{1,5},{2,6},{3,7},{4,0},{5,1},{6,2},{7,3},{8,12},{9,13},{10,... | collective-permute-start | bytes 208904 | tf_op jit(solution)/shard_map/ppermute | solution.py:266
  70.7 1.0 shard_map.54
  71.7 1.6 %collective-permute-start.16 = (f32[264,128]{1,0:T(8,128)S(1)}, f32[264,128]{1,0:T(8,128)S(1)}, u32[]{:S(2)}, u32[]{:S(2)}) collective-permute-start(f32[264,128]{1,0:T(8,128)S(1)} %shard_map.54), channel_id=1, source_target_pairs={{0,8},{1,17},{2,10},{3,19},{4,12},{5,21},{6,14},{7,23},{8,0},{9,25... | collective-permute-start | bytes 405512 | tf_op jit(solution)/shard_map/ppermute | solution.py:273
  73.3 1.2 %collective-permute-done.32.refs_1_ = f32[136,128]{1,0:T(8,128)S(1)} collective-permute-done((f32[136,128]{1,0:T(8,128)S(1)}, f32[136,128]{1,0:T(8,128)S(1)}, u32[]{:S(2)}, u32[]{:S(2)}) %collective-permute-start.32) | collective-permute-done | bytes 69664 | tf_op jit(solution)/shard_map/ppermute | solution.py:266
  74.5 1.0 shard_map.61
  75.5 1.6 %collective-permute-start.35 = (f32[264,128]{1,0:T(8,128)S(1)}, f32[264,128]{1,0:T(8,128)S(1)}, u32[]{:S(2)}, u32[]{:S(2)}) collective-permute-start(f32[264,128]{1,0:T(8,128)S(1)} %shard_map.61), channel_id=1, source_target_pairs={{0,8},{1,17},{2,10},{3,19},{4,12},{5,21},{6,14},{7,23},{8,0},{9,25... | collective-permute-start | bytes 405512 | tf_op jit(solution)/shard_map/ppermute | solution.py:273
  77.1 1.4 %collective-permute-start.17 = (f32[264,128]{1,0:T(8,128)S(1)}, f32[264,128]{1,0:T(8,128)S(1)}, u32[]{:S(2)}, u32[]{:S(2)}) collective-permute-start(f32[264,128]{1,0:T(8,128)S(1)} %add.36.a_ref), channel_id=1, source_target_pairs={{0,16},{1,9},{2,18},{3,11},{4,20},{5,13},{6,22},{7,15},{8,24},{9,1... | collective-permute-start | bytes 405512 | tf_op jit(solution)/shard_map/ppermute | solution.py:273
  78.5 2.1 %collective-permute-done.35 = f32[264,128]{1,0:T(8,128)S(1)} collective-permute-done((f32[264,128]{1,0:T(8,128)S(1)}, f32[264,128]{1,0:T(8,128)S(1)}, u32[]{:S(2)}, u32[]{:S(2)}) %collective-permute-start.35) | collective-permute-done | bytes 135200 | tf_op jit(solution)/shard_map/ppermute | solution.py:273
  80.6 0.9 collective-permute-start.36
  82.2 1.5 %shard_map.55 = (f32[136,128]{1,0:T(8,128)S(1)}, f32[136,128]{1,0:T(8,128)S(1)}, f32[136,128]{1,0:T(8,128)S(1)}, f32[136,128]{1,0:T(8,128)S(1)}, f32[8,128]{1,0:T(8,128)S(1)}, /*index=5*/f32[256,128]{1,0:T(8,128)S(1)}) custom-call(s32[2]{0:T(128)S(1)} %pad_add_fusion.place_ref, f32[264,128]{1,0:T(8,128)S(1)} %add.36.a_ref, ...), custom_call_target="tpu_custom_call" | custom-call | tf_op jit(solution)/shard_map/pallas_call | solution.py:220
  83.7 2.4 %collective-permute-start.18 = (f32[136,128]{1,0:T(8,128)S(1)}, f32[136,128]{1,0:T(8,128)S(1)}, u32[]{:S(2)}, u32[]{:S(2)}) collective-permute-start(f32[136,128]{1,0:T(8,128)S(1)} %get-tuple-element.59), channel_id=1, source_target_pairs={{0,2},{1,3},{2,0},{3,1},{4,6},{5,7},{6,4},{7,5},{8,10},{9,11},{10,... | collective-permute-start | bytes 208904 | tf_op jit(solution)/shard_map/ppermute | solution.py:266
  86.1 1.5 %shard_map.62 = (f32[136,128]{1,0:T(8,128)S(1)}, f32[136,128]{1,0:T(8,128)S(1)}, f32[136,128]{1,0:T(8,128)S(1)}, f32[136,128]{1,0:T(8,128)S(1)}, f32[8,128]{1,0:T(8,128)S(1)}, /*index=5*/f32[256,128]{1,0:T(8,128)S(1)}) custom-call(s32[2]{0:T(128)S(1)} %pad_add_fusion.place_ref, f32[264,128]{1,0:T(8,128)S(1)} %add.38.a_ref, ...), custom_call_target="tpu_custom_call" | custom-call | tf_op jit(solution)/shard_map/pallas_call | solution.py:220
  87.6 1.1 collective-permute-start.37
  88.6 2.2 %collective-permute-start.19 = (f32[136,128]{1,0:T(8,128)S(1)}, f32[136,128]{1,0:T(8,128)S(1)}, u32[]{:S(2)}, u32[]{:S(2)}) collective-permute-start(f32[136,128]{1,0:T(8,128)S(1)} %get-tuple-element.60), channel_id=1, source_target_pairs={{0,4},{1,5},{2,6},{3,7},{4,0},{5,1},{6,2},{7,3},{8,12},{9,13},{10,... | collective-permute-start | bytes 208904 | tf_op jit(solution)/shard_map/ppermute | solution.py:266
  90.9 1.2 collective-permute-start.20
  92.0 0.8 collective-permute-start.38
  92.9 1.8 %collective-permute-start.39 = (f32[136,128]{1,0:T(8,128)S(1)}, f32[136,128]{1,0:T(8,128)S(1)}, u32[]{:S(2)}, u32[]{:S(2)}) collective-permute-start(f32[136,128]{1,0:T(8,128)S(1)} %get-tuple-element.75), channel_id=1, source_target_pairs={{0,6},{1,7},{2,4},{3,5},{4,2},{5,3},{6,0},{7,1},{8,14},{9,15},{10,... | collective-permute-start | bytes 208904 | tf_op jit(solution)/shard_map/ppermute | solution.py:266
  94.7 2.3 %collective-permute-done.20.refs_3_ = f32[136,128]{1,0:T(8,128)S(1)} collective-permute-done((f32[136,128]{1,0:T(8,128)S(1)}, f32[136,128]{1,0:T(8,128)S(1)}, u32[]{:S(2)}, u32[]{:S(2)}) %collective-permute-start.20) | collective-permute-done | bytes 69664 | tf_op jit(solution)/shard_map/ppermute | solution.py:266
  97.0 0.7 shard_map.56
  97.8 1.4 %collective-permute-done.38.refs_2_ = f32[136,128]{1,0:T(8,128)S(1)} collective-permute-done((f32[136,128]{1,0:T(8,128)S(1)}, f32[136,128]{1,0:T(8,128)S(1)}, u32[]{:S(2)}, u32[]{:S(2)}) %collective-permute-start.38) | collective-permute-done | bytes 69664 | tf_op jit(solution)/shard_map/ppermute | solution.py:266
  99.2 0.8 shard_map.63
  101.9 1.4 %collective-permute-start.41 = (f32[8,256]{1,0:T(8,128)S(1)}, f32[8,256]{1,0:T(8,128)S(1)}, u32[]{:S(2)}, u32[]{:S(2)}) collective-permute-start(f32[8,256]{1,0:T(8,128)S(1)} %get-tuple-element.86.known_ref), channel_id=1, source_target_pairs={{0,2},{1,3},{2,0},{3,1},{4,6},{5,7},{6,4},{7,5},{8,10},{9,11},{10,... | collective-permute-start | bytes 24584 | tf_op jit(solution)/shard_map/ppermute | solution.py:266
  103.3 2.3 %collective-permute-done.41 = f32[8,256]{1,0:T(8,128)S(1)} collective-permute-done((f32[8,256]{1,0:T(8,128)S(1)}, f32[8,256]{1,0:T(8,128)S(1)}, u32[]{:S(2)}, u32[]{:S(2)}) %collective-permute-start.41) | collective-permute-done | bytes 8224 | tf_op jit(solution)/shard_map/ppermute | solution.py:266
  105.7 1.3 %collective-permute-start.42 = (f32[8,256]{1,0:T(8,128)S(1)}, f32[8,256]{1,0:T(8,128)S(1)}, u32[]{:S(2)}, u32[]{:S(2)}) collective-permute-start(f32[8,256]{1,0:T(8,128)S(1)} %add.39), channel_id=1, source_target_pairs={{0,4},{1,5},{2,6},{3,7},{4,0},{5,1},{6,2},{7,3},{8,12},{9,13},{10,... | collective-permute-start | bytes 24584 | tf_op jit(solution)/shard_map/ppermute | solution.py:266
  106.9 3.3 %collective-permute-done.42 = f32[8,256]{1,0:T(8,128)S(1)} collective-permute-done((f32[8,256]{1,0:T(8,128)S(1)}, f32[8,256]{1,0:T(8,128)S(1)}, u32[]{:S(2)}, u32[]{:S(2)}) %collective-permute-start.42) | collective-permute-done | bytes 8224 | tf_op jit(solution)/shard_map/ppermute | solution.py:266
  110.2 1.5 %collective-permute-start.43 = (f32[8,256]{1,0:T(8,128)S(1)}, f32[8,256]{1,0:T(8,128)S(1)}, u32[]{:S(2)}, u32[]{:S(2)}) collective-permute-start(f32[8,256]{1,0:T(8,128)S(1)} %add.40), channel_id=1, source_target_pairs={{0,8},{1,17},{2,10},{3,19},{4,12},{5,21},{6,14},{7,23},{8,0},{9,25... | collective-permute-start | bytes 24584 | tf_op jit(solution)/shard_map/ppermute | solution.py:273
  111.7 2.1 %collective-permute-done.43 = f32[8,256]{1,0:T(8,128)S(1)} collective-permute-done((f32[8,256]{1,0:T(8,128)S(1)}, f32[8,256]{1,0:T(8,128)S(1)}, u32[]{:S(2)}, u32[]{:S(2)}) %collective-permute-start.43) | collective-permute-done | bytes 8224 | tf_op jit(solution)/shard_map/ppermute | solution.py:273
  113.9 0.7 collective-permute-start.44
  114.6 1.4 %shard_map.66 = f32[256,256]{1,0:T(8,128)} custom-call(s32[2]{0:T(128)S(1)} %pad_add_fusion.place_ref, f32[256,128]{1,0:T(8,128)S(1)} %get-tuple-element.88.first_ref, f32[256,128]{1,0:T(8,128)S(1)} %get-tuple-element.89.second_ref, f32[128,128]{1,0:T(8,128)S(1)} %collective-permute-done.45.got_first_ref, ...), custom_call_target="tpu_custom_call" | custom-call | tf_op jit(solution)/shard_map/pallas_call | solution.py:220
  116.0 1.5 %collective-permute-done.44.b_ref = f32[8,256]{1,0:T(8,128)S(1)} collective-permute-done((f32[8,256]{1,0:T(8,128)S(1)}, f32[8,256]{1,0:T(8,128)S(1)}, u32[]{:S(2)}, u32[]{:S(2)}) %collective-permute-start.44) | collective-permute-done | bytes 8224 | tf_op jit(solution)/shard_map/ppermute | solution.py:273
  (61 shorter events, 8.4 us)
Async XLA Ops:
  0.6 3.0 %collective-permute-start = (f32[1024,256]{1,0:T(8,128)}, f32[1024,256]{1,0:T(8,128)S(1)}, u32[]{:S(2)}, u32[]{:S(2)}) collective-permute-start(f32[1024,256]{1,0:T(8,128)} %own_ref.1), channel_id=1, source_target_pairs={{0,1},{1,0},{2,3},{3,2},{4,5},{5,4},{6,7},{7,6},{8,9},{9,8},{10,11... | collective-permute-start | bytes 3145736 | tf_op jit(solution)/shard_map/ppermute | solution.py:266
  2.1 1.5 %collective-permute-start.1 = (f32[256,128]{1,0:T(8,128)S(1)}, f32[256,128]{1,0:T(8,128)S(1)}, u32[]{:S(2)}, u32[]{:S(2)}) collective-permute-start(f32[256,128]{1,0:T(8,128)S(1)} %get-tuple-element.91), channel_id=1, source_target_pairs={{0,1},{1,0},{2,3},{3,2},{4,5},{5,4},{6,7},{7,6},{8,9},{9,8},{10,11... | collective-permute-start | bytes 393224 | tf_op jit(solution)/shard_map/ppermute | solution.py:266
  3.6 1.2 %copy-start = (f32[1024,256]{1,0:T(8,128)S(1)}, f32[1024,256]{1,0:T(8,128)}, u32[]{:S(2)}) copy-start(f32[1024,256]{1,0:T(8,128)} %own_ref.1) | copy-start | bytes 3145732
  6.5 10.0 %collective-permute-start.2 = (f32[136,128]{1,0:T(8,128)S(1)}, f32[136,128]{1,0:T(8,128)S(1)}, u32[]{:S(2)}, u32[]{:S(2)}) collective-permute-start(f32[136,128]{1,0:T(8,128)S(1)} %get-tuple-element.48), channel_id=1, source_target_pairs={{0,2},{1,3},{2,0},{3,1},{4,6},{5,7},{6,4},{7,5},{8,10},{9,11},{10,... | collective-permute-start | bytes 208904 | tf_op jit(solution)/shard_map/ppermute | solution.py:266
  9.5 7.8 %collective-permute-start.3 = (f32[136,128]{1,0:T(8,128)S(1)}, f32[136,128]{1,0:T(8,128)S(1)}, u32[]{:S(2)}, u32[]{:S(2)}) collective-permute-start(f32[136,128]{1,0:T(8,128)S(1)} %get-tuple-element.49), channel_id=1, source_target_pairs={{0,4},{1,5},{2,6},{3,7},{4,0},{5,1},{6,2},{7,3},{8,12},{9,13},{10,... | collective-permute-start | bytes 208904 | tf_op jit(solution)/shard_map/ppermute | solution.py:266
  12.1 7.0 %collective-permute-start.4 = (f32[136,128]{1,0:T(8,128)S(1)}, f32[136,128]{1,0:T(8,128)S(1)}, u32[]{:S(2)}, u32[]{:S(2)}) collective-permute-start(f32[136,128]{1,0:T(8,128)S(1)} %get-tuple-element.50), channel_id=1, source_target_pairs={{0,6},{1,7},{2,4},{3,5},{4,2},{5,3},{6,0},{7,1},{8,14},{9,15},{10,... | collective-permute-start | bytes 208904 | tf_op jit(solution)/shard_map/ppermute | solution.py:266
  12.1 14.7 %collective-permute-start.21 = (f32[136,128]{1,0:T(8,128)S(1)}, f32[136,128]{1,0:T(8,128)S(1)}, u32[]{:S(2)}, u32[]{:S(2)}) collective-permute-start(f32[136,128]{1,0:T(8,128)S(1)} %get-tuple-element.64), channel_id=1, source_target_pairs={{0,2},{1,3},{2,0},{3,1},{4,6},{5,7},{6,4},{7,5},{8,10},{9,11},{10,... | collective-permute-start | bytes 208904 | tf_op jit(solution)/shard_map/ppermute | solution.py:266
  13.0 14.3 %collective-permute-start.22 = (f32[136,128]{1,0:T(8,128)S(1)}, f32[136,128]{1,0:T(8,128)S(1)}, u32[]{:S(2)}, u32[]{:S(2)}) collective-permute-start(f32[136,128]{1,0:T(8,128)S(1)} %get-tuple-element.65), channel_id=1, source_target_pairs={{0,4},{1,5},{2,6},{3,7},{4,0},{5,1},{6,2},{7,3},{8,12},{9,13},{10,... | collective-permute-start | bytes 208904 | tf_op jit(solution)/shard_map/ppermute | solution.py:266
  16.5 10.8 %collective-permute-start.23 = (f32[136,128]{1,0:T(8,128)S(1)}, f32[136,128]{1,0:T(8,128)S(1)}, u32[]{:S(2)}, u32[]{:S(2)}) collective-permute-start(f32[136,128]{1,0:T(8,128)S(1)} %get-tuple-element.66), channel_id=1, source_target_pairs={{0,6},{1,7},{2,4},{3,5},{4,2},{5,3},{6,0},{7,1},{8,14},{9,15},{10,... | collective-permute-start | bytes 208904 | tf_op jit(solution)/shard_map/ppermute | solution.py:266
  19.8 11.6 %collective-permute-start.7 = (f32[136,128]{1,0:T(8,128)S(1)}, f32[136,128]{1,0:T(8,128)S(1)}, u32[]{:S(2)}, u32[]{:S(2)}) collective-permute-start(f32[136,128]{1,0:T(8,128)S(1)} %shard_map.50.refs_0_), channel_id=1, source_target_pairs={{0,6},{1,7},{2,4},{3,5},{4,2},{5,3},{6,0},{7,1},{8,14},{9,15},{10,... | collective-permute-start | bytes 208904 | tf_op jit(solution)/shard_map/ppermute | solution.py:266
  26.3 7.3 %collective-permute-start.6 = (f32[136,128]{1,0:T(8,128)S(1)}, f32[136,128]{1,0:T(8,128)S(1)}, u32[]{:S(2)}, u32[]{:S(2)}) collective-permute-start(f32[136,128]{1,0:T(8,128)S(1)} %shard_map.50.refs_0_), channel_id=1, source_target_pairs={{0,4},{1,5},{2,6},{3,7},{4,0},{5,1},{6,2},{7,3},{8,12},{9,13},{10,... | collective-permute-start | bytes 208904 | tf_op jit(solution)/shard_map/ppermute | solution.py:266
  26.8 6.8 %collective-permute-start.5 = (f32[136,128]{1,0:T(8,128)S(1)}, f32[136,128]{1,0:T(8,128)S(1)}, u32[]{:S(2)}, u32[]{:S(2)}) collective-permute-start(f32[136,128]{1,0:T(8,128)S(1)} %shard_map.50.refs_0_), channel_id=1, source_target_pairs={{0,2},{1,3},{2,0},{3,1},{4,6},{5,7},{6,4},{7,5},{8,10},{9,11},{10,... | collective-permute-start | bytes 208904 | tf_op jit(solution)/shard_map/ppermute | solution.py:266
  28.0 8.2 %collective-permute-start.26 = (f32[136,128]{1,0:T(8,128)S(1)}, f32[136,128]{1,0:T(8,128)S(1)}, u32[]{:S(2)}, u32[]{:S(2)}) collective-permute-start(f32[136,128]{1,0:T(8,128)S(1)} %shard_map.57.refs_0_), channel_id=1, source_target_pairs={{0,6},{1,7},{2,4},{3,5},{4,2},{5,3},{6,0},{7,1},{8,14},{9,15},{10,... | collective-permute-start | bytes 208904 | tf_op jit(solution)/shard_map/ppermute | solution.py:266
  31.4 5.5 %collective-permute-start.25 = (f32[136,128]{1,0:T(8,128)S(1)}, f32[136,128]{1,0:T(8,128)S(1)}, u32[]{:S(2)}, u32[]{:S(2)}) collective-permute-start(f32[136,128]{1,0:T(8,128)S(1)} %shard_map.57.refs_0_), channel_id=1, source_target_pairs={{0,4},{1,5},{2,6},{3,7},{4,0},{5,1},{6,2},{7,3},{8,12},{9,13},{10,... | collective-permute-start | bytes 208904 | tf_op jit(solution)/shard_map/ppermute | solution.py:266
  31.4 5.5 %collective-permute-start.24 = (f32[136,128]{1,0:T(8,128)S(1)}, f32[136,128]{1,0:T(8,128)S(1)}, u32[]{:S(2)}, u32[]{:S(2)}) collective-permute-start(f32[136,128]{1,0:T(8,128)S(1)} %shard_map.57.refs_0_), channel_id=1, source_target_pairs={{0,2},{1,3},{2,0},{3,1},{4,6},{5,7},{6,4},{7,5},{8,10},{9,11},{10,... | collective-permute-start | bytes 208904 | tf_op jit(solution)/shard_map/ppermute | solution.py:266
  34.6 5.1 %collective-permute-start.8 = (f32[264,128]{1,0:T(8,128)S(1)}, f32[264,128]{1,0:T(8,128)S(1)}, u32[]{:S(2)}, u32[]{:S(2)}) collective-permute-start(f32[264,128]{1,0:T(8,128)S(1)} %shard_map.51), channel_id=1, source_target_pairs={{0,8},{1,17},{2,10},{3,19},{4,12},{5,21},{6,14},{7,23},{8,0},{9,25... | collective-permute-start | bytes 405512 | tf_op jit(solution)/shard_map/ppermute | solution.py:273
  37.9 5.6 %collective-permute-start.27 = (f32[264,128]{1,0:T(8,128)S(1)}, f32[264,128]{1,0:T(8,128)S(1)}, u32[]{:S(2)}, u32[]{:S(2)}) collective-permute-start(f32[264,128]{1,0:T(8,128)S(1)} %shard_map.58), channel_id=1, source_target_pairs={{0,8},{1,17},{2,10},{3,19},{4,12},{5,21},{6,14},{7,23},{8,0},{9,25... | collective-permute-start | bytes 405512 | tf_op jit(solution)/shard_map/ppermute | solution.py:273
  39.7 5.7 %collective-permute-start.9 = (f32[264,128]{1,0:T(8,128)S(1)}, f32[264,128]{1,0:T(8,128)S(1)}, u32[]{:S(2)}, u32[]{:S(2)}) collective-permute-start(f32[264,128]{1,0:T(8,128)S(1)} %add.35.a_ref), channel_id=1, source_target_pairs={{0,16},{1,9},{2,18},{3,11},{4,20},{5,13},{6,22},{7,15},{8,24},{9,1... | collective-permute-start | bytes 405512 | tf_op jit(solution)/shard_map/ppermute | solution.py:273
  43.5 7.8 %collective-permute-start.28 = (f32[264,128]{1,0:T(8,128)S(1)}, f32[264,128]{1,0:T(8,128)S(1)}, u32[]{:S(2)}, u32[]{:S(2)}) collective-permute-start(f32[264,128]{1,0:T(8,128)S(1)} %add.37.a_ref), channel_id=1, source_target_pairs={{0,16},{1,9},{2,18},{3,11},{4,20},{5,13},{6,22},{7,15},{8,24},{9,1... | collective-permute-start | bytes 405512 | tf_op jit(solution)/shard_map/ppermute | solution.py:273
  46.9 10.4 %collective-permute-start.10 = (f32[136,128]{1,0:T(8,128)S(1)}, f32[136,128]{1,0:T(8,128)S(1)}, u32[]{:S(2)}, u32[]{:S(2)}) collective-permute-start(f32[136,128]{1,0:T(8,128)S(1)} %get-tuple-element.54), channel_id=1, source_target_pairs={{0,2},{1,3},{2,0},{3,1},{4,6},{5,7},{6,4},{7,5},{8,10},{9,11},{10,... | collective-permute-start | bytes 208904 | tf_op jit(solution)/shard_map/ppermute | solution.py:266
  47.9 9.5 %collective-permute-start.11 = (f32[136,128]{1,0:T(8,128)S(1)}, f32[136,128]{1,0:T(8,128)S(1)}, u32[]{:S(2)}, u32[]{:S(2)}) collective-permute-start(f32[136,128]{1,0:T(8,128)S(1)} %get-tuple-element.55), channel_id=1, source_target_pairs={{0,4},{1,5},{2,6},{3,7},{4,0},{5,1},{6,2},{7,3},{8,12},{9,13},{10,... | collective-permute-start | bytes 208904 | tf_op jit(solution)/shard_map/ppermute | solution.py:266
  51.3 6.9 %collective-permute-start.12 = (f32[136,128]{1,0:T(8,128)S(1)}, f32[136,128]{1,0:T(8,128)S(1)}, u32[]{:S(2)}, u32[]{:S(2)}) collective-permute-start(f32[136,128]{1,0:T(8,128)S(1)} %get-tuple-element.56), channel_id=1, source_target_pairs={{0,6},{1,7},{2,4},{3,5},{4,2},{5,3},{6,0},{7,1},{8,14},{9,15},{10,... | collective-permute-start | bytes 208904 | tf_op jit(solution)/shard_map/ppermute | solution.py:266
  52.9 10.8 %collective-permute-start.29 = (f32[136,128]{1,0:T(8,128)S(1)}, f32[136,128]{1,0:T(8,128)S(1)}, u32[]{:S(2)}, u32[]{:S(2)}) collective-permute-start(f32[136,128]{1,0:T(8,128)S(1)} %get-tuple-element.68), channel_id=1, source_target_pairs={{0,2},{1,3},{2,0},{3,1},{4,6},{5,7},{6,4},{7,5},{8,10},{9,11},{10,... | collective-permute-start | bytes 208904 | tf_op jit(solution)/shard_map/ppermute | solution.py:266
  53.5 11.3 %collective-permute-start.30 = (f32[136,128]{1,0:T(8,128)S(1)}, f32[136,128]{1,0:T(8,128)S(1)}, u32[]{:S(2)}, u32[]{:S(2)}) collective-permute-start(f32[136,128]{1,0:T(8,128)S(1)} %get-tuple-element.69), channel_id=1, source_target_pairs={{0,4},{1,5},{2,6},{3,7},{4,0},{5,1},{6,2},{7,3},{8,12},{9,13},{10,... | collective-permute-start | bytes 208904 | tf_op jit(solution)/shard_map/ppermute | solution.py:266
  57.3 7.5 %collective-permute-start.31 = (f32[136,128]{1,0:T(8,128)S(1)}, f32[136,128]{1,0:T(8,128)S(1)}, u32[]{:S(2)}, u32[]{:S(2)}) collective-permute-start(f32[136,128]{1,0:T(8,128)S(1)} %get-tuple-element.70), channel_id=1, source_target_pairs={{0,6},{1,7},{2,4},{3,5},{4,2},{5,3},{6,0},{7,1},{8,14},{9,15},{10,... | collective-permute-start | bytes 208904 | tf_op jit(solution)/shard_map/ppermute | solution.py:266
  59.0 11.2 %collective-permute-start.15 = (f32[136,128]{1,0:T(8,128)S(1)}, f32[136,128]{1,0:T(8,128)S(1)}, u32[]{:S(2)}, u32[]{:S(2)}) collective-permute-start(f32[136,128]{1,0:T(8,128)S(1)} %get-tuple-element.57.refs_0_), channel_id=1, source_target_pairs={{0,6},{1,7},{2,4},{3,5},{4,2},{5,3},{6,0},{7,1},{8,14},{9,15},{10,... | collective-permute-start | bytes 208904 | tf_op jit(solution)/shard_map/ppermute | solution.py:266
  62.0 8.7 %collective-permute-start.14 = (f32[136,128]{1,0:T(8,128)S(1)}, f32[136,128]{1,0:T(8,128)S(1)}, u32[]{:S(2)}, u32[]{:S(2)}) collective-permute-start(f32[136,128]{1,0:T(8,128)S(1)} %get-tuple-element.57.refs_0_), channel_id=1, source_target_pairs={{0,4},{1,5},{2,6},{3,7},{4,0},{5,1},{6,2},{7,3},{8,12},{9,13},{10,... | collective-permute-start | bytes 208904 | tf_op jit(solution)/shard_map/ppermute | solution.py:266
  63.7 7.0 %collective-permute-start.13 = (f32[136,128]{1,0:T(8,128)S(1)}, f32[136,128]{1,0:T(8,128)S(1)}, u32[]{:S(2)}, u32[]{:S(2)}) collective-permute-start(f32[136,128]{1,0:T(8,128)S(1)} %get-tuple-element.57.refs_0_), channel_id=1, source_target_pairs={{0,2},{1,3},{2,0},{3,1},{4,6},{5,7},{6,4},{7,5},{8,10},{9,11},{10,... | collective-permute-start | bytes 208904 | tf_op jit(solution)/shard_map/ppermute | solution.py:266
  65.5 7.8 %collective-permute-start.34 = (f32[136,128]{1,0:T(8,128)S(1)}, f32[136,128]{1,0:T(8,128)S(1)}, u32[]{:S(2)}, u32[]{:S(2)}) collective-permute-start(f32[136,128]{1,0:T(8,128)S(1)} %get-tuple-element.71.refs_0_), channel_id=1, source_target_pairs={{0,6},{1,7},{2,4},{3,5},{4,2},{5,3},{6,0},{7,1},{8,14},{9,15},{10,... | collective-permute-start | bytes 208904 | tf_op jit(solution)/shard_map/ppermute | solution.py:266
  68.0 5.2 %collective-permute-start.33 = (f32[136,128]{1,0:T(8,128)S(1)}, f32[136,128]{1,0:T(8,128)S(1)}, u32[]{:S(2)}, u32[]{:S(2)}) collective-permute-start(f32[136,128]{1,0:T(8,128)S(1)} %get-tuple-element.71.refs_0_), channel_id=1, source_target_pairs={{0,4},{1,5},{2,6},{3,7},{4,0},{5,1},{6,2},{7,3},{8,12},{9,13},{10,... | collective-permute-start | bytes 208904 | tf_op jit(solution)/shard_map/ppermute | solution.py:266
  70.2 4.3 %collective-permute-start.32 = (f32[136,128]{1,0:T(8,128)S(1)}, f32[136,128]{1,0:T(8,128)S(1)}, u32[]{:S(2)}, u32[]{:S(2)}) collective-permute-start(f32[136,128]{1,0:T(8,128)S(1)} %get-tuple-element.71.refs_0_), channel_id=1, source_target_pairs={{0,2},{1,3},{2,0},{3,1},{4,6},{5,7},{6,4},{7,5},{8,10},{9,11},{10,... | collective-permute-start | bytes 208904 | tf_op jit(solution)/shard_map/ppermute | solution.py:266
  71.7 5.4 %collective-permute-start.16 = (f32[264,128]{1,0:T(8,128)S(1)}, f32[264,128]{1,0:T(8,128)S(1)}, u32[]{:S(2)}, u32[]{:S(2)}) collective-permute-start(f32[264,128]{1,0:T(8,128)S(1)} %shard_map.54), channel_id=1, source_target_pairs={{0,8},{1,17},{2,10},{3,19},{4,12},{5,21},{6,14},{7,23},{8,0},{9,25... | collective-permute-start | bytes 405512 | tf_op jit(solution)/shard_map/ppermute | solution.py:273
  75.5 5.1 %collective-permute-start.35 = (f32[264,128]{1,0:T(8,128)S(1)}, f32[264,128]{1,0:T(8,128)S(1)}, u32[]{:S(2)}, u32[]{:S(2)}) collective-permute-start(f32[264,128]{1,0:T(8,128)S(1)} %shard_map.61), channel_id=1, source_target_pairs={{0,8},{1,17},{2,10},{3,19},{4,12},{5,21},{6,14},{7,23},{8,0},{9,25... | collective-permute-start | bytes 405512 | tf_op jit(solution)/shard_map/ppermute | solution.py:273
  77.1 5.1 %collective-permute-start.17 = (f32[264,128]{1,0:T(8,128)S(1)}, f32[264,128]{1,0:T(8,128)S(1)}, u32[]{:S(2)}, u32[]{:S(2)}) collective-permute-start(f32[264,128]{1,0:T(8,128)S(1)} %add.36.a_ref), channel_id=1, source_target_pairs={{0,16},{1,9},{2,18},{3,11},{4,20},{5,13},{6,22},{7,15},{8,24},{9,1... | collective-permute-start | bytes 405512 | tf_op jit(solution)/shard_map/ppermute | solution.py:273
  80.6 5.5 %collective-permute-start.36 = (f32[264,128]{1,0:T(8,128)S(1)}, f32[264,128]{1,0:T(8,128)S(1)}, u32[]{:S(2)}, u32[]{:S(2)}) collective-permute-start(f32[264,128]{1,0:T(8,128)S(1)} %add.38.a_ref), channel_id=1, source_target_pairs={{0,16},{1,9},{2,18},{3,11},{4,20},{5,13},{6,22},{7,15},{8,24},{9,1... | collective-permute-start | bytes 405512 | tf_op jit(solution)/shard_map/ppermute | solution.py:273
  83.7 9.2 %collective-permute-start.18 = (f32[136,128]{1,0:T(8,128)S(1)}, f32[136,128]{1,0:T(8,128)S(1)}, u32[]{:S(2)}, u32[]{:S(2)}) collective-permute-start(f32[136,128]{1,0:T(8,128)S(1)} %get-tuple-element.59), channel_id=1, source_target_pairs={{0,2},{1,3},{2,0},{3,1},{4,6},{5,7},{6,4},{7,5},{8,10},{9,11},{10,... | collective-permute-start | bytes 208904 | tf_op jit(solution)/shard_map/ppermute | solution.py:266
  87.6 10.2 %collective-permute-start.37 = (f32[136,128]{1,0:T(8,128)S(1)}, f32[136,128]{1,0:T(8,128)S(1)}, u32[]{:S(2)}, u32[]{:S(2)}) collective-permute-start(f32[136,128]{1,0:T(8,128)S(1)} %get-tuple-element.73), channel_id=1, source_target_pairs={{0,2},{1,3},{2,0},{3,1},{4,6},{5,7},{6,4},{7,5},{8,10},{9,11},{10,... | collective-permute-start | bytes 208904 | tf_op jit(solution)/shard_map/ppermute | solution.py:266
  88.6 6.1 %collective-permute-start.19 = (f32[136,128]{1,0:T(8,128)S(1)}, f32[136,128]{1,0:T(8,128)S(1)}, u32[]{:S(2)}, u32[]{:S(2)}) collective-permute-start(f32[136,128]{1,0:T(8,128)S(1)} %get-tuple-element.60), channel_id=1, source_target_pairs={{0,4},{1,5},{2,6},{3,7},{4,0},{5,1},{6,2},{7,3},{8,12},{9,13},{10,... | collective-permute-start | bytes 208904 | tf_op jit(solution)/shard_map/ppermute | solution.py:266
  90.9 6.2 %collective-permute-start.20 = (f32[136,128]{1,0:T(8,128)S(1)}, f32[136,128]{1,0:T(8,128)S(1)}, u32[]{:S(2)}, u32[]{:S(2)}) collective-permute-start(f32[136,128]{1,0:T(8,128)S(1)} %get-tuple-element.61), channel_id=1, source_target_pairs={{0,6},{1,7},{2,4},{3,5},{4,2},{5,3},{6,0},{7,1},{8,14},{9,15},{10,... | collective-permute-start | bytes 208904 | tf_op jit(solution)/shard_map/ppermute | solution.py:266
  92.0 7.2 %collective-permute-start.38 = (f32[136,128]{1,0:T(8,128)S(1)}, f32[136,128]{1,0:T(8,128)S(1)}, u32[]{:S(2)}, u32[]{:S(2)}) collective-permute-start(f32[136,128]{1,0:T(8,128)S(1)} %get-tuple-element.74), channel_id=1, source_target_pairs={{0,4},{1,5},{2,6},{3,7},{4,0},{5,1},{6,2},{7,3},{8,12},{9,13},{10,... | collective-permute-start | bytes 208904 | tf_op jit(solution)/shard_map/ppermute | solution.py:266
  92.9 6.3 %collective-permute-start.39 = (f32[136,128]{1,0:T(8,128)S(1)}, f32[136,128]{1,0:T(8,128)S(1)}, u32[]{:S(2)}, u32[]{:S(2)}) collective-permute-start(f32[136,128]{1,0:T(8,128)S(1)} %get-tuple-element.75), channel_id=1, source_target_pairs={{0,6},{1,7},{2,4},{3,5},{4,2},{5,3},{6,0},{7,1},{8,14},{9,15},{10,... | collective-permute-start | bytes 208904 | tf_op jit(solution)/shard_map/ppermute | solution.py:266
  100.0 1.3 %collective-permute-start.40 = (f32[136,128]{1,0:T(8,128)S(1)}, f32[136,128]{1,0:T(8,128)S(1)}, u32[]{:S(2)}, u32[]{:S(2)}) collective-permute-start(f32[136,128]{1,0:T(8,128)S(1)} %get-tuple-element.84), channel_id=1, source_target_pairs={{0,1},{1,0},{2,3},{3,2},{4,5},{5,4},{6,7},{7,6},{8,9},{9,8},{10,11... | collective-permute-start | bytes 208904 | tf_op jit(solution)/shard_map/ppermute | solution.py:266
  100.1 14.5 %collective-permute-start.46 = (f32[128,128]{1,0:T(8,128)S(1)}, f32[128,128]{1,0:T(8,128)S(1)}, u32[]{:S(2)}, u32[]{:S(2)}) collective-permute-start(f32[128,128]{1,0:T(8,128)S(1)} %slice.7), channel_id=1, source_target_pairs={{0,1},{1,0},{2,3},{3,2},{4,5},{5,4},{6,7},{7,6},{8,9},{9,8},{10,11... | collective-permute-start | bytes 196616 | tf_op jit(solution)/shard_map/ppermute | solution.py:266
  100.6 14.0 %collective-permute-start.45 = (f32[128,128]{1,0:T(8,128)S(1)}, f32[128,128]{1,0:T(8,128)S(1)}, u32[]{:S(2)}, u32[]{:S(2)}) collective-permute-start(f32[128,128]{1,0:T(8,128)S(1)} %slice.6), channel_id=1, source_target_pairs={{0,1},{1,0},{2,3},{3,2},{4,5},{5,4},{6,7},{7,6},{8,9},{9,8},{10,11... | collective-permute-start | bytes 196616 | tf_op jit(solution)/shard_map/ppermute | solution.py:266
  101.9 3.7 %collective-permute-start.41 = (f32[8,256]{1,0:T(8,128)S(1)}, f32[8,256]{1,0:T(8,128)S(1)}, u32[]{:S(2)}, u32[]{:S(2)}) collective-permute-start(f32[8,256]{1,0:T(8,128)S(1)} %get-tuple-element.86.known_ref), channel_id=1, source_target_pairs={{0,2},{1,3},{2,0},{3,1},{4,6},{5,7},{6,4},{7,5},{8,10},{9,11},{10,... | collective-permute-start | bytes 24584 | tf_op jit(solution)/shard_map/ppermute | solution.py:266
  105.7 4.5 %collective-permute-start.42 = (f32[8,256]{1,0:T(8,128)S(1)}, f32[8,256]{1,0:T(8,128)S(1)}, u32[]{:S(2)}, u32[]{:S(2)}) collective-permute-start(f32[8,256]{1,0:T(8,128)S(1)} %add.39), channel_id=1, source_target_pairs={{0,4},{1,5},{2,6},{3,7},{4,0},{5,1},{6,2},{7,3},{8,12},{9,13},{10,... | collective-permute-start | bytes 24584 | tf_op jit(solution)/shard_map/ppermute | solution.py:266
  110.2 3.7 %collective-permute-start.43 = (f32[8,256]{1,0:T(8,128)S(1)}, f32[8,256]{1,0:T(8,128)S(1)}, u32[]{:S(2)}, u32[]{:S(2)}) collective-permute-start(f32[8,256]{1,0:T(8,128)S(1)} %add.40), channel_id=1, source_target_pairs={{0,8},{1,17},{2,10},{3,19},{4,12},{5,21},{6,14},{7,23},{8,0},{9,25... | collective-permute-start | bytes 24584 | tf_op jit(solution)/shard_map/ppermute | solution.py:273
  113.9 3.7 %collective-permute-start.44 = (f32[8,256]{1,0:T(8,128)S(1)}, f32[8,256]{1,0:T(8,128)S(1)}, u32[]{:S(2)}, u32[]{:S(2)}) collective-permute-start(f32[8,256]{1,0:T(8,128)S(1)} %add.41.a_ref), channel_id=1, source_target_pairs={{0,16},{1,9},{2,18},{3,11},{4,20},{5,13},{6,22},{7,15},{8,24},{9,1... | collective-permute-start | bytes 24584 | tf_op jit(solution)/shard_map/ppermute | solution.py:273

commit v7 on v5

--- a/solution.py
+++ b/solution.py
@@ -14,7 +14,7 @@
 HALVES = 2
 QUARTER = 64
 COLS = QUARTER // HALVES
-SHARES = (3, 1)
+BLOCKS = 3
 BF16 = jnp.bfloat16
 F32 = jnp.float32
 
@@ -87,24 +87,16 @@
         low_ref[:, cut] = low.astype(BF16)
 
 
-def prepare_kernel(place_ref, sketch_ref, a_ref, mine_ref, first_ref, sem):
-    lead = sketch_ref.shape[0] // 2
-    count = first_ref.shape[0] - lead
-    copy = pltpu.make_async_copy(a_ref.at[pl.ds(0, count)], first_ref.at[pl.ds(lead, count)], sem)
-    copy.start()
+def prepare_kernel(place_ref, sketch_ref, mine_ref, theirs_ref):
     near, far = sketch_ref[:, :LANES], sketch_ref[:, LANES:]
     low = join_lanes(near, far, QUARTER)
     high = join_lanes(turn(near, QUARTER), turn(far, QUARTER), QUARTER)
     zero = place_ref[1] == 0
     mine_ref[...] = jnp.where(zero, low, high)
-    theirs = jnp.where(zero, high, low)
-    first_ref[:lead, :LANES] = theirs[:lead]
-    first_ref[:lead, LANES:] = theirs[lead:]
-    copy.wait()
-
-
-def near_kernel(place_ref, own_ref, core_ref, mine_ref, got_ref, y_ref, high_ref, low_ref, rest_ref):
-    rest_ref[...] = own_ref[own_ref.shape[0] - rest_ref.shape[0] :, :]
+    theirs_ref[...] = jnp.where(zero, high, low)
+
+
+def near_kernel(place_ref, own_ref, core_ref, mine_ref, got_ref, y_ref, high_ref, low_ref):
     store_factors(high_ref, low_ref, (own_ref[...], core_ref[...]))
     rhs = jnp.concatenate([sketch_side(place_ref, ref[...]) for ref in (mine_ref, got_ref)], axis=0)
     for b in range(own_ref.shape[0] // LANES):
@@ -113,51 +105,41 @@
         y_ref[b * QUARTER : (b + 1) * QUARTER, :] = unfold(total.T)
 
 
-def far_kernel(start, skip, place_ref, side_ref, diagonal_ref, *refs):
-    sketches, (near_ref, y_ref, high_ref, low_ref) = refs[:-4], refs[-4:]
-    if not sketches:
-        sketches = (side_ref, diagonal_ref)
-    store_factors(high_ref, low_ref, (side_ref[skip:, :], diagonal_ref[skip:, :]))
-    rhs = []
-    for ref in sketches:
-        for s in range(2):
-            rhs.append(sketch_side(place_ref, ref[:LANES, s * LANES : (s + 1) * LANES]))
-    rhs = jnp.concatenate(rhs, axis=0)
+def split_kernel(side_ref, high_ref, low_ref):
+    store_factors(high_ref, low_ref, (side_ref[...],))
+
+
+def far_kernel(place_ref, high_side_ref, low_side_ref, diagonal_ref, sketch_ref, core_sketch_ref, near_ref, *refs):
+    *halves, high_ref, low_ref = refs
+    store_factors(high_ref, low_ref, (diagonal_ref[...],))
+    side = sketch_side(place_ref, sketch_ref[...])
+    diagonal = sketch_side(place_ref, core_sketch_ref[...])
     for b in range(high_ref.shape[0] // LANES):
         cut = slice(b * LANES, (b + 1) * LANES)
-        total = dot(high_ref[cut, :], rhs) + dot(low_ref[cut, :], rhs)
-        at = (start // LANES + b) * QUARTER
-        y_ref[b * QUARTER : (b + 1) * QUARTER, :] = unfold(total.T) + near_ref[at : at + QUARTER, :]
+        total = dot(high_side_ref[cut, :], side) + dot(low_side_ref[cut, :], side)
+        total += dot(high_ref[cut, :], diagonal) + dot(low_ref[cut, :], diagonal)
+        y = unfold(total.T) + near_ref[b * QUARTER : (b + 1) * QUARTER, :]
+        for h, ref in enumerate(halves):
+            ref[b * COLS : (b + 1) * COLS, :] = y[h * COLS : (h + 1) * COLS]
 
 
 def send_z(y, high_refs, low_refs, z_ref):
     lhs = jnp.concatenate(split(y), axis=0).astype(BF16)
-    near = dot(lhs, high_refs[0][...]) + dot(lhs, low_refs[0][...])
-    far, at = None, 0
-    for high_ref, low_ref in zip(high_refs[1:], low_refs[1:]):
-        cut = slice(at, at + high_ref.shape[0])
-        term = dot(lhs[:, cut], high_ref[...]) + dot(lhs[:, cut], low_ref[...])
-        far = term if far is None else far + term
-        at += high_ref.shape[0]
-    store_blocks(z_ref, 0, unfold(near))
-    store_blocks(z_ref, (z_ref.shape[0] - TILE) // 2, unfold(far))
+    at = 0
+    for high_ref, low_ref in zip(high_refs, low_refs):
+        z = unfold(dot(lhs, high_ref[...]) + dot(lhs, low_ref[...]))
+        store_blocks(z_ref, at, z)
+        at += z.size // LANES
     z_ref[-TILE:, :] = squares_tile(y)
 
 
 def factors(refs):
-    count = len(SHARES) + 1
-    return refs[:count], refs[count : 2 * count]
-
-
-def first_z_kernel(h, *refs):
-    count = len(SHARES)
-    high, low = factors(refs[2 * count :])
-    pieces = []
-    for a_ref, b_ref in zip(refs[:count], refs[count : 2 * count]):
-        for j in range(a_ref.shape[0] // QUARTER):
-            cut = slice(j * QUARTER + h * COLS, j * QUARTER + (h + 1) * COLS)
-            pieces.append(a_ref[cut, :] + b_ref[cut, :])
-    send_z(jnp.concatenate(pieces, axis=1), high, low, refs[-1])
+    return refs[:BLOCKS], refs[BLOCKS : 2 * BLOCKS]
+
+
+def first_z_kernel(a_ref, b_ref, *refs):
+    high, low = factors(refs)
+    send_z(wide(a_ref[...] + b_ref[...], COLS), high, low, refs[-1])
 
 
 def scaled(own_ref, got_ref, count):
@@ -183,16 +165,15 @@
         store_blocks(z_ref, 0, z)
     y_ref[-TILE:, :] = squares_tile(z)
     rhs = jnp.concatenate(split(z), axis=0).T.astype(BF16)
-    middle = rhs.shape[0] // 2
-    at = 0
-    for high_ref, low_ref in zip(high_refs[1:], low_refs[1:]):
-        for b in range(high_ref.shape[0] // LANES):
-            near = slice(at * LANES, (at + 1) * LANES)
-            far = slice(b * LANES, (b + 1) * LANES)
-            total = dot(high_refs[0][near, :], rhs[:middle]) + dot(low_refs[0][near, :], rhs[:middle])
-            total += dot(high_ref[far, :], rhs[middle:]) + dot(low_ref[far, :], rhs[middle:])
-            y_ref[at * COLS : (at + 1) * COLS, :] = unfold(total.T)
-            at += 1
+    for b in range(high_refs[0].shape[0] // LANES):
+        cut = slice(b * LANES, (b + 1) * LANES)
+        total, at = None, 0
+        for high_ref, low_ref in zip(high_refs, low_refs):
+            part = rhs[at : at + high_ref.shape[1]]
+            term = dot(high_ref[cut, :], part) + dot(low_ref[cut, :], part)
+            total = term if total is None else total + term
+            at += high_ref.shape[1]
+        y_ref[b * COLS : (b + 1) * COLS, :] = unfold(total.T)
 
 
 def end_kernel(count, carried, place_ref, own_ref, got_ref, *refs):
@@ -277,17 +258,15 @@
     scale_ref[last:, :] = scale
 
 
-def call(kernel, outs, *args, scalars=1, plain=False, in_place=(), scratch=()):
+def call(kernel, outs, *args, scalars=1, plain=False):
     specs = [pl.BlockSpec(memory_space=pltpu.SMEM)] * scalars
-    for i in range(scalars, len(args)):
-        specs.append(pl.BlockSpec(memory_space=pltpu.HBM if i in in_place else pltpu.VMEM))
+    specs += [pl.BlockSpec(memory_space=pltpu.VMEM)] * (len(args) - scalars)
     out_spec = pl.BlockSpec() if plain else pl.BlockSpec(memory_space=pltpu.VMEM)
     return pl.pallas_call(
         kernel,
         out_shape=[jax.ShapeDtypeStruct(shape, dtype) for shape, dtype in outs],
         in_specs=specs,
         out_specs=[out_spec] * len(outs),
-        scratch_shapes=scratch,
         compiler_params=pltpu.CompilerParams(vmem_limit_bytes=16 * 1024 * 1024),
     )(*args)
 
@@ -345,39 +324,25 @@
         x = x + swap_cell(x, 0)
         return x, swap_cell(x, 1)
 
-    sizes = [n * rows // sum(SHARES) for n in SHARES]
-    lead = width // 2
-
     def factor(count):
-        return [((count, 2 * width), BF16)] * 2
-
-    mine, first = call(
-        prepare_kernel, [((width, LANES), F32), ((lead + sizes[0], width), F32)],
-        place, sketch, snapshots, in_place=(2,), scratch=[pltpu.SemaphoreType.DMA],
-    )
-    side_first = swap_side(first)
-    near_y, near_high, near_low, rest = call(
-        near_kernel,
-        [((rows // LANES * QUARTER, LANES), F32)] + factor(rows) + [((sizes[1], width), F32)],
+        return [((rows, count * width), BF16)] * 2
+
+    side_block = swap_side(snapshots)
+    packed = ((width, LANES), F32)
+    mine, theirs = call(prepare_kernel, [packed, packed], place, sketch)
+    near_y, *near = call(
+        near_kernel, [((rows // LANES * QUARTER, LANES), F32)] + factor(2),
         place, snapshots, swap_core(snapshots), mine, swap_core(mine),
     )
-    side_rest = swap_side(rest)
-    side_first, near_y = lax.optimization_barrier((side_first, near_y))
-    core_first = swap_core(side_first)
-    own_first, high_first, low_first = call(
-        functools.partial(far_kernel, 0, lead),
-        [((sizes[0] // LANES * QUARTER, LANES), F32)] + factor(sizes[0]),
-        place, side_first, core_first, near_y,
+    side_sketch = swap_side(theirs)
+    side_block, near_y = lax.optimization_barrier((side_block, near_y))
+    side = call(split_kernel, factor(1), side_block, scalars=0)
+    half_shape = ((rows // LANES * COLS, LANES), F32)
+    *own, high, low = call(
+        far_kernel, [half_shape] * HALVES + factor(1),
+        place, *side, swap_core(side_block), side_sketch, swap_core(side_sketch), near_y,
     )
-    side_rest, own_first = lax.optimization_barrier((side_rest, own_first))
-    own_rest, high_rest, low_rest = call(
-        functools.partial(far_kernel, sizes[0], 0),
-        [((sizes[1] // LANES * QUARTER, LANES), F32)] + factor(sizes[1]),
-        place, side_rest, swap_core(side_rest), side_first, core_first, near_y,
-    )
-    matrix = (near_high, high_first, high_rest, near_low, low_first, low_rest)
-    own = (own_first, own_rest)
-    got = tuple(swap_pair(y) for y in own)
+    matrix = (near[0], side[0], high, near[1], side[1], low)
 
     flat = (COLS * rows // LANES + TILE, LANES)
     sent_shape = ((COLS * 4 * width // LANES + TILE, LANES), F32)
@@ -385,10 +350,7 @@
     scale_shape = ((TILE, LANES), F32)
     z_shape = ((COLS * 4 * width // LANES, LANES), F32)
     scales = [[] for _ in range(HALVES)]
-    sent = [
-        call(functools.partial(first_z_kernel, h), [sent_shape], *own, *got, *matrix, scalars=0)[0]
-        for h in range(HALVES)
-    ]
+    sent = [call(first_z_kernel, [sent_shape], y, swap_pair(y), *matrix, scalars=0)[0] for y in own]
     ys, zs = [None] * HALVES, [None] * HALVES
     for section in range(ITERS):
         last = section == ITERS - 1

time: 118 us -> 115 us (0.975)
  starting transfers between devices: 29.2 us -> 25.7 us
  waiting for transfers between devices: 64.8 us -> 66.4 us
    ppermute x10, waiting for transfers between devices: 13 us -> 15.9 us  [swap_cell(): return lax.ppermute(x, ('cell', 'snap'), perm)]
    ppermute x15, starting transfers between devices: 15 us -> 13 us  [swap(): return lax.ppermute(x, 'snap', [(i, i ^ bits) for i in range(places)])]
    ppermute x10, starting transfers between devices: 14.1 us -> 12.7 us  [swap_cell(): return lax.ppermute(x, ('cell', 'snap'), perm)]
    ppermute x15, waiting for transfers between devices: 51.7 us -> 50.4 us  [swap(): return lax.ppermute(x, 'snap', [(i, i ^ bits) for i in range(places)])]
  transfers between devices with their start and end apart: 25 -> 25, of which waited for: 22 -> 20; matrix products, arithmetic and copies ran while one was open for 0% -> 0% of each run, Pallas kernels for 15% -> 14%
where the time goes in v7:
time: 115 us; the launch traced here: 114 us
  waiting for transfers between devices  66.4 us (58%)
  starting transfers between devices  25.7 us (22%)
  Pallas kernels  19.3 us (17%)
  local copies, waits for them, and re-layouts  2.18 us (2%)
    ppermute x15, waiting for transfers between devices, swap(): return lax.ppermute(x, 'snap', [(i, i ^ bits) for i in range(places)])  50.4 us
    pallas_call x18, Pallas kernels, call(): pl.pallas_call(kernel, out_shape=[jax.ShapeDtypeStruct(shape, dtype) for...  19.3 us
    ppermute x10, waiting for transfers between devices, swap_cell(): return lax.ppermute(x, ('cell', 'snap'), perm)  15.9 us
    ppermute x15, starting transfers between devices, swap(): return lax.ppermute(x, 'snap', [(i, i ^ bits) for i in range(places)])  13 us
    ppermute x10, starting transfers between devices, swap_cell(): return lax.ppermute(x, ('cell', 'snap'), perm)  12.7 us
  transfers between devices with their start and end apart: 25, of which 20 were waited for; matrix products, arithmetic and copies ran while one was open for 0% of the time, Pallas kernels for 14%

profile of v7, /device:TPU:0, one launch (start us, length us, event | category | flops | bytes accessed | tf_op | source)
XLA Modules:
  0.0 114.4 jit_solution(7954400424529946013)
XLA Ops:
  0.6 0.5 collective-permute-start.1
  1.1 2.7 %collective-permute-start = (f32[1024,256]{1,0:T(8,128)}, f32[1024,256]{1,0:T(8,128)S(1)}, u32[]{:S(2)}, u32[]{:S(2)}) collective-permute-start(f32[1024,256]{1,0:T(8,128)} %own_ref.1), channel_id=1, source_target_pairs={{0,2},{1,3},{2,0},{3,1},{4,6},{5,7},{6,4},{7,5},{8,10},{9,11},{10,... | collective-permute-start | bytes 3145736 | tf_op jit(solution)/shard_map/ppermute | solution.py:310
  3.8 0.1 pad_add_fusion.place_ref
  3.9 0.9 copy-done.1
  4.8 0.7 shard_map.49
  5.5 0.2 collective-permute-start.2
  5.8 1.2 %collective-permute-done.2.got_ref = f32[256,128]{1,0:T(8,128)S(1)} collective-permute-done((f32[256,128]{1,0:T(8,128)S(1)}, f32[256,128]{1,0:T(8,128)S(1)}, u32[]{:S(2)}, u32[]{:S(2)}) %collective-permute-start.2) | collective-permute-done | bytes 131104 | tf_op jit(solution)/shard_map/ppermute | solution.py:310
  7.0 0.0 collective-permute-done.1.core_ref
  7.0 1.2 %copy-done = f32[1024,256]{1,0:T(8,128)S(1)} copy-done((f32[1024,256]{1,0:T(8,128)S(1)}, f32[1024,256]{1,0:T(8,128)}, u32[]{:S(2)}) %copy-start) | copy-done | bytes 1048600
  8.2 1.6 %shard_map.50 = (f32[512,128]{1,0:T(8,128)S(1)}, bf16[1024,512]{1,0:T(8,128)(2,1)S(1)}, bf16[1024,512]{1,0:T(8,128)(2,1)S(1)}) custom-call(s32[4]{0:T(128)S(1)} %pad_add_fusion.place_ref, f32[1024,256]{1,0:T(8,128)S(1)} %copy-done, f32[1024,256]{1,0:T(8,128)S(1)} %collective-permute-done.1.core_ref, f32[256,128]{1,0:T(8,128)S(1)} %get-tuple-element.40.mine_ref, ...), custom_call_target="tpu_custom_call" | custom-call | tf_op jit(solution)/shard_map/pallas_call | solution.py:265
  9.8 18.0 %collective-permute-done.side_ref = f32[1024,256]{1,0:T(8,128)S(1)} collective-permute-done((f32[1024,256]{1,0:T(8,128)}, f32[1024,256]{1,0:T(8,128)S(1)}, u32[]{:S(2)}, u32[]{:S(2)}) %collective-permute-start) | collective-permute-done | bytes 1048608 | tf_op jit(solution)/shard_map/ppermute | solution.py:310
  27.8 1.8 %collective-permute-start.4 = (f32[256,128]{1,0:T(8,128)S(1)}, f32[256,128]{1,0:T(8,128)S(1)}, u32[]{:S(2)}, u32[]{:S(2)}) collective-permute-start(f32[256,128]{1,0:T(8,128)S(1)} %get-tuple-element.45), channel_id=1, source_target_pairs={{0,2},{1,3},{2,0},{3,1},{4,6},{5,7},{6,4},{7,5},{8,10},{9,11},{10,... | collective-permute-start | bytes 393224 | tf_op jit(solution)/shard_map/ppermute | solution.py:310
  29.5 4.2 %collective-permute-done.4.sketch_ref = f32[256,128]{1,0:T(8,128)S(1)} collective-permute-done((f32[256,128]{1,0:T(8,128)S(1)}, f32[256,128]{1,0:T(8,128)S(1)}, u32[]{:S(2)}, u32[]{:S(2)}) %collective-permute-start.4) | collective-permute-done | bytes 131104 | tf_op jit(solution)/shard_map/ppermute | solution.py:310
  33.7 0.1 shard_map.51
  33.8 1.2 %collective-permute-done.5.core_sketch_ref = f32[256,128]{1,0:T(8,128)S(1)} collective-permute-done((f32[256,128]{1,0:T(8,128)S(1)}, f32[256,128]{1,0:T(8,128)S(1)}, u32[]{:S(2)}, u32[]{:S(2)}) %collective-permute-start.5) | collective-permute-done | bytes 131104 | tf_op jit(solution)/shard_map/ppermute | solution.py:310
  35.0 1.5 %shard_map.52 = (f32[256,128]{1,0:T(8,128)S(1)}, f32[256,128]{1,0:T(8,128)S(1)}, bf16[1024,256]{1,0:T(8,128)(2,1)S(1)}, bf16[1024,256]{1,0:T(8,128)(2,1)S(1)}) custom-call(s32[4]{0:T(128)S(1)} %pad_add_fusion.place_ref, bf16[1024,256]{1,0:T(8,128)(2,1)S(1)} %get-tuple-element.43.high_side_ref.refs_1_.refs_3_, ...), custom_call_target="tpu_custom_call" | custom-call | tf_op jit(solution)/shard_map/pallas_call | solution.py:265
  36.6 2.8 %collective-permute-start.6 = (f32[256,128]{1,0:T(8,128)S(1)}, f32[256,128]{1,0:T(8,128)S(1)}, u32[]{:S(2)}, u32[]{:S(2)}) collective-permute-start(f32[256,128]{1,0:T(8,128)S(1)} %get-tuple-element.47.a_ref), channel_id=1, source_target_pairs={{0,4},{1,5},{2,6},{3,7},{4,0},{5,1},{6,2},{7,3},{8,12},{9,13},{10,... | collective-permute-start | bytes 393224 | tf_op jit(solution)/shard_map/ppermute | solution.py:310
  39.4 0.2 collective-permute-start.13
  39.6 9.9 %collective-permute-done.6.b_ref = f32[256,128]{1,0:T(8,128)S(1)} collective-permute-done((f32[256,128]{1,0:T(8,128)S(1)}, f32[256,128]{1,0:T(8,128)S(1)}, u32[]{:S(2)}, u32[]{:S(2)}) %collective-permute-start.6) | collective-permute-done | bytes 131104 | tf_op jit(solution)/shard_map/ppermute | solution.py:310
  49.5 0.8 shard_map.53
  50.3 1.7 %collective-permute-start.7 = (f32[264,128]{1,0:T(8,128)S(1)}, f32[264,128]{1,0:T(8,128)S(1)}, u32[]{:S(2)}, u32[]{:S(2)}) collective-permute-start(f32[264,128]{1,0:T(8,128)S(1)} %shard_map.53), channel_id=1, source_target_pairs={{0,8},{1,17},{2,10},{3,19},{4,12},{5,21},{6,14},{7,23},{8,0},{9,25... | collective-permute-start | bytes 405512 | tf_op jit(solution)/shard_map/ppermute | solution.py:321
  52.0 0.8 shard_map.57
  52.8 1.2 %collective-permute-start.14 = (f32[264,128]{1,0:T(8,128)S(1)}, f32[264,128]{1,0:T(8,128)S(1)}, u32[]{:S(2)}, u32[]{:S(2)}) collective-permute-start(f32[264,128]{1,0:T(8,128)S(1)} %shard_map.57), channel_id=1, source_target_pairs={{0,8},{1,17},{2,10},{3,19},{4,12},{5,21},{6,14},{7,23},{8,0},{9,25... | collective-permute-start | bytes 405512 | tf_op jit(solution)/shard_map/ppermute | solution.py:321
  54.0 1.3 %collective-permute-done.7 = f32[264,128]{1,0:T(8,128)S(1)} collective-permute-done((f32[264,128]{1,0:T(8,128)S(1)}, f32[264,128]{1,0:T(8,128)S(1)}, u32[]{:S(2)}, u32[]{:S(2)}) %collective-permute-start.7) | collective-permute-done | bytes 135200 | tf_op jit(solution)/shard_map/ppermute | solution.py:321
  55.3 1.8 %collective-permute-start.8 = (f32[264,128]{1,0:T(8,128)S(1)}, f32[264,128]{1,0:T(8,128)S(1)}, u32[]{:S(2)}, u32[]{:S(2)}) collective-permute-start(f32[264,128]{1,0:T(8,128)S(1)} %add.25.refs_0_), channel_id=1, source_target_pairs={{0,16},{1,9},{2,18},{3,11},{4,20},{5,13},{6,22},{7,15},{8,24},{9,1... | collective-permute-start | bytes 405512 | tf_op jit(solution)/shard_map/ppermute | solution.py:321
  57.1 1.7 %collective-permute-done.14 = f32[264,128]{1,0:T(8,128)S(1)} collective-permute-done((f32[264,128]{1,0:T(8,128)S(1)}, f32[264,128]{1,0:T(8,128)S(1)}, u32[]{:S(2)}, u32[]{:S(2)}) %collective-permute-start.14) | collective-permute-done | bytes 135200 | tf_op jit(solution)/shard_map/ppermute | solution.py:321
  58.8 1.3 %collective-permute-start.15 = (f32[264,128]{1,0:T(8,128)S(1)}, f32[264,128]{1,0:T(8,128)S(1)}, u32[]{:S(2)}, u32[]{:S(2)}) collective-permute-start(f32[264,128]{1,0:T(8,128)S(1)} %add.27.refs_0_), channel_id=1, source_target_pairs={{0,16},{1,9},{2,18},{3,11},{4,20},{5,13},{6,22},{7,15},{8,24},{9,1... | collective-permute-start | bytes 405512 | tf_op jit(solution)/shard_map/ppermute | solution.py:321
  60.1 0.3 collective-permute-done.8.refs_1_
  60.4 1.5 %shard_map.54 = (f32[264,128]{1,0:T(8,128)S(1)}, f32[8,128]{1,0:T(8,128)S(1)}) custom-call(f32[264,128]{1,0:T(8,128)S(1)} %add.25.refs_0_, f32[264,128]{1,0:T(8,128)S(1)} %collective-permute-done.8.refs_1_, bf16[1024,512]{1,0:T(8,128)(2,1)S(1)} %get-tuple-element.48.refs_0_.refs_2_, bf16[1024,256]{1,0:T(8,128)(2,1)S(1)} %get-tuple-element.43.high_side_ref.refs_1_.refs_3_, ...), custom_call_target="tpu_custom_call" | custom-call | tf_op jit(solution)/shard_map/pallas_call | solution.py:265
  61.9 0.1 collective-permute-start.9
  62.0 1.9 %collective-permute-done.15.refs_1_ = f32[264,128]{1,0:T(8,128)S(1)} collective-permute-done((f32[264,128]{1,0:T(8,128)S(1)}, f32[264,128]{1,0:T(8,128)S(1)}, u32[]{:S(2)}, u32[]{:S(2)}) %collective-permute-start.15) | collective-permute-done | bytes 135200 | tf_op jit(solution)/shard_map/ppermute | solution.py:321
  63.9 1.5 %shard_map.58 = (f32[264,128]{1,0:T(8,128)S(1)}, f32[8,128]{1,0:T(8,128)S(1)}) custom-call(f32[264,128]{1,0:T(8,128)S(1)} %add.27.refs_0_, f32[264,128]{1,0:T(8,128)S(1)} %collective-permute-done.15.refs_1_, bf16[1024,512]{1,0:T(8,128)(2,1)S(1)} %get-tuple-element.48.refs_0_.refs_2_, bf16[1024,256]{1,0:T(8,128)(2,1)S(1)} %get-tuple-element.43.high_side_ref.refs_1_.refs_3_, ...), custom_call_target="tpu_custom_call" | custom-call | tf_op jit(solution)/shard_map/pallas_call | solution.py:265
  65.4 1.1 collective-permute-start.16
  66.4 7.2 %collective-permute-done.9.refs_1_ = f32[264,128]{1,0:T(8,128)S(1)} collective-permute-done((f32[264,128]{1,0:T(8,128)S(1)}, f32[264,128]{1,0:T(8,128)S(1)}, u32[]{:S(2)}, u32[]{:S(2)}) %collective-permute-start.9) | collective-permute-done | bytes 135200 | tf_op jit(solution)/shard_map/ppermute | solution.py:310
  73.7 0.9 shard_map.55
  74.6 1.5 %collective-permute-start.10 = (f32[264,128]{1,0:T(8,128)S(1)}, f32[264,128]{1,0:T(8,128)S(1)}, u32[]{:S(2)}, u32[]{:S(2)}) collective-permute-start(f32[264,128]{1,0:T(8,128)S(1)} %get-tuple-element.53), channel_id=1, source_target_pairs={{0,8},{1,17},{2,10},{3,19},{4,12},{5,21},{6,14},{7,23},{8,0},{9,25... | collective-permute-start | bytes 405512 | tf_op jit(solution)/shard_map/ppermute | solution.py:321
  76.1 0.9 shard_map.59
  77.0 0.5 collective-permute-start.17
  77.5 3.2 %collective-permute-done.10 = f32[264,128]{1,0:T(8,128)S(1)} collective-permute-done((f32[264,128]{1,0:T(8,128)S(1)}, f32[264,128]{1,0:T(8,128)S(1)}, u32[]{:S(2)}, u32[]{:S(2)}) %collective-permute-start.10) | collective-permute-done | bytes 135200 | tf_op jit(solution)/shard_map/ppermute | solution.py:321
  80.8 1.2 %collective-permute-start.11 = (f32[264,128]{1,0:T(8,128)S(1)}, f32[264,128]{1,0:T(8,128)S(1)}, u32[]{:S(2)}, u32[]{:S(2)}) collective-permute-start(f32[264,128]{1,0:T(8,128)S(1)} %add.26.refs_0_), channel_id=1, source_target_pairs={{0,16},{1,9},{2,18},{3,11},{4,20},{5,13},{6,22},{7,15},{8,24},{9,1... | collective-permute-start | bytes 405512 | tf_op jit(solution)/shard_map/ppermute | solution.py:321
  82.0 1.5 %collective-permute-done.17 = f32[264,128]{1,0:T(8,128)S(1)} collective-permute-done((f32[264,128]{1,0:T(8,128)S(1)}, f32[264,128]{1,0:T(8,128)S(1)}, u32[]{:S(2)}, u32[]{:S(2)}) %collective-permute-start.17) | collective-permute-done | bytes 135200 | tf_op jit(solution)/shard_map/ppermute | solution.py:321
  83.5 0.7 collective-permute-start.18
  84.2 1.7 %collective-permute-done.11.refs_1_ = f32[264,128]{1,0:T(8,128)S(1)} collective-permute-done((f32[264,128]{1,0:T(8,128)S(1)}, f32[264,128]{1,0:T(8,128)S(1)}, u32[]{:S(2)}, u32[]{:S(2)}) %collective-permute-start.11) | collective-permute-done | bytes 135200 | tf_op jit(solution)/shard_map/ppermute | solution.py:321
  85.9 1.5 %shard_map.56 = (f32[264,128]{1,0:T(8,128)S(1)}, f32[8,128]{1,0:T(8,128)S(1)}, f32[256,128]{1,0:T(8,128)S(1)}) custom-call(f32[264,128]{1,0:T(8,128)S(1)} %add.26.refs_0_, f32[264,128]{1,0:T(8,128)S(1)} %collective-permute-done.11.refs_1_, bf16[1024,512]{1,0:T(8,128)(2,1)S(1)} %get-tuple-element.48.refs_0_.refs_2_, ...), custom_call_target="tpu_custom_call" | custom-call | tf_op jit(solution)/shard_map/pallas_call | solution.py:265
  87.3 0.1 collective-permute-start.12
  87.4 1.2 %collective-permute-done.18.refs_1_ = f32[264,128]{1,0:T(8,128)S(1)} collective-permute-done((f32[264,128]{1,0:T(8,128)S(1)}, f32[264,128]{1,0:T(8,128)S(1)}, u32[]{:S(2)}, u32[]{:S(2)}) %collective-permute-start.18) | collective-permute-done | bytes 135200 | tf_op jit(solution)/shard_map/ppermute | solution.py:321
  88.6 1.5 %shard_map.60 = (f32[264,128]{1,0:T(8,128)S(1)}, f32[8,128]{1,0:T(8,128)S(1)}, f32[256,128]{1,0:T(8,128)S(1)}) custom-call(f32[264,128]{1,0:T(8,128)S(1)} %add.28.refs_0_, f32[264,128]{1,0:T(8,128)S(1)} %collective-permute-done.18.refs_1_, bf16[1024,512]{1,0:T(8,128)(2,1)S(1)} %get-tuple-element.48.refs_0_.refs_2_, ...), custom_call_target="tpu_custom_call" | custom-call | tf_op jit(solution)/shard_map/pallas_call | solution.py:265
  90.1 1.8 %collective-permute-start.19 = (f32[264,128]{1,0:T(8,128)S(1)}, f32[264,128]{1,0:T(8,128)S(1)}, u32[]{:S(2)}, u32[]{:S(2)}) collective-permute-start(f32[264,128]{1,0:T(8,128)S(1)} %get-tuple-element.64.own_ref), channel_id=1, source_target_pairs={{0,4},{1,5},{2,6},{3,7},{4,0},{5,1},{6,2},{7,3},{8,12},{9,13},{10,... | collective-permute-start | bytes 405512 | tf_op jit(solution)/shard_map/ppermute | solution.py:310
  91.9 4.6 %collective-permute-done.12.got_ref = f32[264,128]{1,0:T(8,128)S(1)} collective-permute-done((f32[264,128]{1,0:T(8,128)S(1)}, f32[264,128]{1,0:T(8,128)S(1)}, u32[]{:S(2)}, u32[]{:S(2)}) %collective-permute-start.12) | collective-permute-done | bytes 135200 | tf_op jit(solution)/shard_map/ppermute | solution.py:310
  96.5 1.3 %shard_map.61 = (f32[72,128]{1,0:T(8,128)S(1)}, f32[328,128]{1,0:T(8,128)S(1)}, f32[256,128]{1,0:T(8,128)}) custom-call(s32[4]{0:T(128)S(1)} %pad_add_fusion.place_ref, f32[264,128]{1,0:T(8,128)S(1)} %get-tuple-element.54.own_ref, f32[264,128]{1,0:T(8,128)S(1)} %collective-permute-done.12.got_ref, f32[256,128]{1,0:T(8,128)S(1)} %get-tuple-element.55.refs_0_.refs_4_, ...), custom_call_target="tpu_custom_call" | custom-call | tf_op jit(solution)/shard_map/pallas_call | solution.py:265
  97.8 0.3 collective-permute-done.19.got_ref
  98.1 1.3 %shard_map.62 = (f32[72,128]{1,0:T(8,128)S(1)}, f32[72,128]{1,0:T(8,128)S(1)}, f32[256,128]{1,0:T(8,128)}) custom-call(s32[4]{0:T(128)S(1)} %pad_add_fusion.place_ref, f32[264,128]{1,0:T(8,128)S(1)} %get-tuple-element.64.own_ref, f32[264,128]{1,0:T(8,128)S(1)} %collective-permute-done.19.got_ref, f32[8,128]{1,0:T(8,128)S(1)} %get-tuple-element.65.refs_0_, ...), custom_call_target="tpu_custom_call" | custom-call | tf_op jit(solution)/shard_map/pallas_call | solution.py:265
  99.4 1.7 %collective-permute-start.21 = (f32[72,128]{1,0:T(8,128)S(1)}, f32[72,128]{1,0:T(8,128)S(1)}, u32[]{:S(2)}, u32[]{:S(2)}) collective-permute-start(f32[72,128]{1,0:T(8,128)S(1)} %get-tuple-element.70), channel_id=1, source_target_pairs={{0,2},{1,3},{2,0},{3,1},{4,6},{5,7},{6,4},{7,5},{8,10},{9,11},{10,... | collective-permute-start | bytes 110600 | tf_op jit(solution)/shard_map/ppermute | solution.py:310
  101.2 2.4 %collective-permute-done.21.refs_3_ = f32[72,128]{1,0:T(8,128)S(1)} collective-permute-done((f32[72,128]{1,0:T(8,128)S(1)}, f32[72,128]{1,0:T(8,128)S(1)}, u32[]{:S(2)}, u32[]{:S(2)}) %collective-permute-start.21) | collective-permute-done | bytes 36896 | tf_op jit(solution)/shard_map/ppermute | solution.py:310
  103.6 0.6 shard_map.63
  104.2 0.0 collective-permute-start.22
  104.3 1.4 %collective-permute-done.22.got_ref.refs_3_ = f32[392,128]{1,0:T(8,128)S(1)} collective-permute-done((f32[392,128]{1,0:T(8,128)S(1)}, f32[392,128]{1,0:T(8,128)S(1)}, u32[]{:S(2)}, u32[]{:S(2)}) %collective-permute-start.22) | collective-permute-done | bytes 200736 | tf_op jit(solution)/shard_map/ppermute | solution.py:310
  105.7 0.6 shard_map.64
  106.3 1.5 %collective-permute-start.23 = (f32[8,256]{1,0:T(8,128)S(1)}, f32[8,256]{1,0:T(8,128)S(1)}, u32[]{:S(2)}, u32[]{:S(2)}) collective-permute-start(f32[8,256]{1,0:T(8,128)S(1)} %get-tuple-element.74.known_ref.refs_4_), channel_id=1, source_target_pairs={{0,8},{1,17},{2,10},{3,19},{4,12},{5,21},{6,14},{7,23},{8,0},{9,25... | collective-permute-start | bytes 24584 | tf_op jit(solution)/shard_map/ppermute | solution.py:321
  107.8 2.3 %collective-permute-done.23 = f32[8,256]{1,0:T(8,128)S(1)} collective-permute-done((f32[8,256]{1,0:T(8,128)S(1)}, f32[8,256]{1,0:T(8,128)S(1)}, u32[]{:S(2)}, u32[]{:S(2)}) %collective-permute-start.23) | collective-permute-done | bytes 8224 | tf_op jit(solution)/shard_map/ppermute | solution.py:321
  110.1 1.3 %collective-permute-start.24 = (f32[8,256]{1,0:T(8,128)S(1)}, f32[8,256]{1,0:T(8,128)S(1)}, u32[]{:S(2)}, u32[]{:S(2)}) collective-permute-start(f32[8,256]{1,0:T(8,128)S(1)} %add.29.a_ref), channel_id=1, source_target_pairs={{0,16},{1,9},{2,18},{3,11},{4,20},{5,13},{6,22},{7,15},{8,24},{9,1... | collective-permute-start | bytes 24584 | tf_op jit(solution)/shard_map/ppermute | solution.py:321
  111.4 1.4 %shard_map.66 = f32[256,256]{1,0:T(8,128)} custom-call(s32[4]{0:T(128)S(1)} %pad_add_fusion.place_ref, f32[256,128]{1,0:T(8,128)S(1)} %get-tuple-element.55.refs_0_.refs_4_, f32[256,128]{1,0:T(8,128)S(1)} %get-tuple-element.59.refs_1_.refs_5_, f32[328,128]{1,0:T(8,128)S(1)} %collective-permute-done.20.refs_2_, ...), custom_call_target="tpu_custom_call" | custom-call | tf_op jit(solution)/shard_map/pallas_call | solution.py:265
  112.8 0.9 collective-permute-done.24.b_ref
  113.7 0.7 shard_map.65
  (14 shorter events, 0.1 us)
Async XLA Ops:
  0.6 6.3 %collective-permute-start.1 = (f32[1024,256]{1,0:T(8,128)}, f32[1024,256]{1,0:T(8,128)S(1)}, u32[]{:S(2)}, u32[]{:S(2)}) collective-permute-start(f32[1024,256]{1,0:T(8,128)} %own_ref.1), channel_id=1, source_target_pairs={{0,1},{1,0},{2,3},{3,2},{4,5},{5,4},{6,7},{7,6},{8,9},{9,8},{10,11... | collective-permute-start | bytes 3145736 | tf_op jit(solution)/shard_map/ppermute | solution.py:310
  1.1 26.6 %collective-permute-start = (f32[1024,256]{1,0:T(8,128)}, f32[1024,256]{1,0:T(8,128)S(1)}, u32[]{:S(2)}, u32[]{:S(2)}) collective-permute-start(f32[1024,256]{1,0:T(8,128)} %own_ref.1), channel_id=1, source_target_pairs={{0,2},{1,3},{2,0},{3,1},{4,6},{5,7},{6,4},{7,5},{8,10},{9,11},{10,... | collective-permute-start | bytes 3145736 | tf_op jit(solution)/shard_map/ppermute | solution.py:310
  3.9 1.0 copy-start.1
  5.5 1.4 %collective-permute-start.2 = (f32[256,128]{1,0:T(8,128)S(1)}, f32[256,128]{1,0:T(8,128)S(1)}, u32[]{:S(2)}, u32[]{:S(2)}) collective-permute-start(f32[256,128]{1,0:T(8,128)S(1)} %get-tuple-element.40.mine_ref), channel_id=1, source_target_pairs={{0,1},{1,0},{2,3},{3,2},{4,5},{5,4},{6,7},{7,6},{8,9},{9,8},{10,11... | collective-permute-start | bytes 393224 | tf_op jit(solution)/shard_map/ppermute | solution.py:310
  7.0 1.2 %copy-start = (f32[1024,256]{1,0:T(8,128)S(1)}, f32[1024,256]{1,0:T(8,128)}, u32[]{:S(2)}) copy-start(f32[1024,256]{1,0:T(8,128)} %own_ref.1) | copy-start | bytes 3145732
  27.8 7.3 %collective-permute-start.3 = (f32[1024,256]{1,0:T(8,128)S(1)}, f32[1024,256]{1,0:T(8,128)S(1)}, u32[]{:S(2)}, u32[]{:S(2)}) collective-permute-start(f32[1024,256]{1,0:T(8,128)S(1)} %collective-permute-done.side_ref), channel_id=1, source_target_pairs={{0,1},{1,0},{2,3},{3,2},{4,5},{5,4},{6,7},{7,6},{8,9},{9,8},{10,11... | collective-permute-start | bytes 3145736 | tf_op jit(solution)/shard_map/ppermute | solution.py:310
  27.8 5.9 %collective-permute-start.4 = (f32[256,128]{1,0:T(8,128)S(1)}, f32[256,128]{1,0:T(8,128)S(1)}, u32[]{:S(2)}, u32[]{:S(2)}) collective-permute-start(f32[256,128]{1,0:T(8,128)S(1)} %get-tuple-element.45), channel_id=1, source_target_pairs={{0,2},{1,3},{2,0},{3,1},{4,6},{5,7},{6,4},{7,5},{8,10},{9,11},{10,... | collective-permute-start | bytes 393224 | tf_op jit(solution)/shard_map/ppermute | solution.py:310
  33.7 1.3 %collective-permute-start.5 = (f32[256,128]{1,0:T(8,128)S(1)}, f32[256,128]{1,0:T(8,128)S(1)}, u32[]{:S(2)}, u32[]{:S(2)}) collective-permute-start(f32[256,128]{1,0:T(8,128)S(1)} %collective-permute-done.4.sketch_ref), channel_id=1, source_target_pairs={{0,1},{1,0},{2,3},{3,2},{4,5},{5,4},{6,7},{7,6},{8,9},{9,8},{10,11... | collective-permute-start | bytes 393224 | tf_op jit(solution)/shard_map/ppermute | solution.py:310
  36.6 12.9 %collective-permute-start.6 = (f32[256,128]{1,0:T(8,128)S(1)}, f32[256,128]{1,0:T(8,128)S(1)}, u32[]{:S(2)}, u32[]{:S(2)}) collective-permute-start(f32[256,128]{1,0:T(8,128)S(1)} %get-tuple-element.47.a_ref), channel_id=1, source_target_pairs={{0,4},{1,5},{2,6},{3,7},{4,0},{5,1},{6,2},{7,3},{8,12},{9,13},{10,... | collective-permute-start | bytes 393224 | tf_op jit(solution)/shard_map/ppermute | solution.py:310
  39.4 12.6 %collective-permute-start.13 = (f32[256,128]{1,0:T(8,128)S(1)}, f32[256,128]{1,0:T(8,128)S(1)}, u32[]{:S(2)}, u32[]{:S(2)}) collective-permute-start(f32[256,128]{1,0:T(8,128)S(1)} %get-tuple-element.56.a_ref), channel_id=1, source_target_pairs={{0,4},{1,5},{2,6},{3,7},{4,0},{5,1},{6,2},{7,3},{8,12},{9,13},{10,... | collective-permute-start | bytes 393224 | tf_op jit(solution)/shard_map/ppermute | solution.py:310
  50.3 5.0 %collective-permute-start.7 = (f32[264,128]{1,0:T(8,128)S(1)}, f32[264,128]{1,0:T(8,128)S(1)}, u32[]{:S(2)}, u32[]{:S(2)}) collective-permute-start(f32[264,128]{1,0:T(8,128)S(1)} %shard_map.53), channel_id=1, source_target_pairs={{0,8},{1,17},{2,10},{3,19},{4,12},{5,21},{6,14},{7,23},{8,0},{9,25... | collective-permute-start | bytes 405512 | tf_op jit(solution)/shard_map/ppermute | solution.py:321
  52.8 6.0 %collective-permute-start.14 = (f32[264,128]{1,0:T(8,128)S(1)}, f32[264,128]{1,0:T(8,128)S(1)}, u32[]{:S(2)}, u32[]{:S(2)}) collective-permute-start(f32[264,128]{1,0:T(8,128)S(1)} %shard_map.57), channel_id=1, source_target_pairs={{0,8},{1,17},{2,10},{3,19},{4,12},{5,21},{6,14},{7,23},{8,0},{9,25... | collective-permute-start | bytes 405512 | tf_op jit(solution)/shard_map/ppermute | solution.py:321
  55.3 5.1 %collective-permute-start.8 = (f32[264,128]{1,0:T(8,128)S(1)}, f32[264,128]{1,0:T(8,128)S(1)}, u32[]{:S(2)}, u32[]{:S(2)}) collective-permute-start(f32[264,128]{1,0:T(8,128)S(1)} %add.25.refs_0_), channel_id=1, source_target_pairs={{0,16},{1,9},{2,18},{3,11},{4,20},{5,13},{6,22},{7,15},{8,24},{9,1... | collective-permute-start | bytes 405512 | tf_op jit(solution)/shard_map/ppermute | solution.py:321
  58.8 5.1 %collective-permute-start.15 = (f32[264,128]{1,0:T(8,128)S(1)}, f32[264,128]{1,0:T(8,128)S(1)}, u32[]{:S(2)}, u32[]{:S(2)}) collective-permute-start(f32[264,128]{1,0:T(8,128)S(1)} %add.27.refs_0_), channel_id=1, source_target_pairs={{0,16},{1,9},{2,18},{3,11},{4,20},{5,13},{6,22},{7,15},{8,24},{9,1... | collective-permute-start | bytes 405512 | tf_op jit(solution)/shard_map/ppermute | solution.py:321
  61.9 11.8 %collective-permute-start.9 = (f32[264,128]{1,0:T(8,128)S(1)}, f32[264,128]{1,0:T(8,128)S(1)}, u32[]{:S(2)}, u32[]{:S(2)}) collective-permute-start(f32[264,128]{1,0:T(8,128)S(1)} %get-tuple-element.52.refs_0_), channel_id=1, source_target_pairs={{0,4},{1,5},{2,6},{3,7},{4,0},{5,1},{6,2},{7,3},{8,12},{9,13},{10,... | collective-permute-start | bytes 405512 | tf_op jit(solution)/shard_map/ppermute | solution.py:310
  65.4 10.7 %collective-permute-start.16 = (f32[264,128]{1,0:T(8,128)S(1)}, f32[264,128]{1,0:T(8,128)S(1)}, u32[]{:S(2)}, u32[]{:S(2)}) collective-permute-start(f32[264,128]{1,0:T(8,128)S(1)} %get-tuple-element.57.refs_0_), channel_id=1, source_target_pairs={{0,4},{1,5},{2,6},{3,7},{4,0},{5,1},{6,2},{7,3},{8,12},{9,13},{10,... | collective-permute-start | bytes 405512 | tf_op jit(solution)/shard_map/ppermute | solution.py:310
  74.6 6.2 %collective-permute-start.10 = (f32[264,128]{1,0:T(8,128)S(1)}, f32[264,128]{1,0:T(8,128)S(1)}, u32[]{:S(2)}, u32[]{:S(2)}) collective-permute-start(f32[264,128]{1,0:T(8,128)S(1)} %get-tuple-element.53), channel_id=1, source_target_pairs={{0,8},{1,17},{2,10},{3,19},{4,12},{5,21},{6,14},{7,23},{8,0},{9,25... | collective-permute-start | bytes 405512 | tf_op jit(solution)/shard_map/ppermute | solution.py:321
  77.0 6.5 %collective-permute-start.17 = (f32[264,128]{1,0:T(8,128)S(1)}, f32[264,128]{1,0:T(8,128)S(1)}, u32[]{:S(2)}, u32[]{:S(2)}) collective-permute-start(f32[264,128]{1,0:T(8,128)S(1)} %get-tuple-element.58), channel_id=1, source_target_pairs={{0,8},{1,17},{2,10},{3,19},{4,12},{5,21},{6,14},{7,23},{8,0},{9,25... | collective-permute-start | bytes 405512 | tf_op jit(solution)/shard_map/ppermute | solution.py:321
  80.8 5.1 %collective-permute-start.11 = (f32[264,128]{1,0:T(8,128)S(1)}, f32[264,128]{1,0:T(8,128)S(1)}, u32[]{:S(2)}, u32[]{:S(2)}) collective-permute-start(f32[264,128]{1,0:T(8,128)S(1)} %add.26.refs_0_), channel_id=1, source_target_pairs={{0,16},{1,9},{2,18},{3,11},{4,20},{5,13},{6,22},{7,15},{8,24},{9,1... | collective-permute-start | bytes 405512 | tf_op jit(solution)/shard_map/ppermute | solution.py:321
  83.5 5.1 %collective-permute-start.18 = (f32[264,128]{1,0:T(8,128)S(1)}, f32[264,128]{1,0:T(8,128)S(1)}, u32[]{:S(2)}, u32[]{:S(2)}) collective-permute-start(f32[264,128]{1,0:T(8,128)S(1)} %add.28.refs_0_), channel_id=1, source_target_pairs={{0,16},{1,9},{2,18},{3,11},{4,20},{5,13},{6,22},{7,15},{8,24},{9,1... | collective-permute-start | bytes 405512 | tf_op jit(solution)/shard_map/ppermute | solution.py:321
  87.3 9.2 %collective-permute-start.12 = (f32[264,128]{1,0:T(8,128)S(1)}, f32[264,128]{1,0:T(8,128)S(1)}, u32[]{:S(2)}, u32[]{:S(2)}) collective-permute-start(f32[264,128]{1,0:T(8,128)S(1)} %get-tuple-element.54.own_ref), channel_id=1, source_target_pairs={{0,4},{1,5},{2,6},{3,7},{4,0},{5,1},{6,2},{7,3},{8,12},{9,13},{10,... | collective-permute-start | bytes 405512 | tf_op jit(solution)/shard_map/ppermute | solution.py:310
  90.1 8.1 %collective-permute-start.19 = (f32[264,128]{1,0:T(8,128)S(1)}, f32[264,128]{1,0:T(8,128)S(1)}, u32[]{:S(2)}, u32[]{:S(2)}) collective-permute-start(f32[264,128]{1,0:T(8,128)S(1)} %get-tuple-element.64.own_ref), channel_id=1, source_target_pairs={{0,4},{1,5},{2,6},{3,7},{4,0},{5,1},{6,2},{7,3},{8,12},{9,13},{10,... | collective-permute-start | bytes 405512 | tf_op jit(solution)/shard_map/ppermute | solution.py:310
  97.8 5.8 %collective-permute-start.20 = (f32[328,128]{1,0:T(8,128)S(1)}, f32[328,128]{1,0:T(8,128)S(1)}, u32[]{:S(2)}, u32[]{:S(2)}) collective-permute-start(f32[328,128]{1,0:T(8,128)S(1)} %get-tuple-element.69), channel_id=1, source_target_pairs={{0,2},{1,3},{2,0},{3,1},{4,6},{5,7},{6,4},{7,5},{8,10},{9,11},{10,... | collective-permute-start | bytes 503816 | tf_op jit(solution)/shard_map/ppermute | solution.py:310
  99.4 4.2 %collective-permute-start.21 = (f32[72,128]{1,0:T(8,128)S(1)}, f32[72,128]{1,0:T(8,128)S(1)}, u32[]{:S(2)}, u32[]{:S(2)}) collective-permute-start(f32[72,128]{1,0:T(8,128)S(1)} %get-tuple-element.70), channel_id=1, source_target_pairs={{0,2},{1,3},{2,0},{3,1},{4,6},{5,7},{6,4},{7,5},{8,10},{9,11},{10,... | collective-permute-start | bytes 110600 | tf_op jit(solution)/shard_map/ppermute | solution.py:310
  104.2 1.5 %collective-permute-start.22 = (f32[392,128]{1,0:T(8,128)S(1)}, f32[392,128]{1,0:T(8,128)S(1)}, u32[]{:S(2)}, u32[]{:S(2)}) collective-permute-start(f32[392,128]{1,0:T(8,128)S(1)} %get-tuple-element.72), channel_id=1, source_target_pairs={{0,1},{1,0},{2,3},{3,2},{4,5},{5,4},{6,7},{7,6},{8,9},{9,8},{10,11... | collective-permute-start | bytes 602120 | tf_op jit(solution)/shard_map/ppermute | solution.py:310
  106.3 3.7 %collective-permute-start.23 = (f32[8,256]{1,0:T(8,128)S(1)}, f32[8,256]{1,0:T(8,128)S(1)}, u32[]{:S(2)}, u32[]{:S(2)}) collective-permute-start(f32[8,256]{1,0:T(8,128)S(1)} %get-tuple-element.74.known_ref.refs_4_), channel_id=1, source_target_pairs={{0,8},{1,17},{2,10},{3,19},{4,12},{5,21},{6,14},{7,23},{8,0},{9,25... | collective-permute-start | bytes 24584 | tf_op jit(solution)/shard_map/ppermute | solution.py:321
  110.1 3.7 %collective-permute-start.24 = (f32[8,256]{1,0:T(8,128)S(1)}, f32[8,256]{1,0:T(8,128)S(1)}, u32[]{:S(2)}, u32[]{:S(2)}) collective-permute-start(f32[8,256]{1,0:T(8,128)S(1)} %add.29.a_ref), channel_id=1, source_target_pairs={{0,16},{1,9},{2,18},{3,11},{4,20},{5,13},{6,22},{7,15},{8,24},{9,1... | collective-permute-start | bytes 24584 | tf_op jit(solution)/shard_map/ppermute | solution.py:321

commit v8 on v7

--- a/solution.py
+++ b/solution.py
@@ -19,6 +19,12 @@
 F32 = jnp.float32
 
 
+def position():
+    seat = lax.axis_index("snap")
+    core, chip = lax.rem(seat, 2), lax.div(seat, 2)
+    return core, lax.rem(chip, 2), chip
+
+
 def split(x):
     high = x.astype(BF16).astype(F32)
     return high, x - high
@@ -74,9 +80,11 @@
     return total[:cols] + total[cols:]
 
 
-def sketch_side(place_ref, x):
-    x = jnp.where(place_ref[0] == 0, x, turn(x, QUARTER))
-    return join_lanes(*split(x), QUARTER).astype(BF16)
+def sketch_sides(x):
+    high, low = split(x)
+    own = join_lanes(high, low, QUARTER)
+    other = join_lanes(turn(high, QUARTER), turn(low, QUARTER), QUARTER)
+    return own.astype(BF16), other.astype(BF16)
 
 
 def store_factors(high_ref, low_ref, blocks):
@@ -87,37 +95,41 @@
         low_ref[:, cut] = low.astype(BF16)
 
 
-def prepare_kernel(place_ref, sketch_ref, mine_ref, theirs_ref):
-    near, far = sketch_ref[:, :LANES], sketch_ref[:, LANES:]
-    low = join_lanes(near, far, QUARTER)
-    high = join_lanes(turn(near, QUARTER), turn(far, QUARTER), QUARTER)
-    zero = place_ref[1] == 0
+def prepare_kernel(near_ref, got_ref, mine_ref, theirs_ref):
+    near, got = near_ref[...], got_ref[...]
+    low = join_lanes(near, got, QUARTER)
+    high = join_lanes(turn(near, QUARTER), turn(got, QUARTER), QUARTER)
+    zero = position()[1] == 0
     mine_ref[...] = jnp.where(zero, low, high)
     theirs_ref[...] = jnp.where(zero, high, low)
 
 
-def near_kernel(place_ref, own_ref, core_ref, mine_ref, got_ref, y_ref, high_ref, low_ref):
+def near_kernel(own_ref, core_ref, sketch_ref, y_ref, high_ref, low_ref):
     store_factors(high_ref, low_ref, (own_ref[...], core_ref[...]))
-    rhs = jnp.concatenate([sketch_side(place_ref, ref[...]) for ref in (mine_ref, got_ref)], axis=0)
+    rhs = jnp.concatenate(sketch_sides(sketch_ref[...]), axis=0)
     for b in range(own_ref.shape[0] // LANES):
         cut = slice(b * LANES, (b + 1) * LANES)
         total = dot(high_ref[cut, :], rhs) + dot(low_ref[cut, :], rhs)
         y_ref[b * QUARTER : (b + 1) * QUARTER, :] = unfold(total.T)
 
 
-def split_kernel(side_ref, high_ref, low_ref):
+def side_kernel(side_ref, sketch_ref, near_ref, y_ref, high_ref, low_ref):
     store_factors(high_ref, low_ref, (side_ref[...],))
-
-
-def far_kernel(place_ref, high_side_ref, low_side_ref, diagonal_ref, sketch_ref, core_sketch_ref, near_ref, *refs):
+    rhs = sketch_sides(sketch_ref[...])[0]
+    for b in range(high_ref.shape[0] // LANES):
+        cut = slice(b * LANES, (b + 1) * LANES)
+        total = dot(high_ref[cut, :], rhs) + dot(low_ref[cut, :], rhs)
+        out = slice(b * QUARTER, (b + 1) * QUARTER)
+        y_ref[out, :] = unfold(total.T) + near_ref[out, :]
+
+
+def far_kernel(diagonal_ref, sketch_ref, near_ref, *refs):
     *halves, high_ref, low_ref = refs
     store_factors(high_ref, low_ref, (diagonal_ref[...],))
-    side = sketch_side(place_ref, sketch_ref[...])
-    diagonal = sketch_side(place_ref, core_sketch_ref[...])
+    rhs = sketch_sides(sketch_ref[...])[1]
     for b in range(high_ref.shape[0] // LANES):
         cut = slice(b * LANES, (b + 1) * LANES)
-        total = dot(high_side_ref[cut, :], side) + dot(low_side_ref[cut, :], side)
-        total += dot(high_ref[cut, :], diagonal) + dot(low_ref[cut, :], diagonal)
+        total = dot(high_ref[cut, :], rhs) + dot(low_ref[cut, :], rhs)
         y = unfold(total.T) + near_ref[b * QUARTER : (b + 1) * QUARTER, :]
         for h, ref in enumerate(halves):
             ref[b * COLS : (b + 1) * COLS, :] = y[h * COLS : (h + 1) * COLS]
@@ -165,18 +177,17 @@
         store_blocks(z_ref, 0, z)
     y_ref[-TILE:, :] = squares_tile(z)
     rhs = jnp.concatenate(split(z), axis=0).T.astype(BF16)
-    for b in range(high_refs[0].shape[0] // LANES):
-        cut = slice(b * LANES, (b + 1) * LANES)
-        total, at = None, 0
-        for high_ref, low_ref in zip(high_refs, low_refs):
-            part = rhs[at : at + high_ref.shape[1]]
-            term = dot(high_ref[cut, :], part) + dot(low_ref[cut, :], part)
-            total = term if total is None else total + term
-            at += high_ref.shape[1]
-        y_ref[b * COLS : (b + 1) * COLS, :] = unfold(total.T)
-
-
-def end_kernel(count, carried, place_ref, own_ref, got_ref, *refs):
+    total, at = None, 0
+    for high_ref, low_ref in zip(high_refs, low_refs):
+        part = rhs[at : at + high_ref.shape[1]]
+        term = dot(high_ref[...], part) + dot(low_ref[...], part)
+        total = term if total is None else total + term
+        at += high_ref.shape[1]
+    for b in range(total.shape[0] // LANES):
+        y_ref[b * COLS : (b + 1) * COLS, :] = unfold(total[b * LANES : (b + 1) * LANES].T)
+
+
+def end_kernel(count, carried, own_ref, got_ref, *refs):
     parts, scales, (keep_ref, send_ref, y_ref) = refs[:carried], refs[carried:-3], refs[-3:]
     y, scale = scaled(own_ref, got_ref, count)
     store_blocks(y_ref, 0, y)
@@ -185,8 +196,9 @@
     for i, known in enumerate([ref[...] for ref in scales] + [scale]):
         tail = jnp.where(row == i, known, tail)
     size = 2 * COLS
-    for ref, chip in ((keep_ref, place_ref[2]), (send_ref, place_ref[3])):
-        start = pl.multiple_of(chip * size, size)
+    chip = position()[2]
+    for ref, owner in ((keep_ref, chip), (send_ref, chip ^ 1)):
+        start = pl.multiple_of(owner * size, size)
         ref[:size, :] = y_ref[pl.ds(start, size), :]
         ref[size : size + TILE, :] = tail
     at = size + TILE
@@ -196,10 +208,11 @@
         at += middle
 
 
-def core_kernel(place_ref, *refs):
+def core_kernel(*refs):
     keeps, gots, parts = (refs[i * HALVES : (i + 1) * HALVES] for i in range(3))
     keep_ref, send_ref = refs[3 * HALVES :]
-    zero_side, zero_core = place_ref[1] == 0, place_ref[0] == 0
+    core, side, _ = position()
+    zero_side, zero_core = side == 0, core == 0
     tail = None
     for s in range(2):
         for h in range(HALVES):
@@ -221,8 +234,8 @@
         send_ref[at : at + size, :] = gots[0][start : start + size, :]
 
 
-def join_kernel(place_ref, keep_ref, got_ref, y_ref, known_ref):
-    zero = place_ref[0] == 0
+def join_kernel(keep_ref, got_ref, y_ref, known_ref):
+    zero = position()[0] == 0
     keep, got = keep_ref[...], got_ref[: LANES + TILE, :]
     for s, x in enumerate((jnp.where(zero, keep, got), jnp.where(zero, got, keep))):
         cut = slice(s * LANES, (s + 1) * LANES)
@@ -230,9 +243,9 @@
         known_ref[:, cut] = x[LANES:]
 
 
-def z_out_kernel(place_ref, *refs):
+def z_out_kernel(*refs):
     parts, (side_ref, core_ref, known_ref, z_ref) = refs[:HALVES], refs[HALVES:]
-    zero_side, zero_core = place_ref[1] == 0, place_ref[0] == 0
+    zero_core, zero_side = (flag == 0 for flag in position()[:2])
     size = 2 * COLS
     side_at, core_at = size + TILE, LANES + TILE
     mine = [ref[:size, :] for ref in parts]
@@ -250,25 +263,31 @@
         z_ref[:, cut] = x.T / known_ref[2 * ITERS - 1 : 2 * ITERS, cut]
 
 
-def q_out_kernel(count, y_ref, known_ref, a_ref, b_ref, q_ref, scale_ref):
+def q_out_kernel(count, y_ref, known_ref, *refs):
+    gots, (q_ref, scale_ref) = refs[:-2], refs[-2:]
     last = 2 * ITERS
-    scale = rms((a_ref[...] + b_ref[...])[last : last + 1], count)
+    row = slice(last, last + 1)
+    total = (known_ref[row, :] + gots[0][row, :]) + (gots[1][row, :] + gots[2][row, :])
+    scale = rms(total, count)
     q_ref[...] = y_ref[...] / scale
     scale_ref[:last, :] = known_ref[:last, :]
     scale_ref[last:, :] = scale
 
 
-def call(kernel, outs, *args, scalars=1, plain=False):
-    specs = [pl.BlockSpec(memory_space=pltpu.SMEM)] * scalars
-    specs += [pl.BlockSpec(memory_space=pltpu.VMEM)] * (len(args) - scalars)
+def call(kernel, outs, *args, plain=False, scratch=(), cost=None):
     out_spec = pl.BlockSpec() if plain else pl.BlockSpec(memory_space=pltpu.VMEM)
     return pl.pallas_call(
         kernel,
         out_shape=[jax.ShapeDtypeStruct(shape, dtype) for shape, dtype in outs],
-        in_specs=specs,
+        in_specs=[pl.BlockSpec(memory_space=pltpu.VMEM)] * len(args),
         out_specs=[out_spec] * len(outs),
+        scratch_shapes=scratch,
+        cost_estimate=cost,
         compiler_params=pltpu.CompilerParams(vmem_limit_bytes=16 * 1024 * 1024),
     )(*args)
+
+
+LONG = pl.CostEstimate(flops=10**11, bytes_accessed=2**28, transcendentals=0)
 
 
 def general(snapshots, sketch):
@@ -302,9 +321,6 @@
         return general(snapshots, sketch)
     all_cells = rows * groups
     all_snaps = width * places
-    seat = lax.axis_index("snap")
-    chip = seat // 2
-    place = jnp.stack([seat % 2, chip % 2, chip, chip ^ 1]).astype(jnp.int32)
 
     def swap(x, bits):
         return lax.ppermute(x, "snap", [(i, i ^ bits) for i in range(places)])
@@ -327,20 +343,21 @@
     def factor(count):
         return [((rows, count * width), BF16)] * 2
 
+    def sketch_half(index):
+        return lax.dynamic_slice_in_dim(sketch, index * LANES, LANES, 1)
+
+    core = lax.rem(lax.axis_index("snap"), 2)
     side_block = swap_side(snapshots)
     packed = ((width, LANES), F32)
-    mine, theirs = call(prepare_kernel, [packed, packed], place, sketch)
-    near_y, *near = call(
-        near_kernel, [((rows // LANES * QUARTER, LANES), F32)] + factor(2),
-        place, snapshots, swap_core(snapshots), mine, swap_core(mine),
-    )
+    mine, theirs = call(prepare_kernel, [packed, packed], sketch_half(core), swap_core(sketch_half(1 - core)))
     side_sketch = swap_side(theirs)
+    quarter_shape = ((rows // LANES * QUARTER, LANES), F32)
+    near_y, *near = call(near_kernel, [quarter_shape] + factor(2), snapshots, swap_core(snapshots), mine)
     side_block, near_y = lax.optimization_barrier((side_block, near_y))
-    side = call(split_kernel, factor(1), side_block, scalars=0)
+    side_y, *side = call(side_kernel, [quarter_shape] + factor(1), side_block, side_sketch, near_y, cost=LONG)
     half_shape = ((rows // LANES * COLS, LANES), F32)
     *own, high, low = call(
-        far_kernel, [half_shape] * HALVES + factor(1),
-        place, *side, swap_core(side_block), side_sketch, swap_core(side_sketch), near_y,
+        far_kernel, [half_shape] * HALVES + factor(1), swap_core(side_block), side_sketch, side_y
     )
     matrix = (near[0], side[0], high, near[1], side[1], low)
 
@@ -350,14 +367,14 @@
     scale_shape = ((TILE, LANES), F32)
     z_shape = ((COLS * 4 * width // LANES, LANES), F32)
     scales = [[] for _ in range(HALVES)]
-    sent = [call(first_z_kernel, [sent_shape], y, swap_pair(y), *matrix, scalars=0)[0] for y in own]
+    sent = [call(first_z_kernel, [sent_shape], y, swap_pair(y), *matrix)[0] for y in own]
     ys, zs = [None] * HALVES, [None] * HALVES
     for section in range(ITERS):
         last = section == ITERS - 1
         for h in range(HALVES):
             ys[h], scale, *z = call(
                 functools.partial(y_kernel, all_cells), [y_shape, scale_shape] + [z_shape] * last,
-                *cell_pair(sent[h]), *matrix, scalars=0,
+                *cell_pair(sent[h]), *matrix,
             )
             scales[h].append(scale)
             if last:
@@ -365,7 +382,7 @@
                 continue
             sent[h], scale = call(
                 functools.partial(z_kernel, all_snaps), [sent_shape, scale_shape],
-                ys[h], swap_pair(ys[h]), *matrix, scalars=0,
+                ys[h], swap_pair(ys[h]), *matrix,
             )
             scales[h].append(scale)
 
@@ -374,25 +391,26 @@
     keeps, gots = [], []
     for h in range(HALVES):
         parts = zs if h == 0 else []
-        keep, send, _ = call(
+        keep, send = call(
             functools.partial(end_kernel, all_snaps, len(parts)),
-            [(small, F32), ((small[0] + carried * (h == 0), LANES), F32), ((flat[0] - TILE, LANES), F32)],
-            place, ys[h], swap_pair(ys[h]), *parts, *scales[h],
+            [(small, F32), ((small[0] + carried * (h == 0), LANES), F32)],
+            ys[h], swap_pair(ys[h]), *parts, *scales[h],
+            scratch=[pltpu.VMEM((flat[0] - TILE, LANES), F32)],
         )
         keeps.append(keep)
         gots.append(swap_side(send))
     keep, send = call(
         core_kernel, [((LANES + TILE, LANES), F32), ((LANES + TILE + carried, LANES), F32)],
-        place, *keeps, *gots, *zs,
+        *keeps, *gots, *zs,
     )
     core_got = swap_core(send)
-    y, known = call(join_kernel, [((LANES, rank), F32), ((TILE, rank), F32)], place, keep, core_got)
-    a, b = cell_pair(known)
-    (z_out,) = call(z_out_kernel, [((width, rank), F32)], place, *zs, gots[0], core_got, known, plain=True)
+    y, known = call(join_kernel, [((LANES, rank), F32), ((TILE, rank), F32)], keep, core_got)
+    others = [lax.ppermute(known, "cell", [(c, c ^ d) for c in range(groups)]) for d in (1, 2, 3)]
+    (z_out,) = call(z_out_kernel, [((width, rank), F32)], *zs, gots[0], core_got, known, plain=True)
     q_out, scale_out = call(
         functools.partial(q_out_kernel, all_cells),
         [((LANES, rank), F32), ((2 * ITERS + 1, rank), F32)],
-        y, known, a, b, scalars=0, plain=True,
+        y, known, *others, plain=True,
     )
     return q_out, z_out, scale_out
 

time: 115 us -> 107 us (0.930)
  Pallas kernels: 19.3 us -> 13.8 us
  waiting for transfers between devices: 66.4 us -> 64.3 us
    pallas_call x18, Pallas kernels: 19.3 us -> 13.8 us  [call(): pl.pallas_call(kernel, out_shape=[jax.ShapeDtypeStruct(shape, dtype) for...]
    ppermute x10 -> x8, waiting for transfers between devices: 15.9 us -> 11.9 us  [swap_cell(): return lax.ppermute(x, ('cell', 'snap'), perm)]
    ppermute x0 -> x3, starting transfers between devices: none -> 3.55 us  [local(): lax.ppermute(known, 'cell', [(c, c ^ d) for c in range(groups)])]
    ppermute x10 -> x8, starting transfers between devices: 12.7 us -> 10.4 us  [swap_cell(): return lax.ppermute(x, ('cell', 'snap'), perm)]
    ppermute x0 -> x3, waiting for transfers between devices: none -> 2.22 us  [local(): lax.ppermute(known, 'cell', [(c, c ^ d) for c in range(groups)])]
    ppermute x15 -> x14, starting transfers between devices: 13 us -> 11.5 us  [swap(): return lax.ppermute(x, 'snap', [(i, i ^ bits) for i in range(places)])]
    ppermute x15 -> x14, waiting for transfers between devices: 50.4 us -> 50.2 us  [swap(): return lax.ppermute(x, 'snap', [(i, i ^ bits) for i in range(places)])]
  transfers between devices with their start and end apart: 25 -> 25, of which waited for: 20 -> 20; matrix products, arithmetic and copies ran while one was open for 0% -> 1% of each run, Pallas kernels for 14% -> 12%
where the time goes in v8:
time: 107 us
  waiting for transfers between devices  64.3 us (60%)
  starting transfers between devices  25.5 us (24%)
  Pallas kernels  13.8 us (13%)
  local copies, waits for them, and re-layouts  2.21 us (2%)
    ppermute x14, waiting for transfers between devices, swap(): return lax.ppermute(x, 'snap', [(i, i ^ bits) for i in range(places)])  50.2 us
    pallas_call x18, Pallas kernels, call(): pl.pallas_call(kernel, out_shape=[jax.ShapeDtypeStruct(shape, dtype) for...  13.8 us
    ppermute x8, waiting for transfers between devices, swap_cell(): return lax.ppermute(x, ('cell', 'snap'), perm)  11.9 us
    ppermute x14, starting transfers between devices, swap(): return lax.ppermute(x, 'snap', [(i, i ^ bits) for i in range(places)])  11.5 us
    ppermute x8, starting transfers between devices, swap_cell(): return lax.ppermute(x, ('cell', 'snap'), perm)  10.4 us
    ppermute x3, starting transfers between devices, local(): lax.ppermute(known, 'cell', [(c, c ^ d) for c in range(groups)])  3.55 us
    ppermute x3, waiting for transfers between devices, local(): lax.ppermute(known, 'cell', [(c, c ^ d) for c in range(groups)])  2.22 us
  transfers between devices with their start and end apart: 25, of which 20 were waited for; matrix products, arithmetic and copies ran while one was open for 1% of the time, Pallas kernels for 12%

profile of v8, /device:TPU:0, one launch (start us, length us, event | category | flops | bytes accessed | tf_op | source)
XLA Modules:
  0.0 106.7 jit_solution(11827420633887885743)
XLA Ops:
  0.6 0.5 collective-permute-start.1
  1.1 2.7 %collective-permute-start = (f32[1024,256]{1,0:T(8,128)}, f32[1024,256]{1,0:T(8,128)S(1)}, u32[]{:S(2)}, u32[]{:S(2)}) collective-permute-start(f32[1024,256]{1,0:T(8,128)} %own_ref.1), channel_id=1, source_target_pairs={{0,2},{1,3},{2,0},{3,1},{4,6},{5,7},{6,4},{7,5},{8,10},{9,11},{10,... | collective-permute-start | bytes 3145736 | tf_op jit(solution)/shard_map/ppermute | solution.py:326
  3.8 1.0 constant_dynamic-slice_fusion
  4.8 0.2 collective-permute-start.2
  5.0 1.2 %collective-permute-done.2.got_ref = f32[256,128]{1,0:T(8,128)S(1)} collective-permute-done((f32[256,128]{1,0:T(8,128)S(1)}, f32[256,128]{1,0:T(8,128)S(1)}, u32[]{:S(2)}, u32[]{:S(2)}) %collective-permute-start.2) | collective-permute-done | bytes 131104 | tf_op jit(solution)/shard_map/ppermute | solution.py:326
  6.2 0.2 shard_map.49
  6.4 0.4 collective-permute-start.4
  6.8 1.2 %copy-done = f32[1024,256]{1,0:T(8,128)S(1)} copy-done((f32[1024,256]{1,0:T(8,128)S(1)}, f32[1024,256]{1,0:T(8,128)}, u32[]{:S(2)}) %copy-start) | copy-done | bytes 1048600
  8.0 1.0 shard_map.50
  9.0 19.0 %collective-permute-done.side_ref = f32[1024,256]{1,0:T(8,128)S(1)} collective-permute-done((f32[1024,256]{1,0:T(8,128)}, f32[1024,256]{1,0:T(8,128)S(1)}, u32[]{:S(2)}, u32[]{:S(2)}) %collective-permute-start) | collective-permute-done | bytes 1048608 | tf_op jit(solution)/shard_map/ppermute | solution.py:326
  28.0 2.5 %collective-permute-done.4.sketch_ref = f32[256,128]{1,0:T(8,128)S(1)} collective-permute-done((f32[256,128]{1,0:T(8,128)S(1)}, f32[256,128]{1,0:T(8,128)S(1)}, u32[]{:S(2)}, u32[]{:S(2)}) %collective-permute-start.4) | collective-permute-done | bytes 131104 | tf_op jit(solution)/shard_map/ppermute | solution.py:326
  30.6 0.6 shard_map.51
  31.2 0.7 shard_map.52
  31.8 2.8 %collective-permute-start.5 = (f32[256,128]{1,0:T(8,128)S(1)}, f32[256,128]{1,0:T(8,128)S(1)}, u32[]{:S(2)}, u32[]{:S(2)}) collective-permute-start(f32[256,128]{1,0:T(8,128)S(1)} %get-tuple-element.47.a_ref), channel_id=1, source_target_pairs={{0,4},{1,5},{2,6},{3,7},{4,0},{5,1},{6,2},{7,3},{8,12},{9,13},{10,... | collective-permute-start | bytes 393224 | tf_op jit(solution)/shard_map/ppermute | solution.py:326
  34.7 0.2 collective-permute-start.12
  34.8 10.0 %collective-permute-done.5.b_ref = f32[256,128]{1,0:T(8,128)S(1)} collective-permute-done((f32[256,128]{1,0:T(8,128)S(1)}, f32[256,128]{1,0:T(8,128)S(1)}, u32[]{:S(2)}, u32[]{:S(2)}) %collective-permute-start.5) | collective-permute-done | bytes 131104 | tf_op jit(solution)/shard_map/ppermute | solution.py:326
  44.8 0.8 shard_map.53
  45.6 1.7 %collective-permute-start.6 = (f32[264,128]{1,0:T(8,128)S(1)}, f32[264,128]{1,0:T(8,128)S(1)}, u32[]{:S(2)}, u32[]{:S(2)}) collective-permute-start(f32[264,128]{1,0:T(8,128)S(1)} %shard_map.53), channel_id=1, source_target_pairs={{0,8},{1,17},{2,10},{3,19},{4,12},{5,21},{6,14},{7,23},{8,0},{9,25... | collective-permute-start | bytes 405512 | tf_op jit(solution)/shard_map/ppermute | solution.py:337
  47.3 0.8 shard_map.57
  48.1 0.9 collective-permute-start.13
  49.0 1.9 %collective-permute-done.6 = f32[264,128]{1,0:T(8,128)S(1)} collective-permute-done((f32[264,128]{1,0:T(8,128)S(1)}, f32[264,128]{1,0:T(8,128)S(1)}, u32[]{:S(2)}, u32[]{:S(2)}) %collective-permute-start.6) | collective-permute-done | bytes 135200 | tf_op jit(solution)/shard_map/ppermute | solution.py:337
  50.9 2.2 %collective-permute-start.7 = (f32[264,128]{1,0:T(8,128)S(1)}, f32[264,128]{1,0:T(8,128)S(1)}, u32[]{:S(2)}, u32[]{:S(2)}) collective-permute-start(f32[264,128]{1,0:T(8,128)S(1)} %add.20.refs_0_), channel_id=1, source_target_pairs={{0,16},{1,9},{2,18},{3,11},{4,20},{5,13},{6,22},{7,15},{8,24},{9,1... | collective-permute-start | bytes 405512 | tf_op jit(solution)/shard_map/ppermute | solution.py:337
  53.1 0.5 collective-permute-done.13
  53.6 2.0 %collective-permute-start.14 = (f32[264,128]{1,0:T(8,128)S(1)}, f32[264,128]{1,0:T(8,128)S(1)}, u32[]{:S(2)}, u32[]{:S(2)}) collective-permute-start(f32[264,128]{1,0:T(8,128)S(1)} %add.22.refs_0_), channel_id=1, source_target_pairs={{0,16},{1,9},{2,18},{3,11},{4,20},{5,13},{6,22},{7,15},{8,24},{9,1... | collective-permute-start | bytes 405512 | tf_op jit(solution)/shard_map/ppermute | solution.py:337
  55.7 0.4 collective-permute-done.7.refs_1_
  56.1 1.5 %shard_map.54 = (f32[264,128]{1,0:T(8,128)S(1)}, f32[8,128]{1,0:T(8,128)S(1)}) custom-call(f32[264,128]{1,0:T(8,128)S(1)} %add.20.refs_0_, f32[264,128]{1,0:T(8,128)S(1)} %collective-permute-done.7.refs_1_, bf16[1024,512]{1,0:T(8,128)(2,1)S(1)} %get-tuple-element.48.refs_0_.refs_2_, bf16[1024,256]{1,0:T(8,128)(2,1)S(1)} %get-tuple-element.49.refs_1_.refs_3_, ...), custom_call_target="tpu_custom_call" | custom-call | tf_op jit(solution)/shard_map/pallas_call | solution.py:279
  57.6 0.1 collective-permute-start.8
  57.6 1.1 %collective-permute-done.14.refs_1_ = f32[264,128]{1,0:T(8,128)S(1)} collective-permute-done((f32[264,128]{1,0:T(8,128)S(1)}, f32[264,128]{1,0:T(8,128)S(1)}, u32[]{:S(2)}, u32[]{:S(2)}) %collective-permute-start.14) | collective-permute-done | bytes 135200 | tf_op jit(solution)/shard_map/ppermute | solution.py:337
  58.7 1.5 %shard_map.58 = (f32[264,128]{1,0:T(8,128)S(1)}, f32[8,128]{1,0:T(8,128)S(1)}) custom-call(f32[264,128]{1,0:T(8,128)S(1)} %add.22.refs_0_, f32[264,128]{1,0:T(8,128)S(1)} %collective-permute-done.14.refs_1_, bf16[1024,512]{1,0:T(8,128)(2,1)S(1)} %get-tuple-element.48.refs_0_.refs_2_, bf16[1024,256]{1,0:T(8,128)(2,1)S(1)} %get-tuple-element.49.refs_1_.refs_3_, ...), custom_call_target="tpu_custom_call" | custom-call | tf_op jit(solution)/shard_map/pallas_call | solution.py:279
  60.2 1.9 %collective-permute-start.15 = (f32[264,128]{1,0:T(8,128)S(1)}, f32[264,128]{1,0:T(8,128)S(1)}, u32[]{:S(2)}, u32[]{:S(2)}) collective-permute-start(f32[264,128]{1,0:T(8,128)S(1)} %get-tuple-element.59.refs_0_), channel_id=1, source_target_pairs={{0,4},{1,5},{2,6},{3,7},{4,0},{5,1},{6,2},{7,3},{8,12},{9,13},{10,... | collective-permute-start | bytes 405512 | tf_op jit(solution)/shard_map/ppermute | solution.py:326
  62.1 6.5 %collective-permute-done.8.refs_1_ = f32[264,128]{1,0:T(8,128)S(1)} collective-permute-done((f32[264,128]{1,0:T(8,128)S(1)}, f32[264,128]{1,0:T(8,128)S(1)}, u32[]{:S(2)}, u32[]{:S(2)}) %collective-permute-start.8) | collective-permute-done | bytes 135200 | tf_op jit(solution)/shard_map/ppermute | solution.py:326
  68.6 0.9 shard_map.55
  69.5 1.5 %collective-permute-start.9 = (f32[264,128]{1,0:T(8,128)S(1)}, f32[264,128]{1,0:T(8,128)S(1)}, u32[]{:S(2)}, u32[]{:S(2)}) collective-permute-start(f32[264,128]{1,0:T(8,128)S(1)} %get-tuple-element.55), channel_id=1, source_target_pairs={{0,8},{1,17},{2,10},{3,19},{4,12},{5,21},{6,14},{7,23},{8,0},{9,25... | collective-permute-start | bytes 405512 | tf_op jit(solution)/shard_map/ppermute | solution.py:337
  71.1 0.9 shard_map.59
  72.0 0.5 collective-permute-start.16
  72.5 3.2 %collective-permute-done.9 = f32[264,128]{1,0:T(8,128)S(1)} collective-permute-done((f32[264,128]{1,0:T(8,128)S(1)}, f32[264,128]{1,0:T(8,128)S(1)}, u32[]{:S(2)}, u32[]{:S(2)}) %collective-permute-start.9) | collective-permute-done | bytes 135200 | tf_op jit(solution)/shard_map/ppermute | solution.py:337
  75.7 1.0 collective-permute-start.10
  76.8 1.9 %collective-permute-done.16 = f32[264,128]{1,0:T(8,128)S(1)} collective-permute-done((f32[264,128]{1,0:T(8,128)S(1)}, f32[264,128]{1,0:T(8,128)S(1)}, u32[]{:S(2)}, u32[]{:S(2)}) %collective-permute-start.16) | collective-permute-done | bytes 135200 | tf_op jit(solution)/shard_map/ppermute | solution.py:337
  78.6 0.5 collective-permute-start.17
  79.2 1.6 %collective-permute-done.10.refs_1_ = f32[264,128]{1,0:T(8,128)S(1)} collective-permute-done((f32[264,128]{1,0:T(8,128)S(1)}, f32[264,128]{1,0:T(8,128)S(1)}, u32[]{:S(2)}, u32[]{:S(2)}) %collective-permute-start.10) | collective-permute-done | bytes 135200 | tf_op jit(solution)/shard_map/ppermute | solution.py:337
  80.8 1.5 %shard_map.56 = (f32[264,128]{1,0:T(8,128)S(1)}, f32[8,128]{1,0:T(8,128)S(1)}, f32[256,128]{1,0:T(8,128)S(1)}) custom-call(f32[264,128]{1,0:T(8,128)S(1)} %add.21.refs_0_, f32[264,128]{1,0:T(8,128)S(1)} %collective-permute-done.10.refs_1_, bf16[1024,512]{1,0:T(8,128)(2,1)S(1)} %get-tuple-element.48.refs_0_.refs_2_, ...), custom_call_target="tpu_custom_call" | custom-call | tf_op jit(solution)/shard_map/pallas_call | solution.py:279
  82.3 0.1 collective-permute-start.11
  82.4 1.3 %collective-permute-done.17.refs_1_ = f32[264,128]{1,0:T(8,128)S(1)} collective-permute-done((f32[264,128]{1,0:T(8,128)S(1)}, f32[264,128]{1,0:T(8,128)S(1)}, u32[]{:S(2)}, u32[]{:S(2)}) %collective-permute-start.17) | collective-permute-done | bytes 135200 | tf_op jit(solution)/shard_map/ppermute | solution.py:337
  83.7 1.5 %shard_map.60 = (f32[264,128]{1,0:T(8,128)S(1)}, f32[8,128]{1,0:T(8,128)S(1)}, f32[256,128]{1,0:T(8,128)S(1)}) custom-call(f32[264,128]{1,0:T(8,128)S(1)} %add.23.refs_0_, f32[264,128]{1,0:T(8,128)S(1)} %collective-permute-done.17.refs_1_, bf16[1024,512]{1,0:T(8,128)(2,1)S(1)} %get-tuple-element.48.refs_0_.refs_2_, ...), custom_call_target="tpu_custom_call" | custom-call | tf_op jit(solution)/shard_map/pallas_call | solution.py:279
  85.2 1.6 %collective-permute-start.18 = (f32[264,128]{1,0:T(8,128)S(1)}, f32[264,128]{1,0:T(8,128)S(1)}, u32[]{:S(2)}, u32[]{:S(2)}) collective-permute-start(f32[264,128]{1,0:T(8,128)S(1)} %get-tuple-element.66.own_ref), channel_id=1, source_target_pairs={{0,4},{1,5},{2,6},{3,7},{4,0},{5,1},{6,2},{7,3},{8,12},{9,13},{10,... | collective-permute-start | bytes 405512 | tf_op jit(solution)/shard_map/ppermute | solution.py:326
  86.8 4.9 %collective-permute-done.11.got_ref = f32[264,128]{1,0:T(8,128)S(1)} collective-permute-done((f32[264,128]{1,0:T(8,128)S(1)}, f32[264,128]{1,0:T(8,128)S(1)}, u32[]{:S(2)}, u32[]{:S(2)}) %collective-permute-start.11) | collective-permute-done | bytes 135200 | tf_op jit(solution)/shard_map/ppermute | solution.py:326
  91.7 0.2 shard_map.61
  91.9 0.1 collective-permute-start.19
  92.0 1.2 %collective-permute-done.18.got_ref = f32[264,128]{1,0:T(8,128)S(1)} collective-permute-done((f32[264,128]{1,0:T(8,128)S(1)}, f32[264,128]{1,0:T(8,128)S(1)}, u32[]{:S(2)}, u32[]{:S(2)}) %collective-permute-start.18) | collective-permute-done | bytes 135200 | tf_op jit(solution)/shard_map/ppermute | solution.py:326
  93.1 0.2 shard_map.62
  93.3 0.9 collective-permute-start.20
  94.3 3.5 %collective-permute-done.20.refs_3_ = f32[72,128]{1,0:T(8,128)S(1)} collective-permute-done((f32[72,128]{1,0:T(8,128)S(1)}, f32[72,128]{1,0:T(8,128)S(1)}, u32[]{:S(2)}, u32[]{:S(2)}) %collective-permute-start.20) | collective-permute-done | bytes 36896 | tf_op jit(solution)/shard_map/ppermute | solution.py:326
  97.7 0.1 shard_map.63
  97.8 0.0 collective-permute-start.21
  97.8 1.4 %collective-permute-done.21.got_ref.refs_3_ = f32[392,128]{1,0:T(8,128)S(1)} collective-permute-done((f32[392,128]{1,0:T(8,128)S(1)}, f32[392,128]{1,0:T(8,128)S(1)}, u32[]{:S(2)}, u32[]{:S(2)}) %collective-permute-start.21) | collective-permute-done | bytes 200736 | tf_op jit(solution)/shard_map/ppermute | solution.py:326
  99.3 0.1 shard_map.64
  99.4 1.4 %collective-permute-start.24 = (f32[8,256]{1,0:T(8,128)S(1)}, f32[8,256]{1,0:T(8,128)S(1)}, u32[]{:S(2)}, u32[]{:S(2)}) collective-permute-start(f32[8,256]{1,0:T(8,128)S(1)} %get-tuple-element.76.known_ref.refs_4_), channel_id=1, source_target_pairs={{0,24},{8,16},{16,8},{24,0},{1,25},{9,17},{17,9},{25,1},{2,26},{10... | collective-permute-start | bytes 24584 | tf_op jit(solution)/shard_map/ppermute | solution.py:408
  100.8 1.6 %collective-permute-start.23 = (f32[8,256]{1,0:T(8,128)S(1)}, f32[8,256]{1,0:T(8,128)S(1)}, u32[]{:S(2)}, u32[]{:S(2)}) collective-permute-start(f32[8,256]{1,0:T(8,128)S(1)} %get-tuple-element.76.known_ref.refs_4_), channel_id=1, source_target_pairs={{0,16},{8,24},{16,0},{24,8},{1,17},{9,25},{17,1},{25,9},{2,18},{10... | collective-permute-start | bytes 24584 | tf_op jit(solution)/shard_map/ppermute | solution.py:408
  102.3 0.6 collective-permute-start.22
  102.9 0.8 shard_map.66
  103.8 0.2 collective-permute-done.24.refs_2_
  104.0 0.4 collective-permute-done.23.refs_1_
  104.4 1.6 %collective-permute-done.22.refs_0_ = f32[8,256]{1,0:T(8,128)S(1)} collective-permute-done((f32[8,256]{1,0:T(8,128)S(1)}, f32[8,256]{1,0:T(8,128)S(1)}, u32[]{:S(2)}, u32[]{:S(2)}) %collective-permute-start.22) | collective-permute-done | bytes 8224 | tf_op jit(solution)/shard_map/ppermute | solution.py:408
  106.0 0.7 shard_map.65
  (11 shorter events, 0.1 us)
Async XLA Ops:
  0.6 6.2 %collective-permute-start.1 = (f32[1024,256]{1,0:T(8,128)}, f32[1024,256]{1,0:T(8,128)S(1)}, u32[]{:S(2)}, u32[]{:S(2)}) collective-permute-start(f32[1024,256]{1,0:T(8,128)} %own_ref.1), channel_id=1, source_target_pairs={{0,1},{1,0},{2,3},{3,2},{4,5},{5,4},{6,7},{7,6},{8,9},{9,8},{10,11... | collective-permute-start | bytes 3145736 | tf_op jit(solution)/shard_map/ppermute | solution.py:326
  1.1 26.9 %collective-permute-start = (f32[1024,256]{1,0:T(8,128)}, f32[1024,256]{1,0:T(8,128)S(1)}, u32[]{:S(2)}, u32[]{:S(2)}) collective-permute-start(f32[1024,256]{1,0:T(8,128)} %own_ref.1), channel_id=1, source_target_pairs={{0,2},{1,3},{2,0},{3,1},{4,6},{5,7},{6,4},{7,5},{8,10},{9,11},{10,... | collective-permute-start | bytes 3145736 | tf_op jit(solution)/shard_map/ppermute | solution.py:326
  4.8 1.4 %collective-permute-start.2 = (f32[256,128]{1,0:T(8,128)S(1)}, f32[256,128]{1,0:T(8,128)S(1)}, u32[]{:S(2)}, u32[]{:S(2)}) collective-permute-start(f32[256,128]{1,0:T(8,128)S(1)} %get-tuple-element.79), channel_id=1, source_target_pairs={{0,1},{1,0},{2,3},{3,2},{4,5},{5,4},{6,7},{7,6},{8,9},{9,8},{10,11... | collective-permute-start | bytes 393224 | tf_op jit(solution)/shard_map/ppermute | solution.py:326
  6.4 24.2 %collective-permute-start.4 = (f32[256,128]{1,0:T(8,128)S(1)}, f32[256,128]{1,0:T(8,128)S(1)}, u32[]{:S(2)}, u32[]{:S(2)}) collective-permute-start(f32[256,128]{1,0:T(8,128)S(1)} %get-tuple-element.44), channel_id=1, source_target_pairs={{0,2},{1,3},{2,0},{3,1},{4,6},{5,7},{6,4},{7,5},{8,10},{9,11},{10,... | collective-permute-start | bytes 393224 | tf_op jit(solution)/shard_map/ppermute | solution.py:326
  6.8 1.2 %copy-start = (f32[1024,256]{1,0:T(8,128)S(1)}, f32[1024,256]{1,0:T(8,128)}, u32[]{:S(2)}) copy-start(f32[1024,256]{1,0:T(8,128)} %own_ref.1) | copy-start | bytes 3145732
  28.0 3.1 %collective-permute-start.3 = (f32[1024,256]{1,0:T(8,128)S(1)}, f32[1024,256]{1,0:T(8,128)S(1)}, u32[]{:S(2)}, u32[]{:S(2)}) collective-permute-start(f32[1024,256]{1,0:T(8,128)S(1)} %collective-permute-done.side_ref), channel_id=1, source_target_pairs={{0,1},{1,0},{2,3},{3,2},{4,5},{5,4},{6,7},{7,6},{8,9},{9,8},{10,11... | collective-permute-start | bytes 3145736 | tf_op jit(solution)/shard_map/ppermute | solution.py:326
  31.8 12.9 %collective-permute-start.5 = (f32[256,128]{1,0:T(8,128)S(1)}, f32[256,128]{1,0:T(8,128)S(1)}, u32[]{:S(2)}, u32[]{:S(2)}) collective-permute-start(f32[256,128]{1,0:T(8,128)S(1)} %get-tuple-element.47.a_ref), channel_id=1, source_target_pairs={{0,4},{1,5},{2,6},{3,7},{4,0},{5,1},{6,2},{7,3},{8,12},{9,13},{10,... | collective-permute-start | bytes 393224 | tf_op jit(solution)/shard_map/ppermute | solution.py:326
  34.7 12.6 %collective-permute-start.12 = (f32[256,128]{1,0:T(8,128)S(1)}, f32[256,128]{1,0:T(8,128)S(1)}, u32[]{:S(2)}, u32[]{:S(2)}) collective-permute-start(f32[256,128]{1,0:T(8,128)S(1)} %get-tuple-element.58.a_ref), channel_id=1, source_target_pairs={{0,4},{1,5},{2,6},{3,7},{4,0},{5,1},{6,2},{7,3},{8,12},{9,13},{10,... | collective-permute-start | bytes 393224 | tf_op jit(solution)/shard_map/ppermute | solution.py:326
  45.6 5.2 %collective-permute-start.6 = (f32[264,128]{1,0:T(8,128)S(1)}, f32[264,128]{1,0:T(8,128)S(1)}, u32[]{:S(2)}, u32[]{:S(2)}) collective-permute-start(f32[264,128]{1,0:T(8,128)S(1)} %shard_map.53), channel_id=1, source_target_pairs={{0,8},{1,17},{2,10},{3,19},{4,12},{5,21},{6,14},{7,23},{8,0},{9,25... | collective-permute-start | bytes 405512 | tf_op jit(solution)/shard_map/ppermute | solution.py:337
  48.1 5.5 %collective-permute-start.13 = (f32[264,128]{1,0:T(8,128)S(1)}, f32[264,128]{1,0:T(8,128)S(1)}, u32[]{:S(2)}, u32[]{:S(2)}) collective-permute-start(f32[264,128]{1,0:T(8,128)S(1)} %shard_map.57), channel_id=1, source_target_pairs={{0,8},{1,17},{2,10},{3,19},{4,12},{5,21},{6,14},{7,23},{8,0},{9,25... | collective-permute-start | bytes 405512 | tf_op jit(solution)/shard_map/ppermute | solution.py:337
  50.9 5.2 %collective-permute-start.7 = (f32[264,128]{1,0:T(8,128)S(1)}, f32[264,128]{1,0:T(8,128)S(1)}, u32[]{:S(2)}, u32[]{:S(2)}) collective-permute-start(f32[264,128]{1,0:T(8,128)S(1)} %add.20.refs_0_), channel_id=1, source_target_pairs={{0,16},{1,9},{2,18},{3,11},{4,20},{5,13},{6,22},{7,15},{8,24},{9,1... | collective-permute-start | bytes 405512 | tf_op jit(solution)/shard_map/ppermute | solution.py:337
  53.6 5.1 %collective-permute-start.14 = (f32[264,128]{1,0:T(8,128)S(1)}, f32[264,128]{1,0:T(8,128)S(1)}, u32[]{:S(2)}, u32[]{:S(2)}) collective-permute-start(f32[264,128]{1,0:T(8,128)S(1)} %add.22.refs_0_), channel_id=1, source_target_pairs={{0,16},{1,9},{2,18},{3,11},{4,20},{5,13},{6,22},{7,15},{8,24},{9,1... | collective-permute-start | bytes 405512 | tf_op jit(solution)/shard_map/ppermute | solution.py:337
  57.6 11.1 %collective-permute-start.8 = (f32[264,128]{1,0:T(8,128)S(1)}, f32[264,128]{1,0:T(8,128)S(1)}, u32[]{:S(2)}, u32[]{:S(2)}) collective-permute-start(f32[264,128]{1,0:T(8,128)S(1)} %get-tuple-element.54.refs_0_), channel_id=1, source_target_pairs={{0,4},{1,5},{2,6},{3,7},{4,0},{5,1},{6,2},{7,3},{8,12},{9,13},{10,... | collective-permute-start | bytes 405512 | tf_op jit(solution)/shard_map/ppermute | solution.py:326
  60.2 10.9 %collective-permute-start.15 = (f32[264,128]{1,0:T(8,128)S(1)}, f32[264,128]{1,0:T(8,128)S(1)}, u32[]{:S(2)}, u32[]{:S(2)}) collective-permute-start(f32[264,128]{1,0:T(8,128)S(1)} %get-tuple-element.59.refs_0_), channel_id=1, source_target_pairs={{0,4},{1,5},{2,6},{3,7},{4,0},{5,1},{6,2},{7,3},{8,12},{9,13},{10,... | collective-permute-start | bytes 405512 | tf_op jit(solution)/shard_map/ppermute | solution.py:326
  69.5 6.2 %collective-permute-start.9 = (f32[264,128]{1,0:T(8,128)S(1)}, f32[264,128]{1,0:T(8,128)S(1)}, u32[]{:S(2)}, u32[]{:S(2)}) collective-permute-start(f32[264,128]{1,0:T(8,128)S(1)} %get-tuple-element.55), channel_id=1, source_target_pairs={{0,8},{1,17},{2,10},{3,19},{4,12},{5,21},{6,14},{7,23},{8,0},{9,25... | collective-permute-start | bytes 405512 | tf_op jit(solution)/shard_map/ppermute | solution.py:337
  72.0 6.7 %collective-permute-start.16 = (f32[264,128]{1,0:T(8,128)S(1)}, f32[264,128]{1,0:T(8,128)S(1)}, u32[]{:S(2)}, u32[]{:S(2)}) collective-permute-start(f32[264,128]{1,0:T(8,128)S(1)} %get-tuple-element.60), channel_id=1, source_target_pairs={{0,8},{1,17},{2,10},{3,19},{4,12},{5,21},{6,14},{7,23},{8,0},{9,25... | collective-permute-start | bytes 405512 | tf_op jit(solution)/shard_map/ppermute | solution.py:337
  75.7 5.1 %collective-permute-start.10 = (f32[264,128]{1,0:T(8,128)S(1)}, f32[264,128]{1,0:T(8,128)S(1)}, u32[]{:S(2)}, u32[]{:S(2)}) collective-permute-start(f32[264,128]{1,0:T(8,128)S(1)} %add.21.refs_0_), channel_id=1, source_target_pairs={{0,16},{1,9},{2,18},{3,11},{4,20},{5,13},{6,22},{7,15},{8,24},{9,1... | collective-permute-start | bytes 405512 | tf_op jit(solution)/shard_map/ppermute | solution.py:337
  78.6 5.1 %collective-permute-start.17 = (f32[264,128]{1,0:T(8,128)S(1)}, f32[264,128]{1,0:T(8,128)S(1)}, u32[]{:S(2)}, u32[]{:S(2)}) collective-permute-start(f32[264,128]{1,0:T(8,128)S(1)} %add.23.refs_0_), channel_id=1, source_target_pairs={{0,16},{1,9},{2,18},{3,11},{4,20},{5,13},{6,22},{7,15},{8,24},{9,1... | collective-permute-start | bytes 405512 | tf_op jit(solution)/shard_map/ppermute | solution.py:337
  82.3 9.4 %collective-permute-start.11 = (f32[264,128]{1,0:T(8,128)S(1)}, f32[264,128]{1,0:T(8,128)S(1)}, u32[]{:S(2)}, u32[]{:S(2)}) collective-permute-start(f32[264,128]{1,0:T(8,128)S(1)} %get-tuple-element.56.own_ref), channel_id=1, source_target_pairs={{0,4},{1,5},{2,6},{3,7},{4,0},{5,1},{6,2},{7,3},{8,12},{9,13},{10,... | collective-permute-start | bytes 405512 | tf_op jit(solution)/shard_map/ppermute | solution.py:326
  85.2 8.0 %collective-permute-start.18 = (f32[264,128]{1,0:T(8,128)S(1)}, f32[264,128]{1,0:T(8,128)S(1)}, u32[]{:S(2)}, u32[]{:S(2)}) collective-permute-start(f32[264,128]{1,0:T(8,128)S(1)} %get-tuple-element.66.own_ref), channel_id=1, source_target_pairs={{0,4},{1,5},{2,6},{3,7},{4,0},{5,1},{6,2},{7,3},{8,12},{9,13},{10,... | collective-permute-start | bytes 405512 | tf_op jit(solution)/shard_map/ppermute | solution.py:326
  91.9 5.8 %collective-permute-start.19 = (f32[328,128]{1,0:T(8,128)S(1)}, f32[328,128]{1,0:T(8,128)S(1)}, u32[]{:S(2)}, u32[]{:S(2)}) collective-permute-start(f32[328,128]{1,0:T(8,128)S(1)} %get-tuple-element.71), channel_id=1, source_target_pairs={{0,2},{1,3},{2,0},{3,1},{4,6},{5,7},{6,4},{7,5},{8,10},{9,11},{10,... | collective-permute-start | bytes 503816 | tf_op jit(solution)/shard_map/ppermute | solution.py:326
  93.3 4.4 %collective-permute-start.20 = (f32[72,128]{1,0:T(8,128)S(1)}, f32[72,128]{1,0:T(8,128)S(1)}, u32[]{:S(2)}, u32[]{:S(2)}) collective-permute-start(f32[72,128]{1,0:T(8,128)S(1)} %get-tuple-element.72), channel_id=1, source_target_pairs={{0,2},{1,3},{2,0},{3,1},{4,6},{5,7},{6,4},{7,5},{8,10},{9,11},{10,... | collective-permute-start | bytes 110600 | tf_op jit(solution)/shard_map/ppermute | solution.py:326
  97.8 1.5 %collective-permute-start.21 = (f32[392,128]{1,0:T(8,128)S(1)}, f32[392,128]{1,0:T(8,128)S(1)}, u32[]{:S(2)}, u32[]{:S(2)}) collective-permute-start(f32[392,128]{1,0:T(8,128)S(1)} %get-tuple-element.74), channel_id=1, source_target_pairs={{0,1},{1,0},{2,3},{3,2},{4,5},{5,4},{6,7},{7,6},{8,9},{9,8},{10,11... | collective-permute-start | bytes 602120 | tf_op jit(solution)/shard_map/ppermute | solution.py:326
  99.4 4.6 %collective-permute-start.24 = (f32[8,256]{1,0:T(8,128)S(1)}, f32[8,256]{1,0:T(8,128)S(1)}, u32[]{:S(2)}, u32[]{:S(2)}) collective-permute-start(f32[8,256]{1,0:T(8,128)S(1)} %get-tuple-element.76.known_ref.refs_4_), channel_id=1, source_target_pairs={{0,24},{8,16},{16,8},{24,0},{1,25},{9,17},{17,9},{25,1},{2,26},{10... | collective-permute-start | bytes 24584 | tf_op jit(solution)/shard_map/ppermute | solution.py:408
  100.8 3.7 %collective-permute-start.23 = (f32[8,256]{1,0:T(8,128)S(1)}, f32[8,256]{1,0:T(8,128)S(1)}, u32[]{:S(2)}, u32[]{:S(2)}) collective-permute-start(f32[8,256]{1,0:T(8,128)S(1)} %get-tuple-element.76.known_ref.refs_4_), channel_id=1, source_target_pairs={{0,16},{8,24},{16,0},{24,8},{1,17},{9,25},{17,1},{25,9},{2,18},{10... | collective-permute-start | bytes 24584 | tf_op jit(solution)/shard_map/ppermute | solution.py:408
  102.3 3.7 %collective-permute-start.22 = (f32[8,256]{1,0:T(8,128)S(1)}, f32[8,256]{1,0:T(8,128)S(1)}, u32[]{:S(2)}, u32[]{:S(2)}) collective-permute-start(f32[8,256]{1,0:T(8,128)S(1)} %get-tuple-element.76.known_ref.refs_4_), channel_id=1, source_target_pairs={{0,8},{8,0},{16,24},{24,16},{1,9},{9,1},{17,25},{25,17},{2,10},{10... | collective-permute-start | bytes 24584 | tf_op jit(solution)/shard_map/ppermute | solution.py:408

commit v9 on v8

--- a/solution.py
+++ b/solution.py
@@ -87,12 +87,16 @@
     return own.astype(BF16), other.astype(BF16)
 
 
-def store_factors(high_ref, low_ref, blocks):
-    for s, block in enumerate(blocks):
+def store_factors(high_ref, low_ref, blocks, axis=1):
+    start = 0
+    for block in blocks:
+        size = block.shape[axis]
+        cut = [slice(None)] * 2
+        cut[axis] = slice(start, start + size)
         high, low = split(block)
-        cut = slice(s * block.shape[1], (s + 1) * block.shape[1])
-        high_ref[:, cut] = high.astype(BF16)
-        low_ref[:, cut] = low.astype(BF16)
+        high_ref[tuple(cut)] = high.astype(BF16)
+        low_ref[tuple(cut)] = low.astype(BF16)
+        start += size
 
 
 def prepare_kernel(near_ref, got_ref, mine_ref, theirs_ref):
@@ -104,8 +108,10 @@
     theirs_ref[...] = jnp.where(zero, high, low)
 
 
-def near_kernel(own_ref, core_ref, sketch_ref, y_ref, high_ref, low_ref):
-    store_factors(high_ref, low_ref, (own_ref[...], core_ref[...]))
+def near_kernel(own_ref, core_ref, sketch_ref, y_ref, high_ref, low_ref, high_t_ref, low_t_ref):
+    blocks = (own_ref[...], core_ref[...])
+    store_factors(high_ref, low_ref, blocks)
+    store_factors(high_t_ref, low_t_ref, [block.T for block in blocks], 0)
     rhs = jnp.concatenate(sketch_sides(sketch_ref[...]), axis=0)
     for b in range(own_ref.shape[0] // LANES):
         cut = slice(b * LANES, (b + 1) * LANES)
@@ -113,8 +119,12 @@
         y_ref[b * QUARTER : (b + 1) * QUARTER, :] = unfold(total.T)
 
 
-def side_kernel(side_ref, sketch_ref, near_ref, y_ref, high_ref, low_ref):
+def side_split_kernel(side_ref, high_ref, low_ref, high_t_ref, low_t_ref):
     store_factors(high_ref, low_ref, (side_ref[...],))
+    store_factors(high_t_ref, low_t_ref, (side_ref[...].T,), 0)
+
+
+def side_kernel(high_ref, low_ref, sketch_ref, near_ref, y_ref):
     rhs = sketch_sides(sketch_ref[...])[0]
     for b in range(high_ref.shape[0] // LANES):
         cut = slice(b * LANES, (b + 1) * LANES)
@@ -123,16 +133,24 @@
         y_ref[out, :] = unfold(total.T) + near_ref[out, :]
 
 
-def far_kernel(diagonal_ref, sketch_ref, near_ref, *refs):
-    *halves, high_ref, low_ref = refs
-    store_factors(high_ref, low_ref, (diagonal_ref[...],))
+def add_far(h, high_ref, low_ref, sketch_ref, near_ref, y_ref):
     rhs = sketch_sides(sketch_ref[...])[1]
     for b in range(high_ref.shape[0] // LANES):
         cut = slice(b * LANES, (b + 1) * LANES)
         total = dot(high_ref[cut, :], rhs) + dot(low_ref[cut, :], rhs)
-        y = unfold(total.T) + near_ref[b * QUARTER : (b + 1) * QUARTER, :]
-        for h, ref in enumerate(halves):
-            ref[b * COLS : (b + 1) * COLS, :] = y[h * COLS : (h + 1) * COLS]
+        y = unfold(total.T)[h * COLS : (h + 1) * COLS]
+        at = b * QUARTER + h * COLS
+        y_ref[b * COLS : (b + 1) * COLS, :] = y + near_ref[at : at + COLS, :]
+
+
+def far_kernel(diagonal_ref, sketch_ref, near_ref, y_ref, high_ref, low_ref):
+    store_factors(high_ref, low_ref, (diagonal_ref[...],))
+    add_far(0, high_ref, low_ref, sketch_ref, near_ref, y_ref)
+
+
+def second_far_kernel(diagonal_ref, high_ref, low_ref, sketch_ref, near_ref, y_ref, high_t_ref, low_t_ref):
+    add_far(1, high_ref, low_ref, sketch_ref, near_ref, y_ref)
+    store_factors(high_t_ref, low_t_ref, (diagonal_ref[...].T,), 0)
 
 
 def send_z(y, high_refs, low_refs, z_ref):
@@ -176,15 +194,14 @@
     for z_ref in z_refs:
         store_blocks(z_ref, 0, z)
     y_ref[-TILE:, :] = squares_tile(z)
-    rhs = jnp.concatenate(split(z), axis=0).T.astype(BF16)
+    lhs = jnp.concatenate(split(z), axis=0).astype(BF16)
     total, at = None, 0
     for high_ref, low_ref in zip(high_refs, low_refs):
-        part = rhs[at : at + high_ref.shape[1]]
-        term = dot(high_ref[...], part) + dot(low_ref[...], part)
+        part = lhs[:, at : at + high_ref.shape[0]]
+        term = dot(part, high_ref[...]) + dot(part, low_ref[...])
         total = term if total is None else total + term
-        at += high_ref.shape[1]
-    for b in range(total.shape[0] // LANES):
-        y_ref[b * COLS : (b + 1) * COLS, :] = unfold(total[b * LANES : (b + 1) * LANES].T)
+        at += high_ref.shape[0]
+    store_blocks(y_ref, 0, unfold(total))
 
 
 def end_kernel(count, carried, own_ref, got_ref, *refs):
@@ -343,6 +360,9 @@
     def factor(count):
         return [((rows, count * width), BF16)] * 2
 
+    def factor_t(count):
+        return [((count * width, rows), BF16)] * 2
+
     def sketch_half(index):
         return lax.dynamic_slice_in_dim(sketch, index * LANES, LANES, 1)
 
@@ -352,14 +372,21 @@
     mine, theirs = call(prepare_kernel, [packed, packed], sketch_half(core), swap_core(sketch_half(1 - core)))
     side_sketch = swap_side(theirs)
     quarter_shape = ((rows // LANES * QUARTER, LANES), F32)
-    near_y, *near = call(near_kernel, [quarter_shape] + factor(2), snapshots, swap_core(snapshots), mine)
+    near_y, *near = call(
+        near_kernel, [quarter_shape] + factor(2) + factor_t(2), snapshots, swap_core(snapshots), mine
+    )
     side_block, near_y = lax.optimization_barrier((side_block, near_y))
-    side_y, *side = call(side_kernel, [quarter_shape] + factor(1), side_block, side_sketch, near_y, cost=LONG)
+    side = call(side_split_kernel, factor(1) + factor_t(1), side_block)
+    (side_y,) = call(side_kernel, [quarter_shape], *side[:2], side_sketch, near_y, cost=LONG)
     half_shape = ((rows // LANES * COLS, LANES), F32)
-    *own, high, low = call(
-        far_kernel, [half_shape] * HALVES + factor(1), swap_core(side_block), side_sketch, side_y
+    diagonal = swap_core(side_block)
+    own_first, *far = call(far_kernel, [half_shape] + factor(1), diagonal, side_sketch, side_y)
+    own_second, *far_t = call(
+        second_far_kernel, [half_shape] + factor_t(1), diagonal, *far, side_sketch, side_y
     )
-    matrix = (near[0], side[0], high, near[1], side[1], low)
+    own = (own_first, own_second)
+    matrix = (near[0], side[0], far[0], near[1], side[1], far[1])
+    matrix_t = (near[2], side[2], far_t[0], near[3], side[3], far_t[1])
 
     flat = (COLS * rows // LANES + TILE, LANES)
     sent_shape = ((COLS * 4 * width // LANES + TILE, LANES), F32)
@@ -367,14 +394,14 @@
     scale_shape = ((TILE, LANES), F32)
     z_shape = ((COLS * 4 * width // LANES, LANES), F32)
     scales = [[] for _ in range(HALVES)]
-    sent = [call(first_z_kernel, [sent_shape], y, swap_pair(y), *matrix)[0] for y in own]
+    sent = [call(first_z_kernel, [sent_shape], y, swap_pair(y), *matrix, cost=LONG)[0] for y in own]
     ys, zs = [None] * HALVES, [None] * HALVES
     for section in range(ITERS):
         last = section == ITERS - 1
         for h in range(HALVES):
             ys[h], scale, *z = call(
                 functools.partial(y_kernel, all_cells), [y_shape, scale_shape] + [z_shape] * last,
-                *cell_pair(sent[h]), *matrix,
+                *cell_pair(sent[h]), *matrix_t,
             )
             scales[h].append(scale)
             if last:

time: 107 us -> 106 us (level)
  starting transfers between devices: 25.5 us -> 24.4 us
    ppermute x14, starting transfers between devices: 11.5 us -> 10.4 us  [swap(): return lax.ppermute(x, 'snap', [(i, i ^ bits) for i in range(places)])]
    pallas_call x18 -> x20, Pallas kernels: 13.8 us -> 13 us  [call(): pl.pallas_call(kernel, out_shape=[jax.ShapeDtypeStruct(shape, dtype) for...]
  transfers between devices with their start and end apart: 25 -> 25, of which waited for: 20 -> 20; matrix products, arithmetic and copies ran while one was open for 1% -> 1% of each run, Pallas kernels for 12% -> 11%
where the time goes in v9:
time: 106 us
  waiting for transfers between devices  65.1 us (61%)
  starting transfers between devices  24.4 us (23%)
  Pallas kernels  13 us (12%)
  local copies, waits for them, and re-layouts  2.21 us (2%)
    ppermute x14, waiting for transfers between devices, swap(): return lax.ppermute(x, 'snap', [(i, i ^ bits) for i in range(places)])  49.8 us
    pallas_call x20, Pallas kernels, call(): pl.pallas_call(kernel, out_shape=[jax.ShapeDtypeStruct(shape, dtype) for...  13 us
    ppermute x8, waiting for transfers between devices, swap_cell(): return lax.ppermute(x, ('cell', 'snap'), perm)  13 us
    ppermute x8, starting transfers between devices, swap_cell(): return lax.ppermute(x, ('cell', 'snap'), perm)  10.5 us
    ppermute x14, starting transfers between devices, swap(): return lax.ppermute(x, 'snap', [(i, i ^ bits) for i in range(places)])  10.4 us
    ppermute x3, starting transfers between devices, local(): lax.ppermute(known, 'cell', [(c, c ^ d) for c in range(groups)])  3.55 us
    ppermute x3, waiting for transfers between devices, local(): lax.ppermute(known, 'cell', [(c, c ^ d) for c in range(groups)])  2.28 us
  transfers between devices with their start and end apart: 25, of which 20 were waited for; matrix products, arithmetic and copies ran while one was open for 1% of the time, Pallas kernels for 11%

profile of v9, /device:TPU:0, one launch (start us, length us, event | category | flops | bytes accessed | tf_op | source)
XLA Modules:
  0.0 105.6 jit_solution(10116139248501915751)
XLA Ops:
  0.6 0.5 collective-permute-start.1
  1.1 2.7 %collective-permute-start = (f32[1024,256]{1,0:T(8,128)}, f32[1024,256]{1,0:T(8,128)S(1)}, u32[]{:S(2)}, u32[]{:S(2)}) collective-permute-start(f32[1024,256]{1,0:T(8,128)} %own_ref.1), channel_id=1, source_target_pairs={{0,2},{1,3},{2,0},{3,1},{4,6},{5,7},{6,4},{7,5},{8,10},{9,11},{10,... | collective-permute-start | bytes 3145736 | tf_op jit(solution)/shard_map/ppermute | solution.py:343
  3.8 1.0 constant_dynamic-slice_fusion
  4.8 0.2 collective-permute-start.2
  5.0 1.2 %collective-permute-done.2.got_ref = f32[256,128]{1,0:T(8,128)S(1)} collective-permute-done((f32[256,128]{1,0:T(8,128)S(1)}, f32[256,128]{1,0:T(8,128)S(1)}, u32[]{:S(2)}, u32[]{:S(2)}) %collective-permute-start.2) | collective-permute-done | bytes 131104 | tf_op jit(solution)/shard_map/ppermute | solution.py:343
  6.2 0.2 shard_map.49
  6.4 0.4 collective-permute-start.4
  6.8 1.2 %copy-done = f32[1024,256]{1,0:T(8,128)S(1)} copy-done((f32[1024,256]{1,0:T(8,128)S(1)}, f32[1024,256]{1,0:T(8,128)}, u32[]{:S(2)}) %copy-start) | copy-done | bytes 1048600
  8.0 1.1 %shard_map.50 = (f32[512,128]{1,0:T(8,128)S(1)}, bf16[1024,512]{1,0:T(8,128)(2,1)S(1)}, bf16[1024,512]{1,0:T(8,128)(2,1)S(1)}, bf16[512,1024]{1,0:T(8,128)(2,1)S(1)}, bf16[512,1024]{1,0:T(8,128)(2,1)S(1)}) custom-call(f32[1024,256]{1,0:T(8,128)S(1)} %copy-done, f32[1024,256]{1,0:T(8,128)S(1)} %collective-permute-done.1.core_ref, ...), custom_call_target="tpu_custom_call" | custom-call | tf_op jit(solution)/shard_map/pallas_call | solution.py:296
  9.1 18.9 %collective-permute-done.side_ref = f32[1024,256]{1,0:T(8,128)S(1)} collective-permute-done((f32[1024,256]{1,0:T(8,128)}, f32[1024,256]{1,0:T(8,128)S(1)}, u32[]{:S(2)}, u32[]{:S(2)}) %collective-permute-start) | collective-permute-done | bytes 1048608 | tf_op jit(solution)/shard_map/ppermute | solution.py:343
  28.0 0.6 shard_map.51
  28.7 1.9 %collective-permute-done.4.sketch_ref = f32[256,128]{1,0:T(8,128)S(1)} collective-permute-done((f32[256,128]{1,0:T(8,128)S(1)}, f32[256,128]{1,0:T(8,128)S(1)}, u32[]{:S(2)}, u32[]{:S(2)}) %collective-permute-start.4) | collective-permute-done | bytes 131104 | tf_op jit(solution)/shard_map/ppermute | solution.py:343
  30.6 0.6 shard_map.52.near_ref
  31.1 0.7 shard_map.53
  31.8 2.8 %collective-permute-start.5 = (f32[256,128]{1,0:T(8,128)S(1)}, f32[256,128]{1,0:T(8,128)S(1)}, u32[]{:S(2)}, u32[]{:S(2)}) collective-permute-start(f32[256,128]{1,0:T(8,128)S(1)} %get-tuple-element.53.a_ref), channel_id=1, source_target_pairs={{0,4},{1,5},{2,6},{3,7},{4,0},{5,1},{6,2},{7,3},{8,12},{9,13},{10,... | collective-permute-start | bytes 393224 | tf_op jit(solution)/shard_map/ppermute | solution.py:343
  34.6 0.7 shard_map.55
  35.4 0.2 collective-permute-start.12
  35.6 9.2 %collective-permute-done.5.b_ref = f32[256,128]{1,0:T(8,128)S(1)} collective-permute-done((f32[256,128]{1,0:T(8,128)S(1)}, f32[256,128]{1,0:T(8,128)S(1)}, u32[]{:S(2)}, u32[]{:S(2)}) %collective-permute-start.5) | collective-permute-done | bytes 131104 | tf_op jit(solution)/shard_map/ppermute | solution.py:343
  44.8 0.8 shard_map.54
  45.6 1.7 %collective-permute-start.6 = (f32[264,128]{1,0:T(8,128)S(1)}, f32[264,128]{1,0:T(8,128)S(1)}, u32[]{:S(2)}, u32[]{:S(2)}) collective-permute-start(f32[264,128]{1,0:T(8,128)S(1)} %shard_map.54), channel_id=1, source_target_pairs={{0,8},{1,17},{2,10},{3,19},{4,12},{5,21},{6,14},{7,23},{8,0},{9,25... | collective-permute-start | bytes 405512 | tf_op jit(solution)/shard_map/ppermute | solution.py:354
  47.3 0.8 shard_map.59
  48.1 0.9 collective-permute-start.13
  49.0 1.8 %collective-permute-done.6 = f32[264,128]{1,0:T(8,128)S(1)} collective-permute-done((f32[264,128]{1,0:T(8,128)S(1)}, f32[264,128]{1,0:T(8,128)S(1)}, u32[]{:S(2)}, u32[]{:S(2)}) %collective-permute-start.6) | collective-permute-done | bytes 135200 | tf_op jit(solution)/shard_map/ppermute | solution.py:354
  50.8 2.2 %collective-permute-start.7 = (f32[264,128]{1,0:T(8,128)S(1)}, f32[264,128]{1,0:T(8,128)S(1)}, u32[]{:S(2)}, u32[]{:S(2)}) collective-permute-start(f32[264,128]{1,0:T(8,128)S(1)} %add.20.refs_0_), channel_id=1, source_target_pairs={{0,16},{1,9},{2,18},{3,11},{4,20},{5,13},{6,22},{7,15},{8,24},{9,1... | collective-permute-start | bytes 405512 | tf_op jit(solution)/shard_map/ppermute | solution.py:354
  53.1 0.5 collective-permute-done.13
  53.6 2.1 %collective-permute-start.14 = (f32[264,128]{1,0:T(8,128)S(1)}, f32[264,128]{1,0:T(8,128)S(1)}, u32[]{:S(2)}, u32[]{:S(2)}) collective-permute-start(f32[264,128]{1,0:T(8,128)S(1)} %add.22.refs_0_), channel_id=1, source_target_pairs={{0,16},{1,9},{2,18},{3,11},{4,20},{5,13},{6,22},{7,15},{8,24},{9,1... | collective-permute-start | bytes 405512 | tf_op jit(solution)/shard_map/ppermute | solution.py:354
  55.7 0.4 collective-permute-done.7.refs_1_
  56.1 0.9 shard_map.56
  57.0 0.1 collective-permute-start.8
  57.0 1.6 %collective-permute-done.14.refs_1_ = f32[264,128]{1,0:T(8,128)S(1)} collective-permute-done((f32[264,128]{1,0:T(8,128)S(1)}, f32[264,128]{1,0:T(8,128)S(1)}, u32[]{:S(2)}, u32[]{:S(2)}) %collective-permute-start.14) | collective-permute-done | bytes 135200 | tf_op jit(solution)/shard_map/ppermute | solution.py:354
  58.7 0.9 shard_map.60
  59.6 1.3 %collective-permute-start.15 = (f32[264,128]{1,0:T(8,128)S(1)}, f32[264,128]{1,0:T(8,128)S(1)}, u32[]{:S(2)}, u32[]{:S(2)}) collective-permute-start(f32[264,128]{1,0:T(8,128)S(1)} %get-tuple-element.69.refs_0_), channel_id=1, source_target_pairs={{0,4},{1,5},{2,6},{3,7},{4,0},{5,1},{6,2},{7,3},{8,12},{9,13},{10,... | collective-permute-start | bytes 405512 | tf_op jit(solution)/shard_map/ppermute | solution.py:343
  60.9 7.1 %collective-permute-done.8.refs_1_ = f32[264,128]{1,0:T(8,128)S(1)} collective-permute-done((f32[264,128]{1,0:T(8,128)S(1)}, f32[264,128]{1,0:T(8,128)S(1)}, u32[]{:S(2)}, u32[]{:S(2)}) %collective-permute-start.8) | collective-permute-done | bytes 135200 | tf_op jit(solution)/shard_map/ppermute | solution.py:343
  68.0 0.9 shard_map.57
  68.9 1.5 %collective-permute-start.9 = (f32[264,128]{1,0:T(8,128)S(1)}, f32[264,128]{1,0:T(8,128)S(1)}, u32[]{:S(2)}, u32[]{:S(2)}) collective-permute-start(f32[264,128]{1,0:T(8,128)S(1)} %get-tuple-element.65), channel_id=1, source_target_pairs={{0,8},{1,17},{2,10},{3,19},{4,12},{5,21},{6,14},{7,23},{8,0},{9,25... | collective-permute-start | bytes 405512 | tf_op jit(solution)/shard_map/ppermute | solution.py:354
  70.5 0.9 shard_map.61
  71.4 0.5 collective-permute-start.16
  71.9 3.2 %collective-permute-done.9 = f32[264,128]{1,0:T(8,128)S(1)} collective-permute-done((f32[264,128]{1,0:T(8,128)S(1)}, f32[264,128]{1,0:T(8,128)S(1)}, u32[]{:S(2)}, u32[]{:S(2)}) %collective-permute-start.9) | collective-permute-done | bytes 135200 | tf_op jit(solution)/shard_map/ppermute | solution.py:354
  75.1 1.0 collective-permute-start.10
  76.2 1.9 %collective-permute-done.16 = f32[264,128]{1,0:T(8,128)S(1)} collective-permute-done((f32[264,128]{1,0:T(8,128)S(1)}, f32[264,128]{1,0:T(8,128)S(1)}, u32[]{:S(2)}, u32[]{:S(2)}) %collective-permute-start.16) | collective-permute-done | bytes 135200 | tf_op jit(solution)/shard_map/ppermute | solution.py:354
  78.0 0.5 collective-permute-start.17
  78.6 1.6 %collective-permute-done.10.refs_1_ = f32[264,128]{1,0:T(8,128)S(1)} collective-permute-done((f32[264,128]{1,0:T(8,128)S(1)}, f32[264,128]{1,0:T(8,128)S(1)}, u32[]{:S(2)}, u32[]{:S(2)}) %collective-permute-start.10) | collective-permute-done | bytes 135200 | tf_op jit(solution)/shard_map/ppermute | solution.py:354
  80.2 0.9 shard_map.58
  81.2 1.9 %collective-permute-done.17.refs_1_ = f32[264,128]{1,0:T(8,128)S(1)} collective-permute-done((f32[264,128]{1,0:T(8,128)S(1)}, f32[264,128]{1,0:T(8,128)S(1)}, u32[]{:S(2)}, u32[]{:S(2)}) %collective-permute-start.17) | collective-permute-done | bytes 135200 | tf_op jit(solution)/shard_map/ppermute | solution.py:354
  83.1 0.9 shard_map.62
  84.0 1.0 collective-permute-start.18
  85.1 5.4 %collective-permute-done.11.got_ref = f32[264,128]{1,0:T(8,128)S(1)} collective-permute-done((f32[264,128]{1,0:T(8,128)S(1)}, f32[264,128]{1,0:T(8,128)S(1)}, u32[]{:S(2)}, u32[]{:S(2)}) %collective-permute-start.11) | collective-permute-done | bytes 135200 | tf_op jit(solution)/shard_map/ppermute | solution.py:343
  90.5 0.2 shard_map.63
  90.7 0.1 collective-permute-start.19
  90.8 1.2 %collective-permute-done.18.got_ref = f32[264,128]{1,0:T(8,128)S(1)} collective-permute-done((f32[264,128]{1,0:T(8,128)S(1)}, f32[264,128]{1,0:T(8,128)S(1)}, u32[]{:S(2)}, u32[]{:S(2)}) %collective-permute-start.18) | collective-permute-done | bytes 135200 | tf_op jit(solution)/shard_map/ppermute | solution.py:343
  92.0 0.2 shard_map.64
  92.2 0.9 collective-permute-start.20
  93.1 3.5 %collective-permute-done.20.refs_3_ = f32[72,128]{1,0:T(8,128)S(1)} collective-permute-done((f32[72,128]{1,0:T(8,128)S(1)}, f32[72,128]{1,0:T(8,128)S(1)}, u32[]{:S(2)}, u32[]{:S(2)}) %collective-permute-start.20) | collective-permute-done | bytes 36896 | tf_op jit(solution)/shard_map/ppermute | solution.py:343
  96.5 0.1 shard_map.65
  96.6 1.4 %collective-permute-done.21.got_ref.refs_3_ = f32[392,128]{1,0:T(8,128)S(1)} collective-permute-done((f32[392,128]{1,0:T(8,128)S(1)}, f32[392,128]{1,0:T(8,128)S(1)}, u32[]{:S(2)}, u32[]{:S(2)}) %collective-permute-start.21) | collective-permute-done | bytes 200736 | tf_op jit(solution)/shard_map/ppermute | solution.py:343
  98.1 0.1 shard_map.66
  98.2 2.1 %collective-permute-start.24 = (f32[8,256]{1,0:T(8,128)S(1)}, f32[8,256]{1,0:T(8,128)S(1)}, u32[]{:S(2)}, u32[]{:S(2)}) collective-permute-start(f32[8,256]{1,0:T(8,128)S(1)} %get-tuple-element.86.known_ref.refs_4_), channel_id=1, source_target_pairs={{0,24},{8,16},{16,8},{24,0},{1,25},{9,17},{17,9},{25,1},{2,26},{10... | collective-permute-start | bytes 24584 | tf_op jit(solution)/shard_map/ppermute | solution.py:435
  100.3 0.9 collective-permute-start.23
  101.2 0.5 collective-permute-start.22
  101.7 0.8 shard_map.68
  102.6 0.2 collective-permute-done.24.refs_2_
  102.8 1.2 %collective-permute-done.23.refs_1_ = f32[8,256]{1,0:T(8,128)S(1)} collective-permute-done((f32[8,256]{1,0:T(8,128)S(1)}, f32[8,256]{1,0:T(8,128)S(1)}, u32[]{:S(2)}, u32[]{:S(2)}) %collective-permute-start.23) | collective-permute-done | bytes 8224 | tf_op jit(solution)/shard_map/ppermute | solution.py:435
  104.0 0.9 collective-permute-done.22.refs_0_
  104.9 0.7 shard_map.67
  (13 shorter events, 0.2 us)
Async XLA Ops:
  0.6 6.2 %collective-permute-start.1 = (f32[1024,256]{1,0:T(8,128)}, f32[1024,256]{1,0:T(8,128)S(1)}, u32[]{:S(2)}, u32[]{:S(2)}) collective-permute-start(f32[1024,256]{1,0:T(8,128)} %own_ref.1), channel_id=1, source_target_pairs={{0,1},{1,0},{2,3},{3,2},{4,5},{5,4},{6,7},{7,6},{8,9},{9,8},{10,11... | collective-permute-start | bytes 3145736 | tf_op jit(solution)/shard_map/ppermute | solution.py:343
  1.1 26.9 %collective-permute-start = (f32[1024,256]{1,0:T(8,128)}, f32[1024,256]{1,0:T(8,128)S(1)}, u32[]{:S(2)}, u32[]{:S(2)}) collective-permute-start(f32[1024,256]{1,0:T(8,128)} %own_ref.1), channel_id=1, source_target_pairs={{0,2},{1,3},{2,0},{3,1},{4,6},{5,7},{6,4},{7,5},{8,10},{9,11},{10,... | collective-permute-start | bytes 3145736 | tf_op jit(solution)/shard_map/ppermute | solution.py:343
  4.8 1.4 %collective-permute-start.2 = (f32[256,128]{1,0:T(8,128)S(1)}, f32[256,128]{1,0:T(8,128)S(1)}, u32[]{:S(2)}, u32[]{:S(2)}) collective-permute-start(f32[256,128]{1,0:T(8,128)S(1)} %get-tuple-element.89), channel_id=1, source_target_pairs={{0,1},{1,0},{2,3},{3,2},{4,5},{5,4},{6,7},{7,6},{8,9},{9,8},{10,11... | collective-permute-start | bytes 393224 | tf_op jit(solution)/shard_map/ppermute | solution.py:343
  6.4 24.2 %collective-permute-start.4 = (f32[256,128]{1,0:T(8,128)S(1)}, f32[256,128]{1,0:T(8,128)S(1)}, u32[]{:S(2)}, u32[]{:S(2)}) collective-permute-start(f32[256,128]{1,0:T(8,128)S(1)} %get-tuple-element.49), channel_id=1, source_target_pairs={{0,2},{1,3},{2,0},{3,1},{4,6},{5,7},{6,4},{7,5},{8,10},{9,11},{10,... | collective-permute-start | bytes 393224 | tf_op jit(solution)/shard_map/ppermute | solution.py:343
  6.8 1.2 %copy-start = (f32[1024,256]{1,0:T(8,128)S(1)}, f32[1024,256]{1,0:T(8,128)}, u32[]{:S(2)}) copy-start(f32[1024,256]{1,0:T(8,128)} %own_ref.1) | copy-start | bytes 3145732
  28.0 3.1 %collective-permute-start.3 = (f32[1024,256]{1,0:T(8,128)S(1)}, f32[1024,256]{1,0:T(8,128)S(1)}, u32[]{:S(2)}, u32[]{:S(2)}) collective-permute-start(f32[1024,256]{1,0:T(8,128)S(1)} %collective-permute-done.side_ref), channel_id=1, source_target_pairs={{0,1},{1,0},{2,3},{3,2},{4,5},{5,4},{6,7},{7,6},{8,9},{9,8},{10,11... | collective-permute-start | bytes 3145736 | tf_op jit(solution)/shard_map/ppermute | solution.py:343
  31.8 12.9 %collective-permute-start.5 = (f32[256,128]{1,0:T(8,128)S(1)}, f32[256,128]{1,0:T(8,128)S(1)}, u32[]{:S(2)}, u32[]{:S(2)}) collective-permute-start(f32[256,128]{1,0:T(8,128)S(1)} %get-tuple-element.53.a_ref), channel_id=1, source_target_pairs={{0,4},{1,5},{2,6},{3,7},{4,0},{5,1},{6,2},{7,3},{8,12},{9,13},{10,... | collective-permute-start | bytes 393224 | tf_op jit(solution)/shard_map/ppermute | solution.py:343
  35.4 11.9 %collective-permute-start.12 = (f32[256,128]{1,0:T(8,128)S(1)}, f32[256,128]{1,0:T(8,128)S(1)}, u32[]{:S(2)}, u32[]{:S(2)}) collective-permute-start(f32[256,128]{1,0:T(8,128)S(1)} %get-tuple-element.68.a_ref), channel_id=1, source_target_pairs={{0,4},{1,5},{2,6},{3,7},{4,0},{5,1},{6,2},{7,3},{8,12},{9,13},{10,... | collective-permute-start | bytes 393224 | tf_op jit(solution)/shard_map/ppermute | solution.py:343
  45.6 5.2 %collective-permute-start.6 = (f32[264,128]{1,0:T(8,128)S(1)}, f32[264,128]{1,0:T(8,128)S(1)}, u32[]{:S(2)}, u32[]{:S(2)}) collective-permute-start(f32[264,128]{1,0:T(8,128)S(1)} %shard_map.54), channel_id=1, source_target_pairs={{0,8},{1,17},{2,10},{3,19},{4,12},{5,21},{6,14},{7,23},{8,0},{9,25... | collective-permute-start | bytes 405512 | tf_op jit(solution)/shard_map/ppermute | solution.py:354
  48.1 5.5 %collective-permute-start.13 = (f32[264,128]{1,0:T(8,128)S(1)}, f32[264,128]{1,0:T(8,128)S(1)}, u32[]{:S(2)}, u32[]{:S(2)}) collective-permute-start(f32[264,128]{1,0:T(8,128)S(1)} %shard_map.59), channel_id=1, source_target_pairs={{0,8},{1,17},{2,10},{3,19},{4,12},{5,21},{6,14},{7,23},{8,0},{9,25... | collective-permute-start | bytes 405512 | tf_op jit(solution)/shard_map/ppermute | solution.py:354
  50.8 5.2 %collective-permute-start.7 = (f32[264,128]{1,0:T(8,128)S(1)}, f32[264,128]{1,0:T(8,128)S(1)}, u32[]{:S(2)}, u32[]{:S(2)}) collective-permute-start(f32[264,128]{1,0:T(8,128)S(1)} %add.20.refs_0_), channel_id=1, source_target_pairs={{0,16},{1,9},{2,18},{3,11},{4,20},{5,13},{6,22},{7,15},{8,24},{9,1... | collective-permute-start | bytes 405512 | tf_op jit(solution)/shard_map/ppermute | solution.py:354
  53.6 5.1 %collective-permute-start.14 = (f32[264,128]{1,0:T(8,128)S(1)}, f32[264,128]{1,0:T(8,128)S(1)}, u32[]{:S(2)}, u32[]{:S(2)}) collective-permute-start(f32[264,128]{1,0:T(8,128)S(1)} %add.22.refs_0_), channel_id=1, source_target_pairs={{0,16},{1,9},{2,18},{3,11},{4,20},{5,13},{6,22},{7,15},{8,24},{9,1... | collective-permute-start | bytes 405512 | tf_op jit(solution)/shard_map/ppermute | solution.py:354
  57.0 11.1 %collective-permute-start.8 = (f32[264,128]{1,0:T(8,128)S(1)}, f32[264,128]{1,0:T(8,128)S(1)}, u32[]{:S(2)}, u32[]{:S(2)}) collective-permute-start(f32[264,128]{1,0:T(8,128)S(1)} %get-tuple-element.64.refs_0_), channel_id=1, source_target_pairs={{0,4},{1,5},{2,6},{3,7},{4,0},{5,1},{6,2},{7,3},{8,12},{9,13},{10,... | collective-permute-start | bytes 405512 | tf_op jit(solution)/shard_map/ppermute | solution.py:343
  59.6 10.9 %collective-permute-start.15 = (f32[264,128]{1,0:T(8,128)S(1)}, f32[264,128]{1,0:T(8,128)S(1)}, u32[]{:S(2)}, u32[]{:S(2)}) collective-permute-start(f32[264,128]{1,0:T(8,128)S(1)} %get-tuple-element.69.refs_0_), channel_id=1, source_target_pairs={{0,4},{1,5},{2,6},{3,7},{4,0},{5,1},{6,2},{7,3},{8,12},{9,13},{10,... | collective-permute-start | bytes 405512 | tf_op jit(solution)/shard_map/ppermute | solution.py:343
  68.9 6.2 %collective-permute-start.9 = (f32[264,128]{1,0:T(8,128)S(1)}, f32[264,128]{1,0:T(8,128)S(1)}, u32[]{:S(2)}, u32[]{:S(2)}) collective-permute-start(f32[264,128]{1,0:T(8,128)S(1)} %get-tuple-element.65), channel_id=1, source_target_pairs={{0,8},{1,17},{2,10},{3,19},{4,12},{5,21},{6,14},{7,23},{8,0},{9,25... | collective-permute-start | bytes 405512 | tf_op jit(solution)/shard_map/ppermute | solution.py:354
  71.4 6.7 %collective-permute-start.16 = (f32[264,128]{1,0:T(8,128)S(1)}, f32[264,128]{1,0:T(8,128)S(1)}, u32[]{:S(2)}, u32[]{:S(2)}) collective-permute-start(f32[264,128]{1,0:T(8,128)S(1)} %get-tuple-element.70), channel_id=1, source_target_pairs={{0,8},{1,17},{2,10},{3,19},{4,12},{5,21},{6,14},{7,23},{8,0},{9,25... | collective-permute-start | bytes 405512 | tf_op jit(solution)/shard_map/ppermute | solution.py:354
  75.1 5.1 %collective-permute-start.10 = (f32[264,128]{1,0:T(8,128)S(1)}, f32[264,128]{1,0:T(8,128)S(1)}, u32[]{:S(2)}, u32[]{:S(2)}) collective-permute-start(f32[264,128]{1,0:T(8,128)S(1)} %add.21.refs_0_), channel_id=1, source_target_pairs={{0,16},{1,9},{2,18},{3,11},{4,20},{5,13},{6,22},{7,15},{8,24},{9,1... | collective-permute-start | bytes 405512 | tf_op jit(solution)/shard_map/ppermute | solution.py:354
  78.0 5.1 %collective-permute-start.17 = (f32[264,128]{1,0:T(8,128)S(1)}, f32[264,128]{1,0:T(8,128)S(1)}, u32[]{:S(2)}, u32[]{:S(2)}) collective-permute-start(f32[264,128]{1,0:T(8,128)S(1)} %add.23.refs_0_), channel_id=1, source_target_pairs={{0,16},{1,9},{2,18},{3,11},{4,20},{5,13},{6,22},{7,15},{8,24},{9,1... | collective-permute-start | bytes 405512 | tf_op jit(solution)/shard_map/ppermute | solution.py:354
  81.1 9.4 %collective-permute-start.11 = (f32[264,128]{1,0:T(8,128)S(1)}, f32[264,128]{1,0:T(8,128)S(1)}, u32[]{:S(2)}, u32[]{:S(2)}) collective-permute-start(f32[264,128]{1,0:T(8,128)S(1)} %get-tuple-element.66.own_ref), channel_id=1, source_target_pairs={{0,4},{1,5},{2,6},{3,7},{4,0},{5,1},{6,2},{7,3},{8,12},{9,13},{10,... | collective-permute-start | bytes 405512 | tf_op jit(solution)/shard_map/ppermute | solution.py:343
  84.0 7.9 %collective-permute-start.18 = (f32[264,128]{1,0:T(8,128)S(1)}, f32[264,128]{1,0:T(8,128)S(1)}, u32[]{:S(2)}, u32[]{:S(2)}) collective-permute-start(f32[264,128]{1,0:T(8,128)S(1)} %get-tuple-element.76.own_ref), channel_id=1, source_target_pairs={{0,4},{1,5},{2,6},{3,7},{4,0},{5,1},{6,2},{7,3},{8,12},{9,13},{10,... | collective-permute-start | bytes 405512 | tf_op jit(solution)/shard_map/ppermute | solution.py:343
  90.7 5.8 %collective-permute-start.19 = (f32[328,128]{1,0:T(8,128)S(1)}, f32[328,128]{1,0:T(8,128)S(1)}, u32[]{:S(2)}, u32[]{:S(2)}) collective-permute-start(f32[328,128]{1,0:T(8,128)S(1)} %get-tuple-element.81), channel_id=1, source_target_pairs={{0,2},{1,3},{2,0},{3,1},{4,6},{5,7},{6,4},{7,5},{8,10},{9,11},{10,... | collective-permute-start | bytes 503816 | tf_op jit(solution)/shard_map/ppermute | solution.py:343
  92.2 4.4 %collective-permute-start.20 = (f32[72,128]{1,0:T(8,128)S(1)}, f32[72,128]{1,0:T(8,128)S(1)}, u32[]{:S(2)}, u32[]{:S(2)}) collective-permute-start(f32[72,128]{1,0:T(8,128)S(1)} %get-tuple-element.82), channel_id=1, source_target_pairs={{0,2},{1,3},{2,0},{3,1},{4,6},{5,7},{6,4},{7,5},{8,10},{9,11},{10,... | collective-permute-start | bytes 110600 | tf_op jit(solution)/shard_map/ppermute | solution.py:343
  96.6 1.5 %collective-permute-start.21 = (f32[392,128]{1,0:T(8,128)S(1)}, f32[392,128]{1,0:T(8,128)S(1)}, u32[]{:S(2)}, u32[]{:S(2)}) collective-permute-start(f32[392,128]{1,0:T(8,128)S(1)} %get-tuple-element.84), channel_id=1, source_target_pairs={{0,1},{1,0},{2,3},{3,2},{4,5},{5,4},{6,7},{7,6},{8,9},{9,8},{10,11... | collective-permute-start | bytes 602120 | tf_op jit(solution)/shard_map/ppermute | solution.py:343
  98.2 4.6 %collective-permute-start.24 = (f32[8,256]{1,0:T(8,128)S(1)}, f32[8,256]{1,0:T(8,128)S(1)}, u32[]{:S(2)}, u32[]{:S(2)}) collective-permute-start(f32[8,256]{1,0:T(8,128)S(1)} %get-tuple-element.86.known_ref.refs_4_), channel_id=1, source_target_pairs={{0,24},{8,16},{16,8},{24,0},{1,25},{9,17},{17,9},{25,1},{2,26},{10... | collective-permute-start | bytes 24584 | tf_op jit(solution)/shard_map/ppermute | solution.py:435
  100.3 3.7 %collective-permute-start.23 = (f32[8,256]{1,0:T(8,128)S(1)}, f32[8,256]{1,0:T(8,128)S(1)}, u32[]{:S(2)}, u32[]{:S(2)}) collective-permute-start(f32[8,256]{1,0:T(8,128)S(1)} %get-tuple-element.86.known_ref.refs_4_), channel_id=1, source_target_pairs={{0,16},{8,24},{16,0},{24,8},{1,17},{9,25},{17,1},{25,9},{2,18},{10... | collective-permute-start | bytes 24584 | tf_op jit(solution)/shard_map/ppermute | solution.py:435
  101.2 3.7 %collective-permute-start.22 = (f32[8,256]{1,0:T(8,128)S(1)}, f32[8,256]{1,0:T(8,128)S(1)}, u32[]{:S(2)}, u32[]{:S(2)}) collective-permute-start(f32[8,256]{1,0:T(8,128)S(1)} %get-tuple-element.86.known_ref.refs_4_), channel_id=1, source_target_pairs={{0,8},{8,0},{16,24},{24,16},{1,9},{9,1},{17,25},{25,17},{2,10},{10... | collective-permute-start | bytes 24584 | tf_op jit(solution)/shard_map/ppermute | solution.py:435

commit v10 on v9

--- a/solution.py
+++ b/solution.py
@@ -22,7 +22,8 @@
 def position():
     seat = lax.axis_index("snap")
     core, chip = lax.rem(seat, 2), lax.div(seat, 2)
-    return core, lax.rem(chip, 2), chip
+    inner = jnp.logical_or(chip == 1, chip == 2)
+    return core, inner.astype(jnp.int32), chip
 
 
 def split(x):
@@ -344,7 +345,7 @@
 
     swap_core = functools.partial(swap, bits=1)
     swap_side = functools.partial(swap, bits=2)
-    swap_pair = functools.partial(swap, bits=4)
+    swap_pair = functools.partial(swap, bits=6)
 
     def swap_cell(x, step):
         def target(cell, i):

time: 106 us -> 99.3 us (0.937)
  waiting for transfers between devices: 65.1 us -> 45 us
  starting transfers between devices: 24.4 us -> 38.1 us
    ppermute x14, waiting for transfers between devices: 49.8 us -> 35.7 us  [swap(): return lax.ppermute(x, 'snap', [(i, i ^ bits) for i in range(places)])]
    ppermute x14, starting transfers between devices: 10.4 us -> 22.9 us  [swap(): return lax.ppermute(x, 'snap', [(i, i ^ bits) for i in range(places)])]
    ppermute x8, waiting for transfers between devices: 13 us -> 6.56 us  [swap_cell(): return lax.ppermute(x, ('cell', 'snap'), perm)]
  transfers between devices with their start and end apart: 25 -> 25, of which waited for: 20 -> 18; matrix products, arithmetic and copies ran while one was open for 1% -> 1% of each run, Pallas kernels for 11% -> 12%
where the time goes in v10:
time: 99.3 us; the launch traced here: 99.1 us
  waiting for transfers between devices  45 us (45%)
  starting transfers between devices  38.1 us (38%)
  Pallas kernels  13 us (13%)
  local copies, waits for them, and re-layouts  2.21 us (2%)
    ppermute x14, waiting for transfers between devices, swap(): return lax.ppermute(x, 'snap', [(i, i ^ bits) for i in range(places)])  35.7 us
    ppermute x14, starting transfers between devices, swap(): return lax.ppermute(x, 'snap', [(i, i ^ bits) for i in range(places)])  22.9 us
    pallas_call x20, Pallas kernels, call(): pl.pallas_call(kernel, out_shape=[jax.ShapeDtypeStruct(shape, dtype) for...  13 us
    ppermute x8, starting transfers between devices, swap_cell(): return lax.ppermute(x, ('cell', 'snap'), perm)  11.3 us
    ppermute x8, waiting for transfers between devices, swap_cell(): return lax.ppermute(x, ('cell', 'snap'), perm)  6.56 us
    ppermute x3, starting transfers between devices, local(): lax.ppermute(known, 'cell', [(c, c ^ d) for c in range(groups)])  3.79 us
    ppermute x3, waiting for transfers between devices, local(): lax.ppermute(known, 'cell', [(c, c ^ d) for c in range(groups)])  2.79 us
  transfers between devices with their start and end apart: 25, of which 18 were waited for; matrix products, arithmetic and copies ran while one was open for 1% of the time, Pallas kernels for 12%

profile of v10, /device:TPU:0, one launch (start us, length us, event | category | flops | bytes accessed | tf_op | source)
XLA Modules:
  0.0 99.1 jit_solution(4214696025106567046)
XLA Ops:
  0.6 0.5 collective-permute-start.1
  1.1 2.7 %collective-permute-start = (f32[1024,256]{1,0:T(8,128)}, f32[1024,256]{1,0:T(8,128)S(1)}, u32[]{:S(2)}, u32[]{:S(2)}) collective-permute-start(f32[1024,256]{1,0:T(8,128)} %own_ref.1), channel_id=1, source_target_pairs={{0,2},{1,3},{2,0},{3,1},{4,6},{5,7},{6,4},{7,5},{8,10},{9,11},{10,... | collective-permute-start | bytes 3145736 | tf_op jit(solution)/shard_map/ppermute | solution.py:344
  3.8 1.0 constant_dynamic-slice_fusion
  4.8 0.2 collective-permute-start.2
  5.0 1.2 %collective-permute-done.2.got_ref = f32[256,128]{1,0:T(8,128)S(1)} collective-permute-done((f32[256,128]{1,0:T(8,128)S(1)}, f32[256,128]{1,0:T(8,128)S(1)}, u32[]{:S(2)}, u32[]{:S(2)}) %collective-permute-start.2) | collective-permute-done | bytes 131104 | tf_op jit(solution)/shard_map/ppermute | solution.py:344
  6.2 0.2 shard_map.49
  6.4 0.4 collective-permute-start.4
  6.8 1.2 %copy-done = f32[1024,256]{1,0:T(8,128)S(1)} copy-done((f32[1024,256]{1,0:T(8,128)S(1)}, f32[1024,256]{1,0:T(8,128)}, u32[]{:S(2)}) %copy-start) | copy-done | bytes 1048600
  8.0 1.1 %shard_map.50 = (f32[512,128]{1,0:T(8,128)S(1)}, bf16[1024,512]{1,0:T(8,128)(2,1)S(1)}, bf16[1024,512]{1,0:T(8,128)(2,1)S(1)}, bf16[512,1024]{1,0:T(8,128)(2,1)S(1)}, bf16[512,1024]{1,0:T(8,128)(2,1)S(1)}) custom-call(f32[1024,256]{1,0:T(8,128)S(1)} %copy-done, f32[1024,256]{1,0:T(8,128)S(1)} %collective-permute-done.1.core_ref, ...), custom_call_target="tpu_custom_call" | custom-call | tf_op jit(solution)/shard_map/pallas_call | solution.py:297
  9.1 18.9 %collective-permute-done.side_ref = f32[1024,256]{1,0:T(8,128)S(1)} collective-permute-done((f32[1024,256]{1,0:T(8,128)}, f32[1024,256]{1,0:T(8,128)S(1)}, u32[]{:S(2)}, u32[]{:S(2)}) %collective-permute-start) | collective-permute-done | bytes 1048608 | tf_op jit(solution)/shard_map/ppermute | solution.py:344
  28.0 0.6 shard_map.51
  28.7 1.9 %collective-permute-done.4.sketch_ref = f32[256,128]{1,0:T(8,128)S(1)} collective-permute-done((f32[256,128]{1,0:T(8,128)S(1)}, f32[256,128]{1,0:T(8,128)S(1)}, u32[]{:S(2)}, u32[]{:S(2)}) %collective-permute-start.4) | collective-permute-done | bytes 131104 | tf_op jit(solution)/shard_map/ppermute | solution.py:344
  30.6 0.6 shard_map.52.near_ref
  31.1 0.7 shard_map.53
  31.8 3.8 %collective-permute-start.5 = (f32[256,128]{1,0:T(8,128)S(1)}, f32[256,128]{1,0:T(8,128)S(1)}, u32[]{:S(2)}, u32[]{:S(2)}) collective-permute-start(f32[256,128]{1,0:T(8,128)S(1)} %get-tuple-element.53.a_ref), channel_id=1, source_target_pairs={{0,6},{1,7},{2,4},{3,5},{4,2},{5,3},{6,0},{7,1},{8,14},{9,15},{10,... | collective-permute-start | bytes 393224 | tf_op jit(solution)/shard_map/ppermute | solution.py:344
  35.7 0.7 shard_map.55
  36.4 0.1 collective-permute-start.12
  36.5 3.1 %collective-permute-done.5.b_ref = f32[256,128]{1,0:T(8,128)S(1)} collective-permute-done((f32[256,128]{1,0:T(8,128)S(1)}, f32[256,128]{1,0:T(8,128)S(1)}, u32[]{:S(2)}, u32[]{:S(2)}) %collective-permute-start.5) | collective-permute-done | bytes 131104 | tf_op jit(solution)/shard_map/ppermute | solution.py:344
  39.6 0.8 shard_map.54
  40.4 1.5 %collective-permute-start.6 = (f32[264,128]{1,0:T(8,128)S(1)}, f32[264,128]{1,0:T(8,128)S(1)}, u32[]{:S(2)}, u32[]{:S(2)}) collective-permute-start(f32[264,128]{1,0:T(8,128)S(1)} %shard_map.54), channel_id=1, source_target_pairs={{0,8},{1,17},{2,10},{3,19},{4,12},{5,21},{6,14},{7,23},{8,0},{9,25... | collective-permute-start | bytes 405512 | tf_op jit(solution)/shard_map/ppermute | solution.py:355
  41.9 1.4 %collective-permute-done.12.b_ref = f32[256,128]{1,0:T(8,128)S(1)} collective-permute-done((f32[256,128]{1,0:T(8,128)S(1)}, f32[256,128]{1,0:T(8,128)S(1)}, u32[]{:S(2)}, u32[]{:S(2)}) %collective-permute-start.12) | collective-permute-done | bytes 131104 | tf_op jit(solution)/shard_map/ppermute | solution.py:344
  43.3 0.8 shard_map.59
  44.1 1.5 %collective-permute-start.13 = (f32[264,128]{1,0:T(8,128)S(1)}, f32[264,128]{1,0:T(8,128)S(1)}, u32[]{:S(2)}, u32[]{:S(2)}) collective-permute-start(f32[264,128]{1,0:T(8,128)S(1)} %shard_map.59), channel_id=1, source_target_pairs={{0,8},{1,17},{2,10},{3,19},{4,12},{5,21},{6,14},{7,23},{8,0},{9,25... | collective-permute-start | bytes 405512 | tf_op jit(solution)/shard_map/ppermute | solution.py:355
  45.7 1.6 %collective-permute-start.7 = (f32[264,128]{1,0:T(8,128)S(1)}, f32[264,128]{1,0:T(8,128)S(1)}, u32[]{:S(2)}, u32[]{:S(2)}) collective-permute-start(f32[264,128]{1,0:T(8,128)S(1)} %add.20.refs_0_), channel_id=1, source_target_pairs={{0,16},{1,9},{2,18},{3,11},{4,20},{5,13},{6,22},{7,15},{8,24},{9,1... | collective-permute-start | bytes 405512 | tf_op jit(solution)/shard_map/ppermute | solution.py:355
  47.3 2.3 %collective-permute-done.13 = f32[264,128]{1,0:T(8,128)S(1)} collective-permute-done((f32[264,128]{1,0:T(8,128)S(1)}, f32[264,128]{1,0:T(8,128)S(1)}, u32[]{:S(2)}, u32[]{:S(2)}) %collective-permute-start.13) | collective-permute-done | bytes 135200 | tf_op jit(solution)/shard_map/ppermute | solution.py:355
  49.6 1.1 %collective-permute-start.14 = (f32[264,128]{1,0:T(8,128)S(1)}, f32[264,128]{1,0:T(8,128)S(1)}, u32[]{:S(2)}, u32[]{:S(2)}) collective-permute-start(f32[264,128]{1,0:T(8,128)S(1)} %add.22.refs_0_), channel_id=1, source_target_pairs={{0,16},{1,9},{2,18},{3,11},{4,20},{5,13},{6,22},{7,15},{8,24},{9,1... | collective-permute-start | bytes 405512 | tf_op jit(solution)/shard_map/ppermute | solution.py:355
  50.8 0.9 shard_map.56
  51.7 4.5 %collective-permute-start.8 = (f32[264,128]{1,0:T(8,128)S(1)}, f32[264,128]{1,0:T(8,128)S(1)}, u32[]{:S(2)}, u32[]{:S(2)}) collective-permute-start(f32[264,128]{1,0:T(8,128)S(1)} %get-tuple-element.64.refs_0_), channel_id=1, source_target_pairs={{0,6},{1,7},{2,4},{3,5},{4,2},{5,3},{6,0},{7,1},{8,14},{9,15},{10,... | collective-permute-start | bytes 405512 | tf_op jit(solution)/shard_map/ppermute | solution.py:344
  56.2 0.9 shard_map.60
  57.1 1.9 %collective-permute-start.15 = (f32[264,128]{1,0:T(8,128)S(1)}, f32[264,128]{1,0:T(8,128)S(1)}, u32[]{:S(2)}, u32[]{:S(2)}) collective-permute-start(f32[264,128]{1,0:T(8,128)S(1)} %get-tuple-element.69.refs_0_), channel_id=1, source_target_pairs={{0,6},{1,7},{2,4},{3,5},{4,2},{5,3},{6,0},{7,1},{8,14},{9,15},{10,... | collective-permute-start | bytes 405512 | tf_op jit(solution)/shard_map/ppermute | solution.py:344
  59.0 1.6 %collective-permute-done.8.refs_1_ = f32[264,128]{1,0:T(8,128)S(1)} collective-permute-done((f32[264,128]{1,0:T(8,128)S(1)}, f32[264,128]{1,0:T(8,128)S(1)}, u32[]{:S(2)}, u32[]{:S(2)}) %collective-permute-start.8) | collective-permute-done | bytes 135200 | tf_op jit(solution)/shard_map/ppermute | solution.py:344
  60.6 0.9 shard_map.57
  61.5 1.0 collective-permute-start.9
  62.5 1.6 %collective-permute-done.15.refs_1_ = f32[264,128]{1,0:T(8,128)S(1)} collective-permute-done((f32[264,128]{1,0:T(8,128)S(1)}, f32[264,128]{1,0:T(8,128)S(1)}, u32[]{:S(2)}, u32[]{:S(2)}) %collective-permute-start.15) | collective-permute-done | bytes 135200 | tf_op jit(solution)/shard_map/ppermute | solution.py:344
  64.1 0.9 shard_map.61
  65.0 1.5 %collective-permute-start.16 = (f32[264,128]{1,0:T(8,128)S(1)}, f32[264,128]{1,0:T(8,128)S(1)}, u32[]{:S(2)}, u32[]{:S(2)}) collective-permute-start(f32[264,128]{1,0:T(8,128)S(1)} %get-tuple-element.70), channel_id=1, source_target_pairs={{0,8},{1,17},{2,10},{3,19},{4,12},{5,21},{6,14},{7,23},{8,0},{9,25... | collective-permute-start | bytes 405512 | tf_op jit(solution)/shard_map/ppermute | solution.py:355
  66.4 1.1 %collective-permute-done.9 = f32[264,128]{1,0:T(8,128)S(1)} collective-permute-done((f32[264,128]{1,0:T(8,128)S(1)}, f32[264,128]{1,0:T(8,128)S(1)}, u32[]{:S(2)}, u32[]{:S(2)}) %collective-permute-start.9) | collective-permute-done | bytes 135200 | tf_op jit(solution)/shard_map/ppermute | solution.py:355
  67.5 1.4 %collective-permute-start.10 = (f32[264,128]{1,0:T(8,128)S(1)}, f32[264,128]{1,0:T(8,128)S(1)}, u32[]{:S(2)}, u32[]{:S(2)}) collective-permute-start(f32[264,128]{1,0:T(8,128)S(1)} %add.21.refs_0_), channel_id=1, source_target_pairs={{0,16},{1,9},{2,18},{3,11},{4,20},{5,13},{6,22},{7,15},{8,24},{9,1... | collective-permute-start | bytes 405512 | tf_op jit(solution)/shard_map/ppermute | solution.py:355
  69.0 2.3 %collective-permute-done.16 = f32[264,128]{1,0:T(8,128)S(1)} collective-permute-done((f32[264,128]{1,0:T(8,128)S(1)}, f32[264,128]{1,0:T(8,128)S(1)}, u32[]{:S(2)}, u32[]{:S(2)}) %collective-permute-start.16) | collective-permute-done | bytes 135200 | tf_op jit(solution)/shard_map/ppermute | solution.py:355
  71.3 1.7 %collective-permute-start.17 = (f32[264,128]{1,0:T(8,128)S(1)}, f32[264,128]{1,0:T(8,128)S(1)}, u32[]{:S(2)}, u32[]{:S(2)}) collective-permute-start(f32[264,128]{1,0:T(8,128)S(1)} %add.23.refs_0_), channel_id=1, source_target_pairs={{0,16},{1,9},{2,18},{3,11},{4,20},{5,13},{6,22},{7,15},{8,24},{9,1... | collective-permute-start | bytes 405512 | tf_op jit(solution)/shard_map/ppermute | solution.py:355
  73.0 0.9 shard_map.58
  73.9 1.7 %collective-permute-start.11 = (f32[264,128]{1,0:T(8,128)S(1)}, f32[264,128]{1,0:T(8,128)S(1)}, u32[]{:S(2)}, u32[]{:S(2)}) collective-permute-start(f32[264,128]{1,0:T(8,128)S(1)} %get-tuple-element.66.own_ref), channel_id=1, source_target_pairs={{0,6},{1,7},{2,4},{3,5},{4,2},{5,3},{6,0},{7,1},{8,14},{9,15},{10,... | collective-permute-start | bytes 405512 | tf_op jit(solution)/shard_map/ppermute | solution.py:344
  75.6 0.8 collective-permute-done.17.refs_1_
  76.4 0.9 shard_map.62
  77.3 1.4 %collective-permute-start.18 = (f32[264,128]{1,0:T(8,128)S(1)}, f32[264,128]{1,0:T(8,128)S(1)}, u32[]{:S(2)}, u32[]{:S(2)}) collective-permute-start(f32[264,128]{1,0:T(8,128)S(1)} %get-tuple-element.76.own_ref), channel_id=1, source_target_pairs={{0,6},{1,7},{2,4},{3,5},{4,2},{5,3},{6,0},{7,1},{8,14},{9,15},{10,... | collective-permute-start | bytes 405512 | tf_op jit(solution)/shard_map/ppermute | solution.py:344
  78.8 2.1 %collective-permute-done.11.got_ref = f32[264,128]{1,0:T(8,128)S(1)} collective-permute-done((f32[264,128]{1,0:T(8,128)S(1)}, f32[264,128]{1,0:T(8,128)S(1)}, u32[]{:S(2)}, u32[]{:S(2)}) %collective-permute-start.11) | collective-permute-done | bytes 135200 | tf_op jit(solution)/shard_map/ppermute | solution.py:344
  80.9 0.2 shard_map.63
  81.1 3.6 %collective-permute-start.19 = (f32[328,128]{1,0:T(8,128)S(1)}, f32[328,128]{1,0:T(8,128)S(1)}, u32[]{:S(2)}, u32[]{:S(2)}) collective-permute-start(f32[328,128]{1,0:T(8,128)S(1)} %get-tuple-element.81), channel_id=1, source_target_pairs={{0,2},{1,3},{2,0},{3,1},{4,6},{5,7},{6,4},{7,5},{8,10},{9,11},{10,... | collective-permute-start | bytes 503816 | tf_op jit(solution)/shard_map/ppermute | solution.py:344
  84.7 0.4 collective-permute-done.18.got_ref
  85.1 0.2 shard_map.64
  85.3 2.0 %collective-permute-start.20 = (f32[72,128]{1,0:T(8,128)S(1)}, f32[72,128]{1,0:T(8,128)S(1)}, u32[]{:S(2)}, u32[]{:S(2)}) collective-permute-start(f32[72,128]{1,0:T(8,128)S(1)} %get-tuple-element.82), channel_id=1, source_target_pairs={{0,2},{1,3},{2,0},{3,1},{4,6},{5,7},{6,4},{7,5},{8,10},{9,11},{10,... | collective-permute-start | bytes 110600 | tf_op jit(solution)/shard_map/ppermute | solution.py:344
  87.3 2.0 %collective-permute-done.20.refs_3_ = f32[72,128]{1,0:T(8,128)S(1)} collective-permute-done((f32[72,128]{1,0:T(8,128)S(1)}, f32[72,128]{1,0:T(8,128)S(1)}, u32[]{:S(2)}, u32[]{:S(2)}) %collective-permute-start.20) | collective-permute-done | bytes 36896 | tf_op jit(solution)/shard_map/ppermute | solution.py:344
  89.3 0.1 shard_map.65
  89.4 0.0 collective-permute-start.21
  89.4 1.4 %collective-permute-done.21.got_ref.refs_3_ = f32[392,128]{1,0:T(8,128)S(1)} collective-permute-done((f32[392,128]{1,0:T(8,128)S(1)}, f32[392,128]{1,0:T(8,128)S(1)}, u32[]{:S(2)}, u32[]{:S(2)}) %collective-permute-start.21) | collective-permute-done | bytes 200736 | tf_op jit(solution)/shard_map/ppermute | solution.py:344
  90.9 0.1 shard_map.66
  91.0 3.2 %collective-permute-start.24 = (f32[8,256]{1,0:T(8,128)S(1)}, f32[8,256]{1,0:T(8,128)S(1)}, u32[]{:S(2)}, u32[]{:S(2)}) collective-permute-start(f32[8,256]{1,0:T(8,128)S(1)} %get-tuple-element.86.known_ref.refs_4_), channel_id=1, source_target_pairs={{0,24},{8,16},{16,8},{24,0},{1,25},{9,17},{17,9},{25,1},{2,26},{10... | collective-permute-start | bytes 24584 | tf_op jit(solution)/shard_map/ppermute | solution.py:436
  94.1 0.6 collective-permute-start.23
  94.7 0.0 collective-permute-start.22
  94.8 0.8 shard_map.68
  95.6 0.1 collective-permute-done.24.refs_2_
  95.7 2.0 %collective-permute-done.23.refs_1_ = f32[8,256]{1,0:T(8,128)S(1)} collective-permute-done((f32[8,256]{1,0:T(8,128)S(1)}, f32[8,256]{1,0:T(8,128)S(1)}, u32[]{:S(2)}, u32[]{:S(2)}) %collective-permute-start.23) | collective-permute-done | bytes 8224 | tf_op jit(solution)/shard_map/ppermute | solution.py:436
  97.8 0.6 collective-permute-done.22.refs_0_
  98.4 0.7 shard_map.67
  (13 shorter events, 0.1 us)
Async XLA Ops:
  0.6 6.2 %collective-permute-start.1 = (f32[1024,256]{1,0:T(8,128)}, f32[1024,256]{1,0:T(8,128)S(1)}, u32[]{:S(2)}, u32[]{:S(2)}) collective-permute-start(f32[1024,256]{1,0:T(8,128)} %own_ref.1), channel_id=1, source_target_pairs={{0,1},{1,0},{2,3},{3,2},{4,5},{5,4},{6,7},{7,6},{8,9},{9,8},{10,11... | collective-permute-start | bytes 3145736 | tf_op jit(solution)/shard_map/ppermute | solution.py:344
  1.1 26.9 %collective-permute-start = (f32[1024,256]{1,0:T(8,128)}, f32[1024,256]{1,0:T(8,128)S(1)}, u32[]{:S(2)}, u32[]{:S(2)}) collective-permute-start(f32[1024,256]{1,0:T(8,128)} %own_ref.1), channel_id=1, source_target_pairs={{0,2},{1,3},{2,0},{3,1},{4,6},{5,7},{6,4},{7,5},{8,10},{9,11},{10,... | collective-permute-start | bytes 3145736 | tf_op jit(solution)/shard_map/ppermute | solution.py:344
  4.8 1.4 %collective-permute-start.2 = (f32[256,128]{1,0:T(8,128)S(1)}, f32[256,128]{1,0:T(8,128)S(1)}, u32[]{:S(2)}, u32[]{:S(2)}) collective-permute-start(f32[256,128]{1,0:T(8,128)S(1)} %get-tuple-element.89), channel_id=1, source_target_pairs={{0,1},{1,0},{2,3},{3,2},{4,5},{5,4},{6,7},{7,6},{8,9},{9,8},{10,11... | collective-permute-start | bytes 393224 | tf_op jit(solution)/shard_map/ppermute | solution.py:344
  6.4 24.2 %collective-permute-start.4 = (f32[256,128]{1,0:T(8,128)S(1)}, f32[256,128]{1,0:T(8,128)S(1)}, u32[]{:S(2)}, u32[]{:S(2)}) collective-permute-start(f32[256,128]{1,0:T(8,128)S(1)} %get-tuple-element.49), channel_id=1, source_target_pairs={{0,2},{1,3},{2,0},{3,1},{4,6},{5,7},{6,4},{7,5},{8,10},{9,11},{10,... | collective-permute-start | bytes 393224 | tf_op jit(solution)/shard_map/ppermute | solution.py:344
  6.8 1.2 %copy-start = (f32[1024,256]{1,0:T(8,128)S(1)}, f32[1024,256]{1,0:T(8,128)}, u32[]{:S(2)}) copy-start(f32[1024,256]{1,0:T(8,128)} %own_ref.1) | copy-start | bytes 3145732
  28.0 3.1 %collective-permute-start.3 = (f32[1024,256]{1,0:T(8,128)S(1)}, f32[1024,256]{1,0:T(8,128)S(1)}, u32[]{:S(2)}, u32[]{:S(2)}) collective-permute-start(f32[1024,256]{1,0:T(8,128)S(1)} %collective-permute-done.side_ref), channel_id=1, source_target_pairs={{0,1},{1,0},{2,3},{3,2},{4,5},{5,4},{6,7},{7,6},{8,9},{9,8},{10,11... | collective-permute-start | bytes 3145736 | tf_op jit(solution)/shard_map/ppermute | solution.py:344
  31.8 7.7 %collective-permute-start.5 = (f32[256,128]{1,0:T(8,128)S(1)}, f32[256,128]{1,0:T(8,128)S(1)}, u32[]{:S(2)}, u32[]{:S(2)}) collective-permute-start(f32[256,128]{1,0:T(8,128)S(1)} %get-tuple-element.53.a_ref), channel_id=1, source_target_pairs={{0,6},{1,7},{2,4},{3,5},{4,2},{5,3},{6,0},{7,1},{8,14},{9,15},{10,... | collective-permute-start | bytes 393224 | tf_op jit(solution)/shard_map/ppermute | solution.py:344
  36.4 6.9 %collective-permute-start.12 = (f32[256,128]{1,0:T(8,128)S(1)}, f32[256,128]{1,0:T(8,128)S(1)}, u32[]{:S(2)}, u32[]{:S(2)}) collective-permute-start(f32[256,128]{1,0:T(8,128)S(1)} %get-tuple-element.68.a_ref), channel_id=1, source_target_pairs={{0,6},{1,7},{2,4},{3,5},{4,2},{5,3},{6,0},{7,1},{8,14},{9,15},{10,... | collective-permute-start | bytes 393224 | tf_op jit(solution)/shard_map/ppermute | solution.py:344
  40.4 5.3 %collective-permute-start.6 = (f32[264,128]{1,0:T(8,128)S(1)}, f32[264,128]{1,0:T(8,128)S(1)}, u32[]{:S(2)}, u32[]{:S(2)}) collective-permute-start(f32[264,128]{1,0:T(8,128)S(1)} %shard_map.54), channel_id=1, source_target_pairs={{0,8},{1,17},{2,10},{3,19},{4,12},{5,21},{6,14},{7,23},{8,0},{9,25... | collective-permute-start | bytes 405512 | tf_op jit(solution)/shard_map/ppermute | solution.py:355
  44.1 5.5 %collective-permute-start.13 = (f32[264,128]{1,0:T(8,128)S(1)}, f32[264,128]{1,0:T(8,128)S(1)}, u32[]{:S(2)}, u32[]{:S(2)}) collective-permute-start(f32[264,128]{1,0:T(8,128)S(1)} %shard_map.59), channel_id=1, source_target_pairs={{0,8},{1,17},{2,10},{3,19},{4,12},{5,21},{6,14},{7,23},{8,0},{9,25... | collective-permute-start | bytes 405512 | tf_op jit(solution)/shard_map/ppermute | solution.py:355
  45.7 5.1 %collective-permute-start.7 = (f32[264,128]{1,0:T(8,128)S(1)}, f32[264,128]{1,0:T(8,128)S(1)}, u32[]{:S(2)}, u32[]{:S(2)}) collective-permute-start(f32[264,128]{1,0:T(8,128)S(1)} %add.20.refs_0_), channel_id=1, source_target_pairs={{0,16},{1,9},{2,18},{3,11},{4,20},{5,13},{6,22},{7,15},{8,24},{9,1... | collective-permute-start | bytes 405512 | tf_op jit(solution)/shard_map/ppermute | solution.py:355
  49.6 6.6 %collective-permute-start.14 = (f32[264,128]{1,0:T(8,128)S(1)}, f32[264,128]{1,0:T(8,128)S(1)}, u32[]{:S(2)}, u32[]{:S(2)}) collective-permute-start(f32[264,128]{1,0:T(8,128)S(1)} %add.22.refs_0_), channel_id=1, source_target_pairs={{0,16},{1,9},{2,18},{3,11},{4,20},{5,13},{6,22},{7,15},{8,24},{9,1... | collective-permute-start | bytes 405512 | tf_op jit(solution)/shard_map/ppermute | solution.py:355
  51.7 8.9 %collective-permute-start.8 = (f32[264,128]{1,0:T(8,128)S(1)}, f32[264,128]{1,0:T(8,128)S(1)}, u32[]{:S(2)}, u32[]{:S(2)}) collective-permute-start(f32[264,128]{1,0:T(8,128)S(1)} %get-tuple-element.64.refs_0_), channel_id=1, source_target_pairs={{0,6},{1,7},{2,4},{3,5},{4,2},{5,3},{6,0},{7,1},{8,14},{9,15},{10,... | collective-permute-start | bytes 405512 | tf_op jit(solution)/shard_map/ppermute | solution.py:344
  57.1 7.0 %collective-permute-start.15 = (f32[264,128]{1,0:T(8,128)S(1)}, f32[264,128]{1,0:T(8,128)S(1)}, u32[]{:S(2)}, u32[]{:S(2)}) collective-permute-start(f32[264,128]{1,0:T(8,128)S(1)} %get-tuple-element.69.refs_0_), channel_id=1, source_target_pairs={{0,6},{1,7},{2,4},{3,5},{4,2},{5,3},{6,0},{7,1},{8,14},{9,15},{10,... | collective-permute-start | bytes 405512 | tf_op jit(solution)/shard_map/ppermute | solution.py:344
  61.5 6.0 %collective-permute-start.9 = (f32[264,128]{1,0:T(8,128)S(1)}, f32[264,128]{1,0:T(8,128)S(1)}, u32[]{:S(2)}, u32[]{:S(2)}) collective-permute-start(f32[264,128]{1,0:T(8,128)S(1)} %get-tuple-element.65), channel_id=1, source_target_pairs={{0,8},{1,17},{2,10},{3,19},{4,12},{5,21},{6,14},{7,23},{8,0},{9,25... | collective-permute-start | bytes 405512 | tf_op jit(solution)/shard_map/ppermute | solution.py:355
  65.0 6.3 %collective-permute-start.16 = (f32[264,128]{1,0:T(8,128)S(1)}, f32[264,128]{1,0:T(8,128)S(1)}, u32[]{:S(2)}, u32[]{:S(2)}) collective-permute-start(f32[264,128]{1,0:T(8,128)S(1)} %get-tuple-element.70), channel_id=1, source_target_pairs={{0,8},{1,17},{2,10},{3,19},{4,12},{5,21},{6,14},{7,23},{8,0},{9,25... | collective-permute-start | bytes 405512 | tf_op jit(solution)/shard_map/ppermute | solution.py:355
  67.5 5.5 %collective-permute-start.10 = (f32[264,128]{1,0:T(8,128)S(1)}, f32[264,128]{1,0:T(8,128)S(1)}, u32[]{:S(2)}, u32[]{:S(2)}) collective-permute-start(f32[264,128]{1,0:T(8,128)S(1)} %add.21.refs_0_), channel_id=1, source_target_pairs={{0,16},{1,9},{2,18},{3,11},{4,20},{5,13},{6,22},{7,15},{8,24},{9,1... | collective-permute-start | bytes 405512 | tf_op jit(solution)/shard_map/ppermute | solution.py:355
  71.3 5.1 %collective-permute-start.17 = (f32[264,128]{1,0:T(8,128)S(1)}, f32[264,128]{1,0:T(8,128)S(1)}, u32[]{:S(2)}, u32[]{:S(2)}) collective-permute-start(f32[264,128]{1,0:T(8,128)S(1)} %add.23.refs_0_), channel_id=1, source_target_pairs={{0,16},{1,9},{2,18},{3,11},{4,20},{5,13},{6,22},{7,15},{8,24},{9,1... | collective-permute-start | bytes 405512 | tf_op jit(solution)/shard_map/ppermute | solution.py:355
  73.9 7.0 %collective-permute-start.11 = (f32[264,128]{1,0:T(8,128)S(1)}, f32[264,128]{1,0:T(8,128)S(1)}, u32[]{:S(2)}, u32[]{:S(2)}) collective-permute-start(f32[264,128]{1,0:T(8,128)S(1)} %get-tuple-element.66.own_ref), channel_id=1, source_target_pairs={{0,6},{1,7},{2,4},{3,5},{4,2},{5,3},{6,0},{7,1},{8,14},{9,15},{10,... | collective-permute-start | bytes 405512 | tf_op jit(solution)/shard_map/ppermute | solution.py:344
  77.3 7.8 %collective-permute-start.18 = (f32[264,128]{1,0:T(8,128)S(1)}, f32[264,128]{1,0:T(8,128)S(1)}, u32[]{:S(2)}, u32[]{:S(2)}) collective-permute-start(f32[264,128]{1,0:T(8,128)S(1)} %get-tuple-element.76.own_ref), channel_id=1, source_target_pairs={{0,6},{1,7},{2,4},{3,5},{4,2},{5,3},{6,0},{7,1},{8,14},{9,15},{10,... | collective-permute-start | bytes 405512 | tf_op jit(solution)/shard_map/ppermute | solution.py:344
  81.1 8.2 %collective-permute-start.19 = (f32[328,128]{1,0:T(8,128)S(1)}, f32[328,128]{1,0:T(8,128)S(1)}, u32[]{:S(2)}, u32[]{:S(2)}) collective-permute-start(f32[328,128]{1,0:T(8,128)S(1)} %get-tuple-element.81), channel_id=1, source_target_pairs={{0,2},{1,3},{2,0},{3,1},{4,6},{5,7},{6,4},{7,5},{8,10},{9,11},{10,... | collective-permute-start | bytes 503816 | tf_op jit(solution)/shard_map/ppermute | solution.py:344
  85.3 4.0 %collective-permute-start.20 = (f32[72,128]{1,0:T(8,128)S(1)}, f32[72,128]{1,0:T(8,128)S(1)}, u32[]{:S(2)}, u32[]{:S(2)}) collective-permute-start(f32[72,128]{1,0:T(8,128)S(1)} %get-tuple-element.82), channel_id=1, source_target_pairs={{0,2},{1,3},{2,0},{3,1},{4,6},{5,7},{6,4},{7,5},{8,10},{9,11},{10,... | collective-permute-start | bytes 110600 | tf_op jit(solution)/shard_map/ppermute | solution.py:344
  89.4 1.5 %collective-permute-start.21 = (f32[392,128]{1,0:T(8,128)S(1)}, f32[392,128]{1,0:T(8,128)S(1)}, u32[]{:S(2)}, u32[]{:S(2)}) collective-permute-start(f32[392,128]{1,0:T(8,128)S(1)} %get-tuple-element.84), channel_id=1, source_target_pairs={{0,1},{1,0},{2,3},{3,2},{4,5},{5,4},{6,7},{7,6},{8,9},{9,8},{10,11... | collective-permute-start | bytes 602120 | tf_op jit(solution)/shard_map/ppermute | solution.py:344
  91.0 4.8 %collective-permute-start.24 = (f32[8,256]{1,0:T(8,128)S(1)}, f32[8,256]{1,0:T(8,128)S(1)}, u32[]{:S(2)}, u32[]{:S(2)}) collective-permute-start(f32[8,256]{1,0:T(8,128)S(1)} %get-tuple-element.86.known_ref.refs_4_), channel_id=1, source_target_pairs={{0,24},{8,16},{16,8},{24,0},{1,25},{9,17},{17,9},{25,1},{2,26},{10... | collective-permute-start | bytes 24584 | tf_op jit(solution)/shard_map/ppermute | solution.py:436
  94.1 3.7 %collective-permute-start.23 = (f32[8,256]{1,0:T(8,128)S(1)}, f32[8,256]{1,0:T(8,128)S(1)}, u32[]{:S(2)}, u32[]{:S(2)}) collective-permute-start(f32[8,256]{1,0:T(8,128)S(1)} %get-tuple-element.86.known_ref.refs_4_), channel_id=1, source_target_pairs={{0,16},{8,24},{16,0},{24,8},{1,17},{9,25},{17,1},{25,9},{2,18},{10... | collective-permute-start | bytes 24584 | tf_op jit(solution)/shard_map/ppermute | solution.py:436
  94.7 3.7 %collective-permute-start.22 = (f32[8,256]{1,0:T(8,128)S(1)}, f32[8,256]{1,0:T(8,128)S(1)}, u32[]{:S(2)}, u32[]{:S(2)}) collective-permute-start(f32[8,256]{1,0:T(8,128)S(1)} %get-tuple-element.86.known_ref.refs_4_), channel_id=1, source_target_pairs={{0,8},{8,0},{16,24},{24,16},{1,9},{9,1},{17,25},{25,17},{2,10},{10... | collective-permute-start | bytes 24584 | tf_op jit(solution)/shard_map/ppermute | solution.py:436

commit v11 on v10

--- a/solution.py
+++ b/solution.py
@@ -81,13 +81,6 @@
     return total[:cols] + total[cols:]
 
 
-def sketch_sides(x):
-    high, low = split(x)
-    own = join_lanes(high, low, QUARTER)
-    other = join_lanes(turn(high, QUARTER), turn(low, QUARTER), QUARTER)
-    return own.astype(BF16), other.astype(BF16)
-
-
 def store_factors(high_ref, low_ref, blocks, axis=1):
     start = 0
     for block in blocks:
@@ -100,58 +93,37 @@
         start += size
 
 
-def prepare_kernel(near_ref, got_ref, mine_ref, theirs_ref):
-    near, got = near_ref[...], got_ref[...]
-    low = join_lanes(near, got, QUARTER)
-    high = join_lanes(turn(near, QUARTER), turn(got, QUARTER), QUARTER)
-    zero = position()[1] == 0
-    mine_ref[...] = jnp.where(zero, low, high)
-    theirs_ref[...] = jnp.where(zero, high, low)
-
-
-def near_kernel(own_ref, core_ref, sketch_ref, y_ref, high_ref, low_ref, high_t_ref, low_t_ref):
+def near_kernel(own_ref, core_ref, near_ref, got_ref, y_ref, high_ref, low_ref, high_t_ref, low_t_ref):
     blocks = (own_ref[...], core_ref[...])
     store_factors(high_ref, low_ref, blocks)
     store_factors(high_t_ref, low_t_ref, [block.T for block in blocks], 0)
-    rhs = jnp.concatenate(sketch_sides(sketch_ref[...]), axis=0)
+    sketch = jnp.concatenate([near_ref[...], got_ref[...]], axis=0)
+    rhs = jnp.concatenate(split(sketch), axis=1).astype(BF16)
+    zero = position()[1] == 0
+    size = y_ref.shape[0] // (2 * HALVES)
     for b in range(own_ref.shape[0] // LANES):
         cut = slice(b * LANES, (b + 1) * LANES)
         total = dot(high_ref[cut, :], rhs) + dot(low_ref[cut, :], rhs)
-        y_ref[b * QUARTER : (b + 1) * QUARTER, :] = unfold(total.T)
-
-
-def side_split_kernel(side_ref, high_ref, low_ref, high_t_ref, low_t_ref):
-    store_factors(high_ref, low_ref, (side_ref[...],))
-    store_factors(high_t_ref, low_t_ref, (side_ref[...].T,), 0)
-
-
-def side_kernel(high_ref, low_ref, sketch_ref, near_ref, y_ref):
-    rhs = sketch_sides(sketch_ref[...])[0]
-    for b in range(high_ref.shape[0] // LANES):
-        cut = slice(b * LANES, (b + 1) * LANES)
-        total = dot(high_ref[cut, :], rhs) + dot(low_ref[cut, :], rhs)
-        out = slice(b * QUARTER, (b + 1) * QUARTER)
-        y_ref[out, :] = unfold(total.T) + near_ref[out, :]
-
-
-def add_far(h, high_ref, low_ref, sketch_ref, near_ref, y_ref):
-    rhs = sketch_sides(sketch_ref[...])[1]
-    for b in range(high_ref.shape[0] // LANES):
-        cut = slice(b * LANES, (b + 1) * LANES)
-        total = dot(high_ref[cut, :], rhs) + dot(low_ref[cut, :], rhs)
-        y = unfold(total.T)[h * COLS : (h + 1) * COLS]
-        at = b * QUARTER + h * COLS
-        y_ref[b * COLS : (b + 1) * COLS, :] = y + near_ref[at : at + COLS, :]
-
-
-def far_kernel(diagonal_ref, sketch_ref, near_ref, y_ref, high_ref, low_ref):
-    store_factors(high_ref, low_ref, (diagonal_ref[...],))
-    add_far(0, high_ref, low_ref, sketch_ref, near_ref, y_ref)
-
-
-def second_far_kernel(diagonal_ref, high_ref, low_ref, sketch_ref, near_ref, y_ref, high_t_ref, low_t_ref):
-    add_far(1, high_ref, low_ref, sketch_ref, near_ref, y_ref)
-    store_factors(high_t_ref, low_t_ref, (diagonal_ref[...].T,), 0)
+        y = (total[:, :LANES] + total[:, LANES:]).T
+        low, high = y[:QUARTER], y[QUARTER:]
+        for s, x in enumerate((jnp.where(zero, low, high), jnp.where(zero, high, low))):
+            for h in range(HALVES):
+                at = (s * HALVES + h) * size + b * COLS
+                y_ref[at : at + COLS, :] = x[h * COLS : (h + 1) * COLS]
+
+
+def cross_kernel(y_ref, got_ref, *refs):
+    for i, ref in enumerate(refs):
+        cut = slice(i * ref.shape[0], (i + 1) * ref.shape[0])
+        ref[...] = y_ref[cut, :] + got_ref[cut, :]
+
+
+def split_kernel(block_ref, high_ref, low_ref):
+    store_factors(high_ref, low_ref, (block_ref[...],))
+
+
+def turned_kernel(block_ref, high_ref, low_ref):
+    store_factors(high_ref, low_ref, (block_ref[...].T,), 0)
 
 
 def send_z(y, high_refs, low_refs, z_ref):
@@ -369,25 +341,23 @@
 
     core = lax.rem(lax.axis_index("snap"), 2)
     side_block = swap_side(snapshots)
-    packed = ((width, LANES), F32)
-    mine, theirs = call(prepare_kernel, [packed, packed], sketch_half(core), swap_core(sketch_half(1 - core)))
-    side_sketch = swap_side(theirs)
-    quarter_shape = ((rows // LANES * QUARTER, LANES), F32)
-    near_y, *near = call(
-        near_kernel, [quarter_shape] + factor(2) + factor_t(2), snapshots, swap_core(snapshots), mine
+    half_rows = rows // LANES * COLS
+    y_near, *near = call(
+        near_kernel,
+        [((2 * HALVES * half_rows, LANES), F32)] + factor(2) + factor_t(2),
+        snapshots, swap_core(snapshots), sketch_half(core), swap_core(sketch_half(1 - core)),
     )
-    side_block, near_y = lax.optimization_barrier((side_block, near_y))
-    side = call(side_split_kernel, factor(1) + factor_t(1), side_block)
-    (side_y,) = call(side_kernel, [quarter_shape], *side[:2], side_sketch, near_y, cost=LONG)
-    half_shape = ((rows // LANES * COLS, LANES), F32)
+    sums = call(cross_kernel, [((half_rows, LANES), F32)] * 2 * HALVES, y_near, swap_pair(y_near))
+    own, others = sums[:HALVES], sums[HALVES:]
+    got = [swap_side(other) for other in others]
+    side_block, *own = lax.optimization_barrier((side_block, *own))
+    side = call(split_kernel, factor(1), side_block)
+    side_t = call(turned_kernel, factor_t(1), side_block)
     diagonal = swap_core(side_block)
-    own_first, *far = call(far_kernel, [half_shape] + factor(1), diagonal, side_sketch, side_y)
-    own_second, *far_t = call(
-        second_far_kernel, [half_shape] + factor_t(1), diagonal, *far, side_sketch, side_y
-    )
-    own = (own_first, own_second)
+    far = call(split_kernel, factor(1), diagonal, cost=LONG)
+    far_t = call(turned_kernel, factor_t(1), diagonal)
     matrix = (near[0], side[0], far[0], near[1], side[1], far[1])
-    matrix_t = (near[2], side[2], far_t[0], near[3], side[3], far_t[1])
+    matrix_t = (near[2], side_t[0], far_t[0], near[3], side_t[1], far_t[1])
 
     flat = (COLS * rows // LANES + TILE, LANES)
     sent_shape = ((COLS * 4 * width // LANES + TILE, LANES), F32)
@@ -395,7 +365,7 @@
     scale_shape = ((TILE, LANES), F32)
     z_shape = ((COLS * 4 * width // LANES, LANES), F32)
     scales = [[] for _ in range(HALVES)]
-    sent = [call(first_z_kernel, [sent_shape], y, swap_pair(y), *matrix, cost=LONG)[0] for y in own]
+    sent = [call(first_z_kernel, [sent_shape], y, g, *matrix, cost=LONG)[0] for y, g in zip(own, got)]
     ys, zs = [None] * HALVES, [None] * HALVES
     for section in range(ITERS):
         last = section == ITERS - 1

time: 99.3 us -> 107 us (1.078)
  waiting for transfers between devices: 45 us -> 55.1 us
  starting transfers between devices: 38.1 us -> 34.7 us
    ppermute x14, waiting for transfers between devices: 35.7 us -> 44.2 us  [swap(): return lax.ppermute(x, 'snap', [(i, i ^ bits) for i in range(places)])]
    ppermute x14, starting transfers between devices: 22.9 us -> 19.4 us  [swap(): return lax.ppermute(x, 'snap', [(i, i ^ bits) for i in range(places)])]
    ppermute x8, waiting for transfers between devices: 6.56 us -> 8.66 us  [swap_cell(): return lax.ppermute(x, ('cell', 'snap'), perm)]
  transfers between devices with their start and end apart: 25 -> 25, of which waited for: 18 -> 19; matrix products, arithmetic and copies ran while one was open for 1% -> 1% of each run, Pallas kernels for 12% -> 11%
where the time goes in v11:
time: 107 us
  waiting for transfers between devices  55.1 us (51%)
  starting transfers between devices  34.7 us (32%)
  Pallas kernels  12.8 us (12%)
  local copies, waits for them, and re-layouts  3.07 us (3%)
    ppermute x14, waiting for transfers between devices, swap(): return lax.ppermute(x, 'snap', [(i, i ^ bits) for i in range(places)])  44.2 us
    ppermute x14, starting transfers between devices, swap(): return lax.ppermute(x, 'snap', [(i, i ^ bits) for i in range(places)])  19.4 us
    pallas_call x20, Pallas kernels, call(): pl.pallas_call(kernel, out_shape=[jax.ShapeDtypeStruct(shape, dtype) for...  12.8 us
    ppermute x8, starting transfers between devices, swap_cell(): return lax.ppermute(x, ('cell', 'snap'), perm)  11.7 us
    ppermute x8, waiting for transfers between devices, swap_cell(): return lax.ppermute(x, ('cell', 'snap'), perm)  8.66 us
    ppermute x3, starting transfers between devices, local(): lax.ppermute(known, 'cell', [(c, c ^ d) for c in range(groups)])  3.55 us
    ppermute x3, waiting for transfers between devices, local(): lax.ppermute(known, 'cell', [(c, c ^ d) for c in range(groups)])  2.27 us
  transfers between devices with their start and end apart: 25, of which 19 were waited for; matrix products, arithmetic and copies ran while one was open for 1% of the time, Pallas kernels for 11%

profile of v11, /device:TPU:0, one launch (start us, length us, event | category | flops | bytes accessed | tf_op | source)
XLA Modules:
  0.0 106.5 jit_solution(14870295427981472835)
XLA Ops:
  0.6 0.5 collective-permute-start.1
  1.1 2.7 %collective-permute-start = (f32[1024,256]{1,0:T(8,128)}, f32[1024,256]{1,0:T(8,128)S(1)}, u32[]{:S(2)}, u32[]{:S(2)}) collective-permute-start(f32[1024,256]{1,0:T(8,128)} %own_ref.1), channel_id=1, source_target_pairs={{0,2},{1,3},{2,0},{3,1},{4,6},{5,7},{6,4},{7,5},{8,10},{9,11},{10,... | collective-permute-start | bytes 3145736 | tf_op jit(solution)/shard_map/ppermute | solution.py:316
  3.8 1.0 constant_dynamic-slice_fusion
  4.8 0.2 collective-permute-start.2
  5.0 1.2 %collective-permute-done.2.got_ref = f32[256,128]{1,0:T(8,128)S(1)} collective-permute-done((f32[256,128]{1,0:T(8,128)S(1)}, f32[256,128]{1,0:T(8,128)S(1)}, u32[]{:S(2)}, u32[]{:S(2)}) %collective-permute-start.2) | collective-permute-done | bytes 131104 | tf_op jit(solution)/shard_map/ppermute | solution.py:316
  6.2 1.2 %copy-done = f32[1024,256]{1,0:T(8,128)S(1)} copy-done((f32[1024,256]{1,0:T(8,128)S(1)}, f32[1024,256]{1,0:T(8,128)}, u32[]{:S(2)}) %copy-start) | copy-done | bytes 1048600
  7.4 1.0 shard_map.49
  8.4 2.5 %collective-permute-start.3 = (f32[1024,128]{1,0:T(8,128)S(1)}, f32[1024,128]{1,0:T(8,128)S(1)}, u32[]{:S(2)}, u32[]{:S(2)}) collective-permute-start(f32[1024,128]{1,0:T(8,128)S(1)} %get-tuple-element.47.y_ref), channel_id=1, source_target_pairs={{0,6},{1,7},{2,4},{3,5},{4,2},{5,3},{6,0},{7,1},{8,14},{9,15},{10,... | collective-permute-start | bytes 1572872 | tf_op jit(solution)/shard_map/ppermute | solution.py:316
  11.0 30.2 %collective-permute-done.3.got_ref = f32[1024,128]{1,0:T(8,128)S(1)} collective-permute-done((f32[1024,128]{1,0:T(8,128)S(1)}, f32[1024,128]{1,0:T(8,128)S(1)}, u32[]{:S(2)}, u32[]{:S(2)}) %collective-permute-start.3) | collective-permute-done | bytes 524320 | tf_op jit(solution)/shard_map/ppermute | solution.py:316
  41.2 0.7 shard_map.50
  41.9 0.1 shard_map.51
  42.1 0.1 collective-permute-start.4
  42.1 2.0 %collective-permute-start.12 = (f32[256,128]{1,0:T(8,128)}, f32[256,128]{1,0:T(8,128)}, u32[]{:S(2)}, u32[]{:S(2)}) collective-permute-start(f32[256,128]{1,0:T(8,128)} %get-tuple-element.70), channel_id=1, source_target_pairs={{0,2},{1,3},{2,0},{3,1},{4,6},{5,7},{6,4},{7,5},{8,10},{9,11},{10,... | collective-permute-start | bytes 393224 | tf_op jit(solution)/shard_map/ppermute | solution.py:316
  44.2 0.4 collective-permute-done.5.block_ref
  44.6 0.1 shard_map.52
  44.7 0.9 copy-done.1
  45.6 2.8 %collective-permute-done.4.b_ref = f32[256,128]{1,0:T(8,128)S(1)} collective-permute-done((f32[256,128]{1,0:T(8,128)S(1)}, f32[256,128]{1,0:T(8,128)S(1)}, u32[]{:S(2)}, u32[]{:S(2)}) %collective-permute-start.4) | collective-permute-done | bytes 131104 | tf_op jit(solution)/shard_map/ppermute | solution.py:316
  48.4 0.8 shard_map.53
  49.2 1.5 %collective-permute-start.6 = (f32[264,128]{1,0:T(8,128)S(1)}, f32[264,128]{1,0:T(8,128)S(1)}, u32[]{:S(2)}, u32[]{:S(2)}) collective-permute-start(f32[264,128]{1,0:T(8,128)S(1)} %shard_map.53), channel_id=1, source_target_pairs={{0,8},{1,17},{2,10},{3,19},{4,12},{5,21},{6,14},{7,23},{8,0},{9,25... | collective-permute-start | bytes 405512 | tf_op jit(solution)/shard_map/ppermute | solution.py:327
  50.7 0.2 collective-permute-done.12.b_ref
  51.0 1.7 %shard_map.59 = f32[264,128]{1,0:T(8,128)S(1)} custom-call(f32[256,128]{1,0:T(8,128)S(1)} %get-tuple-element.69.a_ref, f32[256,128]{1,0:T(8,128)} %collective-permute-done.12.b_ref, bf16[1024,512]{1,0:T(8,128)(2,1)S(1)} %get-tuple-element.52.refs_0_.refs_2_, bf16[1024,256]{1,0:T(8,128)(2,1)S(1)} %get-tuple-element.54.refs_1_.refs_3_, ...), custom_call_target="tpu_custom_call" | custom-call | flops 99999997952 | bytes 268435456 | tf_op jit(solution)/shard_map/pallas_call | solution.py:269
  52.7 1.5 %collective-permute-start.13 = (f32[264,128]{1,0:T(8,128)S(1)}, f32[264,128]{1,0:T(8,128)S(1)}, u32[]{:S(2)}, u32[]{:S(2)}) collective-permute-start(f32[264,128]{1,0:T(8,128)S(1)} %shard_map.59), channel_id=1, source_target_pairs={{0,8},{1,17},{2,10},{3,19},{4,12},{5,21},{6,14},{7,23},{8,0},{9,25... | collective-permute-start | bytes 405512 | tf_op jit(solution)/shard_map/ppermute | solution.py:327
  54.3 1.6 %collective-permute-start.7 = (f32[264,128]{1,0:T(8,128)S(1)}, f32[264,128]{1,0:T(8,128)S(1)}, u32[]{:S(2)}, u32[]{:S(2)}) collective-permute-start(f32[264,128]{1,0:T(8,128)S(1)} %add.20.refs_0_), channel_id=1, source_target_pairs={{0,16},{1,9},{2,18},{3,11},{4,20},{5,13},{6,22},{7,15},{8,24},{9,1... | collective-permute-start | bytes 405512 | tf_op jit(solution)/shard_map/ppermute | solution.py:327
  55.9 3.2 %collective-permute-done.13 = f32[264,128]{1,0:T(8,128)S(1)} collective-permute-done((f32[264,128]{1,0:T(8,128)S(1)}, f32[264,128]{1,0:T(8,128)S(1)}, u32[]{:S(2)}, u32[]{:S(2)}) %collective-permute-start.13) | collective-permute-done | bytes 135200 | tf_op jit(solution)/shard_map/ppermute | solution.py:327
  59.1 0.8 collective-permute-start.14
  59.9 0.4 shard_map.54
  60.2 0.4 shard_map.55
  60.6 0.9 shard_map.56
  61.5 1.5 %collective-permute-start.8 = (f32[264,128]{1,0:T(8,128)S(1)}, f32[264,128]{1,0:T(8,128)S(1)}, u32[]{:S(2)}, u32[]{:S(2)}) collective-permute-start(f32[264,128]{1,0:T(8,128)S(1)} %get-tuple-element.65.refs_0_), channel_id=1, source_target_pairs={{0,6},{1,7},{2,4},{3,5},{4,2},{5,3},{6,0},{7,1},{8,14},{9,15},{10,... | collective-permute-start | bytes 405512 | tf_op jit(solution)/shard_map/ppermute | solution.py:316
  63.0 1.1 %collective-permute-done.14.refs_1_ = f32[264,128]{1,0:T(8,128)S(1)} collective-permute-done((f32[264,128]{1,0:T(8,128)S(1)}, f32[264,128]{1,0:T(8,128)S(1)}, u32[]{:S(2)}, u32[]{:S(2)}) %collective-permute-start.14) | collective-permute-done | bytes 135200 | tf_op jit(solution)/shard_map/ppermute | solution.py:327
  64.2 0.9 shard_map.60
  65.1 1.5 %collective-permute-start.15 = (f32[264,128]{1,0:T(8,128)S(1)}, f32[264,128]{1,0:T(8,128)S(1)}, u32[]{:S(2)}, u32[]{:S(2)}) collective-permute-start(f32[264,128]{1,0:T(8,128)S(1)} %get-tuple-element.71.refs_0_), channel_id=1, source_target_pairs={{0,6},{1,7},{2,4},{3,5},{4,2},{5,3},{6,0},{7,1},{8,14},{9,15},{10,... | collective-permute-start | bytes 405512 | tf_op jit(solution)/shard_map/ppermute | solution.py:316
  66.6 3.2 %collective-permute-done.8.refs_1_ = f32[264,128]{1,0:T(8,128)S(1)} collective-permute-done((f32[264,128]{1,0:T(8,128)S(1)}, f32[264,128]{1,0:T(8,128)S(1)}, u32[]{:S(2)}, u32[]{:S(2)}) %collective-permute-start.8) | collective-permute-done | bytes 135200 | tf_op jit(solution)/shard_map/ppermute | solution.py:316
  69.8 0.9 shard_map.57
  70.7 1.5 %collective-permute-start.9 = (f32[264,128]{1,0:T(8,128)S(1)}, f32[264,128]{1,0:T(8,128)S(1)}, u32[]{:S(2)}, u32[]{:S(2)}) collective-permute-start(f32[264,128]{1,0:T(8,128)S(1)} %get-tuple-element.66), channel_id=1, source_target_pairs={{0,8},{1,17},{2,10},{3,19},{4,12},{5,21},{6,14},{7,23},{8,0},{9,25... | collective-permute-start | bytes 405512 | tf_op jit(solution)/shard_map/ppermute | solution.py:327
  72.2 0.9 shard_map.61
  73.1 1.3 %collective-permute-start.16 = (f32[264,128]{1,0:T(8,128)S(1)}, f32[264,128]{1,0:T(8,128)S(1)}, u32[]{:S(2)}, u32[]{:S(2)}) collective-permute-start(f32[264,128]{1,0:T(8,128)S(1)} %get-tuple-element.72), channel_id=1, source_target_pairs={{0,8},{1,17},{2,10},{3,19},{4,12},{5,21},{6,14},{7,23},{8,0},{9,25... | collective-permute-start | bytes 405512 | tf_op jit(solution)/shard_map/ppermute | solution.py:327
  74.4 2.2 %collective-permute-done.9 = f32[264,128]{1,0:T(8,128)S(1)} collective-permute-done((f32[264,128]{1,0:T(8,128)S(1)}, f32[264,128]{1,0:T(8,128)S(1)}, u32[]{:S(2)}, u32[]{:S(2)}) %collective-permute-start.9) | collective-permute-done | bytes 135200 | tf_op jit(solution)/shard_map/ppermute | solution.py:327
  76.7 1.5 %collective-permute-start.10 = (f32[264,128]{1,0:T(8,128)S(1)}, f32[264,128]{1,0:T(8,128)S(1)}, u32[]{:S(2)}, u32[]{:S(2)}) collective-permute-start(f32[264,128]{1,0:T(8,128)S(1)} %add.21.refs_0_), channel_id=1, source_target_pairs={{0,16},{1,9},{2,18},{3,11},{4,20},{5,13},{6,22},{7,15},{8,24},{9,1... | collective-permute-start | bytes 405512 | tf_op jit(solution)/shard_map/ppermute | solution.py:327
  78.1 0.7 collective-permute-done.16
  78.9 2.0 %collective-permute-start.17 = (f32[264,128]{1,0:T(8,128)S(1)}, f32[264,128]{1,0:T(8,128)S(1)}, u32[]{:S(2)}, u32[]{:S(2)}) collective-permute-start(f32[264,128]{1,0:T(8,128)S(1)} %add.23.refs_0_), channel_id=1, source_target_pairs={{0,16},{1,9},{2,18},{3,11},{4,20},{5,13},{6,22},{7,15},{8,24},{9,1... | collective-permute-start | bytes 405512 | tf_op jit(solution)/shard_map/ppermute | solution.py:327
  80.9 0.9 collective-permute-done.10.refs_1_
  81.8 0.9 shard_map.58
  82.7 0.8 collective-permute-start.11
  83.5 0.5 collective-permute-done.17.refs_1_
  84.0 0.9 shard_map.62
  84.9 2.6 %collective-permute-start.18 = (f32[264,128]{1,0:T(8,128)S(1)}, f32[264,128]{1,0:T(8,128)S(1)}, u32[]{:S(2)}, u32[]{:S(2)}) collective-permute-start(f32[264,128]{1,0:T(8,128)S(1)} %get-tuple-element.78.own_ref), channel_id=1, source_target_pairs={{0,6},{1,7},{2,4},{3,5},{4,2},{5,3},{6,0},{7,1},{8,14},{9,15},{10,... | collective-permute-start | bytes 405512 | tf_op jit(solution)/shard_map/ppermute | solution.py:316
  87.5 2.2 %collective-permute-done.11.got_ref = f32[264,128]{1,0:T(8,128)S(1)} collective-permute-done((f32[264,128]{1,0:T(8,128)S(1)}, f32[264,128]{1,0:T(8,128)S(1)}, u32[]{:S(2)}, u32[]{:S(2)}) %collective-permute-start.11) | collective-permute-done | bytes 135200 | tf_op jit(solution)/shard_map/ppermute | solution.py:316
  89.7 0.2 shard_map.63
  89.9 3.3 %collective-permute-start.19 = (f32[328,128]{1,0:T(8,128)S(1)}, f32[328,128]{1,0:T(8,128)S(1)}, u32[]{:S(2)}, u32[]{:S(2)}) collective-permute-start(f32[328,128]{1,0:T(8,128)S(1)} %get-tuple-element.83), channel_id=1, source_target_pairs={{0,2},{1,3},{2,0},{3,1},{4,6},{5,7},{6,4},{7,5},{8,10},{9,11},{10,... | collective-permute-start | bytes 503816 | tf_op jit(solution)/shard_map/ppermute | solution.py:316
  93.3 0.2 shard_map.64
  93.5 1.6 %collective-permute-start.20 = (f32[72,128]{1,0:T(8,128)S(1)}, f32[72,128]{1,0:T(8,128)S(1)}, u32[]{:S(2)}, u32[]{:S(2)}) collective-permute-start(f32[72,128]{1,0:T(8,128)S(1)} %get-tuple-element.84), channel_id=1, source_target_pairs={{0,2},{1,3},{2,0},{3,1},{4,6},{5,7},{6,4},{7,5},{8,10},{9,11},{10,... | collective-permute-start | bytes 110600 | tf_op jit(solution)/shard_map/ppermute | solution.py:316
  95.0 2.5 %collective-permute-done.20.refs_3_ = f32[72,128]{1,0:T(8,128)S(1)} collective-permute-done((f32[72,128]{1,0:T(8,128)S(1)}, f32[72,128]{1,0:T(8,128)S(1)}, u32[]{:S(2)}, u32[]{:S(2)}) %collective-permute-start.20) | collective-permute-done | bytes 36896 | tf_op jit(solution)/shard_map/ppermute | solution.py:316
  97.5 0.1 shard_map.65
  97.6 1.4 %collective-permute-done.21.got_ref.refs_3_ = f32[392,128]{1,0:T(8,128)S(1)} collective-permute-done((f32[392,128]{1,0:T(8,128)S(1)}, f32[392,128]{1,0:T(8,128)S(1)}, u32[]{:S(2)}, u32[]{:S(2)}) %collective-permute-start.21) | collective-permute-done | bytes 200736 | tf_op jit(solution)/shard_map/ppermute | solution.py:316
  99.1 0.1 shard_map.66
  99.2 2.0 %collective-permute-start.24 = (f32[8,256]{1,0:T(8,128)S(1)}, f32[8,256]{1,0:T(8,128)S(1)}, u32[]{:S(2)}, u32[]{:S(2)}) collective-permute-start(f32[8,256]{1,0:T(8,128)S(1)} %get-tuple-element.88.known_ref.refs_4_), channel_id=1, source_target_pairs={{0,24},{8,16},{16,8},{24,0},{1,25},{9,17},{17,9},{25,1},{2,26},{10... | collective-permute-start | bytes 24584 | tf_op jit(solution)/shard_map/ppermute | solution.py:406
  101.2 1.0 collective-permute-start.23
  102.2 0.5 collective-permute-start.22
  102.7 0.8 shard_map.68
  103.6 0.2 collective-permute-done.24.refs_2_
  103.8 1.0 collective-permute-done.23.refs_1_
  104.8 1.0 collective-permute-done.22.refs_0_
  105.8 0.7 shard_map.67
  (17 shorter events, 0.2 us)
Async XLA Ops:
  0.6 5.6 %collective-permute-start.1 = (f32[1024,256]{1,0:T(8,128)}, f32[1024,256]{1,0:T(8,128)S(1)}, u32[]{:S(2)}, u32[]{:S(2)}) collective-permute-start(f32[1024,256]{1,0:T(8,128)} %own_ref.1), channel_id=1, source_target_pairs={{0,1},{1,0},{2,3},{3,2},{4,5},{5,4},{6,7},{7,6},{8,9},{9,8},{10,11... | collective-permute-start | bytes 3145736 | tf_op jit(solution)/shard_map/ppermute | solution.py:316
  1.1 40.8 %collective-permute-start = (f32[1024,256]{1,0:T(8,128)}, f32[1024,256]{1,0:T(8,128)S(1)}, u32[]{:S(2)}, u32[]{:S(2)}) collective-permute-start(f32[1024,256]{1,0:T(8,128)} %own_ref.1), channel_id=1, source_target_pairs={{0,2},{1,3},{2,0},{3,1},{4,6},{5,7},{6,4},{7,5},{8,10},{9,11},{10,... | collective-permute-start | bytes 3145736 | tf_op jit(solution)/shard_map/ppermute | solution.py:316
  4.8 1.4 %collective-permute-start.2 = (f32[256,128]{1,0:T(8,128)S(1)}, f32[256,128]{1,0:T(8,128)S(1)}, u32[]{:S(2)}, u32[]{:S(2)}) collective-permute-start(f32[256,128]{1,0:T(8,128)S(1)} %get-tuple-element.91), channel_id=1, source_target_pairs={{0,1},{1,0},{2,3},{3,2},{4,5},{5,4},{6,7},{7,6},{8,9},{9,8},{10,11... | collective-permute-start | bytes 393224 | tf_op jit(solution)/shard_map/ppermute | solution.py:316
  6.2 1.2 %copy-start = (f32[1024,256]{1,0:T(8,128)S(1)}, f32[1024,256]{1,0:T(8,128)}, u32[]{:S(2)}) copy-start(f32[1024,256]{1,0:T(8,128)} %own_ref.1) | copy-start | bytes 3145732
  8.4 32.8 %collective-permute-start.3 = (f32[1024,128]{1,0:T(8,128)S(1)}, f32[1024,128]{1,0:T(8,128)S(1)}, u32[]{:S(2)}, u32[]{:S(2)}) collective-permute-start(f32[1024,128]{1,0:T(8,128)S(1)} %get-tuple-element.47.y_ref), channel_id=1, source_target_pairs={{0,6},{1,7},{2,4},{3,5},{4,2},{5,3},{6,0},{7,1},{8,14},{9,15},{10,... | collective-permute-start | bytes 1572872 | tf_op jit(solution)/shard_map/ppermute | solution.py:316
  41.9 2.7 %collective-permute-start.5 = (f32[1024,256]{1,0:T(8,128)S(1)}, f32[1024,256]{1,0:T(8,128)S(1)}, u32[]{:S(2)}, u32[]{:S(2)}) collective-permute-start(f32[1024,256]{1,0:T(8,128)S(1)} %collective-permute-done.block_ref), channel_id=1, source_target_pairs={{0,1},{1,0},{2,3},{3,2},{4,5},{5,4},{6,7},{7,6},{8,9},{9,8},{10,11... | collective-permute-start | bytes 3145736 | tf_op jit(solution)/shard_map/ppermute | solution.py:316
  42.1 6.4 %collective-permute-start.4 = (f32[256,128]{1,0:T(8,128)S(1)}, f32[256,128]{1,0:T(8,128)S(1)}, u32[]{:S(2)}, u32[]{:S(2)}) collective-permute-start(f32[256,128]{1,0:T(8,128)S(1)} %get-tuple-element.51), channel_id=1, source_target_pairs={{0,2},{1,3},{2,0},{3,1},{4,6},{5,7},{6,4},{7,5},{8,10},{9,11},{10,... | collective-permute-start | bytes 393224 | tf_op jit(solution)/shard_map/ppermute | solution.py:316
  42.1 8.8 %collective-permute-start.12 = (f32[256,128]{1,0:T(8,128)}, f32[256,128]{1,0:T(8,128)}, u32[]{:S(2)}, u32[]{:S(2)}) collective-permute-start(f32[256,128]{1,0:T(8,128)} %get-tuple-element.70), channel_id=1, source_target_pairs={{0,2},{1,3},{2,0},{3,1},{4,6},{5,7},{6,4},{7,5},{8,10},{9,11},{10,... | collective-permute-start | bytes 393224 | tf_op jit(solution)/shard_map/ppermute | solution.py:316
  44.6 1.0 copy-start.1
  49.2 5.0 %collective-permute-start.6 = (f32[264,128]{1,0:T(8,128)S(1)}, f32[264,128]{1,0:T(8,128)S(1)}, u32[]{:S(2)}, u32[]{:S(2)}) collective-permute-start(f32[264,128]{1,0:T(8,128)S(1)} %shard_map.53), channel_id=1, source_target_pairs={{0,8},{1,17},{2,10},{3,19},{4,12},{5,21},{6,14},{7,23},{8,0},{9,25... | collective-permute-start | bytes 405512 | tf_op jit(solution)/shard_map/ppermute | solution.py:327
  52.7 7.6 %copy-start.2 = (f32[1024,256]{1,0:T(8,128)S(1)}, f32[1024,256]{1,0:T(8,128)}, u32[]{:S(2)}) copy-start(f32[1024,256]{1,0:T(8,128)} %copy-done.1) | copy-start | bytes 3145732
  52.7 6.4 %collective-permute-start.13 = (f32[264,128]{1,0:T(8,128)S(1)}, f32[264,128]{1,0:T(8,128)S(1)}, u32[]{:S(2)}, u32[]{:S(2)}) collective-permute-start(f32[264,128]{1,0:T(8,128)S(1)} %shard_map.59), channel_id=1, source_target_pairs={{0,8},{1,17},{2,10},{3,19},{4,12},{5,21},{6,14},{7,23},{8,0},{9,25... | collective-permute-start | bytes 405512 | tf_op jit(solution)/shard_map/ppermute | solution.py:327
  54.3 6.3 %collective-permute-start.7 = (f32[264,128]{1,0:T(8,128)S(1)}, f32[264,128]{1,0:T(8,128)S(1)}, u32[]{:S(2)}, u32[]{:S(2)}) collective-permute-start(f32[264,128]{1,0:T(8,128)S(1)} %add.20.refs_0_), channel_id=1, source_target_pairs={{0,16},{1,9},{2,18},{3,11},{4,20},{5,13},{6,22},{7,15},{8,24},{9,1... | collective-permute-start | bytes 405512 | tf_op jit(solution)/shard_map/ppermute | solution.py:327
  59.1 5.1 %collective-permute-start.14 = (f32[264,128]{1,0:T(8,128)S(1)}, f32[264,128]{1,0:T(8,128)S(1)}, u32[]{:S(2)}, u32[]{:S(2)}) collective-permute-start(f32[264,128]{1,0:T(8,128)S(1)} %add.22.refs_0_), channel_id=1, source_target_pairs={{0,16},{1,9},{2,18},{3,11},{4,20},{5,13},{6,22},{7,15},{8,24},{9,1... | collective-permute-start | bytes 405512 | tf_op jit(solution)/shard_map/ppermute | solution.py:327
  61.5 8.2 %collective-permute-start.8 = (f32[264,128]{1,0:T(8,128)S(1)}, f32[264,128]{1,0:T(8,128)S(1)}, u32[]{:S(2)}, u32[]{:S(2)}) collective-permute-start(f32[264,128]{1,0:T(8,128)S(1)} %get-tuple-element.65.refs_0_), channel_id=1, source_target_pairs={{0,6},{1,7},{2,4},{3,5},{4,2},{5,3},{6,0},{7,1},{8,14},{9,15},{10,... | collective-permute-start | bytes 405512 | tf_op jit(solution)/shard_map/ppermute | solution.py:316
  65.1 7.1 %collective-permute-start.15 = (f32[264,128]{1,0:T(8,128)S(1)}, f32[264,128]{1,0:T(8,128)S(1)}, u32[]{:S(2)}, u32[]{:S(2)}) collective-permute-start(f32[264,128]{1,0:T(8,128)S(1)} %get-tuple-element.71.refs_0_), channel_id=1, source_target_pairs={{0,6},{1,7},{2,4},{3,5},{4,2},{5,3},{6,0},{7,1},{8,14},{9,15},{10,... | collective-permute-start | bytes 405512 | tf_op jit(solution)/shard_map/ppermute | solution.py:316
  70.7 6.0 %collective-permute-start.9 = (f32[264,128]{1,0:T(8,128)S(1)}, f32[264,128]{1,0:T(8,128)S(1)}, u32[]{:S(2)}, u32[]{:S(2)}) collective-permute-start(f32[264,128]{1,0:T(8,128)S(1)} %get-tuple-element.66), channel_id=1, source_target_pairs={{0,8},{1,17},{2,10},{3,19},{4,12},{5,21},{6,14},{7,23},{8,0},{9,25... | collective-permute-start | bytes 405512 | tf_op jit(solution)/shard_map/ppermute | solution.py:327
  73.1 5.8 %collective-permute-start.16 = (f32[264,128]{1,0:T(8,128)S(1)}, f32[264,128]{1,0:T(8,128)S(1)}, u32[]{:S(2)}, u32[]{:S(2)}) collective-permute-start(f32[264,128]{1,0:T(8,128)S(1)} %get-tuple-element.72), channel_id=1, source_target_pairs={{0,8},{1,17},{2,10},{3,19},{4,12},{5,21},{6,14},{7,23},{8,0},{9,25... | collective-permute-start | bytes 405512 | tf_op jit(solution)/shard_map/ppermute | solution.py:327
  76.7 5.1 %collective-permute-start.10 = (f32[264,128]{1,0:T(8,128)S(1)}, f32[264,128]{1,0:T(8,128)S(1)}, u32[]{:S(2)}, u32[]{:S(2)}) collective-permute-start(f32[264,128]{1,0:T(8,128)S(1)} %add.21.refs_0_), channel_id=1, source_target_pairs={{0,16},{1,9},{2,18},{3,11},{4,20},{5,13},{6,22},{7,15},{8,24},{9,1... | collective-permute-start | bytes 405512 | tf_op jit(solution)/shard_map/ppermute | solution.py:327
  78.9 5.1 %collective-permute-start.17 = (f32[264,128]{1,0:T(8,128)S(1)}, f32[264,128]{1,0:T(8,128)S(1)}, u32[]{:S(2)}, u32[]{:S(2)}) collective-permute-start(f32[264,128]{1,0:T(8,128)S(1)} %add.23.refs_0_), channel_id=1, source_target_pairs={{0,16},{1,9},{2,18},{3,11},{4,20},{5,13},{6,22},{7,15},{8,24},{9,1... | collective-permute-start | bytes 405512 | tf_op jit(solution)/shard_map/ppermute | solution.py:327
  82.7 7.0 %collective-permute-start.11 = (f32[264,128]{1,0:T(8,128)S(1)}, f32[264,128]{1,0:T(8,128)S(1)}, u32[]{:S(2)}, u32[]{:S(2)}) collective-permute-start(f32[264,128]{1,0:T(8,128)S(1)} %get-tuple-element.67.own_ref), channel_id=1, source_target_pairs={{0,6},{1,7},{2,4},{3,5},{4,2},{5,3},{6,0},{7,1},{8,14},{9,15},{10,... | collective-permute-start | bytes 405512 | tf_op jit(solution)/shard_map/ppermute | solution.py:316
  84.9 8.4 %collective-permute-start.18 = (f32[264,128]{1,0:T(8,128)S(1)}, f32[264,128]{1,0:T(8,128)S(1)}, u32[]{:S(2)}, u32[]{:S(2)}) collective-permute-start(f32[264,128]{1,0:T(8,128)S(1)} %get-tuple-element.78.own_ref), channel_id=1, source_target_pairs={{0,6},{1,7},{2,4},{3,5},{4,2},{5,3},{6,0},{7,1},{8,14},{9,15},{10,... | collective-permute-start | bytes 405512 | tf_op jit(solution)/shard_map/ppermute | solution.py:316
  89.9 7.6 %collective-permute-start.19 = (f32[328,128]{1,0:T(8,128)S(1)}, f32[328,128]{1,0:T(8,128)S(1)}, u32[]{:S(2)}, u32[]{:S(2)}) collective-permute-start(f32[328,128]{1,0:T(8,128)S(1)} %get-tuple-element.83), channel_id=1, source_target_pairs={{0,2},{1,3},{2,0},{3,1},{4,6},{5,7},{6,4},{7,5},{8,10},{9,11},{10,... | collective-permute-start | bytes 503816 | tf_op jit(solution)/shard_map/ppermute | solution.py:316
  93.5 4.0 %collective-permute-start.20 = (f32[72,128]{1,0:T(8,128)S(1)}, f32[72,128]{1,0:T(8,128)S(1)}, u32[]{:S(2)}, u32[]{:S(2)}) collective-permute-start(f32[72,128]{1,0:T(8,128)S(1)} %get-tuple-element.84), channel_id=1, source_target_pairs={{0,2},{1,3},{2,0},{3,1},{4,6},{5,7},{6,4},{7,5},{8,10},{9,11},{10,... | collective-permute-start | bytes 110600 | tf_op jit(solution)/shard_map/ppermute | solution.py:316
  97.6 1.5 %collective-permute-start.21 = (f32[392,128]{1,0:T(8,128)S(1)}, f32[392,128]{1,0:T(8,128)S(1)}, u32[]{:S(2)}, u32[]{:S(2)}) collective-permute-start(f32[392,128]{1,0:T(8,128)S(1)} %get-tuple-element.86), channel_id=1, source_target_pairs={{0,1},{1,0},{2,3},{3,2},{4,5},{5,4},{6,7},{7,6},{8,9},{9,8},{10,11... | collective-permute-start | bytes 602120 | tf_op jit(solution)/shard_map/ppermute | solution.py:316
  99.2 4.6 %collective-permute-start.24 = (f32[8,256]{1,0:T(8,128)S(1)}, f32[8,256]{1,0:T(8,128)S(1)}, u32[]{:S(2)}, u32[]{:S(2)}) collective-permute-start(f32[8,256]{1,0:T(8,128)S(1)} %get-tuple-element.88.known_ref.refs_4_), channel_id=1, source_target_pairs={{0,24},{8,16},{16,8},{24,0},{1,25},{9,17},{17,9},{25,1},{2,26},{10... | collective-permute-start | bytes 24584 | tf_op jit(solution)/shard_map/ppermute | solution.py:406
  101.2 3.7 %collective-permute-start.23 = (f32[8,256]{1,0:T(8,128)S(1)}, f32[8,256]{1,0:T(8,128)S(1)}, u32[]{:S(2)}, u32[]{:S(2)}) collective-permute-start(f32[8,256]{1,0:T(8,128)S(1)} %get-tuple-element.88.known_ref.refs_4_), channel_id=1, source_target_pairs={{0,16},{8,24},{16,0},{24,8},{1,17},{9,25},{17,1},{25,9},{2,18},{10... | collective-permute-start | bytes 24584 | tf_op jit(solution)/shard_map/ppermute | solution.py:406
  102.2 3.7 %collective-permute-start.22 = (f32[8,256]{1,0:T(8,128)S(1)}, f32[8,256]{1,0:T(8,128)S(1)}, u32[]{:S(2)}, u32[]{:S(2)}) collective-permute-start(f32[8,256]{1,0:T(8,128)S(1)} %get-tuple-element.88.known_ref.refs_4_), channel_id=1, source_target_pairs={{0,8},{8,0},{16,24},{24,16},{1,9},{9,1},{17,25},{25,17},{2,10},{10... | collective-permute-start | bytes 24584 | tf_op jit(solution)/shard_map/ppermute | solution.py:406

commit v12 on v11

--- a/solution.py
+++ b/solution.py
@@ -93,7 +93,8 @@
         start += size
 
 
-def near_kernel(own_ref, core_ref, near_ref, got_ref, y_ref, high_ref, low_ref, high_t_ref, low_t_ref):
+def near_kernel(own_ref, core_ref, near_ref, got_ref, y_ref, *refs):
+    high_ref, low_ref, high_t_ref, low_t_ref = refs
     blocks = (own_ref[...], core_ref[...])
     store_factors(high_ref, low_ref, blocks)
     store_factors(high_t_ref, low_t_ref, [block.T for block in blocks], 0)
@@ -112,18 +113,35 @@
                 y_ref[at : at + COLS, :] = x[h * COLS : (h + 1) * COLS]
 
 
-def cross_kernel(y_ref, got_ref, *refs):
+def pack_kernel(own_ref, y_ref, first_ref, second_ref, rest_ref):
+    core = position()[0]
+    part = rest_ref.shape[0]
+    rest_ref[...] = own_ref[own_ref.shape[0] - part :, :]
+    middle = wide_rows(own_ref[part : own_ref.shape[0] - part, :])
+    y = y_ref[...]
+    first_ref[...] = jnp.where(core == 0, middle, y)
+    second_ref[...] = jnp.where(core == 0, y, middle)
+
+
+def wide_rows(x):
+    return jnp.concatenate([x[:, :LANES], x[:, LANES:]], axis=0)
+
+
+def cross_kernel(y_ref, first_ref, second_ref, side_ref, *refs):
+    zero = position()[0] == 0
+    middle = jnp.where(zero, first_ref[...], second_ref[...])
+    count = side_ref.shape[0]
+    side_ref[:, :LANES] = middle[:count]
+    side_ref[:, LANES:] = middle[count:]
+    total = y_ref[...] + jnp.where(zero, second_ref[...], first_ref[...])
     for i, ref in enumerate(refs):
-        cut = slice(i * ref.shape[0], (i + 1) * ref.shape[0])
-        ref[...] = y_ref[cut, :] + got_ref[cut, :]
-
-
-def split_kernel(block_ref, high_ref, low_ref):
-    store_factors(high_ref, low_ref, (block_ref[...],))
-
-
-def turned_kernel(block_ref, high_ref, low_ref):
-    store_factors(high_ref, low_ref, (block_ref[...].T,), 0)
+        ref[...] = total[i * ref.shape[0] : (i + 1) * ref.shape[0]]
+
+
+def split_kernel(*refs):
+    blocks, (high_ref, low_ref, high_t_ref, low_t_ref) = [ref[...] for ref in refs[:-4]], refs[-4:]
+    store_factors(high_ref, low_ref, blocks, 0)
+    store_factors(high_t_ref, low_t_ref, [block.T for block in blocks], 1)
 
 
 def send_z(y, high_refs, low_refs, z_ref):
@@ -273,7 +291,7 @@
         out_specs=[out_spec] * len(outs),
         scratch_shapes=scratch,
         cost_estimate=cost,
-        compiler_params=pltpu.CompilerParams(vmem_limit_bytes=16 * 1024 * 1024),
+        compiler_params=pltpu.CompilerParams(vmem_limit_bytes=10 * 1024 * 1024),
     )(*args)
 
 
@@ -340,24 +358,35 @@
         return lax.dynamic_slice_in_dim(sketch, index * LANES, LANES, 1)
 
     core = lax.rem(lax.axis_index("snap"), 2)
-    side_block = swap_side(snapshots)
+    def mixed(x, first):
+        return lax.ppermute(x, "snap", [(i, i ^ (2 if i % 2 == first else 6)) for i in range(places)])
+
+    part = rows // 4
     half_rows = rows // LANES * COLS
+    sums_shape = ((2 * HALVES * half_rows, LANES), F32)
+    side_first = swap_side(snapshots[:part])
     y_near, *near = call(
         near_kernel,
-        [((2 * HALVES * half_rows, LANES), F32)] + factor(2) + factor_t(2),
+        [sums_shape] + factor(2) + factor_t(2),
         snapshots, swap_core(snapshots), sketch_half(core), swap_core(sketch_half(1 - core)),
     )
-    sums = call(cross_kernel, [((half_rows, LANES), F32)] * 2 * HALVES, y_near, swap_pair(y_near))
+    side_first, y_near = lax.optimization_barrier((side_first, y_near))
+    first, second, rest = call(pack_kernel, [sums_shape] * 2 + [((part, width), F32)], snapshots, y_near)
+    first, second = mixed(first, 0), mixed(second, 1)
+    side_rest = swap_side(rest)
+    side_middle, *sums = call(
+        cross_kernel,
+        [((2 * part, width), F32)] + [((half_rows, LANES), F32)] * 2 * HALVES,
+        y_near, first, second,
+    )
     own, others = sums[:HALVES], sums[HALVES:]
     got = [swap_side(other) for other in others]
-    side_block, *own = lax.optimization_barrier((side_block, *own))
-    side = call(split_kernel, factor(1), side_block)
-    side_t = call(turned_kernel, factor_t(1), side_block)
-    diagonal = swap_core(side_block)
-    far = call(split_kernel, factor(1), diagonal, cost=LONG)
-    far_t = call(turned_kernel, factor_t(1), diagonal)
+    side_blocks = (side_first, side_middle, side_rest)
+    side = call(split_kernel, factor(1) + factor_t(1), *side_blocks)
+    diagonals = [swap_core(block) for block in side_blocks]
+    far = call(split_kernel, factor(1) + factor_t(1), *diagonals, cost=LONG)
     matrix = (near[0], side[0], far[0], near[1], side[1], far[1])
-    matrix_t = (near[2], side_t[0], far_t[0], near[3], side_t[1], far_t[1])
+    matrix_t = (near[2], side[2], far[2], near[3], side[3], far[3])
 
     flat = (COLS * rows // LANES + TILE, LANES)
     sent_shape = ((COLS * 4 * width // LANES + TILE, LANES), F32)

time: 107 us -> 108 us (level)
  starting transfers between devices: 34.7 us -> 46.4 us
  waiting for transfers between devices: 55.1 us -> 45.9 us
  local copies, waits for them, and re-layouts: 3.07 us -> 1.96 us
    ppermute x14 -> x16, waiting for transfers between devices: 44.2 us -> 15.6 us  [swap(): return lax.ppermute(x, 'snap', [(i, i ^ bits) for i in range(places)])]
    ppermute x0 -> x2, waiting for transfers between devices: none -> 23.4 us  [mixed(): lax.ppermute(x, 'snap', [(i, i ^ (2 if i % 2 == first else 6)) for i in r...]
    ppermute x14 -> x16, starting transfers between devices: 19.4 us -> 25.1 us  [swap(): return lax.ppermute(x, 'snap', [(i, i ^ bits) for i in range(places)])]
    ppermute x0 -> x2, starting transfers between devices: none -> 4.29 us  [mixed(): lax.ppermute(x, 'snap', [(i, i ^ (2 if i % 2 == first else 6)) for i in r...]
    ppermute x8, waiting for transfers between devices: 8.66 us -> 4.62 us  [swap_cell(): return lax.ppermute(x, ('cell', 'snap'), perm)]
    unnamed x6 -> x2, local copies, waits for them, and re-layouts: 2.09 us -> 0.01 us
    ppermute x8, starting transfers between devices: 11.7 us -> 13.4 us  [swap_cell(): return lax.ppermute(x, ('cell', 'snap'), perm)]
    pallas_call x20 -> x19, Pallas kernels: 12.8 us -> 12.7 us  [call(): pl.pallas_call(kernel, out_shape=[jax.ShapeDtypeStruct(shape, dtype) for...]
  transfers between devices with their start and end apart: 25 -> 29, of which waited for: 19 -> 20; matrix products, arithmetic and copies ran while one was open for 1% -> 2% of each run, Pallas kernels for 11% -> 11%
where the time goes in v12:
time: 108 us
  starting transfers between devices  46.4 us (43%)
  waiting for transfers between devices  45.9 us (42%)
  Pallas kernels  12.7 us (12%)
  local copies, waits for them, and re-layouts  1.96 us (2%)
    ppermute x16, starting transfers between devices, swap(): return lax.ppermute(x, 'snap', [(i, i ^ bits) for i in range(places)])  25.1 us
    ppermute x2, waiting for transfers between devices, mixed(): lax.ppermute(x, 'snap', [(i, i ^ (2 if i % 2 == first else 6)) for i in r...  23.4 us
    ppermute x16, waiting for transfers between devices, swap(): return lax.ppermute(x, 'snap', [(i, i ^ bits) for i in range(places)])  15.6 us
    ppermute x8, starting transfers between devices, swap_cell(): return lax.ppermute(x, ('cell', 'snap'), perm)  13.4 us
    pallas_call x19, Pallas kernels, call(): pl.pallas_call(kernel, out_shape=[jax.ShapeDtypeStruct(shape, dtype) for...  12.7 us
    ppermute x8, waiting for transfers between devices, swap_cell(): return lax.ppermute(x, ('cell', 'snap'), perm)  4.62 us
    ppermute x2, starting transfers between devices, mixed(): lax.ppermute(x, 'snap', [(i, i ^ (2 if i % 2 == first else 6)) for i in r...  4.29 us
    ppermute x3, starting transfers between devices, local(): lax.ppermute(known, 'cell', [(c, c ^ d) for c in range(groups)])  3.55 us
  transfers between devices with their start and end apart: 29, of which 20 were waited for; matrix products, arithmetic and copies ran while one was open for 2% of the time, Pallas kernels for 11%

profile of v12, /device:TPU:0, one launch (start us, length us, event | category | flops | bytes accessed | tf_op | source)
XLA Modules:
  0.0 107.8 jit_solution(10430727182410422839)
XLA Ops:
  0.6 0.5 collective-permute-start.1
  1.2 1.0 slice.3
  2.1 2.7 %collective-permute-start = (f32[256,256]{1,0:T(8,128)S(1)}, f32[256,256]{1,0:T(8,128)S(1)}, u32[]{:S(2)}, u32[]{:S(2)}) collective-permute-start(f32[256,256]{1,0:T(8,128)S(1)} %slice.3), channel_id=1, source_target_pairs={{0,2},{1,3},{2,0},{3,1},{4,6},{5,7},{6,4},{7,5},{8,10},{9,11},{10,... | collective-permute-start | bytes 786440 | tf_op jit(solution)/shard_map/ppermute | solution.py:334
  4.9 1.0 constant_dynamic-slice_fusion
  5.8 0.2 collective-permute-start.2
  6.1 1.2 %collective-permute-done.2.got_ref = f32[256,128]{1,0:T(8,128)S(1)} collective-permute-done((f32[256,128]{1,0:T(8,128)S(1)}, f32[256,128]{1,0:T(8,128)S(1)}, u32[]{:S(2)}, u32[]{:S(2)}) %collective-permute-start.2) | collective-permute-done | bytes 131104 | tf_op jit(solution)/shard_map/ppermute | solution.py:334
  7.3 1.0 shard_map.49
  8.3 3.5 %collective-permute-done.refs_0_ = f32[256,256]{1,0:T(8,128)S(1)} collective-permute-done((f32[256,256]{1,0:T(8,128)S(1)}, f32[256,256]{1,0:T(8,128)S(1)}, u32[]{:S(2)}, u32[]{:S(2)}) %collective-permute-start) | collective-permute-done | bytes 262176 | tf_op jit(solution)/shard_map/ppermute | solution.py:334
  11.8 1.8 %collective-permute-start.3 = (f32[1024,128]{1,0:T(8,128)S(1)}, f32[1024,128]{1,0:T(8,128)S(1)}, u32[]{:S(2)}, u32[]{:S(2)}) collective-permute-start(f32[1024,128]{1,0:T(8,128)S(1)} %get-tuple-element.52), channel_id=1, source_target_pairs={{0,2},{1,7},{2,0},{3,5},{4,6},{5,3},{6,4},{7,1},{8,10},{9,15},{10,... | collective-permute-start | bytes 1572872 | tf_op jit(solution)/shard_map/ppermute | solution.py:362
  13.7 2.5 %collective-permute-start.4 = (f32[1024,128]{1,0:T(8,128)S(1)}, f32[1024,128]{1,0:T(8,128)S(1)}, u32[]{:S(2)}, u32[]{:S(2)}) collective-permute-start(f32[1024,128]{1,0:T(8,128)S(1)} %get-tuple-element.53), channel_id=1, source_target_pairs={{0,6},{1,3},{2,4},{3,1},{4,2},{5,7},{6,0},{7,5},{8,14},{9,11},{10,... | collective-permute-start | bytes 1572872 | tf_op jit(solution)/shard_map/ppermute | solution.py:362
  16.1 0.7 collective-permute-start.6
  16.8 17.0 %collective-permute-done.3.first_ref = f32[1024,128]{1,0:T(8,128)S(1)} collective-permute-done((f32[1024,128]{1,0:T(8,128)S(1)}, f32[1024,128]{1,0:T(8,128)S(1)}, u32[]{:S(2)}, u32[]{:S(2)}) %collective-permute-start.3) | collective-permute-done | bytes 524320 | tf_op jit(solution)/shard_map/ppermute | solution.py:362
  33.8 6.4 %collective-permute-done.4.second_ref = f32[1024,128]{1,0:T(8,128)S(1)} collective-permute-done((f32[1024,128]{1,0:T(8,128)S(1)}, f32[1024,128]{1,0:T(8,128)S(1)}, u32[]{:S(2)}, u32[]{:S(2)}) %collective-permute-start.4) | collective-permute-done | bytes 524320 | tf_op jit(solution)/shard_map/ppermute | solution.py:362
  40.2 0.8 shard_map.51
  41.0 0.5 collective-permute-start.7
  41.5 1.1 %collective-permute-done.6.refs_2_ = f32[256,256]{1,0:T(8,128)S(1)} collective-permute-done((f32[256,256]{1,0:T(8,128)S(1)}, f32[256,256]{1,0:T(8,128)S(1)}, u32[]{:S(2)}, u32[]{:S(2)}) %collective-permute-start.6) | collective-permute-done | bytes 262176 | tf_op jit(solution)/shard_map/ppermute | solution.py:334
  42.6 0.8 collective-permute-start.9
  43.4 1.8 %collective-permute-start.5 = (f32[256,128]{1,0:T(8,128)S(1)}, f32[256,128]{1,0:T(8,128)S(1)}, u32[]{:S(2)}, u32[]{:S(2)}) collective-permute-start(f32[256,128]{1,0:T(8,128)S(1)} %get-tuple-element.55), channel_id=1, source_target_pairs={{0,2},{1,3},{2,0},{3,1},{4,6},{5,7},{6,4},{7,5},{8,10},{9,11},{10,... | collective-permute-start | bytes 393224 | tf_op jit(solution)/shard_map/ppermute | solution.py:334
  45.1 0.3 collective-permute-start.16
  45.4 0.4 shard_map.52
  45.8 0.4 shard_map.53
  46.2 3.5 %collective-permute-done.5.b_ref = f32[256,128]{1,0:T(8,128)S(1)} collective-permute-done((f32[256,128]{1,0:T(8,128)S(1)}, f32[256,128]{1,0:T(8,128)S(1)}, u32[]{:S(2)}, u32[]{:S(2)}) %collective-permute-start.5) | collective-permute-done | bytes 131104 | tf_op jit(solution)/shard_map/ppermute | solution.py:334
  49.7 0.8 shard_map.54
  50.6 1.7 %collective-permute-start.10 = (f32[264,128]{1,0:T(8,128)S(1)}, f32[264,128]{1,0:T(8,128)S(1)}, u32[]{:S(2)}, u32[]{:S(2)}) collective-permute-start(f32[264,128]{1,0:T(8,128)S(1)} %shard_map.54), channel_id=1, source_target_pairs={{0,8},{1,17},{2,10},{3,19},{4,12},{5,21},{6,14},{7,23},{8,0},{9,25... | collective-permute-start | bytes 405512 | tf_op jit(solution)/shard_map/ppermute | solution.py:345
  52.3 1.7 %shard_map.58 = f32[264,128]{1,0:T(8,128)S(1)} custom-call(f32[256,128]{1,0:T(8,128)S(1)} %get-tuple-element.75.a_ref, f32[256,128]{1,0:T(8,128)} %collective-permute-done.16.b_ref, bf16[1024,512]{1,0:T(8,128)(2,1)S(1)} %get-tuple-element.56.refs_0_.refs_2_, bf16[1024,256]{1,0:T(8,128)(2,1)S(1)} %get-tuple-element.60.refs_1_.refs_3_, ...), custom_call_target="tpu_custom_call" | custom-call | flops 99999997952 | bytes 268435456 | tf_op jit(solution)/shard_map/pallas_call | solution.py:287
  54.0 1.1 %collective-permute-start.17 = (f32[264,128]{1,0:T(8,128)S(1)}, f32[264,128]{1,0:T(8,128)S(1)}, u32[]{:S(2)}, u32[]{:S(2)}) collective-permute-start(f32[264,128]{1,0:T(8,128)S(1)} %shard_map.58), channel_id=1, source_target_pairs={{0,8},{1,17},{2,10},{3,19},{4,12},{5,21},{6,14},{7,23},{8,0},{9,25... | collective-permute-start | bytes 405512 | tf_op jit(solution)/shard_map/ppermute | solution.py:345
  55.1 0.5 collective-permute-done.10
  55.6 1.9 %collective-permute-start.11 = (f32[264,128]{1,0:T(8,128)S(1)}, f32[264,128]{1,0:T(8,128)S(1)}, u32[]{:S(2)}, u32[]{:S(2)}) collective-permute-start(f32[264,128]{1,0:T(8,128)S(1)} %add.20.refs_0_), channel_id=1, source_target_pairs={{0,16},{1,9},{2,18},{3,11},{4,20},{5,13},{6,22},{7,15},{8,24},{9,1... | collective-permute-start | bytes 405512 | tf_op jit(solution)/shard_map/ppermute | solution.py:345
  57.5 2.4 %collective-permute-done.17 = f32[264,128]{1,0:T(8,128)S(1)} collective-permute-done((f32[264,128]{1,0:T(8,128)S(1)}, f32[264,128]{1,0:T(8,128)S(1)}, u32[]{:S(2)}, u32[]{:S(2)}) %collective-permute-start.17) | collective-permute-done | bytes 135200 | tf_op jit(solution)/shard_map/ppermute | solution.py:345
  59.9 0.7 collective-permute-start.18
  60.7 0.9 shard_map.55
  61.6 3.2 %collective-permute-start.12 = (f32[264,128]{1,0:T(8,128)S(1)}, f32[264,128]{1,0:T(8,128)S(1)}, u32[]{:S(2)}, u32[]{:S(2)}) collective-permute-start(f32[264,128]{1,0:T(8,128)S(1)} %get-tuple-element.71.refs_0_), channel_id=1, source_target_pairs={{0,6},{1,7},{2,4},{3,5},{4,2},{5,3},{6,0},{7,1},{8,14},{9,15},{10,... | collective-permute-start | bytes 405512 | tf_op jit(solution)/shard_map/ppermute | solution.py:334
  64.8 0.2 collective-permute-done.18.refs_1_
  65.0 0.9 shard_map.59
  65.9 3.2 %collective-permute-start.19 = (f32[264,128]{1,0:T(8,128)S(1)}, f32[264,128]{1,0:T(8,128)S(1)}, u32[]{:S(2)}, u32[]{:S(2)}) collective-permute-start(f32[264,128]{1,0:T(8,128)S(1)} %get-tuple-element.77.refs_0_), channel_id=1, source_target_pairs={{0,6},{1,7},{2,4},{3,5},{4,2},{5,3},{6,0},{7,1},{8,14},{9,15},{10,... | collective-permute-start | bytes 405512 | tf_op jit(solution)/shard_map/ppermute | solution.py:334
  69.1 0.9 shard_map.56
  70.0 1.5 %collective-permute-start.13 = (f32[264,128]{1,0:T(8,128)S(1)}, f32[264,128]{1,0:T(8,128)S(1)}, u32[]{:S(2)}, u32[]{:S(2)}) collective-permute-start(f32[264,128]{1,0:T(8,128)S(1)} %get-tuple-element.72), channel_id=1, source_target_pairs={{0,8},{1,17},{2,10},{3,19},{4,12},{5,21},{6,14},{7,23},{8,0},{9,25... | collective-permute-start | bytes 405512 | tf_op jit(solution)/shard_map/ppermute | solution.py:345
  71.5 1.4 %collective-permute-done.19.refs_1_ = f32[264,128]{1,0:T(8,128)S(1)} collective-permute-done((f32[264,128]{1,0:T(8,128)S(1)}, f32[264,128]{1,0:T(8,128)S(1)}, u32[]{:S(2)}, u32[]{:S(2)}) %collective-permute-start.19) | collective-permute-done | bytes 135200 | tf_op jit(solution)/shard_map/ppermute | solution.py:334
  72.9 0.9 shard_map.60
  73.8 1.4 %collective-permute-start.20 = (f32[264,128]{1,0:T(8,128)S(1)}, f32[264,128]{1,0:T(8,128)S(1)}, u32[]{:S(2)}, u32[]{:S(2)}) collective-permute-start(f32[264,128]{1,0:T(8,128)S(1)} %get-tuple-element.78), channel_id=1, source_target_pairs={{0,8},{1,17},{2,10},{3,19},{4,12},{5,21},{6,14},{7,23},{8,0},{9,25... | collective-permute-start | bytes 405512 | tf_op jit(solution)/shard_map/ppermute | solution.py:345
  75.1 3.6 %collective-permute-start.14 = (f32[264,128]{1,0:T(8,128)S(1)}, f32[264,128]{1,0:T(8,128)S(1)}, u32[]{:S(2)}, u32[]{:S(2)}) collective-permute-start(f32[264,128]{1,0:T(8,128)S(1)} %add.21.refs_0_), channel_id=1, source_target_pairs={{0,16},{1,9},{2,18},{3,11},{4,20},{5,13},{6,22},{7,15},{8,24},{9,1... | collective-permute-start | bytes 405512 | tf_op jit(solution)/shard_map/ppermute | solution.py:345
  78.8 0.7 collective-permute-done.20
  79.5 1.5 %collective-permute-start.21 = (f32[264,128]{1,0:T(8,128)S(1)}, f32[264,128]{1,0:T(8,128)S(1)}, u32[]{:S(2)}, u32[]{:S(2)}) collective-permute-start(f32[264,128]{1,0:T(8,128)S(1)} %add.23.refs_0_), channel_id=1, source_target_pairs={{0,16},{1,9},{2,18},{3,11},{4,20},{5,13},{6,22},{7,15},{8,24},{9,1... | collective-permute-start | bytes 405512 | tf_op jit(solution)/shard_map/ppermute | solution.py:345
  81.0 0.7 collective-permute-done.14.refs_1_
  81.8 0.9 shard_map.57
  82.7 3.6 %collective-permute-start.15 = (f32[264,128]{1,0:T(8,128)S(1)}, f32[264,128]{1,0:T(8,128)S(1)}, u32[]{:S(2)}, u32[]{:S(2)}) collective-permute-start(f32[264,128]{1,0:T(8,128)S(1)} %get-tuple-element.73.own_ref), channel_id=1, source_target_pairs={{0,6},{1,7},{2,4},{3,5},{4,2},{5,3},{6,0},{7,1},{8,14},{9,15},{10,... | collective-permute-start | bytes 405512 | tf_op jit(solution)/shard_map/ppermute | solution.py:334
  86.3 0.9 shard_map.61
  87.2 2.0 %collective-permute-start.22 = (f32[264,128]{1,0:T(8,128)S(1)}, f32[264,128]{1,0:T(8,128)S(1)}, u32[]{:S(2)}, u32[]{:S(2)}) collective-permute-start(f32[264,128]{1,0:T(8,128)S(1)} %get-tuple-element.84.own_ref), channel_id=1, source_target_pairs={{0,6},{1,7},{2,4},{3,5},{4,2},{5,3},{6,0},{7,1},{8,14},{9,15},{10,... | collective-permute-start | bytes 405512 | tf_op jit(solution)/shard_map/ppermute | solution.py:334
  89.2 1.1 %collective-permute-done.15.got_ref = f32[264,128]{1,0:T(8,128)S(1)} collective-permute-done((f32[264,128]{1,0:T(8,128)S(1)}, f32[264,128]{1,0:T(8,128)S(1)}, u32[]{:S(2)}, u32[]{:S(2)}) %collective-permute-start.15) | collective-permute-done | bytes 135200 | tf_op jit(solution)/shard_map/ppermute | solution.py:334
  90.3 0.2 shard_map.62
  90.5 3.9 %collective-permute-start.23 = (f32[328,128]{1,0:T(8,128)S(1)}, f32[328,128]{1,0:T(8,128)S(1)}, u32[]{:S(2)}, u32[]{:S(2)}) collective-permute-start(f32[328,128]{1,0:T(8,128)S(1)} %get-tuple-element.89), channel_id=1, source_target_pairs={{0,2},{1,3},{2,0},{3,1},{4,6},{5,7},{6,4},{7,5},{8,10},{9,11},{10,... | collective-permute-start | bytes 503816 | tf_op jit(solution)/shard_map/ppermute | solution.py:334
  94.3 0.2 collective-permute-done.22.got_ref
  94.6 0.2 shard_map.63
  94.8 1.8 %collective-permute-start.24 = (f32[72,128]{1,0:T(8,128)S(1)}, f32[72,128]{1,0:T(8,128)S(1)}, u32[]{:S(2)}, u32[]{:S(2)}) collective-permute-start(f32[72,128]{1,0:T(8,128)S(1)} %get-tuple-element.90), channel_id=1, source_target_pairs={{0,2},{1,3},{2,0},{3,1},{4,6},{5,7},{6,4},{7,5},{8,10},{9,11},{10,... | collective-permute-start | bytes 110600 | tf_op jit(solution)/shard_map/ppermute | solution.py:334
  96.6 2.2 %collective-permute-done.24.refs_3_ = f32[72,128]{1,0:T(8,128)S(1)} collective-permute-done((f32[72,128]{1,0:T(8,128)S(1)}, f32[72,128]{1,0:T(8,128)S(1)}, u32[]{:S(2)}, u32[]{:S(2)}) %collective-permute-start.24) | collective-permute-done | bytes 36896 | tf_op jit(solution)/shard_map/ppermute | solution.py:334
  98.9 1.4 %collective-permute-done.25.got_ref.refs_3_ = f32[392,128]{1,0:T(8,128)S(1)} collective-permute-done((f32[392,128]{1,0:T(8,128)S(1)}, f32[392,128]{1,0:T(8,128)S(1)}, u32[]{:S(2)}, u32[]{:S(2)}) %collective-permute-start.25) | collective-permute-done | bytes 200736 | tf_op jit(solution)/shard_map/ppermute | solution.py:334
  100.4 2.9 %collective-permute-start.28 = (f32[8,256]{1,0:T(8,128)S(1)}, f32[8,256]{1,0:T(8,128)S(1)}, u32[]{:S(2)}, u32[]{:S(2)}) collective-permute-start(f32[8,256]{1,0:T(8,128)S(1)} %get-tuple-element.94.known_ref.refs_4_), channel_id=1, source_target_pairs={{0,24},{8,16},{16,8},{24,0},{1,25},{9,17},{17,9},{25,1},{2,26},{10... | collective-permute-start | bytes 24584 | tf_op jit(solution)/shard_map/ppermute | solution.py:435
  103.3 0.1 collective-permute-start.27
  103.5 0.5 collective-permute-start.26
  104.0 0.8 shard_map.67
  104.8 0.2 collective-permute-done.28.refs_2_
  105.1 1.9 %collective-permute-done.27.refs_1_ = f32[8,256]{1,0:T(8,128)S(1)} collective-permute-done((f32[8,256]{1,0:T(8,128)S(1)}, f32[8,256]{1,0:T(8,128)S(1)}, u32[]{:S(2)}, u32[]{:S(2)}) %collective-permute-start.27) | collective-permute-done | bytes 8224 | tf_op jit(solution)/shard_map/ppermute | solution.py:435
  107.0 0.1 collective-permute-done.26.refs_0_
  107.1 0.7 shard_map.66
  (21 shorter events, 0.5 us)
Async XLA Ops:
  0.6 6.6 %copy-start = (f32[1024,256]{1,0:T(8,128)S(1)}, f32[1024,256]{1,0:T(8,128)}, u32[]{:S(2)}) copy-start(f32[1024,256]{1,0:T(8,128)} %own_ref.3) | copy-start | bytes 3145732
  0.6 6.6 %collective-permute-start.1 = (f32[1024,256]{1,0:T(8,128)}, f32[1024,256]{1,0:T(8,128)S(1)}, u32[]{:S(2)}, u32[]{:S(2)}) collective-permute-start(f32[1024,256]{1,0:T(8,128)} %own_ref.3), channel_id=1, source_target_pairs={{0,1},{1,0},{2,3},{3,2},{4,5},{5,4},{6,7},{7,6},{8,9},{9,8},{10,11... | collective-permute-start | bytes 3145736 | tf_op jit(solution)/shard_map/ppermute | solution.py:334
  2.1 9.6 %collective-permute-start = (f32[256,256]{1,0:T(8,128)S(1)}, f32[256,256]{1,0:T(8,128)S(1)}, u32[]{:S(2)}, u32[]{:S(2)}) collective-permute-start(f32[256,256]{1,0:T(8,128)S(1)} %slice.3), channel_id=1, source_target_pairs={{0,2},{1,3},{2,0},{3,1},{4,6},{5,7},{6,4},{7,5},{8,10},{9,11},{10,... | collective-permute-start | bytes 786440 | tf_op jit(solution)/shard_map/ppermute | solution.py:334
  5.8 1.4 %collective-permute-start.2 = (f32[256,128]{1,0:T(8,128)S(1)}, f32[256,128]{1,0:T(8,128)S(1)}, u32[]{:S(2)}, u32[]{:S(2)}) collective-permute-start(f32[256,128]{1,0:T(8,128)S(1)} %get-tuple-element.97), channel_id=1, source_target_pairs={{0,1},{1,0},{2,3},{3,2},{4,5},{5,4},{6,7},{7,6},{8,9},{9,8},{10,11... | collective-permute-start | bytes 393224 | tf_op jit(solution)/shard_map/ppermute | solution.py:334
  11.8 21.9 %collective-permute-start.3 = (f32[1024,128]{1,0:T(8,128)S(1)}, f32[1024,128]{1,0:T(8,128)S(1)}, u32[]{:S(2)}, u32[]{:S(2)}) collective-permute-start(f32[1024,128]{1,0:T(8,128)S(1)} %get-tuple-element.52), channel_id=1, source_target_pairs={{0,2},{1,7},{2,0},{3,5},{4,6},{5,3},{6,4},{7,1},{8,10},{9,15},{10,... | collective-permute-start | bytes 1572872 | tf_op jit(solution)/shard_map/ppermute | solution.py:362
  13.7 26.6 %collective-permute-start.4 = (f32[1024,128]{1,0:T(8,128)S(1)}, f32[1024,128]{1,0:T(8,128)S(1)}, u32[]{:S(2)}, u32[]{:S(2)}) collective-permute-start(f32[1024,128]{1,0:T(8,128)S(1)} %get-tuple-element.53), channel_id=1, source_target_pairs={{0,6},{1,3},{2,4},{3,1},{4,2},{5,7},{6,0},{7,5},{8,14},{9,11},{10,... | collective-permute-start | bytes 1572872 | tf_op jit(solution)/shard_map/ppermute | solution.py:362
  16.1 26.5 %collective-permute-start.6 = (f32[256,256]{1,0:T(8,128)S(1)}, f32[256,256]{1,0:T(8,128)S(1)}, u32[]{:S(2)}, u32[]{:S(2)}) collective-permute-start(f32[256,256]{1,0:T(8,128)S(1)} %get-tuple-element.59), channel_id=1, source_target_pairs={{0,2},{1,3},{2,0},{3,1},{4,6},{5,7},{6,4},{7,5},{8,10},{9,11},{10,... | collective-permute-start | bytes 786440 | tf_op jit(solution)/shard_map/ppermute | solution.py:334
  41.0 4.8 %collective-permute-start.8 = (f32[512,256]{1,0:T(8,128)S(1)}, f32[512,256]{1,0:T(8,128)S(1)}, u32[]{:S(2)}, u32[]{:S(2)}) collective-permute-start(f32[512,256]{1,0:T(8,128)S(1)} %get-tuple-element.58.refs_1_), channel_id=1, source_target_pairs={{0,1},{1,0},{2,3},{3,2},{4,5},{5,4},{6,7},{7,6},{8,9},{9,8},{10,11... | collective-permute-start | bytes 1572872 | tf_op jit(solution)/shard_map/ppermute | solution.py:334
  41.0 4.8 %collective-permute-start.7 = (f32[256,256]{1,0:T(8,128)S(1)}, f32[256,256]{1,0:T(8,128)S(1)}, u32[]{:S(2)}, u32[]{:S(2)}) collective-permute-start(f32[256,256]{1,0:T(8,128)S(1)} %collective-permute-done.refs_0_), channel_id=1, source_target_pairs={{0,1},{1,0},{2,3},{3,2},{4,5},{5,4},{6,7},{7,6},{8,9},{9,8},{10,11... | collective-permute-start | bytes 786440 | tf_op jit(solution)/shard_map/ppermute | solution.py:334
  42.6 3.2 %collective-permute-start.9 = (f32[256,256]{1,0:T(8,128)S(1)}, f32[256,256]{1,0:T(8,128)S(1)}, u32[]{:S(2)}, u32[]{:S(2)}) collective-permute-start(f32[256,256]{1,0:T(8,128)S(1)} %collective-permute-done.6.refs_2_), channel_id=1, source_target_pairs={{0,1},{1,0},{2,3},{3,2},{4,5},{5,4},{6,7},{7,6},{8,9},{9,8},{10,11... | collective-permute-start | bytes 786440 | tf_op jit(solution)/shard_map/ppermute | solution.py:334
  43.4 6.4 %collective-permute-start.5 = (f32[256,128]{1,0:T(8,128)S(1)}, f32[256,128]{1,0:T(8,128)S(1)}, u32[]{:S(2)}, u32[]{:S(2)}) collective-permute-start(f32[256,128]{1,0:T(8,128)S(1)} %get-tuple-element.55), channel_id=1, source_target_pairs={{0,2},{1,3},{2,0},{3,1},{4,6},{5,7},{6,4},{7,5},{8,10},{9,11},{10,... | collective-permute-start | bytes 393224 | tf_op jit(solution)/shard_map/ppermute | solution.py:334
  45.1 7.1 %collective-permute-start.16 = (f32[256,128]{1,0:T(8,128)}, f32[256,128]{1,0:T(8,128)}, u32[]{:S(2)}, u32[]{:S(2)}) collective-permute-start(f32[256,128]{1,0:T(8,128)} %get-tuple-element.76), channel_id=1, source_target_pairs={{0,2},{1,3},{2,0},{3,1},{4,6},{5,7},{6,4},{7,5},{8,10},{9,11},{10,... | collective-permute-start | bytes 393224 | tf_op jit(solution)/shard_map/ppermute | solution.py:334
  50.6 5.0 %collective-permute-start.10 = (f32[264,128]{1,0:T(8,128)S(1)}, f32[264,128]{1,0:T(8,128)S(1)}, u32[]{:S(2)}, u32[]{:S(2)}) collective-permute-start(f32[264,128]{1,0:T(8,128)S(1)} %shard_map.54), channel_id=1, source_target_pairs={{0,8},{1,17},{2,10},{3,19},{4,12},{5,21},{6,14},{7,23},{8,0},{9,25... | collective-permute-start | bytes 405512 | tf_op jit(solution)/shard_map/ppermute | solution.py:345
  54.0 5.9 %collective-permute-start.17 = (f32[264,128]{1,0:T(8,128)S(1)}, f32[264,128]{1,0:T(8,128)S(1)}, u32[]{:S(2)}, u32[]{:S(2)}) collective-permute-start(f32[264,128]{1,0:T(8,128)S(1)} %shard_map.58), channel_id=1, source_target_pairs={{0,8},{1,17},{2,10},{3,19},{4,12},{5,21},{6,14},{7,23},{8,0},{9,25... | collective-permute-start | bytes 405512 | tf_op jit(solution)/shard_map/ppermute | solution.py:345
  55.6 5.1 %collective-permute-start.11 = (f32[264,128]{1,0:T(8,128)S(1)}, f32[264,128]{1,0:T(8,128)S(1)}, u32[]{:S(2)}, u32[]{:S(2)}) collective-permute-start(f32[264,128]{1,0:T(8,128)S(1)} %add.20.refs_0_), channel_id=1, source_target_pairs={{0,16},{1,9},{2,18},{3,11},{4,20},{5,13},{6,22},{7,15},{8,24},{9,1... | collective-permute-start | bytes 405512 | tf_op jit(solution)/shard_map/ppermute | solution.py:345
  59.9 5.1 %collective-permute-start.18 = (f32[264,128]{1,0:T(8,128)S(1)}, f32[264,128]{1,0:T(8,128)S(1)}, u32[]{:S(2)}, u32[]{:S(2)}) collective-permute-start(f32[264,128]{1,0:T(8,128)S(1)} %add.22.refs_0_), channel_id=1, source_target_pairs={{0,16},{1,9},{2,18},{3,11},{4,20},{5,13},{6,22},{7,15},{8,24},{9,1... | collective-permute-start | bytes 405512 | tf_op jit(solution)/shard_map/ppermute | solution.py:345
  61.6 7.5 %collective-permute-start.12 = (f32[264,128]{1,0:T(8,128)S(1)}, f32[264,128]{1,0:T(8,128)S(1)}, u32[]{:S(2)}, u32[]{:S(2)}) collective-permute-start(f32[264,128]{1,0:T(8,128)S(1)} %get-tuple-element.71.refs_0_), channel_id=1, source_target_pairs={{0,6},{1,7},{2,4},{3,5},{4,2},{5,3},{6,0},{7,1},{8,14},{9,15},{10,... | collective-permute-start | bytes 405512 | tf_op jit(solution)/shard_map/ppermute | solution.py:334
  65.9 7.0 %collective-permute-start.19 = (f32[264,128]{1,0:T(8,128)S(1)}, f32[264,128]{1,0:T(8,128)S(1)}, u32[]{:S(2)}, u32[]{:S(2)}) collective-permute-start(f32[264,128]{1,0:T(8,128)S(1)} %get-tuple-element.77.refs_0_), channel_id=1, source_target_pairs={{0,6},{1,7},{2,4},{3,5},{4,2},{5,3},{6,0},{7,1},{8,14},{9,15},{10,... | collective-permute-start | bytes 405512 | tf_op jit(solution)/shard_map/ppermute | solution.py:334
  70.0 5.1 %collective-permute-start.13 = (f32[264,128]{1,0:T(8,128)S(1)}, f32[264,128]{1,0:T(8,128)S(1)}, u32[]{:S(2)}, u32[]{:S(2)}) collective-permute-start(f32[264,128]{1,0:T(8,128)S(1)} %get-tuple-element.72), channel_id=1, source_target_pairs={{0,8},{1,17},{2,10},{3,19},{4,12},{5,21},{6,14},{7,23},{8,0},{9,25... | collective-permute-start | bytes 405512 | tf_op jit(solution)/shard_map/ppermute | solution.py:345
  73.8 5.8 %collective-permute-start.20 = (f32[264,128]{1,0:T(8,128)S(1)}, f32[264,128]{1,0:T(8,128)S(1)}, u32[]{:S(2)}, u32[]{:S(2)}) collective-permute-start(f32[264,128]{1,0:T(8,128)S(1)} %get-tuple-element.78), channel_id=1, source_target_pairs={{0,8},{1,17},{2,10},{3,19},{4,12},{5,21},{6,14},{7,23},{8,0},{9,25... | collective-permute-start | bytes 405512 | tf_op jit(solution)/shard_map/ppermute | solution.py:345
  75.1 6.6 %collective-permute-start.14 = (f32[264,128]{1,0:T(8,128)S(1)}, f32[264,128]{1,0:T(8,128)S(1)}, u32[]{:S(2)}, u32[]{:S(2)}) collective-permute-start(f32[264,128]{1,0:T(8,128)S(1)} %add.21.refs_0_), channel_id=1, source_target_pairs={{0,16},{1,9},{2,18},{3,11},{4,20},{5,13},{6,22},{7,15},{8,24},{9,1... | collective-permute-start | bytes 405512 | tf_op jit(solution)/shard_map/ppermute | solution.py:345
  79.5 6.7 %collective-permute-start.21 = (f32[264,128]{1,0:T(8,128)S(1)}, f32[264,128]{1,0:T(8,128)S(1)}, u32[]{:S(2)}, u32[]{:S(2)}) collective-permute-start(f32[264,128]{1,0:T(8,128)S(1)} %add.23.refs_0_), channel_id=1, source_target_pairs={{0,16},{1,9},{2,18},{3,11},{4,20},{5,13},{6,22},{7,15},{8,24},{9,1... | collective-permute-start | bytes 405512 | tf_op jit(solution)/shard_map/ppermute | solution.py:345
  82.7 7.6 %collective-permute-start.15 = (f32[264,128]{1,0:T(8,128)S(1)}, f32[264,128]{1,0:T(8,128)S(1)}, u32[]{:S(2)}, u32[]{:S(2)}) collective-permute-start(f32[264,128]{1,0:T(8,128)S(1)} %get-tuple-element.73.own_ref), channel_id=1, source_target_pairs={{0,6},{1,7},{2,4},{3,5},{4,2},{5,3},{6,0},{7,1},{8,14},{9,15},{10,... | collective-permute-start | bytes 405512 | tf_op jit(solution)/shard_map/ppermute | solution.py:334
  87.2 7.4 %collective-permute-start.22 = (f32[264,128]{1,0:T(8,128)S(1)}, f32[264,128]{1,0:T(8,128)S(1)}, u32[]{:S(2)}, u32[]{:S(2)}) collective-permute-start(f32[264,128]{1,0:T(8,128)S(1)} %get-tuple-element.84.own_ref), channel_id=1, source_target_pairs={{0,6},{1,7},{2,4},{3,5},{4,2},{5,3},{6,0},{7,1},{8,14},{9,15},{10,... | collective-permute-start | bytes 405512 | tf_op jit(solution)/shard_map/ppermute | solution.py:334
  90.5 8.3 %collective-permute-start.23 = (f32[328,128]{1,0:T(8,128)S(1)}, f32[328,128]{1,0:T(8,128)S(1)}, u32[]{:S(2)}, u32[]{:S(2)}) collective-permute-start(f32[328,128]{1,0:T(8,128)S(1)} %get-tuple-element.89), channel_id=1, source_target_pairs={{0,2},{1,3},{2,0},{3,1},{4,6},{5,7},{6,4},{7,5},{8,10},{9,11},{10,... | collective-permute-start | bytes 503816 | tf_op jit(solution)/shard_map/ppermute | solution.py:334
  94.8 4.0 %collective-permute-start.24 = (f32[72,128]{1,0:T(8,128)S(1)}, f32[72,128]{1,0:T(8,128)S(1)}, u32[]{:S(2)}, u32[]{:S(2)}) collective-permute-start(f32[72,128]{1,0:T(8,128)S(1)} %get-tuple-element.90), channel_id=1, source_target_pairs={{0,2},{1,3},{2,0},{3,1},{4,6},{5,7},{6,4},{7,5},{8,10},{9,11},{10,... | collective-permute-start | bytes 110600 | tf_op jit(solution)/shard_map/ppermute | solution.py:334
  98.9 1.5 %collective-permute-start.25 = (f32[392,128]{1,0:T(8,128)S(1)}, f32[392,128]{1,0:T(8,128)S(1)}, u32[]{:S(2)}, u32[]{:S(2)}) collective-permute-start(f32[392,128]{1,0:T(8,128)S(1)} %get-tuple-element.92), channel_id=1, source_target_pairs={{0,1},{1,0},{2,3},{3,2},{4,5},{5,4},{6,7},{7,6},{8,9},{9,8},{10,11... | collective-permute-start | bytes 602120 | tf_op jit(solution)/shard_map/ppermute | solution.py:334
  100.4 4.6 %collective-permute-start.28 = (f32[8,256]{1,0:T(8,128)S(1)}, f32[8,256]{1,0:T(8,128)S(1)}, u32[]{:S(2)}, u32[]{:S(2)}) collective-permute-start(f32[8,256]{1,0:T(8,128)S(1)} %get-tuple-element.94.known_ref.refs_4_), channel_id=1, source_target_pairs={{0,24},{8,16},{16,8},{24,0},{1,25},{9,17},{17,9},{25,1},{2,26},{10... | collective-permute-start | bytes 24584 | tf_op jit(solution)/shard_map/ppermute | solution.py:435
  103.3 3.7 %collective-permute-start.27 = (f32[8,256]{1,0:T(8,128)S(1)}, f32[8,256]{1,0:T(8,128)S(1)}, u32[]{:S(2)}, u32[]{:S(2)}) collective-permute-start(f32[8,256]{1,0:T(8,128)S(1)} %get-tuple-element.94.known_ref.refs_4_), channel_id=1, source_target_pairs={{0,16},{8,24},{16,0},{24,8},{1,17},{9,25},{17,1},{25,9},{2,18},{10... | collective-permute-start | bytes 24584 | tf_op jit(solution)/shard_map/ppermute | solution.py:435
  103.5 3.7 %collective-permute-start.26 = (f32[8,256]{1,0:T(8,128)S(1)}, f32[8,256]{1,0:T(8,128)S(1)}, u32[]{:S(2)}, u32[]{:S(2)}) collective-permute-start(f32[8,256]{1,0:T(8,128)S(1)} %get-tuple-element.94.known_ref.refs_4_), channel_id=1, source_target_pairs={{0,8},{8,0},{16,24},{24,16},{1,9},{9,1},{17,25},{25,17},{2,10},{10... | collective-permute-start | bytes 24584 | tf_op jit(solution)/shard_map/ppermute | solution.py:435

commit v13 on v10

--- a/solution.py
+++ b/solution.py
@@ -395,7 +395,10 @@
     scale_shape = ((TILE, LANES), F32)
     z_shape = ((COLS * 4 * width // LANES, LANES), F32)
     scales = [[] for _ in range(HALVES)]
-    sent = [call(first_z_kernel, [sent_shape], y, swap_pair(y), *matrix, cost=LONG)[0] for y in own]
+    first_got = swap_pair(own[0])
+    later, first_got = lax.optimization_barrier((own[1], first_got))
+    own, got = (own[0], later), (first_got, swap_pair(later))
+    sent = [call(first_z_kernel, [sent_shape], y, g, *matrix, cost=LONG)[0] for y, g in zip(own, got)]
     ys, zs = [None] * HALVES, [None] * HALVES
     for section in range(ITERS):
         last = section == ITERS - 1

time: 99.3 us -> 100 us (level)
  starting transfers between devices: 38.1 us -> 42.5 us
  waiting for transfers between devices: 45 us -> 41.3 us
    ppermute x14, starting transfers between devices: 22.9 us -> 28.1 us  [swap(): return lax.ppermute(x, 'snap', [(i, i ^ bits) for i in range(places)])]
    ppermute x14, waiting for transfers between devices: 35.7 us -> 33.1 us  [swap(): return lax.ppermute(x, 'snap', [(i, i ^ bits) for i in range(places)])]
    ppermute x3, waiting for transfers between devices: 2.79 us -> 1.61 us  [local(): lax.ppermute(known, 'cell', [(c, c ^ d) for c in range(groups)])]
where the time goes in v13:
time: 100 us; the launch traced here: 99.8 us
  starting transfers between devices  42.5 us (42%)
  waiting for transfers between devices  41.3 us (41%)
  Pallas kernels  13 us (13%)
  local copies, waits for them, and re-layouts  2.21 us (2%)
    ppermute x14, waiting for transfers between devices, swap(): return lax.ppermute(x, 'snap', [(i, i ^ bits) for i in range(places)])  33.1 us
    ppermute x14, starting transfers between devices, swap(): return lax.ppermute(x, 'snap', [(i, i ^ bits) for i in range(places)])  28.1 us
    pallas_call x20, Pallas kernels, call(): pl.pallas_call(kernel, out_shape=[jax.ShapeDtypeStruct(shape, dtype) for...  13 us
    ppermute x8, starting transfers between devices, swap_cell(): return lax.ppermute(x, ('cell', 'snap'), perm)  10.8 us
    ppermute x8, waiting for transfers between devices, swap_cell(): return lax.ppermute(x, ('cell', 'snap'), perm)  6.59 us
    ppermute x3, starting transfers between devices, local(): lax.ppermute(known, 'cell', [(c, c ^ d) for c in range(groups)])  3.55 us
  transfers between devices with their start and end apart: 25, of which 18 were waited for; matrix products, arithmetic and copies ran while one was open for 1% of the time, Pallas kernels for 12%

profile of v13, /device:TPU:0, one launch (start us, length us, event | category | flops | bytes accessed | tf_op | source)
XLA Modules:
  0.0 99.8 jit_solution(3862336212991914508)
XLA Ops:
  0.6 0.5 collective-permute-start.1
  1.1 2.7 %collective-permute-start = (f32[1024,256]{1,0:T(8,128)}, f32[1024,256]{1,0:T(8,128)S(1)}, u32[]{:S(2)}, u32[]{:S(2)}) collective-permute-start(f32[1024,256]{1,0:T(8,128)} %own_ref.1), channel_id=1, source_target_pairs={{0,2},{1,3},{2,0},{3,1},{4,6},{5,7},{6,4},{7,5},{8,10},{9,11},{10,... | collective-permute-start | bytes 3145736 | tf_op jit(solution)/shard_map/ppermute | solution.py:344
  3.8 1.0 constant_dynamic-slice_fusion
  4.8 0.2 collective-permute-start.2
  5.0 1.2 %collective-permute-done.2.got_ref = f32[256,128]{1,0:T(8,128)S(1)} collective-permute-done((f32[256,128]{1,0:T(8,128)S(1)}, f32[256,128]{1,0:T(8,128)S(1)}, u32[]{:S(2)}, u32[]{:S(2)}) %collective-permute-start.2) | collective-permute-done | bytes 131104 | tf_op jit(solution)/shard_map/ppermute | solution.py:344
  6.2 0.2 shard_map.49
  6.4 0.4 collective-permute-start.4
  6.8 1.2 %copy-done = f32[1024,256]{1,0:T(8,128)S(1)} copy-done((f32[1024,256]{1,0:T(8,128)S(1)}, f32[1024,256]{1,0:T(8,128)}, u32[]{:S(2)}) %copy-start) | copy-done | bytes 1048600
  8.0 1.1 %shard_map.50 = (f32[512,128]{1,0:T(8,128)S(1)}, bf16[1024,512]{1,0:T(8,128)(2,1)S(1)}, bf16[1024,512]{1,0:T(8,128)(2,1)S(1)}, bf16[512,1024]{1,0:T(8,128)(2,1)S(1)}, bf16[512,1024]{1,0:T(8,128)(2,1)S(1)}) custom-call(f32[1024,256]{1,0:T(8,128)S(1)} %copy-done, f32[1024,256]{1,0:T(8,128)S(1)} %collective-permute-done.1.core_ref, ...), custom_call_target="tpu_custom_call" | custom-call | tf_op jit(solution)/shard_map/pallas_call | solution.py:297
  9.1 18.9 %collective-permute-done.side_ref = f32[1024,256]{1,0:T(8,128)S(1)} collective-permute-done((f32[1024,256]{1,0:T(8,128)}, f32[1024,256]{1,0:T(8,128)S(1)}, u32[]{:S(2)}, u32[]{:S(2)}) %collective-permute-start) | collective-permute-done | bytes 1048608 | tf_op jit(solution)/shard_map/ppermute | solution.py:344
  28.0 0.6 shard_map.51
  28.7 1.9 %collective-permute-done.4.sketch_ref = f32[256,128]{1,0:T(8,128)S(1)} collective-permute-done((f32[256,128]{1,0:T(8,128)S(1)}, f32[256,128]{1,0:T(8,128)S(1)}, u32[]{:S(2)}, u32[]{:S(2)}) %collective-permute-start.4) | collective-permute-done | bytes 131104 | tf_op jit(solution)/shard_map/ppermute | solution.py:344
  30.6 0.6 shard_map.52.near_ref
  31.1 0.7 shard_map.53
  31.8 3.8 %collective-permute-start.5 = (f32[256,128]{1,0:T(8,128)S(1)}, f32[256,128]{1,0:T(8,128)S(1)}, u32[]{:S(2)}, u32[]{:S(2)}) collective-permute-start(f32[256,128]{1,0:T(8,128)S(1)} %get-tuple-element.55.a_ref), channel_id=1, source_target_pairs={{0,6},{1,7},{2,4},{3,5},{4,2},{5,3},{6,0},{7,1},{8,14},{9,15},{10,... | collective-permute-start | bytes 393224 | tf_op jit(solution)/shard_map/ppermute | solution.py:344
  35.7 0.7 shard_map.54
  36.4 2.9 %collective-permute-done.5.b_ref = f32[256,128]{1,0:T(8,128)S(1)} collective-permute-done((f32[256,128]{1,0:T(8,128)S(1)}, f32[256,128]{1,0:T(8,128)S(1)}, u32[]{:S(2)}, u32[]{:S(2)}) %collective-permute-start.5) | collective-permute-done | bytes 131104 | tf_op jit(solution)/shard_map/ppermute | solution.py:344
  39.3 3.5 %collective-permute-start.12 = (f32[256,128]{1,0:T(8,128)S(1)}, f32[256,128]{1,0:T(8,128)S(1)}, u32[]{:S(2)}, u32[]{:S(2)}) collective-permute-start(f32[256,128]{1,0:T(8,128)S(1)} %get-tuple-element.72.a_ref), channel_id=1, source_target_pairs={{0,6},{1,7},{2,4},{3,5},{4,2},{5,3},{6,0},{7,1},{8,14},{9,15},{10,... | collective-permute-start | bytes 393224 | tf_op jit(solution)/shard_map/ppermute | solution.py:344
  42.8 0.8 shard_map.55
  43.6 1.5 %collective-permute-start.6 = (f32[264,128]{1,0:T(8,128)S(1)}, f32[264,128]{1,0:T(8,128)S(1)}, u32[]{:S(2)}, u32[]{:S(2)}) collective-permute-start(f32[264,128]{1,0:T(8,128)S(1)} %shard_map.55), channel_id=1, source_target_pairs={{0,8},{1,17},{2,10},{3,19},{4,12},{5,21},{6,14},{7,23},{8,0},{9,25... | collective-permute-start | bytes 405512 | tf_op jit(solution)/shard_map/ppermute | solution.py:355
  45.1 1.0 collective-permute-done.12.b_ref
  46.1 0.8 shard_map.59
  46.9 1.5 %collective-permute-start.13 = (f32[264,128]{1,0:T(8,128)S(1)}, f32[264,128]{1,0:T(8,128)S(1)}, u32[]{:S(2)}, u32[]{:S(2)}) collective-permute-start(f32[264,128]{1,0:T(8,128)S(1)} %shard_map.59), channel_id=1, source_target_pairs={{0,8},{1,17},{2,10},{3,19},{4,12},{5,21},{6,14},{7,23},{8,0},{9,25... | collective-permute-start | bytes 405512 | tf_op jit(solution)/shard_map/ppermute | solution.py:355
  48.4 0.2 collective-permute-done.6
  48.7 1.6 %collective-permute-start.7 = (f32[264,128]{1,0:T(8,128)S(1)}, f32[264,128]{1,0:T(8,128)S(1)}, u32[]{:S(2)}, u32[]{:S(2)}) collective-permute-start(f32[264,128]{1,0:T(8,128)S(1)} %add.20.refs_0_), channel_id=1, source_target_pairs={{0,16},{1,9},{2,18},{3,11},{4,20},{5,13},{6,22},{7,15},{8,24},{9,1... | collective-permute-start | bytes 405512 | tf_op jit(solution)/shard_map/ppermute | solution.py:355
  50.3 2.0 %collective-permute-done.13 = f32[264,128]{1,0:T(8,128)S(1)} collective-permute-done((f32[264,128]{1,0:T(8,128)S(1)}, f32[264,128]{1,0:T(8,128)S(1)}, u32[]{:S(2)}, u32[]{:S(2)}) %collective-permute-start.13) | collective-permute-done | bytes 135200 | tf_op jit(solution)/shard_map/ppermute | solution.py:355
  52.3 1.7 %collective-permute-start.14 = (f32[264,128]{1,0:T(8,128)S(1)}, f32[264,128]{1,0:T(8,128)S(1)}, u32[]{:S(2)}, u32[]{:S(2)}) collective-permute-start(f32[264,128]{1,0:T(8,128)S(1)} %add.22.refs_0_), channel_id=1, source_target_pairs={{0,16},{1,9},{2,18},{3,11},{4,20},{5,13},{6,22},{7,15},{8,24},{9,1... | collective-permute-start | bytes 405512 | tf_op jit(solution)/shard_map/ppermute | solution.py:355
  54.1 0.9 shard_map.56
  55.0 3.9 %collective-permute-start.8 = (f32[264,128]{1,0:T(8,128)S(1)}, f32[264,128]{1,0:T(8,128)S(1)}, u32[]{:S(2)}, u32[]{:S(2)}) collective-permute-start(f32[264,128]{1,0:T(8,128)S(1)} %get-tuple-element.68.refs_0_), channel_id=1, source_target_pairs={{0,6},{1,7},{2,4},{3,5},{4,2},{5,3},{6,0},{7,1},{8,14},{9,15},{10,... | collective-permute-start | bytes 405512 | tf_op jit(solution)/shard_map/ppermute | solution.py:344
  58.9 0.9 shard_map.60
  59.8 2.6 %collective-permute-start.15 = (f32[264,128]{1,0:T(8,128)S(1)}, f32[264,128]{1,0:T(8,128)S(1)}, u32[]{:S(2)}, u32[]{:S(2)}) collective-permute-start(f32[264,128]{1,0:T(8,128)S(1)} %get-tuple-element.73.refs_0_), channel_id=1, source_target_pairs={{0,6},{1,7},{2,4},{3,5},{4,2},{5,3},{6,0},{7,1},{8,14},{9,15},{10,... | collective-permute-start | bytes 405512 | tf_op jit(solution)/shard_map/ppermute | solution.py:344
  62.4 0.2 collective-permute-done.8.refs_1_
  62.5 0.9 shard_map.57
  63.4 1.5 %collective-permute-start.9 = (f32[264,128]{1,0:T(8,128)S(1)}, f32[264,128]{1,0:T(8,128)S(1)}, u32[]{:S(2)}, u32[]{:S(2)}) collective-permute-start(f32[264,128]{1,0:T(8,128)S(1)} %get-tuple-element.69), channel_id=1, source_target_pairs={{0,8},{1,17},{2,10},{3,19},{4,12},{5,21},{6,14},{7,23},{8,0},{9,25... | collective-permute-start | bytes 405512 | tf_op jit(solution)/shard_map/ppermute | solution.py:355
  64.9 1.8 %collective-permute-done.15.refs_1_ = f32[264,128]{1,0:T(8,128)S(1)} collective-permute-done((f32[264,128]{1,0:T(8,128)S(1)}, f32[264,128]{1,0:T(8,128)S(1)}, u32[]{:S(2)}, u32[]{:S(2)}) %collective-permute-start.15) | collective-permute-done | bytes 135200 | tf_op jit(solution)/shard_map/ppermute | solution.py:344
  66.8 0.9 shard_map.61
  67.6 1.5 %collective-permute-start.16 = (f32[264,128]{1,0:T(8,128)S(1)}, f32[264,128]{1,0:T(8,128)S(1)}, u32[]{:S(2)}, u32[]{:S(2)}) collective-permute-start(f32[264,128]{1,0:T(8,128)S(1)} %get-tuple-element.74), channel_id=1, source_target_pairs={{0,8},{1,17},{2,10},{3,19},{4,12},{5,21},{6,14},{7,23},{8,0},{9,25... | collective-permute-start | bytes 405512 | tf_op jit(solution)/shard_map/ppermute | solution.py:355
  69.1 0.7 collective-permute-done.9
  69.9 0.2 collective-permute-start.10
  70.1 2.6 %collective-permute-done.16 = f32[264,128]{1,0:T(8,128)S(1)} collective-permute-done((f32[264,128]{1,0:T(8,128)S(1)}, f32[264,128]{1,0:T(8,128)S(1)}, u32[]{:S(2)}, u32[]{:S(2)}) %collective-permute-start.16) | collective-permute-done | bytes 135200 | tf_op jit(solution)/shard_map/ppermute | solution.py:355
  72.7 1.3 %collective-permute-start.17 = (f32[264,128]{1,0:T(8,128)S(1)}, f32[264,128]{1,0:T(8,128)S(1)}, u32[]{:S(2)}, u32[]{:S(2)}) collective-permute-start(f32[264,128]{1,0:T(8,128)S(1)} %add.23.refs_0_), channel_id=1, source_target_pairs={{0,16},{1,9},{2,18},{3,11},{4,20},{5,13},{6,22},{7,15},{8,24},{9,1... | collective-permute-start | bytes 405512 | tf_op jit(solution)/shard_map/ppermute | solution.py:355
  73.9 1.0 %collective-permute-done.10.refs_1_ = f32[264,128]{1,0:T(8,128)S(1)} collective-permute-done((f32[264,128]{1,0:T(8,128)S(1)}, f32[264,128]{1,0:T(8,128)S(1)}, u32[]{:S(2)}, u32[]{:S(2)}) %collective-permute-start.10) | collective-permute-done | bytes 135200 | tf_op jit(solution)/shard_map/ppermute | solution.py:355
  75.0 0.9 shard_map.58
  75.9 2.7 %collective-permute-start.11 = (f32[264,128]{1,0:T(8,128)S(1)}, f32[264,128]{1,0:T(8,128)S(1)}, u32[]{:S(2)}, u32[]{:S(2)}) collective-permute-start(f32[264,128]{1,0:T(8,128)S(1)} %get-tuple-element.70.own_ref), channel_id=1, source_target_pairs={{0,6},{1,7},{2,4},{3,5},{4,2},{5,3},{6,0},{7,1},{8,14},{9,15},{10,... | collective-permute-start | bytes 405512 | tf_op jit(solution)/shard_map/ppermute | solution.py:344
  78.6 0.9 shard_map.62
  79.5 1.8 %collective-permute-start.18 = (f32[264,128]{1,0:T(8,128)S(1)}, f32[264,128]{1,0:T(8,128)S(1)}, u32[]{:S(2)}, u32[]{:S(2)}) collective-permute-start(f32[264,128]{1,0:T(8,128)S(1)} %get-tuple-element.80.own_ref), channel_id=1, source_target_pairs={{0,6},{1,7},{2,4},{3,5},{4,2},{5,3},{6,0},{7,1},{8,14},{9,15},{10,... | collective-permute-start | bytes 405512 | tf_op jit(solution)/shard_map/ppermute | solution.py:344
  81.3 1.7 %collective-permute-done.11.got_ref = f32[264,128]{1,0:T(8,128)S(1)} collective-permute-done((f32[264,128]{1,0:T(8,128)S(1)}, f32[264,128]{1,0:T(8,128)S(1)}, u32[]{:S(2)}, u32[]{:S(2)}) %collective-permute-start.11) | collective-permute-done | bytes 135200 | tf_op jit(solution)/shard_map/ppermute | solution.py:344
  82.9 0.2 shard_map.63
  83.1 4.1 %collective-permute-start.19 = (f32[328,128]{1,0:T(8,128)S(1)}, f32[328,128]{1,0:T(8,128)S(1)}, u32[]{:S(2)}, u32[]{:S(2)}) collective-permute-start(f32[328,128]{1,0:T(8,128)S(1)} %get-tuple-element.85), channel_id=1, source_target_pairs={{0,2},{1,3},{2,0},{3,1},{4,6},{5,7},{6,4},{7,5},{8,10},{9,11},{10,... | collective-permute-start | bytes 503816 | tf_op jit(solution)/shard_map/ppermute | solution.py:344
  87.2 0.0 collective-permute-done.18.got_ref
  87.3 0.2 shard_map.64
  87.5 1.9 %collective-permute-start.20 = (f32[72,128]{1,0:T(8,128)S(1)}, f32[72,128]{1,0:T(8,128)S(1)}, u32[]{:S(2)}, u32[]{:S(2)}) collective-permute-start(f32[72,128]{1,0:T(8,128)S(1)} %get-tuple-element.86), channel_id=1, source_target_pairs={{0,2},{1,3},{2,0},{3,1},{4,6},{5,7},{6,4},{7,5},{8,10},{9,11},{10,... | collective-permute-start | bytes 110600 | tf_op jit(solution)/shard_map/ppermute | solution.py:344
  89.4 2.1 %collective-permute-done.20.refs_3_ = f32[72,128]{1,0:T(8,128)S(1)} collective-permute-done((f32[72,128]{1,0:T(8,128)S(1)}, f32[72,128]{1,0:T(8,128)S(1)}, u32[]{:S(2)}, u32[]{:S(2)}) %collective-permute-start.20) | collective-permute-done | bytes 36896 | tf_op jit(solution)/shard_map/ppermute | solution.py:344
  91.5 0.1 shard_map.65
  91.6 1.4 %collective-permute-done.21.got_ref.refs_3_ = f32[392,128]{1,0:T(8,128)S(1)} collective-permute-done((f32[392,128]{1,0:T(8,128)S(1)}, f32[392,128]{1,0:T(8,128)S(1)}, u32[]{:S(2)}, u32[]{:S(2)}) %collective-permute-start.21) | collective-permute-done | bytes 200736 | tf_op jit(solution)/shard_map/ppermute | solution.py:344
  93.0 0.1 shard_map.66
  93.1 2.2 %collective-permute-start.24 = (f32[8,256]{1,0:T(8,128)S(1)}, f32[8,256]{1,0:T(8,128)S(1)}, u32[]{:S(2)}, u32[]{:S(2)}) collective-permute-start(f32[8,256]{1,0:T(8,128)S(1)} %get-tuple-element.90.known_ref.refs_4_), channel_id=1, source_target_pairs={{0,24},{8,16},{16,8},{24,0},{1,25},{9,17},{17,9},{25,1},{2,26},{10... | collective-permute-start | bytes 24584 | tf_op jit(solution)/shard_map/ppermute | solution.py:439
  95.3 0.2 collective-permute-start.23
  95.5 1.2 %collective-permute-start.22 = (f32[8,256]{1,0:T(8,128)S(1)}, f32[8,256]{1,0:T(8,128)S(1)}, u32[]{:S(2)}, u32[]{:S(2)}) collective-permute-start(f32[8,256]{1,0:T(8,128)S(1)} %get-tuple-element.90.known_ref.refs_4_), channel_id=1, source_target_pairs={{0,8},{8,0},{16,24},{24,16},{1,9},{9,1},{17,25},{25,17},{2,10},{10... | collective-permute-start | bytes 24584 | tf_op jit(solution)/shard_map/ppermute | solution.py:439
  96.7 0.8 shard_map.68
  97.5 0.2 collective-permute-done.24.refs_2_
  97.8 1.2 %collective-permute-done.23.refs_1_ = f32[8,256]{1,0:T(8,128)S(1)} collective-permute-done((f32[8,256]{1,0:T(8,128)S(1)}, f32[8,256]{1,0:T(8,128)S(1)}, u32[]{:S(2)}, u32[]{:S(2)}) %collective-permute-start.23) | collective-permute-done | bytes 8224 | tf_op jit(solution)/shard_map/ppermute | solution.py:439
  99.0 0.2 collective-permute-done.22.refs_0_
  99.2 0.7 shard_map.67
  (13 shorter events, 0.1 us)
Async XLA Ops:
  0.6 6.2 %collective-permute-start.1 = (f32[1024,256]{1,0:T(8,128)}, f32[1024,256]{1,0:T(8,128)S(1)}, u32[]{:S(2)}, u32[]{:S(2)}) collective-permute-start(f32[1024,256]{1,0:T(8,128)} %own_ref.1), channel_id=1, source_target_pairs={{0,1},{1,0},{2,3},{3,2},{4,5},{5,4},{6,7},{7,6},{8,9},{9,8},{10,11... | collective-permute-start | bytes 3145736 | tf_op jit(solution)/shard_map/ppermute | solution.py:344
  1.1 26.9 %collective-permute-start = (f32[1024,256]{1,0:T(8,128)}, f32[1024,256]{1,0:T(8,128)S(1)}, u32[]{:S(2)}, u32[]{:S(2)}) collective-permute-start(f32[1024,256]{1,0:T(8,128)} %own_ref.1), channel_id=1, source_target_pairs={{0,2},{1,3},{2,0},{3,1},{4,6},{5,7},{6,4},{7,5},{8,10},{9,11},{10,... | collective-permute-start | bytes 3145736 | tf_op jit(solution)/shard_map/ppermute | solution.py:344
  4.8 1.4 %collective-permute-start.2 = (f32[256,128]{1,0:T(8,128)S(1)}, f32[256,128]{1,0:T(8,128)S(1)}, u32[]{:S(2)}, u32[]{:S(2)}) collective-permute-start(f32[256,128]{1,0:T(8,128)S(1)} %get-tuple-element.93), channel_id=1, source_target_pairs={{0,1},{1,0},{2,3},{3,2},{4,5},{5,4},{6,7},{7,6},{8,9},{9,8},{10,11... | collective-permute-start | bytes 393224 | tf_op jit(solution)/shard_map/ppermute | solution.py:344
  6.4 24.2 %collective-permute-start.4 = (f32[256,128]{1,0:T(8,128)S(1)}, f32[256,128]{1,0:T(8,128)S(1)}, u32[]{:S(2)}, u32[]{:S(2)}) collective-permute-start(f32[256,128]{1,0:T(8,128)S(1)} %get-tuple-element.51), channel_id=1, source_target_pairs={{0,2},{1,3},{2,0},{3,1},{4,6},{5,7},{6,4},{7,5},{8,10},{9,11},{10,... | collective-permute-start | bytes 393224 | tf_op jit(solution)/shard_map/ppermute | solution.py:344
  6.8 1.2 %copy-start = (f32[1024,256]{1,0:T(8,128)S(1)}, f32[1024,256]{1,0:T(8,128)}, u32[]{:S(2)}) copy-start(f32[1024,256]{1,0:T(8,128)} %own_ref.1) | copy-start | bytes 3145732
  28.0 3.1 %collective-permute-start.3 = (f32[1024,256]{1,0:T(8,128)S(1)}, f32[1024,256]{1,0:T(8,128)S(1)}, u32[]{:S(2)}, u32[]{:S(2)}) collective-permute-start(f32[1024,256]{1,0:T(8,128)S(1)} %collective-permute-done.side_ref), channel_id=1, source_target_pairs={{0,1},{1,0},{2,3},{3,2},{4,5},{5,4},{6,7},{7,6},{8,9},{9,8},{10,11... | collective-permute-start | bytes 3145736 | tf_op jit(solution)/shard_map/ppermute | solution.py:344
  31.8 7.5 %collective-permute-start.5 = (f32[256,128]{1,0:T(8,128)S(1)}, f32[256,128]{1,0:T(8,128)S(1)}, u32[]{:S(2)}, u32[]{:S(2)}) collective-permute-start(f32[256,128]{1,0:T(8,128)S(1)} %get-tuple-element.55.a_ref), channel_id=1, source_target_pairs={{0,6},{1,7},{2,4},{3,5},{4,2},{5,3},{6,0},{7,1},{8,14},{9,15},{10,... | collective-permute-start | bytes 393224 | tf_op jit(solution)/shard_map/ppermute | solution.py:344
  39.3 6.8 %collective-permute-start.12 = (f32[256,128]{1,0:T(8,128)S(1)}, f32[256,128]{1,0:T(8,128)S(1)}, u32[]{:S(2)}, u32[]{:S(2)}) collective-permute-start(f32[256,128]{1,0:T(8,128)S(1)} %get-tuple-element.72.a_ref), channel_id=1, source_target_pairs={{0,6},{1,7},{2,4},{3,5},{4,2},{5,3},{6,0},{7,1},{8,14},{9,15},{10,... | collective-permute-start | bytes 393224 | tf_op jit(solution)/shard_map/ppermute | solution.py:344
  43.6 5.0 %collective-permute-start.6 = (f32[264,128]{1,0:T(8,128)S(1)}, f32[264,128]{1,0:T(8,128)S(1)}, u32[]{:S(2)}, u32[]{:S(2)}) collective-permute-start(f32[264,128]{1,0:T(8,128)S(1)} %shard_map.55), channel_id=1, source_target_pairs={{0,8},{1,17},{2,10},{3,19},{4,12},{5,21},{6,14},{7,23},{8,0},{9,25... | collective-permute-start | bytes 405512 | tf_op jit(solution)/shard_map/ppermute | solution.py:355
  46.9 5.4 %collective-permute-start.13 = (f32[264,128]{1,0:T(8,128)S(1)}, f32[264,128]{1,0:T(8,128)S(1)}, u32[]{:S(2)}, u32[]{:S(2)}) collective-permute-start(f32[264,128]{1,0:T(8,128)S(1)} %shard_map.59), channel_id=1, source_target_pairs={{0,8},{1,17},{2,10},{3,19},{4,12},{5,21},{6,14},{7,23},{8,0},{9,25... | collective-permute-start | bytes 405512 | tf_op jit(solution)/shard_map/ppermute | solution.py:355
  48.7 5.4 %collective-permute-start.7 = (f32[264,128]{1,0:T(8,128)S(1)}, f32[264,128]{1,0:T(8,128)S(1)}, u32[]{:S(2)}, u32[]{:S(2)}) collective-permute-start(f32[264,128]{1,0:T(8,128)S(1)} %add.20.refs_0_), channel_id=1, source_target_pairs={{0,16},{1,9},{2,18},{3,11},{4,20},{5,13},{6,22},{7,15},{8,24},{9,1... | collective-permute-start | bytes 405512 | tf_op jit(solution)/shard_map/ppermute | solution.py:355
  52.3 6.5 %collective-permute-start.14 = (f32[264,128]{1,0:T(8,128)S(1)}, f32[264,128]{1,0:T(8,128)S(1)}, u32[]{:S(2)}, u32[]{:S(2)}) collective-permute-start(f32[264,128]{1,0:T(8,128)S(1)} %add.22.refs_0_), channel_id=1, source_target_pairs={{0,16},{1,9},{2,18},{3,11},{4,20},{5,13},{6,22},{7,15},{8,24},{9,1... | collective-permute-start | bytes 405512 | tf_op jit(solution)/shard_map/ppermute | solution.py:355
  55.0 7.5 %collective-permute-start.8 = (f32[264,128]{1,0:T(8,128)S(1)}, f32[264,128]{1,0:T(8,128)S(1)}, u32[]{:S(2)}, u32[]{:S(2)}) collective-permute-start(f32[264,128]{1,0:T(8,128)S(1)} %get-tuple-element.68.refs_0_), channel_id=1, source_target_pairs={{0,6},{1,7},{2,4},{3,5},{4,2},{5,3},{6,0},{7,1},{8,14},{9,15},{10,... | collective-permute-start | bytes 405512 | tf_op jit(solution)/shard_map/ppermute | solution.py:344
  59.8 7.0 %collective-permute-start.15 = (f32[264,128]{1,0:T(8,128)S(1)}, f32[264,128]{1,0:T(8,128)S(1)}, u32[]{:S(2)}, u32[]{:S(2)}) collective-permute-start(f32[264,128]{1,0:T(8,128)S(1)} %get-tuple-element.73.refs_0_), channel_id=1, source_target_pairs={{0,6},{1,7},{2,4},{3,5},{4,2},{5,3},{6,0},{7,1},{8,14},{9,15},{10,... | collective-permute-start | bytes 405512 | tf_op jit(solution)/shard_map/ppermute | solution.py:344
  63.4 6.5 %collective-permute-start.9 = (f32[264,128]{1,0:T(8,128)S(1)}, f32[264,128]{1,0:T(8,128)S(1)}, u32[]{:S(2)}, u32[]{:S(2)}) collective-permute-start(f32[264,128]{1,0:T(8,128)S(1)} %get-tuple-element.69), channel_id=1, source_target_pairs={{0,8},{1,17},{2,10},{3,19},{4,12},{5,21},{6,14},{7,23},{8,0},{9,25... | collective-permute-start | bytes 405512 | tf_op jit(solution)/shard_map/ppermute | solution.py:355
  67.6 5.0 %collective-permute-start.16 = (f32[264,128]{1,0:T(8,128)S(1)}, f32[264,128]{1,0:T(8,128)S(1)}, u32[]{:S(2)}, u32[]{:S(2)}) collective-permute-start(f32[264,128]{1,0:T(8,128)S(1)} %get-tuple-element.74), channel_id=1, source_target_pairs={{0,8},{1,17},{2,10},{3,19},{4,12},{5,21},{6,14},{7,23},{8,0},{9,25... | collective-permute-start | bytes 405512 | tf_op jit(solution)/shard_map/ppermute | solution.py:355
  69.9 5.1 %collective-permute-start.10 = (f32[264,128]{1,0:T(8,128)S(1)}, f32[264,128]{1,0:T(8,128)S(1)}, u32[]{:S(2)}, u32[]{:S(2)}) collective-permute-start(f32[264,128]{1,0:T(8,128)S(1)} %add.21.refs_0_), channel_id=1, source_target_pairs={{0,16},{1,9},{2,18},{3,11},{4,20},{5,13},{6,22},{7,15},{8,24},{9,1... | collective-permute-start | bytes 405512 | tf_op jit(solution)/shard_map/ppermute | solution.py:355
  72.7 5.9 %collective-permute-start.17 = (f32[264,128]{1,0:T(8,128)S(1)}, f32[264,128]{1,0:T(8,128)S(1)}, u32[]{:S(2)}, u32[]{:S(2)}) collective-permute-start(f32[264,128]{1,0:T(8,128)S(1)} %add.23.refs_0_), channel_id=1, source_target_pairs={{0,16},{1,9},{2,18},{3,11},{4,20},{5,13},{6,22},{7,15},{8,24},{9,1... | collective-permute-start | bytes 405512 | tf_op jit(solution)/shard_map/ppermute | solution.py:355
  75.9 7.0 %collective-permute-start.11 = (f32[264,128]{1,0:T(8,128)S(1)}, f32[264,128]{1,0:T(8,128)S(1)}, u32[]{:S(2)}, u32[]{:S(2)}) collective-permute-start(f32[264,128]{1,0:T(8,128)S(1)} %get-tuple-element.70.own_ref), channel_id=1, source_target_pairs={{0,6},{1,7},{2,4},{3,5},{4,2},{5,3},{6,0},{7,1},{8,14},{9,15},{10,... | collective-permute-start | bytes 405512 | tf_op jit(solution)/shard_map/ppermute | solution.py:344
  79.5 7.8 %collective-permute-start.18 = (f32[264,128]{1,0:T(8,128)S(1)}, f32[264,128]{1,0:T(8,128)S(1)}, u32[]{:S(2)}, u32[]{:S(2)}) collective-permute-start(f32[264,128]{1,0:T(8,128)S(1)} %get-tuple-element.80.own_ref), channel_id=1, source_target_pairs={{0,6},{1,7},{2,4},{3,5},{4,2},{5,3},{6,0},{7,1},{8,14},{9,15},{10,... | collective-permute-start | bytes 405512 | tf_op jit(solution)/shard_map/ppermute | solution.py:344
  83.1 8.4 %collective-permute-start.19 = (f32[328,128]{1,0:T(8,128)S(1)}, f32[328,128]{1,0:T(8,128)S(1)}, u32[]{:S(2)}, u32[]{:S(2)}) collective-permute-start(f32[328,128]{1,0:T(8,128)S(1)} %get-tuple-element.85), channel_id=1, source_target_pairs={{0,2},{1,3},{2,0},{3,1},{4,6},{5,7},{6,4},{7,5},{8,10},{9,11},{10,... | collective-permute-start | bytes 503816 | tf_op jit(solution)/shard_map/ppermute | solution.py:344
  87.5 4.0 %collective-permute-start.20 = (f32[72,128]{1,0:T(8,128)S(1)}, f32[72,128]{1,0:T(8,128)S(1)}, u32[]{:S(2)}, u32[]{:S(2)}) collective-permute-start(f32[72,128]{1,0:T(8,128)S(1)} %get-tuple-element.86), channel_id=1, source_target_pairs={{0,2},{1,3},{2,0},{3,1},{4,6},{5,7},{6,4},{7,5},{8,10},{9,11},{10,... | collective-permute-start | bytes 110600 | tf_op jit(solution)/shard_map/ppermute | solution.py:344
  91.6 1.5 %collective-permute-start.21 = (f32[392,128]{1,0:T(8,128)S(1)}, f32[392,128]{1,0:T(8,128)S(1)}, u32[]{:S(2)}, u32[]{:S(2)}) collective-permute-start(f32[392,128]{1,0:T(8,128)S(1)} %get-tuple-element.88), channel_id=1, source_target_pairs={{0,1},{1,0},{2,3},{3,2},{4,5},{5,4},{6,7},{7,6},{8,9},{9,8},{10,11... | collective-permute-start | bytes 602120 | tf_op jit(solution)/shard_map/ppermute | solution.py:344
  93.1 4.6 %collective-permute-start.24 = (f32[8,256]{1,0:T(8,128)S(1)}, f32[8,256]{1,0:T(8,128)S(1)}, u32[]{:S(2)}, u32[]{:S(2)}) collective-permute-start(f32[8,256]{1,0:T(8,128)S(1)} %get-tuple-element.90.known_ref.refs_4_), channel_id=1, source_target_pairs={{0,24},{8,16},{16,8},{24,0},{1,25},{9,17},{17,9},{25,1},{2,26},{10... | collective-permute-start | bytes 24584 | tf_op jit(solution)/shard_map/ppermute | solution.py:439
  95.3 3.7 %collective-permute-start.23 = (f32[8,256]{1,0:T(8,128)S(1)}, f32[8,256]{1,0:T(8,128)S(1)}, u32[]{:S(2)}, u32[]{:S(2)}) collective-permute-start(f32[8,256]{1,0:T(8,128)S(1)} %get-tuple-element.90.known_ref.refs_4_), channel_id=1, source_target_pairs={{0,16},{8,24},{16,0},{24,8},{1,17},{9,25},{17,1},{25,9},{2,18},{10... | collective-permute-start | bytes 24584 | tf_op jit(solution)/shard_map/ppermute | solution.py:439
  95.5 3.7 %collective-permute-start.22 = (f32[8,256]{1,0:T(8,128)S(1)}, f32[8,256]{1,0:T(8,128)S(1)}, u32[]{:S(2)}, u32[]{:S(2)}) collective-permute-start(f32[8,256]{1,0:T(8,128)S(1)} %get-tuple-element.90.known_ref.refs_4_), channel_id=1, source_target_pairs={{0,8},{8,0},{16,24},{24,16},{1,9},{9,1},{17,25},{25,17},{2,10},{10... | collective-permute-start | bytes 24584 | tf_op jit(solution)/shard_map/ppermute | solution.py:439

commit v14 on v10

--- a/solution.py
+++ b/solution.py
@@ -345,7 +345,12 @@
 
     swap_core = functools.partial(swap, bits=1)
     swap_side = functools.partial(swap, bits=2)
-    swap_pair = functools.partial(swap, bits=6)
+
+    def swap_pair(x):
+        inner = [(i, i ^ 6) for i in range(2, 6)]
+        outer = [(i, i ^ 6) for i in (0, 1, 6, 7)]
+        return lax.ppermute(x, "snap", inner) + lax.ppermute(x, "snap", outer)
+
 
     def swap_cell(x, step):
         def target(cell, i):

time: 99.3 us -> 108 us (1.088)
  starting transfers between devices: 38.1 us -> 53.1 us
  waiting for transfers between devices: 45 us -> 38.4 us
    ppermute x0 -> x12, starting transfers between devices: none -> 27 us  [swap_pair(): return lax.ppermute(x, 'snap', inner) + lax.ppermute(x, 'snap', outer)]
    ppermute x14 -> x8, starting transfers between devices: 22.9 us -> 10.2 us  [swap(): return lax.ppermute(x, 'snap', [(i, i ^ bits) for i in range(places)])]
    ppermute x14 -> x8, waiting for transfers between devices: 35.7 us -> 25.4 us  [swap(): return lax.ppermute(x, 'snap', [(i, i ^ bits) for i in range(places)])]
    ppermute x0 -> x12, waiting for transfers between devices: none -> 6.04 us  [swap_pair(): return lax.ppermute(x, 'snap', inner) + lax.ppermute(x, 'snap', outer)]
    ppermute x8, waiting for transfers between devices: 6.56 us -> 4.78 us  [swap_cell(): return lax.ppermute(x, ('cell', 'snap'), perm)]
  transfers between devices with their start and end apart: 25 -> 31, of which waited for: 18 -> 14; matrix products, arithmetic and copies ran while one was open for 1% -> 1% of each run, Pallas kernels for 12% -> 11%
where the time goes in v14:
time: 108 us
  starting transfers between devices  53.1 us (49%)
  waiting for transfers between devices  38.4 us (36%)
  Pallas kernels  13 us (12%)
  local copies, waits for them, and re-layouts  2.21 us (2%)
    ppermute x12, starting transfers between devices, swap_pair(): return lax.ppermute(x, 'snap', inner) + lax.ppermute(x, 'snap', outer)  27 us
    ppermute x8, waiting for transfers between devices, swap(): return lax.ppermute(x, 'snap', [(i, i ^ bits) for i in range(places)])  25.4 us
    pallas_call x20, Pallas kernels, call(): pl.pallas_call(kernel, out_shape=[jax.ShapeDtypeStruct(shape, dtype) for...  13 us
    ppermute x8, starting transfers between devices, swap_cell(): return lax.ppermute(x, ('cell', 'snap'), perm)  12.3 us
    ppermute x8, starting transfers between devices, swap(): return lax.ppermute(x, 'snap', [(i, i ^ bits) for i in range(places)])  10.2 us
    ppermute x12, waiting for transfers between devices, swap_pair(): return lax.ppermute(x, 'snap', inner) + lax.ppermute(x, 'snap', outer)  6.04 us
    ppermute x8, waiting for transfers between devices, swap_cell(): return lax.ppermute(x, ('cell', 'snap'), perm)  4.78 us
    ppermute x3, starting transfers between devices, local(): lax.ppermute(known, 'cell', [(c, c ^ d) for c in range(groups)])  3.55 us
  transfers between devices with their start and end apart: 31, of which 14 were waited for; matrix products, arithmetic and copies ran while one was open for 1% of the time, Pallas kernels for 11%

profile of v14, /device:TPU:0, one launch (start us, length us, event | category | flops | bytes accessed | tf_op | source)
XLA Modules:
  0.0 107.9 jit_solution(695414602035739123)
XLA Ops:
  0.6 0.5 collective-permute-start.1
  1.1 2.7 %collective-permute-start = (f32[1024,256]{1,0:T(8,128)}, f32[1024,256]{1,0:T(8,128)S(1)}, u32[]{:S(2)}, u32[]{:S(2)}) collective-permute-start(f32[1024,256]{1,0:T(8,128)} %own_ref.1), channel_id=1, source_target_pairs={{0,2},{1,3},{2,0},{3,1},{4,6},{5,7},{6,4},{7,5},{8,10},{9,11},{10,... | collective-permute-start | bytes 3145736 | tf_op jit(solution)/shard_map/ppermute | solution.py:344
  3.8 1.0 constant_dynamic-slice_fusion
  4.8 0.2 collective-permute-start.2
  5.0 1.2 %collective-permute-done.2.got_ref = f32[256,128]{1,0:T(8,128)S(1)} collective-permute-done((f32[256,128]{1,0:T(8,128)S(1)}, f32[256,128]{1,0:T(8,128)S(1)}, u32[]{:S(2)}, u32[]{:S(2)}) %collective-permute-start.2) | collective-permute-done | bytes 131104 | tf_op jit(solution)/shard_map/ppermute | solution.py:344
  6.2 0.2 shard_map.49
  6.4 0.4 collective-permute-start.4
  6.8 1.2 %copy-done = f32[1024,256]{1,0:T(8,128)S(1)} copy-done((f32[1024,256]{1,0:T(8,128)S(1)}, f32[1024,256]{1,0:T(8,128)}, u32[]{:S(2)}) %copy-start) | copy-done | bytes 1048600
  8.0 1.1 %shard_map.50 = (f32[512,128]{1,0:T(8,128)S(1)}, bf16[1024,512]{1,0:T(8,128)(2,1)S(1)}, bf16[1024,512]{1,0:T(8,128)(2,1)S(1)}, bf16[512,1024]{1,0:T(8,128)(2,1)S(1)}, bf16[512,1024]{1,0:T(8,128)(2,1)S(1)}) custom-call(f32[1024,256]{1,0:T(8,128)S(1)} %copy-done, f32[1024,256]{1,0:T(8,128)S(1)} %collective-permute-done.1.core_ref, ...), custom_call_target="tpu_custom_call" | custom-call | tf_op jit(solution)/shard_map/pallas_call | solution.py:297
  9.1 18.9 %collective-permute-done.side_ref = f32[1024,256]{1,0:T(8,128)S(1)} collective-permute-done((f32[1024,256]{1,0:T(8,128)}, f32[1024,256]{1,0:T(8,128)S(1)}, u32[]{:S(2)}, u32[]{:S(2)}) %collective-permute-start) | collective-permute-done | bytes 1048608 | tf_op jit(solution)/shard_map/ppermute | solution.py:344
  28.0 0.6 shard_map.51
  28.7 1.9 %collective-permute-done.4.sketch_ref = f32[256,128]{1,0:T(8,128)S(1)} collective-permute-done((f32[256,128]{1,0:T(8,128)S(1)}, f32[256,128]{1,0:T(8,128)S(1)}, u32[]{:S(2)}, u32[]{:S(2)}) %collective-permute-start.4) | collective-permute-done | bytes 131104 | tf_op jit(solution)/shard_map/ppermute | solution.py:344
  30.6 0.6 shard_map.52.near_ref
  31.1 0.7 shard_map.53
  31.8 5.7 %collective-permute-start.6 = (f32[256,128]{1,0:T(8,128)S(1)}, f32[256,128]{1,0:T(8,128)S(1)}, u32[]{:S(2)}, u32[]{:S(2)}) collective-permute-start(f32[256,128]{1,0:T(8,128)S(1)} %get-tuple-element.53.a_ref), channel_id=1, source_target_pairs={{0,6},{1,7},{6,0},{7,1},{8,14},{9,15},{14,8},{15,9},{16,22},{17,23... | collective-permute-start | bytes 393224 | tf_op jit(solution)/shard_map/ppermute | solution.py:352
  37.5 0.7 collective-permute-start.5
  38.2 0.7 shard_map.55
  38.9 2.0 %collective-permute-start.16 = (f32[256,128]{1,0:T(8,128)S(1)}, f32[256,128]{1,0:T(8,128)S(1)}, u32[]{:S(2)}, u32[]{:S(2)}) collective-permute-start(f32[256,128]{1,0:T(8,128)S(1)} %get-tuple-element.68.a_ref), channel_id=1, source_target_pairs={{0,6},{1,7},{6,0},{7,1},{8,14},{9,15},{14,8},{15,9},{16,22},{17,23... | collective-permute-start | bytes 393224 | tf_op jit(solution)/shard_map/ppermute | solution.py:352
  40.9 0.7 collective-permute-start.15
  41.6 0.8 shard_map.54
  42.4 1.7 %collective-permute-start.7 = (f32[264,128]{1,0:T(8,128)S(1)}, f32[264,128]{1,0:T(8,128)S(1)}, u32[]{:S(2)}, u32[]{:S(2)}) collective-permute-start(f32[264,128]{1,0:T(8,128)S(1)} %shard_map.54), channel_id=1, source_target_pairs={{0,8},{1,17},{2,10},{3,19},{4,12},{5,21},{6,14},{7,23},{8,0},{9,25... | collective-permute-start | bytes 405512 | tf_op jit(solution)/shard_map/ppermute | solution.py:360
  44.1 3.6 %collective-permute-done.16 = f32[256,128]{1,0:T(8,128)S(1)} collective-permute-done((f32[256,128]{1,0:T(8,128)S(1)}, f32[256,128]{1,0:T(8,128)S(1)}, u32[]{:S(2)}, u32[]{:S(2)}) %collective-permute-start.16) | collective-permute-done | bytes 131104 | tf_op jit(solution)/shard_map/ppermute | solution.py:352
  47.7 0.8 shard_map.59
  48.5 1.5 %collective-permute-start.17 = (f32[264,128]{1,0:T(8,128)S(1)}, f32[264,128]{1,0:T(8,128)S(1)}, u32[]{:S(2)}, u32[]{:S(2)}) collective-permute-start(f32[264,128]{1,0:T(8,128)S(1)} %shard_map.59), channel_id=1, source_target_pairs={{0,8},{1,17},{2,10},{3,19},{4,12},{5,21},{6,14},{7,23},{8,0},{9,25... | collective-permute-start | bytes 405512 | tf_op jit(solution)/shard_map/ppermute | solution.py:360
  50.0 1.6 %collective-permute-start.8 = (f32[264,128]{1,0:T(8,128)S(1)}, f32[264,128]{1,0:T(8,128)S(1)}, u32[]{:S(2)}, u32[]{:S(2)}) collective-permute-start(f32[264,128]{1,0:T(8,128)S(1)} %add.39.refs_0_), channel_id=1, source_target_pairs={{0,16},{1,9},{2,18},{3,11},{4,20},{5,13},{6,22},{7,15},{8,24},{9,1... | collective-permute-start | bytes 405512 | tf_op jit(solution)/shard_map/ppermute | solution.py:360
  51.6 2.4 %collective-permute-done.17 = f32[264,128]{1,0:T(8,128)S(1)} collective-permute-done((f32[264,128]{1,0:T(8,128)S(1)}, f32[264,128]{1,0:T(8,128)S(1)}, u32[]{:S(2)}, u32[]{:S(2)}) %collective-permute-start.17) | collective-permute-done | bytes 135200 | tf_op jit(solution)/shard_map/ppermute | solution.py:360
  54.0 1.1 %collective-permute-start.18 = (f32[264,128]{1,0:T(8,128)S(1)}, f32[264,128]{1,0:T(8,128)S(1)}, u32[]{:S(2)}, u32[]{:S(2)}) collective-permute-start(f32[264,128]{1,0:T(8,128)S(1)} %add.44.refs_0_), channel_id=1, source_target_pairs={{0,16},{1,9},{2,18},{3,11},{4,20},{5,13},{6,22},{7,15},{8,24},{9,1... | collective-permute-start | bytes 405512 | tf_op jit(solution)/shard_map/ppermute | solution.py:360
  55.2 0.9 shard_map.56
  56.1 3.6 %collective-permute-start.10 = (f32[264,128]{1,0:T(8,128)S(1)}, f32[264,128]{1,0:T(8,128)S(1)}, u32[]{:S(2)}, u32[]{:S(2)}) collective-permute-start(f32[264,128]{1,0:T(8,128)S(1)} %get-tuple-element.64.refs_0_), channel_id=1, source_target_pairs={{0,6},{1,7},{6,0},{7,1},{8,14},{9,15},{14,8},{15,9},{16,22},{17,23... | collective-permute-start | bytes 405512 | tf_op jit(solution)/shard_map/ppermute | solution.py:352
  59.7 0.7 collective-permute-start.9
  60.4 0.9 shard_map.60
  61.3 4.1 %collective-permute-start.20 = (f32[264,128]{1,0:T(8,128)S(1)}, f32[264,128]{1,0:T(8,128)S(1)}, u32[]{:S(2)}, u32[]{:S(2)}) collective-permute-start(f32[264,128]{1,0:T(8,128)S(1)} %get-tuple-element.69.refs_0_), channel_id=1, source_target_pairs={{0,6},{1,7},{6,0},{7,1},{8,14},{9,15},{14,8},{15,9},{16,22},{17,23... | collective-permute-start | bytes 405512 | tf_op jit(solution)/shard_map/ppermute | solution.py:352
  65.4 0.7 collective-permute-start.19
  66.1 0.9 shard_map.57
  67.0 1.5 %collective-permute-start.11 = (f32[264,128]{1,0:T(8,128)S(1)}, f32[264,128]{1,0:T(8,128)S(1)}, u32[]{:S(2)}, u32[]{:S(2)}) collective-permute-start(f32[264,128]{1,0:T(8,128)S(1)} %get-tuple-element.65), channel_id=1, source_target_pairs={{0,8},{1,17},{2,10},{3,19},{4,12},{5,21},{6,14},{7,23},{8,0},{9,25... | collective-permute-start | bytes 405512 | tf_op jit(solution)/shard_map/ppermute | solution.py:360
  68.5 1.6 %collective-permute-done.20 = f32[264,128]{1,0:T(8,128)S(1)} collective-permute-done((f32[264,128]{1,0:T(8,128)S(1)}, f32[264,128]{1,0:T(8,128)S(1)}, u32[]{:S(2)}, u32[]{:S(2)}) %collective-permute-start.20) | collective-permute-done | bytes 135200 | tf_op jit(solution)/shard_map/ppermute | solution.py:352
  70.1 0.9 shard_map.61
  71.0 1.5 %collective-permute-start.21 = (f32[264,128]{1,0:T(8,128)S(1)}, f32[264,128]{1,0:T(8,128)S(1)}, u32[]{:S(2)}, u32[]{:S(2)}) collective-permute-start(f32[264,128]{1,0:T(8,128)S(1)} %get-tuple-element.70), channel_id=1, source_target_pairs={{0,8},{1,17},{2,10},{3,19},{4,12},{5,21},{6,14},{7,23},{8,0},{9,25... | collective-permute-start | bytes 405512 | tf_op jit(solution)/shard_map/ppermute | solution.py:360
  72.5 0.1 collective-permute-done.11
  72.6 2.2 %collective-permute-start.12 = (f32[264,128]{1,0:T(8,128)S(1)}, f32[264,128]{1,0:T(8,128)S(1)}, u32[]{:S(2)}, u32[]{:S(2)}) collective-permute-start(f32[264,128]{1,0:T(8,128)S(1)} %add.41.refs_0_), channel_id=1, source_target_pairs={{0,16},{1,9},{2,18},{3,11},{4,20},{5,13},{6,22},{7,15},{8,24},{9,1... | collective-permute-start | bytes 405512 | tf_op jit(solution)/shard_map/ppermute | solution.py:360
  74.9 2.3 %collective-permute-done.21 = f32[264,128]{1,0:T(8,128)S(1)} collective-permute-done((f32[264,128]{1,0:T(8,128)S(1)}, f32[264,128]{1,0:T(8,128)S(1)}, u32[]{:S(2)}, u32[]{:S(2)}) %collective-permute-start.21) | collective-permute-done | bytes 135200 | tf_op jit(solution)/shard_map/ppermute | solution.py:360
  77.2 1.1 %collective-permute-start.22 = (f32[264,128]{1,0:T(8,128)S(1)}, f32[264,128]{1,0:T(8,128)S(1)}, u32[]{:S(2)}, u32[]{:S(2)}) collective-permute-start(f32[264,128]{1,0:T(8,128)S(1)} %add.46.refs_0_), channel_id=1, source_target_pairs={{0,16},{1,9},{2,18},{3,11},{4,20},{5,13},{6,22},{7,15},{8,24},{9,1... | collective-permute-start | bytes 405512 | tf_op jit(solution)/shard_map/ppermute | solution.py:360
  78.4 0.9 shard_map.58
  79.3 3.6 %collective-permute-start.14 = (f32[264,128]{1,0:T(8,128)S(1)}, f32[264,128]{1,0:T(8,128)S(1)}, u32[]{:S(2)}, u32[]{:S(2)}) collective-permute-start(f32[264,128]{1,0:T(8,128)S(1)} %get-tuple-element.66.own_ref), channel_id=1, source_target_pairs={{0,6},{1,7},{6,0},{7,1},{8,14},{9,15},{14,8},{15,9},{16,22},{17,23... | collective-permute-start | bytes 405512 | tf_op jit(solution)/shard_map/ppermute | solution.py:352
  82.8 0.7 collective-permute-start.13
  83.5 0.9 shard_map.62
  84.4 4.1 %collective-permute-start.24 = (f32[264,128]{1,0:T(8,128)S(1)}, f32[264,128]{1,0:T(8,128)S(1)}, u32[]{:S(2)}, u32[]{:S(2)}) collective-permute-start(f32[264,128]{1,0:T(8,128)S(1)} %get-tuple-element.76.own_ref), channel_id=1, source_target_pairs={{0,6},{1,7},{6,0},{7,1},{8,14},{9,15},{14,8},{15,9},{16,22},{17,23... | collective-permute-start | bytes 405512 | tf_op jit(solution)/shard_map/ppermute | solution.py:352
  88.5 0.7 collective-permute-start.23
  89.3 0.2 shard_map.63
  89.5 4.2 %collective-permute-start.25 = (f32[328,128]{1,0:T(8,128)S(1)}, f32[328,128]{1,0:T(8,128)S(1)}, u32[]{:S(2)}, u32[]{:S(2)}) collective-permute-start(f32[328,128]{1,0:T(8,128)S(1)} %get-tuple-element.81), channel_id=1, source_target_pairs={{0,2},{1,3},{2,0},{3,1},{4,6},{5,7},{6,4},{7,5},{8,10},{9,11},{10,... | collective-permute-start | bytes 503816 | tf_op jit(solution)/shard_map/ppermute | solution.py:344
  93.7 0.8 collective-permute-done.24
  94.5 0.2 shard_map.64
  94.7 2.2 %collective-permute-start.26 = (f32[72,128]{1,0:T(8,128)S(1)}, f32[72,128]{1,0:T(8,128)S(1)}, u32[]{:S(2)}, u32[]{:S(2)}) collective-permute-start(f32[72,128]{1,0:T(8,128)S(1)} %get-tuple-element.82), channel_id=1, source_target_pairs={{0,2},{1,3},{2,0},{3,1},{4,6},{5,7},{6,4},{7,5},{8,10},{9,11},{10,... | collective-permute-start | bytes 110600 | tf_op jit(solution)/shard_map/ppermute | solution.py:344
  96.9 1.9 %collective-permute-done.26.refs_3_ = f32[72,128]{1,0:T(8,128)S(1)} collective-permute-done((f32[72,128]{1,0:T(8,128)S(1)}, f32[72,128]{1,0:T(8,128)S(1)}, u32[]{:S(2)}, u32[]{:S(2)}) %collective-permute-start.26) | collective-permute-done | bytes 36896 | tf_op jit(solution)/shard_map/ppermute | solution.py:344
  99.0 1.4 %collective-permute-done.27.got_ref.refs_3_ = f32[392,128]{1,0:T(8,128)S(1)} collective-permute-done((f32[392,128]{1,0:T(8,128)S(1)}, f32[392,128]{1,0:T(8,128)S(1)}, u32[]{:S(2)}, u32[]{:S(2)}) %collective-permute-start.27) | collective-permute-done | bytes 200736 | tf_op jit(solution)/shard_map/ppermute | solution.py:344
  100.4 0.1 shard_map.66
  100.5 2.3 %collective-permute-start.30 = (f32[8,256]{1,0:T(8,128)S(1)}, f32[8,256]{1,0:T(8,128)S(1)}, u32[]{:S(2)}, u32[]{:S(2)}) collective-permute-start(f32[8,256]{1,0:T(8,128)S(1)} %get-tuple-element.86.known_ref.refs_4_), channel_id=1, source_target_pairs={{0,24},{8,16},{16,8},{24,0},{1,25},{9,17},{17,9},{25,1},{2,26},{10... | collective-permute-start | bytes 24584 | tf_op jit(solution)/shard_map/ppermute | solution.py:441
  102.8 0.7 collective-permute-start.29
  103.5 0.5 collective-permute-start.28
  104.1 0.8 shard_map.68
  104.9 0.2 collective-permute-done.30.refs_2_
  105.1 1.3 %collective-permute-done.29.refs_1_ = f32[8,256]{1,0:T(8,128)S(1)} collective-permute-done((f32[8,256]{1,0:T(8,128)S(1)}, f32[8,256]{1,0:T(8,128)S(1)}, u32[]{:S(2)}, u32[]{:S(2)}) %collective-permute-start.29) | collective-permute-done | bytes 8224 | tf_op jit(solution)/shard_map/ppermute | solution.py:441
  106.5 0.7 collective-permute-done.28.refs_0_
  107.2 0.7 shard_map.67
  (31 shorter events, 0.3 us)
Async XLA Ops:
  0.6 6.2 %collective-permute-start.1 = (f32[1024,256]{1,0:T(8,128)}, f32[1024,256]{1,0:T(8,128)S(1)}, u32[]{:S(2)}, u32[]{:S(2)}) collective-permute-start(f32[1024,256]{1,0:T(8,128)} %own_ref.1), channel_id=1, source_target_pairs={{0,1},{1,0},{2,3},{3,2},{4,5},{5,4},{6,7},{7,6},{8,9},{9,8},{10,11... | collective-permute-start | bytes 3145736 | tf_op jit(solution)/shard_map/ppermute | solution.py:344
  1.1 26.9 %collective-permute-start = (f32[1024,256]{1,0:T(8,128)}, f32[1024,256]{1,0:T(8,128)S(1)}, u32[]{:S(2)}, u32[]{:S(2)}) collective-permute-start(f32[1024,256]{1,0:T(8,128)} %own_ref.1), channel_id=1, source_target_pairs={{0,2},{1,3},{2,0},{3,1},{4,6},{5,7},{6,4},{7,5},{8,10},{9,11},{10,... | collective-permute-start | bytes 3145736 | tf_op jit(solution)/shard_map/ppermute | solution.py:344
  4.8 1.4 %collective-permute-start.2 = (f32[256,128]{1,0:T(8,128)S(1)}, f32[256,128]{1,0:T(8,128)S(1)}, u32[]{:S(2)}, u32[]{:S(2)}) collective-permute-start(f32[256,128]{1,0:T(8,128)S(1)} %get-tuple-element.89), channel_id=1, source_target_pairs={{0,1},{1,0},{2,3},{3,2},{4,5},{5,4},{6,7},{7,6},{8,9},{9,8},{10,11... | collective-permute-start | bytes 393224 | tf_op jit(solution)/shard_map/ppermute | solution.py:344
  6.4 24.2 %collective-permute-start.4 = (f32[256,128]{1,0:T(8,128)S(1)}, f32[256,128]{1,0:T(8,128)S(1)}, u32[]{:S(2)}, u32[]{:S(2)}) collective-permute-start(f32[256,128]{1,0:T(8,128)S(1)} %get-tuple-element.49), channel_id=1, source_target_pairs={{0,2},{1,3},{2,0},{3,1},{4,6},{5,7},{6,4},{7,5},{8,10},{9,11},{10,... | collective-permute-start | bytes 393224 | tf_op jit(solution)/shard_map/ppermute | solution.py:344
  6.8 1.2 %copy-start = (f32[1024,256]{1,0:T(8,128)S(1)}, f32[1024,256]{1,0:T(8,128)}, u32[]{:S(2)}) copy-start(f32[1024,256]{1,0:T(8,128)} %own_ref.1) | copy-start | bytes 3145732
  28.0 3.1 %collective-permute-start.3 = (f32[1024,256]{1,0:T(8,128)S(1)}, f32[1024,256]{1,0:T(8,128)S(1)}, u32[]{:S(2)}, u32[]{:S(2)}) collective-permute-start(f32[1024,256]{1,0:T(8,128)S(1)} %collective-permute-done.side_ref), channel_id=1, source_target_pairs={{0,1},{1,0},{2,3},{3,2},{4,5},{5,4},{6,7},{7,6},{8,9},{9,8},{10,11... | collective-permute-start | bytes 3145736 | tf_op jit(solution)/shard_map/ppermute | solution.py:344
  31.8 9.7 %collective-permute-start.6 = (f32[256,128]{1,0:T(8,128)S(1)}, f32[256,128]{1,0:T(8,128)S(1)}, u32[]{:S(2)}, u32[]{:S(2)}) collective-permute-start(f32[256,128]{1,0:T(8,128)S(1)} %get-tuple-element.53.a_ref), channel_id=1, source_target_pairs={{0,6},{1,7},{6,0},{7,1},{8,14},{9,15},{14,8},{15,9},{16,22},{17,23... | collective-permute-start | bytes 393224 | tf_op jit(solution)/shard_map/ppermute | solution.py:352
  37.5 4.0 %collective-permute-start.5 = (f32[256,128]{1,0:T(8,128)S(1)}, f32[256,128]{1,0:T(8,128)S(1)}, u32[]{:S(2)}, u32[]{:S(2)}) collective-permute-start(f32[256,128]{1,0:T(8,128)S(1)} %get-tuple-element.53.a_ref), channel_id=1, source_target_pairs={{2,4},{3,5},{4,2},{5,3},{10,12},{11,13},{12,10},{13,11},{18,20},{1... | collective-permute-start | bytes 393224 | tf_op jit(solution)/shard_map/ppermute | solution.py:352
  38.9 8.8 %collective-permute-start.16 = (f32[256,128]{1,0:T(8,128)S(1)}, f32[256,128]{1,0:T(8,128)S(1)}, u32[]{:S(2)}, u32[]{:S(2)}) collective-permute-start(f32[256,128]{1,0:T(8,128)S(1)} %get-tuple-element.68.a_ref), channel_id=1, source_target_pairs={{0,6},{1,7},{6,0},{7,1},{8,14},{9,15},{14,8},{15,9},{16,22},{17,23... | collective-permute-start | bytes 393224 | tf_op jit(solution)/shard_map/ppermute | solution.py:352
  40.9 6.8 %collective-permute-start.15 = (f32[256,128]{1,0:T(8,128)S(1)}, f32[256,128]{1,0:T(8,128)S(1)}, u32[]{:S(2)}, u32[]{:S(2)}) collective-permute-start(f32[256,128]{1,0:T(8,128)S(1)} %get-tuple-element.68.a_ref), channel_id=1, source_target_pairs={{2,4},{3,5},{4,2},{5,3},{10,12},{11,13},{12,10},{13,11},{18,20},{1... | collective-permute-start | bytes 393224 | tf_op jit(solution)/shard_map/ppermute | solution.py:352
  42.4 7.6 %collective-permute-start.7 = (f32[264,128]{1,0:T(8,128)S(1)}, f32[264,128]{1,0:T(8,128)S(1)}, u32[]{:S(2)}, u32[]{:S(2)}) collective-permute-start(f32[264,128]{1,0:T(8,128)S(1)} %shard_map.54), channel_id=1, source_target_pairs={{0,8},{1,17},{2,10},{3,19},{4,12},{5,21},{6,14},{7,23},{8,0},{9,25... | collective-permute-start | bytes 405512 | tf_op jit(solution)/shard_map/ppermute | solution.py:360
  48.5 5.5 %collective-permute-start.17 = (f32[264,128]{1,0:T(8,128)S(1)}, f32[264,128]{1,0:T(8,128)S(1)}, u32[]{:S(2)}, u32[]{:S(2)}) collective-permute-start(f32[264,128]{1,0:T(8,128)S(1)} %shard_map.59), channel_id=1, source_target_pairs={{0,8},{1,17},{2,10},{3,19},{4,12},{5,21},{6,14},{7,23},{8,0},{9,25... | collective-permute-start | bytes 405512 | tf_op jit(solution)/shard_map/ppermute | solution.py:360
  50.0 5.1 %collective-permute-start.8 = (f32[264,128]{1,0:T(8,128)S(1)}, f32[264,128]{1,0:T(8,128)S(1)}, u32[]{:S(2)}, u32[]{:S(2)}) collective-permute-start(f32[264,128]{1,0:T(8,128)S(1)} %add.39.refs_0_), channel_id=1, source_target_pairs={{0,16},{1,9},{2,18},{3,11},{4,20},{5,13},{6,22},{7,15},{8,24},{9,1... | collective-permute-start | bytes 405512 | tf_op jit(solution)/shard_map/ppermute | solution.py:360
  54.0 6.3 %collective-permute-start.18 = (f32[264,128]{1,0:T(8,128)S(1)}, f32[264,128]{1,0:T(8,128)S(1)}, u32[]{:S(2)}, u32[]{:S(2)}) collective-permute-start(f32[264,128]{1,0:T(8,128)S(1)} %add.44.refs_0_), channel_id=1, source_target_pairs={{0,16},{1,9},{2,18},{3,11},{4,20},{5,13},{6,22},{7,15},{8,24},{9,1... | collective-permute-start | bytes 405512 | tf_op jit(solution)/shard_map/ppermute | solution.py:360
  56.1 9.9 %collective-permute-start.10 = (f32[264,128]{1,0:T(8,128)S(1)}, f32[264,128]{1,0:T(8,128)S(1)}, u32[]{:S(2)}, u32[]{:S(2)}) collective-permute-start(f32[264,128]{1,0:T(8,128)S(1)} %get-tuple-element.64.refs_0_), channel_id=1, source_target_pairs={{0,6},{1,7},{6,0},{7,1},{8,14},{9,15},{14,8},{15,9},{16,22},{17,23... | collective-permute-start | bytes 405512 | tf_op jit(solution)/shard_map/ppermute | solution.py:352
  59.7 6.4 %collective-permute-start.9 = (f32[264,128]{1,0:T(8,128)S(1)}, f32[264,128]{1,0:T(8,128)S(1)}, u32[]{:S(2)}, u32[]{:S(2)}) collective-permute-start(f32[264,128]{1,0:T(8,128)S(1)} %get-tuple-element.64.refs_0_), channel_id=1, source_target_pairs={{2,4},{3,5},{4,2},{5,3},{10,12},{11,13},{12,10},{13,11},{18,20},{1... | collective-permute-start | bytes 405512 | tf_op jit(solution)/shard_map/ppermute | solution.py:352
  61.3 8.8 %collective-permute-start.20 = (f32[264,128]{1,0:T(8,128)S(1)}, f32[264,128]{1,0:T(8,128)S(1)}, u32[]{:S(2)}, u32[]{:S(2)}) collective-permute-start(f32[264,128]{1,0:T(8,128)S(1)} %get-tuple-element.69.refs_0_), channel_id=1, source_target_pairs={{0,6},{1,7},{6,0},{7,1},{8,14},{9,15},{14,8},{15,9},{16,22},{17,23... | collective-permute-start | bytes 405512 | tf_op jit(solution)/shard_map/ppermute | solution.py:352
  65.4 4.7 %collective-permute-start.19 = (f32[264,128]{1,0:T(8,128)S(1)}, f32[264,128]{1,0:T(8,128)S(1)}, u32[]{:S(2)}, u32[]{:S(2)}) collective-permute-start(f32[264,128]{1,0:T(8,128)S(1)} %get-tuple-element.69.refs_0_), channel_id=1, source_target_pairs={{2,4},{3,5},{4,2},{5,3},{10,12},{11,13},{12,10},{13,11},{18,20},{1... | collective-permute-start | bytes 405512 | tf_op jit(solution)/shard_map/ppermute | solution.py:352
  67.0 5.7 %collective-permute-start.11 = (f32[264,128]{1,0:T(8,128)S(1)}, f32[264,128]{1,0:T(8,128)S(1)}, u32[]{:S(2)}, u32[]{:S(2)}) collective-permute-start(f32[264,128]{1,0:T(8,128)S(1)} %get-tuple-element.65), channel_id=1, source_target_pairs={{0,8},{1,17},{2,10},{3,19},{4,12},{5,21},{6,14},{7,23},{8,0},{9,25... | collective-permute-start | bytes 405512 | tf_op jit(solution)/shard_map/ppermute | solution.py:360
  71.0 6.2 %collective-permute-start.21 = (f32[264,128]{1,0:T(8,128)S(1)}, f32[264,128]{1,0:T(8,128)S(1)}, u32[]{:S(2)}, u32[]{:S(2)}) collective-permute-start(f32[264,128]{1,0:T(8,128)S(1)} %get-tuple-element.70), channel_id=1, source_target_pairs={{0,8},{1,17},{2,10},{3,19},{4,12},{5,21},{6,14},{7,23},{8,0},{9,25... | collective-permute-start | bytes 405512 | tf_op jit(solution)/shard_map/ppermute | solution.py:360
  72.6 5.7 %collective-permute-start.12 = (f32[264,128]{1,0:T(8,128)S(1)}, f32[264,128]{1,0:T(8,128)S(1)}, u32[]{:S(2)}, u32[]{:S(2)}) collective-permute-start(f32[264,128]{1,0:T(8,128)S(1)} %add.41.refs_0_), channel_id=1, source_target_pairs={{0,16},{1,9},{2,18},{3,11},{4,20},{5,13},{6,22},{7,15},{8,24},{9,1... | collective-permute-start | bytes 405512 | tf_op jit(solution)/shard_map/ppermute | solution.py:360
  77.2 6.3 %collective-permute-start.22 = (f32[264,128]{1,0:T(8,128)S(1)}, f32[264,128]{1,0:T(8,128)S(1)}, u32[]{:S(2)}, u32[]{:S(2)}) collective-permute-start(f32[264,128]{1,0:T(8,128)S(1)} %add.46.refs_0_), channel_id=1, source_target_pairs={{0,16},{1,9},{2,18},{3,11},{4,20},{5,13},{6,22},{7,15},{8,24},{9,1... | collective-permute-start | bytes 405512 | tf_op jit(solution)/shard_map/ppermute | solution.py:360
  79.3 10.0 %collective-permute-start.14 = (f32[264,128]{1,0:T(8,128)S(1)}, f32[264,128]{1,0:T(8,128)S(1)}, u32[]{:S(2)}, u32[]{:S(2)}) collective-permute-start(f32[264,128]{1,0:T(8,128)S(1)} %get-tuple-element.66.own_ref), channel_id=1, source_target_pairs={{0,6},{1,7},{6,0},{7,1},{8,14},{9,15},{14,8},{15,9},{16,22},{17,23... | collective-permute-start | bytes 405512 | tf_op jit(solution)/shard_map/ppermute | solution.py:352
  82.8 6.4 %collective-permute-start.13 = (f32[264,128]{1,0:T(8,128)S(1)}, f32[264,128]{1,0:T(8,128)S(1)}, u32[]{:S(2)}, u32[]{:S(2)}) collective-permute-start(f32[264,128]{1,0:T(8,128)S(1)} %get-tuple-element.66.own_ref), channel_id=1, source_target_pairs={{2,4},{3,5},{4,2},{5,3},{10,12},{11,13},{12,10},{13,11},{18,20},{1... | collective-permute-start | bytes 405512 | tf_op jit(solution)/shard_map/ppermute | solution.py:352
  84.4 10.1 %collective-permute-start.24 = (f32[264,128]{1,0:T(8,128)S(1)}, f32[264,128]{1,0:T(8,128)S(1)}, u32[]{:S(2)}, u32[]{:S(2)}) collective-permute-start(f32[264,128]{1,0:T(8,128)S(1)} %get-tuple-element.76.own_ref), channel_id=1, source_target_pairs={{0,6},{1,7},{6,0},{7,1},{8,14},{9,15},{14,8},{15,9},{16,22},{17,23... | collective-permute-start | bytes 405512 | tf_op jit(solution)/shard_map/ppermute | solution.py:352
  88.5 6.0 %collective-permute-start.23 = (f32[264,128]{1,0:T(8,128)S(1)}, f32[264,128]{1,0:T(8,128)S(1)}, u32[]{:S(2)}, u32[]{:S(2)}) collective-permute-start(f32[264,128]{1,0:T(8,128)S(1)} %get-tuple-element.76.own_ref), channel_id=1, source_target_pairs={{2,4},{3,5},{4,2},{5,3},{10,12},{11,13},{12,10},{13,11},{18,20},{1... | collective-permute-start | bytes 405512 | tf_op jit(solution)/shard_map/ppermute | solution.py:352
  89.5 9.4 %collective-permute-start.25 = (f32[328,128]{1,0:T(8,128)S(1)}, f32[328,128]{1,0:T(8,128)S(1)}, u32[]{:S(2)}, u32[]{:S(2)}) collective-permute-start(f32[328,128]{1,0:T(8,128)S(1)} %get-tuple-element.81), channel_id=1, source_target_pairs={{0,2},{1,3},{2,0},{3,1},{4,6},{5,7},{6,4},{7,5},{8,10},{9,11},{10,... | collective-permute-start | bytes 503816 | tf_op jit(solution)/shard_map/ppermute | solution.py:344
  94.7 4.1 %collective-permute-start.26 = (f32[72,128]{1,0:T(8,128)S(1)}, f32[72,128]{1,0:T(8,128)S(1)}, u32[]{:S(2)}, u32[]{:S(2)}) collective-permute-start(f32[72,128]{1,0:T(8,128)S(1)} %get-tuple-element.82), channel_id=1, source_target_pairs={{0,2},{1,3},{2,0},{3,1},{4,6},{5,7},{6,4},{7,5},{8,10},{9,11},{10,... | collective-permute-start | bytes 110600 | tf_op jit(solution)/shard_map/ppermute | solution.py:344
  99.0 1.5 %collective-permute-start.27 = (f32[392,128]{1,0:T(8,128)S(1)}, f32[392,128]{1,0:T(8,128)S(1)}, u32[]{:S(2)}, u32[]{:S(2)}) collective-permute-start(f32[392,128]{1,0:T(8,128)S(1)} %get-tuple-element.84), channel_id=1, source_target_pairs={{0,1},{1,0},{2,3},{3,2},{4,5},{5,4},{6,7},{7,6},{8,9},{9,8},{10,11... | collective-permute-start | bytes 602120 | tf_op jit(solution)/shard_map/ppermute | solution.py:344
  100.5 4.6 %collective-permute-start.30 = (f32[8,256]{1,0:T(8,128)S(1)}, f32[8,256]{1,0:T(8,128)S(1)}, u32[]{:S(2)}, u32[]{:S(2)}) collective-permute-start(f32[8,256]{1,0:T(8,128)S(1)} %get-tuple-element.86.known_ref.refs_4_), channel_id=1, source_target_pairs={{0,24},{8,16},{16,8},{24,0},{1,25},{9,17},{17,9},{25,1},{2,26},{10... | collective-permute-start | bytes 24584 | tf_op jit(solution)/shard_map/ppermute | solution.py:441
  102.8 3.7 %collective-permute-start.29 = (f32[8,256]{1,0:T(8,128)S(1)}, f32[8,256]{1,0:T(8,128)S(1)}, u32[]{:S(2)}, u32[]{:S(2)}) collective-permute-start(f32[8,256]{1,0:T(8,128)S(1)} %get-tuple-element.86.known_ref.refs_4_), channel_id=1, source_target_pairs={{0,16},{8,24},{16,0},{24,8},{1,17},{9,25},{17,1},{25,9},{2,18},{10... | collective-permute-start | bytes 24584 | tf_op jit(solution)/shard_map/ppermute | solution.py:441
  103.5 3.7 %collective-permute-start.28 = (f32[8,256]{1,0:T(8,128)S(1)}, f32[8,256]{1,0:T(8,128)S(1)}, u32[]{:S(2)}, u32[]{:S(2)}) collective-permute-start(f32[8,256]{1,0:T(8,128)S(1)} %get-tuple-element.86.known_ref.refs_4_), channel_id=1, source_target_pairs={{0,8},{8,0},{16,24},{24,16},{1,9},{9,1},{17,25},{25,17},{2,10},{10... | collective-permute-start | bytes 24584 | tf_op jit(solution)/shard_map/ppermute | solution.py:441

commit v15 on v10

--- a/solution.py
+++ b/solution.py
@@ -354,9 +354,9 @@
         perm = [(c * places + i, target(c, i) * places + i) for c in range(groups) for i in range(places)]
         return lax.ppermute(x, ("cell", "snap"), perm)
 
-    def cell_pair(x):
-        x = x + swap_cell(x, 0)
-        return x, swap_cell(x, 1)
+    def cell_pair(x, h):
+        x = x + swap_cell(x, h)
+        return x, swap_cell(x, 1 - h)
 
     def factor(count):
         return [((rows, count * width), BF16)] * 2
@@ -402,7 +402,7 @@
         for h in range(HALVES):
             ys[h], scale, *z = call(
                 functools.partial(y_kernel, all_cells), [y_shape, scale_shape] + [z_shape] * last,
-                *cell_pair(sent[h]), *matrix_t,
+                *cell_pair(sent[h], h), *matrix_t,
             )
             scales[h].append(scale)
             if last:

time: 99.3 us -> 99.2 us (level)
    ppermute x14, waiting for transfers between devices: 35.7 us -> 36.8 us  [swap(): return lax.ppermute(x, 'snap', [(i, i ^ bits) for i in range(places)])]
where the time goes in v15:
time: 99.2 us; the launch traced here: 99 us
  waiting for transfers between devices  45.2 us (46%)
  starting transfers between devices  37.8 us (38%)
  Pallas kernels  13 us (13%)
  local copies, waits for them, and re-layouts  2.21 us (2%)
    ppermute x14, waiting for transfers between devices, swap(): return lax.ppermute(x, 'snap', [(i, i ^ bits) for i in range(places)])  36.8 us
    ppermute x14, starting transfers between devices, swap(): return lax.ppermute(x, 'snap', [(i, i ^ bits) for i in range(places)])  21.9 us
    pallas_call x20, Pallas kernels, call(): pl.pallas_call(kernel, out_shape=[jax.ShapeDtypeStruct(shape, dtype) for...  13 us
    ppermute x8, starting transfers between devices, swap_cell(): return lax.ppermute(x, ('cell', 'snap'), perm)  12.3 us
    ppermute x8, waiting for transfers between devices, swap_cell(): return lax.ppermute(x, ('cell', 'snap'), perm)  6.32 us
    ppermute x3, starting transfers between devices, local(): lax.ppermute(known, 'cell', [(c, c ^ d) for c in range(groups)])  3.55 us
    ppermute x3, waiting for transfers between devices, local(): lax.ppermute(known, 'cell', [(c, c ^ d) for c in range(groups)])  2.13 us
  transfers between devices with their start and end apart: 25, of which 18 were waited for; matrix products, arithmetic and copies ran while one was open for 1% of the time, Pallas kernels for 12%

profile of v15, /device:TPU:0, one launch (start us, length us, event | category | flops | bytes accessed | tf_op | source)
XLA Modules:
  0.0 99.0 jit_solution(12773388985877630362)
XLA Ops:
  0.6 0.5 collective-permute-start.1
  1.1 2.7 %collective-permute-start = (f32[1024,256]{1,0:T(8,128)}, f32[1024,256]{1,0:T(8,128)S(1)}, u32[]{:S(2)}, u32[]{:S(2)}) collective-permute-start(f32[1024,256]{1,0:T(8,128)} %own_ref.1), channel_id=1, source_target_pairs={{0,2},{1,3},{2,0},{3,1},{4,6},{5,7},{6,4},{7,5},{8,10},{9,11},{10,... | collective-permute-start | bytes 3145736 | tf_op jit(solution)/shard_map/ppermute | solution.py:344
  3.8 1.0 constant_dynamic-slice_fusion
  4.8 0.2 collective-permute-start.2
  5.0 1.2 %collective-permute-done.2.got_ref = f32[256,128]{1,0:T(8,128)S(1)} collective-permute-done((f32[256,128]{1,0:T(8,128)S(1)}, f32[256,128]{1,0:T(8,128)S(1)}, u32[]{:S(2)}, u32[]{:S(2)}) %collective-permute-start.2) | collective-permute-done | bytes 131104 | tf_op jit(solution)/shard_map/ppermute | solution.py:344
  6.2 0.2 shard_map.49
  6.4 0.4 collective-permute-start.4
  6.8 1.2 %copy-done = f32[1024,256]{1,0:T(8,128)S(1)} copy-done((f32[1024,256]{1,0:T(8,128)S(1)}, f32[1024,256]{1,0:T(8,128)}, u32[]{:S(2)}) %copy-start) | copy-done | bytes 1048600
  8.0 1.1 %shard_map.50 = (f32[512,128]{1,0:T(8,128)S(1)}, bf16[1024,512]{1,0:T(8,128)(2,1)S(1)}, bf16[1024,512]{1,0:T(8,128)(2,1)S(1)}, bf16[512,1024]{1,0:T(8,128)(2,1)S(1)}, bf16[512,1024]{1,0:T(8,128)(2,1)S(1)}) custom-call(f32[1024,256]{1,0:T(8,128)S(1)} %copy-done, f32[1024,256]{1,0:T(8,128)S(1)} %collective-permute-done.1.core_ref, ...), custom_call_target="tpu_custom_call" | custom-call | tf_op jit(solution)/shard_map/pallas_call | solution.py:297
  9.1 18.9 %collective-permute-done.side_ref = f32[1024,256]{1,0:T(8,128)S(1)} collective-permute-done((f32[1024,256]{1,0:T(8,128)}, f32[1024,256]{1,0:T(8,128)S(1)}, u32[]{:S(2)}, u32[]{:S(2)}) %collective-permute-start) | collective-permute-done | bytes 1048608 | tf_op jit(solution)/shard_map/ppermute | solution.py:344
  28.0 0.6 shard_map.51
  28.7 1.9 %collective-permute-done.4.sketch_ref = f32[256,128]{1,0:T(8,128)S(1)} collective-permute-done((f32[256,128]{1,0:T(8,128)S(1)}, f32[256,128]{1,0:T(8,128)S(1)}, u32[]{:S(2)}, u32[]{:S(2)}) %collective-permute-start.4) | collective-permute-done | bytes 131104 | tf_op jit(solution)/shard_map/ppermute | solution.py:344
  30.6 0.6 shard_map.52.near_ref
  31.1 0.7 shard_map.53
  31.8 3.8 %collective-permute-start.5 = (f32[256,128]{1,0:T(8,128)S(1)}, f32[256,128]{1,0:T(8,128)S(1)}, u32[]{:S(2)}, u32[]{:S(2)}) collective-permute-start(f32[256,128]{1,0:T(8,128)S(1)} %get-tuple-element.53.a_ref), channel_id=1, source_target_pairs={{0,6},{1,7},{2,4},{3,5},{4,2},{5,3},{6,0},{7,1},{8,14},{9,15},{10,... | collective-permute-start | bytes 393224 | tf_op jit(solution)/shard_map/ppermute | solution.py:344
  35.7 0.7 shard_map.55
  36.4 0.1 collective-permute-start.12
  36.5 3.1 %collective-permute-done.5.b_ref = f32[256,128]{1,0:T(8,128)S(1)} collective-permute-done((f32[256,128]{1,0:T(8,128)S(1)}, f32[256,128]{1,0:T(8,128)S(1)}, u32[]{:S(2)}, u32[]{:S(2)}) %collective-permute-start.5) | collective-permute-done | bytes 131104 | tf_op jit(solution)/shard_map/ppermute | solution.py:344
  39.6 0.8 shard_map.54
  40.4 1.5 %collective-permute-start.6 = (f32[264,128]{1,0:T(8,128)S(1)}, f32[264,128]{1,0:T(8,128)S(1)}, u32[]{:S(2)}, u32[]{:S(2)}) collective-permute-start(f32[264,128]{1,0:T(8,128)S(1)} %shard_map.54), channel_id=1, source_target_pairs={{0,8},{1,17},{2,10},{3,19},{4,12},{5,21},{6,14},{7,23},{8,0},{9,25... | collective-permute-start | bytes 405512 | tf_op jit(solution)/shard_map/ppermute | solution.py:355
  41.9 1.4 %collective-permute-done.12.b_ref = f32[256,128]{1,0:T(8,128)S(1)} collective-permute-done((f32[256,128]{1,0:T(8,128)S(1)}, f32[256,128]{1,0:T(8,128)S(1)}, u32[]{:S(2)}, u32[]{:S(2)}) %collective-permute-start.12) | collective-permute-done | bytes 131104 | tf_op jit(solution)/shard_map/ppermute | solution.py:344
  43.3 0.8 shard_map.59
  44.1 1.5 %collective-permute-start.13 = (f32[264,128]{1,0:T(8,128)S(1)}, f32[264,128]{1,0:T(8,128)S(1)}, u32[]{:S(2)}, u32[]{:S(2)}) collective-permute-start(f32[264,128]{1,0:T(8,128)S(1)} %shard_map.59), channel_id=1, source_target_pairs={{0,16},{1,9},{2,18},{3,11},{4,20},{5,13},{6,22},{7,15},{8,24},{9,1... | collective-permute-start | bytes 405512 | tf_op jit(solution)/shard_map/ppermute | solution.py:355
  45.7 1.5 %collective-permute-start.7 = (f32[264,128]{1,0:T(8,128)S(1)}, f32[264,128]{1,0:T(8,128)S(1)}, u32[]{:S(2)}, u32[]{:S(2)}) collective-permute-start(f32[264,128]{1,0:T(8,128)S(1)} %add.20.refs_0_), channel_id=1, source_target_pairs={{0,16},{1,9},{2,18},{3,11},{4,20},{5,13},{6,22},{7,15},{8,24},{9,1... | collective-permute-start | bytes 405512 | tf_op jit(solution)/shard_map/ppermute | solution.py:355
  47.2 1.9 %collective-permute-done.13 = f32[264,128]{1,0:T(8,128)S(1)} collective-permute-done((f32[264,128]{1,0:T(8,128)S(1)}, f32[264,128]{1,0:T(8,128)S(1)}, u32[]{:S(2)}, u32[]{:S(2)}) %collective-permute-start.13) | collective-permute-done | bytes 135200 | tf_op jit(solution)/shard_map/ppermute | solution.py:355
  49.2 1.6 %collective-permute-start.14 = (f32[264,128]{1,0:T(8,128)S(1)}, f32[264,128]{1,0:T(8,128)S(1)}, u32[]{:S(2)}, u32[]{:S(2)}) collective-permute-start(f32[264,128]{1,0:T(8,128)S(1)} %add.22.refs_0_), channel_id=1, source_target_pairs={{0,8},{1,17},{2,10},{3,19},{4,12},{5,21},{6,14},{7,23},{8,0},{9,25... | collective-permute-start | bytes 405512 | tf_op jit(solution)/shard_map/ppermute | solution.py:355
  50.7 1.4 %collective-permute-done.7.refs_1_ = f32[264,128]{1,0:T(8,128)S(1)} collective-permute-done((f32[264,128]{1,0:T(8,128)S(1)}, f32[264,128]{1,0:T(8,128)S(1)}, u32[]{:S(2)}, u32[]{:S(2)}) %collective-permute-start.7) | collective-permute-done | bytes 135200 | tf_op jit(solution)/shard_map/ppermute | solution.py:355
  52.2 0.9 shard_map.56
  53.1 4.2 %collective-permute-start.8 = (f32[264,128]{1,0:T(8,128)S(1)}, f32[264,128]{1,0:T(8,128)S(1)}, u32[]{:S(2)}, u32[]{:S(2)}) collective-permute-start(f32[264,128]{1,0:T(8,128)S(1)} %get-tuple-element.64.refs_0_), channel_id=1, source_target_pairs={{0,6},{1,7},{2,4},{3,5},{4,2},{5,3},{6,0},{7,1},{8,14},{9,15},{10,... | collective-permute-start | bytes 405512 | tf_op jit(solution)/shard_map/ppermute | solution.py:344
  57.3 0.9 shard_map.60
  58.2 0.7 collective-permute-start.15
  58.9 2.4 %collective-permute-done.8.refs_1_ = f32[264,128]{1,0:T(8,128)S(1)} collective-permute-done((f32[264,128]{1,0:T(8,128)S(1)}, f32[264,128]{1,0:T(8,128)S(1)}, u32[]{:S(2)}, u32[]{:S(2)}) %collective-permute-start.8) | collective-permute-done | bytes 135200 | tf_op jit(solution)/shard_map/ppermute | solution.py:344
  61.2 0.9 shard_map.57
  62.1 1.5 %collective-permute-start.9 = (f32[264,128]{1,0:T(8,128)S(1)}, f32[264,128]{1,0:T(8,128)S(1)}, u32[]{:S(2)}, u32[]{:S(2)}) collective-permute-start(f32[264,128]{1,0:T(8,128)S(1)} %get-tuple-element.65), channel_id=1, source_target_pairs={{0,8},{1,17},{2,10},{3,19},{4,12},{5,21},{6,14},{7,23},{8,0},{9,25... | collective-permute-start | bytes 405512 | tf_op jit(solution)/shard_map/ppermute | solution.py:355
  63.6 1.5 %collective-permute-done.15.refs_1_ = f32[264,128]{1,0:T(8,128)S(1)} collective-permute-done((f32[264,128]{1,0:T(8,128)S(1)}, f32[264,128]{1,0:T(8,128)S(1)}, u32[]{:S(2)}, u32[]{:S(2)}) %collective-permute-start.15) | collective-permute-done | bytes 135200 | tf_op jit(solution)/shard_map/ppermute | solution.py:344
  65.2 0.9 shard_map.61
  66.1 1.5 %collective-permute-start.16 = (f32[264,128]{1,0:T(8,128)S(1)}, f32[264,128]{1,0:T(8,128)S(1)}, u32[]{:S(2)}, u32[]{:S(2)}) collective-permute-start(f32[264,128]{1,0:T(8,128)S(1)} %get-tuple-element.70), channel_id=1, source_target_pairs={{0,16},{1,9},{2,18},{3,11},{4,20},{5,13},{6,22},{7,15},{8,24},{9,1... | collective-permute-start | bytes 405512 | tf_op jit(solution)/shard_map/ppermute | solution.py:355
  67.6 1.0 %collective-permute-done.9 = f32[264,128]{1,0:T(8,128)S(1)} collective-permute-done((f32[264,128]{1,0:T(8,128)S(1)}, f32[264,128]{1,0:T(8,128)S(1)}, u32[]{:S(2)}, u32[]{:S(2)}) %collective-permute-start.9) | collective-permute-done | bytes 135200 | tf_op jit(solution)/shard_map/ppermute | solution.py:355
  68.6 1.6 %collective-permute-start.10 = (f32[264,128]{1,0:T(8,128)S(1)}, f32[264,128]{1,0:T(8,128)S(1)}, u32[]{:S(2)}, u32[]{:S(2)}) collective-permute-start(f32[264,128]{1,0:T(8,128)S(1)} %add.21.refs_0_), channel_id=1, source_target_pairs={{0,16},{1,9},{2,18},{3,11},{4,20},{5,13},{6,22},{7,15},{8,24},{9,1... | collective-permute-start | bytes 405512 | tf_op jit(solution)/shard_map/ppermute | solution.py:355
  70.2 0.9 collective-permute-done.16
  71.1 1.5 %collective-permute-start.17 = (f32[264,128]{1,0:T(8,128)S(1)}, f32[264,128]{1,0:T(8,128)S(1)}, u32[]{:S(2)}, u32[]{:S(2)}) collective-permute-start(f32[264,128]{1,0:T(8,128)S(1)} %add.23.refs_0_), channel_id=1, source_target_pairs={{0,8},{1,17},{2,10},{3,19},{4,12},{5,21},{6,14},{7,23},{8,0},{9,25... | collective-permute-start | bytes 405512 | tf_op jit(solution)/shard_map/ppermute | solution.py:355
  72.7 1.0 %collective-permute-done.10.refs_1_ = f32[264,128]{1,0:T(8,128)S(1)} collective-permute-done((f32[264,128]{1,0:T(8,128)S(1)}, f32[264,128]{1,0:T(8,128)S(1)}, u32[]{:S(2)}, u32[]{:S(2)}) %collective-permute-start.10) | collective-permute-done | bytes 135200 | tf_op jit(solution)/shard_map/ppermute | solution.py:355
  73.7 0.9 shard_map.58
  74.6 1.6 %collective-permute-start.11 = (f32[264,128]{1,0:T(8,128)S(1)}, f32[264,128]{1,0:T(8,128)S(1)}, u32[]{:S(2)}, u32[]{:S(2)}) collective-permute-start(f32[264,128]{1,0:T(8,128)S(1)} %get-tuple-element.66.own_ref), channel_id=1, source_target_pairs={{0,6},{1,7},{2,4},{3,5},{4,2},{5,3},{6,0},{7,1},{8,14},{9,15},{10,... | collective-permute-start | bytes 405512 | tf_op jit(solution)/shard_map/ppermute | solution.py:344
  76.2 0.9 shard_map.62
  77.1 2.3 %collective-permute-start.18 = (f32[264,128]{1,0:T(8,128)S(1)}, f32[264,128]{1,0:T(8,128)S(1)}, u32[]{:S(2)}, u32[]{:S(2)}) collective-permute-start(f32[264,128]{1,0:T(8,128)S(1)} %get-tuple-element.76.own_ref), channel_id=1, source_target_pairs={{0,6},{1,7},{2,4},{3,5},{4,2},{5,3},{6,0},{7,1},{8,14},{9,15},{10,... | collective-permute-start | bytes 405512 | tf_op jit(solution)/shard_map/ppermute | solution.py:344
  79.5 2.2 %collective-permute-done.11.got_ref = f32[264,128]{1,0:T(8,128)S(1)} collective-permute-done((f32[264,128]{1,0:T(8,128)S(1)}, f32[264,128]{1,0:T(8,128)S(1)}, u32[]{:S(2)}, u32[]{:S(2)}) %collective-permute-start.11) | collective-permute-done | bytes 135200 | tf_op jit(solution)/shard_map/ppermute | solution.py:344
  81.7 0.2 shard_map.63
  81.9 4.0 %collective-permute-start.19 = (f32[328,128]{1,0:T(8,128)S(1)}, f32[328,128]{1,0:T(8,128)S(1)}, u32[]{:S(2)}, u32[]{:S(2)}) collective-permute-start(f32[328,128]{1,0:T(8,128)S(1)} %get-tuple-element.81), channel_id=1, source_target_pairs={{0,2},{1,3},{2,0},{3,1},{4,6},{5,7},{6,4},{7,5},{8,10},{9,11},{10,... | collective-permute-start | bytes 503816 | tf_op jit(solution)/shard_map/ppermute | solution.py:344
  85.9 0.2 shard_map.64
  86.1 1.3 %collective-permute-start.20 = (f32[72,128]{1,0:T(8,128)S(1)}, f32[72,128]{1,0:T(8,128)S(1)}, u32[]{:S(2)}, u32[]{:S(2)}) collective-permute-start(f32[72,128]{1,0:T(8,128)S(1)} %get-tuple-element.82), channel_id=1, source_target_pairs={{0,2},{1,3},{2,0},{3,1},{4,6},{5,7},{6,4},{7,5},{8,10},{9,11},{10,... | collective-permute-start | bytes 110600 | tf_op jit(solution)/shard_map/ppermute | solution.py:344
  87.5 2.7 %collective-permute-done.20.refs_3_ = f32[72,128]{1,0:T(8,128)S(1)} collective-permute-done((f32[72,128]{1,0:T(8,128)S(1)}, f32[72,128]{1,0:T(8,128)S(1)}, u32[]{:S(2)}, u32[]{:S(2)}) %collective-permute-start.20) | collective-permute-done | bytes 36896 | tf_op jit(solution)/shard_map/ppermute | solution.py:344
  90.2 0.1 shard_map.65
  90.2 0.0 collective-permute-start.21
  90.3 1.4 %collective-permute-done.21.got_ref.refs_3_ = f32[392,128]{1,0:T(8,128)S(1)} collective-permute-done((f32[392,128]{1,0:T(8,128)S(1)}, f32[392,128]{1,0:T(8,128)S(1)}, u32[]{:S(2)}, u32[]{:S(2)}) %collective-permute-start.21) | collective-permute-done | bytes 200736 | tf_op jit(solution)/shard_map/ppermute | solution.py:344
  91.7 0.1 shard_map.66
  91.8 2.0 %collective-permute-start.24 = (f32[8,256]{1,0:T(8,128)S(1)}, f32[8,256]{1,0:T(8,128)S(1)}, u32[]{:S(2)}, u32[]{:S(2)}) collective-permute-start(f32[8,256]{1,0:T(8,128)S(1)} %get-tuple-element.86.known_ref.refs_4_), channel_id=1, source_target_pairs={{0,24},{8,16},{16,8},{24,0},{1,25},{9,17},{17,9},{25,1},{2,26},{10... | collective-permute-start | bytes 24584 | tf_op jit(solution)/shard_map/ppermute | solution.py:436
  93.8 0.9 collective-permute-start.23
  94.7 0.7 collective-permute-start.22
  95.4 0.8 shard_map.68
  96.2 0.2 collective-permute-done.24.refs_2_
  96.5 1.0 %collective-permute-done.23.refs_1_ = f32[8,256]{1,0:T(8,128)S(1)} collective-permute-done((f32[8,256]{1,0:T(8,128)S(1)}, f32[8,256]{1,0:T(8,128)S(1)}, u32[]{:S(2)}, u32[]{:S(2)}) %collective-permute-start.23) | collective-permute-done | bytes 8224 | tf_op jit(solution)/shard_map/ppermute | solution.py:436
  97.5 0.9 collective-permute-done.22.refs_0_
  98.3 0.7 shard_map.67
  (13 shorter events, 0.1 us)
Async XLA Ops:
  0.6 6.2 %collective-permute-start.1 = (f32[1024,256]{1,0:T(8,128)}, f32[1024,256]{1,0:T(8,128)S(1)}, u32[]{:S(2)}, u32[]{:S(2)}) collective-permute-start(f32[1024,256]{1,0:T(8,128)} %own_ref.1), channel_id=1, source_target_pairs={{0,1},{1,0},{2,3},{3,2},{4,5},{5,4},{6,7},{7,6},{8,9},{9,8},{10,11... | collective-permute-start | bytes 3145736 | tf_op jit(solution)/shard_map/ppermute | solution.py:344
  1.1 26.9 %collective-permute-start = (f32[1024,256]{1,0:T(8,128)}, f32[1024,256]{1,0:T(8,128)S(1)}, u32[]{:S(2)}, u32[]{:S(2)}) collective-permute-start(f32[1024,256]{1,0:T(8,128)} %own_ref.1), channel_id=1, source_target_pairs={{0,2},{1,3},{2,0},{3,1},{4,6},{5,7},{6,4},{7,5},{8,10},{9,11},{10,... | collective-permute-start | bytes 3145736 | tf_op jit(solution)/shard_map/ppermute | solution.py:344
  4.8 1.4 %collective-permute-start.2 = (f32[256,128]{1,0:T(8,128)S(1)}, f32[256,128]{1,0:T(8,128)S(1)}, u32[]{:S(2)}, u32[]{:S(2)}) collective-permute-start(f32[256,128]{1,0:T(8,128)S(1)} %get-tuple-element.89), channel_id=1, source_target_pairs={{0,1},{1,0},{2,3},{3,2},{4,5},{5,4},{6,7},{7,6},{8,9},{9,8},{10,11... | collective-permute-start | bytes 393224 | tf_op jit(solution)/shard_map/ppermute | solution.py:344
  6.4 24.2 %collective-permute-start.4 = (f32[256,128]{1,0:T(8,128)S(1)}, f32[256,128]{1,0:T(8,128)S(1)}, u32[]{:S(2)}, u32[]{:S(2)}) collective-permute-start(f32[256,128]{1,0:T(8,128)S(1)} %get-tuple-element.49), channel_id=1, source_target_pairs={{0,2},{1,3},{2,0},{3,1},{4,6},{5,7},{6,4},{7,5},{8,10},{9,11},{10,... | collective-permute-start | bytes 393224 | tf_op jit(solution)/shard_map/ppermute | solution.py:344
  6.8 1.2 %copy-start = (f32[1024,256]{1,0:T(8,128)S(1)}, f32[1024,256]{1,0:T(8,128)}, u32[]{:S(2)}) copy-start(f32[1024,256]{1,0:T(8,128)} %own_ref.1) | copy-start | bytes 3145732
  28.0 3.1 %collective-permute-start.3 = (f32[1024,256]{1,0:T(8,128)S(1)}, f32[1024,256]{1,0:T(8,128)S(1)}, u32[]{:S(2)}, u32[]{:S(2)}) collective-permute-start(f32[1024,256]{1,0:T(8,128)S(1)} %collective-permute-done.side_ref), channel_id=1, source_target_pairs={{0,1},{1,0},{2,3},{3,2},{4,5},{5,4},{6,7},{7,6},{8,9},{9,8},{10,11... | collective-permute-start | bytes 3145736 | tf_op jit(solution)/shard_map/ppermute | solution.py:344
  31.8 7.7 %collective-permute-start.5 = (f32[256,128]{1,0:T(8,128)S(1)}, f32[256,128]{1,0:T(8,128)S(1)}, u32[]{:S(2)}, u32[]{:S(2)}) collective-permute-start(f32[256,128]{1,0:T(8,128)S(1)} %get-tuple-element.53.a_ref), channel_id=1, source_target_pairs={{0,6},{1,7},{2,4},{3,5},{4,2},{5,3},{6,0},{7,1},{8,14},{9,15},{10,... | collective-permute-start | bytes 393224 | tf_op jit(solution)/shard_map/ppermute | solution.py:344
  36.4 6.9 %collective-permute-start.12 = (f32[256,128]{1,0:T(8,128)S(1)}, f32[256,128]{1,0:T(8,128)S(1)}, u32[]{:S(2)}, u32[]{:S(2)}) collective-permute-start(f32[256,128]{1,0:T(8,128)S(1)} %get-tuple-element.68.a_ref), channel_id=1, source_target_pairs={{0,6},{1,7},{2,4},{3,5},{4,2},{5,3},{6,0},{7,1},{8,14},{9,15},{10,... | collective-permute-start | bytes 393224 | tf_op jit(solution)/shard_map/ppermute | solution.py:344
  40.4 5.3 %collective-permute-start.6 = (f32[264,128]{1,0:T(8,128)S(1)}, f32[264,128]{1,0:T(8,128)S(1)}, u32[]{:S(2)}, u32[]{:S(2)}) collective-permute-start(f32[264,128]{1,0:T(8,128)S(1)} %shard_map.54), channel_id=1, source_target_pairs={{0,8},{1,17},{2,10},{3,19},{4,12},{5,21},{6,14},{7,23},{8,0},{9,25... | collective-permute-start | bytes 405512 | tf_op jit(solution)/shard_map/ppermute | solution.py:355
  44.1 5.0 %collective-permute-start.13 = (f32[264,128]{1,0:T(8,128)S(1)}, f32[264,128]{1,0:T(8,128)S(1)}, u32[]{:S(2)}, u32[]{:S(2)}) collective-permute-start(f32[264,128]{1,0:T(8,128)S(1)} %shard_map.59), channel_id=1, source_target_pairs={{0,16},{1,9},{2,18},{3,11},{4,20},{5,13},{6,22},{7,15},{8,24},{9,1... | collective-permute-start | bytes 405512 | tf_op jit(solution)/shard_map/ppermute | solution.py:355
  45.7 6.5 %collective-permute-start.7 = (f32[264,128]{1,0:T(8,128)S(1)}, f32[264,128]{1,0:T(8,128)S(1)}, u32[]{:S(2)}, u32[]{:S(2)}) collective-permute-start(f32[264,128]{1,0:T(8,128)S(1)} %add.20.refs_0_), channel_id=1, source_target_pairs={{0,16},{1,9},{2,18},{3,11},{4,20},{5,13},{6,22},{7,15},{8,24},{9,1... | collective-permute-start | bytes 405512 | tf_op jit(solution)/shard_map/ppermute | solution.py:355
  49.2 8.1 %collective-permute-start.14 = (f32[264,128]{1,0:T(8,128)S(1)}, f32[264,128]{1,0:T(8,128)S(1)}, u32[]{:S(2)}, u32[]{:S(2)}) collective-permute-start(f32[264,128]{1,0:T(8,128)S(1)} %add.22.refs_0_), channel_id=1, source_target_pairs={{0,8},{1,17},{2,10},{3,19},{4,12},{5,21},{6,14},{7,23},{8,0},{9,25... | collective-permute-start | bytes 405512 | tf_op jit(solution)/shard_map/ppermute | solution.py:355
  53.1 8.1 %collective-permute-start.8 = (f32[264,128]{1,0:T(8,128)S(1)}, f32[264,128]{1,0:T(8,128)S(1)}, u32[]{:S(2)}, u32[]{:S(2)}) collective-permute-start(f32[264,128]{1,0:T(8,128)S(1)} %get-tuple-element.64.refs_0_), channel_id=1, source_target_pairs={{0,6},{1,7},{2,4},{3,5},{4,2},{5,3},{6,0},{7,1},{8,14},{9,15},{10,... | collective-permute-start | bytes 405512 | tf_op jit(solution)/shard_map/ppermute | solution.py:344
  58.2 7.0 %collective-permute-start.15 = (f32[264,128]{1,0:T(8,128)S(1)}, f32[264,128]{1,0:T(8,128)S(1)}, u32[]{:S(2)}, u32[]{:S(2)}) collective-permute-start(f32[264,128]{1,0:T(8,128)S(1)} %get-tuple-element.69.refs_0_), channel_id=1, source_target_pairs={{0,6},{1,7},{2,4},{3,5},{4,2},{5,3},{6,0},{7,1},{8,14},{9,15},{10,... | collective-permute-start | bytes 405512 | tf_op jit(solution)/shard_map/ppermute | solution.py:344
  62.1 6.5 %collective-permute-start.9 = (f32[264,128]{1,0:T(8,128)S(1)}, f32[264,128]{1,0:T(8,128)S(1)}, u32[]{:S(2)}, u32[]{:S(2)}) collective-permute-start(f32[264,128]{1,0:T(8,128)S(1)} %get-tuple-element.65), channel_id=1, source_target_pairs={{0,8},{1,17},{2,10},{3,19},{4,12},{5,21},{6,14},{7,23},{8,0},{9,25... | collective-permute-start | bytes 405512 | tf_op jit(solution)/shard_map/ppermute | solution.py:355
  66.1 5.0 %collective-permute-start.16 = (f32[264,128]{1,0:T(8,128)S(1)}, f32[264,128]{1,0:T(8,128)S(1)}, u32[]{:S(2)}, u32[]{:S(2)}) collective-permute-start(f32[264,128]{1,0:T(8,128)S(1)} %get-tuple-element.70), channel_id=1, source_target_pairs={{0,16},{1,9},{2,18},{3,11},{4,20},{5,13},{6,22},{7,15},{8,24},{9,1... | collective-permute-start | bytes 405512 | tf_op jit(solution)/shard_map/ppermute | solution.py:355
  68.6 5.1 %collective-permute-start.10 = (f32[264,128]{1,0:T(8,128)S(1)}, f32[264,128]{1,0:T(8,128)S(1)}, u32[]{:S(2)}, u32[]{:S(2)}) collective-permute-start(f32[264,128]{1,0:T(8,128)S(1)} %add.21.refs_0_), channel_id=1, source_target_pairs={{0,16},{1,9},{2,18},{3,11},{4,20},{5,13},{6,22},{7,15},{8,24},{9,1... | collective-permute-start | bytes 405512 | tf_op jit(solution)/shard_map/ppermute | solution.py:355
  71.1 5.1 %collective-permute-start.17 = (f32[264,128]{1,0:T(8,128)S(1)}, f32[264,128]{1,0:T(8,128)S(1)}, u32[]{:S(2)}, u32[]{:S(2)}) collective-permute-start(f32[264,128]{1,0:T(8,128)S(1)} %add.23.refs_0_), channel_id=1, source_target_pairs={{0,8},{1,17},{2,10},{3,19},{4,12},{5,21},{6,14},{7,23},{8,0},{9,25... | collective-permute-start | bytes 405512 | tf_op jit(solution)/shard_map/ppermute | solution.py:355
  74.6 7.1 %collective-permute-start.11 = (f32[264,128]{1,0:T(8,128)S(1)}, f32[264,128]{1,0:T(8,128)S(1)}, u32[]{:S(2)}, u32[]{:S(2)}) collective-permute-start(f32[264,128]{1,0:T(8,128)S(1)} %get-tuple-element.66.own_ref), channel_id=1, source_target_pairs={{0,6},{1,7},{2,4},{3,5},{4,2},{5,3},{6,0},{7,1},{8,14},{9,15},{10,... | collective-permute-start | bytes 405512 | tf_op jit(solution)/shard_map/ppermute | solution.py:344
  77.1 8.8 %collective-permute-start.18 = (f32[264,128]{1,0:T(8,128)S(1)}, f32[264,128]{1,0:T(8,128)S(1)}, u32[]{:S(2)}, u32[]{:S(2)}) collective-permute-start(f32[264,128]{1,0:T(8,128)S(1)} %get-tuple-element.76.own_ref), channel_id=1, source_target_pairs={{0,6},{1,7},{2,4},{3,5},{4,2},{5,3},{6,0},{7,1},{8,14},{9,15},{10,... | collective-permute-start | bytes 405512 | tf_op jit(solution)/shard_map/ppermute | solution.py:344
  81.9 8.3 %collective-permute-start.19 = (f32[328,128]{1,0:T(8,128)S(1)}, f32[328,128]{1,0:T(8,128)S(1)}, u32[]{:S(2)}, u32[]{:S(2)}) collective-permute-start(f32[328,128]{1,0:T(8,128)S(1)} %get-tuple-element.81), channel_id=1, source_target_pairs={{0,2},{1,3},{2,0},{3,1},{4,6},{5,7},{6,4},{7,5},{8,10},{9,11},{10,... | collective-permute-start | bytes 503816 | tf_op jit(solution)/shard_map/ppermute | solution.py:344
  86.1 4.0 %collective-permute-start.20 = (f32[72,128]{1,0:T(8,128)S(1)}, f32[72,128]{1,0:T(8,128)S(1)}, u32[]{:S(2)}, u32[]{:S(2)}) collective-permute-start(f32[72,128]{1,0:T(8,128)S(1)} %get-tuple-element.82), channel_id=1, source_target_pairs={{0,2},{1,3},{2,0},{3,1},{4,6},{5,7},{6,4},{7,5},{8,10},{9,11},{10,... | collective-permute-start | bytes 110600 | tf_op jit(solution)/shard_map/ppermute | solution.py:344
  90.2 1.5 %collective-permute-start.21 = (f32[392,128]{1,0:T(8,128)S(1)}, f32[392,128]{1,0:T(8,128)S(1)}, u32[]{:S(2)}, u32[]{:S(2)}) collective-permute-start(f32[392,128]{1,0:T(8,128)S(1)} %get-tuple-element.84), channel_id=1, source_target_pairs={{0,1},{1,0},{2,3},{3,2},{4,5},{5,4},{6,7},{7,6},{8,9},{9,8},{10,11... | collective-permute-start | bytes 602120 | tf_op jit(solution)/shard_map/ppermute | solution.py:344
  91.8 4.6 %collective-permute-start.24 = (f32[8,256]{1,0:T(8,128)S(1)}, f32[8,256]{1,0:T(8,128)S(1)}, u32[]{:S(2)}, u32[]{:S(2)}) collective-permute-start(f32[8,256]{1,0:T(8,128)S(1)} %get-tuple-element.86.known_ref.refs_4_), channel_id=1, source_target_pairs={{0,24},{8,16},{16,8},{24,0},{1,25},{9,17},{17,9},{25,1},{2,26},{10... | collective-permute-start | bytes 24584 | tf_op jit(solution)/shard_map/ppermute | solution.py:436
  93.8 3.7 %collective-permute-start.23 = (f32[8,256]{1,0:T(8,128)S(1)}, f32[8,256]{1,0:T(8,128)S(1)}, u32[]{:S(2)}, u32[]{:S(2)}) collective-permute-start(f32[8,256]{1,0:T(8,128)S(1)} %get-tuple-element.86.known_ref.refs_4_), channel_id=1, source_target_pairs={{0,16},{8,24},{16,0},{24,8},{1,17},{9,25},{17,1},{25,9},{2,18},{10... | collective-permute-start | bytes 24584 | tf_op jit(solution)/shard_map/ppermute | solution.py:436
  94.7 3.7 %collective-permute-start.22 = (f32[8,256]{1,0:T(8,128)S(1)}, f32[8,256]{1,0:T(8,128)S(1)}, u32[]{:S(2)}, u32[]{:S(2)}) collective-permute-start(f32[8,256]{1,0:T(8,128)S(1)} %get-tuple-element.86.known_ref.refs_4_), channel_id=1, source_target_pairs={{0,8},{8,0},{16,24},{24,16},{1,9},{9,1},{17,25},{25,17},{2,10},{10... | collective-permute-start | bytes 24584 | tf_op jit(solution)/shard_map/ppermute | solution.py:436

commit v16 on v9

--- a/solution.py
+++ b/solution.py
@@ -19,10 +19,17 @@
 F32 = jnp.float32
 
 
+def sides():
+    seat = lax.axis_index("snap")
+    core, chip = lax.rem(seat, 2), lax.div(seat, 2)
+    inner = jnp.logical_or(chip == 1, chip == 2).astype(jnp.int32)
+    odd = lax.rem(chip, 2)
+    return jnp.where(core == 0, inner, odd), jnp.where(core == 0, odd, inner)
+
+
 def position():
     seat = lax.axis_index("snap")
-    core, chip = lax.rem(seat, 2), lax.div(seat, 2)
-    return core, lax.rem(chip, 2), chip
+    return lax.rem(seat, 2), sides()[0], lax.div(seat, 2)
 
 
 def split(x):
@@ -269,12 +276,13 @@
     side = [side_ref[side_at + 2 * h * size : side_at + (2 * h + 1) * size, :] for h in range(HALVES)]
     core = [core_ref[core_at + h * size : core_at + (h + 1) * size, :] for h in range(2 * HALVES)]
 
-    def side_order(own, other):
-        low = [jnp.where(zero_side, a, b) for a, b in zip(own, other)]
-        high = [jnp.where(zero_side, b, a) for a, b in zip(own, other)]
+    def side_order(own, other, zero):
+        low = [jnp.where(zero, a, b) for a, b in zip(own, other)]
+        high = [jnp.where(zero, b, a) for a, b in zip(own, other)]
         return jnp.concatenate([wide(x, COLS) for x in low + high], axis=0)
 
-    ours, theirs = side_order(mine, side), side_order(core[:HALVES], core[HALVES:])
+    ours = side_order(mine, side, zero_side)
+    theirs = side_order(core[:HALVES], core[HALVES:], sides()[1] == 0)
     for s, x in enumerate((jnp.where(zero_core, ours, theirs), jnp.where(zero_core, theirs, ours))):
         cut = slice(s * LANES, (s + 1) * LANES)
         z_ref[:, cut] = x.T / known_ref[2 * ITERS - 1 : 2 * ITERS, cut]
@@ -344,7 +352,10 @@
 
     swap_core = functools.partial(swap, bits=1)
     swap_side = functools.partial(swap, bits=2)
-    swap_pair = functools.partial(swap, bits=4)
+
+    def swap_pair(x):
+        return lax.ppermute(x, "snap", [(i, i ^ (4 if i % 2 else 6)) for i in range(places)])
+
 
     def swap_cell(x, step):
         def target(cell, i):

time: 106 us -> 103 us (0.972)
  waiting for transfers between devices: 65.1 us -> 43.9 us
  starting transfers between devices: 24.4 us -> 42.6 us
    ppermute x14 -> x8, waiting for transfers between devices: 49.8 us -> 26 us  [swap(): return lax.ppermute(x, 'snap', [(i, i ^ bits) for i in range(places)])]
    ppermute x0 -> x6, starting transfers between devices: none -> 12.5 us  [swap_pair(): lax.ppermute(x, 'snap', [(i, i ^ (4 if i % 2 else 6)) for i in range(plac...]
    ppermute x0 -> x6, waiting for transfers between devices: none -> 10.9 us  [swap_pair(): lax.ppermute(x, 'snap', [(i, i ^ (4 if i % 2 else 6)) for i in range(plac...]
    ppermute x8, waiting for transfers between devices: 13 us -> 5.33 us  [swap_cell(): return lax.ppermute(x, ('cell', 'snap'), perm)]
    ppermute x8, starting transfers between devices: 10.5 us -> 14.1 us  [swap_cell(): return lax.ppermute(x, ('cell', 'snap'), perm)]
    ppermute x14 -> x8, starting transfers between devices: 10.4 us -> 12.4 us  [swap(): return lax.ppermute(x, 'snap', [(i, i ^ bits) for i in range(places)])]
  transfers between devices with their start and end apart: 25 -> 25, of which waited for: 20 -> 17; matrix products, arithmetic and copies ran while one was open for 1% -> 1% of each run, Pallas kernels for 11% -> 11%
where the time goes in v16:
time: 103 us
  waiting for transfers between devices  43.9 us (43%)
  starting transfers between devices  42.6 us (41%)
  Pallas kernels  13 us (13%)
  local copies, waits for them, and re-layouts  2.21 us (2%)
    ppermute x8, waiting for transfers between devices, swap(): return lax.ppermute(x, 'snap', [(i, i ^ bits) for i in range(places)])  26 us
    ppermute x8, starting transfers between devices, swap_cell(): return lax.ppermute(x, ('cell', 'snap'), perm)  14.1 us
    pallas_call x20, Pallas kernels, call(): pl.pallas_call(kernel, out_shape=[jax.ShapeDtypeStruct(shape, dtype) for...  13 us
    ppermute x6, starting transfers between devices, swap_pair(): lax.ppermute(x, 'snap', [(i, i ^ (4 if i % 2 else 6)) for i in range(plac...  12.5 us
    ppermute x8, starting transfers between devices, swap(): return lax.ppermute(x, 'snap', [(i, i ^ bits) for i in range(places)])  12.4 us
    ppermute x6, waiting for transfers between devices, swap_pair(): lax.ppermute(x, 'snap', [(i, i ^ (4 if i % 2 else 6)) for i in range(plac...  10.9 us
    ppermute x8, waiting for transfers between devices, swap_cell(): return lax.ppermute(x, ('cell', 'snap'), perm)  5.33 us
    ppermute x3, starting transfers between devices, local(): lax.ppermute(known, 'cell', [(c, c ^ d) for c in range(groups)])  3.55 us
  transfers between devices with their start and end apart: 25, of which 17 were waited for; matrix products, arithmetic and copies ran while one was open for 1% of the time, Pallas kernels for 11%

profile of v16, /device:TPU:0, one launch (start us, length us, event | category | flops | bytes accessed | tf_op | source)
XLA Modules:
  0.0 102.5 jit_solution(12941005802678614643)
XLA Ops:
  0.6 0.5 collective-permute-start.1
  1.1 2.7 %collective-permute-start = (f32[1024,256]{1,0:T(8,128)}, f32[1024,256]{1,0:T(8,128)S(1)}, u32[]{:S(2)}, u32[]{:S(2)}) collective-permute-start(f32[1024,256]{1,0:T(8,128)} %own_ref.1), channel_id=1, source_target_pairs={{0,2},{1,3},{2,0},{3,1},{4,6},{5,7},{6,4},{7,5},{8,10},{9,11},{10,... | collective-permute-start | bytes 3145736 | tf_op jit(solution)/shard_map/ppermute | solution.py:351
  3.8 1.0 constant_dynamic-slice_fusion
  4.8 0.2 collective-permute-start.2
  5.0 1.2 %collective-permute-done.2.got_ref = f32[256,128]{1,0:T(8,128)S(1)} collective-permute-done((f32[256,128]{1,0:T(8,128)S(1)}, f32[256,128]{1,0:T(8,128)S(1)}, u32[]{:S(2)}, u32[]{:S(2)}) %collective-permute-start.2) | collective-permute-done | bytes 131104 | tf_op jit(solution)/shard_map/ppermute | solution.py:351
  6.2 0.2 shard_map.49
  6.4 0.4 collective-permute-start.4
  6.8 1.2 %copy-done = f32[1024,256]{1,0:T(8,128)S(1)} copy-done((f32[1024,256]{1,0:T(8,128)S(1)}, f32[1024,256]{1,0:T(8,128)}, u32[]{:S(2)}) %copy-start) | copy-done | bytes 1048600
  8.0 1.1 %shard_map.50 = (f32[512,128]{1,0:T(8,128)S(1)}, bf16[1024,512]{1,0:T(8,128)(2,1)S(1)}, bf16[1024,512]{1,0:T(8,128)(2,1)S(1)}, bf16[512,1024]{1,0:T(8,128)(2,1)S(1)}, bf16[512,1024]{1,0:T(8,128)(2,1)S(1)}) custom-call(f32[1024,256]{1,0:T(8,128)S(1)} %copy-done, f32[1024,256]{1,0:T(8,128)S(1)} %collective-permute-done.1.core_ref, ...), custom_call_target="tpu_custom_call" | custom-call | tf_op jit(solution)/shard_map/pallas_call | solution.py:304
  9.1 18.9 %collective-permute-done.side_ref = f32[1024,256]{1,0:T(8,128)S(1)} collective-permute-done((f32[1024,256]{1,0:T(8,128)}, f32[1024,256]{1,0:T(8,128)S(1)}, u32[]{:S(2)}, u32[]{:S(2)}) %collective-permute-start) | collective-permute-done | bytes 1048608 | tf_op jit(solution)/shard_map/ppermute | solution.py:351
  28.0 0.6 shard_map.51
  28.7 1.9 %collective-permute-done.4.sketch_ref = f32[256,128]{1,0:T(8,128)S(1)} collective-permute-done((f32[256,128]{1,0:T(8,128)S(1)}, f32[256,128]{1,0:T(8,128)S(1)}, u32[]{:S(2)}, u32[]{:S(2)}) %collective-permute-start.4) | collective-permute-done | bytes 131104 | tf_op jit(solution)/shard_map/ppermute | solution.py:351
  30.6 0.6 shard_map.52.near_ref
  31.1 0.7 shard_map.53
  31.8 3.8 %collective-permute-start.5 = (f32[256,128]{1,0:T(8,128)S(1)}, f32[256,128]{1,0:T(8,128)S(1)}, u32[]{:S(2)}, u32[]{:S(2)}) collective-permute-start(f32[256,128]{1,0:T(8,128)S(1)} %get-tuple-element.53.a_ref), channel_id=1, source_target_pairs={{0,6},{1,5},{2,4},{3,7},{4,2},{5,1},{6,0},{7,3},{8,14},{9,13},{10,... | collective-permute-start | bytes 393224 | tf_op jit(solution)/shard_map/ppermute | solution.py:357
  35.7 0.7 shard_map.55
  36.4 0.1 collective-permute-start.12
  36.5 2.8 %collective-permute-done.5.b_ref = f32[256,128]{1,0:T(8,128)S(1)} collective-permute-done((f32[256,128]{1,0:T(8,128)S(1)}, f32[256,128]{1,0:T(8,128)S(1)}, u32[]{:S(2)}, u32[]{:S(2)}) %collective-permute-start.5) | collective-permute-done | bytes 131104 | tf_op jit(solution)/shard_map/ppermute | solution.py:357
  39.3 0.8 shard_map.54
  40.1 1.5 %collective-permute-start.6 = (f32[264,128]{1,0:T(8,128)S(1)}, f32[264,128]{1,0:T(8,128)S(1)}, u32[]{:S(2)}, u32[]{:S(2)}) collective-permute-start(f32[264,128]{1,0:T(8,128)S(1)} %shard_map.54), channel_id=1, source_target_pairs={{0,8},{1,17},{2,10},{3,19},{4,12},{5,21},{6,14},{7,23},{8,0},{9,25... | collective-permute-start | bytes 405512 | tf_op jit(solution)/shard_map/ppermute | solution.py:365
  41.7 1.6 %collective-permute-done.12.b_ref = f32[256,128]{1,0:T(8,128)S(1)} collective-permute-done((f32[256,128]{1,0:T(8,128)S(1)}, f32[256,128]{1,0:T(8,128)S(1)}, u32[]{:S(2)}, u32[]{:S(2)}) %collective-permute-start.12) | collective-permute-done | bytes 131104 | tf_op jit(solution)/shard_map/ppermute | solution.py:357
  43.3 0.8 shard_map.59
  44.1 1.5 %collective-permute-start.13 = (f32[264,128]{1,0:T(8,128)S(1)}, f32[264,128]{1,0:T(8,128)S(1)}, u32[]{:S(2)}, u32[]{:S(2)}) collective-permute-start(f32[264,128]{1,0:T(8,128)S(1)} %shard_map.59), channel_id=1, source_target_pairs={{0,8},{1,17},{2,10},{3,19},{4,12},{5,21},{6,14},{7,23},{8,0},{9,25... | collective-permute-start | bytes 405512 | tf_op jit(solution)/shard_map/ppermute | solution.py:365
  45.7 1.6 %collective-permute-start.7 = (f32[264,128]{1,0:T(8,128)S(1)}, f32[264,128]{1,0:T(8,128)S(1)}, u32[]{:S(2)}, u32[]{:S(2)}) collective-permute-start(f32[264,128]{1,0:T(8,128)S(1)} %add.20.refs_0_), channel_id=1, source_target_pairs={{0,16},{1,9},{2,18},{3,11},{4,20},{5,13},{6,22},{7,15},{8,24},{9,1... | collective-permute-start | bytes 405512 | tf_op jit(solution)/shard_map/ppermute | solution.py:365
  47.2 1.9 %collective-permute-done.13 = f32[264,128]{1,0:T(8,128)S(1)} collective-permute-done((f32[264,128]{1,0:T(8,128)S(1)}, f32[264,128]{1,0:T(8,128)S(1)}, u32[]{:S(2)}, u32[]{:S(2)}) %collective-permute-start.13) | collective-permute-done | bytes 135200 | tf_op jit(solution)/shard_map/ppermute | solution.py:365
  49.2 1.8 %collective-permute-start.14 = (f32[264,128]{1,0:T(8,128)S(1)}, f32[264,128]{1,0:T(8,128)S(1)}, u32[]{:S(2)}, u32[]{:S(2)}) collective-permute-start(f32[264,128]{1,0:T(8,128)S(1)} %add.22.refs_0_), channel_id=1, source_target_pairs={{0,16},{1,9},{2,18},{3,11},{4,20},{5,13},{6,22},{7,15},{8,24},{9,1... | collective-permute-start | bytes 405512 | tf_op jit(solution)/shard_map/ppermute | solution.py:365
  50.9 0.6 collective-permute-done.7.refs_1_
  51.5 0.9 shard_map.56
  52.4 3.5 %collective-permute-start.8 = (f32[264,128]{1,0:T(8,128)S(1)}, f32[264,128]{1,0:T(8,128)S(1)}, u32[]{:S(2)}, u32[]{:S(2)}) collective-permute-start(f32[264,128]{1,0:T(8,128)S(1)} %get-tuple-element.64.refs_0_), channel_id=1, source_target_pairs={{0,6},{1,5},{2,4},{3,7},{4,2},{5,1},{6,0},{7,3},{8,14},{9,13},{10,... | collective-permute-start | bytes 405512 | tf_op jit(solution)/shard_map/ppermute | solution.py:357
  55.9 0.9 shard_map.60
  56.8 1.2 %collective-permute-start.15 = (f32[264,128]{1,0:T(8,128)S(1)}, f32[264,128]{1,0:T(8,128)S(1)}, u32[]{:S(2)}, u32[]{:S(2)}) collective-permute-start(f32[264,128]{1,0:T(8,128)S(1)} %get-tuple-element.69.refs_0_), channel_id=1, source_target_pairs={{0,6},{1,5},{2,4},{3,7},{4,2},{5,1},{6,0},{7,3},{8,14},{9,13},{10,... | collective-permute-start | bytes 405512 | tf_op jit(solution)/shard_map/ppermute | solution.py:357
  58.0 1.4 %collective-permute-done.8.refs_1_ = f32[264,128]{1,0:T(8,128)S(1)} collective-permute-done((f32[264,128]{1,0:T(8,128)S(1)}, f32[264,128]{1,0:T(8,128)S(1)}, u32[]{:S(2)}, u32[]{:S(2)}) %collective-permute-start.8) | collective-permute-done | bytes 135200 | tf_op jit(solution)/shard_map/ppermute | solution.py:357
  59.4 0.9 shard_map.57
  60.3 2.7 %collective-permute-start.9 = (f32[264,128]{1,0:T(8,128)S(1)}, f32[264,128]{1,0:T(8,128)S(1)}, u32[]{:S(2)}, u32[]{:S(2)}) collective-permute-start(f32[264,128]{1,0:T(8,128)S(1)} %get-tuple-element.65), channel_id=1, source_target_pairs={{0,8},{1,17},{2,10},{3,19},{4,12},{5,21},{6,14},{7,23},{8,0},{9,25... | collective-permute-start | bytes 405512 | tf_op jit(solution)/shard_map/ppermute | solution.py:365
  63.1 1.7 %collective-permute-done.15.refs_1_ = f32[264,128]{1,0:T(8,128)S(1)} collective-permute-done((f32[264,128]{1,0:T(8,128)S(1)}, f32[264,128]{1,0:T(8,128)S(1)}, u32[]{:S(2)}, u32[]{:S(2)}) %collective-permute-start.15) | collective-permute-done | bytes 135200 | tf_op jit(solution)/shard_map/ppermute | solution.py:357
  64.8 0.9 shard_map.61
  65.7 1.8 %collective-permute-start.16 = (f32[264,128]{1,0:T(8,128)S(1)}, f32[264,128]{1,0:T(8,128)S(1)}, u32[]{:S(2)}, u32[]{:S(2)}) collective-permute-start(f32[264,128]{1,0:T(8,128)S(1)} %get-tuple-element.70), channel_id=1, source_target_pairs={{0,8},{1,17},{2,10},{3,19},{4,12},{5,21},{6,14},{7,23},{8,0},{9,25... | collective-permute-start | bytes 405512 | tf_op jit(solution)/shard_map/ppermute | solution.py:365
  67.5 1.6 %collective-permute-start.10 = (f32[264,128]{1,0:T(8,128)S(1)}, f32[264,128]{1,0:T(8,128)S(1)}, u32[]{:S(2)}, u32[]{:S(2)}) collective-permute-start(f32[264,128]{1,0:T(8,128)S(1)} %add.21.refs_0_), channel_id=1, source_target_pairs={{0,16},{1,9},{2,18},{3,11},{4,20},{5,13},{6,22},{7,15},{8,24},{9,1... | collective-permute-start | bytes 405512 | tf_op jit(solution)/shard_map/ppermute | solution.py:365
  69.1 1.6 %collective-permute-done.16 = f32[264,128]{1,0:T(8,128)S(1)} collective-permute-done((f32[264,128]{1,0:T(8,128)S(1)}, f32[264,128]{1,0:T(8,128)S(1)}, u32[]{:S(2)}, u32[]{:S(2)}) %collective-permute-start.16) | collective-permute-done | bytes 135200 | tf_op jit(solution)/shard_map/ppermute | solution.py:365
  70.7 1.6 %collective-permute-start.17 = (f32[264,128]{1,0:T(8,128)S(1)}, f32[264,128]{1,0:T(8,128)S(1)}, u32[]{:S(2)}, u32[]{:S(2)}) collective-permute-start(f32[264,128]{1,0:T(8,128)S(1)} %add.23.refs_0_), channel_id=1, source_target_pairs={{0,16},{1,9},{2,18},{3,11},{4,20},{5,13},{6,22},{7,15},{8,24},{9,1... | collective-permute-start | bytes 405512 | tf_op jit(solution)/shard_map/ppermute | solution.py:365
  72.3 1.2 %collective-permute-done.10.refs_1_ = f32[264,128]{1,0:T(8,128)S(1)} collective-permute-done((f32[264,128]{1,0:T(8,128)S(1)}, f32[264,128]{1,0:T(8,128)S(1)}, u32[]{:S(2)}, u32[]{:S(2)}) %collective-permute-start.10) | collective-permute-done | bytes 135200 | tf_op jit(solution)/shard_map/ppermute | solution.py:365
  73.5 0.9 shard_map.58
  74.4 1.4 %collective-permute-start.11 = (f32[264,128]{1,0:T(8,128)S(1)}, f32[264,128]{1,0:T(8,128)S(1)}, u32[]{:S(2)}, u32[]{:S(2)}) collective-permute-start(f32[264,128]{1,0:T(8,128)S(1)} %get-tuple-element.66.own_ref), channel_id=1, source_target_pairs={{0,6},{1,5},{2,4},{3,7},{4,2},{5,1},{6,0},{7,3},{8,14},{9,13},{10,... | collective-permute-start | bytes 405512 | tf_op jit(solution)/shard_map/ppermute | solution.py:357
  75.8 0.0 collective-permute-done.17.refs_1_
  75.8 0.9 shard_map.62
  76.7 2.5 %collective-permute-start.18 = (f32[264,128]{1,0:T(8,128)S(1)}, f32[264,128]{1,0:T(8,128)S(1)}, u32[]{:S(2)}, u32[]{:S(2)}) collective-permute-start(f32[264,128]{1,0:T(8,128)S(1)} %get-tuple-element.76.own_ref), channel_id=1, source_target_pairs={{0,6},{1,5},{2,4},{3,7},{4,2},{5,1},{6,0},{7,3},{8,14},{9,13},{10,... | collective-permute-start | bytes 405512 | tf_op jit(solution)/shard_map/ppermute | solution.py:357
  79.3 3.3 %collective-permute-done.11.got_ref = f32[264,128]{1,0:T(8,128)S(1)} collective-permute-done((f32[264,128]{1,0:T(8,128)S(1)}, f32[264,128]{1,0:T(8,128)S(1)}, u32[]{:S(2)}, u32[]{:S(2)}) %collective-permute-start.11) | collective-permute-done | bytes 135200 | tf_op jit(solution)/shard_map/ppermute | solution.py:357
  82.6 0.2 shard_map.63
  82.8 6.8 %collective-permute-start.19 = (f32[328,128]{1,0:T(8,128)S(1)}, f32[328,128]{1,0:T(8,128)S(1)}, u32[]{:S(2)}, u32[]{:S(2)}) collective-permute-start(f32[328,128]{1,0:T(8,128)S(1)} %get-tuple-element.81), channel_id=1, source_target_pairs={{0,2},{1,3},{2,0},{3,1},{4,6},{5,7},{6,4},{7,5},{8,10},{9,11},{10,... | collective-permute-start | bytes 503816 | tf_op jit(solution)/shard_map/ppermute | solution.py:351
  89.5 0.2 shard_map.64
  89.7 1.8 %collective-permute-start.20 = (f32[72,128]{1,0:T(8,128)S(1)}, f32[72,128]{1,0:T(8,128)S(1)}, u32[]{:S(2)}, u32[]{:S(2)}) collective-permute-start(f32[72,128]{1,0:T(8,128)S(1)} %get-tuple-element.82), channel_id=1, source_target_pairs={{0,2},{1,3},{2,0},{3,1},{4,6},{5,7},{6,4},{7,5},{8,10},{9,11},{10,... | collective-permute-start | bytes 110600 | tf_op jit(solution)/shard_map/ppermute | solution.py:351
  91.5 2.6 %collective-permute-done.20.refs_3_ = f32[72,128]{1,0:T(8,128)S(1)} collective-permute-done((f32[72,128]{1,0:T(8,128)S(1)}, f32[72,128]{1,0:T(8,128)S(1)}, u32[]{:S(2)}, u32[]{:S(2)}) %collective-permute-start.20) | collective-permute-done | bytes 36896 | tf_op jit(solution)/shard_map/ppermute | solution.py:351
  94.1 0.1 shard_map.65
  94.2 0.0 collective-permute-start.21
  94.2 1.4 %collective-permute-done.21.got_ref.refs_3_ = f32[392,128]{1,0:T(8,128)S(1)} collective-permute-done((f32[392,128]{1,0:T(8,128)S(1)}, f32[392,128]{1,0:T(8,128)S(1)}, u32[]{:S(2)}, u32[]{:S(2)}) %collective-permute-start.21) | collective-permute-done | bytes 200736 | tf_op jit(solution)/shard_map/ppermute | solution.py:351
  95.6 0.1 shard_map.66
  95.7 2.2 %collective-permute-start.24 = (f32[8,256]{1,0:T(8,128)S(1)}, f32[8,256]{1,0:T(8,128)S(1)}, u32[]{:S(2)}, u32[]{:S(2)}) collective-permute-start(f32[8,256]{1,0:T(8,128)S(1)} %get-tuple-element.86.known_ref.refs_4_), channel_id=1, source_target_pairs={{0,24},{8,16},{16,8},{24,0},{1,25},{9,17},{17,9},{25,1},{2,26},{10... | collective-permute-start | bytes 24584 | tf_op jit(solution)/shard_map/ppermute | solution.py:446
  97.9 0.3 collective-permute-start.23
  98.2 1.1 %collective-permute-start.22 = (f32[8,256]{1,0:T(8,128)S(1)}, f32[8,256]{1,0:T(8,128)S(1)}, u32[]{:S(2)}, u32[]{:S(2)}) collective-permute-start(f32[8,256]{1,0:T(8,128)S(1)} %get-tuple-element.86.known_ref.refs_4_), channel_id=1, source_target_pairs={{0,8},{8,0},{16,24},{24,16},{1,9},{9,1},{17,25},{25,17},{2,10},{10... | collective-permute-start | bytes 24584 | tf_op jit(solution)/shard_map/ppermute | solution.py:446
  99.3 0.9 shard_map.68
  100.1 0.2 collective-permute-done.24.refs_2_
  100.4 1.2 %collective-permute-done.23.refs_1_ = f32[8,256]{1,0:T(8,128)S(1)} collective-permute-done((f32[8,256]{1,0:T(8,128)S(1)}, f32[8,256]{1,0:T(8,128)S(1)}, u32[]{:S(2)}, u32[]{:S(2)}) %collective-permute-start.23) | collective-permute-done | bytes 8224 | tf_op jit(solution)/shard_map/ppermute | solution.py:446
  101.6 0.3 collective-permute-done.22.refs_0_
  101.8 0.7 shard_map.67
  (13 shorter events, 0.1 us)
Async XLA Ops:
  0.6 6.2 %collective-permute-start.1 = (f32[1024,256]{1,0:T(8,128)}, f32[1024,256]{1,0:T(8,128)S(1)}, u32[]{:S(2)}, u32[]{:S(2)}) collective-permute-start(f32[1024,256]{1,0:T(8,128)} %own_ref.1), channel_id=1, source_target_pairs={{0,1},{1,0},{2,3},{3,2},{4,5},{5,4},{6,7},{7,6},{8,9},{9,8},{10,11... | collective-permute-start | bytes 3145736 | tf_op jit(solution)/shard_map/ppermute | solution.py:351
  1.1 26.9 %collective-permute-start = (f32[1024,256]{1,0:T(8,128)}, f32[1024,256]{1,0:T(8,128)S(1)}, u32[]{:S(2)}, u32[]{:S(2)}) collective-permute-start(f32[1024,256]{1,0:T(8,128)} %own_ref.1), channel_id=1, source_target_pairs={{0,2},{1,3},{2,0},{3,1},{4,6},{5,7},{6,4},{7,5},{8,10},{9,11},{10,... | collective-permute-start | bytes 3145736 | tf_op jit(solution)/shard_map/ppermute | solution.py:351
  4.8 1.4 %collective-permute-start.2 = (f32[256,128]{1,0:T(8,128)S(1)}, f32[256,128]{1,0:T(8,128)S(1)}, u32[]{:S(2)}, u32[]{:S(2)}) collective-permute-start(f32[256,128]{1,0:T(8,128)S(1)} %get-tuple-element.89), channel_id=1, source_target_pairs={{0,1},{1,0},{2,3},{3,2},{4,5},{5,4},{6,7},{7,6},{8,9},{9,8},{10,11... | collective-permute-start | bytes 393224 | tf_op jit(solution)/shard_map/ppermute | solution.py:351
  6.4 24.2 %collective-permute-start.4 = (f32[256,128]{1,0:T(8,128)S(1)}, f32[256,128]{1,0:T(8,128)S(1)}, u32[]{:S(2)}, u32[]{:S(2)}) collective-permute-start(f32[256,128]{1,0:T(8,128)S(1)} %get-tuple-element.49), channel_id=1, source_target_pairs={{0,2},{1,3},{2,0},{3,1},{4,6},{5,7},{6,4},{7,5},{8,10},{9,11},{10,... | collective-permute-start | bytes 393224 | tf_op jit(solution)/shard_map/ppermute | solution.py:351
  6.8 1.2 %copy-start = (f32[1024,256]{1,0:T(8,128)S(1)}, f32[1024,256]{1,0:T(8,128)}, u32[]{:S(2)}) copy-start(f32[1024,256]{1,0:T(8,128)} %own_ref.1) | copy-start | bytes 3145732
  28.0 3.1 %collective-permute-start.3 = (f32[1024,256]{1,0:T(8,128)S(1)}, f32[1024,256]{1,0:T(8,128)S(1)}, u32[]{:S(2)}, u32[]{:S(2)}) collective-permute-start(f32[1024,256]{1,0:T(8,128)S(1)} %collective-permute-done.side_ref), channel_id=1, source_target_pairs={{0,1},{1,0},{2,3},{3,2},{4,5},{5,4},{6,7},{7,6},{8,9},{9,8},{10,11... | collective-permute-start | bytes 3145736 | tf_op jit(solution)/shard_map/ppermute | solution.py:351
  31.8 7.5 %collective-permute-start.5 = (f32[256,128]{1,0:T(8,128)S(1)}, f32[256,128]{1,0:T(8,128)S(1)}, u32[]{:S(2)}, u32[]{:S(2)}) collective-permute-start(f32[256,128]{1,0:T(8,128)S(1)} %get-tuple-element.53.a_ref), channel_id=1, source_target_pairs={{0,6},{1,5},{2,4},{3,7},{4,2},{5,1},{6,0},{7,3},{8,14},{9,13},{10,... | collective-permute-start | bytes 393224 | tf_op jit(solution)/shard_map/ppermute | solution.py:357
  36.4 6.9 %collective-permute-start.12 = (f32[256,128]{1,0:T(8,128)S(1)}, f32[256,128]{1,0:T(8,128)S(1)}, u32[]{:S(2)}, u32[]{:S(2)}) collective-permute-start(f32[256,128]{1,0:T(8,128)S(1)} %get-tuple-element.68.a_ref), channel_id=1, source_target_pairs={{0,6},{1,5},{2,4},{3,7},{4,2},{5,1},{6,0},{7,3},{8,14},{9,13},{10,... | collective-permute-start | bytes 393224 | tf_op jit(solution)/shard_map/ppermute | solution.py:357
  40.1 5.5 %collective-permute-start.6 = (f32[264,128]{1,0:T(8,128)S(1)}, f32[264,128]{1,0:T(8,128)S(1)}, u32[]{:S(2)}, u32[]{:S(2)}) collective-permute-start(f32[264,128]{1,0:T(8,128)S(1)} %shard_map.54), channel_id=1, source_target_pairs={{0,8},{1,17},{2,10},{3,19},{4,12},{5,21},{6,14},{7,23},{8,0},{9,25... | collective-permute-start | bytes 405512 | tf_op jit(solution)/shard_map/ppermute | solution.py:365
  44.1 5.0 %collective-permute-start.13 = (f32[264,128]{1,0:T(8,128)S(1)}, f32[264,128]{1,0:T(8,128)S(1)}, u32[]{:S(2)}, u32[]{:S(2)}) collective-permute-start(f32[264,128]{1,0:T(8,128)S(1)} %shard_map.59), channel_id=1, source_target_pairs={{0,8},{1,17},{2,10},{3,19},{4,12},{5,21},{6,14},{7,23},{8,0},{9,25... | collective-permute-start | bytes 405512 | tf_op jit(solution)/shard_map/ppermute | solution.py:365
  45.7 5.9 %collective-permute-start.7 = (f32[264,128]{1,0:T(8,128)S(1)}, f32[264,128]{1,0:T(8,128)S(1)}, u32[]{:S(2)}, u32[]{:S(2)}) collective-permute-start(f32[264,128]{1,0:T(8,128)S(1)} %add.20.refs_0_), channel_id=1, source_target_pairs={{0,16},{1,9},{2,18},{3,11},{4,20},{5,13},{6,22},{7,15},{8,24},{9,1... | collective-permute-start | bytes 405512 | tf_op jit(solution)/shard_map/ppermute | solution.py:365
  49.2 6.8 %collective-permute-start.14 = (f32[264,128]{1,0:T(8,128)S(1)}, f32[264,128]{1,0:T(8,128)S(1)}, u32[]{:S(2)}, u32[]{:S(2)}) collective-permute-start(f32[264,128]{1,0:T(8,128)S(1)} %add.22.refs_0_), channel_id=1, source_target_pairs={{0,16},{1,9},{2,18},{3,11},{4,20},{5,13},{6,22},{7,15},{8,24},{9,1... | collective-permute-start | bytes 405512 | tf_op jit(solution)/shard_map/ppermute | solution.py:365
  52.4 7.0 %collective-permute-start.8 = (f32[264,128]{1,0:T(8,128)S(1)}, f32[264,128]{1,0:T(8,128)S(1)}, u32[]{:S(2)}, u32[]{:S(2)}) collective-permute-start(f32[264,128]{1,0:T(8,128)S(1)} %get-tuple-element.64.refs_0_), channel_id=1, source_target_pairs={{0,6},{1,5},{2,4},{3,7},{4,2},{5,1},{6,0},{7,3},{8,14},{9,13},{10,... | collective-permute-start | bytes 405512 | tf_op jit(solution)/shard_map/ppermute | solution.py:357
  56.8 7.9 %collective-permute-start.15 = (f32[264,128]{1,0:T(8,128)S(1)}, f32[264,128]{1,0:T(8,128)S(1)}, u32[]{:S(2)}, u32[]{:S(2)}) collective-permute-start(f32[264,128]{1,0:T(8,128)S(1)} %get-tuple-element.69.refs_0_), channel_id=1, source_target_pairs={{0,6},{1,5},{2,4},{3,7},{4,2},{5,1},{6,0},{7,3},{8,14},{9,13},{10,... | collective-permute-start | bytes 405512 | tf_op jit(solution)/shard_map/ppermute | solution.py:357
  60.3 7.2 %collective-permute-start.9 = (f32[264,128]{1,0:T(8,128)S(1)}, f32[264,128]{1,0:T(8,128)S(1)}, u32[]{:S(2)}, u32[]{:S(2)}) collective-permute-start(f32[264,128]{1,0:T(8,128)S(1)} %get-tuple-element.65), channel_id=1, source_target_pairs={{0,8},{1,17},{2,10},{3,19},{4,12},{5,21},{6,14},{7,23},{8,0},{9,25... | collective-permute-start | bytes 405512 | tf_op jit(solution)/shard_map/ppermute | solution.py:365
  65.7 5.0 %collective-permute-start.16 = (f32[264,128]{1,0:T(8,128)S(1)}, f32[264,128]{1,0:T(8,128)S(1)}, u32[]{:S(2)}, u32[]{:S(2)}) collective-permute-start(f32[264,128]{1,0:T(8,128)S(1)} %get-tuple-element.70), channel_id=1, source_target_pairs={{0,8},{1,17},{2,10},{3,19},{4,12},{5,21},{6,14},{7,23},{8,0},{9,25... | collective-permute-start | bytes 405512 | tf_op jit(solution)/shard_map/ppermute | solution.py:365
  67.5 6.0 %collective-permute-start.10 = (f32[264,128]{1,0:T(8,128)S(1)}, f32[264,128]{1,0:T(8,128)S(1)}, u32[]{:S(2)}, u32[]{:S(2)}) collective-permute-start(f32[264,128]{1,0:T(8,128)S(1)} %add.21.refs_0_), channel_id=1, source_target_pairs={{0,16},{1,9},{2,18},{3,11},{4,20},{5,13},{6,22},{7,15},{8,24},{9,1... | collective-permute-start | bytes 405512 | tf_op jit(solution)/shard_map/ppermute | solution.py:365
  70.7 5.1 %collective-permute-start.17 = (f32[264,128]{1,0:T(8,128)S(1)}, f32[264,128]{1,0:T(8,128)S(1)}, u32[]{:S(2)}, u32[]{:S(2)}) collective-permute-start(f32[264,128]{1,0:T(8,128)S(1)} %add.23.refs_0_), channel_id=1, source_target_pairs={{0,16},{1,9},{2,18},{3,11},{4,20},{5,13},{6,22},{7,15},{8,24},{9,1... | collective-permute-start | bytes 405512 | tf_op jit(solution)/shard_map/ppermute | solution.py:365
  74.4 8.1 %collective-permute-start.11 = (f32[264,128]{1,0:T(8,128)S(1)}, f32[264,128]{1,0:T(8,128)S(1)}, u32[]{:S(2)}, u32[]{:S(2)}) collective-permute-start(f32[264,128]{1,0:T(8,128)S(1)} %get-tuple-element.66.own_ref), channel_id=1, source_target_pairs={{0,6},{1,5},{2,4},{3,7},{4,2},{5,1},{6,0},{7,3},{8,14},{9,13},{10,... | collective-permute-start | bytes 405512 | tf_op jit(solution)/shard_map/ppermute | solution.py:357
  76.7 12.8 %collective-permute-start.18 = (f32[264,128]{1,0:T(8,128)S(1)}, f32[264,128]{1,0:T(8,128)S(1)}, u32[]{:S(2)}, u32[]{:S(2)}) collective-permute-start(f32[264,128]{1,0:T(8,128)S(1)} %get-tuple-element.76.own_ref), channel_id=1, source_target_pairs={{0,6},{1,5},{2,4},{3,7},{4,2},{5,1},{6,0},{7,3},{8,14},{9,13},{10,... | collective-permute-start | bytes 405512 | tf_op jit(solution)/shard_map/ppermute | solution.py:357
  82.8 11.3 %collective-permute-start.19 = (f32[328,128]{1,0:T(8,128)S(1)}, f32[328,128]{1,0:T(8,128)S(1)}, u32[]{:S(2)}, u32[]{:S(2)}) collective-permute-start(f32[328,128]{1,0:T(8,128)S(1)} %get-tuple-element.81), channel_id=1, source_target_pairs={{0,2},{1,3},{2,0},{3,1},{4,6},{5,7},{6,4},{7,5},{8,10},{9,11},{10,... | collective-permute-start | bytes 503816 | tf_op jit(solution)/shard_map/ppermute | solution.py:351
  89.7 4.3 %collective-permute-start.20 = (f32[72,128]{1,0:T(8,128)S(1)}, f32[72,128]{1,0:T(8,128)S(1)}, u32[]{:S(2)}, u32[]{:S(2)}) collective-permute-start(f32[72,128]{1,0:T(8,128)S(1)} %get-tuple-element.82), channel_id=1, source_target_pairs={{0,2},{1,3},{2,0},{3,1},{4,6},{5,7},{6,4},{7,5},{8,10},{9,11},{10,... | collective-permute-start | bytes 110600 | tf_op jit(solution)/shard_map/ppermute | solution.py:351
  94.2 1.5 %collective-permute-start.21 = (f32[392,128]{1,0:T(8,128)S(1)}, f32[392,128]{1,0:T(8,128)S(1)}, u32[]{:S(2)}, u32[]{:S(2)}) collective-permute-start(f32[392,128]{1,0:T(8,128)S(1)} %get-tuple-element.84), channel_id=1, source_target_pairs={{0,1},{1,0},{2,3},{3,2},{4,5},{5,4},{6,7},{7,6},{8,9},{9,8},{10,11... | collective-permute-start | bytes 602120 | tf_op jit(solution)/shard_map/ppermute | solution.py:351
  95.7 4.6 %collective-permute-start.24 = (f32[8,256]{1,0:T(8,128)S(1)}, f32[8,256]{1,0:T(8,128)S(1)}, u32[]{:S(2)}, u32[]{:S(2)}) collective-permute-start(f32[8,256]{1,0:T(8,128)S(1)} %get-tuple-element.86.known_ref.refs_4_), channel_id=1, source_target_pairs={{0,24},{8,16},{16,8},{24,0},{1,25},{9,17},{17,9},{25,1},{2,26},{10... | collective-permute-start | bytes 24584 | tf_op jit(solution)/shard_map/ppermute | solution.py:446
  97.9 3.7 %collective-permute-start.23 = (f32[8,256]{1,0:T(8,128)S(1)}, f32[8,256]{1,0:T(8,128)S(1)}, u32[]{:S(2)}, u32[]{:S(2)}) collective-permute-start(f32[8,256]{1,0:T(8,128)S(1)} %get-tuple-element.86.known_ref.refs_4_), channel_id=1, source_target_pairs={{0,16},{8,24},{16,0},{24,8},{1,17},{9,25},{17,1},{25,9},{2,18},{10... | collective-permute-start | bytes 24584 | tf_op jit(solution)/shard_map/ppermute | solution.py:446
  98.2 3.7 %collective-permute-start.22 = (f32[8,256]{1,0:T(8,128)S(1)}, f32[8,256]{1,0:T(8,128)S(1)}, u32[]{:S(2)}, u32[]{:S(2)}) collective-permute-start(f32[8,256]{1,0:T(8,128)S(1)} %get-tuple-element.86.known_ref.refs_4_), channel_id=1, source_target_pairs={{0,8},{8,0},{16,24},{24,16},{1,9},{9,1},{17,25},{25,17},{2,10},{10... | collective-permute-start | bytes 24584 | tf_op jit(solution)/shard_map/ppermute | solution.py:446

commit v17 on v10

--- a/solution.py
+++ b/solution.py
@@ -134,24 +134,24 @@
         y_ref[out, :] = unfold(total.T) + near_ref[out, :]
 
 
-def add_far(h, high_ref, low_ref, sketch_ref, near_ref, y_ref):
+def add_far(high_ref, low_ref, sketch_ref, near_ref, halves):
     rhs = sketch_sides(sketch_ref[...])[1]
     for b in range(high_ref.shape[0] // LANES):
         cut = slice(b * LANES, (b + 1) * LANES)
         total = dot(high_ref[cut, :], rhs) + dot(low_ref[cut, :], rhs)
-        y = unfold(total.T)[h * COLS : (h + 1) * COLS]
-        at = b * QUARTER + h * COLS
-        y_ref[b * COLS : (b + 1) * COLS, :] = y + near_ref[at : at + COLS, :]
-
-
-def far_kernel(diagonal_ref, sketch_ref, near_ref, y_ref, high_ref, low_ref):
+        y = unfold(total.T) + near_ref[b * QUARTER : (b + 1) * QUARTER, :]
+        for h, ref in enumerate(halves):
+            ref[b * COLS : (b + 1) * COLS, :] = y[h * COLS : (h + 1) * COLS]
+
+
+def far_kernel(diagonal_ref, sketch_ref, near_ref, *refs):
+    *halves, high_ref, low_ref = refs
     store_factors(high_ref, low_ref, (diagonal_ref[...],))
-    add_far(0, high_ref, low_ref, sketch_ref, near_ref, y_ref)
-
-
-def second_far_kernel(diagonal_ref, high_ref, low_ref, sketch_ref, near_ref, y_ref, high_t_ref, low_t_ref):
-    add_far(1, high_ref, low_ref, sketch_ref, near_ref, y_ref)
-    store_factors(high_t_ref, low_t_ref, (diagonal_ref[...].T,), 0)
+    add_far(high_ref, low_ref, sketch_ref, near_ref, halves)
+
+
+def turned_kernel(diagonal_ref, high_ref, low_ref):
+    store_factors(high_ref, low_ref, (diagonal_ref[...].T,), 0)
 
 
 def send_z(y, high_refs, low_refs, z_ref):
@@ -381,11 +381,8 @@
     (side_y,) = call(side_kernel, [quarter_shape], *side[:2], side_sketch, near_y, cost=LONG)
     half_shape = ((rows // LANES * COLS, LANES), F32)
     diagonal = swap_core(side_block)
-    own_first, *far = call(far_kernel, [half_shape] + factor(1), diagonal, side_sketch, side_y)
-    own_second, *far_t = call(
-        second_far_kernel, [half_shape] + factor_t(1), diagonal, *far, side_sketch, side_y
-    )
-    own = (own_first, own_second)
+    *own, high, low = call(far_kernel, [half_shape] * HALVES + factor(1), diagonal, side_sketch, side_y)
+    far, far_t = (high, low), call(turned_kernel, factor_t(1), diagonal)
     matrix = (near[0], side[0], far[0], near[1], side[1], far[1])
     matrix_t = (near[2], side[2], far_t[0], near[3], side[3], far_t[1])
 

time: 99.3 us -> 100 us (level)
  starting transfers between devices: 38.1 us -> 40.4 us
    ppermute x14, starting transfers between devices: 22.9 us -> 25.1 us  [swap(): return lax.ppermute(x, 'snap', [(i, i ^ bits) for i in range(places)])]
  transfers between devices with their start and end apart: 25 -> 25, of which waited for: 18 -> 17; matrix products, arithmetic and copies ran while one was open for 1% -> 1% of each run, Pallas kernels for 12% -> 11%
where the time goes in v17:
time: 100 us
  waiting for transfers between devices  44.1 us (44%)
  starting transfers between devices  40.4 us (40%)
  Pallas kernels  12.7 us (13%)
  local copies, waits for them, and re-layouts  2.22 us (2%)
    ppermute x14, waiting for transfers between devices, swap(): return lax.ppermute(x, 'snap', [(i, i ^ bits) for i in range(places)])  35.1 us
    ppermute x14, starting transfers between devices, swap(): return lax.ppermute(x, 'snap', [(i, i ^ bits) for i in range(places)])  25.1 us
    pallas_call x20, Pallas kernels, call(): pl.pallas_call(kernel, out_shape=[jax.ShapeDtypeStruct(shape, dtype) for...  12.7 us
    ppermute x8, starting transfers between devices, swap_cell(): return lax.ppermute(x, ('cell', 'snap'), perm)  11.7 us
    ppermute x8, waiting for transfers between devices, swap_cell(): return lax.ppermute(x, ('cell', 'snap'), perm)  5.98 us
    ppermute x3, starting transfers between devices, local(): lax.ppermute(known, 'cell', [(c, c ^ d) for c in range(groups)])  3.55 us
    ppermute x3, waiting for transfers between devices, local(): lax.ppermute(known, 'cell', [(c, c ^ d) for c in range(groups)])  3.05 us
  transfers between devices with their start and end apart: 25, of which 17 were waited for; matrix products, arithmetic and copies ran while one was open for 1% of the time, Pallas kernels for 11%

profile of v17, /device:TPU:0, one launch (start us, length us, event | category | flops | bytes accessed | tf_op | source)
XLA Modules:
  0.0 100.2 jit_solution(12196150184111808891)
XLA Ops:
  0.6 0.5 collective-permute-start.1
  1.1 2.7 %collective-permute-start = (f32[1024,256]{1,0:T(8,128)}, f32[1024,256]{1,0:T(8,128)S(1)}, u32[]{:S(2)}, u32[]{:S(2)}) collective-permute-start(f32[1024,256]{1,0:T(8,128)} %own_ref.1), channel_id=1, source_target_pairs={{0,2},{1,3},{2,0},{3,1},{4,6},{5,7},{6,4},{7,5},{8,10},{9,11},{10,... | collective-permute-start | bytes 3145736 | tf_op jit(solution)/shard_map/ppermute | solution.py:344
  3.8 1.0 constant_dynamic-slice_fusion
  4.8 0.2 collective-permute-start.2
  5.0 1.2 %collective-permute-done.2.got_ref = f32[256,128]{1,0:T(8,128)S(1)} collective-permute-done((f32[256,128]{1,0:T(8,128)S(1)}, f32[256,128]{1,0:T(8,128)S(1)}, u32[]{:S(2)}, u32[]{:S(2)}) %collective-permute-start.2) | collective-permute-done | bytes 131104 | tf_op jit(solution)/shard_map/ppermute | solution.py:344
  6.2 0.2 shard_map.49
  6.4 0.4 collective-permute-start.4
  6.8 1.2 %copy-done.2 = f32[1024,256]{1,0:T(8,128)S(1)} copy-done((f32[1024,256]{1,0:T(8,128)S(1)}, f32[1024,256]{1,0:T(8,128)}, u32[]{:S(2)}) %copy-start.2) | copy-done | bytes 1048600
  8.0 1.1 %shard_map.50 = (f32[512,128]{1,0:T(8,128)S(1)}, bf16[1024,512]{1,0:T(8,128)(2,1)S(1)}, bf16[1024,512]{1,0:T(8,128)(2,1)S(1)}, bf16[512,1024]{1,0:T(8,128)(2,1)S(1)}, bf16[512,1024]{1,0:T(8,128)(2,1)S(1)}) custom-call(f32[1024,256]{1,0:T(8,128)S(1)} %copy-done.2, f32[1024,256]{1,0:T(8,128)S(1)} %collective-permute-done.1.core_ref, ...), custom_call_target="tpu_custom_call" | custom-call | tf_op jit(solution)/shard_map/pallas_call | solution.py:297
  9.1 18.9 %collective-permute-done.side_ref = f32[1024,256]{1,0:T(8,128)S(1)} collective-permute-done((f32[1024,256]{1,0:T(8,128)}, f32[1024,256]{1,0:T(8,128)S(1)}, u32[]{:S(2)}, u32[]{:S(2)}) %collective-permute-start) | collective-permute-done | bytes 1048608 | tf_op jit(solution)/shard_map/ppermute | solution.py:344
  28.0 0.6 shard_map.51
  28.6 0.1 collective-permute-start.3
  28.7 1.8 %collective-permute-done.4.sketch_ref = f32[256,128]{1,0:T(8,128)S(1)} collective-permute-done((f32[256,128]{1,0:T(8,128)S(1)}, f32[256,128]{1,0:T(8,128)S(1)}, u32[]{:S(2)}, u32[]{:S(2)}) %collective-permute-start.4) | collective-permute-done | bytes 131104 | tf_op jit(solution)/shard_map/ppermute | solution.py:344
  30.6 0.6 shard_map.52.near_ref
  31.1 0.2 collective-permute-done.3.diagonal_ref
  31.4 0.7 shard_map.53
  32.0 4.0 %collective-permute-start.5 = (f32[256,128]{1,0:T(8,128)S(1)}, f32[256,128]{1,0:T(8,128)S(1)}, u32[]{:S(2)}, u32[]{:S(2)}) collective-permute-start(f32[256,128]{1,0:T(8,128)S(1)} %get-tuple-element.53.a_ref), channel_id=1, source_target_pairs={{0,6},{1,7},{2,4},{3,5},{4,2},{5,3},{6,0},{7,1},{8,14},{9,15},{10,... | collective-permute-start | bytes 393224 | tf_op jit(solution)/shard_map/ppermute | solution.py:344
  36.1 0.1 collective-permute-start.12
  36.2 3.8 %collective-permute-done.5.b_ref = f32[256,128]{1,0:T(8,128)S(1)} collective-permute-done((f32[256,128]{1,0:T(8,128)S(1)}, f32[256,128]{1,0:T(8,128)S(1)}, u32[]{:S(2)}, u32[]{:S(2)}) %collective-permute-start.5) | collective-permute-done | bytes 131104 | tf_op jit(solution)/shard_map/ppermute | solution.py:344
  40.0 0.8 shard_map.54
  40.8 1.5 %collective-permute-start.6 = (f32[264,128]{1,0:T(8,128)S(1)}, f32[264,128]{1,0:T(8,128)S(1)}, u32[]{:S(2)}, u32[]{:S(2)}) collective-permute-start(f32[264,128]{1,0:T(8,128)S(1)} %shard_map.54), channel_id=1, source_target_pairs={{0,8},{1,17},{2,10},{3,19},{4,12},{5,21},{6,14},{7,23},{8,0},{9,25... | collective-permute-start | bytes 405512 | tf_op jit(solution)/shard_map/ppermute | solution.py:355
  42.3 0.9 collective-permute-done.12.b_ref
  43.2 0.8 shard_map.59
  44.0 1.5 %collective-permute-start.13 = (f32[264,128]{1,0:T(8,128)S(1)}, f32[264,128]{1,0:T(8,128)S(1)}, u32[]{:S(2)}, u32[]{:S(2)}) collective-permute-start(f32[264,128]{1,0:T(8,128)S(1)} %shard_map.59), channel_id=1, source_target_pairs={{0,8},{1,17},{2,10},{3,19},{4,12},{5,21},{6,14},{7,23},{8,0},{9,25... | collective-permute-start | bytes 405512 | tf_op jit(solution)/shard_map/ppermute | solution.py:355
  45.5 0.3 collective-permute-done.6
  45.9 1.6 %collective-permute-start.7 = (f32[264,128]{1,0:T(8,128)S(1)}, f32[264,128]{1,0:T(8,128)S(1)}, u32[]{:S(2)}, u32[]{:S(2)}) collective-permute-start(f32[264,128]{1,0:T(8,128)S(1)} %add.20.refs_0_), channel_id=1, source_target_pairs={{0,16},{1,9},{2,18},{3,11},{4,20},{5,13},{6,22},{7,15},{8,24},{9,1... | collective-permute-start | bytes 405512 | tf_op jit(solution)/shard_map/ppermute | solution.py:355
  47.5 2.9 %collective-permute-done.13 = f32[264,128]{1,0:T(8,128)S(1)} collective-permute-done((f32[264,128]{1,0:T(8,128)S(1)}, f32[264,128]{1,0:T(8,128)S(1)}, u32[]{:S(2)}, u32[]{:S(2)}) %collective-permute-start.13) | collective-permute-done | bytes 135200 | tf_op jit(solution)/shard_map/ppermute | solution.py:355
  50.4 0.8 collective-permute-start.14
  51.2 0.4 shard_map.55
  51.6 0.9 shard_map.56
  52.5 3.7 %collective-permute-start.8 = (f32[264,128]{1,0:T(8,128)S(1)}, f32[264,128]{1,0:T(8,128)S(1)}, u32[]{:S(2)}, u32[]{:S(2)}) collective-permute-start(f32[264,128]{1,0:T(8,128)S(1)} %get-tuple-element.64.refs_0_), channel_id=1, source_target_pairs={{0,6},{1,7},{2,4},{3,5},{4,2},{5,3},{6,0},{7,1},{8,14},{9,15},{10,... | collective-permute-start | bytes 405512 | tf_op jit(solution)/shard_map/ppermute | solution.py:344
  56.3 0.9 shard_map.60
  57.2 2.3 %collective-permute-start.15 = (f32[264,128]{1,0:T(8,128)S(1)}, f32[264,128]{1,0:T(8,128)S(1)}, u32[]{:S(2)}, u32[]{:S(2)}) collective-permute-start(f32[264,128]{1,0:T(8,128)S(1)} %get-tuple-element.69.refs_0_), channel_id=1, source_target_pairs={{0,6},{1,7},{2,4},{3,5},{4,2},{5,3},{6,0},{7,1},{8,14},{9,15},{10,... | collective-permute-start | bytes 405512 | tf_op jit(solution)/shard_map/ppermute | solution.py:344
  59.4 0.8 collective-permute-done.8.refs_1_
  60.2 0.9 shard_map.57
  61.1 1.2 %collective-permute-start.9 = (f32[264,128]{1,0:T(8,128)S(1)}, f32[264,128]{1,0:T(8,128)S(1)}, u32[]{:S(2)}, u32[]{:S(2)}) collective-permute-start(f32[264,128]{1,0:T(8,128)S(1)} %get-tuple-element.65), channel_id=1, source_target_pairs={{0,8},{1,17},{2,10},{3,19},{4,12},{5,21},{6,14},{7,23},{8,0},{9,25... | collective-permute-start | bytes 405512 | tf_op jit(solution)/shard_map/ppermute | solution.py:355
  62.3 1.8 %collective-permute-done.15.refs_1_ = f32[264,128]{1,0:T(8,128)S(1)} collective-permute-done((f32[264,128]{1,0:T(8,128)S(1)}, f32[264,128]{1,0:T(8,128)S(1)}, u32[]{:S(2)}, u32[]{:S(2)}) %collective-permute-start.15) | collective-permute-done | bytes 135200 | tf_op jit(solution)/shard_map/ppermute | solution.py:344
  64.1 0.9 shard_map.61
  65.0 1.5 %collective-permute-start.16 = (f32[264,128]{1,0:T(8,128)S(1)}, f32[264,128]{1,0:T(8,128)S(1)}, u32[]{:S(2)}, u32[]{:S(2)}) collective-permute-start(f32[264,128]{1,0:T(8,128)S(1)} %get-tuple-element.70), channel_id=1, source_target_pairs={{0,8},{1,17},{2,10},{3,19},{4,12},{5,21},{6,14},{7,23},{8,0},{9,25... | collective-permute-start | bytes 405512 | tf_op jit(solution)/shard_map/ppermute | solution.py:355
  66.5 0.3 collective-permute-done.9
  66.9 2.2 %collective-permute-start.10 = (f32[264,128]{1,0:T(8,128)S(1)}, f32[264,128]{1,0:T(8,128)S(1)}, u32[]{:S(2)}, u32[]{:S(2)}) collective-permute-start(f32[264,128]{1,0:T(8,128)S(1)} %add.21.refs_0_), channel_id=1, source_target_pairs={{0,16},{1,9},{2,18},{3,11},{4,20},{5,13},{6,22},{7,15},{8,24},{9,1... | collective-permute-start | bytes 405512 | tf_op jit(solution)/shard_map/ppermute | solution.py:355
  69.1 2.3 %collective-permute-done.16 = f32[264,128]{1,0:T(8,128)S(1)} collective-permute-done((f32[264,128]{1,0:T(8,128)S(1)}, f32[264,128]{1,0:T(8,128)S(1)}, u32[]{:S(2)}, u32[]{:S(2)}) %collective-permute-start.16) | collective-permute-done | bytes 135200 | tf_op jit(solution)/shard_map/ppermute | solution.py:355
  71.4 1.5 %collective-permute-start.17 = (f32[264,128]{1,0:T(8,128)S(1)}, f32[264,128]{1,0:T(8,128)S(1)}, u32[]{:S(2)}, u32[]{:S(2)}) collective-permute-start(f32[264,128]{1,0:T(8,128)S(1)} %add.23.refs_0_), channel_id=1, source_target_pairs={{0,16},{1,9},{2,18},{3,11},{4,20},{5,13},{6,22},{7,15},{8,24},{9,1... | collective-permute-start | bytes 405512 | tf_op jit(solution)/shard_map/ppermute | solution.py:355
  72.9 0.9 shard_map.58
  73.8 2.6 %collective-permute-start.11 = (f32[264,128]{1,0:T(8,128)S(1)}, f32[264,128]{1,0:T(8,128)S(1)}, u32[]{:S(2)}, u32[]{:S(2)}) collective-permute-start(f32[264,128]{1,0:T(8,128)S(1)} %get-tuple-element.66.own_ref), channel_id=1, source_target_pairs={{0,6},{1,7},{2,4},{3,5},{4,2},{5,3},{6,0},{7,1},{8,14},{9,15},{10,... | collective-permute-start | bytes 405512 | tf_op jit(solution)/shard_map/ppermute | solution.py:344
  76.4 0.0 collective-permute-done.17.refs_1_
  76.5 0.9 shard_map.62
  77.4 1.3 %collective-permute-start.18 = (f32[264,128]{1,0:T(8,128)S(1)}, f32[264,128]{1,0:T(8,128)S(1)}, u32[]{:S(2)}, u32[]{:S(2)}) collective-permute-start(f32[264,128]{1,0:T(8,128)S(1)} %get-tuple-element.76.own_ref), channel_id=1, source_target_pairs={{0,6},{1,7},{2,4},{3,5},{4,2},{5,3},{6,0},{7,1},{8,14},{9,15},{10,... | collective-permute-start | bytes 405512 | tf_op jit(solution)/shard_map/ppermute | solution.py:344
  78.7 2.0 %collective-permute-done.11.got_ref = f32[264,128]{1,0:T(8,128)S(1)} collective-permute-done((f32[264,128]{1,0:T(8,128)S(1)}, f32[264,128]{1,0:T(8,128)S(1)}, u32[]{:S(2)}, u32[]{:S(2)}) %collective-permute-start.11) | collective-permute-done | bytes 135200 | tf_op jit(solution)/shard_map/ppermute | solution.py:344
  80.8 0.2 shard_map.63
  81.0 5.2 %collective-permute-start.19 = (f32[328,128]{1,0:T(8,128)S(1)}, f32[328,128]{1,0:T(8,128)S(1)}, u32[]{:S(2)}, u32[]{:S(2)}) collective-permute-start(f32[328,128]{1,0:T(8,128)S(1)} %get-tuple-element.81), channel_id=1, source_target_pairs={{0,2},{1,3},{2,0},{3,1},{4,6},{5,7},{6,4},{7,5},{8,10},{9,11},{10,... | collective-permute-start | bytes 503816 | tf_op jit(solution)/shard_map/ppermute | solution.py:344
  86.2 0.2 shard_map.64
  86.4 1.9 %collective-permute-start.20 = (f32[72,128]{1,0:T(8,128)S(1)}, f32[72,128]{1,0:T(8,128)S(1)}, u32[]{:S(2)}, u32[]{:S(2)}) collective-permute-start(f32[72,128]{1,0:T(8,128)S(1)} %get-tuple-element.82), channel_id=1, source_target_pairs={{0,2},{1,3},{2,0},{3,1},{4,6},{5,7},{6,4},{7,5},{8,10},{9,11},{10,... | collective-permute-start | bytes 110600 | tf_op jit(solution)/shard_map/ppermute | solution.py:344
  88.3 2.1 %collective-permute-done.20.refs_3_ = f32[72,128]{1,0:T(8,128)S(1)} collective-permute-done((f32[72,128]{1,0:T(8,128)S(1)}, f32[72,128]{1,0:T(8,128)S(1)}, u32[]{:S(2)}, u32[]{:S(2)}) %collective-permute-start.20) | collective-permute-done | bytes 36896 | tf_op jit(solution)/shard_map/ppermute | solution.py:344
  90.4 0.1 shard_map.65
  90.5 1.4 %collective-permute-done.21.got_ref.refs_3_ = f32[392,128]{1,0:T(8,128)S(1)} collective-permute-done((f32[392,128]{1,0:T(8,128)S(1)}, f32[392,128]{1,0:T(8,128)S(1)}, u32[]{:S(2)}, u32[]{:S(2)}) %collective-permute-start.21) | collective-permute-done | bytes 200736 | tf_op jit(solution)/shard_map/ppermute | solution.py:344
  91.9 0.1 shard_map.66
  92.0 1.6 %collective-permute-start.22 = (f32[8,256]{1,0:T(8,128)S(1)}, f32[8,256]{1,0:T(8,128)S(1)}, u32[]{:S(2)}, u32[]{:S(2)}) collective-permute-start(f32[8,256]{1,0:T(8,128)S(1)} %get-tuple-element.86.known_ref.refs_4_), channel_id=1, source_target_pairs={{0,8},{8,0},{16,24},{24,16},{1,9},{9,1},{17,25},{25,17},{2,10},{10... | collective-permute-start | bytes 24584 | tf_op jit(solution)/shard_map/ppermute | solution.py:433
  93.6 1.3 %collective-permute-start.23 = (f32[8,256]{1,0:T(8,128)S(1)}, f32[8,256]{1,0:T(8,128)S(1)}, u32[]{:S(2)}, u32[]{:S(2)}) collective-permute-start(f32[8,256]{1,0:T(8,128)S(1)} %get-tuple-element.86.known_ref.refs_4_), channel_id=1, source_target_pairs={{0,16},{8,24},{16,0},{24,8},{1,17},{9,25},{17,1},{25,9},{2,18},{10... | collective-permute-start | bytes 24584 | tf_op jit(solution)/shard_map/ppermute | solution.py:433
  94.9 0.7 collective-permute-start.24
  95.6 0.8 shard_map.68
  96.4 0.8 collective-permute-done.23.refs_1_
  97.3 2.2 %collective-permute-done.24.refs_2_ = f32[8,256]{1,0:T(8,128)S(1)} collective-permute-done((f32[8,256]{1,0:T(8,128)S(1)}, f32[8,256]{1,0:T(8,128)S(1)}, u32[]{:S(2)}, u32[]{:S(2)}) %collective-permute-start.24) | collective-permute-done | bytes 8224 | tf_op jit(solution)/shard_map/ppermute | solution.py:433
  99.5 0.7 shard_map.67
  (17 shorter events, 0.1 us)
Async XLA Ops:
  0.6 6.2 %collective-permute-start.1 = (f32[1024,256]{1,0:T(8,128)}, f32[1024,256]{1,0:T(8,128)S(1)}, u32[]{:S(2)}, u32[]{:S(2)}) collective-permute-start(f32[1024,256]{1,0:T(8,128)} %own_ref.1), channel_id=1, source_target_pairs={{0,1},{1,0},{2,3},{3,2},{4,5},{5,4},{6,7},{7,6},{8,9},{9,8},{10,11... | collective-permute-start | bytes 3145736 | tf_op jit(solution)/shard_map/ppermute | solution.py:344
  1.1 26.9 %collective-permute-start = (f32[1024,256]{1,0:T(8,128)}, f32[1024,256]{1,0:T(8,128)S(1)}, u32[]{:S(2)}, u32[]{:S(2)}) collective-permute-start(f32[1024,256]{1,0:T(8,128)} %own_ref.1), channel_id=1, source_target_pairs={{0,2},{1,3},{2,0},{3,1},{4,6},{5,7},{6,4},{7,5},{8,10},{9,11},{10,... | collective-permute-start | bytes 3145736 | tf_op jit(solution)/shard_map/ppermute | solution.py:344
  4.8 1.4 %collective-permute-start.2 = (f32[256,128]{1,0:T(8,128)S(1)}, f32[256,128]{1,0:T(8,128)S(1)}, u32[]{:S(2)}, u32[]{:S(2)}) collective-permute-start(f32[256,128]{1,0:T(8,128)S(1)} %get-tuple-element.89), channel_id=1, source_target_pairs={{0,1},{1,0},{2,3},{3,2},{4,5},{5,4},{6,7},{7,6},{8,9},{9,8},{10,11... | collective-permute-start | bytes 393224 | tf_op jit(solution)/shard_map/ppermute | solution.py:344
  6.4 24.2 %collective-permute-start.4 = (f32[256,128]{1,0:T(8,128)S(1)}, f32[256,128]{1,0:T(8,128)S(1)}, u32[]{:S(2)}, u32[]{:S(2)}) collective-permute-start(f32[256,128]{1,0:T(8,128)S(1)} %get-tuple-element.49), channel_id=1, source_target_pairs={{0,2},{1,3},{2,0},{3,1},{4,6},{5,7},{6,4},{7,5},{8,10},{9,11},{10,... | collective-permute-start | bytes 393224 | tf_op jit(solution)/shard_map/ppermute | solution.py:344
  6.8 1.2 %copy-start.2 = (f32[1024,256]{1,0:T(8,128)S(1)}, f32[1024,256]{1,0:T(8,128)}, u32[]{:S(2)}) copy-start(f32[1024,256]{1,0:T(8,128)} %own_ref.1) | copy-start | bytes 3145732
  28.6 2.7 %collective-permute-start.3 = (f32[1024,256]{1,0:T(8,128)S(1)}, f32[1024,256]{1,0:T(8,128)S(1)}, u32[]{:S(2)}, u32[]{:S(2)}) collective-permute-start(f32[1024,256]{1,0:T(8,128)S(1)} %collective-permute-done.side_ref), channel_id=1, source_target_pairs={{0,1},{1,0},{2,3},{3,2},{4,5},{5,4},{6,7},{7,6},{8,9},{9,8},{10,11... | collective-permute-start | bytes 3145736 | tf_op jit(solution)/shard_map/ppermute | solution.py:344
  31.4 9.4 %copy-start = (f32[1024,256]{1,0:T(8,128)}, f32[1024,256]{1,0:T(8,128)S(1)}, u32[]{:S(2)}) copy-start(f32[1024,256]{1,0:T(8,128)S(1)} %collective-permute-done.3.diagonal_ref) | copy-start | bytes 3145732
  32.0 8.0 %collective-permute-start.5 = (f32[256,128]{1,0:T(8,128)S(1)}, f32[256,128]{1,0:T(8,128)S(1)}, u32[]{:S(2)}, u32[]{:S(2)}) collective-permute-start(f32[256,128]{1,0:T(8,128)S(1)} %get-tuple-element.53.a_ref), channel_id=1, source_target_pairs={{0,6},{1,7},{2,4},{3,5},{4,2},{5,3},{6,0},{7,1},{8,14},{9,15},{10,... | collective-permute-start | bytes 393224 | tf_op jit(solution)/shard_map/ppermute | solution.py:344
  36.1 7.1 %collective-permute-start.12 = (f32[256,128]{1,0:T(8,128)S(1)}, f32[256,128]{1,0:T(8,128)S(1)}, u32[]{:S(2)}, u32[]{:S(2)}) collective-permute-start(f32[256,128]{1,0:T(8,128)S(1)} %get-tuple-element.68.a_ref), channel_id=1, source_target_pairs={{0,6},{1,7},{2,4},{3,5},{4,2},{5,3},{6,0},{7,1},{8,14},{9,15},{10,... | collective-permute-start | bytes 393224 | tf_op jit(solution)/shard_map/ppermute | solution.py:344
  40.8 5.0 %collective-permute-start.6 = (f32[264,128]{1,0:T(8,128)S(1)}, f32[264,128]{1,0:T(8,128)S(1)}, u32[]{:S(2)}, u32[]{:S(2)}) collective-permute-start(f32[264,128]{1,0:T(8,128)S(1)} %shard_map.54), channel_id=1, source_target_pairs={{0,8},{1,17},{2,10},{3,19},{4,12},{5,21},{6,14},{7,23},{8,0},{9,25... | collective-permute-start | bytes 405512 | tf_op jit(solution)/shard_map/ppermute | solution.py:355
  43.2 8.0 %copy-start.1 = (f32[1024,256]{1,0:T(8,128)S(1)}, f32[1024,256]{1,0:T(8,128)}, u32[]{:S(2)}) copy-start(f32[1024,256]{1,0:T(8,128)} %copy-done) | copy-start | bytes 3145732
  44.0 6.4 %collective-permute-start.13 = (f32[264,128]{1,0:T(8,128)S(1)}, f32[264,128]{1,0:T(8,128)S(1)}, u32[]{:S(2)}, u32[]{:S(2)}) collective-permute-start(f32[264,128]{1,0:T(8,128)S(1)} %shard_map.59), channel_id=1, source_target_pairs={{0,8},{1,17},{2,10},{3,19},{4,12},{5,21},{6,14},{7,23},{8,0},{9,25... | collective-permute-start | bytes 405512 | tf_op jit(solution)/shard_map/ppermute | solution.py:355
  45.9 5.7 %collective-permute-start.7 = (f32[264,128]{1,0:T(8,128)S(1)}, f32[264,128]{1,0:T(8,128)S(1)}, u32[]{:S(2)}, u32[]{:S(2)}) collective-permute-start(f32[264,128]{1,0:T(8,128)S(1)} %add.20.refs_0_), channel_id=1, source_target_pairs={{0,16},{1,9},{2,18},{3,11},{4,20},{5,13},{6,22},{7,15},{8,24},{9,1... | collective-permute-start | bytes 405512 | tf_op jit(solution)/shard_map/ppermute | solution.py:355
  50.4 5.8 %collective-permute-start.14 = (f32[264,128]{1,0:T(8,128)S(1)}, f32[264,128]{1,0:T(8,128)S(1)}, u32[]{:S(2)}, u32[]{:S(2)}) collective-permute-start(f32[264,128]{1,0:T(8,128)S(1)} %add.22.refs_0_), channel_id=1, source_target_pairs={{0,16},{1,9},{2,18},{3,11},{4,20},{5,13},{6,22},{7,15},{8,24},{9,1... | collective-permute-start | bytes 405512 | tf_op jit(solution)/shard_map/ppermute | solution.py:355
  52.5 7.7 %collective-permute-start.8 = (f32[264,128]{1,0:T(8,128)S(1)}, f32[264,128]{1,0:T(8,128)S(1)}, u32[]{:S(2)}, u32[]{:S(2)}) collective-permute-start(f32[264,128]{1,0:T(8,128)S(1)} %get-tuple-element.64.refs_0_), channel_id=1, source_target_pairs={{0,6},{1,7},{2,4},{3,5},{4,2},{5,3},{6,0},{7,1},{8,14},{9,15},{10,... | collective-permute-start | bytes 405512 | tf_op jit(solution)/shard_map/ppermute | solution.py:344
  57.2 7.0 %collective-permute-start.15 = (f32[264,128]{1,0:T(8,128)S(1)}, f32[264,128]{1,0:T(8,128)S(1)}, u32[]{:S(2)}, u32[]{:S(2)}) collective-permute-start(f32[264,128]{1,0:T(8,128)S(1)} %get-tuple-element.69.refs_0_), channel_id=1, source_target_pairs={{0,6},{1,7},{2,4},{3,5},{4,2},{5,3},{6,0},{7,1},{8,14},{9,15},{10,... | collective-permute-start | bytes 405512 | tf_op jit(solution)/shard_map/ppermute | solution.py:344
  61.1 5.7 %collective-permute-start.9 = (f32[264,128]{1,0:T(8,128)S(1)}, f32[264,128]{1,0:T(8,128)S(1)}, u32[]{:S(2)}, u32[]{:S(2)}) collective-permute-start(f32[264,128]{1,0:T(8,128)S(1)} %get-tuple-element.65), channel_id=1, source_target_pairs={{0,8},{1,17},{2,10},{3,19},{4,12},{5,21},{6,14},{7,23},{8,0},{9,25... | collective-permute-start | bytes 405512 | tf_op jit(solution)/shard_map/ppermute | solution.py:355
  65.0 6.4 %collective-permute-start.16 = (f32[264,128]{1,0:T(8,128)S(1)}, f32[264,128]{1,0:T(8,128)S(1)}, u32[]{:S(2)}, u32[]{:S(2)}) collective-permute-start(f32[264,128]{1,0:T(8,128)S(1)} %get-tuple-element.70), channel_id=1, source_target_pairs={{0,8},{1,17},{2,10},{3,19},{4,12},{5,21},{6,14},{7,23},{8,0},{9,25... | collective-permute-start | bytes 405512 | tf_op jit(solution)/shard_map/ppermute | solution.py:355
  66.9 6.0 %collective-permute-start.10 = (f32[264,128]{1,0:T(8,128)S(1)}, f32[264,128]{1,0:T(8,128)S(1)}, u32[]{:S(2)}, u32[]{:S(2)}) collective-permute-start(f32[264,128]{1,0:T(8,128)S(1)} %add.21.refs_0_), channel_id=1, source_target_pairs={{0,16},{1,9},{2,18},{3,11},{4,20},{5,13},{6,22},{7,15},{8,24},{9,1... | collective-permute-start | bytes 405512 | tf_op jit(solution)/shard_map/ppermute | solution.py:355
  71.4 5.1 %collective-permute-start.17 = (f32[264,128]{1,0:T(8,128)S(1)}, f32[264,128]{1,0:T(8,128)S(1)}, u32[]{:S(2)}, u32[]{:S(2)}) collective-permute-start(f32[264,128]{1,0:T(8,128)S(1)} %add.23.refs_0_), channel_id=1, source_target_pairs={{0,16},{1,9},{2,18},{3,11},{4,20},{5,13},{6,22},{7,15},{8,24},{9,1... | collective-permute-start | bytes 405512 | tf_op jit(solution)/shard_map/ppermute | solution.py:355
  73.8 7.0 %collective-permute-start.11 = (f32[264,128]{1,0:T(8,128)S(1)}, f32[264,128]{1,0:T(8,128)S(1)}, u32[]{:S(2)}, u32[]{:S(2)}) collective-permute-start(f32[264,128]{1,0:T(8,128)S(1)} %get-tuple-element.66.own_ref), channel_id=1, source_target_pairs={{0,6},{1,7},{2,4},{3,5},{4,2},{5,3},{6,0},{7,1},{8,14},{9,15},{10,... | collective-permute-start | bytes 405512 | tf_op jit(solution)/shard_map/ppermute | solution.py:344
  77.4 8.8 %collective-permute-start.18 = (f32[264,128]{1,0:T(8,128)S(1)}, f32[264,128]{1,0:T(8,128)S(1)}, u32[]{:S(2)}, u32[]{:S(2)}) collective-permute-start(f32[264,128]{1,0:T(8,128)S(1)} %get-tuple-element.76.own_ref), channel_id=1, source_target_pairs={{0,6},{1,7},{2,4},{3,5},{4,2},{5,3},{6,0},{7,1},{8,14},{9,15},{10,... | collective-permute-start | bytes 405512 | tf_op jit(solution)/shard_map/ppermute | solution.py:344
  81.0 9.4 %collective-permute-start.19 = (f32[328,128]{1,0:T(8,128)S(1)}, f32[328,128]{1,0:T(8,128)S(1)}, u32[]{:S(2)}, u32[]{:S(2)}) collective-permute-start(f32[328,128]{1,0:T(8,128)S(1)} %get-tuple-element.81), channel_id=1, source_target_pairs={{0,2},{1,3},{2,0},{3,1},{4,6},{5,7},{6,4},{7,5},{8,10},{9,11},{10,... | collective-permute-start | bytes 503816 | tf_op jit(solution)/shard_map/ppermute | solution.py:344
  86.4 4.0 %collective-permute-start.20 = (f32[72,128]{1,0:T(8,128)S(1)}, f32[72,128]{1,0:T(8,128)S(1)}, u32[]{:S(2)}, u32[]{:S(2)}) collective-permute-start(f32[72,128]{1,0:T(8,128)S(1)} %get-tuple-element.82), channel_id=1, source_target_pairs={{0,2},{1,3},{2,0},{3,1},{4,6},{5,7},{6,4},{7,5},{8,10},{9,11},{10,... | collective-permute-start | bytes 110600 | tf_op jit(solution)/shard_map/ppermute | solution.py:344
  90.5 1.5 %collective-permute-start.21 = (f32[392,128]{1,0:T(8,128)S(1)}, f32[392,128]{1,0:T(8,128)S(1)}, u32[]{:S(2)}, u32[]{:S(2)}) collective-permute-start(f32[392,128]{1,0:T(8,128)S(1)} %get-tuple-element.84), channel_id=1, source_target_pairs={{0,1},{1,0},{2,3},{3,2},{4,5},{5,4},{6,7},{7,6},{8,9},{9,8},{10,11... | collective-permute-start | bytes 602120 | tf_op jit(solution)/shard_map/ppermute | solution.py:344
  92.0 4.4 %collective-permute-start.22 = (f32[8,256]{1,0:T(8,128)S(1)}, f32[8,256]{1,0:T(8,128)S(1)}, u32[]{:S(2)}, u32[]{:S(2)}) collective-permute-start(f32[8,256]{1,0:T(8,128)S(1)} %get-tuple-element.86.known_ref.refs_4_), channel_id=1, source_target_pairs={{0,8},{8,0},{16,24},{24,16},{1,9},{9,1},{17,25},{25,17},{2,10},{10... | collective-permute-start | bytes 24584 | tf_op jit(solution)/shard_map/ppermute | solution.py:433
  93.6 3.7 %collective-permute-start.23 = (f32[8,256]{1,0:T(8,128)S(1)}, f32[8,256]{1,0:T(8,128)S(1)}, u32[]{:S(2)}, u32[]{:S(2)}) collective-permute-start(f32[8,256]{1,0:T(8,128)S(1)} %get-tuple-element.86.known_ref.refs_4_), channel_id=1, source_target_pairs={{0,16},{8,24},{16,0},{24,8},{1,17},{9,25},{17,1},{25,9},{2,18},{10... | collective-permute-start | bytes 24584 | tf_op jit(solution)/shard_map/ppermute | solution.py:433
  94.9 4.5 %collective-permute-start.24 = (f32[8,256]{1,0:T(8,128)S(1)}, f32[8,256]{1,0:T(8,128)S(1)}, u32[]{:S(2)}, u32[]{:S(2)}) collective-permute-start(f32[8,256]{1,0:T(8,128)S(1)} %get-tuple-element.86.known_ref.refs_4_), channel_id=1, source_target_pairs={{0,24},{8,16},{16,8},{24,0},{1,25},{9,17},{17,9},{25,1},{2,26},{10... | collective-permute-start | bytes 24584 | tf_op jit(solution)/shard_map/ppermute | solution.py:433
